TPU v7x, 32 devices: a whole 2x2x4 slice. The times are simulated.
32 devices in a mesh: groups: 2 (over x), node: 16 (over z, y, core).
Axes of the slice: x: 2, y: 2, z: 4, core: 2. Of those that a mesh axis runs over, the one named last changes fastest.
Arguments:
- tokens: bfloat16 [4096, 3584], P(('groups', 'node')), parts along dimension 0, may hold values from -6 to 6
- expert_ids: int32 [4096, 4], P(('groups', 'node')), parts along dimension 0, may hold values from 0 to 7, all different within a row; in each aligned block of 128 rows (0 to 127, 128 to 255, ...) at most 80 rows name the same one
- gate_codes: int32 [4096, 4], P(('groups', 'node')), parts along dimension 0, may hold values from 1 to 4096
- w_gate: bfloat16 [3584, 8192], P(None, 'node'), may hold values from -0.09375 to 0.09375
- w_up: bfloat16 [3584, 8192], P(None, 'node'), may hold values from -0.09375 to 0.09375
- w_down: bfloat16 [8192, 3584], P('node'), may hold values from -0.1875 to 0.1875
Outputs:
- mixed: bfloat16 [4096, 3584], P(('groups', 'node')), parts along dimension 0
There are 2 independent parts, one for each index of `groups`. A program takes and returns all parts, laid end to end along the dimension named above; an argument that names none is the same for every part. Nothing has to cross between parts.
Inputs may be any that keep to these rules, and one draw needn't show every extreme that they name: `expert_ids`: each row names 4 different experts. In the rows of one device no expert is named more than 80 times, a bound that some block reaches.
All inputs are finite; a program needn't handle non-finite values.
Results may differ from a plain program's by a relative error of at most 0.0067.
Values may be sent and summed in bfloat16 or wider, within the bound.
No kernel may reach another device: no remote copies, remote signals or barrier semaphores. Data moves between devices by JAX's collectives and lax.ppermute only.
A program may use at most 128 MiB of HBM per device.

v0:
```python
import jax
import jax.numpy as jnp
from jax import lax
from jax.sharding import PartitionSpec as P

SPAN = 2


def body(tokens, expert_ids, gate_codes, w_gate, w_up, w_down):
    nodes = lax.axis_size("node")
    experts = nodes // SPAN
    tok, top = expert_ids.shape
    dim = tokens.shape[1]
    cap = 2 * (tok * top * 5 // (8 * experts))
    flat = expert_ids.reshape(-1)
    onehot = (flat[:, None] == jnp.arange(experts, dtype=jnp.int32)[None, :]).astype(jnp.int32)
    ranks = jnp.sum((jnp.cumsum(onehot, 0) - onehot) * onehot, 1)
    slots = flat * cap + ranks
    owners = (
        jnp.full((experts * cap,), -1, jnp.int32)
        .at[slots]
        .set(jnp.arange(tok * top, dtype=jnp.int32) // top)
    )
    filled = owners >= 0
    outgoing = jnp.where(
        filled[:, None], tokens[jnp.maximum(owners, 0)], jnp.zeros((), tokens.dtype)
    )
    copies = jnp.broadcast_to(
        outgoing.reshape(experts, 1, cap, dim), (experts, SPAN, cap, dim)
    ).reshape(nodes, cap, dim)
    rows = lax.all_to_all(copies, "node", split_axis=0, concat_axis=0, tiled=True).reshape(
        nodes * cap, dim
    )
    gate = jnp.dot(rows, w_gate, preferred_element_type=jnp.float32)
    upward = jnp.dot(rows, w_up, preferred_element_type=jnp.float32)
    hidden = (jax.nn.silu(gate) * upward).astype(jnp.bfloat16)
    partial_out = jnp.dot(hidden, w_down, preferred_element_type=jnp.float32).astype(jnp.bfloat16)
    returned = lax.all_to_all(
        partial_out.reshape(nodes, cap, dim), "node", split_axis=0, concat_axis=0, tiled=True
    )
    returned = returned.reshape(experts, SPAN, cap, dim)
    combined = (returned[:, 0].astype(jnp.float32) + returned[:, 1].astype(jnp.float32)).astype(
        jnp.bfloat16
    )
    combined = combined.reshape(experts * cap, dim)
    picked = combined[slots].astype(jnp.float32).reshape(tok, top, dim)
    weights = gate_codes.astype(jnp.float32) * (1.0 / 4096.0)
    return jnp.sum(picked * weights[:, :, None], 1).astype(jnp.bfloat16)


def solution(mesh):
    in_specs = (
        P(("groups", "node"), None),
        P(("groups", "node"), None),
        P(("groups", "node"), None),
        P(None, "node"),
        P(None, "node"),
        P("node", None),
    )
    out_specs = P(("groups", "node"), None)
    return jax.shard_map(body, mesh=mesh, in_specs=in_specs, out_specs=out_specs, check_vma=False)
```

profile of v0, /device:TPU:13, one launch (start us, length us, event | category | flops | bytes accessed | tf_op | source)
XLA Modules:
  0.0 495.2 jit_solution(1432347729159648811)
XLA Ops:
  0.0 0.0 copy-start
  0.0 0.9 copy.11
  0.9 0.1 eq.29
  1.0 0.1 eq.25
  1.1 0.7 broadcast_multiply_fusion
  1.8 1.1 reduce-window.6
  2.9 0.2 slice_reduce_fusion
  3.2 0.1 copy.10
  3.3 0.1 mul.42
  3.4 0.1 fusion.2
  3.5 2.4 scatter_custom_fusion
  6.0 0.1 broadcast_in_dim.31
  6.1 0.0 copy-done
  6.1 5.1 %gather_fusion = bf16[640,3584]{1,0:T(8,128)(2,1)} fusion(bf16[128,3584]{1,0:T(8,128)(2,1)S(1)} %copy-done, s32[1024]{0:T(1024)S(1)} %pad_clamp_fusion.1), kind=kCustom, calls=%fused_computation | custom fusion | bytes 9177600 | tf_op jit(solution)/shard_map/gather | solution.py:26
  11.2 4.9 broadcast_select_fusion
  16.1 6.7 %broadcast_in_dim.35 = bf16[8,2,80,3584]{3,2,1,0:T(8,128)(2,1)} broadcast(bf16[8,80,3584]{2,1,0:T(8,128)(2,1)} %broadcast_select_fusion), dimensions={0,2,3} | broadcast | bytes 13762560 | tf_op jit(solution)/shard_map/broadcast_in_dim | solution.py:28
  22.8 0.0 copy-start.4
  22.8 205.8 %all_to_all.10 = bf16[16,80,3584]{2,1,0:T(8,128)(2,1)S(1)} all-to-all(bf16[16,80,3584]{2,1,0:T(8,128)(2,1)} %bitcast.39), channel_id=1, replica_groups=mesh['groups'=2,'node'=16] {'node'}, dimensions={0} | all-to-all | bytes 18350080 | tf_op jit(solution)/shard_map/all_to_all | solution.py:31
  228.6 0.0 copy-start.2
  228.6 3.5 copy-done.2
  232.1 0.0 copy-done.4
  232.1 6.4 %fusion.9 = f32[1280,512]{1,0:T(8,128)} fusion(bf16[1280,3584]{1,0:T(8,128)(2,1)S(1)} %bitcast.42, bf16[3584,512]{1,0:T(8,128)(2,1)S(1)} %copy-done.4), kind=kOutput, calls=%fused_computation.34 | convolution fusion | flops 4697620480 | bytes 15466496 | tf_op jit(solution)/shard_map/dot_general | solution.py:34
  238.5 17.0 %convolution_convert_fusion = bf16[1280,3584]{1,0:T(8,128)(2,1)} fusion(bf16[512,3584]{1,0:T(8,128)(2,1)} %param.11, bf16[1280,3584]{1,0:T(8,128)(2,1)} %bitcast.43, bf16[3584,512]{1,0:T(8,128)(2,1)} %param.10, f32[1280,512]{1,0:T(8,128)} %fusion.9), kind=kOutput, calls=%fused_computation.3 | convolution fusion | flops 9403760640 | bytes 28311552 | tf_op jit(solution)/shard_map/dot_general | solution.py:37
  255.5 0.0 copy-start.3
  255.5 5.9 %all-to-all-start.1 = ((bf16[16,80,3584]{2,1,0:T(8,128)(2,1)}), bf16[16,80,3584]{2,1,0:T(8,128)(2,1)}, u32[]{:S(2)}, u32[]{:S(2)}) async-start(bf16[16,80,3584]{2,1,0:T(8,128)(2,1)} %bitcast.41), calls=%async_computation.1 | async-start | bytes 18350080 | tf_op jit(solution)/shard_map/all_to_all | solution.py:38
  261.4 0.0 copy-done.3
  261.4 0.1 copy.15
  261.5 199.1 %all-to-all-done.1 = bf16[16,80,3584]{2,1,0:T(8,128)(2,1)} async-done(((bf16[16,80,3584]{2,1,0:T(8,128)(2,1)}), bf16[16,80,3584]{2,1,0:T(8,128)(2,1)}, u32[]{:S(2)}, u32[]{:S(2)}) %all-to-all-start.1) | async-done | bytes 9175072 | tf_op jit(solution)/shard_map/all_to_all | solution.py:38
  460.6 6.9 %add_convert_fusion = bf16[8,1,80,3584]{3,2,0,1:T(8,128)(2,1)} fusion(bf16[8,2,80,3584]{3,2,1,0:T(8,128)(2,1)} %bitcast.8), kind=kLoop, calls=%fused_computation.4 | loop fusion | flops 9175040 | bytes 13762560 | tf_op jit(solution)/shard_map/convert_element_type | solution.py:42
  467.5 10.8 %gather_fusion.1 = bf16[512,3584]{1,0:T(8,128)(2,1)} fusion(bf16[640,3584]{1,0:T(8,128)(2,1)} %bitcast.38, s32[1024]{0:T(1024)S(1)} %pad_clamp_fusion), kind=kCustom, calls=%fused_computation.1 | custom fusion | bytes 7342080 | tf_op jit(solution)/shard_map/gather | solution.py:46
  478.3 0.0 copy-start.1
  478.3 7.6 %reshape.89 = f32[128,4,3584]{2,1,0:T(4,128)} reshape(bf16[512,3584]{1,0:T(8,128)(2,1)} %gather_fusion.1) | data formatting | bytes 11010048 | tf_op jit(solution)/shard_map/convert_element_type | solution.py:46
  485.9 9.3 %multiply_reduce_fusion = bf16[128,3584]{1,0:T(8,128)(2,1)} fusion(f32[128,4,3584]{2,1,0:T(4,128)} %reshape.89, f32[128,4]{1,0:T(8,128)S(1)} %copy.15), kind=kLoop, calls=%fused_computation.5 | loop fusion | flops 3211264 | bytes 8259584 | tf_op jit(solution)/shard_map/reduce_sum | solution.py:48
  495.2 0.0 copy-done.1
  (10 shorter events, 0.1 us)
Async XLA Ops:
  0.0 6.1 %copy-start = (bf16[128,3584]{1,0:T(8,128)(2,1)S(1)}, bf16[128,3584]{1,0:T(8,128)(2,1)}, u32[]{:S(2)}) copy-start(bf16[128,3584]{1,0:T(8,128)(2,1)} %param.6) | copy-start | bytes 2752516
  22.8 209.4 %copy-start.4 = (bf16[3584,512]{1,0:T(8,128)(2,1)S(1)}, bf16[3584,512]{1,0:T(8,128)(2,1)}, u32[]{:S(2)}) copy-start(bf16[3584,512]{1,0:T(8,128)(2,1)} %param.9) | copy-start | bytes 11010052
  228.6 3.6 copy-start.2
  255.5 5.9 %copy-start.3 = (s32[128,4]{0,1:T(4,128)S(1)}, s32[128,4]{0,1:T(4,128)}, u32[]{:S(2)}) copy-start(s32[128,4]{0,1:T(4,128)} %param.8) | copy-start | bytes 6148
  255.5 205.1 %all-to-all-start.1 = ((bf16[16,80,3584]{2,1,0:T(8,128)(2,1)}), bf16[16,80,3584]{2,1,0:T(8,128)(2,1)}, u32[]{:S(2)}, u32[]{:S(2)}) async-start(bf16[16,80,3584]{2,1,0:T(8,128)(2,1)} %bitcast.41), calls=%async_computation.1 | async-start | bytes 18350080 | tf_op jit(solution)/shard_map/all_to_all | solution.py:38
  478.3 16.8 %copy-start.1 = (bf16[128,3584]{1,0:T(8,128)(2,1)S(1)}, bf16[128,3584]{1,0:T(8,128)(2,1)}, u32[]{:S(2)}) copy-start(bf16[128,3584]{1,0:T(8,128)(2,1)} %param.6) | copy-start | bytes 2752516
where the time goes:
time: 496 us; the launch traced here: 495 us
  blocking collectives  206 us (42%)
  waiting for transfers between devices  199 us (40%)
  local copies, waits for them, and re-layouts  37.9 us (8%)
  matrix products  23.3 us (5%)
  other arithmetic  23 us (5%)
  starting transfers between devices  5.91 us (1%)
    all_to_all x1, blocking collectives, body(): lax.all_to_all(copies, 'node', split_axis=0, concat_axis=0, tiled=True)  206 us
    all_to_all x1, waiting for transfers between devices, body(): lax.all_to_all(partial_out.reshape(nodes, cap, dim), 'node', split_axis=0...  199 us
    dot_general x1, matrix products, body(): jnp.dot(hidden, w_down, preferred_element_type=jnp.float32)  17 us
    gather x1, local copies, waits for them, and re-layouts, body(): picked = combined[slots].astype(jnp.float32).reshape(tok, top, dim)  10.8 us
  transfers between devices with their start and end apart: 1, of which 1 were waited for; matrix products, arithmetic and copies ran while one was open for 0% of the time, Pallas kernels for 0%

commit v1 on v0

v1 whole, which is shorter than its diff:
```python
import jax
import jax.numpy as jnp
from jax import lax
from jax.sharding import PartitionSpec as P

SPAN = 2
CHUNKS = 4


def body(tokens, expert_ids, gate_codes, w_gate, w_up, w_down):
    nodes = lax.axis_size("node")
    expert = lax.axis_index("node") // SPAN
    tok, top = expert_ids.shape
    dim = tokens.shape[1]
    rows_of = tok // CHUNKS
    table = lax.all_gather(
        jnp.concatenate([expert_ids, gate_codes], 1), "node", axis=0, tiled=False
    )
    ids, codes = table[:, :, :top], table[:, :, top:]
    scale = jnp.sum(jnp.where(ids == expert, codes, 0), 2).astype(jnp.float32) * (1.0 / 4096.0)
    outs = []
    for c in range(CHUNKS):
        mine = tokens[c * rows_of : (c + 1) * rows_of]
        rows = lax.all_gather(mine, "node", axis=0, tiled=True)
        weight = scale[:, c * rows_of : (c + 1) * rows_of].reshape(nodes * rows_of, 1)
        gate = jnp.dot(rows, w_gate, preferred_element_type=jnp.float32)
        upward = jnp.dot(rows, w_up, preferred_element_type=jnp.float32)
        hidden = (jax.nn.silu(gate) * upward * weight).astype(jnp.bfloat16)
        part = jnp.dot(hidden, w_down, preferred_element_type=jnp.float32).astype(jnp.bfloat16)
        outs.append(lax.psum_scatter(part, "node", scatter_dimension=0, tiled=True))
    return jnp.concatenate(outs, 0)


def solution(mesh):
    in_specs = (
        P(("groups", "node"), None),
        P(("groups", "node"), None),
        P(("groups", "node"), None),
        P(None, "node"),
        P(None, "node"),
        P("node", None),
    )
    out_specs = P(("groups", "node"), None)
    return jax.shard_map(body, mesh=mesh, in_specs=in_specs, out_specs=out_specs, check_vma=False)
```

time: 496 us -> 502 us (1.012)
  the two profiles are of different devices: /device:TPU:13 before, /device:TPU:0 now
where the time goes in v1:
time: 502 us
  waiting for transfers between devices  397 us (79%)
  matrix products  61.9 us (12%)
  blocking collectives  23.3 us (5%)
  between operations  13.5 us (3%)
    reduce_scatter x4, waiting for transfers between devices, body(): outs.append(lax.psum_scatter(part, 'node', scatter_dimension=0, tiled=True))  271 us
    all_gather x4, waiting for transfers between devices, body(): rows = lax.all_gather(mine, 'node', axis=0, tiled=True)  124 us
    dot_general x4, matrix products, body(): jnp.dot(hidden, w_down, preferred_element_type=jnp.float32)  41 us
    all_gather x1, blocking collectives, body(): lax.all_gather(jnp.concatenate([expert_ids, gate_codes], 1), 'node', axis...  23.3 us
    dot_general x4, matrix products, body(): gate = jnp.dot(rows, w_gate, preferred_element_type=jnp.float32)  20.8 us
  transfers between devices with their start and end apart: 8, of which 8 were waited for; matrix products, arithmetic and copies ran while one was open for 13% of the time, Pallas kernels for 0%

profile of v1, /device:TPU:0, one launch (start us, length us, event | category | flops | bytes accessed | tf_op | source)
XLA Modules:
  0.0 501.8 jit_solution(13913483510730824366)
XLA Ops:
  6.5 0.0 all-gather.6.cloned.1.call-start
  6.5 2.2 fusion.21
  8.7 0.0 all-gather.6.cloned.1.call-update
  8.8 0.0 all-gather.8.cloned.1.call-start
  8.8 0.7 all-gather.8.cloned.1.call-update
  9.5 0.0 all-gather.10.cloned.1.call-start
  9.6 0.7 all-gather.10.cloned.1.call-update
  10.3 0.0 all-gather.12.cloned.1.call-start
  10.3 0.5 all-gather.12.cloned.1.call-update
  10.8 0.0 reduce-scatter.5.cloned.1.call-start
  10.9 0.7 pad_add_fusion
  11.6 23.3 %all-gather = s32[2048,8]{0,1:T(8,128)S(1)} all-gather(s32[128,8]{0,1:T(8,128)S(1)} %pad_add_fusion), channel_id=2, replica_groups=mesh['groups'=2,'node'=16] {'node'}, dimensions={0}, use_global_device_ids=true | all-gather | bytes 69632 | tf_op jit(solution)/shard_map/all_gather | solution.py:16
  35.0 0.1 fusion.22
  35.0 0.1 mul.75
  35.1 24.8 %all-gather.6.cloned.1.call-done = bf16[512,3584]{1,0:T(8,128)(2,1)} async-done(((bf16[32,3584]{1,0:T(8,128)(2,1)}), bf16[512,3584]{1,0:T(8,128)(2,1)}) %all-gather.6.cloned.1.call-update) | async-done | bytes 3670032 | tf_op jit(solution)/shard_map/all_gather | solution.py:24
  59.9 5.2 %fusion.23 = f32[512,512]{1,0:T(8,128)S(1)} fusion(bf16[512,3584]{1,0:T(8,128)(2,1)} %all-gather.6.cloned.1.call-done, bf16[3584,512]{1,0:T(8,128)(2,1)} %param.9), kind=kOutput, calls=%fused_computation.36 | convolution fusion | flops 1879048192 | bytes 8388608 | tf_op jit(solution)/shard_map/dot_general | solution.py:26
  65.1 10.2 %convolution_convert_fusion.3 = bf16[512,3584]{1,0:T(8,128)(2,1)} fusion(bf16[512,3584]{1,0:T(8,128)(2,1)} %param.11, bf16[512,3584]{1,0:T(8,128)(2,1)} %all-gather.6.cloned.1.call-done, bf16[3584,512]{1,0:T(8,128)(2,1)} %param.10, f32[512,512]{1,0:T(8,128)S(1)} %fusion.23, f32[512]{0:T(512)S(1)} %mul.75), kind=kOutput, calls=%fused_computation.3 | convolution fusion | flops 3761766400 | bytes 15730688 | tf_op jit(solution)/shard_map/dot_general | solution.py:29
  75.3 0.0 reduce-scatter.5.cloned.1.call-update
  75.4 0.0 reduce-scatter.7.cloned.1.call-start
  75.4 0.1 mul.80
  75.5 33.3 %all-gather.8.cloned.1.call-done = bf16[512,3584]{1,0:T(8,128)(2,1)} async-done(((bf16[32,3584]{1,0:T(8,128)(2,1)}), bf16[512,3584]{1,0:T(8,128)(2,1)}) %all-gather.8.cloned.1.call-update) | async-done | bytes 3670032 | tf_op jit(solution)/shard_map/all_gather | solution.py:24
  108.8 5.2 %fusion.24 = f32[512,512]{1,0:T(8,128)S(1)} fusion(bf16[512,3584]{1,0:T(8,128)(2,1)} %all-gather.8.cloned.1.call-done, bf16[3584,512]{1,0:T(8,128)(2,1)} %param.9), kind=kOutput, calls=%fused_computation.37 | convolution fusion | flops 1879048192 | bytes 8388608 | tf_op jit(solution)/shard_map/dot_general | solution.py:26
  114.0 10.3 %convolution_convert_fusion.2 = bf16[512,3584]{1,0:T(8,128)(2,1)} fusion(bf16[512,3584]{1,0:T(8,128)(2,1)} %param.11, bf16[512,3584]{1,0:T(8,128)(2,1)} %all-gather.8.cloned.1.call-done, bf16[3584,512]{1,0:T(8,128)(2,1)} %param.10, f32[512,512]{1,0:T(8,128)S(1)} %fusion.24, f32[512]{0:T(512)S(1)} %mul.80), kind=kOutput, calls=%fused_computation.2 | convolution fusion | flops 3761766400 | bytes 15730688 | tf_op jit(solution)/shard_map/dot_general | solution.py:29
  124.3 0.0 reduce-scatter.7.cloned.1.call-update
  124.3 0.0 reduce-scatter.9.cloned.1.call-start
  124.4 0.1 mul.85
  124.5 33.2 %all-gather.10.cloned.1.call-done = bf16[512,3584]{1,0:T(8,128)(2,1)} async-done(((bf16[32,3584]{1,0:T(8,128)(2,1)}), bf16[512,3584]{1,0:T(8,128)(2,1)}) %all-gather.10.cloned.1.call-update) | async-done | bytes 3670032 | tf_op jit(solution)/shard_map/all_gather | solution.py:24
  157.7 5.2 %fusion.25 = f32[512,512]{1,0:T(8,128)S(1)} fusion(bf16[512,3584]{1,0:T(8,128)(2,1)} %all-gather.10.cloned.1.call-done, bf16[3584,512]{1,0:T(8,128)(2,1)} %param.9), kind=kOutput, calls=%fused_computation.38 | convolution fusion | flops 1879048192 | bytes 8388608 | tf_op jit(solution)/shard_map/dot_general | solution.py:26
  162.9 10.2 %convolution_convert_fusion.1 = bf16[512,3584]{1,0:T(8,128)(2,1)} fusion(bf16[512,3584]{1,0:T(8,128)(2,1)} %param.11, bf16[512,3584]{1,0:T(8,128)(2,1)} %all-gather.10.cloned.1.call-done, bf16[3584,512]{1,0:T(8,128)(2,1)} %param.10, f32[512,512]{1,0:T(8,128)S(1)} %fusion.25, f32[512]{0:T(512)S(1)} %mul.85), kind=kOutput, calls=%fused_computation.1 | convolution fusion | flops 3761766400 | bytes 15730688 | tf_op jit(solution)/shard_map/dot_general | solution.py:29
  173.1 0.0 reduce-scatter.9.cloned.1.call-update
  173.1 0.2 reduce-scatter.11.cloned.1.call-start
  173.4 0.1 mul.90
  173.5 33.0 %all-gather.12.cloned.1.call-done = bf16[512,3584]{1,0:T(8,128)(2,1)} async-done(((bf16[32,3584]{1,0:T(8,128)(2,1)}), bf16[512,3584]{1,0:T(8,128)(2,1)}) %all-gather.12.cloned.1.call-update) | async-done | bytes 3670032 | tf_op jit(solution)/shard_map/all_gather | solution.py:24
  206.4 5.2 %fusion.26 = f32[512,512]{1,0:T(8,128)S(1)} fusion(bf16[512,3584]{1,0:T(8,128)(2,1)} %all-gather.12.cloned.1.call-done, bf16[3584,512]{1,0:T(8,128)(2,1)} %param.9), kind=kOutput, calls=%fused_computation.39 | convolution fusion | flops 1879048192 | bytes 8388608 | tf_op jit(solution)/shard_map/dot_general | solution.py:26
  211.6 10.3 %convolution_convert_fusion = bf16[512,3584]{1,0:T(8,128)(2,1)} fusion(bf16[512,3584]{1,0:T(8,128)(2,1)} %param.11, bf16[512,3584]{1,0:T(8,128)(2,1)} %all-gather.12.cloned.1.call-done, bf16[3584,512]{1,0:T(8,128)(2,1)} %param.10, f32[512,512]{1,0:T(8,128)S(1)} %fusion.26, f32[512]{0:T(512)S(1)} %mul.90), kind=kOutput, calls=%fused_computation | convolution fusion | flops 3761766400 | bytes 15730688 | tf_op jit(solution)/shard_map/dot_general | solution.py:29
  221.9 0.0 reduce-scatter.11.cloned.1.call-update
  222.0 55.8 %reduce-scatter.5.cloned.1.call-done = bf16[32,3584]{1,0:T(8,128)(2,1)} async-done(((bf16[512,3584]{1,0:T(8,128)(2,1)}), bf16[32,3584]{1,0:T(8,128)(2,1)}) %reduce-scatter.5.cloned.1.call-update) | async-done | bytes 229392 | tf_op jit(solution)/shard_map/reduce_scatter | solution.py:30
  277.8 71.8 %reduce-scatter.7.cloned.1.call-done = bf16[32,3584]{1,0:T(8,128)(2,1)} async-done(((bf16[512,3584]{1,0:T(8,128)(2,1)}), bf16[32,3584]{1,0:T(8,128)(2,1)}) %reduce-scatter.7.cloned.1.call-update) | async-done | bytes 229392 | tf_op jit(solution)/shard_map/reduce_scatter | solution.py:30
  349.6 71.2 %reduce-scatter.9.cloned.1.call-done = bf16[32,3584]{1,0:T(8,128)(2,1)} async-done(((bf16[512,3584]{1,0:T(8,128)(2,1)}), bf16[32,3584]{1,0:T(8,128)(2,1)}) %reduce-scatter.9.cloned.1.call-update) | async-done | bytes 229392 | tf_op jit(solution)/shard_map/reduce_scatter | solution.py:30
  420.7 72.0 %reduce-scatter.11.cloned.1.call-done = bf16[32,3584]{1,0:T(8,128)(2,1)} async-done(((bf16[512,3584]{1,0:T(8,128)(2,1)}), bf16[32,3584]{1,0:T(8,128)(2,1)}) %reduce-scatter.11.cloned.1.call-update) | async-done | bytes 229392 | tf_op jit(solution)/shard_map/reduce_scatter | solution.py:30
  492.7 2.3 pad_maximum_fusion
  (2 shorter events, 0.0 us)
Async XLA Ops:
  6.5 53.4 %all-gather.6.cloned.1.call-start = ((), (), s32[]{:S(2)}) async-start(), calls=%async_computation.4 | async-start | bytes 3899392 | tf_op jit(solution)/shard_map/all_gather | solution.py:24
  8.8 100.0 %all-gather.8.cloned.1.call-start = ((), (), s32[]{:S(2)}) async-start(), calls=%async_computation.6 | async-start | bytes 3899392 | tf_op jit(solution)/shard_map/all_gather | solution.py:24
  9.5 148.2 %all-gather.10.cloned.1.call-start = ((), (), s32[]{:S(2)}) async-start(), calls=%async_computation.8 | async-start | bytes 3899392 | tf_op jit(solution)/shard_map/all_gather | solution.py:24
  10.3 196.2 %all-gather.12.cloned.1.call-start = ((), (), s32[]{:S(2)}) async-start(), calls=%async_computation.10 | async-start | bytes 3899392 | tf_op jit(solution)/shard_map/all_gather | solution.py:24
  10.8 266.9 %reduce-scatter.5.cloned.1.call-start = ((), (), s32[]{:S(2)}) async-start(), calls=%async_computation.5 | async-start | bytes 3899392 | tf_op jit(solution)/shard_map/reduce_scatter | solution.py:30
  75.4 274.2 %reduce-scatter.7.cloned.1.call-start = ((), (), s32[]{:S(2)}) async-start(), calls=%async_computation.7 | async-start | bytes 3899392 | tf_op jit(solution)/shard_map/reduce_scatter | solution.py:30
  124.3 296.4 %reduce-scatter.9.cloned.1.call-start = ((), (), s32[]{:S(2)}) async-start(), calls=%async_computation.9 | async-start | bytes 3899392 | tf_op jit(solution)/shard_map/reduce_scatter | solution.py:30
  173.1 319.6 %reduce-scatter.11.cloned.1.call-start = ((), (), s32[]{:S(2)}) async-start(), calls=%async_computation.11 | async-start | bytes 3899392 | tf_op jit(solution)/shard_map/reduce_scatter | solution.py:30
Sparse Core Ops, SparseCore 0:
  9.6 50.2 all-gather.5
  62.2 46.5 all-gather.7
  111.1 46.5 all-gather.9
  159.8 46.5 all-gather.11
  210.1 67.6 reduce-scatter.4
  282.0 67.5 reduce-scatter.6
  353.4 67.3 reduce-scatter.8
  425.1 67.5 reduce-scatter.10

commit v2 on v1

v2 whole, which is shorter than its diff:
```python
import jax
import jax.numpy as jnp
from jax import lax
from jax.sharding import PartitionSpec as P

SPAN = 2


def body(tokens, expert_ids, gate_codes, w_gate, w_up, w_down):
    nodes = lax.axis_size("node")
    ring = nodes // SPAN
    far = ring // 2
    tok, top = expert_ids.shape
    half = tok // 2

    def chip_at(pos):
        return 2 * pos if pos < far else 2 * (ring - 1 - pos) + 1

    def perm(step):
        return [
            (chip_at(pos) * SPAN + core, chip_at((pos + step) % ring) * SPAN + core)
            for pos in range(ring)
            for core in range(SPAN)
        ]

    forward, backward = perm(1), perm(-1)
    swap = [(node, node ^ 1) for node in range(nodes)]

    me = lax.axis_index("node")
    expert, core = me // SPAN, me % SPAN
    pos = jnp.where(expert % 2 == 0, expert // 2, ring - 1 - expert // 2)

    ahead = [[tokens[:half]], [tokens[half:]]]
    behind = [[tokens[:half]], [tokens[half:]]]
    for s in range(1, far + 1):
        for h in range(2):
            if s < far or h == 0:
                ahead[h].append(lax.ppermute(ahead[h][-1], "node", forward))
            if s < far or h == 1:
                behind[h].append(lax.ppermute(behind[h][-1], "node", backward))

    others = [lax.ppermute(w, "node", swap) for w in (w_gate, w_up, w_down)]
    pairs = [(w_gate, w_up, w_down), tuple(others)]

    table = lax.all_gather(
        jnp.concatenate([expert_ids, gate_codes], 1), "node", axis=0, tiled=False
    )
    ids, codes = table[:, :, :top], table[:, :, top:]
    scale = jnp.sum(jnp.where(ids == expert, codes, 0), 2).astype(jnp.float32) * (1.0 / 4096.0)

    def scale_at(offset):
        origin = (pos + offset) % ring
        chip = jnp.where(origin < far, 2 * origin, 2 * (ring - 1 - origin) + 1)
        return lax.dynamic_index_in_dim(scale, chip * SPAN + core, 0, keepdims=False)

    def expert_part(rows, weight):
        total = None
        for gate_w, up_w, down_w in pairs:
            gate = jnp.dot(rows, gate_w, preferred_element_type=jnp.float32)
            upward = jnp.dot(rows, up_w, preferred_element_type=jnp.float32)
            hidden = (jax.nn.silu(gate) * upward * weight[:, None]).astype(jnp.bfloat16)
            part = jnp.dot(hidden, down_w, preferred_element_type=jnp.float32)
            total = part if total is None else total + part
        return total.astype(jnp.bfloat16)

    parts = {}

    def work(offsets):
        blocks, weights, names = [], [], []
        for offset in offsets:
            source = ahead if offset <= 0 else behind
            for h in range(2):
                if abs(offset) == far:
                    blocks.append((ahead, behind)[h][h][far])
                else:
                    blocks.append(source[h][abs(offset)])
                names.append((offset, h))
            weights.append(scale_at(offset))
        out = expert_part(jnp.concatenate(blocks, 0), jnp.concatenate(weights, 0))
        for i, (offset, h) in enumerate(names):
            parts[offset, h] = out[i * half : (i + 1) * half]

    work([0])
    for s in range(1, far):
        work([-s, s])
    work([far])
    parts[-far, 1] = parts[far, 1]

    def add(*terms):
        return sum(t.astype(jnp.float32) for t in terms).astype(jnp.bfloat16)

    outs = []
    for h in range(2):
        came = {}
        for sign, way in ((1, forward), (-1, backward)):
            first = far if (h == 0) == (sign == 1) else far - 1
            total = parts[sign * first, h]
            for d in range(first - 1, -1, -1):
                arrived = lax.ppermute(total, "node", way)
                total = add(parts[sign * d, h], arrived) if d else arrived
            came[sign] = total
        outs.append(add(parts[0, h], came[1], came[-1]))
    return jnp.concatenate(outs, 0)


def solution(mesh):
    in_specs = (
        P(("groups", "node"), None),
        P(("groups", "node"), None),
        P(("groups", "node"), None),
        P(None, "node"),
        P(None, "node"),
        P("node", None),
    )
    out_specs = P(("groups", "node"), None)
    return jax.shard_map(body, mesh=mesh, in_specs=in_specs, out_specs=out_specs, check_vma=False)
```

time: 502 us -> 243 us (0.48)
  waiting for transfers between devices: 397 us -> 58.7 us
  matrix products: 61.9 us -> 99.8 us
  starting transfers between devices: 0.46 us -> 23.3 us
  local copies, waits for them, and re-layouts: 2.59 us -> 17.8 us
  between operations: 13.5 us -> 0.48 us
  other arithmetic: 3 us -> 11.4 us
  blocking collectives: 23.3 us -> 30.8 us
    reduce_scatter x4 -> x0, waiting for transfers between devices: 271 us -> none  [body(): outs.append(lax.psum_scatter(part, 'node', scatter_dimension=0, tiled=True))]
    all_gather x4 -> x0, waiting for transfers between devices: 124 us -> none  [body(): rows = lax.all_gather(mine, 'node', axis=0, tiled=True)]
    ppermute x0 -> x31, waiting for transfers between devices: none -> 58.7 us  [the longest x7 26.3 us: body(): ahead[h].append(lax.ppermute(ahead[h][-1], 'node', forward))]
    dot_general x8 -> x20, matrix products: 61.9 us -> 99.8 us  [the longest x10 66 us: expert_part(): part = jnp.dot(hidden, down_w, preferred_element_type=jnp.float32)]
    ppermute x0 -> x31, starting transfers between devices: none -> 23.3 us  [the longest x14 14.2 us: body(): arrived = lax.ppermute(total, 'node', way)]
    convert_element_type x0 -> x5, other arithmetic: none -> 11.3 us  [add(): return sum((t.astype(jnp.float32) for t in terms)).astype(jnp.bfloat16)]
    unnamed x0 -> x40, local copies, waits for them, and re-layouts: none -> 9.26 us
    all_gather x1, blocking collectives: 23.3 us -> 30.8 us  [body(): lax.all_gather(jnp.concatenate([expert_ids, gate_codes], 1), 'node', axis...]
  transfers between devices with their start and end apart: 8 -> 31, of which waited for: 8 -> 15; matrix products, arithmetic and copies ran while one was open for 13% -> 46% of each run, Pallas kernels for 0% -> 0%
where the time goes in v2:
time: 243 us; the launch traced here: 242 us
  matrix products  99.8 us (41%)
  waiting for transfers between devices  58.7 us (24%)
  blocking collectives  30.8 us (13%)
  starting transfers between devices  23.3 us (10%)
  local copies, waits for them, and re-layouts  17.8 us (7%)
  other arithmetic  11.4 us (5%)
    dot_general x10, matrix products, expert_part(): part = jnp.dot(hidden, down_w, preferred_element_type=jnp.float32)  66 us
    dot_general x10, matrix products, expert_part(): gate = jnp.dot(rows, gate_w, preferred_element_type=jnp.float32)  33.7 us
    all_gather x1, blocking collectives, body(): lax.all_gather(jnp.concatenate([expert_ids, gate_codes], 1), 'node', axis...  30.8 us
    ppermute x7, waiting for transfers between devices, body(): ahead[h].append(lax.ppermute(ahead[h][-1], 'node', forward))  26.3 us
    ppermute x7, waiting for transfers between devices, body(): behind[h].append(lax.ppermute(behind[h][-1], 'node', backward))  19.5 us
    ppermute x14, starting transfers between devices, body(): arrived = lax.ppermute(total, 'node', way)  14.2 us
    ppermute x14, waiting for transfers between devices, body(): arrived = lax.ppermute(total, 'node', way)  12.9 us
    convert_element_type x5, other arithmetic, add(): return sum((t.astype(jnp.float32) for t in terms)).astype(jnp.bfloat16)  11.3 us
  transfers between devices with their start and end apart: 31, of which 15 were waited for; matrix products, arithmetic and copies ran while one was open for 46% of the time, Pallas kernels for 0%

profile of v2, /device:TPU:0, one launch (start us, length us, event | category | flops | bytes accessed | tf_op | source)
XLA Modules:
  0.0 242.2 jit_solution(9748008246254910397)
XLA Ops:
  0.0 2.1 fusion.58
  2.1 3.0 %collective-permute-start.3 = (bf16[64,3584]{1,0:T(8,128)(2,1)}, bf16[64,3584]{1,0:T(8,128)(2,1)}, u32[]{:S(2)}, u32[]{:S(2)}) collective-permute-start(bf16[64,3584]{1,0:T(8,128)(2,1)} %get-tuple-element.22), channel_id=1, source_target_pairs={{0,4},{1,5},{4,8},{5,9},{8,12},{9,13},{12,14},{13,15},{14,10},{15,... | collective-permute-start | bytes 1376264 | tf_op jit(solution)/shard_map/ppermute | solution.py:38
  5.1 2.0 collective-permute-start.4
  7.2 3.0 %fusion.77 = f32[128,512]{1,0:T(8,128)S(1)} fusion(bf16[128,3584]{1,0:T(8,128)(2,1)} %param.6, bf16[3584,512]{1,0:T(8,128)(2,1)} %param.9), kind=kOutput, calls=%fused_computation.125 | convolution fusion | flops 469762048 | bytes 4849664 | tf_op jit(solution)/shard_map/dot_general | solution.py:59
  10.2 30.8 %all-gather = s32[2048,8]{0,1:T(8,128)S(1)} all-gather(s32[128,8]{0,1:T(8,128)S(1)} %pad_add_fusion), channel_id=2, replica_groups=mesh['groups'=2,'node'=16] {'node'}, dimensions={0}, use_global_device_ids=true | all-gather | bytes 69632 | tf_op jit(solution)/shard_map/all_gather | solution.py:45
  41.1 5.6 %fusion.7 = f32[128,3584]{1,0:T(8,128)} fusion(bf16[512,3584]{1,0:T(8,128)(2,1)} %param.11, bf16[128,3584]{1,0:T(8,128)(2,1)S(1)} %copy-done, bf16[3584,512]{1,0:T(8,128)(2,1)} %param.10, f32[128,512]{1,0:T(8,128)S(1)} %fusion.77, f32[128]{0:T(128)S(1)} %get-tuple-element.23), kind=kOutput, calls=%fused_computation.13 | convolution fusion | flops 939982848 | bytes 10355200 | tf_op jit(solution)/shard_map/dot_general | solution.py:62
  51.6 3.8 %fusion.79 = f32[256,512]{1,0:T(8,128)S(1)} fusion(bf16[256,3584]{1,0:T(8,128)(2,1)S(1)} %constant_dynamic-update-slice_fusion, bf16[3584,512]{1,0:T(8,128)(2,1)} %param.9), kind=kOutput, calls=%fused_computation.127 | convolution fusion | flops 939524096 | bytes 6029312 | tf_op jit(solution)/shard_map/dot_general | solution.py:59
  55.5 7.2 %fusion.8 = f32[256,3584]{1,0:T(8,128)} fusion(bf16[512,3584]{1,0:T(8,128)(2,1)} %param.11, f32[256,512]{1,0:T(8,128)S(1)} %fusion.79, f32[256]{0:T(256)S(1)} %pad_maximum_fusion.1, bf16[256,3584]{1,0:T(8,128)(2,1)S(1)} %constant_dynamic-update-slice_fusion, bf16[3584,512]{1,0:T(8,128)(2,1)} %param.10), kind=kOutput, calls=%fused_computation.33 | convolution fusion | flops 1879965696 | bytes 13370368 | tf_op jit(solution)/shard_map/dot_general | solution.py:62
  62.8 6.4 %collective-permute-done.7 = bf16[64,3584]{1,0:T(8,128)(2,1)} collective-permute-done((bf16[64,3584]{1,0:T(8,128)(2,1)}, bf16[64,3584]{1,0:T(8,128)(2,1)}, u32[]{:S(2)}, u32[]{:S(2)}) %collective-permute-start.7) | collective-permute-done | bytes 458784 | tf_op jit(solution)/shard_map/ppermute | solution.py:38
  70.5 7.9 %collective-permute-done.8 = bf16[64,3584]{1,0:T(8,128)(2,1)} collective-permute-done((bf16[64,3584]{1,0:T(8,128)(2,1)}, bf16[64,3584]{1,0:T(8,128)(2,1)}, u32[]{:S(2)}, u32[]{:S(2)}) %collective-permute-start.8) | collective-permute-done | bytes 458784 | tf_op jit(solution)/shard_map/ppermute | solution.py:38
  80.7 9.8 %collective-permute-done.10 = bf16[64,3584]{1,0:T(8,128)(2,1)S(1)} collective-permute-done((bf16[64,3584]{1,0:T(8,128)(2,1)}, bf16[64,3584]{1,0:T(8,128)(2,1)S(1)}, u32[]{:S(2)}, u32[]{:S(2)}) %collective-permute-start.10) | collective-permute-done | bytes 458784 | tf_op jit(solution)/shard_map/ppermute | solution.py:40
  91.3 3.8 %fusion.81 = f32[256,512]{1,0:T(8,128)S(1)} fusion(bf16[256,3584]{1,0:T(8,128)(2,1)S(1)} %constant_dynamic-update-slice_fusion.4, bf16[3584,512]{1,0:T(8,128)(2,1)} %param.9), kind=kOutput, calls=%fused_computation.129 | convolution fusion | flops 939524096 | bytes 6029312 | tf_op jit(solution)/shard_map/dot_general | solution.py:59
  95.9 7.1 %fusion.9 = f32[256,3584]{1,0:T(8,128)} fusion(bf16[512,3584]{1,0:T(8,128)(2,1)} %param.11, f32[256,512]{1,0:T(8,128)S(1)} %fusion.81, f32[256]{0:T(256)S(1)} %pad_maximum_fusion.2, bf16[256,3584]{1,0:T(8,128)(2,1)S(1)} %constant_dynamic-update-slice_fusion.4, bf16[3584,512]{1,0:T(8,128)(2,1)} %param.10), kind=kOutput, calls=%fused_computation.34 | convolution fusion | flops 1879965696 | bytes 13370368 | tf_op jit(solution)/shard_map/dot_general | solution.py:62
  103.0 5.9 %collective-permute-done.11 = bf16[64,3584]{1,0:T(8,128)(2,1)} collective-permute-done((bf16[64,3584]{1,0:T(8,128)(2,1)}, bf16[64,3584]{1,0:T(8,128)(2,1)}, u32[]{:S(2)}, u32[]{:S(2)}) %collective-permute-start.11) | collective-permute-done | bytes 458784 | tf_op jit(solution)/shard_map/ppermute | solution.py:38
  110.3 6.1 %collective-permute-done.12 = bf16[64,3584]{1,0:T(8,128)(2,1)} collective-permute-done((bf16[64,3584]{1,0:T(8,128)(2,1)}, bf16[64,3584]{1,0:T(8,128)(2,1)}, u32[]{:S(2)}, u32[]{:S(2)}) %collective-permute-start.12) | collective-permute-done | bytes 458784 | tf_op jit(solution)/shard_map/ppermute | solution.py:38
  118.4 1.2 collective-permute-start.15
  119.5 8.1 %collective-permute-done.14 = bf16[64,3584]{1,0:T(8,128)(2,1)} collective-permute-done((bf16[64,3584]{1,0:T(8,128)(2,1)}, bf16[64,3584]{1,0:T(8,128)(2,1)}, u32[]{:S(2)}, u32[]{:S(2)}) %collective-permute-start.14) | collective-permute-done | bytes 458784 | tf_op jit(solution)/shard_map/ppermute | solution.py:40
  127.9 1.1 constant_dynamic-update-slice_fusion.8
  129.0 3.8 %fusion.83 = f32[256,512]{1,0:T(8,128)S(1)} fusion(bf16[256,3584]{1,0:T(8,128)(2,1)S(1)} %constant_dynamic-update-slice_fusion.8, bf16[3584,512]{1,0:T(8,128)(2,1)} %param.9), kind=kOutput, calls=%fused_computation.131 | convolution fusion | flops 939524096 | bytes 6029312 | tf_op jit(solution)/shard_map/dot_general | solution.py:59
  132.9 7.2 %fusion.10 = f32[256,3584]{1,0:T(8,128)} fusion(bf16[512,3584]{1,0:T(8,128)(2,1)} %param.11, f32[256,512]{1,0:T(8,128)S(1)} %fusion.83, f32[256]{0:T(256)S(1)} %pad_maximum_fusion.3, bf16[256,3584]{1,0:T(8,128)(2,1)S(1)} %constant_dynamic-update-slice_fusion.8, bf16[3584,512]{1,0:T(8,128)(2,1)} %param.10), kind=kOutput, calls=%fused_computation.35 | convolution fusion | flops 1879965696 | bytes 13370368 | tf_op jit(solution)/shard_map/dot_general | solution.py:62
  142.2 2.7 %fusion.85 = f32[128,512]{1,0:T(8,128)S(1)} fusion(bf16[128,3584]{1,0:T(8,128)(2,1)S(1)} %constant_dynamic-update-slice_fusion.12, bf16[3584,512]{1,0:T(8,128)(2,1)} %param.9), kind=kOutput, calls=%fused_computation.133 | convolution fusion | flops 469762048 | bytes 4849664 | tf_op jit(solution)/shard_map/dot_general | solution.py:59
  144.9 5.6 %fusion.28 = f32[128,3584]{1,0:T(8,128)} fusion(bf16[512,3584]{1,0:T(8,128)(2,1)} %param.11, f32[128,512]{1,0:T(8,128)S(1)} %fusion.85, f32[128]{0:T(128)S(1)} %get-tuple-element.24, bf16[128,3584]{1,0:T(8,128)(2,1)S(1)} %constant_dynamic-update-slice_fusion.12, bf16[3584,512]{1,0:T(8,128)(2,1)} %param.10), kind=kOutput, calls=%fused_computation.56 | convolution fusion | flops 939982848 | bytes 10355200 | tf_op jit(solution)/shard_map/dot_general | solution.py:62
  150.5 2.7 %fusion.86 = f32[128,512]{1,0:T(8,128)S(1)} fusion(bf16[128,3584]{1,0:T(8,128)(2,1)S(1)} %constant_dynamic-update-slice_fusion.12, bf16[3584,512]{1,0:T(8,128)(2,1)} %collective-permute-done), kind=kOutput, calls=%fused_computation.134 | convolution fusion | flops 469762048 | bytes 4849664 | tf_op jit(solution)/shard_map/dot_general | solution.py:59
  153.2 4.9 %fusion.4 = bf16[128,3584]{1,0:T(8,128)(2,1)S(1)} fusion(f32[128,3584]{1,0:T(8,128)} %fusion.28, bf16[512,3584]{1,0:T(8,128)(2,1)} %collective-permute-done.2, f32[128,512]{1,0:T(8,128)S(1)} %fusion.86, f32[128]{0:T(128)S(1)} %get-tuple-element.24, bf16[128,3584]{1,0:T(8,128)(2,1)S(1)} %constant_dynamic-update-slice_fusion.12, ...), kind=kOutput, calls=%fused_computation.9 | convolution fusion | flops 940900352 | bytes 11272704 | tf_op jit(solution)/shard_map/dot_general | solution.py:62
  159.1 1.7 collective-permute-start.17
  161.2 3.7 %fusion.84 = f32[256,512]{1,0:T(8,128)S(1)} fusion(bf16[256,3584]{1,0:T(8,128)(2,1)} %copy-done.1, bf16[3584,512]{1,0:T(8,128)(2,1)} %collective-permute-done), kind=kOutput, calls=%fused_computation.132 | convolution fusion | flops 939524096 | bytes 6029312 | tf_op jit(solution)/shard_map/dot_general | solution.py:59
  164.9 7.7 %fusion.2 = bf16[256,3584]{1,0:T(8,128)(2,1)} fusion(f32[256,3584]{1,0:T(8,128)} %fusion.10, bf16[512,3584]{1,0:T(8,128)(2,1)} %collective-permute-done.2, f32[256,512]{1,0:T(8,128)S(1)} %fusion.84, f32[256]{0:T(256)S(1)} %pad_maximum_fusion.3, bf16[256,3584]{1,0:T(8,128)(2,1)S(1)} %copy-done.2, bf16[3584,512]{1,0:T(8,128)(2,1)} %collective-permute-done.1), kind=kOutput, calls=%fused_computation.5 | convolution fusion | flops 1881800704 | bytes 15205376 | tf_op jit(solution)/shard_map/dot_general | solution.py:62
  172.6 2.1 fusion.56
  175.0 1.7 collective-permute-start.24
  176.8 3.7 %fusion.82 = f32[256,512]{1,0:T(8,128)S(1)} fusion(bf16[256,3584]{1,0:T(8,128)(2,1)} %copy-done.3, bf16[3584,512]{1,0:T(8,128)(2,1)} %collective-permute-done), kind=kOutput, calls=%fused_computation.130 | convolution fusion | flops 939524096 | bytes 6029312 | tf_op jit(solution)/shard_map/dot_general | solution.py:59
  180.5 2.3 add_convert_fusion.11
  182.8 1.7 collective-permute-start.18
  184.8 7.6 %fusion.1 = bf16[256,3584]{1,0:T(8,128)(2,1)} fusion(f32[256,3584]{1,0:T(8,128)} %fusion.9, bf16[512,3584]{1,0:T(8,128)(2,1)} %collective-permute-done.2, f32[256,512]{1,0:T(8,128)S(1)} %fusion.82, f32[256]{0:T(256)S(1)} %pad_maximum_fusion.2, bf16[256,3584]{1,0:T(8,128)(2,1)S(1)} %copy-done.4, bf16[3584,512]{1,0:T(8,128)(2,1)} %collective-permute-done.1), kind=kOutput, calls=%fused_computation.4 | convolution fusion | flops 1881800704 | bytes 15205376 | tf_op jit(solution)/shard_map/dot_general | solution.py:62
  192.4 3.8 %fusion.80 = f32[256,512]{1,0:T(8,128)S(1)} fusion(bf16[256,3584]{1,0:T(8,128)(2,1)} %copy-done.5, bf16[3584,512]{1,0:T(8,128)(2,1)} %collective-permute-done), kind=kOutput, calls=%fused_computation.128 | convolution fusion | flops 939524096 | bytes 6029312 | tf_op jit(solution)/shard_map/dot_general | solution.py:59
  196.3 3.2 %add_convert_fusion.10 = (bf16[64,3584]{1,0:T(8,128)(2,1)}, bf16[64,3584]{1,0:T(8,128)(2,1)}, bf16[64,3584]{1,0:T(8,128)(2,1)}, bf16[64,3584]{1,0:T(8,128)(2,1)}) fusion(bf16[64,3584]{1,0:T(8,128)(2,1)} %collective-permute-done.18, bf16[256,3584]{1,0:T(8,128)(2,1)S(1)} %copy-done.10, bf16[64,3584]{1,0:T(8,128)(2,1)} %collective-permute-done.28, ...), kind=kLoop, calls=%fused_computation.25 | loop fusion | flops 3670016 | bytes 5505024 | tf_op jit(solution)/shard_map/convert_element_type | solution.py:90
  199.5 1.7 collective-permute-start.19
  201.5 1.7 collective-permute-start.25
  203.5 7.6 %fusion = bf16[256,3584]{1,0:T(8,128)(2,1)} fusion(f32[256,3584]{1,0:T(8,128)} %fusion.8, bf16[512,3584]{1,0:T(8,128)(2,1)} %collective-permute-done.2, f32[256,512]{1,0:T(8,128)S(1)} %fusion.80, f32[256]{0:T(256)S(1)} %pad_maximum_fusion.1, bf16[256,3584]{1,0:T(8,128)(2,1)S(1)} %copy-done.6, bf16[3584,512]{1,0:T(8,128)(2,1)} %collective-permute-done.1), kind=kOutput, calls=%fused_computation.3 | convolution fusion | flops 1881800704 | bytes 15205376 | tf_op jit(solution)/shard_map/dot_general | solution.py:62
  211.1 2.8 %fusion.78 = f32[128,512]{1,0:T(8,128)S(1)} fusion(bf16[128,3584]{1,0:T(8,128)(2,1)S(1)} %copy-done, bf16[3584,512]{1,0:T(8,128)(2,1)} %collective-permute-done), kind=kOutput, calls=%fused_computation.126 | convolution fusion | flops 469762048 | bytes 4849664 | tf_op jit(solution)/shard_map/dot_general | solution.py:59
  214.2 3.5 %collective-permute-done.25 = bf16[64,3584]{1,0:T(8,128)(2,1)} collective-permute-done((bf16[64,3584]{1,0:T(8,128)(2,1)}, bf16[64,3584]{1,0:T(8,128)(2,1)}, u32[]{:S(2)}, u32[]{:S(2)}) %collective-permute-start.25) | collective-permute-done | bytes 458784 | tf_op jit(solution)/shard_map/ppermute | solution.py:99
  217.7 1.4 collective-permute-done.29
  219.1 3.0 %add_convert_fusion.9 = (bf16[64,3584]{1,0:T(8,128)(2,1)}, bf16[64,3584]{1,0:T(8,128)(2,1)}, bf16[64,3584]{1,0:T(8,128)(2,1)}, bf16[64,3584]{1,0:T(8,128)(2,1)}) fusion(bf16[64,3584]{1,0:T(8,128)(2,1)} %collective-permute-done.19, bf16[256,3584]{1,0:T(8,128)(2,1)S(1)} %copy-done.9, bf16[64,3584]{1,0:T(8,128)(2,1)} %collective-permute-done.29, ...), kind=kLoop, calls=%fused_computation.24 | loop fusion | flops 3670016 | bytes 5505024 | tf_op jit(solution)/shard_map/convert_element_type | solution.py:90
  222.5 1.6 collective-permute-start.23
  224.6 1.6 collective-permute-start.30
  226.2 5.4 %fusion.3 = bf16[128,3584]{1,0:T(8,128)(2,1)} fusion(f32[128,3584]{1,0:T(8,128)S(1)} %copy-done.8, bf16[512,3584]{1,0:T(8,128)(2,1)} %collective-permute-done.2, f32[128,512]{1,0:T(8,128)S(1)} %fusion.78, f32[128]{0:T(128)S(1)} %get-tuple-element.23, bf16[128,3584]{1,0:T(8,128)(2,1)S(1)} %copy-done, bf16[3584,512]{1,0:T(8,128)(2,1)} %collective-permute-done.1), kind=kOutput, calls=%fused_computation.8 | convolution fusion | flops 940900352 | bytes 11272704 | tf_op jit(solution)/shard_map/dot_general | solution.py:62
  231.6 2.5 %collective-permute-done.20 = bf16[64,3584]{1,0:T(8,128)(2,1)S(1)} collective-permute-done((bf16[64,3584]{1,0:T(8,128)(2,1)}, bf16[64,3584]{1,0:T(8,128)(2,1)S(1)}, u32[]{:S(2)}, u32[]{:S(2)}) %collective-permute-start.20) | collective-permute-done | bytes 458784 | tf_op jit(solution)/shard_map/ppermute | solution.py:99
  234.4 4.6 %collective-permute-done.26 = bf16[64,3584]{1,0:T(8,128)(2,1)} collective-permute-done((bf16[64,3584]{1,0:T(8,128)(2,1)}, bf16[64,3584]{1,0:T(8,128)(2,1)}, u32[]{:S(2)}, u32[]{:S(2)}) %collective-permute-start.26) | collective-permute-done | bytes 458784 | tf_op jit(solution)/shard_map/ppermute | solution.py:99
  239.3 2.8 %add_convert_fusion.6 = (bf16[128,3584]{1,0:T(8,128)(2,1)}, bf16[128,3584]{1,0:T(8,128)(2,1)}) fusion(bf16[64,3584]{1,0:T(8,128)(2,1)} %collective-permute-done.23, bf16[64,3584]{1,0:T(8,128)(2,1)S(1)} %collective-permute-done.20, bf16[128,3584]{1,0:T(8,128)(2,1)} %fusion.3, ...), kind=kLoop, output_to_operand_aliasing={{0}: (5, {}), {1}: (5, {})}, calls=%fused_computation.21 | loop fusion | flops 2752512 | bytes 3670016 | tf_op jit(solution)/shard_map/convert_element_type | solution.py:90
  (94 shorter events, 20.2 us)
Async XLA Ops:
  0.0 41.1 %copy-start = (bf16[128,3584]{1,0:T(8,128)(2,1)S(1)}, bf16[128,3584]{1,0:T(8,128)(2,1)}, u32[]{:S(2)}) copy-start(bf16[128,3584]{1,0:T(8,128)(2,1)} %param.6) | copy-start | bytes 2752516
  0.0 10.1 %copy-start.14 = (s32[128,4]{0,1:T(4,128)S(1)}, s32[128,4]{0,1:T(4,128)}, u32[]{:S(2)}) copy-start(s32[128,4]{0,1:T(4,128)} %param.7) | copy-start | bytes 6148
  0.0 10.1 %copy-start.13 = (s32[128,4]{0,1:T(4,128)S(1)}, s32[128,4]{0,1:T(4,128)}, u32[]{:S(2)}) copy-start(s32[128,4]{0,1:T(4,128)} %param.8) | copy-start | bytes 6148
  2.1 44.7 %collective-permute-start.3 = (bf16[64,3584]{1,0:T(8,128)(2,1)}, bf16[64,3584]{1,0:T(8,128)(2,1)}, u32[]{:S(2)}, u32[]{:S(2)}) collective-permute-start(bf16[64,3584]{1,0:T(8,128)(2,1)} %get-tuple-element.22), channel_id=1, source_target_pairs={{0,4},{1,5},{4,8},{5,9},{8,12},{9,13},{12,14},{13,15},{14,10},{15,... | collective-permute-start | bytes 1376264 | tf_op jit(solution)/shard_map/ppermute | solution.py:38
  5.1 44.3 %collective-permute-start.5 = (bf16[64,3584]{1,0:T(8,128)(2,1)}, bf16[64,3584]{1,0:T(8,128)(2,1)}, u32[]{:S(2)}, u32[]{:S(2)}) collective-permute-start(bf16[64,3584]{1,0:T(8,128)(2,1)} %get-tuple-element.22), channel_id=1, source_target_pairs={{0,2},{1,3},{4,0},{5,1},{8,4},{9,5},{12,8},{13,9},{14,12},{15,13},... | collective-permute-start | bytes 1376264 | tf_op jit(solution)/shard_map/ppermute | solution.py:40
  5.1 43.0 %collective-permute-start.4 = (bf16[64,3584]{1,0:T(8,128)(2,1)S(1)}, bf16[64,3584]{1,0:T(8,128)(2,1)}, u32[]{:S(2)}, u32[]{:S(2)}) collective-permute-start(bf16[64,3584]{1,0:T(8,128)(2,1)S(1)} %get-tuple-element.21), channel_id=1, source_target_pairs={{0,4},{1,5},{4,8},{5,9},{8,12},{9,13},{12,14},{13,15},{14,10},{15,... | collective-permute-start | bytes 1376264 | tf_op jit(solution)/shard_map/ppermute | solution.py:38
  7.1 43.4 %collective-permute-start.6 = (bf16[64,3584]{1,0:T(8,128)(2,1)S(1)}, bf16[64,3584]{1,0:T(8,128)(2,1)}, u32[]{:S(2)}, u32[]{:S(2)}) collective-permute-start(bf16[64,3584]{1,0:T(8,128)(2,1)S(1)} %get-tuple-element.21), channel_id=1, source_target_pairs={{0,2},{1,3},{4,0},{5,1},{8,4},{9,5},{12,8},{13,9},{14,12},{15,13},... | collective-permute-start | bytes 1376264 | tf_op jit(solution)/shard_map/ppermute | solution.py:40
  7.1 143.4 %collective-permute-start = (bf16[3584,512]{1,0:T(8,128)(2,1)}, bf16[3584,512]{1,0:T(8,128)(2,1)}, u32[]{:S(2)}, u32[]{:S(2)}) collective-permute-start(bf16[3584,512]{1,0:T(8,128)(2,1)} %param.9), channel_id=1, source_target_pairs={{0,1},{1,0},{2,3},{3,2},{4,5},{5,4},{6,7},{7,6},{8,9},{9,8},{10,11... | collective-permute-start | bytes 11010056 | tf_op jit(solution)/shard_map/ppermute | solution.py:42
  46.8 106.4 %collective-permute-start.1 = (bf16[3584,512]{1,0:T(8,128)(2,1)}, bf16[3584,512]{1,0:T(8,128)(2,1)}, u32[]{:S(2)}, u32[]{:S(2)}) collective-permute-start(bf16[3584,512]{1,0:T(8,128)(2,1)} %param.10), channel_id=1, source_target_pairs={{0,1},{1,0},{2,3},{3,2},{4,5},{5,4},{6,7},{7,6},{8,9},{9,8},{10,11... | collective-permute-start | bytes 11010056 | tf_op jit(solution)/shard_map/ppermute | solution.py:42
  48.2 105.0 %collective-permute-start.2 = (bf16[512,3584]{1,0:T(8,128)(2,1)}, bf16[512,3584]{1,0:T(8,128)(2,1)}, u32[]{:S(2)}, u32[]{:S(2)}) collective-permute-start(bf16[512,3584]{1,0:T(8,128)(2,1)} %param.11), channel_id=1, source_target_pairs={{0,1},{1,0},{2,3},{3,2},{4,5},{5,4},{6,7},{7,6},{8,9},{9,8},{10,11... | collective-permute-start | bytes 11010056 | tf_op jit(solution)/shard_map/ppermute | solution.py:42
  51.6 11.2 %copy-start.5 = (bf16[256,3584]{1,0:T(8,128)(2,1)}, bf16[256,3584]{1,0:T(8,128)(2,1)S(1)}, u32[]{:S(2)}) copy-start(bf16[256,3584]{1,0:T(8,128)(2,1)S(1)} %constant_dynamic-update-slice_fusion) | copy-start | bytes 5505028
  55.4 13.7 %collective-permute-start.7 = (bf16[64,3584]{1,0:T(8,128)(2,1)}, bf16[64,3584]{1,0:T(8,128)(2,1)}, u32[]{:S(2)}, u32[]{:S(2)}) collective-permute-start(bf16[64,3584]{1,0:T(8,128)(2,1)} %collective-permute-done.3), channel_id=1, source_target_pairs={{0,4},{1,5},{4,8},{5,9},{8,12},{9,13},{12,14},{13,15},{14,10},{15,... | collective-permute-start | bytes 1376264 | tf_op jit(solution)/shard_map/ppermute | solution.py:38
  55.5 22.9 %collective-permute-start.8 = (bf16[64,3584]{1,0:T(8,128)(2,1)}, bf16[64,3584]{1,0:T(8,128)(2,1)}, u32[]{:S(2)}, u32[]{:S(2)}) collective-permute-start(bf16[64,3584]{1,0:T(8,128)(2,1)} %collective-permute-done.4), channel_id=1, source_target_pairs={{0,4},{1,5},{4,8},{5,9},{8,12},{9,13},{12,14},{13,15},{14,10},{15,... | collective-permute-start | bytes 1376264 | tf_op jit(solution)/shard_map/ppermute | solution.py:38
  69.1 11.6 %collective-permute-start.9 = (bf16[64,3584]{1,0:T(8,128)(2,1)}, bf16[64,3584]{1,0:T(8,128)(2,1)S(1)}, u32[]{:S(2)}, u32[]{:S(2)}) collective-permute-start(bf16[64,3584]{1,0:T(8,128)(2,1)} %collective-permute-done.5), channel_id=1, source_target_pairs={{0,2},{1,3},{4,0},{5,1},{8,4},{9,5},{12,8},{13,9},{14,12},{15,13},... | collective-permute-start | bytes 1376264 | tf_op jit(solution)/shard_map/ppermute | solution.py:40
  78.4 12.2 %collective-permute-start.10 = (bf16[64,3584]{1,0:T(8,128)(2,1)}, bf16[64,3584]{1,0:T(8,128)(2,1)S(1)}, u32[]{:S(2)}, u32[]{:S(2)}) collective-permute-start(bf16[64,3584]{1,0:T(8,128)(2,1)} %collective-permute-done.6), channel_id=1, source_target_pairs={{0,2},{1,3},{4,0},{5,1},{8,4},{9,5},{12,8},{13,9},{14,12},{15,13},... | collective-permute-start | bytes 1376264 | tf_op jit(solution)/shard_map/ppermute | solution.py:40
  80.7 9.8 %copy-start.11 = (bf16[64,3584]{1,0:T(8,128)(2,1)}, bf16[64,3584]{1,0:T(8,128)(2,1)S(1)}, u32[]{:S(2)}) copy-start(bf16[64,3584]{1,0:T(8,128)(2,1)S(1)} %collective-permute-done.9) | copy-start | bytes 1376260
  90.5 0.8 copy-start.12
  91.3 11.7 %copy-start.3 = (bf16[256,3584]{1,0:T(8,128)(2,1)}, bf16[256,3584]{1,0:T(8,128)(2,1)S(1)}, u32[]{:S(2)}) copy-start(bf16[256,3584]{1,0:T(8,128)(2,1)S(1)} %constant_dynamic-update-slice_fusion.4) | copy-start | bytes 5505028
  95.2 13.8 %collective-permute-start.11 = (bf16[64,3584]{1,0:T(8,128)(2,1)}, bf16[64,3584]{1,0:T(8,128)(2,1)}, u32[]{:S(2)}, u32[]{:S(2)}) collective-permute-start(bf16[64,3584]{1,0:T(8,128)(2,1)} %collective-permute-done.7), channel_id=1, source_target_pairs={{0,4},{1,5},{4,8},{5,9},{8,12},{9,13},{12,14},{13,15},{14,10},{15,... | collective-permute-start | bytes 1376264 | tf_op jit(solution)/shard_map/ppermute | solution.py:38
  95.8 20.6 %collective-permute-start.12 = (bf16[64,3584]{1,0:T(8,128)(2,1)}, bf16[64,3584]{1,0:T(8,128)(2,1)}, u32[]{:S(2)}, u32[]{:S(2)}) collective-permute-start(bf16[64,3584]{1,0:T(8,128)(2,1)} %collective-permute-done.8), channel_id=1, source_target_pairs={{0,4},{1,5},{4,8},{5,9},{8,12},{9,13},{12,14},{13,15},{14,10},{15,... | collective-permute-start | bytes 1376264 | tf_op jit(solution)/shard_map/ppermute | solution.py:38
  109.0 9.4 %collective-permute-start.13 = (bf16[64,3584]{1,0:T(8,128)(2,1)}, bf16[64,3584]{1,0:T(8,128)(2,1)S(1)}, u32[]{:S(2)}, u32[]{:S(2)}) collective-permute-start(bf16[64,3584]{1,0:T(8,128)(2,1)} %copy-done.11), channel_id=1, source_target_pairs={{0,2},{1,3},{4,0},{5,1},{8,4},{9,5},{12,8},{13,9},{14,12},{15,13},... | collective-permute-start | bytes 1376264 | tf_op jit(solution)/shard_map/ppermute | solution.py:40
  116.4 11.2 %collective-permute-start.14 = (bf16[64,3584]{1,0:T(8,128)(2,1)}, bf16[64,3584]{1,0:T(8,128)(2,1)}, u32[]{:S(2)}, u32[]{:S(2)}) collective-permute-start(bf16[64,3584]{1,0:T(8,128)(2,1)} %copy-done.12), channel_id=1, source_target_pairs={{0,2},{1,3},{4,0},{5,1},{8,4},{9,5},{12,8},{13,9},{14,12},{15,13},... | collective-permute-start | bytes 1376264 | tf_op jit(solution)/shard_map/ppermute | solution.py:40
  118.4 21.7 %collective-permute-start.15 = (bf16[64,3584]{1,0:T(8,128)(2,1)}, bf16[64,3584]{1,0:T(8,128)(2,1)}, u32[]{:S(2)}, u32[]{:S(2)}) collective-permute-start(bf16[64,3584]{1,0:T(8,128)(2,1)} %collective-permute-done.11), channel_id=1, source_target_pairs={{0,4},{1,5},{4,8},{5,9},{8,12},{9,13},{12,14},{13,15},{14,10},{15,... | collective-permute-start | bytes 1376264 | tf_op jit(solution)/shard_map/ppermute | solution.py:38
  127.6 13.5 %collective-permute-start.16 = (bf16[64,3584]{1,0:T(8,128)(2,1)}, bf16[64,3584]{1,0:T(8,128)(2,1)}, u32[]{:S(2)}, u32[]{:S(2)}) collective-permute-start(bf16[64,3584]{1,0:T(8,128)(2,1)} %collective-permute-done.14), channel_id=1, source_target_pairs={{0,2},{1,3},{4,0},{5,1},{8,4},{9,5},{12,8},{13,9},{14,12},{15,13},... | collective-permute-start | bytes 1376264 | tf_op jit(solution)/shard_map/ppermute | solution.py:40
  129.0 11.0 %copy-start.1 = (bf16[256,3584]{1,0:T(8,128)(2,1)}, bf16[256,3584]{1,0:T(8,128)(2,1)S(1)}, u32[]{:S(2)}) copy-start(bf16[256,3584]{1,0:T(8,128)(2,1)S(1)} %constant_dynamic-update-slice_fusion.8) | copy-start | bytes 5505028
  159.1 5.7 %copy-start.2 = (bf16[256,3584]{1,0:T(8,128)(2,1)S(1)}, bf16[256,3584]{1,0:T(8,128)(2,1)}, u32[]{:S(2)}) copy-start(bf16[256,3584]{1,0:T(8,128)(2,1)} %copy-done.1) | copy-start | bytes 5505028
  159.1 21.3 %collective-permute-start.17 = (bf16[64,3584]{1,0:T(8,128)(2,1)}, bf16[64,3584]{1,0:T(8,128)(2,1)}, u32[]{:S(2)}, u32[]{:S(2)}) collective-permute-start(bf16[64,3584]{1,0:T(8,128)(2,1)} %get-tuple-element.19), channel_id=1, source_target_pairs={{0,4},{1,5},{4,8},{5,9},{8,12},{9,13},{12,14},{13,15},{14,10},{15,... | collective-permute-start | bytes 1376264 | tf_op jit(solution)/shard_map/ppermute | solution.py:99
  160.9 19.6 %collective-permute-start.27 = (bf16[64,3584]{1,0:T(8,128)(2,1)}, bf16[64,3584]{1,0:T(8,128)(2,1)}, u32[]{:S(2)}, u32[]{:S(2)}) collective-permute-start(bf16[64,3584]{1,0:T(8,128)(2,1)} %get-tuple-element.20), channel_id=1, source_target_pairs={{0,2},{1,3},{4,0},{5,1},{8,4},{9,5},{12,8},{13,9},{14,12},{15,13},... | collective-permute-start | bytes 1376264 | tf_op jit(solution)/shard_map/ppermute | solution.py:99
  174.7 5.8 %copy-start.7 = (bf16[256,3584]{1,0:T(8,128)(2,1)S(1)}, bf16[256,3584]{1,0:T(8,128)(2,1)}, u32[]{:S(2)}) copy-start(bf16[256,3584]{1,0:T(8,128)(2,1)} %fusion.2) | copy-start | bytes 5505028
  174.7 21.5 %collective-permute-start.21 = (bf16[64,3584]{1,0:T(8,128)(2,1)}, bf16[64,3584]{1,0:T(8,128)(2,1)}, u32[]{:S(2)}, u32[]{:S(2)}) collective-permute-start(bf16[64,3584]{1,0:T(8,128)(2,1)} %get-tuple-element.15), channel_id=1, source_target_pairs={{0,2},{1,3},{4,0},{5,1},{8,4},{9,5},{12,8},{13,9},{14,12},{15,13},... | collective-permute-start | bytes 1376264 | tf_op jit(solution)/shard_map/ppermute | solution.py:99
  175.0 9.8 %copy-start.4 = (bf16[256,3584]{1,0:T(8,128)(2,1)S(1)}, bf16[256,3584]{1,0:T(8,128)(2,1)}, u32[]{:S(2)}) copy-start(bf16[256,3584]{1,0:T(8,128)(2,1)} %copy-done.3) | copy-start | bytes 5505028
  175.0 21.3 %collective-permute-start.24 = (bf16[64,3584]{1,0:T(8,128)(2,1)}, bf16[64,3584]{1,0:T(8,128)(2,1)}, u32[]{:S(2)}, u32[]{:S(2)}) collective-permute-start(bf16[64,3584]{1,0:T(8,128)(2,1)} %get-tuple-element.16), channel_id=1, source_target_pairs={{0,4},{1,5},{4,8},{5,9},{8,12},{9,13},{12,14},{13,15},{14,10},{15,... | collective-permute-start | bytes 1376264 | tf_op jit(solution)/shard_map/ppermute | solution.py:99
  182.8 13.5 %collective-permute-start.18 = (bf16[64,3584]{1,0:T(8,128)(2,1)}, bf16[64,3584]{1,0:T(8,128)(2,1)}, u32[]{:S(2)}, u32[]{:S(2)}) collective-permute-start(bf16[64,3584]{1,0:T(8,128)(2,1)} %get-tuple-element.13), channel_id=1, source_target_pairs={{0,4},{1,5},{4,8},{5,9},{8,12},{9,13},{12,14},{13,15},{14,10},{15,... | collective-permute-start | bytes 1376264 | tf_op jit(solution)/shard_map/ppermute | solution.py:99
  184.5 11.8 %collective-permute-start.28 = (bf16[64,3584]{1,0:T(8,128)(2,1)}, bf16[64,3584]{1,0:T(8,128)(2,1)}, u32[]{:S(2)}, u32[]{:S(2)}) collective-permute-start(bf16[64,3584]{1,0:T(8,128)(2,1)} %get-tuple-element.14), channel_id=1, source_target_pairs={{0,2},{1,3},{4,0},{5,1},{8,4},{9,5},{12,8},{13,9},{14,12},{15,13},... | collective-permute-start | bytes 1376264 | tf_op jit(solution)/shard_map/ppermute | solution.py:99
  192.4 3.9 %copy-start.10 = (bf16[256,3584]{1,0:T(8,128)(2,1)S(1)}, bf16[256,3584]{1,0:T(8,128)(2,1)}, u32[]{:S(2)}) copy-start(bf16[256,3584]{1,0:T(8,128)(2,1)} %fusion.1) | copy-start | bytes 5505028
  196.3 7.3 %copy-start.6 = (bf16[256,3584]{1,0:T(8,128)(2,1)S(1)}, bf16[256,3584]{1,0:T(8,128)(2,1)}, u32[]{:S(2)}) copy-start(bf16[256,3584]{1,0:T(8,128)(2,1)} %copy-done.5) | copy-start | bytes 5505028
  199.5 14.5 %collective-permute-start.19 = (bf16[64,3584]{1,0:T(8,128)(2,1)}, bf16[64,3584]{1,0:T(8,128)(2,1)}, u32[]{:S(2)}, u32[]{:S(2)}) collective-permute-start(bf16[64,3584]{1,0:T(8,128)(2,1)} %get-tuple-element.9), channel_id=1, source_target_pairs={{0,4},{1,5},{4,8},{5,9},{8,12},{9,13},{12,14},{13,15},{14,10},{15,... | collective-permute-start | bytes 1376264 | tf_op jit(solution)/shard_map/ppermute | solution.py:99
  201.2 12.9 %collective-permute-start.22 = (bf16[64,3584]{1,0:T(8,128)(2,1)}, bf16[64,3584]{1,0:T(8,128)(2,1)}, u32[]{:S(2)}, u32[]{:S(2)}) collective-permute-start(bf16[64,3584]{1,0:T(8,128)(2,1)} %get-tuple-element.12), channel_id=1, source_target_pairs={{0,2},{1,3},{4,0},{5,1},{8,4},{9,5},{12,8},{13,9},{14,12},{15,13},... | collective-permute-start | bytes 1376264 | tf_op jit(solution)/shard_map/ppermute | solution.py:99
  201.5 16.2 %collective-permute-start.25 = (bf16[64,3584]{1,0:T(8,128)(2,1)}, bf16[64,3584]{1,0:T(8,128)(2,1)}, u32[]{:S(2)}, u32[]{:S(2)}) collective-permute-start(bf16[64,3584]{1,0:T(8,128)(2,1)} %get-tuple-element.11), channel_id=1, source_target_pairs={{0,4},{1,5},{4,8},{5,9},{8,12},{9,13},{12,14},{13,15},{14,10},{15,... | collective-permute-start | bytes 1376264 | tf_op jit(solution)/shard_map/ppermute | solution.py:99
  203.2 15.8 %collective-permute-start.29 = (bf16[64,3584]{1,0:T(8,128)(2,1)}, bf16[64,3584]{1,0:T(8,128)(2,1)}, u32[]{:S(2)}, u32[]{:S(2)}) collective-permute-start(bf16[64,3584]{1,0:T(8,128)(2,1)} %get-tuple-element.10), channel_id=1, source_target_pairs={{0,2},{1,3},{4,0},{5,1},{8,4},{9,5},{12,8},{13,9},{14,12},{15,13},... | collective-permute-start | bytes 1376264 | tf_op jit(solution)/shard_map/ppermute | solution.py:99
  211.1 8.0 %copy-start.9 = (bf16[256,3584]{1,0:T(8,128)(2,1)S(1)}, bf16[256,3584]{1,0:T(8,128)(2,1)}, u32[]{:S(2)}) copy-start(bf16[256,3584]{1,0:T(8,128)(2,1)} %fusion) | copy-start | bytes 5505028
  213.9 12.2 %copy-start.8 = (f32[128,3584]{1,0:T(8,128)S(1)}, f32[128,3584]{1,0:T(8,128)}, u32[]{:S(2)}) copy-start(f32[128,3584]{1,0:T(8,128)} %fusion.7) | copy-start | bytes 5505028
  222.1 11.9 %collective-permute-start.20 = (bf16[64,3584]{1,0:T(8,128)(2,1)}, bf16[64,3584]{1,0:T(8,128)(2,1)S(1)}, u32[]{:S(2)}, u32[]{:S(2)}) collective-permute-start(bf16[64,3584]{1,0:T(8,128)(2,1)} %get-tuple-element.5), channel_id=1, source_target_pairs={{0,4},{1,5},{4,8},{5,9},{8,12},{9,13},{12,14},{13,15},{14,10},{15,... | collective-permute-start | bytes 1376264 | tf_op jit(solution)/shard_map/ppermute | solution.py:99
  222.5 11.9 %collective-permute-start.23 = (bf16[64,3584]{1,0:T(8,128)(2,1)}, bf16[64,3584]{1,0:T(8,128)(2,1)}, u32[]{:S(2)}, u32[]{:S(2)}) collective-permute-start(bf16[64,3584]{1,0:T(8,128)(2,1)} %get-tuple-element.8), channel_id=1, source_target_pairs={{0,2},{1,3},{4,0},{5,1},{8,4},{9,5},{12,8},{13,9},{14,12},{15,13},... | collective-permute-start | bytes 1376264 | tf_op jit(solution)/shard_map/ppermute | solution.py:99
  224.1 14.9 %collective-permute-start.26 = (bf16[64,3584]{1,0:T(8,128)(2,1)}, bf16[64,3584]{1,0:T(8,128)(2,1)}, u32[]{:S(2)}, u32[]{:S(2)}) collective-permute-start(bf16[64,3584]{1,0:T(8,128)(2,1)} %get-tuple-element.7), channel_id=1, source_target_pairs={{0,4},{1,5},{4,8},{5,9},{8,12},{9,13},{12,14},{13,15},{14,10},{15,... | collective-permute-start | bytes 1376264 | tf_op jit(solution)/shard_map/ppermute | solution.py:99
  224.6 14.8 %collective-permute-start.30 = (bf16[64,3584]{1,0:T(8,128)(2,1)}, bf16[64,3584]{1,0:T(8,128)(2,1)}, u32[]{:S(2)}, u32[]{:S(2)}) collective-permute-start(bf16[64,3584]{1,0:T(8,128)(2,1)} %get-tuple-element.6), channel_id=1, source_target_pairs={{0,2},{1,3},{4,0},{5,1},{8,4},{9,5},{12,8},{13,9},{14,12},{15,13},... | collective-permute-start | bytes 1376264 | tf_op jit(solution)/shard_map/ppermute | solution.py:99

commit v3 on v1

v3 whole, which is shorter than its diff:
```python
import functools

import jax
import jax.numpy as jnp
from jax import lax
from jax.experimental import pallas as pl
from jax.experimental.pallas import tpu as pltpu
from jax.sharding import PartitionSpec as P

SPAN = 2
LANES = 128
DIGIT = 64
TILE = 256
WIDE = 512
MIB = 1 << 20


def expert_kernel(n, experts, dim, half, tiles, expert_ref, *refs):
    blocks, weights, outs = refs[:n], refs[n : n + 6], refs[n + 6 : 2 * n + 6]
    rows_ref, scale_ref, total_ref = refs[2 * n + 6 :]
    step = pl.program_id(0)

    @pl.when(step == 0)
    def _():
        lane = lax.broadcasted_iota(jnp.int32, (half, LANES), 1)
        expert = expert_ref[0]
        for i, block in enumerate(blocks):
            at = pl.ds(i * half, half)
            rows_ref[at, :] = block[:, :dim]
            digits = block[:, dim:].astype(jnp.float32)
            codes = jnp.where(lane == expert, digits * float(DIGIT), 0.0)
            codes = codes + jnp.where(lane == expert + experts, digits, 0.0)
            code = jnp.sum(codes, 1, keepdims=True) * (1.0 / 4096.0)
            scale_ref[at, :] = jnp.broadcast_to(code, (half, LANES))

    def add_tile(gate_ref, up_ref, down_ref, first):
        rows = rows_ref[...]
        gate = jnp.dot(rows, gate_ref[...], preferred_element_type=jnp.float32)
        upward = jnp.dot(rows, up_ref[...], preferred_element_type=jnp.float32)
        hidden = gate / (1.0 + jnp.exp(-gate)) * upward * scale_ref[:, :1]
        hidden = hidden.astype(jnp.bfloat16)
        for c in range(0, dim, WIDE):
            part = jnp.dot(hidden, down_ref[:, c : c + WIDE], preferred_element_type=jnp.float32)
            if first:
                total_ref[:, c : c + WIDE] = part
            else:
                total_ref[:, c : c + WIDE] += part

    @pl.when(step == 0)
    def _():
        add_tile(*weights[:3], True)

    @pl.when((step > 0) & (step < tiles))
    def _():
        add_tile(*weights[:3], False)

    @pl.when(step >= tiles)
    def _():
        add_tile(*weights[3:], False)

    @pl.when(step == 2 * tiles - 1)
    def _():
        for i, out in enumerate(outs):
            out[...] = total_ref[i * half : (i + 1) * half, :].astype(jnp.bfloat16)


def expert_parts(experts, expert, blocks, own, other):
    half, wide = blocks[0].shape
    dim, hid = own[0].shape
    n, tiles = len(blocks), hid // TILE

    def mine(j):
        return jnp.minimum(j, tiles - 1)

    def theirs(j):
        return jnp.maximum(j - tiles, 0)

    specs = [pl.BlockSpec(memory_space=pltpu.SMEM)]
    specs += [pl.BlockSpec((half, wide), lambda j: (0, 0))] * n
    for at in (mine, theirs):
        column = pl.BlockSpec((dim, TILE), lambda j, at=at: (0, at(j)))
        specs += [column, column, pl.BlockSpec((TILE, dim), lambda j, at=at: (at(j), 0))]
    return pl.pallas_call(
        functools.partial(expert_kernel, n, experts, dim, half, tiles),
        grid=(2 * tiles,),
        in_specs=specs,
        out_specs=[pl.BlockSpec((half, dim), lambda j: (0, 0))] * n,
        out_shape=[jax.ShapeDtypeStruct((half, dim), jnp.bfloat16)] * n,
        scratch_shapes=[
            pltpu.VMEM((n * half, dim), jnp.bfloat16),
            pltpu.VMEM((n * half, LANES), jnp.float32),
            pltpu.VMEM((n * half, dim), jnp.float32),
        ],
        compiler_params=pltpu.CompilerParams(vmem_limit_bytes=48 * MIB),
        cost_estimate=pl.CostEstimate(flops=1024, bytes_accessed=1024, transcendentals=0),
    )(expert, *blocks, *own, *other)


def add_kernel(*refs):
    total = refs[0][...].astype(jnp.float32)
    for ref in refs[1:-1]:
        total = total + ref[...].astype(jnp.float32)
    refs[-1][...] = total.astype(refs[-1].dtype)


def add(*terms):
    rows, dim = terms[0].shape
    block = pl.BlockSpec((rows, dim // 2), lambda j: (0, j))
    return pl.pallas_call(
        add_kernel,
        grid=(2,),
        in_specs=[block] * len(terms),
        out_specs=block,
        out_shape=jax.ShapeDtypeStruct((rows, dim), jnp.bfloat16),
        cost_estimate=pl.CostEstimate(flops=1024, bytes_accessed=1024, transcendentals=0),
    )(*terms)


def rows_kernel(experts, top, half, tokens_ref, ids_ref, codes_ref, *outs):
    dim = tokens_ref.shape[1]
    lane = lax.broadcasted_iota(jnp.int32, (half, LANES), 1)
    expert = jnp.where(lane < experts, lane, lane - experts)
    for i, out in enumerate(outs):
        at = pl.ds(i * half, half)
        ids, codes = ids_ref[at, :], codes_ref[at, :]
        code = jnp.zeros((half, LANES), jnp.int32)
        for k in range(top):
            code = code + jnp.where(ids[:, k : k + 1] == expert, codes[:, k : k + 1], 0)
        digits = jnp.where(lane < experts, code // DIGIT, code % DIGIT)
        out[:, :dim] = tokens_ref[at, :]
        out[:, dim:] = digits.astype(jnp.float32).astype(out.dtype)


def with_codes(experts, tokens, ids, codes):
    tok, dim = tokens.shape
    half = tok // 2
    return pl.pallas_call(
        functools.partial(rows_kernel, experts, ids.shape[1], half),
        out_shape=[jax.ShapeDtypeStruct((half, dim + LANES), tokens.dtype)] * 2,
        cost_estimate=pl.CostEstimate(flops=1024, bytes_accessed=1024, transcendentals=0),
    )(tokens, ids, codes)


def body(tokens, expert_ids, gate_codes, w_gate, w_up, w_down):
    nodes = lax.axis_size("node")
    ring = nodes // SPAN
    far = ring // 2
    tok, top = expert_ids.shape
    half = tok // 2

    def chip_at(pos):
        return 2 * pos if pos < far else 2 * (ring - 1 - pos) + 1

    def perm(step):
        return [
            (chip_at(pos) * SPAN + core, chip_at((pos + step) % ring) * SPAN + core)
            for pos in range(ring)
            for core in range(SPAN)
        ]

    forward, backward = perm(1), perm(-1)
    swap = [(node, node ^ 1) for node in range(nodes)]
    expert = (lax.axis_index("node") // SPAN).astype(jnp.int32).reshape(1)

    rows = with_codes(ring, tokens, expert_ids, gate_codes)

    ahead = [[rows[0]], [rows[1]]]
    behind = [[rows[0]], [rows[1]]]
    parts = {}

    def send(s, after):
        held = [parts[name] for name in after]
        sides = [(ahead, h, forward) for h in range(2) if s < far or h == 0]
        sides += [(behind, h, backward) for h in range(2) if s < far or h == 1]
        last = [(side, h) for side in (ahead, behind) for h in range(2)]
        if s > 1:
            blocks = [side[h][s - 1] for side, h in last]
            blocks, held = lax.optimization_barrier((blocks, held))
            parts.update(zip(after, held))
            for (side, h), block in zip(last, blocks):
                side[h][s - 1] = block
        for side, h, way in sides:
            side[h].append(lax.ppermute(side[h][s - 1], "node", way))

    def work(offsets, after=()):
        names = [(offset, h) for offset in offsets for h in range(2)]
        blocks = []
        for offset, h in names:
            if abs(offset) == far:
                blocks.append((ahead, behind)[h][h][far])
            else:
                blocks.append((ahead if offset <= 0 else behind)[h][abs(offset)])
        held = [parts[name] for name in after]
        blocks, held = lax.optimization_barrier((blocks, held))
        parts.update(zip(after, held))
        parts.update(zip(names, expert_parts(ring, expert, blocks, own, other)))
        return names

    send(1, [])
    own, _ = lax.optimization_barrier(((w_gate, w_up, w_down), rows))
    other = tuple(lax.ppermute(w, "node", swap) for w in own)
    done = []
    for s in range(2, far + 1):
        send(s, done)
        done = work([0, -1, 1] if s == 2 else [1 - s, s - 1])
    work([far], done)
    parts[-far, 1] = parts[far, 1]

    outs = []
    for h in range(2):
        came = {}
        for sign, way in ((1, forward), (-1, backward)):
            first = far if (h == 0) == (sign == 1) else far - 1
            total = parts[sign * first, h]
            for d in range(first - 1, -1, -1):
                arrived = lax.ppermute(total, "node", way)
                total = add(parts[sign * d, h], arrived) if d else arrived
            came[sign] = total
        outs.append(add(parts[0, h], came[1], came[-1]))
    return jnp.concatenate(outs, 0)


def solution(mesh):
    in_specs = (
        P(("groups", "node"), None),
        P(("groups", "node"), None),
        P(("groups", "node"), None),
        P(None, "node"),
        P(None, "node"),
        P("node", None),
    )
    out_specs = P(("groups", "node"), None)
    return jax.shard_map(body, mesh=mesh, in_specs=in_specs, out_specs=out_specs, check_vma=False)
```

time: 502 us -> 195 us (0.39)
  waiting for transfers between devices: 397 us -> 58.5 us
  Pallas kernels: 0 us -> 76.5 us
  matrix products: 61.9 us -> 0 us
  starting transfers between devices: 0.46 us -> 33.4 us
  blocking collectives: 23.3 us -> 0 us
  local copies, waits for them, and re-layouts: 2.59 us -> 23.7 us
  between operations: 13.5 us -> 0.22 us
    reduce_scatter x4 -> x0, waiting for transfers between devices: 271 us -> none  [body(): outs.append(lax.psum_scatter(part, 'node', scatter_dimension=0, tiled=True))]
    all_gather x4 -> x0, waiting for transfers between devices: 124 us -> none  [body(): rows = lax.all_gather(mine, 'node', axis=0, tiled=True)]
    pallas_call x0 -> x17, Pallas kernels: none -> 76.5 us  [the longest x4 49.5 us: expert_parts(): pl.pallas_call(functools.partial(expert_kernel, n, experts, dim, half, ti...]
    dot_general x8 -> x0, matrix products: 61.9 us -> none  [the longest x4 41 us: body(): jnp.dot(hidden, w_down, preferred_element_type=jnp.float32)]
    ppermute x0 -> x31, waiting for transfers between devices: none -> 58.5 us  [the longest x14 33.7 us: send(): side[h].append(lax.ppermute(side[h][s - 1], 'node', way))]
    ppermute x0 -> x31, starting transfers between devices: none -> 33.4 us  [the longest x14 18.2 us: send(): side[h].append(lax.ppermute(side[h][s - 1], 'node', way))]
    unnamed x0 -> x64, local copies, waits for them, and re-layouts: none -> 23.7 us
    all_gather x1 -> x0, blocking collectives: 23.3 us -> none  [body(): lax.all_gather(jnp.concatenate([expert_ids, gate_codes], 1), 'node', axis...]
  transfers between devices with their start and end apart: 8 -> 31, of which waited for: 8 -> 13; matrix products, arithmetic and copies ran while one was open for 13% -> 0% of each run, Pallas kernels for 0% -> 32%
where the time goes in v3:
time: 195 us
  Pallas kernels  76.5 us (39%)
  waiting for transfers between devices  58.5 us (30%)
  starting transfers between devices  33.4 us (17%)
  local copies, waits for them, and re-layouts  23.7 us (12%)
  other arithmetic  2.14 us (1%)
    pallas_call x4, Pallas kernels, expert_parts(): pl.pallas_call(functools.partial(expert_kernel, n, experts, dim, half, ti...  49.5 us
    ppermute x14, waiting for transfers between devices, send(): side[h].append(lax.ppermute(side[h][s - 1], 'node', way))  33.7 us
    ppermute x14, waiting for transfers between devices, body(): arrived = lax.ppermute(total, 'node', way)  24.8 us
    pallas_call x12, Pallas kernels, add(): pl.pallas_call(add_kernel, grid=(2,), in_specs=[block] * len(terms), out_...  24.7 us
    unnamed x64, local copies, waits for them, and re-layouts  23.7 us
    ppermute x14, starting transfers between devices, send(): side[h].append(lax.ppermute(side[h][s - 1], 'node', way))  18.2 us
    ppermute x14, starting transfers between devices, body(): arrived = lax.ppermute(total, 'node', way)  14.2 us
  transfers between devices with their start and end apart: 31, of which 13 were waited for; matrix products, arithmetic and copies ran while one was open for 0% of the time, Pallas kernels for 32%

profile of v3, /device:TPU:0, one launch (start us, length us, event | category | flops | bytes accessed | tf_op | source)
XLA Modules:
  0.0 194.5 jit_solution(17864177721555919182)
XLA Ops:
  0.0 1.4 copy.7.ids_ref
  1.4 1.4 copy.8.codes_ref
  2.8 2.4 %shard_map.64 = (bf16[64,3712]{1,0:T(8,128)(2,1)}, bf16[64,3712]{1,0:T(8,128)(2,1)}) custom-call(bf16[128,3584]{1,0:T(8,128)(2,1)} %tokens_ref.1, s32[128,4]{1,0:T(8,128)} %copy.7.ids_ref, s32[128,4]{1,0:T(8,128)} %copy.8.codes_ref), custom_call_target="tpu_custom_call" | custom-call | flops 1024 | bytes 1024 | tf_op jit(solution)/shard_map/pallas_call | solution.py:137
  6.1 2.6 %collective-permute-start = (bf16[64,3712]{1,0:T(8,128)(2,1)}, bf16[64,3712]{1,0:T(8,128)(2,1)S(1)}, u32[]{:S(2)}, u32[]{:S(2)}) collective-permute-start(bf16[64,3712]{1,0:T(8,128)(2,1)} %get-tuple-element.74.refs_0_), channel_id=1, source_target_pairs={{0,4},{1,5},{4,8},{5,9},{8,12},{9,13},{12,14},{13,15},{14,10},{15,... | collective-permute-start | bytes 1425416 | tf_op jit(solution)/shard_map/ppermute | solution.py:183
  8.7 1.6 collective-permute-start.1
  10.3 10.3 %collective-permute-done.refs_2_ = bf16[64,3712]{1,0:T(8,128)(2,1)S(1)} collective-permute-done((bf16[64,3712]{1,0:T(8,128)(2,1)}, bf16[64,3712]{1,0:T(8,128)(2,1)S(1)}, u32[]{:S(2)}, u32[]{:S(2)}) %collective-permute-start) | collective-permute-done | bytes 475168 | tf_op jit(solution)/shard_map/ppermute | solution.py:183
  20.6 1.9 %collective-permute-start.2 = (bf16[64,3712]{1,0:T(8,128)(2,1)}, bf16[64,3712]{1,0:T(8,128)(2,1)S(1)}, u32[]{:S(2)}, u32[]{:S(2)}) collective-permute-start(bf16[64,3712]{1,0:T(8,128)(2,1)} %get-tuple-element.74.refs_0_), channel_id=1, source_target_pairs={{0,2},{1,3},{4,0},{5,1},{8,4},{9,5},{12,8},{13,9},{14,12},{15,13},... | collective-permute-start | bytes 1425416 | tf_op jit(solution)/shard_map/ppermute | solution.py:183
  22.5 8.1 %collective-permute-done.1.refs_3_ = bf16[64,3712]{1,0:T(8,128)(2,1)S(1)} collective-permute-done((bf16[64,3712]{1,0:T(8,128)(2,1)}, bf16[64,3712]{1,0:T(8,128)(2,1)S(1)}, u32[]{:S(2)}, u32[]{:S(2)}) %collective-permute-start.1) | collective-permute-done | bytes 475168 | tf_op jit(solution)/shard_map/ppermute | solution.py:183
  30.6 1.7 collective-permute-start.3
  33.3 10.3 %collective-permute-done.3.refs_5_ = bf16[64,3712]{1,0:T(8,128)(2,1)} collective-permute-done((bf16[64,3712]{1,0:T(8,128)(2,1)}, bf16[64,3712]{1,0:T(8,128)(2,1)}, u32[]{:S(2)}, u32[]{:S(2)}) %collective-permute-start.3) | collective-permute-done | bytes 475168 | tf_op jit(solution)/shard_map/ppermute | solution.py:183
  43.6 1.6 collective-permute-start.4
  45.2 1.6 collective-permute-start.5
  47.2 1.4 copy-done.15
  48.6 1.8 copy-done.16
  53.0 15.0 %shard_map.65 = (bf16[64,3584]{1,0:T(8,128)(2,1)S(1)}, bf16[64,3584]{1,0:T(8,128)(2,1)S(1)}, bf16[64,3584]{1,0:T(8,128)(2,1)S(1)}, bf16[64,3584]{1,0:T(8,128)(2,...) custom-call(s32[1]{0:T(128)} %bitcast.expert_ref, bf16[64,3712]{1,0:T(8,128)(2,1)S(1)} %copy-done.1, ...), custom_call_target="tpu_custom_call" | custom-call | flops 1024 | bytes 1024 | tf_op jit(solution)/shard_map/pallas_call | solution.py:83
  70.3 1.6 collective-permute-start.11
  72.0 1.6 collective-permute-start.12
  74.4 12.3 %shard_map.66 = (bf16[64,3584]{1,0:T(8,128)(2,1)S(1)}, bf16[64,3584]{1,0:T(8,128)(2,1)S(1)}, bf16[64,3584]{1,0:T(8,128)(2,1)S(1)}, bf16[64,3584]{1,0:T(8,128)(2,1)S(1)}) custom-call(s32[1]{0:T(128)} %bitcast.expert_ref, bf16[64,3712]{1,0:T(8,128)(2,1)S(1)} %collective-permute-done.4.refs_0_, bf16[64,3712]{1,0:T(8,128)(2,1)S(1)} %collective-permute-done.5.refs_1_, ...), custom_call_target="tpu_custom_call" | custom-call | flops 1024 | bytes 1024 | tf_op jit(solution)/shard_map/pallas_call | solution.py:83
  89.9 1.5 collective-permute-done.12.refs_1_
  91.4 2.6 %collective-permute-done.14.refs_3_ = bf16[64,3712]{1,0:T(8,128)(2,1)S(1)} collective-permute-done((bf16[64,3712]{1,0:T(8,128)(2,1)S(1)}, bf16[64,3712]{1,0:T(8,128)(2,1)S(1)}, u32[]{:S(2)}, u32[]{:S(2)}) %collective-permute-start.14) | collective-permute-done | bytes 475168 | tf_op jit(solution)/shard_map/ppermute | solution.py:183
  93.9 2.2 %collective-permute-start.15 = (bf16[64,3712]{1,0:T(8,128)(2,1)S(1)}, bf16[64,3712]{1,0:T(8,128)(2,1)S(1)}, u32[]{:S(2)}, u32[]{:S(2)}) collective-permute-start(bf16[64,3712]{1,0:T(8,128)(2,1)S(1)} %collective-permute-done.11.refs_0_), channel_id=1, source_target_pairs={{0,4},{1,5},{4,8},{5,9},{8,12},{9,13},{12,14},{13,15},{14,10},{15,... | collective-permute-start | bytes 1425416 | tf_op jit(solution)/shard_map/ppermute | solution.py:183
  96.1 12.3 %shard_map.67 = (bf16[64,3584]{1,0:T(8,128)(2,1)S(1)}, bf16[64,3584]{1,0:T(8,128)(2,1)S(1)}, bf16[64,3584]{1,0:T(8,128)(2,1)S(1)}, bf16[64,3584]{1,0:T(8,128)(2,1)S(1)}) custom-call(s32[1]{0:T(128)} %bitcast.expert_ref, bf16[64,3712]{1,0:T(8,128)(2,1)S(1)} %collective-permute-done.11.refs_0_, bf16[64,3712]{1,0:T(8,128)(2,1)S(1)} %collective-permute-done.12.refs_1_, ...), custom_call_target="tpu_custom_call" | custom-call | flops 1024 | bytes 1024 | tf_op jit(solution)/shard_map/pallas_call | solution.py:83
  108.5 9.9 %shard_map.68 = (bf16[64,3584]{1,0:T(8,128)(2,1)S(1)}, bf16[64,3584]{1,0:T(8,128)(2,1)S(1)}) custom-call(s32[1]{0:T(128)} %bitcast.expert_ref, bf16[64,3712]{1,0:T(8,128)(2,1)S(1)} %collective-permute-done.15.refs_0_, bf16[64,3712]{1,0:T(8,128)(2,1)S(1)} %collective-permute-done.16.refs_1_, bf16[3584,512]{1,0:T(8,128)(2,1)S(1)} %copy-done, ...), custom_call_target="tpu_custom_call" | custom-call | flops 1024 | bytes 1024 | tf_op jit(solution)/shard_map/pallas_call | solution.py:83
  118.4 2.1 %collective-permute-start.17 = (bf16[64,3584]{1,0:T(8,128)(2,1)S(1)}, bf16[64,3584]{1,0:T(8,128)(2,1)S(1)}, u32[]{:S(2)}, u32[]{:S(2)}) collective-permute-start(bf16[64,3584]{1,0:T(8,128)(2,1)S(1)} %get-tuple-element.119), channel_id=1, source_target_pairs={{0,4},{1,5},{4,8},{5,9},{8,12},{9,13},{12,14},{13,15},{14,10},{15,... | collective-permute-start | bytes 1376264 | tf_op jit(solution)/shard_map/ppermute | solution.py:216
  120.8 1.8 collective-permute-start.24
  122.5 9.4 %collective-permute-done.17.refs_1_ = bf16[64,3584]{1,0:T(8,128)(2,1)S(1)} collective-permute-done((bf16[64,3584]{1,0:T(8,128)(2,1)S(1)}, bf16[64,3584]{1,0:T(8,128)(2,1)S(1)}, u32[]{:S(2)}, u32[]{:S(2)}) %collective-permute-start.17) | collective-permute-done | bytes 458784 | tf_op jit(solution)/shard_map/ppermute | solution.py:216
  132.7 2.0 %shard_map.69 = bf16[64,3584]{1,0:T(8,128)(2,1)} custom-call(bf16[64,3584]{1,0:T(8,128)(2,1)} %copy-done.14, bf16[64,3584]{1,0:T(8,128)(2,1)} %copy-done.30), custom_call_target="tpu_custom_call" | custom-call | flops 1024 | bytes 1024 | tf_op jit(solution)/shard_map/pallas_call | solution.py:109
  134.7 2.0 %collective-permute-start.18 = (bf16[64,3584]{1,0:T(8,128)(2,1)}, bf16[64,3584]{1,0:T(8,128)(2,1)S(1)}, u32[]{:S(2)}, u32[]{:S(2)}) collective-permute-start(bf16[64,3584]{1,0:T(8,128)(2,1)} %shard_map.69), channel_id=1, source_target_pairs={{0,4},{1,5},{4,8},{5,9},{8,12},{9,13},{12,14},{13,15},{14,10},{15,... | collective-permute-start | bytes 1376264 | tf_op jit(solution)/shard_map/ppermute | solution.py:216
  137.5 2.0 %shard_map.77 = bf16[64,3584]{1,0:T(8,128)(2,1)} custom-call(bf16[64,3584]{1,0:T(8,128)(2,1)} %copy-done.13, bf16[64,3584]{1,0:T(8,128)(2,1)} %copy-done.29), custom_call_target="tpu_custom_call" | custom-call | flops 1024 | bytes 1024 | tf_op jit(solution)/shard_map/pallas_call | solution.py:109
  139.6 4.1 %collective-permute-done.21.refs_1_ = bf16[64,3584]{1,0:T(8,128)(2,1)S(1)} collective-permute-done((bf16[64,3584]{1,0:T(8,128)(2,1)S(1)}, bf16[64,3584]{1,0:T(8,128)(2,1)S(1)}, u32[]{:S(2)}, u32[]{:S(2)}) %collective-permute-start.21) | collective-permute-done | bytes 458784 | tf_op jit(solution)/shard_map/ppermute | solution.py:216
  144.5 2.0 %shard_map.72 = bf16[64,3584]{1,0:T(8,128)(2,1)} custom-call(bf16[64,3584]{1,0:T(8,128)(2,1)} %copy-done.12, bf16[64,3584]{1,0:T(8,128)(2,1)} %copy-done.28), custom_call_target="tpu_custom_call" | custom-call | flops 1024 | bytes 1024 | tf_op jit(solution)/shard_map/pallas_call | solution.py:109
  147.4 2.0 %shard_map.75 = bf16[64,3584]{1,0:T(8,128)(2,1)} custom-call(bf16[64,3584]{1,0:T(8,128)(2,1)} %copy-done.11, bf16[64,3584]{1,0:T(8,128)(2,1)} %copy-done.21), custom_call_target="tpu_custom_call" | custom-call | flops 1024 | bytes 1024 | tf_op jit(solution)/shard_map/pallas_call | solution.py:109
  149.4 2.0 %collective-permute-start.25 = (bf16[64,3584]{1,0:T(8,128)(2,1)}, bf16[64,3584]{1,0:T(8,128)(2,1)S(1)}, u32[]{:S(2)}, u32[]{:S(2)}) collective-permute-start(bf16[64,3584]{1,0:T(8,128)(2,1)} %shard_map.75), channel_id=1, source_target_pairs={{0,4},{1,5},{4,8},{5,9},{8,12},{9,13},{12,14},{13,15},{14,10},{15,... | collective-permute-start | bytes 1376264 | tf_op jit(solution)/shard_map/ppermute | solution.py:216
  152.4 2.0 %shard_map.70 = bf16[64,3584]{1,0:T(8,128)(2,1)} custom-call(bf16[64,3584]{1,0:T(8,128)(2,1)} %copy-done.10, bf16[64,3584]{1,0:T(8,128)(2,1)} %copy-done.22), custom_call_target="tpu_custom_call" | custom-call | flops 1024 | bytes 1024 | tf_op jit(solution)/shard_map/pallas_call | solution.py:109
  154.4 2.0 %collective-permute-start.19 = (bf16[64,3584]{1,0:T(8,128)(2,1)}, bf16[64,3584]{1,0:T(8,128)(2,1)S(1)}, u32[]{:S(2)}, u32[]{:S(2)}) collective-permute-start(bf16[64,3584]{1,0:T(8,128)(2,1)} %shard_map.70), channel_id=1, source_target_pairs={{0,4},{1,5},{4,8},{5,9},{8,12},{9,13},{12,14},{13,15},{14,10},{15,... | collective-permute-start | bytes 1376264 | tf_op jit(solution)/shard_map/ppermute | solution.py:216
  157.2 2.0 %shard_map.78 = bf16[64,3584]{1,0:T(8,128)(2,1)} custom-call(bf16[64,3584]{1,0:T(8,128)(2,1)} %copy-done.9, bf16[64,3584]{1,0:T(8,128)(2,1)} %copy-done.23), custom_call_target="tpu_custom_call" | custom-call | flops 1024 | bytes 1024 | tf_op jit(solution)/shard_map/pallas_call | solution.py:109
  159.2 4.2 %collective-permute-done.22.refs_1_ = bf16[64,3584]{1,0:T(8,128)(2,1)S(1)} collective-permute-done((bf16[64,3584]{1,0:T(8,128)(2,1)}, bf16[64,3584]{1,0:T(8,128)(2,1)S(1)}, u32[]{:S(2)}, u32[]{:S(2)}) %collective-permute-start.22) | collective-permute-done | bytes 458784 | tf_op jit(solution)/shard_map/ppermute | solution.py:216
  164.2 2.0 %shard_map.73 = bf16[64,3584]{1,0:T(8,128)(2,1)} custom-call(bf16[64,3584]{1,0:T(8,128)(2,1)} %copy-done.8, bf16[64,3584]{1,0:T(8,128)(2,1)} %copy-done.24), custom_call_target="tpu_custom_call" | custom-call | flops 1024 | bytes 1024 | tf_op jit(solution)/shard_map/pallas_call | solution.py:109
  167.0 2.0 %shard_map.76 = bf16[64,3584]{1,0:T(8,128)(2,1)} custom-call(bf16[64,3584]{1,0:T(8,128)(2,1)} %copy-done.7, bf16[64,3584]{1,0:T(8,128)(2,1)} %copy-done.25), custom_call_target="tpu_custom_call" | custom-call | flops 1024 | bytes 1024 | tf_op jit(solution)/shard_map/pallas_call | solution.py:109
  169.1 2.0 %collective-permute-start.26 = (bf16[64,3584]{1,0:T(8,128)(2,1)}, bf16[64,3584]{1,0:T(8,128)(2,1)S(1)}, u32[]{:S(2)}, u32[]{:S(2)}) collective-permute-start(bf16[64,3584]{1,0:T(8,128)(2,1)} %shard_map.76), channel_id=1, source_target_pairs={{0,4},{1,5},{4,8},{5,9},{8,12},{9,13},{12,14},{13,15},{14,10},{15,... | collective-permute-start | bytes 1376264 | tf_op jit(solution)/shard_map/ppermute | solution.py:216
  172.0 2.0 %shard_map.71 = bf16[64,3584]{1,0:T(8,128)(2,1)} custom-call(bf16[64,3584]{1,0:T(8,128)(2,1)} %copy-done.6, bf16[64,3584]{1,0:T(8,128)(2,1)} %copy-done.26), custom_call_target="tpu_custom_call" | custom-call | flops 1024 | bytes 1024 | tf_op jit(solution)/shard_map/pallas_call | solution.py:109
  174.0 2.0 %collective-permute-start.20 = (bf16[64,3584]{1,0:T(8,128)(2,1)}, bf16[64,3584]{1,0:T(8,128)(2,1)S(1)}, u32[]{:S(2)}, u32[]{:S(2)}) collective-permute-start(bf16[64,3584]{1,0:T(8,128)(2,1)} %shard_map.71), channel_id=1, source_target_pairs={{0,4},{1,5},{4,8},{5,9},{8,12},{9,13},{12,14},{13,15},{14,10},{15,... | collective-permute-start | bytes 1376264 | tf_op jit(solution)/shard_map/ppermute | solution.py:216
  176.8 2.0 %shard_map.79 = bf16[64,3584]{1,0:T(8,128)(2,1)} custom-call(bf16[64,3584]{1,0:T(8,128)(2,1)} %copy-done.5, bf16[64,3584]{1,0:T(8,128)(2,1)} %copy-done.27), custom_call_target="tpu_custom_call" | custom-call | flops 1024 | bytes 1024 | tf_op jit(solution)/shard_map/pallas_call | solution.py:109
  178.8 3.1 %collective-permute-done.23.refs_2_ = bf16[64,3584]{1,0:T(8,128)(2,1)S(1)} collective-permute-done((bf16[64,3584]{1,0:T(8,128)(2,1)}, bf16[64,3584]{1,0:T(8,128)(2,1)S(1)}, u32[]{:S(2)}, u32[]{:S(2)}) %collective-permute-start.23) | collective-permute-done | bytes 458784 | tf_op jit(solution)/shard_map/ppermute | solution.py:216
  182.0 3.7 %collective-permute-done.20.refs_1_ = bf16[64,3584]{1,0:T(8,128)(2,1)S(1)} collective-permute-done((bf16[64,3584]{1,0:T(8,128)(2,1)}, bf16[64,3584]{1,0:T(8,128)(2,1)S(1)}, u32[]{:S(2)}, u32[]{:S(2)}) %collective-permute-start.20) | collective-permute-done | bytes 458784 | tf_op jit(solution)/shard_map/ppermute | solution.py:216
  186.4 2.2 %shard_map.74 = bf16[64,3584]{1,0:T(8,128)(2,1)} custom-call(bf16[64,3584]{1,0:T(8,128)(2,1)} %copy-done.4, bf16[64,3584]{1,0:T(8,128)(2,1)} %copy-done.20, bf16[64,3584]{1,0:T(8,128)(2,1)} %copy-done.18), custom_call_target="tpu_custom_call" | custom-call | flops 1024 | bytes 1024 | tf_op jit(solution)/shard_map/pallas_call | solution.py:109
  190.2 2.2 %shard_map.80 = bf16[64,3584]{1,0:T(8,128)(2,1)} custom-call(bf16[64,3584]{1,0:T(8,128)(2,1)} %copy-done.3, bf16[64,3584]{1,0:T(8,128)(2,1)} %copy-done.17, bf16[64,3584]{1,0:T(8,128)(2,1)} %copy-done.19), custom_call_target="tpu_custom_call" | custom-call | flops 1024 | bytes 1024 | tf_op jit(solution)/shard_map/pallas_call | solution.py:109
  192.4 2.1 %pad_maximum_fusion = bf16[128,3584]{1,0:T(8,128)(2,1)} fusion(bf16[64,3584]{1,0:T(8,128)(2,1)} %shard_map.80, bf16[64,3584]{1,0:T(8,128)(2,1)} %shard_map.74), kind=kLoop, calls=%fused_computation | loop fusion | flops 1835008 | bytes 1835008 | tf_op jit(solution)/shard_map/concatenate | solution.py:220
  (96 shorter events, 22.3 us)
Async XLA Ops:
  5.2 41.6 %collective-permute-start.10 = (bf16[512,3584]{1,0:T(8,128)(2,1)}, bf16[512,3584]{1,0:T(8,128)(2,1)S(1)}, u32[]{:S(2)}, u32[]{:S(2)}) collective-permute-start(bf16[512,3584]{1,0:T(8,128)(2,1)} %refs_4_.2), channel_id=1, source_target_pairs={{0,1},{1,0},{2,3},{3,2},{4,5},{5,4},{6,7},{7,6},{8,9},{9,8},{10,11... | collective-permute-start | bytes 11010056 | tf_op jit(solution)/shard_map/ppermute | solution.py:201
  5.6 43.0 %collective-permute-start.8 = (bf16[3584,512]{1,0:T(8,128)(2,1)}, bf16[3584,512]{1,0:T(8,128)(2,1)S(1)}, u32[]{:S(2)}, u32[]{:S(2)}) collective-permute-start(bf16[3584,512]{1,0:T(8,128)(2,1)} %refs_2_), channel_id=1, source_target_pairs={{0,1},{1,0},{2,3},{3,2},{4,5},{5,4},{6,7},{7,6},{8,9},{9,8},{10,11... | collective-permute-start | bytes 11010056 | tf_op jit(solution)/shard_map/ppermute | solution.py:201
  5.7 45.2 %collective-permute-start.9 = (bf16[3584,512]{1,0:T(8,128)(2,1)}, bf16[3584,512]{1,0:T(8,128)(2,1)}, u32[]{:S(2)}, u32[]{:S(2)}) collective-permute-start(bf16[3584,512]{1,0:T(8,128)(2,1)} %refs_3_), channel_id=1, source_target_pairs={{0,1},{1,0},{2,3},{3,2},{4,5},{5,4},{6,7},{7,6},{8,9},{9,8},{10,11... | collective-permute-start | bytes 11010056 | tf_op jit(solution)/shard_map/ppermute | solution.py:201
  6.1 14.4 %collective-permute-start = (bf16[64,3712]{1,0:T(8,128)(2,1)}, bf16[64,3712]{1,0:T(8,128)(2,1)S(1)}, u32[]{:S(2)}, u32[]{:S(2)}) collective-permute-start(bf16[64,3712]{1,0:T(8,128)(2,1)} %get-tuple-element.74.refs_0_), channel_id=1, source_target_pairs={{0,4},{1,5},{4,8},{5,9},{8,12},{9,13},{12,14},{13,15},{14,10},{15,... | collective-permute-start | bytes 1425416 | tf_op jit(solution)/shard_map/ppermute | solution.py:183
  8.7 21.9 %collective-permute-start.1 = (bf16[64,3712]{1,0:T(8,128)(2,1)}, bf16[64,3712]{1,0:T(8,128)(2,1)S(1)}, u32[]{:S(2)}, u32[]{:S(2)}) collective-permute-start(bf16[64,3712]{1,0:T(8,128)(2,1)} %get-tuple-element.75.refs_1_), channel_id=1, source_target_pairs={{0,4},{1,5},{4,8},{5,9},{8,12},{9,13},{12,14},{13,15},{14,10},{15,... | collective-permute-start | bytes 1425416 | tf_op jit(solution)/shard_map/ppermute | solution.py:183
  20.6 12.7 %collective-permute-start.2 = (bf16[64,3712]{1,0:T(8,128)(2,1)}, bf16[64,3712]{1,0:T(8,128)(2,1)S(1)}, u32[]{:S(2)}, u32[]{:S(2)}) collective-permute-start(bf16[64,3712]{1,0:T(8,128)(2,1)} %get-tuple-element.74.refs_0_), channel_id=1, source_target_pairs={{0,2},{1,3},{4,0},{5,1},{8,4},{9,5},{12,8},{13,9},{14,12},{15,13},... | collective-permute-start | bytes 1425416 | tf_op jit(solution)/shard_map/ppermute | solution.py:183
  30.6 13.0 %collective-permute-start.3 = (bf16[64,3712]{1,0:T(8,128)(2,1)}, bf16[64,3712]{1,0:T(8,128)(2,1)}, u32[]{:S(2)}, u32[]{:S(2)}) collective-permute-start(bf16[64,3712]{1,0:T(8,128)(2,1)} %get-tuple-element.75.refs_1_), channel_id=1, source_target_pairs={{0,2},{1,3},{4,0},{5,1},{8,4},{9,5},{12,8},{13,9},{14,12},{15,13},... | collective-permute-start | bytes 1425416 | tf_op jit(solution)/shard_map/ppermute | solution.py:183
  43.6 26.7 %collective-permute-start.4 = (bf16[64,3712]{1,0:T(8,128)(2,1)S(1)}, bf16[64,3712]{1,0:T(8,128)(2,1)S(1)}, u32[]{:S(2)}, u32[]{:S(2)}) collective-permute-start(bf16[64,3712]{1,0:T(8,128)(2,1)S(1)} %collective-permute-done.refs_2_), channel_id=1, source_target_pairs={{0,4},{1,5},{4,8},{5,9},{8,12},{9,13},{12,14},{13,15},{14,10},{15,... | collective-permute-start | bytes 1425416 | tf_op jit(solution)/shard_map/ppermute | solution.py:183
  45.2 25.1 %collective-permute-start.5 = (bf16[64,3712]{1,0:T(8,128)(2,1)S(1)}, bf16[64,3712]{1,0:T(8,128)(2,1)S(1)}, u32[]{:S(2)}, u32[]{:S(2)}) collective-permute-start(bf16[64,3712]{1,0:T(8,128)(2,1)S(1)} %collective-permute-done.1.refs_3_), channel_id=1, source_target_pairs={{0,4},{1,5},{4,8},{5,9},{8,12},{9,13},{12,14},{13,15},{14,10},{15,... | collective-permute-start | bytes 1425416 | tf_op jit(solution)/shard_map/ppermute | solution.py:183
  46.8 1.8 copy-start.15
  46.8 23.5 %collective-permute-start.6 = (bf16[64,3712]{1,0:T(8,128)(2,1)S(1)}, bf16[64,3712]{1,0:T(8,128)(2,1)S(1)}, u32[]{:S(2)}, u32[]{:S(2)}) collective-permute-start(bf16[64,3712]{1,0:T(8,128)(2,1)S(1)} %collective-permute-done.2.refs_4_), channel_id=1, source_target_pairs={{0,2},{1,3},{4,0},{5,1},{8,4},{9,5},{12,8},{13,9},{14,12},{15,13},... | collective-permute-start | bytes 1425416 | tf_op jit(solution)/shard_map/ppermute | solution.py:183
  48.6 1.8 copy-start.16
  50.5 19.9 %collective-permute-start.7 = (bf16[64,3712]{1,0:T(8,128)(2,1)}, bf16[64,3712]{1,0:T(8,128)(2,1)S(1)}, u32[]{:S(2)}, u32[]{:S(2)}) collective-permute-start(bf16[64,3712]{1,0:T(8,128)(2,1)} %collective-permute-done.3.refs_5_), channel_id=1, source_target_pairs={{0,2},{1,3},{4,0},{5,1},{8,4},{9,5},{12,8},{13,9},{14,12},{15,13},... | collective-permute-start | bytes 1425416 | tf_op jit(solution)/shard_map/ppermute | solution.py:183
  50.9 1.0 copy-start.1
  52.0 1.0 copy-start.2
  70.3 16.5 %copy-start.5 = (bf16[64,3584]{1,0:T(8,128)(2,1)}, bf16[64,3584]{1,0:T(8,128)(2,1)S(1)}, u32[]{:S(2)}) copy-start(bf16[64,3584]{1,0:T(8,128)(2,1)S(1)} %get-tuple-element.127.refs_0_) | copy-start | bytes 1376260
  70.3 16.5 %copy-start.6 = (bf16[64,3584]{1,0:T(8,128)(2,1)}, bf16[64,3584]{1,0:T(8,128)(2,1)S(1)}, u32[]{:S(2)}) copy-start(bf16[64,3584]{1,0:T(8,128)(2,1)S(1)} %get-tuple-element.90.refs_0_) | copy-start | bytes 1376260
  70.3 16.5 %copy-start.7 = (bf16[64,3584]{1,0:T(8,128)(2,1)}, bf16[64,3584]{1,0:T(8,128)(2,1)S(1)}, u32[]{:S(2)}) copy-start(bf16[64,3584]{1,0:T(8,128)(2,1)S(1)} %get-tuple-element.124.refs_0_) | copy-start | bytes 1376260
  70.3 19.5 %collective-permute-start.11 = (bf16[64,3712]{1,0:T(8,128)(2,1)S(1)}, bf16[64,3712]{1,0:T(8,128)(2,1)S(1)}, u32[]{:S(2)}, u32[]{:S(2)}) collective-permute-start(bf16[64,3712]{1,0:T(8,128)(2,1)S(1)} %collective-permute-done.4.refs_0_), channel_id=1, source_target_pairs={{0,4},{1,5},{4,8},{5,9},{8,12},{9,13},{12,14},{13,15},{14,10},{15,... | collective-permute-start | bytes 1425416 | tf_op jit(solution)/shard_map/ppermute | solution.py:183
  72.0 19.4 %collective-permute-start.12 = (bf16[64,3712]{1,0:T(8,128)(2,1)S(1)}, bf16[64,3712]{1,0:T(8,128)(2,1)S(1)}, u32[]{:S(2)}, u32[]{:S(2)}) collective-permute-start(bf16[64,3712]{1,0:T(8,128)(2,1)S(1)} %collective-permute-done.5.refs_1_), channel_id=1, source_target_pairs={{0,4},{1,5},{4,8},{5,9},{8,12},{9,13},{12,14},{13,15},{14,10},{15,... | collective-permute-start | bytes 1425416 | tf_op jit(solution)/shard_map/ppermute | solution.py:183
  73.5 17.8 %collective-permute-start.13 = (bf16[64,3712]{1,0:T(8,128)(2,1)S(1)}, bf16[64,3712]{1,0:T(8,128)(2,1)S(1)}, u32[]{:S(2)}, u32[]{:S(2)}) collective-permute-start(bf16[64,3712]{1,0:T(8,128)(2,1)S(1)} %collective-permute-done.6.refs_2_), channel_id=1, source_target_pairs={{0,2},{1,3},{4,0},{5,1},{8,4},{9,5},{12,8},{13,9},{14,12},{15,13},... | collective-permute-start | bytes 1425416 | tf_op jit(solution)/shard_map/ppermute | solution.py:183
  74.0 19.9 %collective-permute-start.14 = (bf16[64,3712]{1,0:T(8,128)(2,1)S(1)}, bf16[64,3712]{1,0:T(8,128)(2,1)S(1)}, u32[]{:S(2)}, u32[]{:S(2)}) collective-permute-start(bf16[64,3712]{1,0:T(8,128)(2,1)S(1)} %collective-permute-done.7.refs_3_), channel_id=1, source_target_pairs={{0,2},{1,3},{4,0},{5,1},{8,4},{9,5},{12,8},{13,9},{14,12},{15,13},... | collective-permute-start | bytes 1425416 | tf_op jit(solution)/shard_map/ppermute | solution.py:183
  86.8 0.8 copy-start.9
  93.9 14.5 %copy-start = (bf16[3584,512]{1,0:T(8,128)(2,1)S(1)}, bf16[3584,512]{1,0:T(8,128)(2,1)}, u32[]{:S(2)}) copy-start(bf16[3584,512]{1,0:T(8,128)(2,1)} %refs_2_) | copy-start | bytes 11010052
  93.9 14.5 %collective-permute-start.15 = (bf16[64,3712]{1,0:T(8,128)(2,1)S(1)}, bf16[64,3712]{1,0:T(8,128)(2,1)S(1)}, u32[]{:S(2)}, u32[]{:S(2)}) collective-permute-start(bf16[64,3712]{1,0:T(8,128)(2,1)S(1)} %collective-permute-done.11.refs_0_), channel_id=1, source_target_pairs={{0,4},{1,5},{4,8},{5,9},{8,12},{9,13},{12,14},{13,15},{14,10},{15,... | collective-permute-start | bytes 1425416 | tf_op jit(solution)/shard_map/ppermute | solution.py:183
  96.1 12.3 %collective-permute-start.16 = (bf16[64,3712]{1,0:T(8,128)(2,1)S(1)}, bf16[64,3712]{1,0:T(8,128)(2,1)S(1)}, u32[]{:S(2)}, u32[]{:S(2)}) collective-permute-start(bf16[64,3712]{1,0:T(8,128)(2,1)S(1)} %collective-permute-done.14.refs_3_), channel_id=1, source_target_pairs={{0,2},{1,3},{4,0},{5,1},{8,4},{9,5},{12,8},{13,9},{14,12},{15,13},... | collective-permute-start | bytes 1425416 | tf_op jit(solution)/shard_map/ppermute | solution.py:183
  108.4 9.9 %copy-start.13 = (bf16[64,3584]{1,0:T(8,128)(2,1)}, bf16[64,3584]{1,0:T(8,128)(2,1)S(1)}, u32[]{:S(2)}) copy-start(bf16[64,3584]{1,0:T(8,128)(2,1)S(1)} %get-tuple-element.129.refs_0_) | copy-start | bytes 1376260
  108.4 9.9 %copy-start.14 = (bf16[64,3584]{1,0:T(8,128)(2,1)}, bf16[64,3584]{1,0:T(8,128)(2,1)S(1)}, u32[]{:S(2)}) copy-start(bf16[64,3584]{1,0:T(8,128)(2,1)S(1)} %get-tuple-element.116.refs_0_) | copy-start | bytes 1376260
  118.4 13.5 %collective-permute-start.17 = (bf16[64,3584]{1,0:T(8,128)(2,1)S(1)}, bf16[64,3584]{1,0:T(8,128)(2,1)S(1)}, u32[]{:S(2)}, u32[]{:S(2)}) collective-permute-start(bf16[64,3584]{1,0:T(8,128)(2,1)S(1)} %get-tuple-element.119), channel_id=1, source_target_pairs={{0,4},{1,5},{4,8},{5,9},{8,12},{9,13},{12,14},{13,15},{14,10},{15,... | collective-permute-start | bytes 1376264 | tf_op jit(solution)/shard_map/ppermute | solution.py:216
  120.4 16.3 %collective-permute-start.27 = (bf16[64,3584]{1,0:T(8,128)(2,1)S(1)}, bf16[64,3584]{1,0:T(8,128)(2,1)S(1)}, u32[]{:S(2)}, u32[]{:S(2)}) collective-permute-start(bf16[64,3584]{1,0:T(8,128)(2,1)S(1)} %get-tuple-element.130), channel_id=1, source_target_pairs={{0,2},{1,3},{4,0},{5,1},{8,4},{9,5},{12,8},{13,9},{14,12},{15,13},... | collective-permute-start | bytes 1376264 | tf_op jit(solution)/shard_map/ppermute | solution.py:216
  120.5 23.3 %collective-permute-start.21 = (bf16[64,3584]{1,0:T(8,128)(2,1)S(1)}, bf16[64,3584]{1,0:T(8,128)(2,1)S(1)}, u32[]{:S(2)}, u32[]{:S(2)}) collective-permute-start(bf16[64,3584]{1,0:T(8,128)(2,1)S(1)} %get-tuple-element.122), channel_id=1, source_target_pairs={{0,2},{1,3},{4,0},{5,1},{8,4},{9,5},{12,8},{13,9},{14,12},{15,13},... | collective-permute-start | bytes 1376264 | tf_op jit(solution)/shard_map/ppermute | solution.py:216
  120.8 25.8 %collective-permute-start.24 = (bf16[64,3584]{1,0:T(8,128)(2,1)S(1)}, bf16[64,3584]{1,0:T(8,128)(2,1)S(1)}, u32[]{:S(2)}, u32[]{:S(2)}) collective-permute-start(bf16[64,3584]{1,0:T(8,128)(2,1)S(1)} %get-tuple-element.126), channel_id=1, source_target_pairs={{0,4},{1,5},{4,8},{5,9},{8,12},{9,13},{12,14},{13,15},{14,10},{15,... | collective-permute-start | bytes 1376264 | tf_op jit(solution)/shard_map/ppermute | solution.py:216
  131.9 0.8 copy-start.30
  134.7 16.8 %collective-permute-start.18 = (bf16[64,3584]{1,0:T(8,128)(2,1)}, bf16[64,3584]{1,0:T(8,128)(2,1)S(1)}, u32[]{:S(2)}, u32[]{:S(2)}) collective-permute-start(bf16[64,3584]{1,0:T(8,128)(2,1)} %shard_map.69), channel_id=1, source_target_pairs={{0,4},{1,5},{4,8},{5,9},{8,12},{9,13},{12,14},{13,15},{14,10},{15,... | collective-permute-start | bytes 1376264 | tf_op jit(solution)/shard_map/ppermute | solution.py:216
  136.7 0.8 copy-start.29
  139.6 16.8 %collective-permute-start.28 = (bf16[64,3584]{1,0:T(8,128)(2,1)}, bf16[64,3584]{1,0:T(8,128)(2,1)S(1)}, u32[]{:S(2)}, u32[]{:S(2)}) collective-permute-start(bf16[64,3584]{1,0:T(8,128)(2,1)} %shard_map.77), channel_id=1, source_target_pairs={{0,2},{1,3},{4,0},{5,1},{8,4},{9,5},{12,8},{13,9},{14,12},{15,13},... | collective-permute-start | bytes 1376264 | tf_op jit(solution)/shard_map/ppermute | solution.py:216
  143.7 0.8 copy-start.28
  146.6 16.8 %collective-permute-start.22 = (bf16[64,3584]{1,0:T(8,128)(2,1)}, bf16[64,3584]{1,0:T(8,128)(2,1)S(1)}, u32[]{:S(2)}, u32[]{:S(2)}) collective-permute-start(bf16[64,3584]{1,0:T(8,128)(2,1)} %shard_map.72), channel_id=1, source_target_pairs={{0,2},{1,3},{4,0},{5,1},{8,4},{9,5},{12,8},{13,9},{14,12},{15,13},... | collective-permute-start | bytes 1376264 | tf_op jit(solution)/shard_map/ppermute | solution.py:216
  149.4 16.8 %collective-permute-start.25 = (bf16[64,3584]{1,0:T(8,128)(2,1)}, bf16[64,3584]{1,0:T(8,128)(2,1)S(1)}, u32[]{:S(2)}, u32[]{:S(2)}) collective-permute-start(bf16[64,3584]{1,0:T(8,128)(2,1)} %shard_map.75), channel_id=1, source_target_pairs={{0,4},{1,5},{4,8},{5,9},{8,12},{9,13},{12,14},{13,15},{14,10},{15,... | collective-permute-start | bytes 1376264 | tf_op jit(solution)/shard_map/ppermute | solution.py:216
  151.6 0.8 copy-start.22
  154.4 16.9 %collective-permute-start.19 = (bf16[64,3584]{1,0:T(8,128)(2,1)}, bf16[64,3584]{1,0:T(8,128)(2,1)S(1)}, u32[]{:S(2)}, u32[]{:S(2)}) collective-permute-start(bf16[64,3584]{1,0:T(8,128)(2,1)} %shard_map.70), channel_id=1, source_target_pairs={{0,4},{1,5},{4,8},{5,9},{8,12},{9,13},{12,14},{13,15},{14,10},{15,... | collective-permute-start | bytes 1376264 | tf_op jit(solution)/shard_map/ppermute | solution.py:216
  159.2 16.8 %collective-permute-start.29 = (bf16[64,3584]{1,0:T(8,128)(2,1)}, bf16[64,3584]{1,0:T(8,128)(2,1)S(1)}, u32[]{:S(2)}, u32[]{:S(2)}) collective-permute-start(bf16[64,3584]{1,0:T(8,128)(2,1)} %shard_map.78), channel_id=1, source_target_pairs={{0,2},{1,3},{4,0},{5,1},{8,4},{9,5},{12,8},{13,9},{14,12},{15,13},... | collective-permute-start | bytes 1376264 | tf_op jit(solution)/shard_map/ppermute | solution.py:216
  166.2 15.8 %collective-permute-start.23 = (bf16[64,3584]{1,0:T(8,128)(2,1)}, bf16[64,3584]{1,0:T(8,128)(2,1)S(1)}, u32[]{:S(2)}, u32[]{:S(2)}) collective-permute-start(bf16[64,3584]{1,0:T(8,128)(2,1)} %shard_map.73), channel_id=1, source_target_pairs={{0,2},{1,3},{4,0},{5,1},{8,4},{9,5},{12,8},{13,9},{14,12},{15,13},... | collective-permute-start | bytes 1376264 | tf_op jit(solution)/shard_map/ppermute | solution.py:216
  166.2 0.8 copy-start.25
  169.1 19.6 %collective-permute-start.26 = (bf16[64,3584]{1,0:T(8,128)(2,1)}, bf16[64,3584]{1,0:T(8,128)(2,1)S(1)}, u32[]{:S(2)}, u32[]{:S(2)}) collective-permute-start(bf16[64,3584]{1,0:T(8,128)(2,1)} %shard_map.76), channel_id=1, source_target_pairs={{0,4},{1,5},{4,8},{5,9},{8,12},{9,13},{12,14},{13,15},{14,10},{15,... | collective-permute-start | bytes 1376264 | tf_op jit(solution)/shard_map/ppermute | solution.py:216
  174.0 11.6 %collective-permute-start.20 = (bf16[64,3584]{1,0:T(8,128)(2,1)}, bf16[64,3584]{1,0:T(8,128)(2,1)S(1)}, u32[]{:S(2)}, u32[]{:S(2)}) collective-permute-start(bf16[64,3584]{1,0:T(8,128)(2,1)} %shard_map.71), channel_id=1, source_target_pairs={{0,4},{1,5},{4,8},{5,9},{8,12},{9,13},{12,14},{13,15},{14,10},{15,... | collective-permute-start | bytes 1376264 | tf_op jit(solution)/shard_map/ppermute | solution.py:216
  178.8 9.8 %collective-permute-start.30 = (bf16[64,3584]{1,0:T(8,128)(2,1)}, bf16[64,3584]{1,0:T(8,128)(2,1)S(1)}, u32[]{:S(2)}, u32[]{:S(2)}) collective-permute-start(bf16[64,3584]{1,0:T(8,128)(2,1)} %shard_map.79), channel_id=1, source_target_pairs={{0,2},{1,3},{4,0},{5,1},{8,4},{9,5},{12,8},{13,9},{14,12},{15,13},... | collective-permute-start | bytes 1376264 | tf_op jit(solution)/shard_map/ppermute | solution.py:216
  182.0 3.7 %copy-start.18 = (bf16[64,3584]{1,0:T(8,128)(2,1)}, bf16[64,3584]{1,0:T(8,128)(2,1)S(1)}, u32[]{:S(2)}) copy-start(bf16[64,3584]{1,0:T(8,128)(2,1)S(1)} %collective-permute-done.23.refs_2_) | copy-start | bytes 1376260
  (14 other events, 10.9 us)

commit v4 on v1

v4 whole, which is shorter than its diff:
```python
import functools

import jax
import jax.numpy as jnp
from jax import lax
from jax.experimental import pallas as pl
from jax.experimental.pallas import tpu as pltpu
from jax.sharding import PartitionSpec as P

SPAN = 2
LANES = 128
DIGIT = 64
TILE = 256
WIDE = 512
MIB = 1 << 20


def expert_kernel(n, experts, dim, half, expert_ref, *refs):
    blocks, weights, outs = refs[:n], refs[n : n + 6], refs[n + 6 : 2 * n + 6]
    rows_ref, scale_ref, hidden_ref = refs[2 * n + 6 :]
    hid = weights[0].shape[1]
    lane = lax.broadcasted_iota(jnp.int32, (half, LANES), 1)
    expert = expert_ref[0]
    for i, block in enumerate(blocks):
        at = pl.ds(i * half, half)
        rows_ref[at, :] = block[:, :dim]
        digits = block[:, dim:].astype(jnp.float32)
        codes = jnp.where(lane == expert, digits * float(DIGIT), 0.0)
        codes = codes + jnp.where(lane == expert + experts, digits, 0.0)
        code = jnp.sum(codes, 1, keepdims=True) * (1.0 / 4096.0)
        scale_ref[at, :] = jnp.broadcast_to(code, (half, LANES))

    for side in range(SPAN):
        gate_ref, up_ref, _ = weights[3 * side : 3 * side + 3]

        def hidden_tile(j, carry, side=side, gate_ref=gate_ref, up_ref=up_ref):
            at = pl.ds(pl.multiple_of(j * TILE, TILE), TILE)
            rows = rows_ref[...]
            gate = jnp.dot(rows, gate_ref[:, at], preferred_element_type=jnp.float32)
            upward = jnp.dot(rows, up_ref[:, at], preferred_element_type=jnp.float32)
            hidden = gate / (1.0 + jnp.exp(-gate)) * upward * scale_ref[:, :1]
            to = pl.ds(pl.multiple_of(side * hid + j * TILE, TILE), TILE)
            hidden_ref[:, to] = hidden.astype(jnp.bfloat16)
            return carry

        lax.fori_loop(0, hid // TILE, hidden_tile, 0)

    def out_tile(j, carry):
        at = pl.ds(pl.multiple_of(j * WIDE, WIDE), WIDE)
        part = jnp.dot(
            hidden_ref[:, :hid], weights[2][:, at], preferred_element_type=jnp.float32
        ) + jnp.dot(hidden_ref[:, hid:], weights[5][:, at], preferred_element_type=jnp.float32)
        part = part.astype(jnp.bfloat16)
        for i, out in enumerate(outs):
            out[:, at] = part[i * half : (i + 1) * half, :]
        return carry

    lax.fori_loop(0, dim // WIDE, out_tile, 0)


def small_cost():
    return pl.CostEstimate(flops=1024, bytes_accessed=1024, transcendentals=0)


def expert_parts(experts, expert, blocks, own, other):
    half = blocks[0].shape[0]
    dim, hid = own[0].shape
    n = len(blocks)
    specs = [pl.BlockSpec(memory_space=pltpu.SMEM)]
    specs += [pl.BlockSpec(memory_space=pltpu.VMEM)] * (n + 6)
    return pl.pallas_call(
        functools.partial(expert_kernel, n, experts, dim, half),
        in_specs=specs,
        out_specs=[pl.BlockSpec(memory_space=pltpu.VMEM)] * n,
        out_shape=[jax.ShapeDtypeStruct((half, dim), jnp.bfloat16)] * n,
        scratch_shapes=[
            pltpu.VMEM((n * half, dim), jnp.bfloat16),
            pltpu.VMEM((n * half, LANES), jnp.float32),
            pltpu.VMEM((n * half, SPAN * hid), jnp.bfloat16),
        ],
        compiler_params=pltpu.CompilerParams(vmem_limit_bytes=16 * MIB),
        cost_estimate=small_cost(),
    )(expert, *blocks, *own, *other)


def add_kernel(left_ref, right_ref, out_ref):
    total = left_ref[...].astype(jnp.float32) + right_ref[...].astype(jnp.float32)
    out_ref[...] = total.astype(out_ref.dtype)


def add(left, right):
    return pl.pallas_call(
        add_kernel,
        out_shape=jax.ShapeDtypeStruct(left.shape, left.dtype),
        cost_estimate=small_cost(),
    )(left, right)


def close_kernel(*refs):
    out_ref = refs[-1]
    half = refs[0].shape[0]
    for h in range(2):
        terms = refs[3 * h : 3 * h + 3]
        total = sum(ref[...].astype(jnp.float32) for ref in terms)
        out_ref[h * half : (h + 1) * half, :] = total.astype(out_ref.dtype)


def close(terms):
    half, dim = terms[0].shape
    return pl.pallas_call(
        close_kernel,
        out_shape=jax.ShapeDtypeStruct((2 * half, dim), terms[0].dtype),
        cost_estimate=small_cost(),
    )(*terms)


def rows_kernel(experts, top, half, tokens_ref, ids_ref, codes_ref, *outs):
    dim = tokens_ref.shape[1]
    row = lax.broadcasted_iota(jnp.int32, (LANES, 2 * half), 0)
    expert = jnp.where(row < experts, row, row - experts)
    code = jnp.zeros((LANES, 2 * half), jnp.int32)
    for k in range(top):
        code = code + jnp.where(ids_ref[k : k + 1, :] == expert, codes_ref[k : k + 1, :], 0)
    digits = jnp.where(row < experts, code // DIGIT, code % DIGIT)
    digits = jnp.transpose(digits.astype(jnp.float32)).astype(tokens_ref.dtype)
    for i, out in enumerate(outs):
        out[:, :dim] = tokens_ref[pl.ds(i * half, half), :]
        out[:, dim:] = digits[i * half : (i + 1) * half, :]


def with_codes(experts, tokens, ids, codes):
    tok, dim = tokens.shape
    half = tok // 2
    return pl.pallas_call(
        functools.partial(rows_kernel, experts, ids.shape[1], half),
        out_shape=[jax.ShapeDtypeStruct((half, dim + LANES), tokens.dtype)] * 2,
        cost_estimate=small_cost(),
    )(tokens, ids.T, codes.T)


def body(tokens, expert_ids, gate_codes, w_gate, w_up, w_down):
    nodes = lax.axis_size("node")
    ring = nodes // SPAN
    far = ring // 2
    tok, top = expert_ids.shape
    half = tok // 2

    def chip_at(pos):
        return 2 * pos if pos < far else 2 * (ring - 1 - pos) + 1

    def perm(step):
        return [
            (chip_at(pos) * SPAN + core, chip_at((pos + step) % ring) * SPAN + core)
            for pos in range(ring)
            for core in range(SPAN)
        ]

    forward, backward = perm(1), perm(-1)
    swap = [(node, node ^ 1) for node in range(nodes)]
    expert = (lax.axis_index("node") // SPAN).astype(jnp.int32).reshape(1)

    rows = with_codes(ring, tokens, expert_ids, gate_codes)

    ahead = [[rows[0]], [rows[1]]]
    behind = [[rows[0]], [rows[1]]]
    parts = {}

    def send(s, after):
        for h in range(2):
            if s > 1:
                held = [parts[name] for name in after]
                pair, held = lax.optimization_barrier(([ahead[h][s - 1], behind[h][s - 1]], held))
                parts.update(zip(after, held))
                ahead[h][s - 1], behind[h][s - 1] = pair
            if s < far or h == 0:
                ahead[h].append(lax.ppermute(ahead[h][s - 1], "node", forward))
            if s < far or h == 1:
                behind[h].append(lax.ppermute(behind[h][s - 1], "node", backward))

    def work(offsets, after=()):
        names = [(offset, h) for offset in offsets for h in range(2)]
        blocks = []
        for offset, h in names:
            if abs(offset) == far:
                blocks.append((ahead, behind)[h][h][far])
            else:
                blocks.append((ahead if offset <= 0 else behind)[h][abs(offset)])
        held = [parts[name] for name in after]
        blocks, held = lax.optimization_barrier((blocks, held))
        parts.update(zip(after, held))
        parts.update(zip(names, expert_parts(ring, expert, blocks, own, other)))
        return names

    send(1, [])
    own, _ = lax.optimization_barrier(((w_gate, w_up, w_down), rows))
    other = []
    for weight in own:
        weight, *other = lax.optimization_barrier((weight, *other))
        other.append(lax.ppermute(weight, "node", swap))
    done = []
    for s in range(2, far + 1):
        send(s, done)
        done = work([0, -1, 1] if s == 2 else [1 - s, s - 1])
    work([far], done)
    parts[-far, 1] = parts[far, 1]

    streams = [(h, sign) for h in range(2) for sign in (1, -1)]
    ways = {1: forward, -1: backward}
    early = [(h, sign) for h, sign in streams if (h == 0) != (sign == 1)]
    late = [stream for stream in streams if stream not in early]
    came = {}
    for h, sign in early:
        came[h, sign] = lax.ppermute(parts[sign * (far - 1), h], "node", ways[sign])
    first = [parts[sign * far, h] for h, sign in late]
    first, held = lax.optimization_barrier((first, [came[stream] for stream in early]))
    came.update(zip(early, held))
    for (h, sign), total in zip(late, first):
        came[h, sign] = lax.ppermute(total, "node", ways[sign])
    for d in range(far - 1, 0, -1):
        for h, sign in early + late:
            at = d - 1 if (h, sign) in early else d
            if at:
                total = add(parts[sign * at, h], came[h, sign])
                came[h, sign] = lax.ppermute(total, "node", ways[sign])
    return close([t for h in range(2) for t in (parts[0, h], came[h, 1], came[h, -1])])


def solution(mesh):
    in_specs = (
        P(("groups", "node"), None),
        P(("groups", "node"), None),
        P(("groups", "node"), None),
        P(None, "node"),
        P(None, "node"),
        P("node", None),
    )
    out_specs = P(("groups", "node"), None)
    return jax.shard_map(body, mesh=mesh, in_specs=in_specs, out_specs=out_specs, check_vma=False)
```

time: 502 us -> 189 us (0.38)
  waiting for transfers between devices: 397 us -> 62.3 us
  Pallas kernels: 0 us -> 65.6 us
  matrix products: 61.9 us -> 0 us
  starting transfers between devices: 0.46 us -> 29.9 us
  local copies, waits for them, and re-layouts: 2.59 us -> 30 us
  blocking collectives: 23.3 us -> 0 us
  between operations: 13.5 us -> 0.19 us
    reduce_scatter x4 -> x0, waiting for transfers between devices: 271 us -> none  [body(): outs.append(lax.psum_scatter(part, 'node', scatter_dimension=0, tiled=True))]
    all_gather x4 -> x0, waiting for transfers between devices: 124 us -> none  [body(): rows = lax.all_gather(mine, 'node', axis=0, tiled=True)]
    pallas_call x0 -> x16, Pallas kernels: none -> 65.6 us  [the longest x4 39.9 us: expert_parts(): pl.pallas_call(functools.partial(expert_kernel, n, experts, dim, half), i...]
    ppermute x0 -> x31, waiting for transfers between devices: none -> 62.3 us  [the longest x12 22.3 us: body(): came[h, sign] = lax.ppermute(total, 'node', ways[sign])]
    dot_general x8 -> x0, matrix products: 61.9 us -> none  [the longest x4 41 us: body(): jnp.dot(hidden, w_down, preferred_element_type=jnp.float32)]
    unnamed x0 -> x70, local copies, waits for them, and re-layouts: none -> 30 us
    ppermute x0 -> x31, starting transfers between devices: none -> 29.9 us  [the longest x7 12.7 us: send(): ahead[h].append(lax.ppermute(ahead[h][s - 1], 'node', forward))]
    all_gather x1 -> x0, blocking collectives: 23.3 us -> none  [body(): lax.all_gather(jnp.concatenate([expert_ids, gate_codes], 1), 'node', axis...]
  transfers between devices with their start and end apart: 8 -> 31, of which waited for: 8 -> 18; matrix products, arithmetic and copies ran while one was open for 13% -> 0% of each run, Pallas kernels for 0% -> 32%
where the time goes in v4:
time: 189 us; the launch traced here: 188 us
  Pallas kernels  65.6 us (35%)
  waiting for transfers between devices  62.3 us (33%)
  local copies, waits for them, and re-layouts  30 us (16%)
  starting transfers between devices  29.9 us (16%)
    pallas_call x4, Pallas kernels, expert_parts(): pl.pallas_call(functools.partial(expert_kernel, n, experts, dim, half), i...  39.9 us
    unnamed x70, local copies, waits for them, and re-layouts  30 us
    ppermute x12, waiting for transfers between devices, body(): came[h, sign] = lax.ppermute(total, 'node', ways[sign])  22.3 us
    pallas_call x10, Pallas kernels, add(): pl.pallas_call(add_kernel, out_shape=jax.ShapeDtypeStruct(left.shape, lef...  20.4 us
    ppermute x7, waiting for transfers between devices, send(): ahead[h].append(lax.ppermute(ahead[h][s - 1], 'node', forward))  19.4 us
    ppermute x7, starting transfers between devices, send(): ahead[h].append(lax.ppermute(ahead[h][s - 1], 'node', forward))  12.7 us
    ppermute x3, waiting for transfers between devices, body(): other.append(lax.ppermute(weight, 'node', swap))  12.5 us
    ppermute x12, starting transfers between devices, body(): came[h, sign] = lax.ppermute(total, 'node', ways[sign])  11.7 us
  transfers between devices with their start and end apart: 31, of which 18 were waited for; matrix products, arithmetic and copies ran while one was open for 0% of the time, Pallas kernels for 32%

profile of v4, /device:TPU:0, one launch (start us, length us, event | category | flops | bytes accessed | tf_op | source)
XLA Modules:
  0.0 187.9 jit_solution(4831923186437744551)
XLA Ops:
  0.0 2.3 %shard_map.64 = (bf16[64,3712]{1,0:T(8,128)(2,1)}, bf16[64,3712]{1,0:T(8,128)(2,1)}) custom-call(bf16[128,3584]{1,0:T(8,128)(2,1)} %tokens_ref.1, s32[4,128]{1,0:T(4,128)} %bitcast.3, s32[4,128]{1,0:T(4,128)} %bitcast.4), custom_call_target="tpu_custom_call" | custom-call | flops 1024 | bytes 1024 | tf_op jit(solution)/shard_map/pallas_call | solution.py:134
  2.7 6.2 %collective-permute-done.8.refs_9_.refs_7_.refs_5_ = bf16[3584,512]{1,0:T(8,128)(2,1)S(1)} collective-permute-done((bf16[3584,512]{1,0:T(8,128)(2,1)}, bf16[3584,512]{1,0:T(8,128)(2,1)S(1)}, u32[]{:S(2)}, u32[]{:S(2)}) %collective-permute-start.8) | collective-permute-done | bytes 3670048 | tf_op jit(solution)/shard_map/ppermute | solution.py:199
  9.0 1.8 copy-done.3
  11.2 6.2 %collective-permute-done.9.refs_10_.refs_8_.refs_6_ = bf16[3584,512]{1,0:T(8,128)(2,1)S(1)} collective-permute-done((bf16[3584,512]{1,0:T(8,128)(2,1)}, bf16[3584,512]{1,0:T(8,128)(2,1)S(1)}, u32[]{:S(2)}, u32[]{:S(2)}) %collective-permute-start.9) | collective-permute-done | bytes 3670048 | tf_op jit(solution)/shard_map/ppermute | solution.py:199
  17.4 1.8 copy-done.5
  19.6 2.7 %collective-permute-start.4 = (bf16[64,3712]{1,0:T(8,128)(2,1)}, bf16[64,3712]{1,0:T(8,128)(2,1)S(1)}, u32[]{:S(2)}, u32[]{:S(2)}) collective-permute-start(bf16[64,3712]{1,0:T(8,128)(2,1)} %get-tuple-element.93.refs_0_), channel_id=1, source_target_pairs={{0,4},{1,5},{4,8},{5,9},{8,12},{9,13},{12,14},{13,15},{14,10},{15,... | collective-permute-start | bytes 1425416 | tf_op jit(solution)/shard_map/ppermute | solution.py:176
  22.3 2.0 %collective-permute-start = (bf16[64,3712]{1,0:T(8,128)(2,1)}, bf16[64,3712]{1,0:T(8,128)(2,1)S(1)}, u32[]{:S(2)}, u32[]{:S(2)}) collective-permute-start(bf16[64,3712]{1,0:T(8,128)(2,1)} %get-tuple-element.94.refs_1_), channel_id=1, source_target_pairs={{0,4},{1,5},{4,8},{5,9},{8,12},{9,13},{12,14},{13,15},{14,10},{15,... | collective-permute-start | bytes 1425416 | tf_op jit(solution)/shard_map/ppermute | solution.py:176
  24.4 9.8 %collective-permute-done.4.refs_2_ = bf16[64,3712]{1,0:T(8,128)(2,1)S(1)} collective-permute-done((bf16[64,3712]{1,0:T(8,128)(2,1)}, bf16[64,3712]{1,0:T(8,128)(2,1)S(1)}, u32[]{:S(2)}, u32[]{:S(2)}) %collective-permute-start.4) | collective-permute-done | bytes 475168 | tf_op jit(solution)/shard_map/ppermute | solution.py:176
  34.2 2.2 %collective-permute-done.5.refs_4_ = bf16[64,3712]{1,0:T(8,128)(2,1)} collective-permute-done((bf16[64,3712]{1,0:T(8,128)(2,1)}, bf16[64,3712]{1,0:T(8,128)(2,1)}, u32[]{:S(2)}, u32[]{:S(2)}) %collective-permute-start.5) | collective-permute-done | bytes 475168 | tf_op jit(solution)/shard_map/ppermute | solution.py:178
  36.4 1.6 collective-permute-start.6
  38.4 6.0 %collective-permute-done.refs_3_ = bf16[64,3712]{1,0:T(8,128)(2,1)S(1)} collective-permute-done((bf16[64,3712]{1,0:T(8,128)(2,1)}, bf16[64,3712]{1,0:T(8,128)(2,1)S(1)}, u32[]{:S(2)}, u32[]{:S(2)}) %collective-permute-start) | collective-permute-done | bytes 475168 | tf_op jit(solution)/shard_map/ppermute | solution.py:176
  44.4 2.1 %collective-permute-done.1.refs_5_ = bf16[64,3712]{1,0:T(8,128)(2,1)S(1)} collective-permute-done((bf16[64,3712]{1,0:T(8,128)(2,1)}, bf16[64,3712]{1,0:T(8,128)(2,1)S(1)}, u32[]{:S(2)}, u32[]{:S(2)}) %collective-permute-start.1) | collective-permute-done | bytes 475168 | tf_op jit(solution)/shard_map/ppermute | solution.py:178
  46.5 1.6 collective-permute-start.2
  48.5 2.0 %copy-done = bf16[3584,512]{1,0:T(8,128)(2,1)S(1)} copy-done((bf16[3584,512]{1,0:T(8,128)(2,1)S(1)}, bf16[3584,512]{1,0:T(8,128)(2,1)}, u32[]{:S(2)}) %copy-start) | copy-done | bytes 3670040
  50.5 2.0 %copy-done.1 = bf16[3584,512]{1,0:T(8,128)(2,1)S(1)} copy-done((bf16[3584,512]{1,0:T(8,128)(2,1)S(1)}, bf16[3584,512]{1,0:T(8,128)(2,1)}, u32[]{:S(2)}) %copy-start.1) | copy-done | bytes 3670040
  52.6 2.0 %copy-done.2 = bf16[512,3584]{1,0:T(8,128)(2,1)S(1)} copy-done((bf16[512,3584]{1,0:T(8,128)(2,1)S(1)}, bf16[512,3584]{1,0:T(8,128)(2,1)}, u32[]{:S(2)}) %copy-start.2) | copy-done | bytes 3670040
  54.6 2.0 %copy-done.4 = bf16[3584,512]{1,0:T(8,128)(2,1)S(1)} copy-done((bf16[3584,512]{1,0:T(8,128)(2,1)S(1)}, bf16[3584,512]{1,0:T(8,128)(2,1)}, u32[]{:S(2)}) %copy-start.4) | copy-done | bytes 3670040
  56.7 2.0 %copy-done.6 = bf16[3584,512]{1,0:T(8,128)(2,1)S(1)} copy-done((bf16[3584,512]{1,0:T(8,128)(2,1)S(1)}, bf16[3584,512]{1,0:T(8,128)(2,1)}, u32[]{:S(2)}) %copy-start.6) | copy-done | bytes 3670040
  60.7 13.0 %shard_map.65 = (bf16[64,3584]{1,0:T(8,128)(2,1)S(1)}, bf16[64,3584]{1,0:T(8,128)(2,1)S(1)}, bf16[64,3584]{1,0:T(8,128)(2,1)S(1)}, bf16[64,3584]{1,0:T(8,128)(2,...) custom-call(s32[1]{0:T(128)} %bitcast.2.expert_ref, bf16[64,3712]{1,0:T(8,128)(2,1)S(1)} %copy-done.7, ...), custom_call_target="tpu_custom_call" | custom-call | flops 1024 | bytes 1024 | tf_op jit(solution)/shard_map/pallas_call | solution.py:71
  77.7 1.6 collective-permute-start.13
  79.8 1.6 collective-permute-start.11
  81.8 9.9 %shard_map.66 = (bf16[64,3584]{1,0:T(8,128)(2,1)S(1)}, bf16[64,3584]{1,0:T(8,128)(2,1)S(1)}, bf16[64,3584]{1,0:T(8,128)(2,1)S(1)}, bf16[64,3584]{1,0:T(8,128)(2,1)S(1)}) custom-call(s32[1]{0:T(128)} %bitcast.2.expert_ref, bf16[64,3712]{1,0:T(8,128)(2,1)S(1)} %collective-permute-done.6.refs_0_, bf16[64,3712]{1,0:T(8,128)(2,1)S(1)} %collective-permute-done.2.refs_1_, ...), custom_call_target="tpu_custom_call" | custom-call | flops 1024 | bytes 1024 | tf_op jit(solution)/shard_map/pallas_call | solution.py:71
  94.9 3.6 %collective-permute-done.11.refs_1_ = bf16[64,3712]{1,0:T(8,128)(2,1)S(1)} collective-permute-done((bf16[64,3712]{1,0:T(8,128)(2,1)S(1)}, bf16[64,3712]{1,0:T(8,128)(2,1)S(1)}, u32[]{:S(2)}, u32[]{:S(2)}) %collective-permute-start.11) | collective-permute-done | bytes 475168 | tf_op jit(solution)/shard_map/ppermute | solution.py:176
  98.5 2.0 %collective-permute-done.12.refs_3_ = bf16[64,3712]{1,0:T(8,128)(2,1)S(1)} collective-permute-done((bf16[64,3712]{1,0:T(8,128)(2,1)S(1)}, bf16[64,3712]{1,0:T(8,128)(2,1)S(1)}, u32[]{:S(2)}, u32[]{:S(2)}) %collective-permute-start.12) | collective-permute-done | bytes 475168 | tf_op jit(solution)/shard_map/ppermute | solution.py:178
  101.0 1.6 collective-permute-start.15
  102.5 9.9 %shard_map.67 = (bf16[64,3584]{1,0:T(8,128)(2,1)S(1)}, bf16[64,3584]{1,0:T(8,128)(2,1)S(1)}, bf16[64,3584]{1,0:T(8,128)(2,1)S(1)}, bf16[64,3584]{1,0:T(8,128)(2,1)S(1)}) custom-call(s32[1]{0:T(128)} %bitcast.2.expert_ref, bf16[64,3712]{1,0:T(8,128)(2,1)S(1)} %collective-permute-done.13.refs_0_, bf16[64,3712]{1,0:T(8,128)(2,1)S(1)} %collective-permute-done.11.refs_1_, ...), custom_call_target="tpu_custom_call" | custom-call | flops 1024 | bytes 1024 | tf_op jit(solution)/shard_map/pallas_call | solution.py:71
  113.0 1.6 collective-permute-start.18
  114.6 7.1 %shard_map.68 = (bf16[64,3584]{1,0:T(8,128)(2,1)S(1)}, bf16[64,3584]{1,0:T(8,128)(2,1)S(1)}) custom-call(s32[1]{0:T(128)} %bitcast.2.expert_ref, bf16[64,3712]{1,0:T(8,128)(2,1)S(1)} %collective-permute-done.15.refs_0_, bf16[64,3712]{1,0:T(8,128)(2,1)S(1)} %collective-permute-done.16.refs_1_, bf16[3584,512]{1,0:T(8,128)(2,1)S(1)} %copy-done, ...), custom_call_target="tpu_custom_call" | custom-call | flops 1024 | bytes 1024 | tf_op jit(solution)/shard_map/pallas_call | solution.py:71
  123.5 2.0 %collective-permute-start.19 = (bf16[64,3584]{1,0:T(8,128)(2,1)S(1)}, bf16[64,3584]{1,0:T(8,128)(2,1)S(1)}, u32[]{:S(2)}, u32[]{:S(2)}) collective-permute-start(bf16[64,3584]{1,0:T(8,128)(2,1)S(1)} %get-tuple-element.157), channel_id=1, source_target_pairs={{0,4},{1,5},{4,8},{5,9},{8,12},{9,13},{12,14},{13,15},{14,10},{15,... | collective-permute-start | bytes 1376264 | tf_op jit(solution)/shard_map/ppermute | solution.py:218
  125.6 7.0 %collective-permute-done.27.right_ref = bf16[64,3584]{1,0:T(8,128)(2,1)S(1)} collective-permute-done((bf16[64,3584]{1,0:T(8,128)(2,1)S(1)}, bf16[64,3584]{1,0:T(8,128)(2,1)S(1)}, u32[]{:S(2)}, u32[]{:S(2)}) %collective-permute-start.27) | collective-permute-done | bytes 458784 | tf_op jit(solution)/shard_map/ppermute | solution.py:218
  133.4 2.0 %shard_map.76 = bf16[64,3584]{1,0:T(8,128)(2,1)} custom-call(bf16[64,3584]{1,0:T(8,128)(2,1)} %copy-done.20, bf16[64,3584]{1,0:T(8,128)(2,1)} %copy-done.34), custom_call_target="tpu_custom_call" | custom-call | flops 1024 | bytes 1024 | tf_op jit(solution)/shard_map/pallas_call | solution.py:92
  136.2 2.0 %shard_map.69 = bf16[64,3584]{1,0:T(8,128)(2,1)} custom-call(bf16[64,3584]{1,0:T(8,128)(2,1)} %copy-done.19, bf16[64,3584]{1,0:T(8,128)(2,1)} %copy-done.33), custom_call_target="tpu_custom_call" | custom-call | flops 1024 | bytes 1024 | tf_op jit(solution)/shard_map/pallas_call | solution.py:92
  138.2 2.0 %collective-permute-start.20 = (bf16[64,3584]{1,0:T(8,128)(2,1)}, bf16[64,3584]{1,0:T(8,128)(2,1)S(1)}, u32[]{:S(2)}, u32[]{:S(2)}) collective-permute-start(bf16[64,3584]{1,0:T(8,128)(2,1)} %shard_map.69), channel_id=1, source_target_pairs={{0,4},{1,5},{4,8},{5,9},{8,12},{9,13},{12,14},{13,15},{14,10},{15,... | collective-permute-start | bytes 1376264 | tf_op jit(solution)/shard_map/ppermute | solution.py:224
  140.2 2.0 %shard_map.74 = bf16[64,3584]{1,0:T(8,128)(2,1)} custom-call(bf16[64,3584]{1,0:T(8,128)(2,1)} %copy-done.18, bf16[64,3584]{1,0:T(8,128)(2,1)} %copy-done.26), custom_call_target="tpu_custom_call" | custom-call | flops 1024 | bytes 1024 | tf_op jit(solution)/shard_map/pallas_call | solution.py:92
  142.3 1.6 collective-permute-start.25
  143.8 2.1 %shard_map.72 = bf16[64,3584]{1,0:T(8,128)(2,1)} custom-call(bf16[64,3584]{1,0:T(8,128)(2,1)} %copy-done.17, bf16[64,3584]{1,0:T(8,128)(2,1)} %copy-done.25), custom_call_target="tpu_custom_call" | custom-call | flops 1024 | bytes 1024 | tf_op jit(solution)/shard_map/pallas_call | solution.py:92
  147.8 2.0 %shard_map.77 = bf16[64,3584]{1,0:T(8,128)(2,1)} custom-call(bf16[64,3584]{1,0:T(8,128)(2,1)} %copy-done.16, bf16[64,3584]{1,0:T(8,128)(2,1)} %copy-done.31), custom_call_target="tpu_custom_call" | custom-call | flops 1024 | bytes 1024 | tf_op jit(solution)/shard_map/pallas_call | solution.py:92
  151.9 2.0 %shard_map.70 = bf16[64,3584]{1,0:T(8,128)(2,1)} custom-call(bf16[64,3584]{1,0:T(8,128)(2,1)} %copy-done.15, bf16[64,3584]{1,0:T(8,128)(2,1)} %copy-done.32), custom_call_target="tpu_custom_call" | custom-call | flops 1024 | bytes 1024 | tf_op jit(solution)/shard_map/pallas_call | solution.py:92
  153.9 1.6 collective-permute-start.21
  155.5 5.4 %collective-permute-done.25.right_ref = bf16[64,3584]{1,0:T(8,128)(2,1)S(1)} collective-permute-done((bf16[64,3584]{1,0:T(8,128)(2,1)}, bf16[64,3584]{1,0:T(8,128)(2,1)S(1)}, u32[]{:S(2)}, u32[]{:S(2)}) %collective-permute-start.25) | collective-permute-done | bytes 458784 | tf_op jit(solution)/shard_map/ppermute | solution.py:224
  161.7 2.0 %shard_map.75 = bf16[64,3584]{1,0:T(8,128)(2,1)} custom-call(bf16[64,3584]{1,0:T(8,128)(2,1)} %copy-done.14, bf16[64,3584]{1,0:T(8,128)(2,1)} %copy-done.30), custom_call_target="tpu_custom_call" | custom-call | flops 1024 | bytes 1024 | tf_op jit(solution)/shard_map/pallas_call | solution.py:92
  163.7 1.6 collective-permute-start.26
  166.1 2.1 %shard_map.73 = bf16[64,3584]{1,0:T(8,128)(2,1)} custom-call(bf16[64,3584]{1,0:T(8,128)(2,1)} %copy-done.13, bf16[64,3584]{1,0:T(8,128)(2,1)} %copy-done.27), custom_call_target="tpu_custom_call" | custom-call | flops 1024 | bytes 1024 | tf_op jit(solution)/shard_map/pallas_call | solution.py:92
  170.4 2.0 %shard_map.78 = bf16[64,3584]{1,0:T(8,128)(2,1)} custom-call(bf16[64,3584]{1,0:T(8,128)(2,1)} %copy-done.12, bf16[64,3584]{1,0:T(8,128)(2,1)} %copy-done.28), custom_call_target="tpu_custom_call" | custom-call | flops 1024 | bytes 1024 | tf_op jit(solution)/shard_map/pallas_call | solution.py:92
  173.5 2.0 %shard_map.71 = bf16[64,3584]{1,0:T(8,128)(2,1)} custom-call(bf16[64,3584]{1,0:T(8,128)(2,1)} %copy-done.11, bf16[64,3584]{1,0:T(8,128)(2,1)} %copy-done.29), custom_call_target="tpu_custom_call" | custom-call | flops 1024 | bytes 1024 | tf_op jit(solution)/shard_map/pallas_call | solution.py:92
  175.5 1.7 collective-permute-start.22
  178.6 4.8 %collective-permute-done.30.refs_5_ = bf16[64,3584]{1,0:T(8,128)(2,1)S(1)} collective-permute-done((bf16[64,3584]{1,0:T(8,128)(2,1)}, bf16[64,3584]{1,0:T(8,128)(2,1)S(1)}, u32[]{:S(2)}, u32[]{:S(2)}) %collective-permute-start.30) | collective-permute-done | bytes 458784 | tf_op jit(solution)/shard_map/ppermute | solution.py:224
  185.0 3.0 %shard_map.79 = bf16[128,3584]{1,0:T(8,128)(2,1)} custom-call(bf16[64,3584]{1,0:T(8,128)(2,1)} %copy-done.9, bf16[64,3584]{1,0:T(8,128)(2,1)} %copy-done.24, bf16[64,3584]{1,0:T(8,128)(2,1)} %copy-done.22, bf16[64,3584]{1,0:T(8,128)(2,1)} %copy-done.10, bf16[64,3584]{1,0:T(8,128)(2,1)} %copy-done.21, bf16[64,3584]{1,0:T(8,128)(2,1)} %copy-done.23), custom_call_target="tpu_custom_call" | custom-call | flops 1024 | bytes 1024 | tf_op jit(solution)/shard_map/pallas_call | solution.py:110
  (100 shorter events, 28.2 us)
Async XLA Ops:
  2.3 6.7 %collective-permute-start.8 = (bf16[3584,512]{1,0:T(8,128)(2,1)}, bf16[3584,512]{1,0:T(8,128)(2,1)S(1)}, u32[]{:S(2)}, u32[]{:S(2)}) collective-permute-start(bf16[3584,512]{1,0:T(8,128)(2,1)} %refs_2_), channel_id=1, source_target_pairs={{0,1},{1,0},{2,3},{3,2},{4,5},{5,4},{6,7},{7,6},{8,9},{9,8},{10,11... | collective-permute-start | bytes 11010056 | tf_op jit(solution)/shard_map/ppermute | solution.py:199
  9.0 1.8 copy-start.3
  10.8 6.6 %collective-permute-start.9 = (bf16[3584,512]{1,0:T(8,128)(2,1)}, bf16[3584,512]{1,0:T(8,128)(2,1)S(1)}, u32[]{:S(2)}, u32[]{:S(2)}) collective-permute-start(bf16[3584,512]{1,0:T(8,128)(2,1)} %refs_3_), channel_id=1, source_target_pairs={{0,1},{1,0},{2,3},{3,2},{4,5},{5,4},{6,7},{7,6},{8,9},{9,8},{10,11... | collective-permute-start | bytes 11010056 | tf_op jit(solution)/shard_map/ppermute | solution.py:199
  17.4 1.8 copy-start.5
  19.2 29.2 %collective-permute-start.10 = (bf16[512,3584]{1,0:T(8,128)(2,1)}, bf16[512,3584]{1,0:T(8,128)(2,1)}, u32[]{:S(2)}, u32[]{:S(2)}) collective-permute-start(bf16[512,3584]{1,0:T(8,128)(2,1)} %refs_4_.2), channel_id=1, source_target_pairs={{0,1},{1,0},{2,3},{3,2},{4,5},{5,4},{6,7},{7,6},{8,9},{9,8},{10,11... | collective-permute-start | bytes 11010056 | tf_op jit(solution)/shard_map/ppermute | solution.py:199
  19.6 14.6 %collective-permute-start.4 = (bf16[64,3712]{1,0:T(8,128)(2,1)}, bf16[64,3712]{1,0:T(8,128)(2,1)S(1)}, u32[]{:S(2)}, u32[]{:S(2)}) collective-permute-start(bf16[64,3712]{1,0:T(8,128)(2,1)} %get-tuple-element.93.refs_0_), channel_id=1, source_target_pairs={{0,4},{1,5},{4,8},{5,9},{8,12},{9,13},{12,14},{13,15},{14,10},{15,... | collective-permute-start | bytes 1425416 | tf_op jit(solution)/shard_map/ppermute | solution.py:176
  22.3 14.0 %collective-permute-start.5 = (bf16[64,3712]{1,0:T(8,128)(2,1)}, bf16[64,3712]{1,0:T(8,128)(2,1)}, u32[]{:S(2)}, u32[]{:S(2)}) collective-permute-start(bf16[64,3712]{1,0:T(8,128)(2,1)} %get-tuple-element.93.refs_0_), channel_id=1, source_target_pairs={{0,2},{1,3},{4,0},{5,1},{8,4},{9,5},{12,8},{13,9},{14,12},{15,13},... | collective-permute-start | bytes 1425416 | tf_op jit(solution)/shard_map/ppermute | solution.py:178
  22.3 22.0 %collective-permute-start = (bf16[64,3712]{1,0:T(8,128)(2,1)}, bf16[64,3712]{1,0:T(8,128)(2,1)S(1)}, u32[]{:S(2)}, u32[]{:S(2)}) collective-permute-start(bf16[64,3712]{1,0:T(8,128)(2,1)} %get-tuple-element.94.refs_1_), channel_id=1, source_target_pairs={{0,4},{1,5},{4,8},{5,9},{8,12},{9,13},{12,14},{13,15},{14,10},{15,... | collective-permute-start | bytes 1425416 | tf_op jit(solution)/shard_map/ppermute | solution.py:176
  24.4 22.1 %collective-permute-start.1 = (bf16[64,3712]{1,0:T(8,128)(2,1)}, bf16[64,3712]{1,0:T(8,128)(2,1)S(1)}, u32[]{:S(2)}, u32[]{:S(2)}) collective-permute-start(bf16[64,3712]{1,0:T(8,128)(2,1)} %get-tuple-element.94.refs_1_), channel_id=1, source_target_pairs={{0,2},{1,3},{4,0},{5,1},{8,4},{9,5},{12,8},{13,9},{14,12},{15,13},... | collective-permute-start | bytes 1425416 | tf_op jit(solution)/shard_map/ppermute | solution.py:178
  36.4 41.3 %collective-permute-start.6 = (bf16[64,3712]{1,0:T(8,128)(2,1)S(1)}, bf16[64,3712]{1,0:T(8,128)(2,1)S(1)}, u32[]{:S(2)}, u32[]{:S(2)}) collective-permute-start(bf16[64,3712]{1,0:T(8,128)(2,1)S(1)} %collective-permute-done.4.refs_2_), channel_id=1, source_target_pairs={{0,4},{1,5},{4,8},{5,9},{8,12},{9,13},{12,14},{13,15},{14,10},{15,... | collective-permute-start | bytes 1425416 | tf_op jit(solution)/shard_map/ppermute | solution.py:176
  38.0 39.7 %collective-permute-start.7 = (bf16[64,3712]{1,0:T(8,128)(2,1)}, bf16[64,3712]{1,0:T(8,128)(2,1)S(1)}, u32[]{:S(2)}, u32[]{:S(2)}) collective-permute-start(bf16[64,3712]{1,0:T(8,128)(2,1)} %collective-permute-done.5.refs_4_), channel_id=1, source_target_pairs={{0,2},{1,3},{4,0},{5,1},{8,4},{9,5},{12,8},{13,9},{14,12},{15,13},... | collective-permute-start | bytes 1425416 | tf_op jit(solution)/shard_map/ppermute | solution.py:178
  46.5 33.3 %collective-permute-start.2 = (bf16[64,3712]{1,0:T(8,128)(2,1)S(1)}, bf16[64,3712]{1,0:T(8,128)(2,1)S(1)}, u32[]{:S(2)}, u32[]{:S(2)}) collective-permute-start(bf16[64,3712]{1,0:T(8,128)(2,1)S(1)} %collective-permute-done.refs_3_), channel_id=1, source_target_pairs={{0,4},{1,5},{4,8},{5,9},{8,12},{9,13},{12,14},{13,15},{14,10},{15,... | collective-permute-start | bytes 1425416 | tf_op jit(solution)/shard_map/ppermute | solution.py:176
  48.0 31.7 %collective-permute-start.3 = (bf16[64,3712]{1,0:T(8,128)(2,1)S(1)}, bf16[64,3712]{1,0:T(8,128)(2,1)S(1)}, u32[]{:S(2)}, u32[]{:S(2)}) collective-permute-start(bf16[64,3712]{1,0:T(8,128)(2,1)S(1)} %collective-permute-done.1.refs_5_), channel_id=1, source_target_pairs={{0,2},{1,3},{4,0},{5,1},{8,4},{9,5},{12,8},{13,9},{14,12},{15,13},... | collective-permute-start | bytes 1425416 | tf_op jit(solution)/shard_map/ppermute | solution.py:178
  48.5 2.0 %copy-start = (bf16[3584,512]{1,0:T(8,128)(2,1)S(1)}, bf16[3584,512]{1,0:T(8,128)(2,1)}, u32[]{:S(2)}) copy-start(bf16[3584,512]{1,0:T(8,128)(2,1)} %refs_2_) | copy-start | bytes 11010052
  50.5 2.0 %copy-start.1 = (bf16[3584,512]{1,0:T(8,128)(2,1)S(1)}, bf16[3584,512]{1,0:T(8,128)(2,1)}, u32[]{:S(2)}) copy-start(bf16[3584,512]{1,0:T(8,128)(2,1)} %refs_3_) | copy-start | bytes 11010052
  52.6 2.0 %copy-start.2 = (bf16[512,3584]{1,0:T(8,128)(2,1)S(1)}, bf16[512,3584]{1,0:T(8,128)(2,1)}, u32[]{:S(2)}) copy-start(bf16[512,3584]{1,0:T(8,128)(2,1)} %refs_4_.2) | copy-start | bytes 11010052
  54.6 2.0 %copy-start.4 = (bf16[3584,512]{1,0:T(8,128)(2,1)S(1)}, bf16[3584,512]{1,0:T(8,128)(2,1)}, u32[]{:S(2)}) copy-start(bf16[3584,512]{1,0:T(8,128)(2,1)} %copy-done.3) | copy-start | bytes 11010052
  56.7 2.0 %copy-start.6 = (bf16[3584,512]{1,0:T(8,128)(2,1)S(1)}, bf16[3584,512]{1,0:T(8,128)(2,1)}, u32[]{:S(2)}) copy-start(bf16[3584,512]{1,0:T(8,128)(2,1)} %copy-done.5) | copy-start | bytes 11010052
  58.7 1.0 copy-start.7
  59.7 1.0 copy-start.8
  77.7 14.0 %copy-start.12 = (bf16[64,3584]{1,0:T(8,128)(2,1)}, bf16[64,3584]{1,0:T(8,128)(2,1)S(1)}, u32[]{:S(2)}) copy-start(bf16[64,3584]{1,0:T(8,128)(2,1)S(1)} %get-tuple-element.165.left_ref) | copy-start | bytes 1376260
  77.7 17.2 %collective-permute-start.13 = (bf16[64,3712]{1,0:T(8,128)(2,1)S(1)}, bf16[64,3712]{1,0:T(8,128)(2,1)S(1)}, u32[]{:S(2)}, u32[]{:S(2)}) collective-permute-start(bf16[64,3712]{1,0:T(8,128)(2,1)S(1)} %collective-permute-done.6.refs_0_), channel_id=1, source_target_pairs={{0,4},{1,5},{4,8},{5,9},{8,12},{9,13},{12,14},{13,15},{14,10},{15,... | collective-permute-start | bytes 1425416 | tf_op jit(solution)/shard_map/ppermute | solution.py:176
  79.3 15.6 %collective-permute-start.14 = (bf16[64,3712]{1,0:T(8,128)(2,1)S(1)}, bf16[64,3712]{1,0:T(8,128)(2,1)S(1)}, u32[]{:S(2)}, u32[]{:S(2)}) collective-permute-start(bf16[64,3712]{1,0:T(8,128)(2,1)S(1)} %collective-permute-done.7.refs_2_), channel_id=1, source_target_pairs={{0,2},{1,3},{4,0},{5,1},{8,4},{9,5},{12,8},{13,9},{14,12},{15,13},... | collective-permute-start | bytes 1425416 | tf_op jit(solution)/shard_map/ppermute | solution.py:178
  79.8 18.7 %collective-permute-start.11 = (bf16[64,3712]{1,0:T(8,128)(2,1)S(1)}, bf16[64,3712]{1,0:T(8,128)(2,1)S(1)}, u32[]{:S(2)}, u32[]{:S(2)}) collective-permute-start(bf16[64,3712]{1,0:T(8,128)(2,1)S(1)} %collective-permute-done.2.refs_1_), channel_id=1, source_target_pairs={{0,4},{1,5},{4,8},{5,9},{8,12},{9,13},{12,14},{13,15},{14,10},{15,... | collective-permute-start | bytes 1425416 | tf_op jit(solution)/shard_map/ppermute | solution.py:176
  81.3 19.2 %collective-permute-start.12 = (bf16[64,3712]{1,0:T(8,128)(2,1)S(1)}, bf16[64,3712]{1,0:T(8,128)(2,1)S(1)}, u32[]{:S(2)}, u32[]{:S(2)}) collective-permute-start(bf16[64,3712]{1,0:T(8,128)(2,1)S(1)} %collective-permute-done.3.refs_3_), channel_id=1, source_target_pairs={{0,2},{1,3},{4,0},{5,1},{8,4},{9,5},{12,8},{13,9},{14,12},{15,13},... | collective-permute-start | bytes 1425416 | tf_op jit(solution)/shard_map/ppermute | solution.py:178
  93.3 0.8 copy-start.17
  100.5 12.0 %collective-permute-start.16 = (bf16[64,3712]{1,0:T(8,128)(2,1)S(1)}, bf16[64,3712]{1,0:T(8,128)(2,1)S(1)}, u32[]{:S(2)}, u32[]{:S(2)}) collective-permute-start(bf16[64,3712]{1,0:T(8,128)(2,1)S(1)} %collective-permute-done.12.refs_3_), channel_id=1, source_target_pairs={{0,2},{1,3},{4,0},{5,1},{8,4},{9,5},{12,8},{13,9},{14,12},{15,13},... | collective-permute-start | bytes 1425416 | tf_op jit(solution)/shard_map/ppermute | solution.py:178
  101.0 11.5 %collective-permute-start.15 = (bf16[64,3712]{1,0:T(8,128)(2,1)S(1)}, bf16[64,3712]{1,0:T(8,128)(2,1)S(1)}, u32[]{:S(2)}, u32[]{:S(2)}) collective-permute-start(bf16[64,3712]{1,0:T(8,128)(2,1)S(1)} %collective-permute-done.13.refs_0_), channel_id=1, source_target_pairs={{0,4},{1,5},{4,8},{5,9},{8,12},{9,13},{12,14},{13,15},{14,10},{15,... | collective-permute-start | bytes 1425416 | tf_op jit(solution)/shard_map/ppermute | solution.py:176
  112.5 9.3 %copy-start.19 = (bf16[64,3584]{1,0:T(8,128)(2,1)}, bf16[64,3584]{1,0:T(8,128)(2,1)S(1)}, u32[]{:S(2)}) copy-start(bf16[64,3584]{1,0:T(8,128)(2,1)S(1)} %get-tuple-element.150.left_ref) | copy-start | bytes 1376260
  112.5 9.3 %copy-start.20 = (bf16[64,3584]{1,0:T(8,128)(2,1)}, bf16[64,3584]{1,0:T(8,128)(2,1)S(1)}, u32[]{:S(2)}) copy-start(bf16[64,3584]{1,0:T(8,128)(2,1)S(1)} %get-tuple-element.167.left_ref) | copy-start | bytes 1376260
  112.5 10.3 %collective-permute-start.17 = (bf16[64,3584]{1,0:T(8,128)(2,1)S(1)}, bf16[64,3584]{1,0:T(8,128)(2,1)S(1)}, u32[]{:S(2)}, u32[]{:S(2)}) collective-permute-start(bf16[64,3584]{1,0:T(8,128)(2,1)S(1)} %get-tuple-element.155), channel_id=1, source_target_pairs={{0,2},{1,3},{4,0},{5,1},{8,4},{9,5},{12,8},{13,9},{14,12},{15,13},... | collective-permute-start | bytes 1376264 | tf_op jit(solution)/shard_map/ppermute | solution.py:213
  113.0 10.5 %collective-permute-start.18 = (bf16[64,3584]{1,0:T(8,128)(2,1)S(1)}, bf16[64,3584]{1,0:T(8,128)(2,1)S(1)}, u32[]{:S(2)}, u32[]{:S(2)}) collective-permute-start(bf16[64,3584]{1,0:T(8,128)(2,1)S(1)} %get-tuple-element.156), channel_id=1, source_target_pairs={{0,4},{1,5},{4,8},{5,9},{8,12},{9,13},{12,14},{13,15},{14,10},{15,... | collective-permute-start | bytes 1376264 | tf_op jit(solution)/shard_map/ppermute | solution.py:213
  122.8 21.0 %copy-start.25 = (bf16[64,3584]{1,0:T(8,128)(2,1)}, bf16[64,3584]{1,0:T(8,128)(2,1)S(1)}, u32[]{:S(2)}) copy-start(bf16[64,3584]{1,0:T(8,128)(2,1)S(1)} %collective-permute-done.17.right_ref) | copy-start | bytes 1376260
  123.5 16.7 %copy-start.26 = (bf16[64,3584]{1,0:T(8,128)(2,1)}, bf16[64,3584]{1,0:T(8,128)(2,1)S(1)}, u32[]{:S(2)}) copy-start(bf16[64,3584]{1,0:T(8,128)(2,1)S(1)} %collective-permute-done.18.right_ref) | copy-start | bytes 1376260
  123.5 9.1 %collective-permute-start.27 = (bf16[64,3584]{1,0:T(8,128)(2,1)S(1)}, bf16[64,3584]{1,0:T(8,128)(2,1)S(1)}, u32[]{:S(2)}, u32[]{:S(2)}) collective-permute-start(bf16[64,3584]{1,0:T(8,128)(2,1)S(1)} %get-tuple-element.168), channel_id=1, source_target_pairs={{0,2},{1,3},{4,0},{5,1},{8,4},{9,5},{12,8},{13,9},{14,12},{15,13},... | collective-permute-start | bytes 1376264 | tf_op jit(solution)/shard_map/ppermute | solution.py:218
  123.5 11.9 %collective-permute-start.19 = (bf16[64,3584]{1,0:T(8,128)(2,1)S(1)}, bf16[64,3584]{1,0:T(8,128)(2,1)S(1)}, u32[]{:S(2)}, u32[]{:S(2)}) collective-permute-start(bf16[64,3584]{1,0:T(8,128)(2,1)S(1)} %get-tuple-element.157), channel_id=1, source_target_pairs={{0,4},{1,5},{4,8},{5,9},{8,12},{9,13},{12,14},{13,15},{14,10},{15,... | collective-permute-start | bytes 1376264 | tf_op jit(solution)/shard_map/ppermute | solution.py:218
  135.4 11.7 %collective-permute-start.28 = (bf16[64,3584]{1,0:T(8,128)(2,1)}, bf16[64,3584]{1,0:T(8,128)(2,1)S(1)}, u32[]{:S(2)}, u32[]{:S(2)}) collective-permute-start(bf16[64,3584]{1,0:T(8,128)(2,1)} %shard_map.76), channel_id=1, source_target_pairs={{0,2},{1,3},{4,0},{5,1},{8,4},{9,5},{12,8},{13,9},{14,12},{15,13},... | collective-permute-start | bytes 1376264 | tf_op jit(solution)/shard_map/ppermute | solution.py:224
  138.2 12.9 %collective-permute-start.20 = (bf16[64,3584]{1,0:T(8,128)(2,1)}, bf16[64,3584]{1,0:T(8,128)(2,1)S(1)}, u32[]{:S(2)}, u32[]{:S(2)}) collective-permute-start(bf16[64,3584]{1,0:T(8,128)(2,1)} %shard_map.69), channel_id=1, source_target_pairs={{0,4},{1,5},{4,8},{5,9},{8,12},{9,13},{12,14},{13,15},{14,10},{15,... | collective-permute-start | bytes 1376264 | tf_op jit(solution)/shard_map/ppermute | solution.py:224
  142.3 18.7 %collective-permute-start.25 = (bf16[64,3584]{1,0:T(8,128)(2,1)}, bf16[64,3584]{1,0:T(8,128)(2,1)S(1)}, u32[]{:S(2)}, u32[]{:S(2)}) collective-permute-start(bf16[64,3584]{1,0:T(8,128)(2,1)} %shard_map.74), channel_id=1, source_target_pairs={{0,4},{1,5},{4,8},{5,9},{8,12},{9,13},{12,14},{13,15},{14,10},{15,... | collective-permute-start | bytes 1376264 | tf_op jit(solution)/shard_map/ppermute | solution.py:224
  145.9 19.4 %collective-permute-start.23 = (bf16[64,3584]{1,0:T(8,128)(2,1)}, bf16[64,3584]{1,0:T(8,128)(2,1)S(1)}, u32[]{:S(2)}, u32[]{:S(2)}) collective-permute-start(bf16[64,3584]{1,0:T(8,128)(2,1)} %shard_map.72), channel_id=1, source_target_pairs={{0,2},{1,3},{4,0},{5,1},{8,4},{9,5},{12,8},{13,9},{14,12},{15,13},... | collective-permute-start | bytes 1376264 | tf_op jit(solution)/shard_map/ppermute | solution.py:224
  149.9 19.7 %collective-permute-start.29 = (bf16[64,3584]{1,0:T(8,128)(2,1)}, bf16[64,3584]{1,0:T(8,128)(2,1)S(1)}, u32[]{:S(2)}, u32[]{:S(2)}) collective-permute-start(bf16[64,3584]{1,0:T(8,128)(2,1)} %shard_map.77), channel_id=1, source_target_pairs={{0,2},{1,3},{4,0},{5,1},{8,4},{9,5},{12,8},{13,9},{14,12},{15,13},... | collective-permute-start | bytes 1376264 | tf_op jit(solution)/shard_map/ppermute | solution.py:224
  153.9 18.8 %collective-permute-start.21 = (bf16[64,3584]{1,0:T(8,128)(2,1)}, bf16[64,3584]{1,0:T(8,128)(2,1)S(1)}, u32[]{:S(2)}, u32[]{:S(2)}) collective-permute-start(bf16[64,3584]{1,0:T(8,128)(2,1)} %shard_map.70), channel_id=1, source_target_pairs={{0,4},{1,5},{4,8},{5,9},{8,12},{9,13},{12,14},{13,15},{14,10},{15,... | collective-permute-start | bytes 1376264 | tf_op jit(solution)/shard_map/ppermute | solution.py:224
  163.7 14.9 %collective-permute-start.26 = (bf16[64,3584]{1,0:T(8,128)(2,1)}, bf16[64,3584]{1,0:T(8,128)(2,1)S(1)}, u32[]{:S(2)}, u32[]{:S(2)}) collective-permute-start(bf16[64,3584]{1,0:T(8,128)(2,1)} %shard_map.75), channel_id=1, source_target_pairs={{0,4},{1,5},{4,8},{5,9},{8,12},{9,13},{12,14},{13,15},{14,10},{15,... | collective-permute-start | bytes 1376264 | tf_op jit(solution)/shard_map/ppermute | solution.py:224
  168.2 10.4 %collective-permute-start.24 = (bf16[64,3584]{1,0:T(8,128)(2,1)}, bf16[64,3584]{1,0:T(8,128)(2,1)S(1)}, u32[]{:S(2)}, u32[]{:S(2)}) collective-permute-start(bf16[64,3584]{1,0:T(8,128)(2,1)} %shard_map.73), channel_id=1, source_target_pairs={{0,2},{1,3},{4,0},{5,1},{8,4},{9,5},{12,8},{13,9},{14,12},{15,13},... | collective-permute-start | bytes 1376264 | tf_op jit(solution)/shard_map/ppermute | solution.py:224
  172.4 11.0 %collective-permute-start.30 = (bf16[64,3584]{1,0:T(8,128)(2,1)}, bf16[64,3584]{1,0:T(8,128)(2,1)S(1)}, u32[]{:S(2)}, u32[]{:S(2)}) collective-permute-start(bf16[64,3584]{1,0:T(8,128)(2,1)} %shard_map.78), channel_id=1, source_target_pairs={{0,2},{1,3},{4,0},{5,1},{8,4},{9,5},{12,8},{13,9},{14,12},{15,13},... | collective-permute-start | bytes 1376264 | tf_op jit(solution)/shard_map/ppermute | solution.py:224
  175.5 8.7 %collective-permute-start.22 = (bf16[64,3584]{1,0:T(8,128)(2,1)}, bf16[64,3584]{1,0:T(8,128)(2,1)S(1)}, u32[]{:S(2)}, u32[]{:S(2)}) collective-permute-start(bf16[64,3584]{1,0:T(8,128)(2,1)} %shard_map.71), channel_id=1, source_target_pairs={{0,4},{1,5},{4,8},{5,9},{8,12},{9,13},{12,14},{13,15},{14,10},{15,... | collective-permute-start | bytes 1376264 | tf_op jit(solution)/shard_map/ppermute | solution.py:224
  178.6 5.6 %copy-start.21 = (bf16[64,3584]{1,0:T(8,128)(2,1)}, bf16[64,3584]{1,0:T(8,128)(2,1)S(1)}, u32[]{:S(2)}) copy-start(bf16[64,3584]{1,0:T(8,128)(2,1)S(1)} %collective-permute-done.26.refs_4_) | copy-start | bytes 1376260
  178.6 5.6 %copy-start.22 = (bf16[64,3584]{1,0:T(8,128)(2,1)}, bf16[64,3584]{1,0:T(8,128)(2,1)S(1)}, u32[]{:S(2)}) copy-start(bf16[64,3584]{1,0:T(8,128)(2,1)S(1)} %collective-permute-done.24.refs_2_) | copy-start | bytes 1376260
  (18 other events, 14.1 us)

commit v5 on v4

--- a/solution.py
+++ b/solution.py
@@ -78,22 +78,23 @@
             pltpu.VMEM((n * half, LANES), jnp.float32),
             pltpu.VMEM((n * half, SPAN * hid), jnp.bfloat16),
         ],
-        compiler_params=pltpu.CompilerParams(vmem_limit_bytes=16 * MIB),
+        compiler_params=pltpu.CompilerParams(vmem_limit_bytes=10 * MIB),
         cost_estimate=small_cost(),
     )(expert, *blocks, *own, *other)
 
 
-def add_kernel(left_ref, right_ref, out_ref):
-    total = left_ref[...].astype(jnp.float32) + right_ref[...].astype(jnp.float32)
-    out_ref[...] = total.astype(out_ref.dtype)
-
-
-def add(left, right):
-    return pl.pallas_call(
-        add_kernel,
-        out_shape=jax.ShapeDtypeStruct(left.shape, left.dtype),
-        cost_estimate=small_cost(),
-    )(left, right)
+def add_kernel(n, *refs):
+    for left_ref, right_ref, out_ref in zip(refs[:n], refs[n : 2 * n], refs[2 * n :]):
+        out_ref[...] = left_ref[...] + right_ref[...]
+
+
+def add(lefts, rights):
+    n = len(lefts)
+    return pl.pallas_call(
+        functools.partial(add_kernel, n),
+        out_shape=[jax.ShapeDtypeStruct(left.shape, left.dtype) for left in lefts],
+        cost_estimate=small_cost(),
+    )(*lefts, *rights)
 
 
 def close_kernel(*refs):
@@ -138,6 +139,21 @@
     )(tokens, ids.T, codes.T)
 
 
+def hand_on_kernel(expert_ref, *refs):
+    refs[-1][0] = expert_ref[0]
+
+
+def hand_on(expert, arrays):
+    return pl.pallas_call(
+        hand_on_kernel,
+        in_specs=[pl.BlockSpec(memory_space=pltpu.SMEM)]
+        + [pl.BlockSpec(memory_space=pltpu.VMEM)] * len(arrays),
+        out_specs=pl.BlockSpec(memory_space=pltpu.SMEM),
+        out_shape=jax.ShapeDtypeStruct(expert.shape, expert.dtype),
+        cost_estimate=small_cost(),
+    )(expert, *arrays)
+
+
 def body(tokens, expert_ids, gate_codes, w_gate, w_up, w_down):
     nodes = lax.axis_size("node")
     ring = nodes // SPAN
@@ -177,7 +193,7 @@
             if s < far or h == 1:
                 behind[h].append(lax.ppermute(behind[h][s - 1], "node", backward))
 
-    def work(offsets, after=()):
+    def work(offsets, expert, after=()):
         names = [(offset, h) for offset in offsets for h in range(2)]
         blocks = []
         for offset, h in names:
@@ -193,15 +209,19 @@
 
     send(1, [])
     own, _ = lax.optimization_barrier(((w_gate, w_up, w_down), rows))
-    other = []
-    for weight in own:
-        weight, *other = lax.optimization_barrier((weight, *other))
+    expert = hand_on(expert, own)
+    other = [lax.ppermute(own[0], "node", swap)]
+    for h, weight in ((0, own[1]), (1, own[2])):
+        pair, expert, weight = lax.optimization_barrier(
+            ([ahead[h][1], behind[h][1]], expert, weight)
+        )
+        ahead[h][1], behind[h][1] = pair
         other.append(lax.ppermute(weight, "node", swap))
     done = []
     for s in range(2, far + 1):
         send(s, done)
-        done = work([0, -1, 1] if s == 2 else [1 - s, s - 1])
-    work([far], done)
+        done = work([1 - s, s - 1], expert)
+    work([0, far], expert, done)
     parts[-far, 1] = parts[far, 1]
 
     streams = [(h, sign) for h in range(2) for sign in (1, -1)]
@@ -217,11 +237,12 @@
     for (h, sign), total in zip(late, first):
         came[h, sign] = lax.ppermute(total, "node", ways[sign])
     for d in range(far - 1, 0, -1):
-        for h, sign in early + late:
-            at = d - 1 if (h, sign) in early else d
+        for group, at in ((early, d - 1), (late, d)):
             if at:
-                total = add(parts[sign * at, h], came[h, sign])
-                came[h, sign] = lax.ppermute(total, "node", ways[sign])
+                lefts = [parts[sign * at, h] for h, sign in group]
+                totals = add(lefts, [came[stream] for stream in group])
+                for (h, sign), total in zip(group, totals):
+                    came[h, sign] = lax.ppermute(total, "node", ways[sign])
     return close([t for h in range(2) for t in (parts[0, h], came[h, 1], came[h, -1])])
 
 

time: 189 us -> 180 us (0.952)
  local copies, waits for them, and re-layouts: 30 us -> 18.7 us
  waiting for transfers between devices: 62.3 us -> 65.6 us
    ppermute x12, waiting for transfers between devices: 22.3 us -> 37 us  [body(): came[h, sign] = lax.ppermute(total, 'node', ways[sign])]
    unnamed x70 -> x62, local copies, waits for them, and re-layouts: 30 us -> 18.7 us
    ppermute x3 -> x2, waiting for transfers between devices: 12.5 us -> 7.43 us  [body(): other.append(lax.ppermute(weight, 'node', swap))]
    pallas_call x10 -> x6, Pallas kernels: 20.4 us -> 16.8 us  [the longest x5 12.1 us: add(): pl.pallas_call(functools.partial(add_kernel, n), out_shape=[jax.ShapeDtyp...]
    ppermute x7, waiting for transfers between devices: 6.31 us -> 3.69 us  [send(): behind[h].append(lax.ppermute(behind[h][s - 1], 'node', backward))]
    pallas_call x4, Pallas kernels: 39.9 us -> 42.5 us  [expert_parts(): pl.pallas_call(functools.partial(expert_kernel, n, experts, dim, half), i...]
  transfers between devices with their start and end apart: 31 -> 31, of which waited for: 18 -> 17; matrix products, arithmetic and copies ran while one was open for 0% -> 0% of each run, Pallas kernels for 32% -> 32%
where the time goes in v5:
time: 180 us; the launch traced here: 179 us
  waiting for transfers between devices  65.6 us (36%)
  Pallas kernels  64.5 us (36%)
  starting transfers between devices  29.9 us (17%)
  local copies, waits for them, and re-layouts  18.7 us (10%)
    pallas_call x4, Pallas kernels, expert_parts(): pl.pallas_call(functools.partial(expert_kernel, n, experts, dim, half), i...  42.5 us
    ppermute x12, waiting for transfers between devices, body(): came[h, sign] = lax.ppermute(total, 'node', ways[sign])  37 us
    unnamed x62, local copies, waits for them, and re-layouts  18.7 us
    ppermute x7, waiting for transfers between devices, send(): ahead[h].append(lax.ppermute(ahead[h][s - 1], 'node', forward))  17.5 us
    ppermute x12, starting transfers between devices, body(): came[h, sign] = lax.ppermute(total, 'node', ways[sign])  12.2 us
    pallas_call x5, Pallas kernels, add(): pl.pallas_call(functools.partial(add_kernel, n), out_shape=[jax.ShapeDtyp...  12.1 us
    ppermute x7, starting transfers between devices, send(): ahead[h].append(lax.ppermute(ahead[h][s - 1], 'node', forward))  11.9 us
    ppermute x2, waiting for transfers between devices, body(): other.append(lax.ppermute(weight, 'node', swap))  7.43 us
  transfers between devices with their start and end apart: 31, of which 17 were waited for; matrix products, arithmetic and copies ran while one was open for 0% of the time, Pallas kernels for 32%

profile of v5, /device:TPU:0, one launch (start us, length us, event | category | flops | bytes accessed | tf_op | source)
XLA Modules:
  0.0 178.9 jit_solution(17082044171279924651)
XLA Ops:
  0.0 2.3 %shard_map.64 = (bf16[64,3712]{1,0:T(8,128)(2,1)}, bf16[64,3712]{1,0:T(8,128)(2,1)}) custom-call(bf16[128,3584]{1,0:T(8,128)(2,1)} %tokens_ref.1, s32[4,128]{1,0:T(4,128)} %bitcast.3, s32[4,128]{1,0:T(4,128)} %bitcast.4), custom_call_target="tpu_custom_call" | custom-call | flops 1024 | bytes 1024 | tf_op jit(solution)/shard_map/pallas_call | solution.py:135
  2.3 3.0 %collective-permute-start.2 = (bf16[64,3712]{1,0:T(8,128)(2,1)}, bf16[64,3712]{1,0:T(8,128)(2,1)S(1)}, u32[]{:S(2)}, u32[]{:S(2)}) collective-permute-start(bf16[64,3712]{1,0:T(8,128)(2,1)} %get-tuple-element.153.refs_0_), channel_id=1, source_target_pairs={{0,4},{1,5},{4,8},{5,9},{8,12},{9,13},{12,14},{13,15},{14,10},{15,... | collective-permute-start | bytes 1425416 | tf_op jit(solution)/shard_map/ppermute | solution.py:192
  5.3 2.0 %collective-permute-start = (bf16[64,3712]{1,0:T(8,128)(2,1)}, bf16[64,3712]{1,0:T(8,128)(2,1)S(1)}, u32[]{:S(2)}, u32[]{:S(2)}) collective-permute-start(bf16[64,3712]{1,0:T(8,128)(2,1)} %get-tuple-element.154.refs_1_), channel_id=1, source_target_pairs={{0,4},{1,5},{4,8},{5,9},{8,12},{9,13},{12,14},{13,15},{14,10},{15,... | collective-permute-start | bytes 1425416 | tf_op jit(solution)/shard_map/ppermute | solution.py:192
  7.3 4.7 %shard_map.65.expert_ref = s32[1]{0:T(128)} custom-call(s32[1]{0:T(128)} %bitcast.2.expert_ref, bf16[3584,512]{1,0:T(8,128)(2,1)} %refs_4_.3, bf16[3584,512]{1,0:T(8,128)(2,1)} %refs_5_.3, bf16[512,3584]{1,0:T(8,128)(2,1)} %refs_6_.3), custom_call_target="tpu_custom_call" | custom-call | flops 1024 | bytes 1024 | tf_op jit(solution)/shard_map/pallas_call | solution.py:147
  12.0 5.1 %collective-permute-done.2.refs_0_ = bf16[64,3712]{1,0:T(8,128)(2,1)S(1)} collective-permute-done((bf16[64,3712]{1,0:T(8,128)(2,1)}, bf16[64,3712]{1,0:T(8,128)(2,1)S(1)}, u32[]{:S(2)}, u32[]{:S(2)}) %collective-permute-start.2) | collective-permute-done | bytes 475168 | tf_op jit(solution)/shard_map/ppermute | solution.py:192
  17.1 2.2 %collective-permute-done.3.refs_2_ = bf16[64,3712]{1,0:T(8,128)(2,1)S(1)} collective-permute-done((bf16[64,3712]{1,0:T(8,128)(2,1)}, bf16[64,3712]{1,0:T(8,128)(2,1)S(1)}, u32[]{:S(2)}, u32[]{:S(2)}) %collective-permute-start.3) | collective-permute-done | bytes 475168 | tf_op jit(solution)/shard_map/ppermute | solution.py:194
  19.3 7.2 %collective-permute-done.refs_1_ = bf16[64,3712]{1,0:T(8,128)(2,1)S(1)} collective-permute-done((bf16[64,3712]{1,0:T(8,128)(2,1)}, bf16[64,3712]{1,0:T(8,128)(2,1)S(1)}, u32[]{:S(2)}, u32[]{:S(2)}) %collective-permute-start) | collective-permute-done | bytes 475168 | tf_op jit(solution)/shard_map/ppermute | solution.py:192
  26.5 1.5 collective-permute-done.1.refs_3_
  28.5 1.6 collective-permute-start.4
  30.6 1.6 collective-permute-start.11
  32.1 2.5 %collective-permute-done.8.refs_9_ = bf16[512,3584]{1,0:T(8,128)(2,1)S(1)} collective-permute-done((bf16[512,3584]{1,0:T(8,128)(2,1)}, bf16[512,3584]{1,0:T(8,128)(2,1)S(1)}, u32[]{:S(2)}, u32[]{:S(2)}) %collective-permute-start.8) | collective-permute-done | bytes 3670048 | tf_op jit(solution)/shard_map/ppermute | solution.py:219
  34.9 4.9 %collective-permute-done.7.refs_8_ = bf16[3584,512]{1,0:T(8,128)(2,1)S(1)} collective-permute-done((bf16[3584,512]{1,0:T(8,128)(2,1)}, bf16[3584,512]{1,0:T(8,128)(2,1)S(1)}, u32[]{:S(2)}, u32[]{:S(2)}) %collective-permute-start.7) | collective-permute-done | bytes 3670048 | tf_op jit(solution)/shard_map/ppermute | solution.py:219
  39.9 2.0 %copy-done = bf16[3584,512]{1,0:T(8,128)(2,1)S(1)} copy-done((bf16[3584,512]{1,0:T(8,128)(2,1)S(1)}, bf16[3584,512]{1,0:T(8,128)(2,1)}, u32[]{:S(2)}) %copy-start) | copy-done | bytes 3670040
  41.9 2.0 %copy-done.1 = bf16[3584,512]{1,0:T(8,128)(2,1)S(1)} copy-done((bf16[3584,512]{1,0:T(8,128)(2,1)S(1)}, bf16[3584,512]{1,0:T(8,128)(2,1)}, u32[]{:S(2)}) %copy-start.1) | copy-done | bytes 3670040
  44.0 2.0 %copy-done.2 = bf16[512,3584]{1,0:T(8,128)(2,1)S(1)} copy-done((bf16[512,3584]{1,0:T(8,128)(2,1)S(1)}, bf16[512,3584]{1,0:T(8,128)(2,1)}, u32[]{:S(2)}) %copy-start.2) | copy-done | bytes 3670040
  46.0 10.6 %shard_map.66 = (bf16[64,3584]{1,0:T(8,128)(2,1)S(1)}, bf16[64,3584]{1,0:T(8,128)(2,1)S(1)}, bf16[64,3584]{1,0:T(8,128)(2,1)S(1)}, bf16[64,3584]{1,0:T(8,128)(2,1)S(1)}) custom-call(s32[1]{0:T(128)} %shard_map.65.expert_ref, bf16[64,3712]{1,0:T(8,128)(2,1)S(1)} %collective-permute-done.2.refs_0_, bf16[64,3712]{1,0:T(8,128)(2,1)S(1)} %collective-permute-done.refs_1_, ...), custom_call_target="tpu_custom_call" | custom-call | flops 1024 | bytes 1024 | tf_op jit(solution)/shard_map/pallas_call | solution.py:71
  59.3 1.7 collective-permute-start.9
  61.1 1.6 collective-permute-start.14
  63.1 10.6 %shard_map.67 = (bf16[64,3584]{1,0:T(8,128)(2,1)S(1)}, bf16[64,3584]{1,0:T(8,128)(2,1)S(1)}, bf16[64,3584]{1,0:T(8,128)(2,1)S(1)}, bf16[64,3584]{1,0:T(8,128)(2,1)S(1)}) custom-call(s32[1]{0:T(128)} %shard_map.65.expert_ref, bf16[64,3712]{1,0:T(8,128)(2,1)S(1)} %collective-permute-done.4.refs_0_, bf16[64,3712]{1,0:T(8,128)(2,1)S(1)} %collective-permute-done.11.refs_1_, ...), custom_call_target="tpu_custom_call" | custom-call | flops 1024 | bytes 1024 | tf_op jit(solution)/shard_map/pallas_call | solution.py:71
  75.3 0.8 copy-done.13
  76.9 5.2 %collective-permute-done.14.refs_1_ = bf16[64,3712]{1,0:T(8,128)(2,1)S(1)} collective-permute-done((bf16[64,3712]{1,0:T(8,128)(2,1)S(1)}, bf16[64,3712]{1,0:T(8,128)(2,1)S(1)}, u32[]{:S(2)}, u32[]{:S(2)}) %collective-permute-start.14) | collective-permute-done | bytes 475168 | tf_op jit(solution)/shard_map/ppermute | solution.py:192
  82.2 1.6 collective-permute-start.16
  84.2 10.6 %shard_map.68 = (bf16[64,3584]{1,0:T(8,128)(2,1)S(1)}, bf16[64,3584]{1,0:T(8,128)(2,1)S(1)}, bf16[64,3584]{1,0:T(8,128)(2,1)S(1)}, bf16[64,3584]{1,0:T(8,128)(2,1)S(1)}) custom-call(s32[1]{0:T(128)} %shard_map.65.expert_ref, bf16[64,3712]{1,0:T(8,128)(2,1)S(1)} %collective-permute-done.9.refs_0_, bf16[64,3712]{1,0:T(8,128)(2,1)S(1)} %collective-permute-done.14.refs_1_, ...), custom_call_target="tpu_custom_call" | custom-call | flops 1024 | bytes 1024 | tf_op jit(solution)/shard_map/pallas_call | solution.py:71
  95.7 1.7 collective-permute-start.17
  97.8 10.6 %shard_map.69 = (bf16[64,3584]{1,0:T(8,128)(2,1)S(1)}, bf16[64,3584]{1,0:T(8,128)(2,1)S(1)}, bf16[64,3584]{1,0:T(8,128)(2,1)S(1)}, bf16[64,3584]{1,0:T(8,128)(2,1)S(1)}) custom-call(s32[1]{0:T(128)} %shard_map.65.expert_ref, bf16[64,3712]{1,0:T(8,128)(2,1)S(1)} %copy-done.3, bf16[64,3712]{1,0:T(8,128)(2,1)S(1)} %copy-done.4, ...), custom_call_target="tpu_custom_call" | custom-call | flops 1024 | bytes 1024 | tf_op jit(solution)/shard_map/pallas_call | solution.py:71
  110.0 1.7 collective-permute-start.19
  112.1 8.5 %collective-permute-done.19.refs_2_ = bf16[64,3584]{1,0:T(8,128)(2,1)S(1)} collective-permute-done((bf16[64,3584]{1,0:T(8,128)(2,1)S(1)}, bf16[64,3584]{1,0:T(8,128)(2,1)S(1)}, u32[]{:S(2)}, u32[]{:S(2)}) %collective-permute-start.19) | collective-permute-done | bytes 458784 | tf_op jit(solution)/shard_map/ppermute | solution.py:238
  120.6 1.3 collective-permute-done.20.refs_3_
  122.7 2.4 %shard_map.70 = (bf16[64,3584]{1,0:T(8,128)(2,1)}, bf16[64,3584]{1,0:T(8,128)(2,1)}) custom-call(bf16[64,3584]{1,0:T(8,128)(2,1)} %copy-done.16, bf16[64,3584]{1,0:T(8,128)(2,1)} %copy-done.15, bf16[64,3584]{1,0:T(8,128)(2,1)} %copy-done.29, bf16[64,3584]{1,0:T(8,128)(2,1)} %copy-done.30), custom_call_target="tpu_custom_call" | custom-call | flops 1024 | bytes 1024 | tf_op jit(solution)/shard_map/pallas_call | solution.py:93
  125.1 1.6 collective-permute-start.21
  127.1 2.4 %shard_map.73 = (bf16[64,3584]{1,0:T(8,128)(2,1)}, bf16[64,3584]{1,0:T(8,128)(2,1)}) custom-call(bf16[64,3584]{1,0:T(8,128)(2,1)} %copy-done.13, bf16[64,3584]{1,0:T(8,128)(2,1)} %copy-done.14, bf16[64,3584]{1,0:T(8,128)(2,1)} %copy-done.17, bf16[64,3584]{1,0:T(8,128)(2,1)} %copy-done.18), custom_call_target="tpu_custom_call" | custom-call | flops 1024 | bytes 1024 | tf_op jit(solution)/shard_map/pallas_call | solution.py:93
  129.6 0.9 collective-permute-start.26
  130.4 1.2 collective-permute-start.27
  131.6 7.2 %collective-permute-done.21.refs_2_ = bf16[64,3584]{1,0:T(8,128)(2,1)S(1)} collective-permute-done((bf16[64,3584]{1,0:T(8,128)(2,1)}, bf16[64,3584]{1,0:T(8,128)(2,1)S(1)}, u32[]{:S(2)}, u32[]{:S(2)}) %collective-permute-start.21) | collective-permute-done | bytes 458784 | tf_op jit(solution)/shard_map/ppermute | solution.py:245
  138.8 1.6 collective-permute-done.22.refs_3_
  141.1 2.4 %shard_map.71 = (bf16[64,3584]{1,0:T(8,128)(2,1)}, bf16[64,3584]{1,0:T(8,128)(2,1)}) custom-call(bf16[64,3584]{1,0:T(8,128)(2,1)} %copy-done.12, bf16[64,3584]{1,0:T(8,128)(2,1)} %copy-done.11, bf16[64,3584]{1,0:T(8,128)(2,1)} %copy-done.25, bf16[64,3584]{1,0:T(8,128)(2,1)} %copy-done.26), custom_call_target="tpu_custom_call" | custom-call | flops 1024 | bytes 1024 | tf_op jit(solution)/shard_map/pallas_call | solution.py:93
  143.5 1.5 collective-permute-start.23
  145.6 4.6 %collective-permute-done.26.refs_2_ = bf16[64,3584]{1,0:T(8,128)(2,1)S(1)} collective-permute-done((bf16[64,3584]{1,0:T(8,128)(2,1)}, bf16[64,3584]{1,0:T(8,128)(2,1)S(1)}, u32[]{:S(2)}, u32[]{:S(2)}) %collective-permute-start.26) | collective-permute-done | bytes 458784 | tf_op jit(solution)/shard_map/ppermute | solution.py:245
  151.7 2.4 %shard_map.74 = (bf16[64,3584]{1,0:T(8,128)(2,1)}, bf16[64,3584]{1,0:T(8,128)(2,1)}) custom-call(bf16[64,3584]{1,0:T(8,128)(2,1)} %copy-done.7, bf16[64,3584]{1,0:T(8,128)(2,1)} %copy-done.8, bf16[64,3584]{1,0:T(8,128)(2,1)} %copy-done.21, bf16[64,3584]{1,0:T(8,128)(2,1)} %copy-done.23), custom_call_target="tpu_custom_call" | custom-call | flops 1024 | bytes 1024 | tf_op jit(solution)/shard_map/pallas_call | solution.py:93
  154.6 1.6 collective-permute-start.29
  156.2 2.3 %collective-permute-done.23.refs_2_ = bf16[64,3584]{1,0:T(8,128)(2,1)S(1)} collective-permute-done((bf16[64,3584]{1,0:T(8,128)(2,1)}, bf16[64,3584]{1,0:T(8,128)(2,1)S(1)}, u32[]{:S(2)}, u32[]{:S(2)}) %collective-permute-start.23) | collective-permute-done | bytes 458784 | tf_op jit(solution)/shard_map/ppermute | solution.py:245
  158.4 1.6 collective-permute-done.24.refs_3_
  160.8 2.4 %shard_map.72 = (bf16[64,3584]{1,0:T(8,128)(2,1)}, bf16[64,3584]{1,0:T(8,128)(2,1)}) custom-call(bf16[64,3584]{1,0:T(8,128)(2,1)} %copy-done.6, bf16[64,3584]{1,0:T(8,128)(2,1)} %copy-done.5, bf16[64,3584]{1,0:T(8,128)(2,1)} %copy-done.22, bf16[64,3584]{1,0:T(8,128)(2,1)} %copy-done.24), custom_call_target="tpu_custom_call" | custom-call | flops 1024 | bytes 1024 | tf_op jit(solution)/shard_map/pallas_call | solution.py:93
  163.2 1.5 collective-permute-start.25
  165.2 4.6 %collective-permute-done.28.refs_2_ = bf16[64,3584]{1,0:T(8,128)(2,1)S(1)} collective-permute-done((bf16[64,3584]{1,0:T(8,128)(2,1)}, bf16[64,3584]{1,0:T(8,128)(2,1)S(1)}, u32[]{:S(2)}, u32[]{:S(2)}) %collective-permute-start.28) | collective-permute-done | bytes 458784 | tf_op jit(solution)/shard_map/ppermute | solution.py:245
  169.9 4.0 %collective-permute-done.25.refs_1_ = bf16[64,3584]{1,0:T(8,128)(2,1)S(1)} collective-permute-done((bf16[64,3584]{1,0:T(8,128)(2,1)}, bf16[64,3584]{1,0:T(8,128)(2,1)S(1)}, u32[]{:S(2)}, u32[]{:S(2)}) %collective-permute-start.25) | collective-permute-done | bytes 458784 | tf_op jit(solution)/shard_map/ppermute | solution.py:245
  173.9 1.3 collective-permute-done.30.refs_5_
  176.0 3.0 %shard_map.75 = bf16[128,3584]{1,0:T(8,128)(2,1)} custom-call(bf16[64,3584]{1,0:T(8,128)(2,1)} %copy-done.9, bf16[64,3584]{1,0:T(8,128)(2,1)} %copy-done.27, bf16[64,3584]{1,0:T(8,128)(2,1)} %copy-done.19, bf16[64,3584]{1,0:T(8,128)(2,1)} %copy-done.10, bf16[64,3584]{1,0:T(8,128)(2,1)} %copy-done.20, bf16[64,3584]{1,0:T(8,128)(2,1)} %copy-done.28), custom_call_target="tpu_custom_call" | custom-call | flops 1024 | bytes 1024 | tf_op jit(solution)/shard_map/pallas_call | solution.py:111
  (88 shorter events, 16.9 us)
Async XLA Ops:
  2.3 14.9 %collective-permute-start.2 = (bf16[64,3712]{1,0:T(8,128)(2,1)}, bf16[64,3712]{1,0:T(8,128)(2,1)S(1)}, u32[]{:S(2)}, u32[]{:S(2)}) collective-permute-start(bf16[64,3712]{1,0:T(8,128)(2,1)} %get-tuple-element.153.refs_0_), channel_id=1, source_target_pairs={{0,4},{1,5},{4,8},{5,9},{8,12},{9,13},{12,14},{13,15},{14,10},{15,... | collective-permute-start | bytes 1425416 | tf_op jit(solution)/shard_map/ppermute | solution.py:192
  5.3 14.0 %collective-permute-start.3 = (bf16[64,3712]{1,0:T(8,128)(2,1)}, bf16[64,3712]{1,0:T(8,128)(2,1)S(1)}, u32[]{:S(2)}, u32[]{:S(2)}) collective-permute-start(bf16[64,3712]{1,0:T(8,128)(2,1)} %get-tuple-element.153.refs_0_), channel_id=1, source_target_pairs={{0,2},{1,3},{4,0},{5,1},{8,4},{9,5},{12,8},{13,9},{14,12},{15,13},... | collective-permute-start | bytes 1425416 | tf_op jit(solution)/shard_map/ppermute | solution.py:194
  5.3 21.2 %collective-permute-start = (bf16[64,3712]{1,0:T(8,128)(2,1)}, bf16[64,3712]{1,0:T(8,128)(2,1)S(1)}, u32[]{:S(2)}, u32[]{:S(2)}) collective-permute-start(bf16[64,3712]{1,0:T(8,128)(2,1)} %get-tuple-element.154.refs_1_), channel_id=1, source_target_pairs={{0,4},{1,5},{4,8},{5,9},{8,12},{9,13},{12,14},{13,15},{14,10},{15,... | collective-permute-start | bytes 1425416 | tf_op jit(solution)/shard_map/ppermute | solution.py:192
  7.3 20.7 %collective-permute-start.1 = (bf16[64,3712]{1,0:T(8,128)(2,1)}, bf16[64,3712]{1,0:T(8,128)(2,1)S(1)}, u32[]{:S(2)}, u32[]{:S(2)}) collective-permute-start(bf16[64,3712]{1,0:T(8,128)(2,1)} %get-tuple-element.154.refs_1_), channel_id=1, source_target_pairs={{0,2},{1,3},{4,0},{5,1},{8,4},{9,5},{12,8},{13,9},{14,12},{15,13},... | collective-permute-start | bytes 1425416 | tf_op jit(solution)/shard_map/ppermute | solution.py:194
  7.3 23.2 %collective-permute-start.6 = (bf16[3584,512]{1,0:T(8,128)(2,1)}, bf16[3584,512]{1,0:T(8,128)(2,1)}, u32[]{:S(2)}, u32[]{:S(2)}) collective-permute-start(bf16[3584,512]{1,0:T(8,128)(2,1)} %refs_4_.3), channel_id=1, source_target_pairs={{0,1},{1,0},{2,3},{3,2},{4,5},{5,4},{6,7},{7,6},{8,9},{9,8},{10,11... | collective-permute-start | bytes 11010056 | tf_op jit(solution)/shard_map/ppermute | solution.py:213
  28.0 6.6 %collective-permute-start.8 = (bf16[512,3584]{1,0:T(8,128)(2,1)}, bf16[512,3584]{1,0:T(8,128)(2,1)S(1)}, u32[]{:S(2)}, u32[]{:S(2)}) collective-permute-start(bf16[512,3584]{1,0:T(8,128)(2,1)} %refs_6_.3), channel_id=1, source_target_pairs={{0,1},{1,0},{2,3},{3,2},{4,5},{5,4},{6,7},{7,6},{8,9},{9,8},{10,11... | collective-permute-start | bytes 11010056 | tf_op jit(solution)/shard_map/ppermute | solution.py:219
  28.0 11.9 %collective-permute-start.7 = (bf16[3584,512]{1,0:T(8,128)(2,1)}, bf16[3584,512]{1,0:T(8,128)(2,1)S(1)}, u32[]{:S(2)}, u32[]{:S(2)}) collective-permute-start(bf16[3584,512]{1,0:T(8,128)(2,1)} %refs_5_.3), channel_id=1, source_target_pairs={{0,1},{1,0},{2,3},{3,2},{4,5},{5,4},{6,7},{7,6},{8,9},{9,8},{10,11... | collective-permute-start | bytes 11010056 | tf_op jit(solution)/shard_map/ppermute | solution.py:219
  28.5 30.4 %collective-permute-start.4 = (bf16[64,3712]{1,0:T(8,128)(2,1)S(1)}, bf16[64,3712]{1,0:T(8,128)(2,1)S(1)}, u32[]{:S(2)}, u32[]{:S(2)}) collective-permute-start(bf16[64,3712]{1,0:T(8,128)(2,1)S(1)} %collective-permute-done.2.refs_0_), channel_id=1, source_target_pairs={{0,4},{1,5},{4,8},{5,9},{8,12},{9,13},{12,14},{13,15},{14,10},{15,... | collective-permute-start | bytes 1425416 | tf_op jit(solution)/shard_map/ppermute | solution.py:192
  30.1 28.9 %collective-permute-start.5 = (bf16[64,3712]{1,0:T(8,128)(2,1)S(1)}, bf16[64,3712]{1,0:T(8,128)(2,1)S(1)}, u32[]{:S(2)}, u32[]{:S(2)}) collective-permute-start(bf16[64,3712]{1,0:T(8,128)(2,1)S(1)} %collective-permute-done.3.refs_2_), channel_id=1, source_target_pairs={{0,2},{1,3},{4,0},{5,1},{8,4},{9,5},{12,8},{13,9},{14,12},{15,13},... | collective-permute-start | bytes 1425416 | tf_op jit(solution)/shard_map/ppermute | solution.py:194
  30.6 30.5 %collective-permute-start.11 = (bf16[64,3712]{1,0:T(8,128)(2,1)S(1)}, bf16[64,3712]{1,0:T(8,128)(2,1)S(1)}, u32[]{:S(2)}, u32[]{:S(2)}) collective-permute-start(bf16[64,3712]{1,0:T(8,128)(2,1)S(1)} %collective-permute-done.refs_1_), channel_id=1, source_target_pairs={{0,4},{1,5},{4,8},{5,9},{8,12},{9,13},{12,14},{13,15},{14,10},{15,... | collective-permute-start | bytes 1425416 | tf_op jit(solution)/shard_map/ppermute | solution.py:192
  34.6 26.4 %collective-permute-start.12 = (bf16[64,3712]{1,0:T(8,128)(2,1)S(1)}, bf16[64,3712]{1,0:T(8,128)(2,1)S(1)}, u32[]{:S(2)}, u32[]{:S(2)}) collective-permute-start(bf16[64,3712]{1,0:T(8,128)(2,1)S(1)} %collective-permute-done.1.refs_3_), channel_id=1, source_target_pairs={{0,2},{1,3},{4,0},{5,1},{8,4},{9,5},{12,8},{13,9},{14,12},{15,13},... | collective-permute-start | bytes 1425416 | tf_op jit(solution)/shard_map/ppermute | solution.py:194
  39.9 2.0 %copy-start = (bf16[3584,512]{1,0:T(8,128)(2,1)S(1)}, bf16[3584,512]{1,0:T(8,128)(2,1)}, u32[]{:S(2)}) copy-start(bf16[3584,512]{1,0:T(8,128)(2,1)} %refs_4_.3) | copy-start | bytes 11010052
  41.9 2.0 %copy-start.1 = (bf16[3584,512]{1,0:T(8,128)(2,1)S(1)}, bf16[3584,512]{1,0:T(8,128)(2,1)}, u32[]{:S(2)}) copy-start(bf16[3584,512]{1,0:T(8,128)(2,1)} %refs_5_.3) | copy-start | bytes 11010052
  44.0 2.0 %copy-start.2 = (bf16[512,3584]{1,0:T(8,128)(2,1)S(1)}, bf16[512,3584]{1,0:T(8,128)(2,1)}, u32[]{:S(2)}) copy-start(bf16[512,3584]{1,0:T(8,128)(2,1)} %refs_6_.3) | copy-start | bytes 11010052
  59.0 14.8 %copy-start.7 = (bf16[64,3584]{1,0:T(8,128)(2,1)}, bf16[64,3584]{1,0:T(8,128)(2,1)S(1)}, u32[]{:S(2)}) copy-start(bf16[64,3584]{1,0:T(8,128)(2,1)S(1)} %get-tuple-element.175.refs_0_) | copy-start | bytes 1376260
  59.0 17.9 %collective-permute-start.10 = (bf16[64,3712]{1,0:T(8,128)(2,1)S(1)}, bf16[64,3712]{1,0:T(8,128)(2,1)S(1)}, u32[]{:S(2)}, u32[]{:S(2)}) collective-permute-start(bf16[64,3712]{1,0:T(8,128)(2,1)S(1)} %collective-permute-done.5.refs_2_), channel_id=1, source_target_pairs={{0,2},{1,3},{4,0},{5,1},{8,4},{9,5},{12,8},{13,9},{14,12},{15,13},... | collective-permute-start | bytes 1425416 | tf_op jit(solution)/shard_map/ppermute | solution.py:194
  59.3 17.6 %collective-permute-start.9 = (bf16[64,3712]{1,0:T(8,128)(2,1)S(1)}, bf16[64,3712]{1,0:T(8,128)(2,1)S(1)}, u32[]{:S(2)}, u32[]{:S(2)}) collective-permute-start(bf16[64,3712]{1,0:T(8,128)(2,1)S(1)} %collective-permute-done.4.refs_0_), channel_id=1, source_target_pairs={{0,4},{1,5},{4,8},{5,9},{8,12},{9,13},{12,14},{13,15},{14,10},{15,... | collective-permute-start | bytes 1425416 | tf_op jit(solution)/shard_map/ppermute | solution.py:192
  61.1 21.1 %collective-permute-start.14 = (bf16[64,3712]{1,0:T(8,128)(2,1)S(1)}, bf16[64,3712]{1,0:T(8,128)(2,1)S(1)}, u32[]{:S(2)}, u32[]{:S(2)}) collective-permute-start(bf16[64,3712]{1,0:T(8,128)(2,1)S(1)} %collective-permute-done.11.refs_1_), channel_id=1, source_target_pairs={{0,4},{1,5},{4,8},{5,9},{8,12},{9,13},{12,14},{13,15},{14,10},{15,... | collective-permute-start | bytes 1425416 | tf_op jit(solution)/shard_map/ppermute | solution.py:192
  62.6 19.5 %collective-permute-start.15 = (bf16[64,3712]{1,0:T(8,128)(2,1)S(1)}, bf16[64,3712]{1,0:T(8,128)(2,1)S(1)}, u32[]{:S(2)}, u32[]{:S(2)}) collective-permute-start(bf16[64,3712]{1,0:T(8,128)(2,1)S(1)} %collective-permute-done.12.refs_3_), channel_id=1, source_target_pairs={{0,2},{1,3},{4,0},{5,1},{8,4},{9,5},{12,8},{13,9},{14,12},{15,13},... | collective-permute-start | bytes 1425416 | tf_op jit(solution)/shard_map/ppermute | solution.py:194
  75.3 0.8 copy-start.13
  76.9 20.8 %copy-start.3 = (bf16[64,3712]{1,0:T(8,128)(2,1)S(1)}, bf16[64,3712]{1,0:T(8,128)(2,1)}, u32[]{:S(2)}) copy-start(bf16[64,3712]{1,0:T(8,128)(2,1)} %get-tuple-element.153.refs_0_) | copy-start | bytes 1425412
  76.9 20.8 %copy-start.4 = (bf16[64,3712]{1,0:T(8,128)(2,1)S(1)}, bf16[64,3712]{1,0:T(8,128)(2,1)}, u32[]{:S(2)}) copy-start(bf16[64,3712]{1,0:T(8,128)(2,1)} %get-tuple-element.154.refs_1_) | copy-start | bytes 1425412
  82.2 13.5 %collective-permute-start.16 = (bf16[64,3712]{1,0:T(8,128)(2,1)S(1)}, bf16[64,3712]{1,0:T(8,128)(2,1)S(1)}, u32[]{:S(2)}, u32[]{:S(2)}) collective-permute-start(bf16[64,3712]{1,0:T(8,128)(2,1)S(1)} %collective-permute-done.15.refs_3_), channel_id=1, source_target_pairs={{0,2},{1,3},{4,0},{5,1},{8,4},{9,5},{12,8},{13,9},{14,12},{15,13},... | collective-permute-start | bytes 1425416 | tf_op jit(solution)/shard_map/ppermute | solution.py:194
  83.8 11.9 %collective-permute-start.13 = (bf16[64,3712]{1,0:T(8,128)(2,1)S(1)}, bf16[64,3712]{1,0:T(8,128)(2,1)S(1)}, u32[]{:S(2)}, u32[]{:S(2)}) collective-permute-start(bf16[64,3712]{1,0:T(8,128)(2,1)S(1)} %collective-permute-done.9.refs_0_), channel_id=1, source_target_pairs={{0,4},{1,5},{4,8},{5,9},{8,12},{9,13},{12,14},{13,15},{14,10},{15,... | collective-permute-start | bytes 1425416 | tf_op jit(solution)/shard_map/ppermute | solution.py:192
  94.8 0.8 copy-start.16
  95.7 12.7 %copy-start.15 = (bf16[64,3584]{1,0:T(8,128)(2,1)}, bf16[64,3584]{1,0:T(8,128)(2,1)S(1)}, u32[]{:S(2)}) copy-start(bf16[64,3584]{1,0:T(8,128)(2,1)S(1)} %get-tuple-element.163.refs_1_) | copy-start | bytes 1376260
  95.7 14.3 %collective-permute-start.17 = (bf16[64,3584]{1,0:T(8,128)(2,1)S(1)}, bf16[64,3584]{1,0:T(8,128)(2,1)S(1)}, u32[]{:S(2)}, u32[]{:S(2)}) collective-permute-start(bf16[64,3584]{1,0:T(8,128)(2,1)S(1)} %get-tuple-element.166), channel_id=1, source_target_pairs={{0,2},{1,3},{4,0},{5,1},{8,4},{9,5},{12,8},{13,9},{14,12},{15,13},... | collective-permute-start | bytes 1376264 | tf_op jit(solution)/shard_map/ppermute | solution.py:233
  97.4 12.6 %collective-permute-start.18 = (bf16[64,3584]{1,0:T(8,128)(2,1)S(1)}, bf16[64,3584]{1,0:T(8,128)(2,1)S(1)}, u32[]{:S(2)}, u32[]{:S(2)}) collective-permute-start(bf16[64,3584]{1,0:T(8,128)(2,1)S(1)} %get-tuple-element.167), channel_id=1, source_target_pairs={{0,4},{1,5},{4,8},{5,9},{8,12},{9,13},{12,14},{13,15},{14,10},{15,... | collective-permute-start | bytes 1376264 | tf_op jit(solution)/shard_map/ppermute | solution.py:233
  110.0 17.2 %copy-start.17 = (bf16[64,3584]{1,0:T(8,128)(2,1)}, bf16[64,3584]{1,0:T(8,128)(2,1)S(1)}, u32[]{:S(2)}) copy-start(bf16[64,3584]{1,0:T(8,128)(2,1)S(1)} %collective-permute-done.17.refs_2_) | copy-start | bytes 1376260
  110.0 17.2 %copy-start.18 = (bf16[64,3584]{1,0:T(8,128)(2,1)}, bf16[64,3584]{1,0:T(8,128)(2,1)S(1)}, u32[]{:S(2)}) copy-start(bf16[64,3584]{1,0:T(8,128)(2,1)S(1)} %collective-permute-done.18.refs_3_) | copy-start | bytes 1376260
  110.0 10.6 %collective-permute-start.19 = (bf16[64,3584]{1,0:T(8,128)(2,1)S(1)}, bf16[64,3584]{1,0:T(8,128)(2,1)S(1)}, u32[]{:S(2)}, u32[]{:S(2)}) collective-permute-start(bf16[64,3584]{1,0:T(8,128)(2,1)S(1)} %get-tuple-element.168), channel_id=1, source_target_pairs={{0,4},{1,5},{4,8},{5,9},{8,12},{9,13},{12,14},{13,15},{14,10},{15,... | collective-permute-start | bytes 1376264 | tf_op jit(solution)/shard_map/ppermute | solution.py:238
  111.7 10.2 %collective-permute-start.20 = (bf16[64,3584]{1,0:T(8,128)(2,1)S(1)}, bf16[64,3584]{1,0:T(8,128)(2,1)S(1)}, u32[]{:S(2)}, u32[]{:S(2)}) collective-permute-start(bf16[64,3584]{1,0:T(8,128)(2,1)S(1)} %get-tuple-element.169), channel_id=1, source_target_pairs={{0,2},{1,3},{4,0},{5,1},{8,4},{9,5},{12,8},{13,9},{14,12},{15,13},... | collective-permute-start | bytes 1376264 | tf_op jit(solution)/shard_map/ppermute | solution.py:238
  120.6 1.3 copy-start.29
  125.1 13.7 %collective-permute-start.21 = (bf16[64,3584]{1,0:T(8,128)(2,1)}, bf16[64,3584]{1,0:T(8,128)(2,1)S(1)}, u32[]{:S(2)}, u32[]{:S(2)}) collective-permute-start(bf16[64,3584]{1,0:T(8,128)(2,1)} %get-tuple-element.170), channel_id=1, source_target_pairs={{0,4},{1,5},{4,8},{5,9},{8,12},{9,13},{12,14},{13,15},{14,10},{15,... | collective-permute-start | bytes 1376264 | tf_op jit(solution)/shard_map/ppermute | solution.py:245
  126.7 13.7 %collective-permute-start.22 = (bf16[64,3584]{1,0:T(8,128)(2,1)}, bf16[64,3584]{1,0:T(8,128)(2,1)S(1)}, u32[]{:S(2)}, u32[]{:S(2)}) collective-permute-start(bf16[64,3584]{1,0:T(8,128)(2,1)} %get-tuple-element.171), channel_id=1, source_target_pairs={{0,2},{1,3},{4,0},{5,1},{8,4},{9,5},{12,8},{13,9},{14,12},{15,13},... | collective-permute-start | bytes 1376264 | tf_op jit(solution)/shard_map/ppermute | solution.py:245
  129.6 20.6 %collective-permute-start.26 = (bf16[64,3584]{1,0:T(8,128)(2,1)}, bf16[64,3584]{1,0:T(8,128)(2,1)S(1)}, u32[]{:S(2)}, u32[]{:S(2)}) collective-permute-start(bf16[64,3584]{1,0:T(8,128)(2,1)} %get-tuple-element.181), channel_id=1, source_target_pairs={{0,2},{1,3},{4,0},{5,1},{8,4},{9,5},{12,8},{13,9},{14,12},{15,13},... | collective-permute-start | bytes 1376264 | tf_op jit(solution)/shard_map/ppermute | solution.py:245
  130.4 19.8 %collective-permute-start.27 = (bf16[64,3584]{1,0:T(8,128)(2,1)}, bf16[64,3584]{1,0:T(8,128)(2,1)S(1)}, u32[]{:S(2)}, u32[]{:S(2)}) collective-permute-start(bf16[64,3584]{1,0:T(8,128)(2,1)} %get-tuple-element.182), channel_id=1, source_target_pairs={{0,4},{1,5},{4,8},{5,9},{8,12},{9,13},{12,14},{13,15},{14,10},{15,... | collective-permute-start | bytes 1376264 | tf_op jit(solution)/shard_map/ppermute | solution.py:245
  138.8 1.6 copy-start.25
  143.5 14.9 %collective-permute-start.23 = (bf16[64,3584]{1,0:T(8,128)(2,1)}, bf16[64,3584]{1,0:T(8,128)(2,1)S(1)}, u32[]{:S(2)}, u32[]{:S(2)}) collective-permute-start(bf16[64,3584]{1,0:T(8,128)(2,1)} %get-tuple-element.172), channel_id=1, source_target_pairs={{0,4},{1,5},{4,8},{5,9},{8,12},{9,13},{12,14},{13,15},{14,10},{15,... | collective-permute-start | bytes 1376264 | tf_op jit(solution)/shard_map/ppermute | solution.py:245
  145.1 15.0 %collective-permute-start.24 = (bf16[64,3584]{1,0:T(8,128)(2,1)}, bf16[64,3584]{1,0:T(8,128)(2,1)S(1)}, u32[]{:S(2)}, u32[]{:S(2)}) collective-permute-start(bf16[64,3584]{1,0:T(8,128)(2,1)} %get-tuple-element.173), channel_id=1, source_target_pairs={{0,2},{1,3},{4,0},{5,1},{8,4},{9,5},{12,8},{13,9},{14,12},{15,13},... | collective-permute-start | bytes 1376264 | tf_op jit(solution)/shard_map/ppermute | solution.py:245
  154.2 15.7 %collective-permute-start.28 = (bf16[64,3584]{1,0:T(8,128)(2,1)}, bf16[64,3584]{1,0:T(8,128)(2,1)S(1)}, u32[]{:S(2)}, u32[]{:S(2)}) collective-permute-start(bf16[64,3584]{1,0:T(8,128)(2,1)} %get-tuple-element.183), channel_id=1, source_target_pairs={{0,2},{1,3},{4,0},{5,1},{8,4},{9,5},{12,8},{13,9},{14,12},{15,13},... | collective-permute-start | bytes 1376264 | tf_op jit(solution)/shard_map/ppermute | solution.py:245
  154.6 15.3 %collective-permute-start.29 = (bf16[64,3584]{1,0:T(8,128)(2,1)}, bf16[64,3584]{1,0:T(8,128)(2,1)S(1)}, u32[]{:S(2)}, u32[]{:S(2)}) collective-permute-start(bf16[64,3584]{1,0:T(8,128)(2,1)} %get-tuple-element.185), channel_id=1, source_target_pairs={{0,4},{1,5},{4,8},{5,9},{8,12},{9,13},{12,14},{13,15},{14,10},{15,... | collective-permute-start | bytes 1376264 | tf_op jit(solution)/shard_map/ppermute | solution.py:245
  158.4 1.6 copy-start.22
  163.2 10.7 %collective-permute-start.25 = (bf16[64,3584]{1,0:T(8,128)(2,1)}, bf16[64,3584]{1,0:T(8,128)(2,1)S(1)}, u32[]{:S(2)}, u32[]{:S(2)}) collective-permute-start(bf16[64,3584]{1,0:T(8,128)(2,1)} %get-tuple-element.174), channel_id=1, source_target_pairs={{0,4},{1,5},{4,8},{5,9},{8,12},{9,13},{12,14},{13,15},{14,10},{15,... | collective-permute-start | bytes 1376264 | tf_op jit(solution)/shard_map/ppermute | solution.py:245
  164.7 10.5 %collective-permute-start.30 = (bf16[64,3584]{1,0:T(8,128)(2,1)}, bf16[64,3584]{1,0:T(8,128)(2,1)S(1)}, u32[]{:S(2)}, u32[]{:S(2)}) collective-permute-start(bf16[64,3584]{1,0:T(8,128)(2,1)} %get-tuple-element.186), channel_id=1, source_target_pairs={{0,2},{1,3},{4,0},{5,1},{8,4},{9,5},{12,8},{13,9},{14,12},{15,13},... | collective-permute-start | bytes 1376264 | tf_op jit(solution)/shard_map/ppermute | solution.py:245
  169.9 5.3 %copy-start.19 = (bf16[64,3584]{1,0:T(8,128)(2,1)}, bf16[64,3584]{1,0:T(8,128)(2,1)S(1)}, u32[]{:S(2)}) copy-start(bf16[64,3584]{1,0:T(8,128)(2,1)S(1)} %collective-permute-done.28.refs_2_) | copy-start | bytes 1376260
  169.9 5.3 %copy-start.20 = (bf16[64,3584]{1,0:T(8,128)(2,1)}, bf16[64,3584]{1,0:T(8,128)(2,1)S(1)}, u32[]{:S(2)}) copy-start(bf16[64,3584]{1,0:T(8,128)(2,1)S(1)} %collective-permute-done.29.refs_4_) | copy-start | bytes 1376260
  173.9 1.3 copy-start.27
  (14 other events, 10.9 us)

commit v6 on v5

--- a/solution.py
+++ b/solution.py
@@ -84,17 +84,21 @@
 
 
 def add_kernel(n, *refs):
-    for left_ref, right_ref, out_ref in zip(refs[:n], refs[n : 2 * n], refs[2 * n :]):
+    for left_ref, right_ref, out_ref in zip(refs[:n], refs[n : 2 * n], refs[-n:]):
         out_ref[...] = left_ref[...] + right_ref[...]
 
 
-def add(lefts, rights):
+def add(lefts, rights, after):
     n = len(lefts)
     return pl.pallas_call(
         functools.partial(add_kernel, n),
+        in_specs=[pl.BlockSpec(memory_space=pltpu.VMEM)] * (2 * n)
+        + [pl.BlockSpec(memory_space=pl.ANY)] * len(after),
+        out_specs=[pl.BlockSpec(memory_space=pltpu.VMEM)] * n,
         out_shape=[jax.ShapeDtypeStruct(left.shape, left.dtype) for left in lefts],
-        cost_estimate=small_cost(),
-    )(*lefts, *rights)
+        compiler_params=pltpu.CompilerParams(vmem_limit_bytes=6 * MIB),
+        cost_estimate=small_cost(),
+    )(*lefts, *rights, *after)
 
 
 def close_kernel(*refs):
@@ -111,6 +115,7 @@
     return pl.pallas_call(
         close_kernel,
         out_shape=jax.ShapeDtypeStruct((2 * half, dim), terms[0].dtype),
+        compiler_params=pltpu.CompilerParams(vmem_limit_bytes=8 * MIB),
         cost_estimate=small_cost(),
     )(*terms)
 
@@ -135,6 +140,7 @@
     return pl.pallas_call(
         functools.partial(rows_kernel, experts, ids.shape[1], half),
         out_shape=[jax.ShapeDtypeStruct((half, dim + LANES), tokens.dtype)] * 2,
+        compiler_params=pltpu.CompilerParams(vmem_limit_bytes=6 * MIB),
         cost_estimate=small_cost(),
     )(tokens, ids.T, codes.T)
 
@@ -150,6 +156,7 @@
         + [pl.BlockSpec(memory_space=pltpu.VMEM)] * len(arrays),
         out_specs=pl.BlockSpec(memory_space=pltpu.SMEM),
         out_shape=jax.ShapeDtypeStruct(expert.shape, expert.dtype),
+        compiler_params=pltpu.CompilerParams(vmem_limit_bytes=2 * MIB),
         cost_estimate=small_cost(),
     )(expert, *arrays)
 
@@ -181,12 +188,13 @@
     behind = [[rows[0]], [rows[1]]]
     parts = {}
 
-    def send(s, after):
+    def send(s, after=(), behind_half=0):
         for h in range(2):
             if s > 1:
-                held = [parts[name] for name in after]
+                names = after if h == behind_half else ()
+                held = [parts[name] for name in names]
                 pair, held = lax.optimization_barrier(([ahead[h][s - 1], behind[h][s - 1]], held))
-                parts.update(zip(after, held))
+                parts.update(zip(names, held))
                 ahead[h][s - 1], behind[h][s - 1] = pair
             if s < far or h == 0:
                 ahead[h].append(lax.ppermute(ahead[h][s - 1], "node", forward))
@@ -207,19 +215,17 @@
         parts.update(zip(names, expert_parts(ring, expert, blocks, own, other)))
         return names
 
-    send(1, [])
+    send(1)
     own, _ = lax.optimization_barrier(((w_gate, w_up, w_down), rows))
     expert = hand_on(expert, own)
     other = [lax.ppermute(own[0], "node", swap)]
-    for h, weight in ((0, own[1]), (1, own[2])):
-        pair, expert, weight = lax.optimization_barrier(
-            ([ahead[h][1], behind[h][1]], expert, weight)
-        )
-        ahead[h][1], behind[h][1] = pair
-        other.append(lax.ppermute(weight, "node", swap))
+    arrived = [ahead[0][1], behind[0][1], ahead[1][1], behind[1][1]]
+    arrived, expert, up, down = lax.optimization_barrier((arrived, expert, own[1], own[2]))
+    ahead[0][1], behind[0][1], ahead[1][1], behind[1][1] = arrived
+    other += [lax.ppermute(up, "node", swap), lax.ppermute(down, "node", swap)]
     done = []
     for s in range(2, far + 1):
-        send(s, done)
+        send(s, done, 1 if s < far else 0)
         done = work([1 - s, s - 1], expert)
     work([0, far], expert, done)
     parts[-far, 1] = parts[far, 1]
@@ -229,20 +235,26 @@
     early = [(h, sign) for h, sign in streams if (h == 0) != (sign == 1)]
     late = [stream for stream in streams if stream not in early]
     came = {}
-    for h, sign in early:
-        came[h, sign] = lax.ppermute(parts[sign * (far - 1), h], "node", ways[sign])
-    first = [parts[sign * far, h] for h, sign in late]
-    first, held = lax.optimization_barrier((first, [came[stream] for stream in early]))
+
+    def pass_on(group, totals):
+        for (h, sign), total in zip(group, totals):
+            came[h, sign] = lax.ppermute(total, "node", ways[sign])
+
+    def summed(group, at, after=()):
+        lefts = [parts[sign * at, h] for h, sign in group]
+        return add(lefts, [came[stream] for stream in group], after)
+
+    pass_on(early, [parts[sign * (far - 1), h] for h, sign in early])
+    late_totals = [parts[sign * far, h] for h, sign in late]
+    held = [came[stream] for stream in early]
+    late_totals, held = lax.optimization_barrier((late_totals, held))
     came.update(zip(early, held))
-    for (h, sign), total in zip(late, first):
-        came[h, sign] = lax.ppermute(total, "node", ways[sign])
-    for d in range(far - 1, 0, -1):
-        for group, at in ((early, d - 1), (late, d)):
-            if at:
-                lefts = [parts[sign * at, h] for h, sign in group]
-                totals = add(lefts, [came[stream] for stream in group])
-                for (h, sign), total in zip(group, totals):
-                    came[h, sign] = lax.ppermute(total, "node", ways[sign])
+    for at in range(far - 1, -1, -1):
+        if at > 1:
+            pass_on(early, summed(early, at - 1))
+        pass_on(late, late_totals)
+        if at:
+            late_totals = summed(late, at, [came[stream] for stream in early])
     return close([t for h in range(2) for t in (parts[0, h], came[h, 1], came[h, -1])])
 
 

time: 180 us -> 166 us (0.922)
  Pallas kernels: 64.5 us -> 44.6 us
  waiting for transfers between devices: 65.6 us -> 81.1 us
  local copies, waits for them, and re-layouts: 18.7 us -> 8.67 us
    pallas_call x5, Pallas kernels: 12.1 us -> 0.47 us  [add(): pl.pallas_call(functools.partial(add_kernel, n), in_specs=[pl.BlockSpec(m...]
    unnamed x62 -> x18, local copies, waits for them, and re-layouts: 18.7 us -> 8.67 us
    ppermute x7, starting transfers between devices: 3.22 us -> 12.2 us  [send(): behind[h].append(lax.ppermute(behind[h][s - 1], 'node', backward))]
    ppermute x7, starting transfers between devices: 11.9 us -> 3.87 us  [send(): ahead[h].append(lax.ppermute(ahead[h][s - 1], 'node', forward))]
    ppermute x7, waiting for transfers between devices: 3.69 us -> 10.3 us  [send(): behind[h].append(lax.ppermute(behind[h][s - 1], 'node', backward))]
    ppermute x16, waiting for transfers between devices: 44.4 us -> 51 us  [the longest x14 51 us: pass_on(): came[h, sign] = lax.ppermute(total, 'node', ways[sign])]
    pallas_call x1, Pallas kernels: 4.72 us -> 0.52 us  [hand_on(): pl.pallas_call(hand_on_kernel, in_specs=[pl.BlockSpec(memory_space=pltpu....]
    ppermute x7, waiting for transfers between devices: 17.5 us -> 19.8 us  [send(): ahead[h].append(lax.ppermute(ahead[h][s - 1], 'node', forward))]
  transfers between devices with their start and end apart: 31 -> 31, of which waited for: 17 -> 16; matrix products, arithmetic and copies ran while one was open for 0% -> 0% of each run, Pallas kernels for 32% -> 26%
where the time goes in v6:
time: 166 us
  waiting for transfers between devices  81.1 us (49%)
  Pallas kernels  44.6 us (27%)
  starting transfers between devices  31.1 us (19%)
  local copies, waits for them, and re-layouts  8.67 us (5%)
    ppermute x14, waiting for transfers between devices, pass_on(): came[h, sign] = lax.ppermute(total, 'node', ways[sign])  51 us
    pallas_call x4, Pallas kernels, expert_parts(): pl.pallas_call(functools.partial(expert_kernel, n, experts, dim, half), i...  42.3 us
    ppermute x7, waiting for transfers between devices, send(): ahead[h].append(lax.ppermute(ahead[h][s - 1], 'node', forward))  19.8 us
    ppermute x14, starting transfers between devices, pass_on(): came[h, sign] = lax.ppermute(total, 'node', ways[sign])  14.5 us
    ppermute x7, starting transfers between devices, send(): behind[h].append(lax.ppermute(behind[h][s - 1], 'node', backward))  12.2 us
    ppermute x7, waiting for transfers between devices, send(): behind[h].append(lax.ppermute(behind[h][s - 1], 'node', backward))  10.3 us
    unnamed x18, local copies, waits for them, and re-layouts  8.67 us
    ppermute x7, starting transfers between devices, send(): ahead[h].append(lax.ppermute(ahead[h][s - 1], 'node', forward))  3.87 us
  transfers between devices with their start and end apart: 31, of which 16 were waited for; matrix products, arithmetic and copies ran while one was open for 0% of the time, Pallas kernels for 26%

profile of v6, /device:TPU:0, one launch (start us, length us, event | category | flops | bytes accessed | tf_op | source)
XLA Modules:
  0.0 165.7 jit_solution(15164259489817165310)
XLA Ops:
  0.0 1.2 copy-done.6
  1.2 0.7 copy-done.7
  1.9 0.7 copy-done.8
  2.7 3.0 %collective-permute-start.1 = (bf16[64,3712]{1,0:T(8,128)(2,1)S(1)}, bf16[64,3712]{1,0:T(8,128)(2,1)S(1)}, u32[]{:S(2)}, u32[]{:S(2)}) collective-permute-start(bf16[64,3712]{1,0:T(8,128)(2,1)S(1)} %get-tuple-element.135.refs_0_), channel_id=1, source_target_pairs={{0,2},{1,3},{4,0},{5,1},{8,4},{9,5},{12,8},{13,9},{14,12},{15,13},... | collective-permute-start | bytes 1425416 | tf_op jit(solution)/shard_map/ppermute | solution.py:202
  5.8 1.9 %collective-permute-start.3 = (bf16[64,3712]{1,0:T(8,128)(2,1)S(1)}, bf16[64,3712]{1,0:T(8,128)(2,1)S(1)}, u32[]{:S(2)}, u32[]{:S(2)}) collective-permute-start(bf16[64,3712]{1,0:T(8,128)(2,1)S(1)} %get-tuple-element.136.refs_1_), channel_id=1, source_target_pairs={{0,2},{1,3},{4,0},{5,1},{8,4},{9,5},{12,8},{13,9},{14,12},{15,13},... | collective-permute-start | bytes 1425416 | tf_op jit(solution)/shard_map/ppermute | solution.py:202
  7.9 2.0 %copy-done = bf16[3584,512]{1,0:T(8,128)(2,1)S(1)} copy-done((bf16[3584,512]{1,0:T(8,128)(2,1)S(1)}, bf16[3584,512]{1,0:T(8,128)(2,1)}, u32[]{:S(2)}) %copy-start) | copy-done | bytes 3670040
  9.9 2.0 %copy-done.2 = bf16[3584,512]{1,0:T(8,128)(2,1)S(1)} copy-done((bf16[3584,512]{1,0:T(8,128)(2,1)S(1)}, bf16[3584,512]{1,0:T(8,128)(2,1)}, u32[]{:S(2)}) %copy-start.2) | copy-done | bytes 3670040
  11.9 2.0 %copy-done.4 = bf16[512,3584]{1,0:T(8,128)(2,1)S(1)} copy-done((bf16[512,3584]{1,0:T(8,128)(2,1)S(1)}, bf16[512,3584]{1,0:T(8,128)(2,1)}, u32[]{:S(2)}) %copy-start.4) | copy-done | bytes 3670040
  14.0 0.5 shard_map.65.expert_ref
  14.5 3.0 %collective-permute-done.1.refs_2_ = bf16[64,3712]{1,0:T(8,128)(2,1)S(1)} collective-permute-done((bf16[64,3712]{1,0:T(8,128)(2,1)S(1)}, bf16[64,3712]{1,0:T(8,128)(2,1)S(1)}, u32[]{:S(2)}, u32[]{:S(2)}) %collective-permute-start.1) | collective-permute-done | bytes 475168 | tf_op jit(solution)/shard_map/ppermute | solution.py:202
  17.5 2.0 %collective-permute-done.refs_0_ = bf16[64,3712]{1,0:T(8,128)(2,1)S(1)} collective-permute-done((bf16[64,3712]{1,0:T(8,128)(2,1)S(1)}, bf16[64,3712]{1,0:T(8,128)(2,1)S(1)}, u32[]{:S(2)}, u32[]{:S(2)}) %collective-permute-start) | collective-permute-done | bytes 475168 | tf_op jit(solution)/shard_map/ppermute | solution.py:200
  19.5 7.3 %collective-permute-done.3.refs_3_ = bf16[64,3712]{1,0:T(8,128)(2,1)S(1)} collective-permute-done((bf16[64,3712]{1,0:T(8,128)(2,1)S(1)}, bf16[64,3712]{1,0:T(8,128)(2,1)S(1)}, u32[]{:S(2)}, u32[]{:S(2)}) %collective-permute-start.3) | collective-permute-done | bytes 475168 | tf_op jit(solution)/shard_map/ppermute | solution.py:202
  26.8 1.4 collective-permute-done.2.refs_1_
  28.2 0.5 collective-permute-start.12
  29.1 1.6 collective-permute-start.5
  30.7 10.8 %collective-permute-done.4.refs_0_ = bf16[64,3712]{1,0:T(8,128)(2,1)S(1)} collective-permute-done((bf16[64,3712]{1,0:T(8,128)(2,1)S(1)}, bf16[64,3712]{1,0:T(8,128)(2,1)S(1)}, u32[]{:S(2)}, u32[]{:S(2)}) %collective-permute-start.4) | collective-permute-done | bytes 475168 | tf_op jit(solution)/shard_map/ppermute | solution.py:200
  41.9 1.6 collective-permute-start.9
  43.9 1.6 collective-permute-start.7
  45.6 10.6 %shard_map.66 = (bf16[64,3584]{1,0:T(8,128)(2,1)S(1)}, bf16[64,3584]{1,0:T(8,128)(2,1)S(1)}, bf16[64,3584]{1,0:T(8,128)(2,1)S(1)}, bf16[64,3584]{1,0:T(8,128)(2,1)S(1)}) custom-call(s32[1]{0:T(128)} %shard_map.65.expert_ref, bf16[64,3712]{1,0:T(8,128)(2,1)S(1)} %collective-permute-done.refs_0_, bf16[64,3712]{1,0:T(8,128)(2,1)S(1)} %collective-permute-done.2.refs_1_, ...), custom_call_target="tpu_custom_call" | custom-call | flops 1024 | bytes 1024 | tf_op jit(solution)/shard_map/pallas_call | solution.py:71
  56.2 1.2 collective-permute-start.14
  57.4 0.9 collective-permute-start.15
  58.3 10.6 %shard_map.67 = (bf16[64,3584]{1,0:T(8,128)(2,1)S(1)}, bf16[64,3584]{1,0:T(8,128)(2,1)S(1)}, bf16[64,3584]{1,0:T(8,128)(2,1)S(1)}, bf16[64,3584]{1,0:T(8,128)(2,1)S(1)}) custom-call(s32[1]{0:T(128)} %shard_map.65.expert_ref, bf16[64,3712]{1,0:T(8,128)(2,1)S(1)} %collective-permute-done.4.refs_0_, bf16[64,3712]{1,0:T(8,128)(2,1)S(1)} %collective-permute-done.8.refs_1_, ...), custom_call_target="tpu_custom_call" | custom-call | flops 1024 | bytes 1024 | tf_op jit(solution)/shard_map/pallas_call | solution.py:71
  68.9 1.2 collective-permute-start.13
  70.1 5.6 %collective-permute-done.14.refs_1_ = bf16[64,3712]{1,0:T(8,128)(2,1)S(1)} collective-permute-done((bf16[64,3712]{1,0:T(8,128)(2,1)S(1)}, bf16[64,3712]{1,0:T(8,128)(2,1)S(1)}, u32[]{:S(2)}, u32[]{:S(2)}) %collective-permute-start.14) | collective-permute-done | bytes 475168 | tf_op jit(solution)/shard_map/ppermute | solution.py:200
  75.7 1.6 collective-permute-start.16
  77.3 10.6 %shard_map.68 = (bf16[64,3584]{1,0:T(8,128)(2,1)S(1)}, bf16[64,3584]{1,0:T(8,128)(2,1)S(1)}, bf16[64,3584]{1,0:T(8,128)(2,1)S(1)}, bf16[64,3584]{1,0:T(8,128)(2,1)S(1)}) custom-call(s32[1]{0:T(128)} %shard_map.65.expert_ref, bf16[64,3712]{1,0:T(8,128)(2,1)S(1)} %collective-permute-done.6.refs_0_, bf16[64,3712]{1,0:T(8,128)(2,1)S(1)} %collective-permute-done.14.refs_1_, ...), custom_call_target="tpu_custom_call" | custom-call | flops 1024 | bytes 1024 | tf_op jit(solution)/shard_map/pallas_call | solution.py:71
  87.8 1.6 collective-permute-start.17
  89.9 10.6 %shard_map.69 = (bf16[64,3584]{1,0:T(8,128)(2,1)S(1)}, bf16[64,3584]{1,0:T(8,128)(2,1)S(1)}, bf16[64,3584]{1,0:T(8,128)(2,1)S(1)}, bf16[64,3584]{1,0:T(8,128)(2,1)S(1)}) custom-call(s32[1]{0:T(128)} %shard_map.65.expert_ref, bf16[64,3712]{1,0:T(8,128)(2,1)S(1)} %get-tuple-element.135.refs_0_, bf16[64,3712]{1,0:T(8,128)(2,1)S(1)} %get-tuple-element.136.refs_1_, ...), custom_call_target="tpu_custom_call" | custom-call | flops 1024 | bytes 1024 | tf_op jit(solution)/shard_map/pallas_call | solution.py:71
  100.6 1.6 collective-permute-start.21
  102.7 0.5 collective-permute-start.19
  103.2 1.6 collective-permute-start.20
  104.7 9.4 %collective-permute-done.21.refs_4_.refs_2_ = bf16[64,3584]{1,0:T(8,128)(2,1)S(1)} collective-permute-done((bf16[64,3584]{1,0:T(8,128)(2,1)S(1)}, bf16[64,3584]{1,0:T(8,128)(2,1)S(1)}, u32[]{:S(2)}, u32[]{:S(2)}) %collective-permute-start.21) | collective-permute-done | bytes 458784 | tf_op jit(solution)/shard_map/ppermute | solution.py:241
  114.1 1.6 collective-permute-done.22.refs_5_.refs_3_
  115.8 1.6 collective-permute-start.25
  117.4 0.4 collective-permute-start.26
  117.9 7.7 %collective-permute-done.19.refs_2_ = bf16[64,3584]{1,0:T(8,128)(2,1)S(1)} collective-permute-done((bf16[64,3584]{1,0:T(8,128)(2,1)S(1)}, bf16[64,3584]{1,0:T(8,128)(2,1)S(1)}, u32[]{:S(2)}, u32[]{:S(2)}) %collective-permute-start.19) | collective-permute-done | bytes 458784 | tf_op jit(solution)/shard_map/ppermute | solution.py:241
  125.6 0.5 collective-permute-start.23
  126.1 1.6 collective-permute-start.24
  127.7 5.5 %collective-permute-done.25.refs_4_.refs_2_ = bf16[64,3584]{1,0:T(8,128)(2,1)S(1)} collective-permute-done((bf16[64,3584]{1,0:T(8,128)(2,1)S(1)}, bf16[64,3584]{1,0:T(8,128)(2,1)S(1)}, u32[]{:S(2)}, u32[]{:S(2)}) %collective-permute-start.25) | collective-permute-done | bytes 458784 | tf_op jit(solution)/shard_map/ppermute | solution.py:241
  133.2 1.3 collective-permute-done.26.refs_5_.refs_4_
  134.5 7.8 %collective-permute-done.23.refs_2_ = bf16[64,3584]{1,0:T(8,128)(2,1)S(1)} collective-permute-done((bf16[64,3584]{1,0:T(8,128)(2,1)S(1)}, bf16[64,3584]{1,0:T(8,128)(2,1)S(1)}, u32[]{:S(2)}, u32[]{:S(2)}) %collective-permute-start.23) | collective-permute-done | bytes 458784 | tf_op jit(solution)/shard_map/ppermute | solution.py:241
  142.4 0.5 collective-permute-start.27
  142.9 1.6 collective-permute-start.28
  144.5 10.5 %collective-permute-done.27.refs_2_ = bf16[64,3584]{1,0:T(8,128)(2,1)S(1)} collective-permute-done((bf16[64,3584]{1,0:T(8,128)(2,1)S(1)}, bf16[64,3584]{1,0:T(8,128)(2,1)S(1)}, u32[]{:S(2)}, u32[]{:S(2)}) %collective-permute-start.27) | collective-permute-done | bytes 458784 | tf_op jit(solution)/shard_map/ppermute | solution.py:241
  155.0 0.8 collective-permute-done.28.refs_3_
  155.9 2.0 %collective-permute-start.30 = (bf16[64,3584]{1,0:T(8,128)(2,1)S(1)}, bf16[64,3584]{1,0:T(8,128)(2,1)S(1)}, u32[]{:S(2)}, u32[]{:S(2)}) collective-permute-start(bf16[64,3584]{1,0:T(8,128)(2,1)S(1)} %get-tuple-element.168), channel_id=1, source_target_pairs={{0,2},{1,3},{4,0},{5,1},{8,4},{9,5},{12,8},{13,9},{14,12},{15,13},... | collective-permute-start | bytes 1376264 | tf_op jit(solution)/shard_map/ppermute | solution.py:241
  157.9 6.5 %collective-permute-done.29.refs_1_ = bf16[64,3584]{1,0:T(8,128)(2,1)S(1)} collective-permute-done((bf16[64,3584]{1,0:T(8,128)(2,1)S(1)}, bf16[64,3584]{1,0:T(8,128)(2,1)S(1)}, u32[]{:S(2)}, u32[]{:S(2)}) %collective-permute-start.29) | collective-permute-done | bytes 458784 | tf_op jit(solution)/shard_map/ppermute | solution.py:241
  164.4 1.3 shard_map.75
  (44 shorter events, 3.1 us)
Async XLA Ops:
  0.0 1.2 copy-start.6
  1.2 0.7 copy-start.7
  1.9 0.7 copy-start.8
  2.7 14.8 %collective-permute-start.1 = (bf16[64,3712]{1,0:T(8,128)(2,1)S(1)}, bf16[64,3712]{1,0:T(8,128)(2,1)S(1)}, u32[]{:S(2)}, u32[]{:S(2)}) collective-permute-start(bf16[64,3712]{1,0:T(8,128)(2,1)S(1)} %get-tuple-element.135.refs_0_), channel_id=1, source_target_pairs={{0,2},{1,3},{4,0},{5,1},{8,4},{9,5},{12,8},{13,9},{14,12},{15,13},... | collective-permute-start | bytes 1425416 | tf_op jit(solution)/shard_map/ppermute | solution.py:202
  5.7 13.8 %collective-permute-start = (bf16[64,3712]{1,0:T(8,128)(2,1)S(1)}, bf16[64,3712]{1,0:T(8,128)(2,1)S(1)}, u32[]{:S(2)}, u32[]{:S(2)}) collective-permute-start(bf16[64,3712]{1,0:T(8,128)(2,1)S(1)} %get-tuple-element.135.refs_0_), channel_id=1, source_target_pairs={{0,4},{1,5},{4,8},{5,9},{8,12},{9,13},{12,14},{13,15},{14,10},{15,... | collective-permute-start | bytes 1425416 | tf_op jit(solution)/shard_map/ppermute | solution.py:200
  5.8 21.0 %collective-permute-start.3 = (bf16[64,3712]{1,0:T(8,128)(2,1)S(1)}, bf16[64,3712]{1,0:T(8,128)(2,1)S(1)}, u32[]{:S(2)}, u32[]{:S(2)}) collective-permute-start(bf16[64,3712]{1,0:T(8,128)(2,1)S(1)} %get-tuple-element.136.refs_1_), channel_id=1, source_target_pairs={{0,2},{1,3},{4,0},{5,1},{8,4},{9,5},{12,8},{13,9},{14,12},{15,13},... | collective-permute-start | bytes 1425416 | tf_op jit(solution)/shard_map/ppermute | solution.py:202
  7.7 20.5 %collective-permute-start.2 = (bf16[64,3712]{1,0:T(8,128)(2,1)S(1)}, bf16[64,3712]{1,0:T(8,128)(2,1)S(1)}, u32[]{:S(2)}, u32[]{:S(2)}) collective-permute-start(bf16[64,3712]{1,0:T(8,128)(2,1)S(1)} %get-tuple-element.136.refs_1_), channel_id=1, source_target_pairs={{0,4},{1,5},{4,8},{5,9},{8,12},{9,13},{12,14},{13,15},{14,10},{15,... | collective-permute-start | bytes 1425416 | tf_op jit(solution)/shard_map/ppermute | solution.py:200
  7.8 35.7 %collective-permute-start.10 = (bf16[3584,512]{1,0:T(8,128)(2,1)}, bf16[3584,512]{1,0:T(8,128)(2,1)}, u32[]{:S(2)}, u32[]{:S(2)}) collective-permute-start(bf16[3584,512]{1,0:T(8,128)(2,1)} %refs_4_.3), channel_id=1, source_target_pairs={{0,1},{1,0},{2,3},{3,2},{4,5},{5,4},{6,7},{7,6},{8,9},{9,8},{10,11... | collective-permute-start | bytes 11010056 | tf_op jit(solution)/shard_map/ppermute | solution.py:221
  7.9 2.0 %copy-start = (bf16[3584,512]{1,0:T(8,128)(2,1)S(1)}, bf16[3584,512]{1,0:T(8,128)(2,1)}, u32[]{:S(2)}) copy-start(bf16[3584,512]{1,0:T(8,128)(2,1)} %refs_4_.3) | copy-start | bytes 11010052
  9.9 2.0 %copy-start.2 = (bf16[3584,512]{1,0:T(8,128)(2,1)S(1)}, bf16[3584,512]{1,0:T(8,128)(2,1)}, u32[]{:S(2)}) copy-start(bf16[3584,512]{1,0:T(8,128)(2,1)} %refs_5_.3) | copy-start | bytes 11010052
  11.9 2.0 %copy-start.4 = (bf16[512,3584]{1,0:T(8,128)(2,1)S(1)}, bf16[512,3584]{1,0:T(8,128)(2,1)}, u32[]{:S(2)}) copy-start(bf16[512,3584]{1,0:T(8,128)(2,1)} %refs_6_.3) | copy-start | bytes 11010052
  14.0 31.6 %copy-start.1 = (bf16[3584,512]{1,0:T(8,128)(2,1)S(1)}, bf16[3584,512]{1,0:T(8,128)(2,1)}, u32[]{:S(2)}) copy-start(bf16[3584,512]{1,0:T(8,128)(2,1)} %refs_4_.3) | copy-start | bytes 11010052
  14.0 31.6 %copy-start.3 = (bf16[3584,512]{1,0:T(8,128)(2,1)S(1)}, bf16[3584,512]{1,0:T(8,128)(2,1)}, u32[]{:S(2)}) copy-start(bf16[3584,512]{1,0:T(8,128)(2,1)} %refs_5_.3) | copy-start | bytes 11010052
  14.0 31.6 %copy-start.5 = (bf16[512,3584]{1,0:T(8,128)(2,1)S(1)}, bf16[512,3584]{1,0:T(8,128)(2,1)}, u32[]{:S(2)}) copy-start(bf16[512,3584]{1,0:T(8,128)(2,1)} %refs_6_.3) | copy-start | bytes 11010052
  28.2 15.7 %collective-permute-start.11 = (bf16[3584,512]{1,0:T(8,128)(2,1)S(1)}, bf16[3584,512]{1,0:T(8,128)(2,1)S(1)}, u32[]{:S(2)}, u32[]{:S(2)}) collective-permute-start(bf16[3584,512]{1,0:T(8,128)(2,1)S(1)} %copy-done.2), channel_id=1, source_target_pairs={{0,1},{1,0},{2,3},{3,2},{4,5},{5,4},{6,7},{7,6},{8,9},{9,8},{10,11... | collective-permute-start | bytes 11010056 | tf_op jit(solution)/shard_map/ppermute | solution.py:225
  28.2 17.4 %collective-permute-start.12 = (bf16[512,3584]{1,0:T(8,128)(2,1)S(1)}, bf16[512,3584]{1,0:T(8,128)(2,1)S(1)}, u32[]{:S(2)}, u32[]{:S(2)}) collective-permute-start(bf16[512,3584]{1,0:T(8,128)(2,1)S(1)} %copy-done.4), channel_id=1, source_target_pairs={{0,1},{1,0},{2,3},{3,2},{4,5},{5,4},{6,7},{7,6},{8,9},{9,8},{10,11... | collective-permute-start | bytes 11010056 | tf_op jit(solution)/shard_map/ppermute | solution.py:225
  28.7 12.8 %collective-permute-start.4 = (bf16[64,3712]{1,0:T(8,128)(2,1)S(1)}, bf16[64,3712]{1,0:T(8,128)(2,1)S(1)}, u32[]{:S(2)}, u32[]{:S(2)}) collective-permute-start(bf16[64,3712]{1,0:T(8,128)(2,1)S(1)} %collective-permute-done.refs_0_), channel_id=1, source_target_pairs={{0,4},{1,5},{4,8},{5,9},{8,12},{9,13},{12,14},{13,15},{14,10},{15,... | collective-permute-start | bytes 1425416 | tf_op jit(solution)/shard_map/ppermute | solution.py:200
  29.1 12.8 %collective-permute-start.5 = (bf16[64,3712]{1,0:T(8,128)(2,1)S(1)}, bf16[64,3712]{1,0:T(8,128)(2,1)S(1)}, u32[]{:S(2)}, u32[]{:S(2)}) collective-permute-start(bf16[64,3712]{1,0:T(8,128)(2,1)S(1)} %collective-permute-done.1.refs_2_), channel_id=1, source_target_pairs={{0,2},{1,3},{4,0},{5,1},{8,4},{9,5},{12,8},{13,9},{14,12},{15,13},... | collective-permute-start | bytes 1425416 | tf_op jit(solution)/shard_map/ppermute | solution.py:202
  41.5 14.7 %collective-permute-start.8 = (bf16[64,3712]{1,0:T(8,128)(2,1)S(1)}, bf16[64,3712]{1,0:T(8,128)(2,1)S(1)}, u32[]{:S(2)}, u32[]{:S(2)}) collective-permute-start(bf16[64,3712]{1,0:T(8,128)(2,1)S(1)} %collective-permute-done.2.refs_1_), channel_id=1, source_target_pairs={{0,4},{1,5},{4,8},{5,9},{8,12},{9,13},{12,14},{13,15},{14,10},{15,... | collective-permute-start | bytes 1425416 | tf_op jit(solution)/shard_map/ppermute | solution.py:200
  41.9 14.3 %collective-permute-start.9 = (bf16[64,3712]{1,0:T(8,128)(2,1)S(1)}, bf16[64,3712]{1,0:T(8,128)(2,1)S(1)}, u32[]{:S(2)}, u32[]{:S(2)}) collective-permute-start(bf16[64,3712]{1,0:T(8,128)(2,1)S(1)} %collective-permute-done.3.refs_3_), channel_id=1, source_target_pairs={{0,2},{1,3},{4,0},{5,1},{8,4},{9,5},{12,8},{13,9},{14,12},{15,13},... | collective-permute-start | bytes 1425416 | tf_op jit(solution)/shard_map/ppermute | solution.py:202
  43.5 25.3 %collective-permute-start.6 = (bf16[64,3712]{1,0:T(8,128)(2,1)S(1)}, bf16[64,3712]{1,0:T(8,128)(2,1)S(1)}, u32[]{:S(2)}, u32[]{:S(2)}) collective-permute-start(bf16[64,3712]{1,0:T(8,128)(2,1)S(1)} %collective-permute-done.4.refs_0_), channel_id=1, source_target_pairs={{0,4},{1,5},{4,8},{5,9},{8,12},{9,13},{12,14},{13,15},{14,10},{15,... | collective-permute-start | bytes 1425416 | tf_op jit(solution)/shard_map/ppermute | solution.py:200
  43.9 24.9 %collective-permute-start.7 = (bf16[64,3712]{1,0:T(8,128)(2,1)S(1)}, bf16[64,3712]{1,0:T(8,128)(2,1)S(1)}, u32[]{:S(2)}, u32[]{:S(2)}) collective-permute-start(bf16[64,3712]{1,0:T(8,128)(2,1)S(1)} %collective-permute-done.5.refs_2_), channel_id=1, source_target_pairs={{0,2},{1,3},{4,0},{5,1},{8,4},{9,5},{12,8},{13,9},{14,12},{15,13},... | collective-permute-start | bytes 1425416 | tf_op jit(solution)/shard_map/ppermute | solution.py:202
  56.2 19.5 %collective-permute-start.14 = (bf16[64,3712]{1,0:T(8,128)(2,1)S(1)}, bf16[64,3712]{1,0:T(8,128)(2,1)S(1)}, u32[]{:S(2)}, u32[]{:S(2)}) collective-permute-start(bf16[64,3712]{1,0:T(8,128)(2,1)S(1)} %collective-permute-done.8.refs_1_), channel_id=1, source_target_pairs={{0,4},{1,5},{4,8},{5,9},{8,12},{9,13},{12,14},{13,15},{14,10},{15,... | collective-permute-start | bytes 1425416 | tf_op jit(solution)/shard_map/ppermute | solution.py:200
  57.4 18.3 %collective-permute-start.15 = (bf16[64,3712]{1,0:T(8,128)(2,1)S(1)}, bf16[64,3712]{1,0:T(8,128)(2,1)S(1)}, u32[]{:S(2)}, u32[]{:S(2)}) collective-permute-start(bf16[64,3712]{1,0:T(8,128)(2,1)S(1)} %collective-permute-done.9.refs_3_), channel_id=1, source_target_pairs={{0,2},{1,3},{4,0},{5,1},{8,4},{9,5},{12,8},{13,9},{14,12},{15,13},... | collective-permute-start | bytes 1425416 | tf_op jit(solution)/shard_map/ppermute | solution.py:202
  68.9 19.0 %collective-permute-start.13 = (bf16[64,3712]{1,0:T(8,128)(2,1)S(1)}, bf16[64,3712]{1,0:T(8,128)(2,1)S(1)}, u32[]{:S(2)}, u32[]{:S(2)}) collective-permute-start(bf16[64,3712]{1,0:T(8,128)(2,1)S(1)} %collective-permute-done.6.refs_0_), channel_id=1, source_target_pairs={{0,4},{1,5},{4,8},{5,9},{8,12},{9,13},{12,14},{13,15},{14,10},{15,... | collective-permute-start | bytes 1425416 | tf_op jit(solution)/shard_map/ppermute | solution.py:200
  75.7 12.2 %collective-permute-start.16 = (bf16[64,3712]{1,0:T(8,128)(2,1)S(1)}, bf16[64,3712]{1,0:T(8,128)(2,1)S(1)}, u32[]{:S(2)}, u32[]{:S(2)}) collective-permute-start(bf16[64,3712]{1,0:T(8,128)(2,1)S(1)} %collective-permute-done.15.refs_3_), channel_id=1, source_target_pairs={{0,2},{1,3},{4,0},{5,1},{8,4},{9,5},{12,8},{13,9},{14,12},{15,13},... | collective-permute-start | bytes 1425416 | tf_op jit(solution)/shard_map/ppermute | solution.py:202
  87.8 12.7 %collective-permute-start.17 = (bf16[64,3584]{1,0:T(8,128)(2,1)S(1)}, bf16[64,3584]{1,0:T(8,128)(2,1)S(1)}, u32[]{:S(2)}, u32[]{:S(2)}) collective-permute-start(bf16[64,3584]{1,0:T(8,128)(2,1)S(1)} %get-tuple-element.148), channel_id=1, source_target_pairs={{0,2},{1,3},{4,0},{5,1},{8,4},{9,5},{12,8},{13,9},{14,12},{15,13},... | collective-permute-start | bytes 1376264 | tf_op jit(solution)/shard_map/ppermute | solution.py:241
  89.5 11.0 %collective-permute-start.18 = (bf16[64,3584]{1,0:T(8,128)(2,1)S(1)}, bf16[64,3584]{1,0:T(8,128)(2,1)S(1)}, u32[]{:S(2)}, u32[]{:S(2)}) collective-permute-start(bf16[64,3584]{1,0:T(8,128)(2,1)S(1)} %get-tuple-element.149), channel_id=1, source_target_pairs={{0,4},{1,5},{4,8},{5,9},{8,12},{9,13},{12,14},{13,15},{14,10},{15,... | collective-permute-start | bytes 1376264 | tf_op jit(solution)/shard_map/ppermute | solution.py:241
  100.6 13.5 %collective-permute-start.21 = (bf16[64,3584]{1,0:T(8,128)(2,1)S(1)}, bf16[64,3584]{1,0:T(8,128)(2,1)S(1)}, u32[]{:S(2)}, u32[]{:S(2)}) collective-permute-start(bf16[64,3584]{1,0:T(8,128)(2,1)S(1)} %get-tuple-element.156), channel_id=1, source_target_pairs={{0,2},{1,3},{4,0},{5,1},{8,4},{9,5},{12,8},{13,9},{14,12},{15,13},... | collective-permute-start | bytes 1376264 | tf_op jit(solution)/shard_map/ppermute | solution.py:241
  102.3 13.5 %collective-permute-start.22 = (bf16[64,3584]{1,0:T(8,128)(2,1)S(1)}, bf16[64,3584]{1,0:T(8,128)(2,1)S(1)}, u32[]{:S(2)}, u32[]{:S(2)}) collective-permute-start(bf16[64,3584]{1,0:T(8,128)(2,1)S(1)} %get-tuple-element.157), channel_id=1, source_target_pairs={{0,4},{1,5},{4,8},{5,9},{8,12},{9,13},{12,14},{13,15},{14,10},{15,... | collective-permute-start | bytes 1376264 | tf_op jit(solution)/shard_map/ppermute | solution.py:241
  102.7 22.8 %collective-permute-start.19 = (bf16[64,3584]{1,0:T(8,128)(2,1)S(1)}, bf16[64,3584]{1,0:T(8,128)(2,1)S(1)}, u32[]{:S(2)}, u32[]{:S(2)}) collective-permute-start(bf16[64,3584]{1,0:T(8,128)(2,1)S(1)} %get-tuple-element.150), channel_id=1, source_target_pairs={{0,4},{1,5},{4,8},{5,9},{8,12},{9,13},{12,14},{13,15},{14,10},{15,... | collective-permute-start | bytes 1376264 | tf_op jit(solution)/shard_map/ppermute | solution.py:241
  103.2 22.4 %collective-permute-start.20 = (bf16[64,3584]{1,0:T(8,128)(2,1)S(1)}, bf16[64,3584]{1,0:T(8,128)(2,1)S(1)}, u32[]{:S(2)}, u32[]{:S(2)}) collective-permute-start(bf16[64,3584]{1,0:T(8,128)(2,1)S(1)} %get-tuple-element.151), channel_id=1, source_target_pairs={{0,2},{1,3},{4,0},{5,1},{8,4},{9,5},{12,8},{13,9},{14,12},{15,13},... | collective-permute-start | bytes 1376264 | tf_op jit(solution)/shard_map/ppermute | solution.py:241
  115.8 17.4 %collective-permute-start.25 = (bf16[64,3584]{1,0:T(8,128)(2,1)S(1)}, bf16[64,3584]{1,0:T(8,128)(2,1)S(1)}, u32[]{:S(2)}, u32[]{:S(2)}) collective-permute-start(bf16[64,3584]{1,0:T(8,128)(2,1)S(1)} %get-tuple-element.162), channel_id=1, source_target_pairs={{0,2},{1,3},{4,0},{5,1},{8,4},{9,5},{12,8},{13,9},{14,12},{15,13},... | collective-permute-start | bytes 1376264 | tf_op jit(solution)/shard_map/ppermute | solution.py:241
  117.4 17.0 %collective-permute-start.26 = (bf16[64,3584]{1,0:T(8,128)(2,1)S(1)}, bf16[64,3584]{1,0:T(8,128)(2,1)S(1)}, u32[]{:S(2)}, u32[]{:S(2)}) collective-permute-start(bf16[64,3584]{1,0:T(8,128)(2,1)S(1)} %get-tuple-element.163), channel_id=1, source_target_pairs={{0,4},{1,5},{4,8},{5,9},{8,12},{9,13},{12,14},{13,15},{14,10},{15,... | collective-permute-start | bytes 1376264 | tf_op jit(solution)/shard_map/ppermute | solution.py:241
  125.6 16.6 %collective-permute-start.23 = (bf16[64,3584]{1,0:T(8,128)(2,1)S(1)}, bf16[64,3584]{1,0:T(8,128)(2,1)S(1)}, u32[]{:S(2)}, u32[]{:S(2)}) collective-permute-start(bf16[64,3584]{1,0:T(8,128)(2,1)S(1)} %get-tuple-element.158), channel_id=1, source_target_pairs={{0,4},{1,5},{4,8},{5,9},{8,12},{9,13},{12,14},{13,15},{14,10},{15,... | collective-permute-start | bytes 1376264 | tf_op jit(solution)/shard_map/ppermute | solution.py:241
  126.1 16.1 %collective-permute-start.24 = (bf16[64,3584]{1,0:T(8,128)(2,1)S(1)}, bf16[64,3584]{1,0:T(8,128)(2,1)S(1)}, u32[]{:S(2)}, u32[]{:S(2)}) collective-permute-start(bf16[64,3584]{1,0:T(8,128)(2,1)S(1)} %get-tuple-element.159), channel_id=1, source_target_pairs={{0,2},{1,3},{4,0},{5,1},{8,4},{9,5},{12,8},{13,9},{14,12},{15,13},... | collective-permute-start | bytes 1376264 | tf_op jit(solution)/shard_map/ppermute | solution.py:241
  142.4 12.6 %collective-permute-start.27 = (bf16[64,3584]{1,0:T(8,128)(2,1)S(1)}, bf16[64,3584]{1,0:T(8,128)(2,1)S(1)}, u32[]{:S(2)}, u32[]{:S(2)}) collective-permute-start(bf16[64,3584]{1,0:T(8,128)(2,1)S(1)} %get-tuple-element.164), channel_id=1, source_target_pairs={{0,4},{1,5},{4,8},{5,9},{8,12},{9,13},{12,14},{13,15},{14,10},{15,... | collective-permute-start | bytes 1376264 | tf_op jit(solution)/shard_map/ppermute | solution.py:241
  142.9 12.8 %collective-permute-start.28 = (bf16[64,3584]{1,0:T(8,128)(2,1)S(1)}, bf16[64,3584]{1,0:T(8,128)(2,1)S(1)}, u32[]{:S(2)}, u32[]{:S(2)}) collective-permute-start(bf16[64,3584]{1,0:T(8,128)(2,1)S(1)} %get-tuple-element.165), channel_id=1, source_target_pairs={{0,2},{1,3},{4,0},{5,1},{8,4},{9,5},{12,8},{13,9},{14,12},{15,13},... | collective-permute-start | bytes 1376264 | tf_op jit(solution)/shard_map/ppermute | solution.py:241
  155.8 8.5 %collective-permute-start.29 = (bf16[64,3584]{1,0:T(8,128)(2,1)S(1)}, bf16[64,3584]{1,0:T(8,128)(2,1)S(1)}, u32[]{:S(2)}, u32[]{:S(2)}) collective-permute-start(bf16[64,3584]{1,0:T(8,128)(2,1)S(1)} %get-tuple-element.166), channel_id=1, source_target_pairs={{0,4},{1,5},{4,8},{5,9},{8,12},{9,13},{12,14},{13,15},{14,10},{15,... | collective-permute-start | bytes 1376264 | tf_op jit(solution)/shard_map/ppermute | solution.py:241
  155.9 8.5 %collective-permute-start.30 = (bf16[64,3584]{1,0:T(8,128)(2,1)S(1)}, bf16[64,3584]{1,0:T(8,128)(2,1)S(1)}, u32[]{:S(2)}, u32[]{:S(2)}) collective-permute-start(bf16[64,3584]{1,0:T(8,128)(2,1)S(1)} %get-tuple-element.168), channel_id=1, source_target_pairs={{0,2},{1,3},{4,0},{5,1},{8,4},{9,5},{12,8},{13,9},{14,12},{15,13},... | collective-permute-start | bytes 1376264 | tf_op jit(solution)/shard_map/ppermute | solution.py:241

commit v7 on v6

v7 whole, which is shorter than its diff:
```python
import functools

import jax
import jax.numpy as jnp
from jax import lax
from jax.experimental import pallas as pl
from jax.experimental.pallas import tpu as pltpu
from jax.sharding import PartitionSpec as P

SPAN = 2
LANES = 128
DIGIT = 64
TILE = 256
WIDE = 512
MIB = 1 << 20


def expert_kernel(n, experts, dim, half, expert_ref, *refs):
    blocks, weights, outs = refs[:n], refs[n : n + 6], refs[n + 6 : -3]
    rows_ref, scale_ref, hidden_ref = refs[-3:]
    hid = weights[0].shape[1]
    expert = expert_ref[0]
    first = 0
    for block in blocks:
        count = block.shape[0]
        lane = lax.broadcasted_iota(jnp.int32, (count, LANES), 1)
        at = pl.ds(first, count)
        first += count
        rows_ref[at, :] = block[:, :dim]
        digits = block[:, dim:].astype(jnp.float32)
        codes = jnp.where(lane == expert, digits * float(DIGIT), 0.0)
        codes = codes + jnp.where(lane == expert + experts, digits, 0.0)
        code = jnp.sum(codes, 1, keepdims=True) * (1.0 / 4096.0)
        scale_ref[at, :] = jnp.broadcast_to(code, (count, LANES))

    for side in range(SPAN):
        gate_ref, up_ref, _ = weights[3 * side : 3 * side + 3]

        def hidden_tile(j, carry, side=side, gate_ref=gate_ref, up_ref=up_ref):
            at = pl.ds(pl.multiple_of(j * TILE, TILE), TILE)
            rows = rows_ref[...]
            gate = jnp.dot(rows, gate_ref[:, at], preferred_element_type=jnp.float32)
            upward = jnp.dot(rows, up_ref[:, at], preferred_element_type=jnp.float32)
            hidden = gate / (1.0 + jnp.exp(-gate)) * upward * scale_ref[:, :1]
            to = pl.ds(pl.multiple_of(side * hid + j * TILE, TILE), TILE)
            hidden_ref[:, to] = hidden.astype(jnp.bfloat16)
            return carry

        lax.fori_loop(0, hid // TILE, hidden_tile, 0)

    def out_tile(j, carry):
        at = pl.ds(pl.multiple_of(j * WIDE, WIDE), WIDE)
        part = jnp.dot(
            hidden_ref[:, :hid], weights[2][:, at], preferred_element_type=jnp.float32
        ) + jnp.dot(hidden_ref[:, hid:], weights[5][:, at], preferred_element_type=jnp.float32)
        part = part.astype(jnp.bfloat16)
        for i, out in enumerate(outs):
            out[:, at] = part[i * half : (i + 1) * half, :]
        return carry

    lax.fori_loop(0, dim // WIDE, out_tile, 0)


def small_cost():
    return pl.CostEstimate(flops=1024, bytes_accessed=1024, transcendentals=0)


def expert_parts(experts, half, expert, blocks, own, other):
    dim, hid = own[0].shape
    n, rows = len(blocks), sum(block.shape[0] for block in blocks)
    specs = [pl.BlockSpec(memory_space=pltpu.SMEM)]
    specs += [pl.BlockSpec(memory_space=pltpu.VMEM)] * (n + 6)
    return pl.pallas_call(
        functools.partial(expert_kernel, n, experts, dim, half),
        in_specs=specs,
        out_specs=[pl.BlockSpec(memory_space=pltpu.VMEM)] * (rows // half),
        out_shape=[jax.ShapeDtypeStruct((half, dim), jnp.bfloat16)] * (rows // half),
        scratch_shapes=[
            pltpu.VMEM((rows, dim), jnp.bfloat16),
            pltpu.VMEM((rows, LANES), jnp.float32),
            pltpu.VMEM((rows, SPAN * hid), jnp.bfloat16),
        ],
        compiler_params=pltpu.CompilerParams(vmem_limit_bytes=(13 if rows <= 256 else 16) * MIB),
        cost_estimate=small_cost(),
    )(expert, *blocks, *own, *other)


def add_kernel(n, pieces, first, *refs):
    outs = refs[-n * pieces :]
    size = outs[0].shape[0]
    for i, (left_ref, right_ref) in enumerate(zip(refs[:n], refs[n : 2 * n])):
        for p in range(pieces):
            left = left_ref[first + p * size : first + (p + 1) * size, :]
            outs[i * pieces + p][...] = left + right_ref[p * size : (p + 1) * size, :]


def add(lefts, rights, after=(), pieces=1, first=0):
    n = len(lefts)
    rows, dim = rights[0].shape
    shape = jax.ShapeDtypeStruct((rows // pieces, dim), rights[0].dtype)
    return pl.pallas_call(
        functools.partial(add_kernel, n, pieces, first),
        in_specs=[pl.BlockSpec(memory_space=pltpu.VMEM)] * (2 * n)
        + [pl.BlockSpec(memory_space=pl.ANY)] * len(after),
        out_specs=[pl.BlockSpec(memory_space=pltpu.VMEM)] * (n * pieces),
        out_shape=[shape] * (n * pieces),
        compiler_params=pltpu.CompilerParams(vmem_limit_bytes=6 * MIB),
        cost_estimate=small_cost(),
    )(*lefts, *rights, *after)


def split_kernel(n, *refs):
    for i, ref in enumerate(refs[:n]):
        half = ref.shape[0] // 2
        for h in range(2):
            refs[n + 2 * i + h][...] = ref[h * half : (h + 1) * half, :]


def split(arrays):
    n = len(arrays)
    rows, dim = arrays[0].shape
    return pl.pallas_call(
        functools.partial(split_kernel, n),
        in_specs=[pl.BlockSpec(memory_space=pltpu.VMEM)] * n,
        out_specs=[pl.BlockSpec(memory_space=pltpu.VMEM)] * (2 * n),
        out_shape=[jax.ShapeDtypeStruct((rows // 2, dim), arrays[0].dtype)] * (2 * n),
        compiler_params=pltpu.CompilerParams(vmem_limit_bytes=6 * MIB),
        cost_estimate=small_cost(),
    )(*arrays)


def close_kernel(halves, *refs):
    out_ref, taken = refs[-1], 0
    for h, pieces in enumerate(halves):
        base_ref, whole_ref = refs[taken : taken + 2]
        half = base_ref.shape[0]
        size = half // pieces
        for p in range(pieces):
            at = slice(p * size, (p + 1) * size)
            total = base_ref[at, :].astype(jnp.float32) + whole_ref[at, :].astype(jnp.float32)
            total = total + refs[taken + 2 + p][...].astype(jnp.float32)
            out_ref[h * half + p * size : h * half + (p + 1) * size, :] = total.astype(out_ref.dtype)
        taken += 2 + pieces


def close(halves):
    half, dim = halves[0][0].shape
    terms = [term for terms in halves for term in terms]
    return pl.pallas_call(
        functools.partial(close_kernel, [len(terms) - 2 for terms in halves]),
        in_specs=[pl.BlockSpec(memory_space=pltpu.VMEM)] * len(terms),
        out_shape=jax.ShapeDtypeStruct((2 * half, dim), terms[0].dtype),
        compiler_params=pltpu.CompilerParams(vmem_limit_bytes=8 * MIB),
        cost_estimate=small_cost(),
    )(*terms)


def rows_kernel(experts, top, tokens_ref, ids_ref, codes_ref, out_ref):
    tok, dim = tokens_ref.shape
    row = lax.broadcasted_iota(jnp.int32, (LANES, tok), 0)
    expert = jnp.where(row < experts, row, row - experts)
    code = jnp.zeros((LANES, tok), jnp.int32)
    for k in range(top):
        code = code + jnp.where(ids_ref[k : k + 1, :] == expert, codes_ref[k : k + 1, :], 0)
    digits = jnp.where(row < experts, code // DIGIT, code % DIGIT)
    out_ref[:, :dim] = tokens_ref[...]
    out_ref[:, dim:] = jnp.transpose(digits.astype(jnp.float32)).astype(out_ref.dtype)


def with_codes(experts, tokens, ids, codes):
    tok, dim = tokens.shape
    return pl.pallas_call(
        functools.partial(rows_kernel, experts, ids.shape[1]),
        out_shape=jax.ShapeDtypeStruct((tok, dim + LANES), tokens.dtype),
        compiler_params=pltpu.CompilerParams(vmem_limit_bytes=6 * MIB),
        cost_estimate=small_cost(),
    )(tokens, ids.T, codes.T)


def hand_on_kernel(expert_ref, *refs):
    refs[-1][0] = expert_ref[0]


def hand_on(expert, arrays):
    return pl.pallas_call(
        hand_on_kernel,
        in_specs=[pl.BlockSpec(memory_space=pltpu.SMEM)]
        + [pl.BlockSpec(memory_space=pltpu.VMEM)] * len(arrays),
        out_specs=pl.BlockSpec(memory_space=pltpu.SMEM),
        out_shape=jax.ShapeDtypeStruct(expert.shape, expert.dtype),
        compiler_params=pltpu.CompilerParams(vmem_limit_bytes=2 * MIB),
        cost_estimate=small_cost(),
    )(expert, *arrays)


def body(tokens, expert_ids, gate_codes, w_gate, w_up, w_down):
    nodes = lax.axis_size("node")
    ring = nodes // SPAN
    far = ring // 2
    tok, top = expert_ids.shape
    half = tok // 2

    def chip_at(pos):
        return 2 * pos if pos < far else 2 * (ring - 1 - pos) + 1

    def perm(step):
        return [
            (chip_at(pos) * SPAN + core, chip_at((pos + step) % ring) * SPAN + core)
            for pos in range(ring)
            for core in range(SPAN)
        ]

    forward, backward = perm(1), perm(-1)
    swap = [(node, node ^ 1) for node in range(nodes)]
    expert = (lax.axis_index("node") // SPAN).astype(jnp.int32).reshape(1)

    rows = with_codes(ring, tokens, expert_ids, gate_codes)

    near = [lax.ppermute(rows, "node", forward), lax.ppermute(rows, "node", backward)]
    own, _ = lax.optimization_barrier(((w_gate, w_up, w_down), rows))
    expert = hand_on(expert, own)
    other = [lax.ppermute(weight, "node", swap) for weight in own]

    near, expert = lax.optimization_barrier((near, expert))
    halves = split(near)
    ahead, behind = ([None, halves[0]], [None, halves[1]]), ([None, halves[2]], [None, halves[3]])
    parts = {}

    def work(names, blocks, after=()):
        held = [parts[name] for name in after]
        blocks, held = lax.optimization_barrier((blocks, held))
        parts.update(zip(after, held))
        parts.update(zip(names, expert_parts(ring, half, expert, blocks, own, other)))
        return names

    def send(s, h, after):
        held = [parts[name] for name in after]
        pair, held = lax.optimization_barrier(([ahead[h][s - 1], behind[h][s - 1]], held))
        parts.update(zip(after, held))
        ahead[h][s - 1], behind[h][s - 1] = pair
        if s < far or h == 0:
            ahead[h].append(lax.ppermute(ahead[h][s - 1], "node", forward))
        if s < far or h == 1:
            behind[h].append(lax.ppermute(behind[h][s - 1], "node", backward))

    for h in range(2):
        send(2, h, [])
    names = [(offset, h) for offset in (0, -1, 1) for h in range(2)]
    done = [work(names, [rows, *near])]
    for s in range(3, far + 1):
        for h in range(2):
            send(s, h, done.pop(0))
            done.append(work([(1 - s, h), (s - 1, h)], [ahead[h][s - 1], behind[h][s - 1]]))
    last = done.pop()
    firsts = [(1 - far, 0), (far - 1, 1)]
    held, ahead[0][far] = lax.optimization_barrier(
        ([parts[name] for name in firsts], ahead[0][far])
    )
    parts.update(zip(firsts, held))
    work([(far, 0), (far, 1)], [ahead[0][far], behind[1][far]], last)
    parts[-far, 1] = parts[far, 1]

    streams = [(h, sign) for h in range(2) for sign in (1, -1)]
    ways = {1: forward, -1: backward}
    early = [(h, sign) for h, sign in streams if (h == 0) != (sign == 1)]
    late = [stream for stream in streams if stream not in early]
    came = {}

    def pass_on(group, totals):
        for (h, sign), total in zip(group, totals):
            came[h, sign] = lax.ppermute(total, "node", ways[sign])

    def summed(group, at, after=(), **how):
        lefts = [parts[sign * at, h] for h, sign in group]
        return add(lefts, [came[stream] for stream in group], after, **how)

    pass_on(early, [parts[sign * (far - 1), h] for h, sign in early])
    late_totals = [parts[sign * far, h] for h, sign in late]
    held = [came[stream] for stream in early]
    late_totals, held = lax.optimization_barrier((late_totals, held))
    came.update(zip(early, held))
    for at in range(far - 1, 1, -1):
        pass_on(early, summed(early, at - 1))
        pass_on(late, late_totals)
        waited = [came[stream] for stream in early]
        late_totals = summed(late, at, waited, pieces=2 if at == 2 else 1)

    pieces = []
    for p in range(2):
        pass_on(late, late_totals[p::2])
        pass_on(late, summed(late, 1, first=p * (half // 2)))
        pieces.append([came[stream] for stream in late])
    shorter = dict(early)
    return close(
        [
            [parts[0, h], came[h, shorter[h]], *(piece[h] for piece in pieces)]
            for h in range(2)
        ]
    )


def solution(mesh):
    in_specs = (
        P(("groups", "node"), None),
        P(("groups", "node"), None),
        P(("groups", "node"), None),
        P(None, "node"),
        P(None, "node"),
        P("node", None),
    )
    out_specs = P(("groups", "node"), None)
    return jax.shard_map(body, mesh=mesh, in_specs=in_specs, out_specs=out_specs, check_vma=False)
```

time: 166 us -> 170 us (1.024)
  Pallas kernels: 44.6 us -> 67.5 us
  waiting for transfers between devices: 81.1 us -> 60.5 us
    pallas_call x4 -> x6, Pallas kernels: 42.3 us -> 64.9 us  [expert_parts(): pl.pallas_call(functools.partial(expert_kernel, n, experts, dim, half), i...]
    ppermute x7 -> x5, waiting for transfers between devices: 19.8 us -> 0.01 us  [send(): ahead[h].append(lax.ppermute(ahead[h][s - 1], 'node', forward))]
    ppermute x3 -> x5, waiting for transfers between devices: 0.01 us -> 16.4 us  [the longest x1 15 us: body(): lax.ppermute(rows, 'node', backward)]
    ppermute x7 -> x5, waiting for transfers between devices: 10.3 us -> 0.01 us  [send(): behind[h].append(lax.ppermute(behind[h][s - 1], 'node', backward))]
    ppermute x14 -> x18, waiting for transfers between devices: 51 us -> 44.1 us  [pass_on(): came[h, sign] = lax.ppermute(total, 'node', ways[sign])]
    ppermute x14 -> x18, starting transfers between devices: 14.5 us -> 18.6 us  [pass_on(): came[h, sign] = lax.ppermute(total, 'node', ways[sign])]
    ppermute x7 -> x5, starting transfers between devices: 12.2 us -> 8.48 us  [send(): behind[h].append(lax.ppermute(behind[h][s - 1], 'node', backward))]
    ppermute x3 -> x5, starting transfers between devices: 0.51 us -> 3.68 us  [the longest x1 2.6 us: body(): lax.ppermute(rows, 'node', backward)]
  transfers between devices with their start and end apart: 31 -> 33, of which waited for: 16 -> 16; matrix products, arithmetic and copies ran while one was open for 0% -> 0% of each run, Pallas kernels for 26% -> 39%
where the time goes in v7:
time: 170 us
  Pallas kernels  67.5 us (40%)
  waiting for transfers between devices  60.5 us (36%)
  starting transfers between devices  32.7 us (19%)
  local copies, waits for them, and re-layouts  8.67 us (5%)
    pallas_call x6, Pallas kernels, expert_parts(): pl.pallas_call(functools.partial(expert_kernel, n, experts, dim, half), i...  64.9 us
    ppermute x18, waiting for transfers between devices, pass_on(): came[h, sign] = lax.ppermute(total, 'node', ways[sign])  44.1 us
    ppermute x18, starting transfers between devices, pass_on(): came[h, sign] = lax.ppermute(total, 'node', ways[sign])  18.6 us
    ppermute x1, waiting for transfers between devices, body(): lax.ppermute(rows, 'node', backward)  15 us
    unnamed x18, local copies, waits for them, and re-layouts  8.67 us
    ppermute x5, starting transfers between devices, send(): behind[h].append(lax.ppermute(behind[h][s - 1], 'node', backward))  8.48 us
  transfers between devices with their start and end apart: 33, of which 16 were waited for; matrix products, arithmetic and copies ran while one was open for 0% of the time, Pallas kernels for 39%

profile of v7, /device:TPU:0, one launch (start us, length us, event | category | flops | bytes accessed | tf_op | source)
XLA Modules:
  0.0 169.6 jit_solution(11821356314010125647)
XLA Ops:
  0.0 1.2 copy-done.6
  1.2 0.7 copy-done.7
  1.9 0.7 copy-done.8
  2.7 0.5 collective-permute-start.4
  3.7 2.6 %collective-permute-start.1 = (bf16[128,3712]{1,0:T(8,128)(2,1)S(1)}, bf16[128,3712]{1,0:T(8,128)(2,1)S(1)}, u32[]{:S(2)}, u32[]{:S(2)}) collective-permute-start(bf16[128,3712]{1,0:T(8,128)(2,1)S(1)} %shard_map.64.refs_0_), channel_id=1, source_target_pairs={{0,2},{1,3},{4,0},{5,1},{8,4},{9,5},{12,8},{13,9},{14,12},{15,13},... | collective-permute-start | bytes 2850824 | tf_op jit(solution)/shard_map/ppermute | solution.py:219
  6.4 2.0 %copy-done = bf16[3584,512]{1,0:T(8,128)(2,1)S(1)} copy-done((bf16[3584,512]{1,0:T(8,128)(2,1)S(1)}, bf16[3584,512]{1,0:T(8,128)(2,1)}, u32[]{:S(2)}) %copy-start) | copy-done | bytes 3670040
  8.4 2.0 %copy-done.2 = bf16[3584,512]{1,0:T(8,128)(2,1)S(1)} copy-done((bf16[3584,512]{1,0:T(8,128)(2,1)S(1)}, bf16[3584,512]{1,0:T(8,128)(2,1)}, u32[]{:S(2)}) %copy-start.2) | copy-done | bytes 3670040
  10.5 2.0 %copy-done.4 = bf16[512,3584]{1,0:T(8,128)(2,1)S(1)} copy-done((bf16[512,3584]{1,0:T(8,128)(2,1)S(1)}, bf16[512,3584]{1,0:T(8,128)(2,1)}, u32[]{:S(2)}) %copy-start.4) | copy-done | bytes 3670040
  12.5 0.5 shard_map.65.expert_ref
  13.0 15.0 %collective-permute-done.1.refs_1_.refs_2_ = bf16[128,3712]{1,0:T(8,128)(2,1)S(1)} collective-permute-done((bf16[128,3712]{1,0:T(8,128)(2,1)S(1)}, bf16[128,3712]{1,0:T(8,128)(2,1)S(1)}, u32[]{:S(2)}, u32[]{:S(2)}) %collective-permute-start.1) | collective-permute-done | bytes 950304 | tf_op jit(solution)/shard_map/ppermute | solution.py:219
  28.0 1.4 collective-permute-done.refs_0_.refs_1_
  30.0 1.7 collective-permute-start.3
  32.0 1.7 collective-permute-start.8
  33.7 15.6 %shard_map.67 = (bf16[64,3584]{1,0:T(8,128)(2,1)S(1)}, bf16[64,3584]{1,0:T(8,128)(2,1)S(1)}, bf16[64,3584]{1,0:T(8,128)(2,1)S(1)}, bf16[64,3584]{1,0:T(8,128)(2,...) custom-call(s32[1]{0:T(128)} %shard_map.65.expert_ref, bf16[128,3712]{1,0:T(8,128)(2,1)S(1)} %shard_map.64.refs_0_, ...), custom_call_target="tpu_custom_call" | custom-call | flops 1024 | bytes 1024 | tf_op jit(solution)/shard_map/pallas_call | solution.py:73
  49.7 1.7 collective-permute-start.10
  51.4 9.9 %shard_map.68 = (bf16[64,3584]{1,0:T(8,128)(2,1)S(1)}, bf16[64,3584]{1,0:T(8,128)(2,1)S(1)}) custom-call(s32[1]{0:T(128)} %shard_map.65.expert_ref, bf16[64,3712]{1,0:T(8,128)(2,1)S(1)} %collective-permute-done.2.refs_0_, bf16[64,3712]{1,0:T(8,128)(2,1)S(1)} %collective-permute-done.3.refs_1_, bf16[3584,512]{1,0:T(8,128)(2,1)S(1)} %copy-done.1, ...), custom_call_target="tpu_custom_call" | custom-call | flops 1024 | bytes 1024 | tf_op jit(solution)/shard_map/pallas_call | solution.py:73
  61.7 1.7 collective-permute-start.12
  63.3 9.9 %shard_map.69 = (bf16[64,3584]{1,0:T(8,128)(2,1)S(1)}, bf16[64,3584]{1,0:T(8,128)(2,1)S(1)}) custom-call(s32[1]{0:T(128)} %shard_map.65.expert_ref, bf16[64,3712]{1,0:T(8,128)(2,1)S(1)} %collective-permute-done.7.refs_0_, bf16[64,3712]{1,0:T(8,128)(2,1)S(1)} %collective-permute-done.8.refs_1_, bf16[3584,512]{1,0:T(8,128)(2,1)S(1)} %copy-done.1, ...), custom_call_target="tpu_custom_call" | custom-call | flops 1024 | bytes 1024 | tf_op jit(solution)/shard_map/pallas_call | solution.py:73
  73.6 9.9 %shard_map.70 = (bf16[64,3584]{1,0:T(8,128)(2,1)S(1)}, bf16[64,3584]{1,0:T(8,128)(2,1)S(1)}) custom-call(s32[1]{0:T(128)} %shard_map.65.expert_ref, bf16[64,3712]{1,0:T(8,128)(2,1)S(1)} %collective-permute-done.9.refs_0_, bf16[64,3712]{1,0:T(8,128)(2,1)S(1)} %collective-permute-done.10.refs_1_, bf16[3584,512]{1,0:T(8,128)(2,1)S(1)} %copy-done.1, ...), custom_call_target="tpu_custom_call" | custom-call | flops 1024 | bytes 1024 | tf_op jit(solution)/shard_map/pallas_call | solution.py:73
  83.5 1.7 %collective-permute-start.14 = (bf16[64,3712]{1,0:T(8,128)(2,1)S(1)}, bf16[64,3712]{1,0:T(8,128)(2,1)S(1)}, u32[]{:S(2)}, u32[]{:S(2)}) collective-permute-start(bf16[64,3712]{1,0:T(8,128)(2,1)S(1)} %collective-permute-done.12.refs_1_), channel_id=1, source_target_pairs={{0,2},{1,3},{4,0},{5,1},{8,4},{9,5},{12,8},{13,9},{14,12},{15,13},... | collective-permute-start | bytes 1425416 | tf_op jit(solution)/shard_map/ppermute | solution.py:244
  85.3 9.9 %shard_map.71 = (bf16[64,3584]{1,0:T(8,128)(2,1)S(1)}, bf16[64,3584]{1,0:T(8,128)(2,1)S(1)}) custom-call(s32[1]{0:T(128)} %shard_map.65.expert_ref, bf16[64,3712]{1,0:T(8,128)(2,1)S(1)} %collective-permute-done.11.refs_0_, bf16[64,3712]{1,0:T(8,128)(2,1)S(1)} %collective-permute-done.12.refs_1_, bf16[3584,512]{1,0:T(8,128)(2,1)S(1)} %copy-done.1, ...), custom_call_target="tpu_custom_call" | custom-call | flops 1024 | bytes 1024 | tf_op jit(solution)/shard_map/pallas_call | solution.py:73
  95.6 1.7 collective-permute-start.15
  97.3 9.9 %shard_map.72 = (bf16[64,3584]{1,0:T(8,128)(2,1)S(1)}, bf16[64,3584]{1,0:T(8,128)(2,1)S(1)}) custom-call(s32[1]{0:T(128)} %shard_map.65.expert_ref, bf16[64,3712]{1,0:T(8,128)(2,1)S(1)} %collective-permute-done.13.refs_0_, bf16[64,3712]{1,0:T(8,128)(2,1)S(1)} %collective-permute-done.14.refs_1_, bf16[3584,512]{1,0:T(8,128)(2,1)S(1)} %copy-done.1, ...), custom_call_target="tpu_custom_call" | custom-call | flops 1024 | bytes 1024 | tf_op jit(solution)/shard_map/pallas_call | solution.py:73
  107.3 1.6 collective-permute-start.17
  108.9 0.4 collective-permute-start.18
  109.7 1.7 collective-permute-start.21
  111.4 9.4 %collective-permute-done.17.refs_2_.refs_4_ = bf16[64,3584]{1,0:T(8,128)(2,1)S(1)} collective-permute-done((bf16[64,3584]{1,0:T(8,128)(2,1)S(1)}, bf16[64,3584]{1,0:T(8,128)(2,1)S(1)}, u32[]{:S(2)}, u32[]{:S(2)}) %collective-permute-start.17) | collective-permute-done | bytes 458784 | tf_op jit(solution)/shard_map/ppermute | solution.py:271
  120.8 1.6 collective-permute-done.18.refs_3_.refs_5_
  122.5 1.6 collective-permute-start.19
  124.5 7.7 %collective-permute-done.20.refs_2_ = bf16[64,3584]{1,0:T(8,128)(2,1)S(1)} collective-permute-done((bf16[64,3584]{1,0:T(8,128)(2,1)S(1)}, bf16[64,3584]{1,0:T(8,128)(2,1)S(1)}, u32[]{:S(2)}, u32[]{:S(2)}) %collective-permute-start.20) | collective-permute-done | bytes 458784 | tf_op jit(solution)/shard_map/ppermute | solution.py:271
  132.3 0.5 collective-permute-start.22
  132.8 1.6 collective-permute-start.23
  134.4 5.9 %collective-permute-done.19.refs_4_.refs_1_ = bf16[64,3584]{1,0:T(8,128)(2,1)S(1)} collective-permute-done((bf16[64,3584]{1,0:T(8,128)(2,1)S(1)}, bf16[64,3584]{1,0:T(8,128)(2,1)S(1)}, u32[]{:S(2)}, u32[]{:S(2)}) %collective-permute-start.19) | collective-permute-done | bytes 458784 | tf_op jit(solution)/shard_map/ppermute | solution.py:271
  140.3 1.3 collective-permute-done.24.refs_5_
  141.6 7.3 %collective-permute-done.22.refs_2_ = bf16[64,3584]{1,0:T(8,128)(2,1)S(1)} collective-permute-done((bf16[64,3584]{1,0:T(8,128)(2,1)S(1)}, bf16[64,3584]{1,0:T(8,128)(2,1)S(1)}, u32[]{:S(2)}, u32[]{:S(2)}) %collective-permute-start.22) | collective-permute-done | bytes 458784 | tf_op jit(solution)/shard_map/ppermute | solution.py:271
  149.0 0.5 collective-permute-start.25
  149.5 1.6 collective-permute-start.26
  151.1 0.5 collective-permute-start.28
  151.6 1.6 collective-permute-start.29
  153.1 4.4 %collective-permute-done.25.refs_2_ = bf16[32,3584]{1,0:T(8,128)(2,1)S(1)} collective-permute-done((bf16[32,3584]{1,0:T(8,128)(2,1)S(1)}, bf16[32,3584]{1,0:T(8,128)(2,1)S(1)}, u32[]{:S(2)}, u32[]{:S(2)}) %collective-permute-start.25) | collective-permute-done | bytes 229408 | tf_op jit(solution)/shard_map/ppermute | solution.py:271
  157.5 0.5 collective-permute-done.26.refs_3_
  158.5 1.7 %collective-permute-start.31 = (bf16[32,3584]{1,0:T(8,128)(2,1)S(1)}, bf16[32,3584]{1,0:T(8,128)(2,1)S(1)}, u32[]{:S(2)}, u32[]{:S(2)}) collective-permute-start(bf16[32,3584]{1,0:T(8,128)(2,1)S(1)} %get-tuple-element.175), channel_id=1, source_target_pairs={{0,2},{1,3},{4,0},{5,1},{8,4},{9,5},{12,8},{13,9},{14,12},{15,13},... | collective-permute-start | bytes 688136 | tf_op jit(solution)/shard_map/ppermute | solution.py:271
  160.2 1.4 collective-permute-done.28.refs_2_
  161.8 0.5 collective-permute-start.30
  162.3 1.6 collective-permute-start.32
  164.5 3.4 %collective-permute-done.30.refs_3_ = bf16[32,3584]{1,0:T(8,128)(2,1)S(1)} collective-permute-done((bf16[32,3584]{1,0:T(8,128)(2,1)S(1)}, bf16[32,3584]{1,0:T(8,128)(2,1)S(1)}, u32[]{:S(2)}, u32[]{:S(2)}) %collective-permute-start.30) | collective-permute-done | bytes 229408 | tf_op jit(solution)/shard_map/ppermute | solution.py:271
  167.9 0.5 collective-permute-done.32.refs_7_
  168.3 1.3 shard_map.79
  (52 shorter events, 5.7 us)
Async XLA Ops:
  0.0 1.2 copy-start.6
  1.2 0.7 copy-start.7
  1.9 0.7 copy-start.8
  2.7 29.0 %collective-permute-start.4 = (bf16[3584,512]{1,0:T(8,128)(2,1)}, bf16[3584,512]{1,0:T(8,128)(2,1)}, u32[]{:S(2)}, u32[]{:S(2)}) collective-permute-start(bf16[3584,512]{1,0:T(8,128)(2,1)} %refs_2_.5), channel_id=1, source_target_pairs={{0,1},{1,0},{2,3},{3,2},{4,5},{5,4},{6,7},{7,6},{8,9},{9,8},{10,11... | collective-permute-start | bytes 11010056 | tf_op jit(solution)/shard_map/ppermute | solution.py:222
  3.2 28.8 %collective-permute-start.5 = (bf16[3584,512]{1,0:T(8,128)(2,1)}, bf16[3584,512]{1,0:T(8,128)(2,1)}, u32[]{:S(2)}, u32[]{:S(2)}) collective-permute-start(bf16[3584,512]{1,0:T(8,128)(2,1)} %refs_3_.5), channel_id=1, source_target_pairs={{0,1},{1,0},{2,3},{3,2},{4,5},{5,4},{6,7},{7,6},{8,9},{9,8},{10,11... | collective-permute-start | bytes 11010056 | tf_op jit(solution)/shard_map/ppermute | solution.py:222
  3.3 30.4 %collective-permute-start.6 = (bf16[512,3584]{1,0:T(8,128)(2,1)}, bf16[512,3584]{1,0:T(8,128)(2,1)}, u32[]{:S(2)}, u32[]{:S(2)}) collective-permute-start(bf16[512,3584]{1,0:T(8,128)(2,1)} %refs_4_.5), channel_id=1, source_target_pairs={{0,1},{1,0},{2,3},{3,2},{4,5},{5,4},{6,7},{7,6},{8,9},{9,8},{10,11... | collective-permute-start | bytes 11010056 | tf_op jit(solution)/shard_map/ppermute | solution.py:222
  3.7 24.3 %collective-permute-start.1 = (bf16[128,3712]{1,0:T(8,128)(2,1)S(1)}, bf16[128,3712]{1,0:T(8,128)(2,1)S(1)}, u32[]{:S(2)}, u32[]{:S(2)}) collective-permute-start(bf16[128,3712]{1,0:T(8,128)(2,1)S(1)} %shard_map.64.refs_0_), channel_id=1, source_target_pairs={{0,2},{1,3},{4,0},{5,1},{8,4},{9,5},{12,8},{13,9},{14,12},{15,13},... | collective-permute-start | bytes 2850824 | tf_op jit(solution)/shard_map/ppermute | solution.py:219
  6.3 23.1 %collective-permute-start = (bf16[128,3712]{1,0:T(8,128)(2,1)S(1)}, bf16[128,3712]{1,0:T(8,128)(2,1)S(1)}, u32[]{:S(2)}, u32[]{:S(2)}) collective-permute-start(bf16[128,3712]{1,0:T(8,128)(2,1)S(1)} %shard_map.64.refs_0_), channel_id=1, source_target_pairs={{0,4},{1,5},{4,8},{5,9},{8,12},{9,13},{12,14},{13,15},{14,10},{15,... | collective-permute-start | bytes 2850824 | tf_op jit(solution)/shard_map/ppermute | solution.py:219
  6.4 2.0 %copy-start = (bf16[3584,512]{1,0:T(8,128)(2,1)S(1)}, bf16[3584,512]{1,0:T(8,128)(2,1)}, u32[]{:S(2)}) copy-start(bf16[3584,512]{1,0:T(8,128)(2,1)} %refs_2_.5) | copy-start | bytes 11010052
  8.4 2.0 %copy-start.2 = (bf16[3584,512]{1,0:T(8,128)(2,1)S(1)}, bf16[3584,512]{1,0:T(8,128)(2,1)}, u32[]{:S(2)}) copy-start(bf16[3584,512]{1,0:T(8,128)(2,1)} %refs_3_.5) | copy-start | bytes 11010052
  10.4 2.0 %copy-start.4 = (bf16[512,3584]{1,0:T(8,128)(2,1)S(1)}, bf16[512,3584]{1,0:T(8,128)(2,1)}, u32[]{:S(2)}) copy-start(bf16[512,3584]{1,0:T(8,128)(2,1)} %refs_4_.5) | copy-start | bytes 11010052
  12.5 21.2 %copy-start.1 = (bf16[3584,512]{1,0:T(8,128)(2,1)S(1)}, bf16[3584,512]{1,0:T(8,128)(2,1)}, u32[]{:S(2)}) copy-start(bf16[3584,512]{1,0:T(8,128)(2,1)} %refs_2_.5) | copy-start | bytes 11010052
  12.5 21.2 %copy-start.3 = (bf16[3584,512]{1,0:T(8,128)(2,1)S(1)}, bf16[3584,512]{1,0:T(8,128)(2,1)}, u32[]{:S(2)}) copy-start(bf16[3584,512]{1,0:T(8,128)(2,1)} %refs_3_.5) | copy-start | bytes 11010052
  12.5 21.2 %copy-start.5 = (bf16[512,3584]{1,0:T(8,128)(2,1)S(1)}, bf16[512,3584]{1,0:T(8,128)(2,1)}, u32[]{:S(2)}) copy-start(bf16[512,3584]{1,0:T(8,128)(2,1)} %refs_4_.5) | copy-start | bytes 11010052
  29.6 19.7 %collective-permute-start.2 = (bf16[64,3712]{1,0:T(8,128)(2,1)S(1)}, bf16[64,3712]{1,0:T(8,128)(2,1)S(1)}, u32[]{:S(2)}, u32[]{:S(2)}) collective-permute-start(bf16[64,3712]{1,0:T(8,128)(2,1)S(1)} %get-tuple-element.98), channel_id=1, source_target_pairs={{0,4},{1,5},{4,8},{5,9},{8,12},{9,13},{12,14},{13,15},{14,10},{15,... | collective-permute-start | bytes 1425416 | tf_op jit(solution)/shard_map/ppermute | solution.py:242
  30.0 19.3 %collective-permute-start.3 = (bf16[64,3712]{1,0:T(8,128)(2,1)S(1)}, bf16[64,3712]{1,0:T(8,128)(2,1)S(1)}, u32[]{:S(2)}, u32[]{:S(2)}) collective-permute-start(bf16[64,3712]{1,0:T(8,128)(2,1)S(1)} %get-tuple-element.99), channel_id=1, source_target_pairs={{0,2},{1,3},{4,0},{5,1},{8,4},{9,5},{12,8},{13,9},{14,12},{15,13},... | collective-permute-start | bytes 1425416 | tf_op jit(solution)/shard_map/ppermute | solution.py:244
  31.6 29.6 %collective-permute-start.7 = (bf16[64,3712]{1,0:T(8,128)(2,1)S(1)}, bf16[64,3712]{1,0:T(8,128)(2,1)S(1)}, u32[]{:S(2)}, u32[]{:S(2)}) collective-permute-start(bf16[64,3712]{1,0:T(8,128)(2,1)S(1)} %get-tuple-element.115), channel_id=1, source_target_pairs={{0,4},{1,5},{4,8},{5,9},{8,12},{9,13},{12,14},{13,15},{14,10},{15,... | collective-permute-start | bytes 1425416 | tf_op jit(solution)/shard_map/ppermute | solution.py:242
  32.0 29.3 %collective-permute-start.8 = (bf16[64,3712]{1,0:T(8,128)(2,1)S(1)}, bf16[64,3712]{1,0:T(8,128)(2,1)S(1)}, u32[]{:S(2)}, u32[]{:S(2)}) collective-permute-start(bf16[64,3712]{1,0:T(8,128)(2,1)S(1)} %get-tuple-element.116), channel_id=1, source_target_pairs={{0,2},{1,3},{4,0},{5,1},{8,4},{9,5},{12,8},{13,9},{14,12},{15,13},... | collective-permute-start | bytes 1425416 | tf_op jit(solution)/shard_map/ppermute | solution.py:244
  49.3 23.9 %collective-permute-start.9 = (bf16[64,3712]{1,0:T(8,128)(2,1)S(1)}, bf16[64,3712]{1,0:T(8,128)(2,1)S(1)}, u32[]{:S(2)}, u32[]{:S(2)}) collective-permute-start(bf16[64,3712]{1,0:T(8,128)(2,1)S(1)} %collective-permute-done.2.refs_0_), channel_id=1, source_target_pairs={{0,4},{1,5},{4,8},{5,9},{8,12},{9,13},{12,14},{13,15},{14,10},{15,... | collective-permute-start | bytes 1425416 | tf_op jit(solution)/shard_map/ppermute | solution.py:242
  49.7 23.6 %collective-permute-start.10 = (bf16[64,3712]{1,0:T(8,128)(2,1)S(1)}, bf16[64,3712]{1,0:T(8,128)(2,1)S(1)}, u32[]{:S(2)}, u32[]{:S(2)}) collective-permute-start(bf16[64,3712]{1,0:T(8,128)(2,1)S(1)} %collective-permute-done.3.refs_1_), channel_id=1, source_target_pairs={{0,2},{1,3},{4,0},{5,1},{8,4},{9,5},{12,8},{13,9},{14,12},{15,13},... | collective-permute-start | bytes 1425416 | tf_op jit(solution)/shard_map/ppermute | solution.py:244
  61.3 22.3 %collective-permute-start.11 = (bf16[64,3712]{1,0:T(8,128)(2,1)S(1)}, bf16[64,3712]{1,0:T(8,128)(2,1)S(1)}, u32[]{:S(2)}, u32[]{:S(2)}) collective-permute-start(bf16[64,3712]{1,0:T(8,128)(2,1)S(1)} %collective-permute-done.7.refs_0_), channel_id=1, source_target_pairs={{0,4},{1,5},{4,8},{5,9},{8,12},{9,13},{12,14},{13,15},{14,10},{15,... | collective-permute-start | bytes 1425416 | tf_op jit(solution)/shard_map/ppermute | solution.py:242
  61.7 21.9 %collective-permute-start.12 = (bf16[64,3712]{1,0:T(8,128)(2,1)S(1)}, bf16[64,3712]{1,0:T(8,128)(2,1)S(1)}, u32[]{:S(2)}, u32[]{:S(2)}) collective-permute-start(bf16[64,3712]{1,0:T(8,128)(2,1)S(1)} %collective-permute-done.8.refs_1_), channel_id=1, source_target_pairs={{0,2},{1,3},{4,0},{5,1},{8,4},{9,5},{12,8},{13,9},{14,12},{15,13},... | collective-permute-start | bytes 1425416 | tf_op jit(solution)/shard_map/ppermute | solution.py:244
  73.2 21.9 %collective-permute-start.13 = (bf16[64,3712]{1,0:T(8,128)(2,1)S(1)}, bf16[64,3712]{1,0:T(8,128)(2,1)S(1)}, u32[]{:S(2)}, u32[]{:S(2)}) collective-permute-start(bf16[64,3712]{1,0:T(8,128)(2,1)S(1)} %collective-permute-done.9.refs_0_), channel_id=1, source_target_pairs={{0,4},{1,5},{4,8},{5,9},{8,12},{9,13},{12,14},{13,15},{14,10},{15,... | collective-permute-start | bytes 1425416 | tf_op jit(solution)/shard_map/ppermute | solution.py:242
  83.5 11.6 %collective-permute-start.14 = (bf16[64,3712]{1,0:T(8,128)(2,1)S(1)}, bf16[64,3712]{1,0:T(8,128)(2,1)S(1)}, u32[]{:S(2)}, u32[]{:S(2)}) collective-permute-start(bf16[64,3712]{1,0:T(8,128)(2,1)S(1)} %collective-permute-done.12.refs_1_), channel_id=1, source_target_pairs={{0,2},{1,3},{4,0},{5,1},{8,4},{9,5},{12,8},{13,9},{14,12},{15,13},... | collective-permute-start | bytes 1425416 | tf_op jit(solution)/shard_map/ppermute | solution.py:244
  95.2 12.0 %collective-permute-start.16 = (bf16[64,3584]{1,0:T(8,128)(2,1)S(1)}, bf16[64,3584]{1,0:T(8,128)(2,1)S(1)}, u32[]{:S(2)}, u32[]{:S(2)}) collective-permute-start(bf16[64,3584]{1,0:T(8,128)(2,1)S(1)} %get-tuple-element.151), channel_id=1, source_target_pairs={{0,4},{1,5},{4,8},{5,9},{8,12},{9,13},{12,14},{13,15},{14,10},{15,... | collective-permute-start | bytes 1376264 | tf_op jit(solution)/shard_map/ppermute | solution.py:271
  95.6 11.6 %collective-permute-start.15 = (bf16[64,3584]{1,0:T(8,128)(2,1)S(1)}, bf16[64,3584]{1,0:T(8,128)(2,1)S(1)}, u32[]{:S(2)}, u32[]{:S(2)}) collective-permute-start(bf16[64,3584]{1,0:T(8,128)(2,1)S(1)} %get-tuple-element.150), channel_id=1, source_target_pairs={{0,2},{1,3},{4,0},{5,1},{8,4},{9,5},{12,8},{13,9},{14,12},{15,13},... | collective-permute-start | bytes 1376264 | tf_op jit(solution)/shard_map/ppermute | solution.py:271
  107.3 13.5 %collective-permute-start.17 = (bf16[64,3584]{1,0:T(8,128)(2,1)S(1)}, bf16[64,3584]{1,0:T(8,128)(2,1)S(1)}, u32[]{:S(2)}, u32[]{:S(2)}) collective-permute-start(bf16[64,3584]{1,0:T(8,128)(2,1)S(1)} %get-tuple-element.154), channel_id=1, source_target_pairs={{0,2},{1,3},{4,0},{5,1},{8,4},{9,5},{12,8},{13,9},{14,12},{15,13},... | collective-permute-start | bytes 1376264 | tf_op jit(solution)/shard_map/ppermute | solution.py:271
  108.9 13.5 %collective-permute-start.18 = (bf16[64,3584]{1,0:T(8,128)(2,1)S(1)}, bf16[64,3584]{1,0:T(8,128)(2,1)S(1)}, u32[]{:S(2)}, u32[]{:S(2)}) collective-permute-start(bf16[64,3584]{1,0:T(8,128)(2,1)S(1)} %get-tuple-element.155), channel_id=1, source_target_pairs={{0,4},{1,5},{4,8},{5,9},{8,12},{9,13},{12,14},{13,15},{14,10},{15,... | collective-permute-start | bytes 1376264 | tf_op jit(solution)/shard_map/ppermute | solution.py:271
  109.4 22.8 %collective-permute-start.20 = (bf16[64,3584]{1,0:T(8,128)(2,1)S(1)}, bf16[64,3584]{1,0:T(8,128)(2,1)S(1)}, u32[]{:S(2)}, u32[]{:S(2)}) collective-permute-start(bf16[64,3584]{1,0:T(8,128)(2,1)S(1)} %get-tuple-element.163), channel_id=1, source_target_pairs={{0,4},{1,5},{4,8},{5,9},{8,12},{9,13},{12,14},{13,15},{14,10},{15,... | collective-permute-start | bytes 1376264 | tf_op jit(solution)/shard_map/ppermute | solution.py:271
  109.7 22.5 %collective-permute-start.21 = (bf16[64,3584]{1,0:T(8,128)(2,1)S(1)}, bf16[64,3584]{1,0:T(8,128)(2,1)S(1)}, u32[]{:S(2)}, u32[]{:S(2)}) collective-permute-start(bf16[64,3584]{1,0:T(8,128)(2,1)S(1)} %get-tuple-element.164), channel_id=1, source_target_pairs={{0,2},{1,3},{4,0},{5,1},{8,4},{9,5},{12,8},{13,9},{14,12},{15,13},... | collective-permute-start | bytes 1376264 | tf_op jit(solution)/shard_map/ppermute | solution.py:271
  122.5 17.9 %collective-permute-start.19 = (bf16[64,3584]{1,0:T(8,128)(2,1)S(1)}, bf16[64,3584]{1,0:T(8,128)(2,1)S(1)}, u32[]{:S(2)}, u32[]{:S(2)}) collective-permute-start(bf16[64,3584]{1,0:T(8,128)(2,1)S(1)} %get-tuple-element.156), channel_id=1, source_target_pairs={{0,2},{1,3},{4,0},{5,1},{8,4},{9,5},{12,8},{13,9},{14,12},{15,13},... | collective-permute-start | bytes 1376264 | tf_op jit(solution)/shard_map/ppermute | solution.py:271
  124.1 17.5 %collective-permute-start.24 = (bf16[64,3584]{1,0:T(8,128)(2,1)S(1)}, bf16[64,3584]{1,0:T(8,128)(2,1)S(1)}, u32[]{:S(2)}, u32[]{:S(2)}) collective-permute-start(bf16[64,3584]{1,0:T(8,128)(2,1)S(1)} %get-tuple-element.167), channel_id=1, source_target_pairs={{0,4},{1,5},{4,8},{5,9},{8,12},{9,13},{12,14},{13,15},{14,10},{15,... | collective-permute-start | bytes 1376264 | tf_op jit(solution)/shard_map/ppermute | solution.py:271
  132.3 16.6 %collective-permute-start.22 = (bf16[64,3584]{1,0:T(8,128)(2,1)S(1)}, bf16[64,3584]{1,0:T(8,128)(2,1)S(1)}, u32[]{:S(2)}, u32[]{:S(2)}) collective-permute-start(bf16[64,3584]{1,0:T(8,128)(2,1)S(1)} %get-tuple-element.165), channel_id=1, source_target_pairs={{0,4},{1,5},{4,8},{5,9},{8,12},{9,13},{12,14},{13,15},{14,10},{15,... | collective-permute-start | bytes 1376264 | tf_op jit(solution)/shard_map/ppermute | solution.py:271
  132.8 16.1 %collective-permute-start.23 = (bf16[64,3584]{1,0:T(8,128)(2,1)S(1)}, bf16[64,3584]{1,0:T(8,128)(2,1)S(1)}, u32[]{:S(2)}, u32[]{:S(2)}) collective-permute-start(bf16[64,3584]{1,0:T(8,128)(2,1)S(1)} %get-tuple-element.166), channel_id=1, source_target_pairs={{0,2},{1,3},{4,0},{5,1},{8,4},{9,5},{12,8},{13,9},{14,12},{15,13},... | collective-permute-start | bytes 1376264 | tf_op jit(solution)/shard_map/ppermute | solution.py:271
  149.0 8.5 %collective-permute-start.25 = (bf16[32,3584]{1,0:T(8,128)(2,1)S(1)}, bf16[32,3584]{1,0:T(8,128)(2,1)S(1)}, u32[]{:S(2)}, u32[]{:S(2)}) collective-permute-start(bf16[32,3584]{1,0:T(8,128)(2,1)S(1)} %get-tuple-element.168), channel_id=1, source_target_pairs={{0,4},{1,5},{4,8},{5,9},{8,12},{9,13},{12,14},{13,15},{14,10},{15,... | collective-permute-start | bytes 688136 | tf_op jit(solution)/shard_map/ppermute | solution.py:271
  149.5 8.5 %collective-permute-start.26 = (bf16[32,3584]{1,0:T(8,128)(2,1)S(1)}, bf16[32,3584]{1,0:T(8,128)(2,1)S(1)}, u32[]{:S(2)}, u32[]{:S(2)}) collective-permute-start(bf16[32,3584]{1,0:T(8,128)(2,1)S(1)} %get-tuple-element.169), channel_id=1, source_target_pairs={{0,2},{1,3},{4,0},{5,1},{8,4},{9,5},{12,8},{13,9},{14,12},{15,13},... | collective-permute-start | bytes 688136 | tf_op jit(solution)/shard_map/ppermute | solution.py:271
  151.1 10.4 %collective-permute-start.28 = (bf16[32,3584]{1,0:T(8,128)(2,1)S(1)}, bf16[32,3584]{1,0:T(8,128)(2,1)S(1)}, u32[]{:S(2)}, u32[]{:S(2)}) collective-permute-start(bf16[32,3584]{1,0:T(8,128)(2,1)S(1)} %get-tuple-element.171), channel_id=1, source_target_pairs={{0,4},{1,5},{4,8},{5,9},{8,12},{9,13},{12,14},{13,15},{14,10},{15,... | collective-permute-start | bytes 688136 | tf_op jit(solution)/shard_map/ppermute | solution.py:271
  151.6 10.2 %collective-permute-start.29 = (bf16[32,3584]{1,0:T(8,128)(2,1)S(1)}, bf16[32,3584]{1,0:T(8,128)(2,1)S(1)}, u32[]{:S(2)}, u32[]{:S(2)}) collective-permute-start(bf16[32,3584]{1,0:T(8,128)(2,1)S(1)} %get-tuple-element.172), channel_id=1, source_target_pairs={{0,2},{1,3},{4,0},{5,1},{8,4},{9,5},{12,8},{13,9},{14,12},{15,13},... | collective-permute-start | bytes 688136 | tf_op jit(solution)/shard_map/ppermute | solution.py:271
  158.1 6.1 %collective-permute-start.27 = (bf16[32,3584]{1,0:T(8,128)(2,1)S(1)}, bf16[32,3584]{1,0:T(8,128)(2,1)S(1)}, u32[]{:S(2)}, u32[]{:S(2)}) collective-permute-start(bf16[32,3584]{1,0:T(8,128)(2,1)S(1)} %get-tuple-element.170), channel_id=1, source_target_pairs={{0,4},{1,5},{4,8},{5,9},{8,12},{9,13},{12,14},{13,15},{14,10},{15,... | collective-permute-start | bytes 688136 | tf_op jit(solution)/shard_map/ppermute | solution.py:271
  158.5 6.0 %collective-permute-start.31 = (bf16[32,3584]{1,0:T(8,128)(2,1)S(1)}, bf16[32,3584]{1,0:T(8,128)(2,1)S(1)}, u32[]{:S(2)}, u32[]{:S(2)}) collective-permute-start(bf16[32,3584]{1,0:T(8,128)(2,1)S(1)} %get-tuple-element.175), channel_id=1, source_target_pairs={{0,2},{1,3},{4,0},{5,1},{8,4},{9,5},{12,8},{13,9},{14,12},{15,13},... | collective-permute-start | bytes 688136 | tf_op jit(solution)/shard_map/ppermute | solution.py:271
  161.8 6.1 %collective-permute-start.30 = (bf16[32,3584]{1,0:T(8,128)(2,1)S(1)}, bf16[32,3584]{1,0:T(8,128)(2,1)S(1)}, u32[]{:S(2)}, u32[]{:S(2)}) collective-permute-start(bf16[32,3584]{1,0:T(8,128)(2,1)S(1)} %get-tuple-element.173), channel_id=1, source_target_pairs={{0,4},{1,5},{4,8},{5,9},{8,12},{9,13},{12,14},{13,15},{14,10},{15,... | collective-permute-start | bytes 688136 | tf_op jit(solution)/shard_map/ppermute | solution.py:271
  162.3 6.0 %collective-permute-start.32 = (bf16[32,3584]{1,0:T(8,128)(2,1)S(1)}, bf16[32,3584]{1,0:T(8,128)(2,1)S(1)}, u32[]{:S(2)}, u32[]{:S(2)}) collective-permute-start(bf16[32,3584]{1,0:T(8,128)(2,1)S(1)} %get-tuple-element.176), channel_id=1, source_target_pairs={{0,2},{1,3},{4,0},{5,1},{8,4},{9,5},{12,8},{13,9},{14,12},{15,13},... | collective-permute-start | bytes 688136 | tf_op jit(solution)/shard_map/ppermute | solution.py:271

commit v8 on v7

--- a/solution.py
+++ b/solution.py
@@ -80,7 +80,7 @@
             pltpu.VMEM((rows, LANES), jnp.float32),
             pltpu.VMEM((rows, SPAN * hid), jnp.bfloat16),
         ],
-        compiler_params=pltpu.CompilerParams(vmem_limit_bytes=(13 if rows <= 256 else 16) * MIB),
+        compiler_params=pltpu.CompilerParams(vmem_limit_bytes=8 * MIB),
         cost_estimate=small_cost(),
     )(expert, *blocks, *own, *other)
 
@@ -177,20 +177,27 @@
     )(tokens, ids.T, codes.T)
 
 
-def hand_on_kernel(expert_ref, *refs):
-    refs[-1][0] = expert_ref[0]
-
-
-def hand_on(expert, arrays):
-    return pl.pallas_call(
-        hand_on_kernel,
-        in_specs=[pl.BlockSpec(memory_space=pltpu.SMEM)]
-        + [pl.BlockSpec(memory_space=pltpu.VMEM)] * len(arrays),
-        out_specs=pl.BlockSpec(memory_space=pltpu.SMEM),
-        out_shape=jax.ShapeDtypeStruct(expert.shape, expert.dtype),
+def bring_in_kernel(n, *refs):
+    copies = [
+        pltpu.make_async_copy(refs[i], refs[n + i], refs[2 * n].at[i]) for i in range(n)
+    ]
+    for copy in copies:
+        copy.start()
+    for copy in copies:
+        copy.wait()
+
+
+def bring_in(arrays):
+    n = len(arrays)
+    return pl.pallas_call(
+        functools.partial(bring_in_kernel, n),
+        in_specs=[pl.BlockSpec(memory_space=pl.ANY)] * n,
+        out_specs=[pl.BlockSpec(memory_space=pltpu.VMEM)] * n,
+        out_shape=[jax.ShapeDtypeStruct(array.shape, array.dtype) for array in arrays],
+        scratch_shapes=[pltpu.SemaphoreType.DMA((n,))],
         compiler_params=pltpu.CompilerParams(vmem_limit_bytes=2 * MIB),
         cost_estimate=small_cost(),
-    )(expert, *arrays)
+    )(*arrays)
 
 
 def body(tokens, expert_ids, gate_codes, w_gate, w_up, w_down):
@@ -212,16 +219,17 @@
 
     forward, backward = perm(1), perm(-1)
     swap = [(node, node ^ 1) for node in range(nodes)]
-    expert = (lax.axis_index("node") // SPAN).astype(jnp.int32).reshape(1)
+    expert = lax.div(lax.axis_index("node"), jnp.int32(SPAN)).reshape(1)
+    tokens, expert = lax.optimization_barrier((tokens, expert))
 
     rows = with_codes(ring, tokens, expert_ids, gate_codes)
 
     near = [lax.ppermute(rows, "node", forward), lax.ppermute(rows, "node", backward)]
-    own, _ = lax.optimization_barrier(((w_gate, w_up, w_down), rows))
-    expert = hand_on(expert, own)
-    other = [lax.ppermute(weight, "node", swap) for weight in own]
-
-    near, expert = lax.optimization_barrier((near, expert))
+    weights, _ = lax.optimization_barrier(((w_gate, w_up, w_down), rows))
+    other = [lax.ppermute(weight, "node", swap) for weight in weights]
+    own = bring_in(weights)
+
+    near, own = lax.optimization_barrier((near, own))
     halves = split(near)
     ahead, behind = ([None, halves[0]], [None, halves[1]]), ([None, halves[2]], [None, halves[3]])
     parts = {}

time: 170 us -> 159 us (0.935)
  Pallas kernels: 67.5 us -> 39 us
  waiting for transfers between devices: 60.5 us -> 77.1 us
    pallas_call x6, Pallas kernels: 64.9 us -> 36.3 us  [expert_parts(): pl.pallas_call(functools.partial(expert_kernel, n, experts, dim, half), i...]
    ppermute x5, waiting for transfers between devices: 0.01 us -> 9.44 us  [send(): ahead[h].append(lax.ppermute(ahead[h][s - 1], 'node', forward))]
    ppermute x18, waiting for transfers between devices: 44.1 us -> 49.4 us  [pass_on(): came[h, sign] = lax.ppermute(total, 'node', ways[sign])]
    ppermute x5, starting transfers between devices: 1.91 us -> 5.27 us  [send(): ahead[h].append(lax.ppermute(ahead[h][s - 1], 'node', forward))]
    ppermute x5, starting transfers between devices: 8.48 us -> 6.26 us  [send(): behind[h].append(lax.ppermute(behind[h][s - 1], 'node', backward))]
    ppermute x5, waiting for transfers between devices: 0.01 us -> 2.12 us  [send(): behind[h].append(lax.ppermute(behind[h][s - 1], 'node', backward))]
    unnamed x18 -> x12, local copies, waits for them, and re-layouts: 8.67 us -> 8.65 us
  transfers between devices with their start and end apart: 33 -> 33, of which waited for: 16 -> 24; matrix products, arithmetic and copies ran while one was open for 0% -> 0% of each run, Pallas kernels for 39% -> 24%
where the time goes in v8:
time: 159 us
  waiting for transfers between devices  77.1 us (48%)
  Pallas kernels  39 us (25%)
  starting transfers between devices  33.8 us (21%)
  local copies, waits for them, and re-layouts  8.65 us (5%)
    ppermute x18, waiting for transfers between devices, pass_on(): came[h, sign] = lax.ppermute(total, 'node', ways[sign])  49.4 us
    pallas_call x6, Pallas kernels, expert_parts(): pl.pallas_call(functools.partial(expert_kernel, n, experts, dim, half), i...  36.3 us
    ppermute x18, starting transfers between devices, pass_on(): came[h, sign] = lax.ppermute(total, 'node', ways[sign])  18.5 us
    ppermute x1, waiting for transfers between devices, body(): lax.ppermute(rows, 'node', backward)  14.8 us
    ppermute x5, waiting for transfers between devices, send(): ahead[h].append(lax.ppermute(ahead[h][s - 1], 'node', forward))  9.44 us
    unnamed x12, local copies, waits for them, and re-layouts  8.65 us
    ppermute x5, starting transfers between devices, send(): behind[h].append(lax.ppermute(behind[h][s - 1], 'node', backward))  6.26 us
    ppermute x5, starting transfers between devices, send(): ahead[h].append(lax.ppermute(ahead[h][s - 1], 'node', forward))  5.27 us
  transfers between devices with their start and end apart: 33, of which 24 were waited for; matrix products, arithmetic and copies ran while one was open for 0% of the time, Pallas kernels for 24%

profile of v8, /device:TPU:0, one launch (start us, length us, event | category | flops | bytes accessed | tf_op | source)
XLA Modules:
  0.0 158.7 jit_solution(4032557683323898881)
XLA Ops:
  0.0 1.2 copy-done.3
  3.7 2.6 %collective-permute-start.1 = (bf16[128,3712]{1,0:T(8,128)(2,1)S(1)}, bf16[128,3712]{1,0:T(8,128)(2,1)S(1)}, u32[]{:S(2)}, u32[]{:S(2)}) collective-permute-start(bf16[128,3712]{1,0:T(8,128)(2,1)S(1)} %shard_map.64.refs_0_), channel_id=1, source_target_pairs={{0,2},{1,3},{4,0},{5,1},{8,4},{9,5},{12,8},{13,9},{14,12},{15,13},... | collective-permute-start | bytes 2850824 | tf_op jit(solution)/shard_map/ppermute | solution.py:227
  6.4 2.0 %copy-done = bf16[3584,512]{1,0:T(8,128)(2,1)S(1)} copy-done((bf16[3584,512]{1,0:T(8,128)(2,1)S(1)}, bf16[3584,512]{1,0:T(8,128)(2,1)}, u32[]{:S(2)}) %copy-start) | copy-done | bytes 3670040
  8.4 2.0 %copy-done.1 = bf16[3584,512]{1,0:T(8,128)(2,1)S(1)} copy-done((bf16[3584,512]{1,0:T(8,128)(2,1)S(1)}, bf16[3584,512]{1,0:T(8,128)(2,1)}, u32[]{:S(2)}) %copy-start.1) | copy-done | bytes 3670040
  10.5 2.0 %copy-done.2 = bf16[512,3584]{1,0:T(8,128)(2,1)S(1)} copy-done((bf16[512,3584]{1,0:T(8,128)(2,1)S(1)}, bf16[512,3584]{1,0:T(8,128)(2,1)}, u32[]{:S(2)}) %copy-start.2) | copy-done | bytes 3670040
  13.3 14.8 %collective-permute-done.1.refs_1_.refs_2_ = bf16[128,3712]{1,0:T(8,128)(2,1)S(1)} collective-permute-done((bf16[128,3712]{1,0:T(8,128)(2,1)S(1)}, bf16[128,3712]{1,0:T(8,128)(2,1)S(1)}, u32[]{:S(2)}, u32[]{:S(2)}) %collective-permute-start.1) | collective-permute-done | bytes 950304 | tf_op jit(solution)/shard_map/ppermute | solution.py:227
  28.0 1.4 collective-permute-done.refs_0_.refs_1_
  30.0 1.7 %collective-permute-start.3 = (bf16[64,3712]{1,0:T(8,128)(2,1)S(1)}, bf16[64,3712]{1,0:T(8,128)(2,1)S(1)}, u32[]{:S(2)}, u32[]{:S(2)}) collective-permute-start(bf16[64,3712]{1,0:T(8,128)(2,1)S(1)} %get-tuple-element.110), channel_id=1, source_target_pairs={{0,2},{1,3},{4,0},{5,1},{8,4},{9,5},{12,8},{13,9},{14,12},{15,13},... | collective-permute-start | bytes 1425416 | tf_op jit(solution)/shard_map/ppermute | solution.py:252
  32.0 1.7 %collective-permute-start.8 = (bf16[64,3712]{1,0:T(8,128)(2,1)S(1)}, bf16[64,3712]{1,0:T(8,128)(2,1)S(1)}, u32[]{:S(2)}, u32[]{:S(2)}) collective-permute-start(bf16[64,3712]{1,0:T(8,128)(2,1)S(1)} %get-tuple-element.130), channel_id=1, source_target_pairs={{0,2},{1,3},{4,0},{5,1},{8,4},{9,5},{12,8},{13,9},{14,12},{15,13},... | collective-permute-start | bytes 1425416 | tf_op jit(solution)/shard_map/ppermute | solution.py:252
  33.7 10.8 %shard_map.67 = (bf16[64,3584]{1,0:T(8,128)(2,1)S(1)}, bf16[64,3584]{1,0:T(8,128)(2,1)S(1)}, bf16[64,3584]{1,0:T(8,128)(2,1)S(1)}, bf16[64,3584]{1,0:T(8,128)(2,...) custom-call(s32[1]{0:T(128)} %bitcast.expert_ref, bf16[128,3712]{1,0:T(8,128)(2,1)S(1)} %shard_map.64.refs_0_, ...), custom_call_target="tpu_custom_call" | custom-call | flops 1024 | bytes 1024 | tf_op jit(solution)/shard_map/pallas_call | solution.py:73
  44.5 1.0 collective-permute-start.9
  45.5 1.0 collective-permute-start.10
  46.5 5.1 %shard_map.68 = (bf16[64,3584]{1,0:T(8,128)(2,1)S(1)}, bf16[64,3584]{1,0:T(8,128)(2,1)S(1)}) custom-call(s32[1]{0:T(128)} %bitcast.expert_ref, bf16[64,3712]{1,0:T(8,128)(2,1)S(1)} %collective-permute-done.2.refs_0_, bf16[64,3712]{1,0:T(8,128)(2,1)S(1)} %collective-permute-done.3.refs_1_, bf16[3584,512]{1,0:T(8,128)(2,1)S(1)} %get-tuple-element.115.refs_3_.refs_2_, ...), custom_call_target="tpu_custom_call" | custom-call | flops 1024 | bytes 1024 | tf_op jit(solution)/shard_map/pallas_call | solution.py:73
  51.7 1.9 %collective-permute-done.7.refs_0_ = bf16[64,3712]{1,0:T(8,128)(2,1)S(1)} collective-permute-done((bf16[64,3712]{1,0:T(8,128)(2,1)S(1)}, bf16[64,3712]{1,0:T(8,128)(2,1)S(1)}, u32[]{:S(2)}, u32[]{:S(2)}) %collective-permute-start.7) | collective-permute-done | bytes 475168 | tf_op jit(solution)/shard_map/ppermute | solution.py:250
  53.9 1.7 %collective-permute-start.11 = (bf16[64,3712]{1,0:T(8,128)(2,1)S(1)}, bf16[64,3712]{1,0:T(8,128)(2,1)S(1)}, u32[]{:S(2)}, u32[]{:S(2)}) collective-permute-start(bf16[64,3712]{1,0:T(8,128)(2,1)S(1)} %collective-permute-done.7.refs_0_), channel_id=1, source_target_pairs={{0,4},{1,5},{4,8},{5,9},{8,12},{9,13},{12,14},{13,15},{14,10},{15,... | collective-permute-start | bytes 1425416 | tf_op jit(solution)/shard_map/ppermute | solution.py:250
  56.0 5.1 %shard_map.69 = (bf16[64,3584]{1,0:T(8,128)(2,1)S(1)}, bf16[64,3584]{1,0:T(8,128)(2,1)S(1)}) custom-call(s32[1]{0:T(128)} %bitcast.expert_ref, bf16[64,3712]{1,0:T(8,128)(2,1)S(1)} %collective-permute-done.7.refs_0_, bf16[64,3712]{1,0:T(8,128)(2,1)S(1)} %collective-permute-done.8.refs_1_, bf16[3584,512]{1,0:T(8,128)(2,1)S(1)} %get-tuple-element.115.refs_3_.refs_2_, ...), custom_call_target="tpu_custom_call" | custom-call | flops 1024 | bytes 1024 | tf_op jit(solution)/shard_map/pallas_call | solution.py:73
  61.1 2.7 %collective-permute-done.9.refs_0_ = bf16[64,3712]{1,0:T(8,128)(2,1)S(1)} collective-permute-done((bf16[64,3712]{1,0:T(8,128)(2,1)S(1)}, bf16[64,3712]{1,0:T(8,128)(2,1)S(1)}, u32[]{:S(2)}, u32[]{:S(2)}) %collective-permute-start.9) | collective-permute-done | bytes 475168 | tf_op jit(solution)/shard_map/ppermute | solution.py:250
  64.1 1.7 %collective-permute-start.13 = (bf16[64,3712]{1,0:T(8,128)(2,1)S(1)}, bf16[64,3712]{1,0:T(8,128)(2,1)S(1)}, u32[]{:S(2)}, u32[]{:S(2)}) collective-permute-start(bf16[64,3712]{1,0:T(8,128)(2,1)S(1)} %collective-permute-done.9.refs_0_), channel_id=1, source_target_pairs={{0,4},{1,5},{4,8},{5,9},{8,12},{9,13},{12,14},{13,15},{14,10},{15,... | collective-permute-start | bytes 1425416 | tf_op jit(solution)/shard_map/ppermute | solution.py:250
  65.9 5.1 %shard_map.70 = (bf16[64,3584]{1,0:T(8,128)(2,1)S(1)}, bf16[64,3584]{1,0:T(8,128)(2,1)S(1)}) custom-call(s32[1]{0:T(128)} %bitcast.expert_ref, bf16[64,3712]{1,0:T(8,128)(2,1)S(1)} %collective-permute-done.9.refs_0_, bf16[64,3712]{1,0:T(8,128)(2,1)S(1)} %collective-permute-done.10.refs_1_, bf16[3584,512]{1,0:T(8,128)(2,1)S(1)} %get-tuple-element.115.refs_3_.refs_2_, ...), custom_call_target="tpu_custom_call" | custom-call | flops 1024 | bytes 1024 | tf_op jit(solution)/shard_map/pallas_call | solution.py:73
  71.0 3.0 %collective-permute-done.11.refs_0_ = bf16[64,3712]{1,0:T(8,128)(2,1)S(1)} collective-permute-done((bf16[64,3712]{1,0:T(8,128)(2,1)S(1)}, bf16[64,3712]{1,0:T(8,128)(2,1)S(1)}, u32[]{:S(2)}, u32[]{:S(2)}) %collective-permute-start.11) | collective-permute-done | bytes 475168 | tf_op jit(solution)/shard_map/ppermute | solution.py:250
  74.0 1.6 collective-permute-start.14
  75.5 5.1 %shard_map.71 = (bf16[64,3584]{1,0:T(8,128)(2,1)S(1)}, bf16[64,3584]{1,0:T(8,128)(2,1)S(1)}) custom-call(s32[1]{0:T(128)} %bitcast.expert_ref, bf16[64,3712]{1,0:T(8,128)(2,1)S(1)} %collective-permute-done.11.refs_0_, bf16[64,3712]{1,0:T(8,128)(2,1)S(1)} %collective-permute-done.12.refs_1_, bf16[3584,512]{1,0:T(8,128)(2,1)S(1)} %get-tuple-element.115.refs_3_.refs_2_, ...), custom_call_target="tpu_custom_call" | custom-call | flops 1024 | bytes 1024 | tf_op jit(solution)/shard_map/pallas_call | solution.py:73
  80.7 1.8 %collective-permute-done.13.refs_0_ = bf16[64,3712]{1,0:T(8,128)(2,1)S(1)} collective-permute-done((bf16[64,3712]{1,0:T(8,128)(2,1)S(1)}, bf16[64,3712]{1,0:T(8,128)(2,1)S(1)}, u32[]{:S(2)}, u32[]{:S(2)}) %collective-permute-start.13) | collective-permute-done | bytes 475168 | tf_op jit(solution)/shard_map/ppermute | solution.py:250
  82.5 1.4 collective-permute-done.14.refs_1_
  83.9 1.4 collective-permute-start.16
  85.9 5.1 %shard_map.72 = (bf16[64,3584]{1,0:T(8,128)(2,1)S(1)}, bf16[64,3584]{1,0:T(8,128)(2,1)S(1)}) custom-call(s32[1]{0:T(128)} %bitcast.expert_ref, bf16[64,3712]{1,0:T(8,128)(2,1)S(1)} %collective-permute-done.13.refs_0_, bf16[64,3712]{1,0:T(8,128)(2,1)S(1)} %collective-permute-done.14.refs_1_, bf16[3584,512]{1,0:T(8,128)(2,1)S(1)} %get-tuple-element.115.refs_3_.refs_2_, ...), custom_call_target="tpu_custom_call" | custom-call | flops 1024 | bytes 1024 | tf_op jit(solution)/shard_map/pallas_call | solution.py:73
  91.0 2.3 %collective-permute-done.16.refs_3_ = bf16[64,3584]{1,0:T(8,128)(2,1)S(1)} collective-permute-done((bf16[64,3584]{1,0:T(8,128)(2,1)S(1)}, bf16[64,3584]{1,0:T(8,128)(2,1)S(1)}, u32[]{:S(2)}, u32[]{:S(2)}) %collective-permute-start.16) | collective-permute-done | bytes 458784 | tf_op jit(solution)/shard_map/ppermute | solution.py:279
  93.3 2.5 %collective-permute-done.15.refs_2_ = bf16[64,3584]{1,0:T(8,128)(2,1)S(1)} collective-permute-done((bf16[64,3584]{1,0:T(8,128)(2,1)S(1)}, bf16[64,3584]{1,0:T(8,128)(2,1)S(1)}, u32[]{:S(2)}, u32[]{:S(2)}) %collective-permute-start.15) | collective-permute-done | bytes 458784 | tf_op jit(solution)/shard_map/ppermute | solution.py:279
  96.1 1.9 %collective-permute-start.18 = (bf16[64,3584]{1,0:T(8,128)(2,1)S(1)}, bf16[64,3584]{1,0:T(8,128)(2,1)S(1)}, u32[]{:S(2)}, u32[]{:S(2)}) collective-permute-start(bf16[64,3584]{1,0:T(8,128)(2,1)S(1)} %get-tuple-element.169), channel_id=1, source_target_pairs={{0,4},{1,5},{4,8},{5,9},{8,12},{9,13},{12,14},{13,15},{14,10},{15,... | collective-permute-start | bytes 1376264 | tf_op jit(solution)/shard_map/ppermute | solution.py:279
  98.0 1.6 collective-permute-start.20
  100.0 9.4 %collective-permute-done.17.refs_2_.refs_4_ = bf16[64,3584]{1,0:T(8,128)(2,1)S(1)} collective-permute-done((bf16[64,3584]{1,0:T(8,128)(2,1)S(1)}, bf16[64,3584]{1,0:T(8,128)(2,1)S(1)}, u32[]{:S(2)}, u32[]{:S(2)}) %collective-permute-start.17) | collective-permute-done | bytes 458784 | tf_op jit(solution)/shard_map/ppermute | solution.py:279
  109.6 1.6 %collective-permute-start.19 = (bf16[64,3584]{1,0:T(8,128)(2,1)S(1)}, bf16[64,3584]{1,0:T(8,128)(2,1)S(1)}, u32[]{:S(2)}, u32[]{:S(2)}) collective-permute-start(bf16[64,3584]{1,0:T(8,128)(2,1)S(1)} %get-tuple-element.170), channel_id=1, source_target_pairs={{0,2},{1,3},{4,0},{5,1},{8,4},{9,5},{12,8},{13,9},{14,12},{15,13},... | collective-permute-start | bytes 1376264 | tf_op jit(solution)/shard_map/ppermute | solution.py:279
  111.7 7.7 %collective-permute-done.20.refs_2_ = bf16[64,3584]{1,0:T(8,128)(2,1)S(1)} collective-permute-done((bf16[64,3584]{1,0:T(8,128)(2,1)S(1)}, bf16[64,3584]{1,0:T(8,128)(2,1)S(1)}, u32[]{:S(2)}, u32[]{:S(2)}) %collective-permute-start.20) | collective-permute-done | bytes 458784 | tf_op jit(solution)/shard_map/ppermute | solution.py:279
  119.5 2.0 %collective-permute-start.22 = (bf16[64,3584]{1,0:T(8,128)(2,1)S(1)}, bf16[64,3584]{1,0:T(8,128)(2,1)S(1)}, u32[]{:S(2)}, u32[]{:S(2)}) collective-permute-start(bf16[64,3584]{1,0:T(8,128)(2,1)S(1)} %get-tuple-element.179), channel_id=1, source_target_pairs={{0,4},{1,5},{4,8},{5,9},{8,12},{9,13},{12,14},{13,15},{14,10},{15,... | collective-permute-start | bytes 1376264 | tf_op jit(solution)/shard_map/ppermute | solution.py:279
  121.5 7.6 %collective-permute-done.19.refs_4_.refs_1_ = bf16[64,3584]{1,0:T(8,128)(2,1)S(1)} collective-permute-done((bf16[64,3584]{1,0:T(8,128)(2,1)S(1)}, bf16[64,3584]{1,0:T(8,128)(2,1)S(1)}, u32[]{:S(2)}, u32[]{:S(2)}) %collective-permute-start.19) | collective-permute-done | bytes 458784 | tf_op jit(solution)/shard_map/ppermute | solution.py:279
  129.1 5.1 %collective-permute-done.22.refs_2_ = bf16[64,3584]{1,0:T(8,128)(2,1)S(1)} collective-permute-done((bf16[64,3584]{1,0:T(8,128)(2,1)S(1)}, bf16[64,3584]{1,0:T(8,128)(2,1)S(1)}, u32[]{:S(2)}, u32[]{:S(2)}) %collective-permute-start.22) | collective-permute-done | bytes 458784 | tf_op jit(solution)/shard_map/ppermute | solution.py:279
  135.2 1.6 collective-permute-start.25
  137.3 1.5 collective-permute-start.28
  139.3 4.2 %collective-permute-done.25.refs_2_ = bf16[32,3584]{1,0:T(8,128)(2,1)S(1)} collective-permute-done((bf16[32,3584]{1,0:T(8,128)(2,1)S(1)}, bf16[32,3584]{1,0:T(8,128)(2,1)S(1)}, u32[]{:S(2)}, u32[]{:S(2)}) %collective-permute-start.25) | collective-permute-done | bytes 229408 | tf_op jit(solution)/shard_map/ppermute | solution.py:279
  143.5 1.7 %collective-permute-done.26.refs_3_ = bf16[32,3584]{1,0:T(8,128)(2,1)S(1)} collective-permute-done((bf16[32,3584]{1,0:T(8,128)(2,1)S(1)}, bf16[32,3584]{1,0:T(8,128)(2,1)S(1)}, u32[]{:S(2)}, u32[]{:S(2)}) %collective-permute-start.26) | collective-permute-done | bytes 229408 | tf_op jit(solution)/shard_map/ppermute | solution.py:279
  145.3 1.8 %collective-permute-start.27 = (bf16[32,3584]{1,0:T(8,128)(2,1)S(1)}, bf16[32,3584]{1,0:T(8,128)(2,1)S(1)}, u32[]{:S(2)}, u32[]{:S(2)}) collective-permute-start(bf16[32,3584]{1,0:T(8,128)(2,1)S(1)} %get-tuple-element.184), channel_id=1, source_target_pairs={{0,4},{1,5},{4,8},{5,9},{8,12},{9,13},{12,14},{13,15},{14,10},{15,... | collective-permute-start | bytes 688136 | tf_op jit(solution)/shard_map/ppermute | solution.py:279
  147.4 1.0 collective-permute-done.28.refs_2_
  148.4 1.6 collective-permute-done.29.refs_3_
  150.0 1.4 collective-permute-start.30
  152.1 1.0 collective-permute-done.31.refs_6_
  153.1 3.0 %collective-permute-done.30.refs_3_ = bf16[32,3584]{1,0:T(8,128)(2,1)S(1)} collective-permute-done((bf16[32,3584]{1,0:T(8,128)(2,1)S(1)}, bf16[32,3584]{1,0:T(8,128)(2,1)S(1)}, u32[]{:S(2)}, u32[]{:S(2)}) %collective-permute-start.30) | collective-permute-done | bytes 229408 | tf_op jit(solution)/shard_map/ppermute | solution.py:279
  156.1 1.4 collective-permute-done.32.refs_7_
  157.5 1.2 shard_map.79
  (46 shorter events, 10.4 us)
Async XLA Ops:
  0.0 1.2 copy-start.3
  1.2 0.7 copy-start.4
  1.9 0.7 copy-start.5
  2.7 29.0 %collective-permute-start.4 = (bf16[3584,512]{1,0:T(8,128)(2,1)}, bf16[3584,512]{1,0:T(8,128)(2,1)S(1)}, u32[]{:S(2)}, u32[]{:S(2)}) collective-permute-start(bf16[3584,512]{1,0:T(8,128)(2,1)} %refs_0_), channel_id=1, source_target_pairs={{0,1},{1,0},{2,3},{3,2},{4,5},{5,4},{6,7},{7,6},{8,9},{9,8},{10,11... | collective-permute-start | bytes 11010056 | tf_op jit(solution)/shard_map/ppermute | solution.py:229
  3.2 28.8 %collective-permute-start.5 = (bf16[3584,512]{1,0:T(8,128)(2,1)}, bf16[3584,512]{1,0:T(8,128)(2,1)S(1)}, u32[]{:S(2)}, u32[]{:S(2)}) collective-permute-start(bf16[3584,512]{1,0:T(8,128)(2,1)} %refs_1_), channel_id=1, source_target_pairs={{0,1},{1,0},{2,3},{3,2},{4,5},{5,4},{6,7},{7,6},{8,9},{9,8},{10,11... | collective-permute-start | bytes 11010056 | tf_op jit(solution)/shard_map/ppermute | solution.py:229
  3.3 30.4 %collective-permute-start.6 = (bf16[512,3584]{1,0:T(8,128)(2,1)}, bf16[512,3584]{1,0:T(8,128)(2,1)S(1)}, u32[]{:S(2)}, u32[]{:S(2)}) collective-permute-start(bf16[512,3584]{1,0:T(8,128)(2,1)} %refs_2_), channel_id=1, source_target_pairs={{0,1},{1,0},{2,3},{3,2},{4,5},{5,4},{6,7},{7,6},{8,9},{9,8},{10,11... | collective-permute-start | bytes 11010056 | tf_op jit(solution)/shard_map/ppermute | solution.py:229
  3.7 24.3 %collective-permute-start.1 = (bf16[128,3712]{1,0:T(8,128)(2,1)S(1)}, bf16[128,3712]{1,0:T(8,128)(2,1)S(1)}, u32[]{:S(2)}, u32[]{:S(2)}) collective-permute-start(bf16[128,3712]{1,0:T(8,128)(2,1)S(1)} %shard_map.64.refs_0_), channel_id=1, source_target_pairs={{0,2},{1,3},{4,0},{5,1},{8,4},{9,5},{12,8},{13,9},{14,12},{15,13},... | collective-permute-start | bytes 2850824 | tf_op jit(solution)/shard_map/ppermute | solution.py:227
  6.3 23.1 %collective-permute-start = (bf16[128,3712]{1,0:T(8,128)(2,1)S(1)}, bf16[128,3712]{1,0:T(8,128)(2,1)S(1)}, u32[]{:S(2)}, u32[]{:S(2)}) collective-permute-start(bf16[128,3712]{1,0:T(8,128)(2,1)S(1)} %shard_map.64.refs_0_), channel_id=1, source_target_pairs={{0,4},{1,5},{4,8},{5,9},{8,12},{9,13},{12,14},{13,15},{14,10},{15,... | collective-permute-start | bytes 2850824 | tf_op jit(solution)/shard_map/ppermute | solution.py:227
  6.4 2.0 %copy-start = (bf16[3584,512]{1,0:T(8,128)(2,1)S(1)}, bf16[3584,512]{1,0:T(8,128)(2,1)}, u32[]{:S(2)}) copy-start(bf16[3584,512]{1,0:T(8,128)(2,1)} %refs_0_) | copy-start | bytes 11010052
  8.4 2.0 %copy-start.1 = (bf16[3584,512]{1,0:T(8,128)(2,1)S(1)}, bf16[3584,512]{1,0:T(8,128)(2,1)}, u32[]{:S(2)}) copy-start(bf16[3584,512]{1,0:T(8,128)(2,1)} %refs_1_) | copy-start | bytes 11010052
  10.4 2.0 %copy-start.2 = (bf16[512,3584]{1,0:T(8,128)(2,1)S(1)}, bf16[512,3584]{1,0:T(8,128)(2,1)}, u32[]{:S(2)}) copy-start(bf16[512,3584]{1,0:T(8,128)(2,1)} %refs_2_) | copy-start | bytes 11010052
  29.6 14.9 %collective-permute-start.2 = (bf16[64,3712]{1,0:T(8,128)(2,1)S(1)}, bf16[64,3712]{1,0:T(8,128)(2,1)S(1)}, u32[]{:S(2)}, u32[]{:S(2)}) collective-permute-start(bf16[64,3712]{1,0:T(8,128)(2,1)S(1)} %get-tuple-element.109), channel_id=1, source_target_pairs={{0,4},{1,5},{4,8},{5,9},{8,12},{9,13},{12,14},{13,15},{14,10},{15,... | collective-permute-start | bytes 1425416 | tf_op jit(solution)/shard_map/ppermute | solution.py:250
  30.0 14.5 %collective-permute-start.3 = (bf16[64,3712]{1,0:T(8,128)(2,1)S(1)}, bf16[64,3712]{1,0:T(8,128)(2,1)S(1)}, u32[]{:S(2)}, u32[]{:S(2)}) collective-permute-start(bf16[64,3712]{1,0:T(8,128)(2,1)S(1)} %get-tuple-element.110), channel_id=1, source_target_pairs={{0,2},{1,3},{4,0},{5,1},{8,4},{9,5},{12,8},{13,9},{14,12},{15,13},... | collective-permute-start | bytes 1425416 | tf_op jit(solution)/shard_map/ppermute | solution.py:252
  31.6 22.0 %collective-permute-start.7 = (bf16[64,3712]{1,0:T(8,128)(2,1)S(1)}, bf16[64,3712]{1,0:T(8,128)(2,1)S(1)}, u32[]{:S(2)}, u32[]{:S(2)}) collective-permute-start(bf16[64,3712]{1,0:T(8,128)(2,1)S(1)} %get-tuple-element.129), channel_id=1, source_target_pairs={{0,4},{1,5},{4,8},{5,9},{8,12},{9,13},{12,14},{13,15},{14,10},{15,... | collective-permute-start | bytes 1425416 | tf_op jit(solution)/shard_map/ppermute | solution.py:250
  32.0 22.0 %collective-permute-start.8 = (bf16[64,3712]{1,0:T(8,128)(2,1)S(1)}, bf16[64,3712]{1,0:T(8,128)(2,1)S(1)}, u32[]{:S(2)}, u32[]{:S(2)}) collective-permute-start(bf16[64,3712]{1,0:T(8,128)(2,1)S(1)} %get-tuple-element.130), channel_id=1, source_target_pairs={{0,2},{1,3},{4,0},{5,1},{8,4},{9,5},{12,8},{13,9},{14,12},{15,13},... | collective-permute-start | bytes 1425416 | tf_op jit(solution)/shard_map/ppermute | solution.py:252
  44.5 19.3 %collective-permute-start.9 = (bf16[64,3712]{1,0:T(8,128)(2,1)S(1)}, bf16[64,3712]{1,0:T(8,128)(2,1)S(1)}, u32[]{:S(2)}, u32[]{:S(2)}) collective-permute-start(bf16[64,3712]{1,0:T(8,128)(2,1)S(1)} %collective-permute-done.2.refs_0_), channel_id=1, source_target_pairs={{0,4},{1,5},{4,8},{5,9},{8,12},{9,13},{12,14},{13,15},{14,10},{15,... | collective-permute-start | bytes 1425416 | tf_op jit(solution)/shard_map/ppermute | solution.py:250
  45.5 18.6 %collective-permute-start.10 = (bf16[64,3712]{1,0:T(8,128)(2,1)S(1)}, bf16[64,3712]{1,0:T(8,128)(2,1)S(1)}, u32[]{:S(2)}, u32[]{:S(2)}) collective-permute-start(bf16[64,3712]{1,0:T(8,128)(2,1)S(1)} %collective-permute-done.3.refs_1_), channel_id=1, source_target_pairs={{0,2},{1,3},{4,0},{5,1},{8,4},{9,5},{12,8},{13,9},{14,12},{15,13},... | collective-permute-start | bytes 1425416 | tf_op jit(solution)/shard_map/ppermute | solution.py:252
  53.9 20.0 %collective-permute-start.11 = (bf16[64,3712]{1,0:T(8,128)(2,1)S(1)}, bf16[64,3712]{1,0:T(8,128)(2,1)S(1)}, u32[]{:S(2)}, u32[]{:S(2)}) collective-permute-start(bf16[64,3712]{1,0:T(8,128)(2,1)S(1)} %collective-permute-done.7.refs_0_), channel_id=1, source_target_pairs={{0,4},{1,5},{4,8},{5,9},{8,12},{9,13},{12,14},{13,15},{14,10},{15,... | collective-permute-start | bytes 1425416 | tf_op jit(solution)/shard_map/ppermute | solution.py:250
  55.7 18.3 %collective-permute-start.12 = (bf16[64,3712]{1,0:T(8,128)(2,1)S(1)}, bf16[64,3712]{1,0:T(8,128)(2,1)S(1)}, u32[]{:S(2)}, u32[]{:S(2)}) collective-permute-start(bf16[64,3712]{1,0:T(8,128)(2,1)S(1)} %collective-permute-done.8.refs_1_), channel_id=1, source_target_pairs={{0,2},{1,3},{4,0},{5,1},{8,4},{9,5},{12,8},{13,9},{14,12},{15,13},... | collective-permute-start | bytes 1425416 | tf_op jit(solution)/shard_map/ppermute | solution.py:252
  64.1 18.3 %collective-permute-start.13 = (bf16[64,3712]{1,0:T(8,128)(2,1)S(1)}, bf16[64,3712]{1,0:T(8,128)(2,1)S(1)}, u32[]{:S(2)}, u32[]{:S(2)}) collective-permute-start(bf16[64,3712]{1,0:T(8,128)(2,1)S(1)} %collective-permute-done.9.refs_0_), channel_id=1, source_target_pairs={{0,4},{1,5},{4,8},{5,9},{8,12},{9,13},{12,14},{13,15},{14,10},{15,... | collective-permute-start | bytes 1425416 | tf_op jit(solution)/shard_map/ppermute | solution.py:250
  74.0 9.9 %collective-permute-start.14 = (bf16[64,3712]{1,0:T(8,128)(2,1)S(1)}, bf16[64,3712]{1,0:T(8,128)(2,1)S(1)}, u32[]{:S(2)}, u32[]{:S(2)}) collective-permute-start(bf16[64,3712]{1,0:T(8,128)(2,1)S(1)} %collective-permute-done.12.refs_1_), channel_id=1, source_target_pairs={{0,2},{1,3},{4,0},{5,1},{8,4},{9,5},{12,8},{13,9},{14,12},{15,13},... | collective-permute-start | bytes 1425416 | tf_op jit(solution)/shard_map/ppermute | solution.py:252
  83.9 9.4 %collective-permute-start.16 = (bf16[64,3584]{1,0:T(8,128)(2,1)S(1)}, bf16[64,3584]{1,0:T(8,128)(2,1)S(1)}, u32[]{:S(2)}, u32[]{:S(2)}) collective-permute-start(bf16[64,3584]{1,0:T(8,128)(2,1)S(1)} %get-tuple-element.165), channel_id=1, source_target_pairs={{0,4},{1,5},{4,8},{5,9},{8,12},{9,13},{12,14},{13,15},{14,10},{15,... | collective-permute-start | bytes 1376264 | tf_op jit(solution)/shard_map/ppermute | solution.py:279
  85.3 10.5 %collective-permute-start.15 = (bf16[64,3584]{1,0:T(8,128)(2,1)S(1)}, bf16[64,3584]{1,0:T(8,128)(2,1)S(1)}, u32[]{:S(2)}, u32[]{:S(2)}) collective-permute-start(bf16[64,3584]{1,0:T(8,128)(2,1)S(1)} %get-tuple-element.164), channel_id=1, source_target_pairs={{0,2},{1,3},{4,0},{5,1},{8,4},{9,5},{12,8},{13,9},{14,12},{15,13},... | collective-permute-start | bytes 1376264 | tf_op jit(solution)/shard_map/ppermute | solution.py:279
  95.9 13.5 %collective-permute-start.17 = (bf16[64,3584]{1,0:T(8,128)(2,1)S(1)}, bf16[64,3584]{1,0:T(8,128)(2,1)S(1)}, u32[]{:S(2)}, u32[]{:S(2)}) collective-permute-start(bf16[64,3584]{1,0:T(8,128)(2,1)S(1)} %get-tuple-element.168), channel_id=1, source_target_pairs={{0,2},{1,3},{4,0},{5,1},{8,4},{9,5},{12,8},{13,9},{14,12},{15,13},... | collective-permute-start | bytes 1376264 | tf_op jit(solution)/shard_map/ppermute | solution.py:279
  96.1 13.5 %collective-permute-start.18 = (bf16[64,3584]{1,0:T(8,128)(2,1)S(1)}, bf16[64,3584]{1,0:T(8,128)(2,1)S(1)}, u32[]{:S(2)}, u32[]{:S(2)}) collective-permute-start(bf16[64,3584]{1,0:T(8,128)(2,1)S(1)} %get-tuple-element.169), channel_id=1, source_target_pairs={{0,4},{1,5},{4,8},{5,9},{8,12},{9,13},{12,14},{13,15},{14,10},{15,... | collective-permute-start | bytes 1376264 | tf_op jit(solution)/shard_map/ppermute | solution.py:279
  98.0 21.3 %collective-permute-start.20 = (bf16[64,3584]{1,0:T(8,128)(2,1)S(1)}, bf16[64,3584]{1,0:T(8,128)(2,1)S(1)}, u32[]{:S(2)}, u32[]{:S(2)}) collective-permute-start(bf16[64,3584]{1,0:T(8,128)(2,1)S(1)} %get-tuple-element.177), channel_id=1, source_target_pairs={{0,4},{1,5},{4,8},{5,9},{8,12},{9,13},{12,14},{13,15},{14,10},{15,... | collective-permute-start | bytes 1376264 | tf_op jit(solution)/shard_map/ppermute | solution.py:279
  99.6 19.8 %collective-permute-start.21 = (bf16[64,3584]{1,0:T(8,128)(2,1)S(1)}, bf16[64,3584]{1,0:T(8,128)(2,1)S(1)}, u32[]{:S(2)}, u32[]{:S(2)}) collective-permute-start(bf16[64,3584]{1,0:T(8,128)(2,1)S(1)} %get-tuple-element.178), channel_id=1, source_target_pairs={{0,2},{1,3},{4,0},{5,1},{8,4},{9,5},{12,8},{13,9},{14,12},{15,13},... | collective-permute-start | bytes 1376264 | tf_op jit(solution)/shard_map/ppermute | solution.py:279
  109.6 19.5 %collective-permute-start.19 = (bf16[64,3584]{1,0:T(8,128)(2,1)S(1)}, bf16[64,3584]{1,0:T(8,128)(2,1)S(1)}, u32[]{:S(2)}, u32[]{:S(2)}) collective-permute-start(bf16[64,3584]{1,0:T(8,128)(2,1)S(1)} %get-tuple-element.170), channel_id=1, source_target_pairs={{0,2},{1,3},{4,0},{5,1},{8,4},{9,5},{12,8},{13,9},{14,12},{15,13},... | collective-permute-start | bytes 1376264 | tf_op jit(solution)/shard_map/ppermute | solution.py:279
  111.3 17.9 %collective-permute-start.24 = (bf16[64,3584]{1,0:T(8,128)(2,1)S(1)}, bf16[64,3584]{1,0:T(8,128)(2,1)S(1)}, u32[]{:S(2)}, u32[]{:S(2)}) collective-permute-start(bf16[64,3584]{1,0:T(8,128)(2,1)S(1)} %get-tuple-element.181), channel_id=1, source_target_pairs={{0,4},{1,5},{4,8},{5,9},{8,12},{9,13},{12,14},{13,15},{14,10},{15,... | collective-permute-start | bytes 1376264 | tf_op jit(solution)/shard_map/ppermute | solution.py:279
  119.5 14.7 %collective-permute-start.22 = (bf16[64,3584]{1,0:T(8,128)(2,1)S(1)}, bf16[64,3584]{1,0:T(8,128)(2,1)S(1)}, u32[]{:S(2)}, u32[]{:S(2)}) collective-permute-start(bf16[64,3584]{1,0:T(8,128)(2,1)S(1)} %get-tuple-element.179), channel_id=1, source_target_pairs={{0,4},{1,5},{4,8},{5,9},{8,12},{9,13},{12,14},{13,15},{14,10},{15,... | collective-permute-start | bytes 1376264 | tf_op jit(solution)/shard_map/ppermute | solution.py:279
  121.5 13.7 %collective-permute-start.23 = (bf16[64,3584]{1,0:T(8,128)(2,1)S(1)}, bf16[64,3584]{1,0:T(8,128)(2,1)S(1)}, u32[]{:S(2)}, u32[]{:S(2)}) collective-permute-start(bf16[64,3584]{1,0:T(8,128)(2,1)S(1)} %get-tuple-element.180), channel_id=1, source_target_pairs={{0,2},{1,3},{4,0},{5,1},{8,4},{9,5},{12,8},{13,9},{14,12},{15,13},... | collective-permute-start | bytes 1376264 | tf_op jit(solution)/shard_map/ppermute | solution.py:279
  135.2 8.3 %collective-permute-start.25 = (bf16[32,3584]{1,0:T(8,128)(2,1)S(1)}, bf16[32,3584]{1,0:T(8,128)(2,1)S(1)}, u32[]{:S(2)}, u32[]{:S(2)}) collective-permute-start(bf16[32,3584]{1,0:T(8,128)(2,1)S(1)} %get-tuple-element.182), channel_id=1, source_target_pairs={{0,4},{1,5},{4,8},{5,9},{8,12},{9,13},{12,14},{13,15},{14,10},{15,... | collective-permute-start | bytes 688136 | tf_op jit(solution)/shard_map/ppermute | solution.py:279
  136.8 8.5 %collective-permute-start.26 = (bf16[32,3584]{1,0:T(8,128)(2,1)S(1)}, bf16[32,3584]{1,0:T(8,128)(2,1)S(1)}, u32[]{:S(2)}, u32[]{:S(2)}) collective-permute-start(bf16[32,3584]{1,0:T(8,128)(2,1)S(1)} %get-tuple-element.183), channel_id=1, source_target_pairs={{0,2},{1,3},{4,0},{5,1},{8,4},{9,5},{12,8},{13,9},{14,12},{15,13},... | collective-permute-start | bytes 688136 | tf_op jit(solution)/shard_map/ppermute | solution.py:279
  137.3 11.1 %collective-permute-start.28 = (bf16[32,3584]{1,0:T(8,128)(2,1)S(1)}, bf16[32,3584]{1,0:T(8,128)(2,1)S(1)}, u32[]{:S(2)}, u32[]{:S(2)}) collective-permute-start(bf16[32,3584]{1,0:T(8,128)(2,1)S(1)} %get-tuple-element.185), channel_id=1, source_target_pairs={{0,4},{1,5},{4,8},{5,9},{8,12},{9,13},{12,14},{13,15},{14,10},{15,... | collective-permute-start | bytes 688136 | tf_op jit(solution)/shard_map/ppermute | solution.py:279
  138.8 11.2 %collective-permute-start.29 = (bf16[32,3584]{1,0:T(8,128)(2,1)S(1)}, bf16[32,3584]{1,0:T(8,128)(2,1)S(1)}, u32[]{:S(2)}, u32[]{:S(2)}) collective-permute-start(bf16[32,3584]{1,0:T(8,128)(2,1)S(1)} %get-tuple-element.186), channel_id=1, source_target_pairs={{0,2},{1,3},{4,0},{5,1},{8,4},{9,5},{12,8},{13,9},{14,12},{15,13},... | collective-permute-start | bytes 688136 | tf_op jit(solution)/shard_map/ppermute | solution.py:279
  145.3 6.8 %collective-permute-start.27 = (bf16[32,3584]{1,0:T(8,128)(2,1)S(1)}, bf16[32,3584]{1,0:T(8,128)(2,1)S(1)}, u32[]{:S(2)}, u32[]{:S(2)}) collective-permute-start(bf16[32,3584]{1,0:T(8,128)(2,1)S(1)} %get-tuple-element.184), channel_id=1, source_target_pairs={{0,4},{1,5},{4,8},{5,9},{8,12},{9,13},{12,14},{13,15},{14,10},{15,... | collective-permute-start | bytes 688136 | tf_op jit(solution)/shard_map/ppermute | solution.py:279
  147.1 6.0 %collective-permute-start.31 = (bf16[32,3584]{1,0:T(8,128)(2,1)S(1)}, bf16[32,3584]{1,0:T(8,128)(2,1)S(1)}, u32[]{:S(2)}, u32[]{:S(2)}) collective-permute-start(bf16[32,3584]{1,0:T(8,128)(2,1)S(1)} %get-tuple-element.189), channel_id=1, source_target_pairs={{0,2},{1,3},{4,0},{5,1},{8,4},{9,5},{12,8},{13,9},{14,12},{15,13},... | collective-permute-start | bytes 688136 | tf_op jit(solution)/shard_map/ppermute | solution.py:279
  150.0 6.1 %collective-permute-start.30 = (bf16[32,3584]{1,0:T(8,128)(2,1)S(1)}, bf16[32,3584]{1,0:T(8,128)(2,1)S(1)}, u32[]{:S(2)}, u32[]{:S(2)}) collective-permute-start(bf16[32,3584]{1,0:T(8,128)(2,1)S(1)} %get-tuple-element.187), channel_id=1, source_target_pairs={{0,4},{1,5},{4,8},{5,9},{8,12},{9,13},{12,14},{13,15},{14,10},{15,... | collective-permute-start | bytes 688136 | tf_op jit(solution)/shard_map/ppermute | solution.py:279
  151.4 6.0 %collective-permute-start.32 = (bf16[32,3584]{1,0:T(8,128)(2,1)S(1)}, bf16[32,3584]{1,0:T(8,128)(2,1)S(1)}, u32[]{:S(2)}, u32[]{:S(2)}) collective-permute-start(bf16[32,3584]{1,0:T(8,128)(2,1)S(1)} %get-tuple-element.190), channel_id=1, source_target_pairs={{0,2},{1,3},{4,0},{5,1},{8,4},{9,5},{12,8},{13,9},{14,12},{15,13},... | collective-permute-start | bytes 688136 | tf_op jit(solution)/shard_map/ppermute | solution.py:279

commit v9 on v8

--- a/solution.py
+++ b/solution.py
@@ -13,6 +13,7 @@
 TILE = 256
 WIDE = 512
 MIB = 1 << 20
+AHEAD = 6 * MIB
 
 
 def expert_kernel(n, experts, dim, half, expert_ref, *refs):
@@ -91,13 +92,15 @@
     for i, (left_ref, right_ref) in enumerate(zip(refs[:n], refs[n : 2 * n])):
         for p in range(pieces):
             left = left_ref[first + p * size : first + (p + 1) * size, :]
-            outs[i * pieces + p][...] = left + right_ref[p * size : (p + 1) * size, :]
-
-
-def add(lefts, rights, after=(), pieces=1, first=0):
+            right = right_ref[p * size : (p + 1) * size, :]
+            out = outs[i * pieces + p]
+            out[...] = left.astype(out.dtype) + right.astype(out.dtype)
+
+
+def add(lefts, rights, after=(), pieces=1, first=0, dtype=None, cost=1024):
     n = len(lefts)
     rows, dim = rights[0].shape
-    shape = jax.ShapeDtypeStruct((rows // pieces, dim), rights[0].dtype)
+    shape = jax.ShapeDtypeStruct((rows // pieces, dim), dtype or rights[0].dtype)
     return pl.pallas_call(
         functools.partial(add_kernel, n, pieces, first),
         in_specs=[pl.BlockSpec(memory_space=pltpu.VMEM)] * (2 * n)
@@ -105,7 +108,7 @@
         out_specs=[pl.BlockSpec(memory_space=pltpu.VMEM)] * (n * pieces),
         out_shape=[shape] * (n * pieces),
         compiler_params=pltpu.CompilerParams(vmem_limit_bytes=6 * MIB),
-        cost_estimate=small_cost(),
+        cost_estimate=pl.CostEstimate(flops=1024, bytes_accessed=cost, transcendentals=0),
     )(*lefts, *rights, *after)
 
 
@@ -129,30 +132,27 @@
     )(*arrays)
 
 
-def close_kernel(halves, *refs):
-    out_ref, taken = refs[-1], 0
-    for h, pieces in enumerate(halves):
-        base_ref, whole_ref = refs[taken : taken + 2]
+def close_kernel(*refs):
+    out_ref, bases, pieces = refs[-1], refs[:2], refs[2:-1]
+    size = pieces[0].shape[0]
+    for h, base_ref in enumerate(bases):
         half = base_ref.shape[0]
-        size = half // pieces
-        for p in range(pieces):
+        for p in range(len(pieces) // 2):
             at = slice(p * size, (p + 1) * size)
-            total = base_ref[at, :].astype(jnp.float32) + whole_ref[at, :].astype(jnp.float32)
-            total = total + refs[taken + 2 + p][...].astype(jnp.float32)
+            total = base_ref[at, :] + pieces[2 * p + h][...].astype(jnp.float32)
             out_ref[h * half + p * size : h * half + (p + 1) * size, :] = total.astype(out_ref.dtype)
-        taken += 2 + pieces
-
-
-def close(halves):
-    half, dim = halves[0][0].shape
-    terms = [term for terms in halves for term in terms]
-    return pl.pallas_call(
-        functools.partial(close_kernel, [len(terms) - 2 for terms in halves]),
-        in_specs=[pl.BlockSpec(memory_space=pltpu.VMEM)] * len(terms),
+
+
+def close(bases, pieces):
+    terms = [term for piece in pieces for term in piece]
+    half, dim = bases[0].shape
+    return pl.pallas_call(
+        close_kernel,
+        in_specs=[pl.BlockSpec(memory_space=pltpu.VMEM)] * (len(terms) + 2),
         out_shape=jax.ShapeDtypeStruct((2 * half, dim), terms[0].dtype),
         compiler_params=pltpu.CompilerParams(vmem_limit_bytes=8 * MIB),
         cost_estimate=small_cost(),
-    )(*terms)
+    )(*bases, *terms)
 
 
 def rows_kernel(experts, top, tokens_ref, ids_ref, codes_ref, out_ref):
@@ -260,7 +260,7 @@
             send(s, h, done.pop(0))
             done.append(work([(1 - s, h), (s - 1, h)], [ahead[h][s - 1], behind[h][s - 1]]))
     last = done.pop()
-    firsts = [(1 - far, 0), (far - 1, 1)]
+    firsts = [(far - 1, 1)]
     held, ahead[0][far] = lax.optimization_barrier(
         ([parts[name] for name in firsts], ahead[0][far])
     )
@@ -268,43 +268,36 @@
     work([(far, 0), (far, 1)], [ahead[0][far], behind[1][far]], last)
     parts[-far, 1] = parts[far, 1]
 
-    streams = [(h, sign) for h in range(2) for sign in (1, -1)]
+    early = [(h, sign) for h in range(2) for sign in (1, -1) if (h == 0) != (sign == 1)]
+    late = [(h, -sign) for h, sign in early]
     ways = {1: forward, -1: backward}
-    early = [(h, sign) for h, sign in streams if (h == 0) != (sign == 1)]
-    late = [stream for stream in streams if stream not in early]
-    came = {}
 
     def pass_on(group, totals):
-        for (h, sign), total in zip(group, totals):
-            came[h, sign] = lax.ppermute(total, "node", ways[sign])
-
-    def summed(group, at, after=(), **how):
-        lefts = [parts[sign * at, h] for h, sign in group]
-        return add(lefts, [came[stream] for stream in group], after, **how)
-
-    pass_on(early, [parts[sign * (far - 1), h] for h, sign in early])
-    late_totals = [parts[sign * far, h] for h, sign in late]
-    held = [came[stream] for stream in early]
-    late_totals, held = lax.optimization_barrier((late_totals, held))
-    came.update(zip(early, held))
-    for at in range(far - 1, 1, -1):
-        pass_on(early, summed(early, at - 1))
-        pass_on(late, late_totals)
-        waited = [came[stream] for stream in early]
-        late_totals = summed(late, at, waited, pieces=2 if at == 2 else 1)
-
-    pieces = []
-    for p in range(2):
-        pass_on(late, late_totals[p::2])
-        pass_on(late, summed(late, 1, first=p * (half // 2)))
-        pieces.append([came[stream] for stream in late])
-    shorter = dict(early)
-    return close(
-        [
-            [parts[0, h], came[h, shorter[h]], *(piece[h] for piece in pieces)]
-            for h in range(2)
-        ]
-    )
+        return [lax.ppermute(t, "node", ways[sign]) for t, (h, sign) in zip(totals, group)]
+
+    def shares(group, offset):
+        return [parts[sign * offset, h] for h, sign in group]
+
+    first = pass_on(early, shares(early, far - 1))
+    last = [pass_on(late, shares(late, far))]
+    for k in range(2, far + 1):
+        if k < far:
+            first = pass_on(early, add(shares(early, far - k), first, cost=AHEAD))
+            after = []
+        else:
+            first = add(shares(early, 0), first, dtype=jnp.float32, cost=AHEAD)
+            after = first
+        terms = shares(late, far - k + 1)
+        if k == far - 1:
+            totals = add(terms, last[0], after, pieces=2)
+            last = [pass_on(late, totals[p::2]) for p in range(2)]
+        else:
+            size = half // len(last)
+            last = [
+                pass_on(late, add(terms, came, after, first=p * size))
+                for p, came in enumerate(last)
+            ]
+    return close(first, last)
 
 
 def solution(mesh):

time: 159 us -> 158 us (level)
  starting transfers between devices: 33.8 us -> 32.2 us
    ppermute x5, waiting for transfers between devices: 2.12 us -> 6.01 us  [send(): behind[h].append(lax.ppermute(behind[h][s - 1], 'node', backward))]
    ppermute x18, waiting for transfers between devices: 49.4 us -> 47.6 us  [pass_on(): lax.ppermute(t, 'node', ways[sign])]
  transfers between devices with their start and end apart: 33 -> 33, of which waited for: 24 -> 23; matrix products, arithmetic and copies ran while one was open for 0% -> 0% of each run, Pallas kernels for 24% -> 24%
where the time goes in v9:
time: 158 us
  waiting for transfers between devices  77.7 us (49%)
  Pallas kernels  39 us (25%)
  starting transfers between devices  32.2 us (20%)
  local copies, waits for them, and re-layouts  8.65 us (5%)
    ppermute x18, waiting for transfers between devices, pass_on(): lax.ppermute(t, 'node', ways[sign])  47.6 us
    pallas_call x6, Pallas kernels, expert_parts(): pl.pallas_call(functools.partial(expert_kernel, n, experts, dim, half), i...  36.2 us
    ppermute x18, starting transfers between devices, pass_on(): lax.ppermute(t, 'node', ways[sign])  17 us
    ppermute x1, waiting for transfers between devices, body(): lax.ppermute(rows, 'node', backward)  14.8 us
    unnamed x12, local copies, waits for them, and re-layouts  8.65 us
    ppermute x5, waiting for transfers between devices, send(): ahead[h].append(lax.ppermute(ahead[h][s - 1], 'node', forward))  7.87 us
    ppermute x5, starting transfers between devices, send(): behind[h].append(lax.ppermute(behind[h][s - 1], 'node', backward))  6.26 us
    ppermute x5, waiting for transfers between devices, send(): behind[h].append(lax.ppermute(behind[h][s - 1], 'node', backward))  6.01 us
  transfers between devices with their start and end apart: 33, of which 23 were waited for; matrix products, arithmetic and copies ran while one was open for 0% of the time, Pallas kernels for 24%

profile of v9, /device:TPU:0, one launch (start us, length us, event | category | flops | bytes accessed | tf_op | source)
XLA Modules:
  0.0 157.7 jit_solution(4893209060559524130)
XLA Ops:
  0.0 1.2 copy-done.3
  1.2 0.7 copy-done.4
  1.9 0.7 copy-done.5
  3.7 2.6 %collective-permute-start.1 = (bf16[128,3712]{1,0:T(8,128)(2,1)S(1)}, bf16[128,3712]{1,0:T(8,128)(2,1)S(1)}, u32[]{:S(2)}, u32[]{:S(2)}) collective-permute-start(bf16[128,3712]{1,0:T(8,128)(2,1)S(1)} %shard_map.64.refs_0_), channel_id=1, source_target_pairs={{0,2},{1,3},{4,0},{5,1},{8,4},{9,5},{12,8},{13,9},{14,12},{15,13},... | collective-permute-start | bytes 2850824 | tf_op jit(solution)/shard_map/ppermute | solution.py:227
  6.4 2.0 %copy-done = bf16[3584,512]{1,0:T(8,128)(2,1)S(1)} copy-done((bf16[3584,512]{1,0:T(8,128)(2,1)S(1)}, bf16[3584,512]{1,0:T(8,128)(2,1)}, u32[]{:S(2)}) %copy-start) | copy-done | bytes 3670040
  8.4 2.0 %copy-done.1 = bf16[3584,512]{1,0:T(8,128)(2,1)S(1)} copy-done((bf16[3584,512]{1,0:T(8,128)(2,1)S(1)}, bf16[3584,512]{1,0:T(8,128)(2,1)}, u32[]{:S(2)}) %copy-start.1) | copy-done | bytes 3670040
  10.5 2.0 %copy-done.2 = bf16[512,3584]{1,0:T(8,128)(2,1)S(1)} copy-done((bf16[512,3584]{1,0:T(8,128)(2,1)S(1)}, bf16[512,3584]{1,0:T(8,128)(2,1)}, u32[]{:S(2)}) %copy-start.2) | copy-done | bytes 3670040
  12.5 0.8 shard_map.65
  13.3 14.8 %collective-permute-done.1.refs_1_.refs_2_ = bf16[128,3712]{1,0:T(8,128)(2,1)S(1)} collective-permute-done((bf16[128,3712]{1,0:T(8,128)(2,1)S(1)}, bf16[128,3712]{1,0:T(8,128)(2,1)S(1)}, u32[]{:S(2)}, u32[]{:S(2)}) %collective-permute-start.1) | collective-permute-done | bytes 950304 | tf_op jit(solution)/shard_map/ppermute | solution.py:227
  28.0 1.4 collective-permute-done.refs_0_.refs_1_
  30.0 1.7 %collective-permute-start.3 = (bf16[64,3712]{1,0:T(8,128)(2,1)S(1)}, bf16[64,3712]{1,0:T(8,128)(2,1)S(1)}, u32[]{:S(2)}, u32[]{:S(2)}) collective-permute-start(bf16[64,3712]{1,0:T(8,128)(2,1)S(1)} %get-tuple-element.107), channel_id=1, source_target_pairs={{0,2},{1,3},{4,0},{5,1},{8,4},{9,5},{12,8},{13,9},{14,12},{15,13},... | collective-permute-start | bytes 1425416 | tf_op jit(solution)/shard_map/ppermute | solution.py:252
  32.0 1.7 %collective-permute-start.8 = (bf16[64,3712]{1,0:T(8,128)(2,1)S(1)}, bf16[64,3712]{1,0:T(8,128)(2,1)S(1)}, u32[]{:S(2)}, u32[]{:S(2)}) collective-permute-start(bf16[64,3712]{1,0:T(8,128)(2,1)S(1)} %get-tuple-element.128), channel_id=1, source_target_pairs={{0,2},{1,3},{4,0},{5,1},{8,4},{9,5},{12,8},{13,9},{14,12},{15,13},... | collective-permute-start | bytes 1425416 | tf_op jit(solution)/shard_map/ppermute | solution.py:252
  33.7 10.8 %shard_map.67 = (bf16[64,3584]{1,0:T(8,128)(2,1)S(1)}, bf16[64,3584]{1,0:T(8,128)(2,1)S(1)}, bf16[64,3584]{1,0:T(8,128)(2,1)S(1)}, bf16[64,3584]{1,0:T(8,128)(2,...) custom-call(s32[1]{0:T(128)} %bitcast.expert_ref, bf16[128,3712]{1,0:T(8,128)(2,1)S(1)} %shard_map.64.refs_0_, ...), custom_call_target="tpu_custom_call" | custom-call | flops 1024 | bytes 1024 | tf_op jit(solution)/shard_map/pallas_call | solution.py:74
  44.5 1.0 collective-permute-start.9
  45.5 1.0 collective-permute-start.10
  46.5 5.1 %shard_map.68 = (bf16[64,3584]{1,0:T(8,128)(2,1)S(1)}, bf16[64,3584]{1,0:T(8,128)(2,1)S(1)}) custom-call(s32[1]{0:T(128)} %bitcast.expert_ref, bf16[64,3712]{1,0:T(8,128)(2,1)S(1)} %collective-permute-done.2.refs_0_, bf16[64,3712]{1,0:T(8,128)(2,1)S(1)} %collective-permute-done.3.refs_1_, bf16[3584,512]{1,0:T(8,128)(2,1)S(1)} %get-tuple-element.112.refs_3_.refs_2_, ...), custom_call_target="tpu_custom_call" | custom-call | flops 1024 | bytes 1024 | tf_op jit(solution)/shard_map/pallas_call | solution.py:74
  51.7 1.9 %collective-permute-done.7.refs_0_ = bf16[64,3712]{1,0:T(8,128)(2,1)S(1)} collective-permute-done((bf16[64,3712]{1,0:T(8,128)(2,1)S(1)}, bf16[64,3712]{1,0:T(8,128)(2,1)S(1)}, u32[]{:S(2)}, u32[]{:S(2)}) %collective-permute-start.7) | collective-permute-done | bytes 475168 | tf_op jit(solution)/shard_map/ppermute | solution.py:250
  53.9 1.7 %collective-permute-start.11 = (bf16[64,3712]{1,0:T(8,128)(2,1)S(1)}, bf16[64,3712]{1,0:T(8,128)(2,1)S(1)}, u32[]{:S(2)}, u32[]{:S(2)}) collective-permute-start(bf16[64,3712]{1,0:T(8,128)(2,1)S(1)} %collective-permute-done.7.refs_0_), channel_id=1, source_target_pairs={{0,4},{1,5},{4,8},{5,9},{8,12},{9,13},{12,14},{13,15},{14,10},{15,... | collective-permute-start | bytes 1425416 | tf_op jit(solution)/shard_map/ppermute | solution.py:250
  56.0 5.1 %shard_map.69 = (bf16[64,3584]{1,0:T(8,128)(2,1)S(1)}, bf16[64,3584]{1,0:T(8,128)(2,1)S(1)}) custom-call(s32[1]{0:T(128)} %bitcast.expert_ref, bf16[64,3712]{1,0:T(8,128)(2,1)S(1)} %collective-permute-done.7.refs_0_, bf16[64,3712]{1,0:T(8,128)(2,1)S(1)} %collective-permute-done.8.refs_1_, bf16[3584,512]{1,0:T(8,128)(2,1)S(1)} %get-tuple-element.112.refs_3_.refs_2_, ...), custom_call_target="tpu_custom_call" | custom-call | flops 1024 | bytes 1024 | tf_op jit(solution)/shard_map/pallas_call | solution.py:74
  61.1 2.7 %collective-permute-done.9.refs_0_ = bf16[64,3712]{1,0:T(8,128)(2,1)S(1)} collective-permute-done((bf16[64,3712]{1,0:T(8,128)(2,1)S(1)}, bf16[64,3712]{1,0:T(8,128)(2,1)S(1)}, u32[]{:S(2)}, u32[]{:S(2)}) %collective-permute-start.9) | collective-permute-done | bytes 475168 | tf_op jit(solution)/shard_map/ppermute | solution.py:250
  64.1 1.7 %collective-permute-start.14 = (bf16[64,3712]{1,0:T(8,128)(2,1)S(1)}, bf16[64,3712]{1,0:T(8,128)(2,1)S(1)}, u32[]{:S(2)}, u32[]{:S(2)}) collective-permute-start(bf16[64,3712]{1,0:T(8,128)(2,1)S(1)} %collective-permute-done.9.refs_0_), channel_id=1, source_target_pairs={{0,4},{1,5},{4,8},{5,9},{8,12},{9,13},{12,14},{13,15},{14,10},{15,... | collective-permute-start | bytes 1425416 | tf_op jit(solution)/shard_map/ppermute | solution.py:250
  65.9 5.1 %shard_map.70 = (bf16[64,3584]{1,0:T(8,128)(2,1)S(1)}, bf16[64,3584]{1,0:T(8,128)(2,1)S(1)}) custom-call(s32[1]{0:T(128)} %bitcast.expert_ref, bf16[64,3712]{1,0:T(8,128)(2,1)S(1)} %collective-permute-done.9.refs_0_, bf16[64,3712]{1,0:T(8,128)(2,1)S(1)} %collective-permute-done.10.refs_1_, bf16[3584,512]{1,0:T(8,128)(2,1)S(1)} %get-tuple-element.112.refs_3_.refs_2_, ...), custom_call_target="tpu_custom_call" | custom-call | flops 1024 | bytes 1024 | tf_op jit(solution)/shard_map/pallas_call | solution.py:74
  71.0 3.0 %collective-permute-done.11.refs_0_ = bf16[64,3712]{1,0:T(8,128)(2,1)S(1)} collective-permute-done((bf16[64,3712]{1,0:T(8,128)(2,1)S(1)}, bf16[64,3712]{1,0:T(8,128)(2,1)S(1)}, u32[]{:S(2)}, u32[]{:S(2)}) %collective-permute-start.11) | collective-permute-done | bytes 475168 | tf_op jit(solution)/shard_map/ppermute | solution.py:250
  74.0 1.6 %collective-permute-start.15 = (bf16[64,3712]{1,0:T(8,128)(2,1)S(1)}, bf16[64,3712]{1,0:T(8,128)(2,1)S(1)}, u32[]{:S(2)}, u32[]{:S(2)}) collective-permute-start(bf16[64,3712]{1,0:T(8,128)(2,1)S(1)} %collective-permute-done.12.refs_1_), channel_id=1, source_target_pairs={{0,2},{1,3},{4,0},{5,1},{8,4},{9,5},{12,8},{13,9},{14,12},{15,13},... | collective-permute-start | bytes 1425416 | tf_op jit(solution)/shard_map/ppermute | solution.py:252
  75.5 1.6 collective-permute-start.13
  77.1 5.1 %shard_map.71 = (bf16[64,3584]{1,0:T(8,128)(2,1)S(1)}, bf16[64,3584]{1,0:T(8,128)(2,1)S(1)}) custom-call(s32[1]{0:T(128)} %bitcast.expert_ref, bf16[64,3712]{1,0:T(8,128)(2,1)S(1)} %collective-permute-done.11.refs_0_, bf16[64,3712]{1,0:T(8,128)(2,1)S(1)} %collective-permute-done.12.refs_1_, bf16[3584,512]{1,0:T(8,128)(2,1)S(1)} %get-tuple-element.112.refs_3_.refs_2_, ...), custom_call_target="tpu_custom_call" | custom-call | flops 1024 | bytes 1024 | tf_op jit(solution)/shard_map/pallas_call | solution.py:74
  82.5 5.3 %collective-permute-done.15.refs_1_ = bf16[64,3712]{1,0:T(8,128)(2,1)S(1)} collective-permute-done((bf16[64,3712]{1,0:T(8,128)(2,1)S(1)}, bf16[64,3712]{1,0:T(8,128)(2,1)S(1)}, u32[]{:S(2)}, u32[]{:S(2)}) %collective-permute-start.15) | collective-permute-done | bytes 475168 | tf_op jit(solution)/shard_map/ppermute | solution.py:252
  88.1 5.1 %shard_map.75 = (bf16[64,3584]{1,0:T(8,128)(2,1)S(1)}, bf16[64,3584]{1,0:T(8,128)(2,1)S(1)}) custom-call(s32[1]{0:T(128)} %bitcast.expert_ref, bf16[64,3712]{1,0:T(8,128)(2,1)S(1)} %collective-permute-done.14.refs_0_, bf16[64,3712]{1,0:T(8,128)(2,1)S(1)} %collective-permute-done.15.refs_1_, bf16[3584,512]{1,0:T(8,128)(2,1)S(1)} %get-tuple-element.112.refs_3_.refs_2_, ...), custom_call_target="tpu_custom_call" | custom-call | flops 1024 | bytes 1024 | tf_op jit(solution)/shard_map/pallas_call | solution.py:74
  93.2 1.8 %collective-permute-start.21 = (bf16[64,3584]{1,0:T(8,128)(2,1)S(1)}, bf16[64,3584]{1,0:T(8,128)(2,1)S(1)}, u32[]{:S(2)}, u32[]{:S(2)}) collective-permute-start(bf16[64,3584]{1,0:T(8,128)(2,1)S(1)} %get-tuple-element.173), channel_id=1, source_target_pairs={{0,4},{1,5},{4,8},{5,9},{8,12},{9,13},{12,14},{13,15},{14,10},{15,... | collective-permute-start | bytes 1376264 | tf_op jit(solution)/shard_map/ppermute | solution.py:276
  95.3 0.9 collective-permute-done.13.refs_2_
  96.2 5.0 %collective-permute-done.16.refs_3_ = bf16[64,3584]{1,0:T(8,128)(2,1)S(1)} collective-permute-done((bf16[64,3584]{1,0:T(8,128)(2,1)S(1)}, bf16[64,3584]{1,0:T(8,128)(2,1)S(1)}, u32[]{:S(2)}, u32[]{:S(2)}) %collective-permute-start.16) | collective-permute-done | bytes 458784 | tf_op jit(solution)/shard_map/ppermute | solution.py:276
  101.3 1.7 %collective-permute-start.17 = (bf16[64,3584]{1,0:T(8,128)(2,1)S(1)}, bf16[64,3584]{1,0:T(8,128)(2,1)S(1)}, u32[]{:S(2)}, u32[]{:S(2)}) collective-permute-start(bf16[64,3584]{1,0:T(8,128)(2,1)S(1)} %get-tuple-element.159), channel_id=1, source_target_pairs={{0,2},{1,3},{4,0},{5,1},{8,4},{9,5},{12,8},{13,9},{14,12},{15,13},... | collective-permute-start | bytes 1376264 | tf_op jit(solution)/shard_map/ppermute | solution.py:276
  103.4 7.7 %collective-permute-done.21.refs_2_ = bf16[64,3584]{1,0:T(8,128)(2,1)S(1)} collective-permute-done((bf16[64,3584]{1,0:T(8,128)(2,1)S(1)}, bf16[64,3584]{1,0:T(8,128)(2,1)S(1)}, u32[]{:S(2)}, u32[]{:S(2)}) %collective-permute-start.21) | collective-permute-done | bytes 458784 | tf_op jit(solution)/shard_map/ppermute | solution.py:276
  111.5 1.7 %collective-permute-start.24 = (bf16[64,3584]{1,0:T(8,128)(2,1)S(1)}, bf16[64,3584]{1,0:T(8,128)(2,1)S(1)}, u32[]{:S(2)}, u32[]{:S(2)}) collective-permute-start(bf16[64,3584]{1,0:T(8,128)(2,1)S(1)} %get-tuple-element.176), channel_id=1, source_target_pairs={{0,2},{1,3},{4,0},{5,1},{8,4},{9,5},{12,8},{13,9},{14,12},{15,13},... | collective-permute-start | bytes 1376264 | tf_op jit(solution)/shard_map/ppermute | solution.py:276
  113.2 5.1 %collective-permute-done.17.refs_2_ = bf16[64,3584]{1,0:T(8,128)(2,1)S(1)} collective-permute-done((bf16[64,3584]{1,0:T(8,128)(2,1)S(1)}, bf16[64,3584]{1,0:T(8,128)(2,1)S(1)}, u32[]{:S(2)}, u32[]{:S(2)}) %collective-permute-start.17) | collective-permute-done | bytes 458784 | tf_op jit(solution)/shard_map/ppermute | solution.py:276
  118.3 2.6 %collective-permute-done.18.refs_3_ = bf16[64,3584]{1,0:T(8,128)(2,1)S(1)} collective-permute-done((bf16[64,3584]{1,0:T(8,128)(2,1)S(1)}, bf16[64,3584]{1,0:T(8,128)(2,1)S(1)}, u32[]{:S(2)}, u32[]{:S(2)}) %collective-permute-start.18) | collective-permute-done | bytes 458784 | tf_op jit(solution)/shard_map/ppermute | solution.py:276
  121.0 1.7 %collective-permute-start.19 = (bf16[64,3584]{1,0:T(8,128)(2,1)S(1)}, bf16[64,3584]{1,0:T(8,128)(2,1)S(1)}, u32[]{:S(2)}, u32[]{:S(2)}) collective-permute-start(bf16[64,3584]{1,0:T(8,128)(2,1)S(1)} %get-tuple-element.161), channel_id=1, source_target_pairs={{0,2},{1,3},{4,0},{5,1},{8,4},{9,5},{12,8},{13,9},{14,12},{15,13},... | collective-permute-start | bytes 1376264 | tf_op jit(solution)/shard_map/ppermute | solution.py:276
  123.0 7.7 %collective-permute-done.23.refs_2_ = bf16[64,3584]{1,0:T(8,128)(2,1)S(1)} collective-permute-done((bf16[64,3584]{1,0:T(8,128)(2,1)S(1)}, bf16[64,3584]{1,0:T(8,128)(2,1)S(1)}, u32[]{:S(2)}, u32[]{:S(2)}) %collective-permute-start.23) | collective-permute-done | bytes 458784 | tf_op jit(solution)/shard_map/ppermute | solution.py:276
  131.1 1.7 %collective-permute-start.26 = (bf16[32,3584]{1,0:T(8,128)(2,1)S(1)}, bf16[32,3584]{1,0:T(8,128)(2,1)S(1)}, u32[]{:S(2)}, u32[]{:S(2)}) collective-permute-start(bf16[32,3584]{1,0:T(8,128)(2,1)S(1)} %get-tuple-element.178), channel_id=1, source_target_pairs={{0,2},{1,3},{4,0},{5,1},{8,4},{9,5},{12,8},{13,9},{14,12},{15,13},... | collective-permute-start | bytes 688136 | tf_op jit(solution)/shard_map/ppermute | solution.py:276
  133.2 4.8 %collective-permute-done.19.refs_2_ = bf16[64,3584]{1,0:T(8,128)(2,1)S(1)} collective-permute-done((bf16[64,3584]{1,0:T(8,128)(2,1)S(1)}, bf16[64,3584]{1,0:T(8,128)(2,1)S(1)}, u32[]{:S(2)}, u32[]{:S(2)}) %collective-permute-start.19) | collective-permute-done | bytes 458784 | tf_op jit(solution)/shard_map/ppermute | solution.py:276
  138.2 2.3 %collective-permute-done.20.refs_3_ = bf16[64,3584]{1,0:T(8,128)(2,1)S(1)} collective-permute-done((bf16[64,3584]{1,0:T(8,128)(2,1)S(1)}, bf16[64,3584]{1,0:T(8,128)(2,1)S(1)}, u32[]{:S(2)}, u32[]{:S(2)}) %collective-permute-start.20) | collective-permute-done | bytes 458784 | tf_op jit(solution)/shard_map/ppermute | solution.py:276
  140.7 4.7 %collective-permute-done.25.refs_2_ = bf16[32,3584]{1,0:T(8,128)(2,1)S(1)} collective-permute-done((bf16[32,3584]{1,0:T(8,128)(2,1)S(1)}, bf16[32,3584]{1,0:T(8,128)(2,1)S(1)}, u32[]{:S(2)}, u32[]{:S(2)}) %collective-permute-start.25) | collective-permute-done | bytes 229408 | tf_op jit(solution)/shard_map/ppermute | solution.py:276
  145.8 1.7 %collective-permute-start.28 = (bf16[32,3584]{1,0:T(8,128)(2,1)S(1)}, bf16[32,3584]{1,0:T(8,128)(2,1)S(1)}, u32[]{:S(2)}, u32[]{:S(2)}) collective-permute-start(bf16[32,3584]{1,0:T(8,128)(2,1)S(1)} %get-tuple-element.180), channel_id=1, source_target_pairs={{0,2},{1,3},{4,0},{5,1},{8,4},{9,5},{12,8},{13,9},{14,12},{15,13},... | collective-permute-start | bytes 688136 | tf_op jit(solution)/shard_map/ppermute | solution.py:276
  147.6 1.5 collective-permute-done.29.refs_2_
  149.1 1.4 collective-permute-start.31
  151.9 3.3 %collective-permute-done.31.refs_4_ = bf16[32,3584]{1,0:T(8,128)(2,1)S(1)} collective-permute-done((bf16[32,3584]{1,0:T(8,128)(2,1)S(1)}, bf16[32,3584]{1,0:T(8,128)(2,1)S(1)}, u32[]{:S(2)}, u32[]{:S(2)}) %collective-permute-start.31) | collective-permute-done | bytes 229408 | tf_op jit(solution)/shard_map/ppermute | solution.py:276
  155.2 1.4 collective-permute-done.32.refs_5_
  156.6 1.1 shard_map.80
  (47 shorter events, 8.2 us)
Async XLA Ops:
  0.0 1.2 copy-start.3
  1.2 0.7 copy-start.4
  1.9 0.7 copy-start.5
  2.7 29.0 %collective-permute-start.4 = (bf16[3584,512]{1,0:T(8,128)(2,1)}, bf16[3584,512]{1,0:T(8,128)(2,1)S(1)}, u32[]{:S(2)}, u32[]{:S(2)}) collective-permute-start(bf16[3584,512]{1,0:T(8,128)(2,1)} %refs_0_), channel_id=1, source_target_pairs={{0,1},{1,0},{2,3},{3,2},{4,5},{5,4},{6,7},{7,6},{8,9},{9,8},{10,11... | collective-permute-start | bytes 11010056 | tf_op jit(solution)/shard_map/ppermute | solution.py:229
  3.2 28.8 %collective-permute-start.5 = (bf16[3584,512]{1,0:T(8,128)(2,1)}, bf16[3584,512]{1,0:T(8,128)(2,1)S(1)}, u32[]{:S(2)}, u32[]{:S(2)}) collective-permute-start(bf16[3584,512]{1,0:T(8,128)(2,1)} %refs_1_), channel_id=1, source_target_pairs={{0,1},{1,0},{2,3},{3,2},{4,5},{5,4},{6,7},{7,6},{8,9},{9,8},{10,11... | collective-permute-start | bytes 11010056 | tf_op jit(solution)/shard_map/ppermute | solution.py:229
  3.3 30.4 %collective-permute-start.6 = (bf16[512,3584]{1,0:T(8,128)(2,1)}, bf16[512,3584]{1,0:T(8,128)(2,1)S(1)}, u32[]{:S(2)}, u32[]{:S(2)}) collective-permute-start(bf16[512,3584]{1,0:T(8,128)(2,1)} %refs_2_), channel_id=1, source_target_pairs={{0,1},{1,0},{2,3},{3,2},{4,5},{5,4},{6,7},{7,6},{8,9},{9,8},{10,11... | collective-permute-start | bytes 11010056 | tf_op jit(solution)/shard_map/ppermute | solution.py:229
  3.7 24.3 %collective-permute-start.1 = (bf16[128,3712]{1,0:T(8,128)(2,1)S(1)}, bf16[128,3712]{1,0:T(8,128)(2,1)S(1)}, u32[]{:S(2)}, u32[]{:S(2)}) collective-permute-start(bf16[128,3712]{1,0:T(8,128)(2,1)S(1)} %shard_map.64.refs_0_), channel_id=1, source_target_pairs={{0,2},{1,3},{4,0},{5,1},{8,4},{9,5},{12,8},{13,9},{14,12},{15,13},... | collective-permute-start | bytes 2850824 | tf_op jit(solution)/shard_map/ppermute | solution.py:227
  6.3 23.1 %collective-permute-start = (bf16[128,3712]{1,0:T(8,128)(2,1)S(1)}, bf16[128,3712]{1,0:T(8,128)(2,1)S(1)}, u32[]{:S(2)}, u32[]{:S(2)}) collective-permute-start(bf16[128,3712]{1,0:T(8,128)(2,1)S(1)} %shard_map.64.refs_0_), channel_id=1, source_target_pairs={{0,4},{1,5},{4,8},{5,9},{8,12},{9,13},{12,14},{13,15},{14,10},{15,... | collective-permute-start | bytes 2850824 | tf_op jit(solution)/shard_map/ppermute | solution.py:227
  6.4 2.0 %copy-start = (bf16[3584,512]{1,0:T(8,128)(2,1)S(1)}, bf16[3584,512]{1,0:T(8,128)(2,1)}, u32[]{:S(2)}) copy-start(bf16[3584,512]{1,0:T(8,128)(2,1)} %refs_0_) | copy-start | bytes 11010052
  8.4 2.0 %copy-start.1 = (bf16[3584,512]{1,0:T(8,128)(2,1)S(1)}, bf16[3584,512]{1,0:T(8,128)(2,1)}, u32[]{:S(2)}) copy-start(bf16[3584,512]{1,0:T(8,128)(2,1)} %refs_1_) | copy-start | bytes 11010052
  10.4 2.0 %copy-start.2 = (bf16[512,3584]{1,0:T(8,128)(2,1)S(1)}, bf16[512,3584]{1,0:T(8,128)(2,1)}, u32[]{:S(2)}) copy-start(bf16[512,3584]{1,0:T(8,128)(2,1)} %refs_2_) | copy-start | bytes 11010052
  29.6 14.9 %collective-permute-start.2 = (bf16[64,3712]{1,0:T(8,128)(2,1)S(1)}, bf16[64,3712]{1,0:T(8,128)(2,1)S(1)}, u32[]{:S(2)}, u32[]{:S(2)}) collective-permute-start(bf16[64,3712]{1,0:T(8,128)(2,1)S(1)} %get-tuple-element.106), channel_id=1, source_target_pairs={{0,4},{1,5},{4,8},{5,9},{8,12},{9,13},{12,14},{13,15},{14,10},{15,... | collective-permute-start | bytes 1425416 | tf_op jit(solution)/shard_map/ppermute | solution.py:250
  30.0 14.5 %collective-permute-start.3 = (bf16[64,3712]{1,0:T(8,128)(2,1)S(1)}, bf16[64,3712]{1,0:T(8,128)(2,1)S(1)}, u32[]{:S(2)}, u32[]{:S(2)}) collective-permute-start(bf16[64,3712]{1,0:T(8,128)(2,1)S(1)} %get-tuple-element.107), channel_id=1, source_target_pairs={{0,2},{1,3},{4,0},{5,1},{8,4},{9,5},{12,8},{13,9},{14,12},{15,13},... | collective-permute-start | bytes 1425416 | tf_op jit(solution)/shard_map/ppermute | solution.py:252
  31.6 22.0 %collective-permute-start.7 = (bf16[64,3712]{1,0:T(8,128)(2,1)S(1)}, bf16[64,3712]{1,0:T(8,128)(2,1)S(1)}, u32[]{:S(2)}, u32[]{:S(2)}) collective-permute-start(bf16[64,3712]{1,0:T(8,128)(2,1)S(1)} %get-tuple-element.127), channel_id=1, source_target_pairs={{0,4},{1,5},{4,8},{5,9},{8,12},{9,13},{12,14},{13,15},{14,10},{15,... | collective-permute-start | bytes 1425416 | tf_op jit(solution)/shard_map/ppermute | solution.py:250
  32.0 22.0 %collective-permute-start.8 = (bf16[64,3712]{1,0:T(8,128)(2,1)S(1)}, bf16[64,3712]{1,0:T(8,128)(2,1)S(1)}, u32[]{:S(2)}, u32[]{:S(2)}) collective-permute-start(bf16[64,3712]{1,0:T(8,128)(2,1)S(1)} %get-tuple-element.128), channel_id=1, source_target_pairs={{0,2},{1,3},{4,0},{5,1},{8,4},{9,5},{12,8},{13,9},{14,12},{15,13},... | collective-permute-start | bytes 1425416 | tf_op jit(solution)/shard_map/ppermute | solution.py:252
  44.5 19.3 %collective-permute-start.9 = (bf16[64,3712]{1,0:T(8,128)(2,1)S(1)}, bf16[64,3712]{1,0:T(8,128)(2,1)S(1)}, u32[]{:S(2)}, u32[]{:S(2)}) collective-permute-start(bf16[64,3712]{1,0:T(8,128)(2,1)S(1)} %collective-permute-done.2.refs_0_), channel_id=1, source_target_pairs={{0,4},{1,5},{4,8},{5,9},{8,12},{9,13},{12,14},{13,15},{14,10},{15,... | collective-permute-start | bytes 1425416 | tf_op jit(solution)/shard_map/ppermute | solution.py:250
  45.5 18.6 %collective-permute-start.10 = (bf16[64,3712]{1,0:T(8,128)(2,1)S(1)}, bf16[64,3712]{1,0:T(8,128)(2,1)S(1)}, u32[]{:S(2)}, u32[]{:S(2)}) collective-permute-start(bf16[64,3712]{1,0:T(8,128)(2,1)S(1)} %collective-permute-done.3.refs_1_), channel_id=1, source_target_pairs={{0,2},{1,3},{4,0},{5,1},{8,4},{9,5},{12,8},{13,9},{14,12},{15,13},... | collective-permute-start | bytes 1425416 | tf_op jit(solution)/shard_map/ppermute | solution.py:252
  53.9 20.0 %collective-permute-start.11 = (bf16[64,3712]{1,0:T(8,128)(2,1)S(1)}, bf16[64,3712]{1,0:T(8,128)(2,1)S(1)}, u32[]{:S(2)}, u32[]{:S(2)}) collective-permute-start(bf16[64,3712]{1,0:T(8,128)(2,1)S(1)} %collective-permute-done.7.refs_0_), channel_id=1, source_target_pairs={{0,4},{1,5},{4,8},{5,9},{8,12},{9,13},{12,14},{13,15},{14,10},{15,... | collective-permute-start | bytes 1425416 | tf_op jit(solution)/shard_map/ppermute | solution.py:250
  55.7 18.3 %collective-permute-start.12 = (bf16[64,3712]{1,0:T(8,128)(2,1)S(1)}, bf16[64,3712]{1,0:T(8,128)(2,1)S(1)}, u32[]{:S(2)}, u32[]{:S(2)}) collective-permute-start(bf16[64,3712]{1,0:T(8,128)(2,1)S(1)} %collective-permute-done.8.refs_1_), channel_id=1, source_target_pairs={{0,2},{1,3},{4,0},{5,1},{8,4},{9,5},{12,8},{13,9},{14,12},{15,13},... | collective-permute-start | bytes 1425416 | tf_op jit(solution)/shard_map/ppermute | solution.py:252
  64.1 18.3 %collective-permute-start.14 = (bf16[64,3712]{1,0:T(8,128)(2,1)S(1)}, bf16[64,3712]{1,0:T(8,128)(2,1)S(1)}, u32[]{:S(2)}, u32[]{:S(2)}) collective-permute-start(bf16[64,3712]{1,0:T(8,128)(2,1)S(1)} %collective-permute-done.9.refs_0_), channel_id=1, source_target_pairs={{0,4},{1,5},{4,8},{5,9},{8,12},{9,13},{12,14},{13,15},{14,10},{15,... | collective-permute-start | bytes 1425416 | tf_op jit(solution)/shard_map/ppermute | solution.py:250
  74.0 13.8 %collective-permute-start.15 = (bf16[64,3712]{1,0:T(8,128)(2,1)S(1)}, bf16[64,3712]{1,0:T(8,128)(2,1)S(1)}, u32[]{:S(2)}, u32[]{:S(2)}) collective-permute-start(bf16[64,3712]{1,0:T(8,128)(2,1)S(1)} %collective-permute-done.12.refs_1_), channel_id=1, source_target_pairs={{0,2},{1,3},{4,0},{5,1},{8,4},{9,5},{12,8},{13,9},{14,12},{15,13},... | collective-permute-start | bytes 1425416 | tf_op jit(solution)/shard_map/ppermute | solution.py:252
  75.5 20.6 %collective-permute-start.13 = (bf16[64,3584]{1,0:T(8,128)(2,1)S(1)}, bf16[64,3584]{1,0:T(8,128)(2,1)S(1)}, u32[]{:S(2)}, u32[]{:S(2)}) collective-permute-start(bf16[64,3584]{1,0:T(8,128)(2,1)S(1)} %get-tuple-element.149), channel_id=1, source_target_pairs={{0,2},{1,3},{4,0},{5,1},{8,4},{9,5},{12,8},{13,9},{14,12},{15,13},... | collective-permute-start | bytes 1376264 | tf_op jit(solution)/shard_map/ppermute | solution.py:276
  87.8 13.4 %collective-permute-start.16 = (bf16[64,3584]{1,0:T(8,128)(2,1)S(1)}, bf16[64,3584]{1,0:T(8,128)(2,1)S(1)}, u32[]{:S(2)}, u32[]{:S(2)}) collective-permute-start(bf16[64,3584]{1,0:T(8,128)(2,1)S(1)} %get-tuple-element.158), channel_id=1, source_target_pairs={{0,4},{1,5},{4,8},{5,9},{8,12},{9,13},{12,14},{13,15},{14,10},{15,... | collective-permute-start | bytes 1376264 | tf_op jit(solution)/shard_map/ppermute | solution.py:276
  93.2 17.8 %collective-permute-start.21 = (bf16[64,3584]{1,0:T(8,128)(2,1)S(1)}, bf16[64,3584]{1,0:T(8,128)(2,1)S(1)}, u32[]{:S(2)}, u32[]{:S(2)}) collective-permute-start(bf16[64,3584]{1,0:T(8,128)(2,1)S(1)} %get-tuple-element.173), channel_id=1, source_target_pairs={{0,4},{1,5},{4,8},{5,9},{8,12},{9,13},{12,14},{13,15},{14,10},{15,... | collective-permute-start | bytes 1376264 | tf_op jit(solution)/shard_map/ppermute | solution.py:276
  95.0 16.0 %collective-permute-start.22 = (bf16[64,3584]{1,0:T(8,128)(2,1)S(1)}, bf16[64,3584]{1,0:T(8,128)(2,1)S(1)}, u32[]{:S(2)}, u32[]{:S(2)}) collective-permute-start(bf16[64,3584]{1,0:T(8,128)(2,1)S(1)} %get-tuple-element.174), channel_id=1, source_target_pairs={{0,2},{1,3},{4,0},{5,1},{8,4},{9,5},{12,8},{13,9},{14,12},{15,13},... | collective-permute-start | bytes 1376264 | tf_op jit(solution)/shard_map/ppermute | solution.py:276
  101.3 17.0 %collective-permute-start.17 = (bf16[64,3584]{1,0:T(8,128)(2,1)S(1)}, bf16[64,3584]{1,0:T(8,128)(2,1)S(1)}, u32[]{:S(2)}, u32[]{:S(2)}) collective-permute-start(bf16[64,3584]{1,0:T(8,128)(2,1)S(1)} %get-tuple-element.159), channel_id=1, source_target_pairs={{0,2},{1,3},{4,0},{5,1},{8,4},{9,5},{12,8},{13,9},{14,12},{15,13},... | collective-permute-start | bytes 1376264 | tf_op jit(solution)/shard_map/ppermute | solution.py:276
  103.0 17.9 %collective-permute-start.18 = (bf16[64,3584]{1,0:T(8,128)(2,1)S(1)}, bf16[64,3584]{1,0:T(8,128)(2,1)S(1)}, u32[]{:S(2)}, u32[]{:S(2)}) collective-permute-start(bf16[64,3584]{1,0:T(8,128)(2,1)S(1)} %get-tuple-element.160), channel_id=1, source_target_pairs={{0,4},{1,5},{4,8},{5,9},{8,12},{9,13},{12,14},{13,15},{14,10},{15,... | collective-permute-start | bytes 1376264 | tf_op jit(solution)/shard_map/ppermute | solution.py:276
  111.1 19.6 %collective-permute-start.23 = (bf16[64,3584]{1,0:T(8,128)(2,1)S(1)}, bf16[64,3584]{1,0:T(8,128)(2,1)S(1)}, u32[]{:S(2)}, u32[]{:S(2)}) collective-permute-start(bf16[64,3584]{1,0:T(8,128)(2,1)S(1)} %get-tuple-element.175), channel_id=1, source_target_pairs={{0,4},{1,5},{4,8},{5,9},{8,12},{9,13},{12,14},{13,15},{14,10},{15,... | collective-permute-start | bytes 1376264 | tf_op jit(solution)/shard_map/ppermute | solution.py:276
  111.5 19.2 %collective-permute-start.24 = (bf16[64,3584]{1,0:T(8,128)(2,1)S(1)}, bf16[64,3584]{1,0:T(8,128)(2,1)S(1)}, u32[]{:S(2)}, u32[]{:S(2)}) collective-permute-start(bf16[64,3584]{1,0:T(8,128)(2,1)S(1)} %get-tuple-element.176), channel_id=1, source_target_pairs={{0,2},{1,3},{4,0},{5,1},{8,4},{9,5},{12,8},{13,9},{14,12},{15,13},... | collective-permute-start | bytes 1376264 | tf_op jit(solution)/shard_map/ppermute | solution.py:276
  121.0 17.0 %collective-permute-start.19 = (bf16[64,3584]{1,0:T(8,128)(2,1)S(1)}, bf16[64,3584]{1,0:T(8,128)(2,1)S(1)}, u32[]{:S(2)}, u32[]{:S(2)}) collective-permute-start(bf16[64,3584]{1,0:T(8,128)(2,1)S(1)} %get-tuple-element.161), channel_id=1, source_target_pairs={{0,2},{1,3},{4,0},{5,1},{8,4},{9,5},{12,8},{13,9},{14,12},{15,13},... | collective-permute-start | bytes 1376264 | tf_op jit(solution)/shard_map/ppermute | solution.py:276
  122.6 17.9 %collective-permute-start.20 = (bf16[64,3584]{1,0:T(8,128)(2,1)S(1)}, bf16[64,3584]{1,0:T(8,128)(2,1)S(1)}, u32[]{:S(2)}, u32[]{:S(2)}) collective-permute-start(bf16[64,3584]{1,0:T(8,128)(2,1)S(1)} %get-tuple-element.162), channel_id=1, source_target_pairs={{0,4},{1,5},{4,8},{5,9},{8,12},{9,13},{12,14},{13,15},{14,10},{15,... | collective-permute-start | bytes 1376264 | tf_op jit(solution)/shard_map/ppermute | solution.py:276
  130.8 14.6 %collective-permute-start.25 = (bf16[32,3584]{1,0:T(8,128)(2,1)S(1)}, bf16[32,3584]{1,0:T(8,128)(2,1)S(1)}, u32[]{:S(2)}, u32[]{:S(2)}) collective-permute-start(bf16[32,3584]{1,0:T(8,128)(2,1)S(1)} %get-tuple-element.177), channel_id=1, source_target_pairs={{0,4},{1,5},{4,8},{5,9},{8,12},{9,13},{12,14},{13,15},{14,10},{15,... | collective-permute-start | bytes 688136 | tf_op jit(solution)/shard_map/ppermute | solution.py:276
  131.1 14.3 %collective-permute-start.26 = (bf16[32,3584]{1,0:T(8,128)(2,1)S(1)}, bf16[32,3584]{1,0:T(8,128)(2,1)S(1)}, u32[]{:S(2)}, u32[]{:S(2)}) collective-permute-start(bf16[32,3584]{1,0:T(8,128)(2,1)S(1)} %get-tuple-element.178), channel_id=1, source_target_pairs={{0,2},{1,3},{4,0},{5,1},{8,4},{9,5},{12,8},{13,9},{14,12},{15,13},... | collective-permute-start | bytes 688136 | tf_op jit(solution)/shard_map/ppermute | solution.py:276
  132.9 16.2 %collective-permute-start.29 = (bf16[32,3584]{1,0:T(8,128)(2,1)S(1)}, bf16[32,3584]{1,0:T(8,128)(2,1)S(1)}, u32[]{:S(2)}, u32[]{:S(2)}) collective-permute-start(bf16[32,3584]{1,0:T(8,128)(2,1)S(1)} %get-tuple-element.181), channel_id=1, source_target_pairs={{0,4},{1,5},{4,8},{5,9},{8,12},{9,13},{12,14},{13,15},{14,10},{15,... | collective-permute-start | bytes 688136 | tf_op jit(solution)/shard_map/ppermute | solution.py:276
  138.0 11.1 %collective-permute-start.30 = (bf16[32,3584]{1,0:T(8,128)(2,1)S(1)}, bf16[32,3584]{1,0:T(8,128)(2,1)S(1)}, u32[]{:S(2)}, u32[]{:S(2)}) collective-permute-start(bf16[32,3584]{1,0:T(8,128)(2,1)S(1)} %get-tuple-element.182), channel_id=1, source_target_pairs={{0,2},{1,3},{4,0},{5,1},{8,4},{9,5},{12,8},{13,9},{14,12},{15,13},... | collective-permute-start | bytes 688136 | tf_op jit(solution)/shard_map/ppermute | solution.py:276
  145.5 6.1 %collective-permute-start.27 = (bf16[32,3584]{1,0:T(8,128)(2,1)S(1)}, bf16[32,3584]{1,0:T(8,128)(2,1)S(1)}, u32[]{:S(2)}, u32[]{:S(2)}) collective-permute-start(bf16[32,3584]{1,0:T(8,128)(2,1)S(1)} %get-tuple-element.179), channel_id=1, source_target_pairs={{0,4},{1,5},{4,8},{5,9},{8,12},{9,13},{12,14},{13,15},{14,10},{15,... | collective-permute-start | bytes 688136 | tf_op jit(solution)/shard_map/ppermute | solution.py:276
  145.8 6.0 %collective-permute-start.28 = (bf16[32,3584]{1,0:T(8,128)(2,1)S(1)}, bf16[32,3584]{1,0:T(8,128)(2,1)S(1)}, u32[]{:S(2)}, u32[]{:S(2)}) collective-permute-start(bf16[32,3584]{1,0:T(8,128)(2,1)S(1)} %get-tuple-element.180), channel_id=1, source_target_pairs={{0,2},{1,3},{4,0},{5,1},{8,4},{9,5},{12,8},{13,9},{14,12},{15,13},... | collective-permute-start | bytes 688136 | tf_op jit(solution)/shard_map/ppermute | solution.py:276
  149.1 6.1 %collective-permute-start.31 = (bf16[32,3584]{1,0:T(8,128)(2,1)S(1)}, bf16[32,3584]{1,0:T(8,128)(2,1)S(1)}, u32[]{:S(2)}, u32[]{:S(2)}) collective-permute-start(bf16[32,3584]{1,0:T(8,128)(2,1)S(1)} %get-tuple-element.183), channel_id=1, source_target_pairs={{0,4},{1,5},{4,8},{5,9},{8,12},{9,13},{12,14},{13,15},{14,10},{15,... | collective-permute-start | bytes 688136 | tf_op jit(solution)/shard_map/ppermute | solution.py:276
  150.6 6.0 %collective-permute-start.32 = (bf16[32,3584]{1,0:T(8,128)(2,1)S(1)}, bf16[32,3584]{1,0:T(8,128)(2,1)S(1)}, u32[]{:S(2)}, u32[]{:S(2)}) collective-permute-start(bf16[32,3584]{1,0:T(8,128)(2,1)S(1)} %get-tuple-element.184), channel_id=1, source_target_pairs={{0,2},{1,3},{4,0},{5,1},{8,4},{9,5},{12,8},{13,9},{14,12},{15,13},... | collective-permute-start | bytes 688136 | tf_op jit(solution)/shard_map/ppermute | solution.py:276

commit v10 on v9

--- a/solution.py
+++ b/solution.py
@@ -66,7 +66,7 @@
     return pl.CostEstimate(flops=1024, bytes_accessed=1024, transcendentals=0)
 
 
-def expert_parts(experts, half, expert, blocks, own, other):
+def expert_parts(experts, half, expert, blocks, own, other, cost=1024):
     dim, hid = own[0].shape
     n, rows = len(blocks), sum(block.shape[0] for block in blocks)
     specs = [pl.BlockSpec(memory_space=pltpu.SMEM)]
@@ -82,7 +82,7 @@
             pltpu.VMEM((rows, SPAN * hid), jnp.bfloat16),
         ],
         compiler_params=pltpu.CompilerParams(vmem_limit_bytes=8 * MIB),
-        cost_estimate=small_cost(),
+        cost_estimate=pl.CostEstimate(flops=1024, bytes_accessed=cost, transcendentals=0),
     )(expert, *blocks, *own, *other)
 
 
@@ -231,42 +231,45 @@
 
     near, own = lax.optimization_barrier((near, own))
     halves = split(near)
-    ahead, behind = ([None, halves[0]], [None, halves[1]]), ([None, halves[2]], [None, halves[3]])
+    ahead = [[None, halves[0]], [None, halves[1]]]
+    behind = [[None, halves[3]], [None, halves[2]]]
     parts = {}
 
-    def work(names, blocks, after=()):
+    def work(names, blocks, after=(), **how):
         held = [parts[name] for name in after]
         blocks, held = lax.optimization_barrier((blocks, held))
         parts.update(zip(after, held))
-        parts.update(zip(names, expert_parts(ring, half, expert, blocks, own, other)))
+        parts.update(zip(names, expert_parts(ring, half, expert, blocks, own, other, **how)))
         return names
 
-    def send(s, h, after):
+    def send(s, wave, after):
         held = [parts[name] for name in after]
-        pair, held = lax.optimization_barrier(([ahead[h][s - 1], behind[h][s - 1]], held))
+        pair, held = lax.optimization_barrier(((ahead[wave][-1], behind[wave][-1]), held))
         parts.update(zip(after, held))
-        ahead[h][s - 1], behind[h][s - 1] = pair
-        if s < far or h == 0:
-            ahead[h].append(lax.ppermute(ahead[h][s - 1], "node", forward))
-        if s < far or h == 1:
-            behind[h].append(lax.ppermute(behind[h][s - 1], "node", backward))
-
-    for h in range(2):
-        send(2, h, [])
+        ahead[wave][-1], behind[wave][-1] = pair
+        ahead[wave].append(lax.ppermute(pair[0], "node", forward))
+        behind[wave].append(lax.ppermute(pair[1], "node", backward))
+
+    for wave in range(2):
+        send(2, wave, [])
     names = [(offset, h) for offset in (0, -1, 1) for h in range(2)]
     done = [work(names, [rows, *near])]
     for s in range(3, far + 1):
-        for h in range(2):
-            send(s, h, done.pop(0))
-            done.append(work([(1 - s, h), (s - 1, h)], [ahead[h][s - 1], behind[h][s - 1]]))
-    last = done.pop()
-    firsts = [(far - 1, 1)]
-    held, ahead[0][far] = lax.optimization_barrier(
-        ([parts[name] for name in firsts], ahead[0][far])
+        for wave in range(2):
+            if s < far or wave == 0:
+                send(s, wave, done.pop(0))
+            names = [(1 - s, wave), (s - 1, 1 - wave)]
+            after = done[-1] if s == far and wave == 1 else []
+            done.append(work(names, [ahead[wave][s - 1], behind[wave][s - 1]], after))
+    work([(far, 0), (far, 1)], [ahead[0][far], behind[0][far]], done[-1])
+    parts[-far, 1] = parts[far, 1]
+
+    firsts = [(1 - far, 0), (far - 1, 1)]
+    held, after = lax.optimization_barrier(
+        ([parts[name] for name in firsts], [parts[name] for name in done[-1]])
     )
     parts.update(zip(firsts, held))
-    work([(far, 0), (far, 1)], [ahead[0][far], behind[1][far]], last)
-    parts[-far, 1] = parts[far, 1]
+    parts.update(zip(done[-1], after))
 
     early = [(h, sign) for h in range(2) for sign in (1, -1) if (h == 0) != (sign == 1)]
     late = [(h, -sign) for h, sign in early]

time: 158 us -> 156 us (0.987)
  waiting for transfers between devices: 77.7 us -> 75.4 us
    ppermute x1, waiting for transfers between devices: 1.42 us -> 14.7 us  [body(): lax.ppermute(rows, 'node', forward)]
    ppermute x1, waiting for transfers between devices: 14.8 us -> 1.53 us  [body(): lax.ppermute(rows, 'node', backward)]
    ppermute x1, starting transfers between devices: 2.59 us -> 0.01 us  [body(): lax.ppermute(rows, 'node', backward)]
    ppermute x1, starting transfers between devices: 0.06 us -> 2.65 us  [body(): lax.ppermute(rows, 'node', forward)]
    ppermute x18, starting transfers between devices: 17 us -> 18.6 us  [pass_on(): lax.ppermute(t, 'node', ways[sign])]
  transfers between devices with their start and end apart: 33 -> 33, of which waited for: 23 -> 24; matrix products, arithmetic and copies ran while one was open for 0% -> 0% of each run, Pallas kernels for 24% -> 24%
where the time goes in v10:
time: 156 us
  waiting for transfers between devices  75.4 us (48%)
  Pallas kernels  39 us (25%)
  starting transfers between devices  32.4 us (21%)
  local copies, waits for them, and re-layouts  8.65 us (6%)
    ppermute x18, waiting for transfers between devices, pass_on(): lax.ppermute(t, 'node', ways[sign])  46.4 us
    pallas_call x6, Pallas kernels, expert_parts(): pl.pallas_call(functools.partial(expert_kernel, n, experts, dim, half), i...  36.3 us
    ppermute x18, starting transfers between devices, pass_on(): lax.ppermute(t, 'node', ways[sign])  18.6 us
    ppermute x1, waiting for transfers between devices, body(): lax.ppermute(rows, 'node', forward)  14.7 us
    unnamed x12, local copies, waits for them, and re-layouts  8.65 us
    ppermute x5, starting transfers between devices, send(): ahead[wave].append(lax.ppermute(pair[0], 'node', forward))  7.94 us
    ppermute x5, waiting for transfers between devices, send(): behind[wave].append(lax.ppermute(pair[1], 'node', backward))  6.57 us
    ppermute x5, waiting for transfers between devices, send(): ahead[wave].append(lax.ppermute(pair[0], 'node', forward))  6.21 us
  transfers between devices with their start and end apart: 33, of which 24 were waited for; matrix products, arithmetic and copies ran while one was open for 0% of the time, Pallas kernels for 24%

profile of v10, /device:TPU:0, one launch (start us, length us, event | category | flops | bytes accessed | tf_op | source)
XLA Modules:
  0.0 155.7 jit_solution(11153942479366590021)
XLA Ops:
  0.0 1.2 copy-done.3
  3.7 2.7 %collective-permute-start = (bf16[128,3712]{1,0:T(8,128)(2,1)S(1)}, bf16[128,3712]{1,0:T(8,128)(2,1)S(1)}, u32[]{:S(2)}, u32[]{:S(2)}) collective-permute-start(bf16[128,3712]{1,0:T(8,128)(2,1)S(1)} %shard_map.64.refs_0_), channel_id=1, source_target_pairs={{0,4},{1,5},{4,8},{5,9},{8,12},{9,13},{12,14},{13,15},{14,10},{15,... | collective-permute-start | bytes 2850824 | tf_op jit(solution)/shard_map/ppermute | solution.py:227
  6.4 2.0 %copy-done = bf16[3584,512]{1,0:T(8,128)(2,1)S(1)} copy-done((bf16[3584,512]{1,0:T(8,128)(2,1)S(1)}, bf16[3584,512]{1,0:T(8,128)(2,1)}, u32[]{:S(2)}) %copy-start) | copy-done | bytes 3670040
  8.4 2.0 %copy-done.1 = bf16[3584,512]{1,0:T(8,128)(2,1)S(1)} copy-done((bf16[3584,512]{1,0:T(8,128)(2,1)S(1)}, bf16[3584,512]{1,0:T(8,128)(2,1)}, u32[]{:S(2)}) %copy-start.1) | copy-done | bytes 3670040
  10.5 2.0 %copy-done.2 = bf16[512,3584]{1,0:T(8,128)(2,1)S(1)} copy-done((bf16[512,3584]{1,0:T(8,128)(2,1)S(1)}, bf16[512,3584]{1,0:T(8,128)(2,1)}, u32[]{:S(2)}) %copy-start.2) | copy-done | bytes 3670040
  13.3 14.7 %collective-permute-done.refs_0_.refs_1_ = bf16[128,3712]{1,0:T(8,128)(2,1)S(1)} collective-permute-done((bf16[128,3712]{1,0:T(8,128)(2,1)S(1)}, bf16[128,3712]{1,0:T(8,128)(2,1)S(1)}, u32[]{:S(2)}, u32[]{:S(2)}) %collective-permute-start) | collective-permute-done | bytes 950304 | tf_op jit(solution)/shard_map/ppermute | solution.py:227
  28.0 1.5 collective-permute-done.1.refs_1_.refs_2_
  29.6 1.6 %collective-permute-start.2 = (bf16[64,3712]{1,0:T(8,128)(2,1)S(1)}, bf16[64,3712]{1,0:T(8,128)(2,1)S(1)}, u32[]{:S(2)}, u32[]{:S(2)}) collective-permute-start(bf16[64,3712]{1,0:T(8,128)(2,1)S(1)} %get-tuple-element.106), channel_id=1, source_target_pairs={{0,4},{1,5},{4,8},{5,9},{8,12},{9,13},{12,14},{13,15},{14,10},{15,... | collective-permute-start | bytes 1425416 | tf_op jit(solution)/shard_map/ppermute | solution.py:250
  31.7 1.6 %collective-permute-start.7 = (bf16[64,3712]{1,0:T(8,128)(2,1)S(1)}, bf16[64,3712]{1,0:T(8,128)(2,1)S(1)}, u32[]{:S(2)}, u32[]{:S(2)}) collective-permute-start(bf16[64,3712]{1,0:T(8,128)(2,1)S(1)} %get-tuple-element.127), channel_id=1, source_target_pairs={{0,4},{1,5},{4,8},{5,9},{8,12},{9,13},{12,14},{13,15},{14,10},{15,... | collective-permute-start | bytes 1425416 | tf_op jit(solution)/shard_map/ppermute | solution.py:250
  33.7 10.8 %shard_map.67 = (bf16[64,3584]{1,0:T(8,128)(2,1)S(1)}, bf16[64,3584]{1,0:T(8,128)(2,1)S(1)}, bf16[64,3584]{1,0:T(8,128)(2,1)S(1)}, bf16[64,3584]{1,0:T(8,128)(2,...) custom-call(s32[1]{0:T(128)} %bitcast.expert_ref, bf16[128,3712]{1,0:T(8,128)(2,1)S(1)} %shard_map.64.refs_0_, ...), custom_call_target="tpu_custom_call" | custom-call | flops 1024 | bytes 1024 | tf_op jit(solution)/shard_map/pallas_call | solution.py:74
  45.1 1.6 %collective-permute-start.11 = (bf16[64,3712]{1,0:T(8,128)(2,1)S(1)}, bf16[64,3712]{1,0:T(8,128)(2,1)S(1)}, u32[]{:S(2)}, u32[]{:S(2)}) collective-permute-start(bf16[64,3712]{1,0:T(8,128)(2,1)S(1)} %collective-permute-done.2.refs_0_), channel_id=1, source_target_pairs={{0,4},{1,5},{4,8},{5,9},{8,12},{9,13},{12,14},{13,15},{14,10},{15,... | collective-permute-start | bytes 1425416 | tf_op jit(solution)/shard_map/ppermute | solution.py:250
  47.1 5.1 %shard_map.68 = (bf16[64,3584]{1,0:T(8,128)(2,1)S(1)}, bf16[64,3584]{1,0:T(8,128)(2,1)S(1)}) custom-call(s32[1]{0:T(128)} %bitcast.expert_ref, bf16[64,3712]{1,0:T(8,128)(2,1)S(1)} %collective-permute-done.2.refs_0_, bf16[64,3712]{1,0:T(8,128)(2,1)S(1)} %collective-permute-done.3.refs_1_, bf16[3584,512]{1,0:T(8,128)(2,1)S(1)} %get-tuple-element.112.refs_3_.refs_2_, ...), custom_call_target="tpu_custom_call" | custom-call | flops 1024 | bytes 1024 | tf_op jit(solution)/shard_map/pallas_call | solution.py:74
  52.2 1.5 collective-permute-done.7.refs_0_
  53.7 1.6 %collective-permute-done.8.refs_1_ = bf16[64,3712]{1,0:T(8,128)(2,1)S(1)} collective-permute-done((bf16[64,3712]{1,0:T(8,128)(2,1)S(1)}, bf16[64,3712]{1,0:T(8,128)(2,1)S(1)}, u32[]{:S(2)}, u32[]{:S(2)}) %collective-permute-start.8) | collective-permute-done | bytes 475168 | tf_op jit(solution)/shard_map/ppermute | solution.py:251
  55.2 1.6 %collective-permute-start.9 = (bf16[64,3712]{1,0:T(8,128)(2,1)S(1)}, bf16[64,3712]{1,0:T(8,128)(2,1)S(1)}, u32[]{:S(2)}, u32[]{:S(2)}) collective-permute-start(bf16[64,3712]{1,0:T(8,128)(2,1)S(1)} %collective-permute-done.7.refs_0_), channel_id=1, source_target_pairs={{0,4},{1,5},{4,8},{5,9},{8,12},{9,13},{12,14},{13,15},{14,10},{15,... | collective-permute-start | bytes 1425416 | tf_op jit(solution)/shard_map/ppermute | solution.py:250
  57.3 5.1 %shard_map.69 = (bf16[64,3584]{1,0:T(8,128)(2,1)S(1)}, bf16[64,3584]{1,0:T(8,128)(2,1)S(1)}) custom-call(s32[1]{0:T(128)} %bitcast.expert_ref, bf16[64,3712]{1,0:T(8,128)(2,1)S(1)} %collective-permute-done.7.refs_0_, bf16[64,3712]{1,0:T(8,128)(2,1)S(1)} %collective-permute-done.8.refs_1_, bf16[3584,512]{1,0:T(8,128)(2,1)S(1)} %get-tuple-element.112.refs_3_.refs_2_, ...), custom_call_target="tpu_custom_call" | custom-call | flops 1024 | bytes 1024 | tf_op jit(solution)/shard_map/pallas_call | solution.py:74
  62.4 1.5 collective-permute-done.11.refs_0_
  63.8 1.6 %collective-permute-done.12.refs_1_ = bf16[64,3712]{1,0:T(8,128)(2,1)S(1)} collective-permute-done((bf16[64,3712]{1,0:T(8,128)(2,1)S(1)}, bf16[64,3712]{1,0:T(8,128)(2,1)S(1)}, u32[]{:S(2)}, u32[]{:S(2)}) %collective-permute-start.12) | collective-permute-done | bytes 475168 | tf_op jit(solution)/shard_map/ppermute | solution.py:251
  65.4 1.6 %collective-permute-start.13 = (bf16[64,3712]{1,0:T(8,128)(2,1)S(1)}, bf16[64,3712]{1,0:T(8,128)(2,1)S(1)}, u32[]{:S(2)}, u32[]{:S(2)}) collective-permute-start(bf16[64,3712]{1,0:T(8,128)(2,1)S(1)} %collective-permute-done.11.refs_0_), channel_id=1, source_target_pairs={{0,4},{1,5},{4,8},{5,9},{8,12},{9,13},{12,14},{13,15},{14,10},{15,... | collective-permute-start | bytes 1425416 | tf_op jit(solution)/shard_map/ppermute | solution.py:250
  67.4 5.1 %shard_map.70 = (bf16[64,3584]{1,0:T(8,128)(2,1)S(1)}, bf16[64,3584]{1,0:T(8,128)(2,1)S(1)}) custom-call(s32[1]{0:T(128)} %bitcast.expert_ref, bf16[64,3712]{1,0:T(8,128)(2,1)S(1)} %collective-permute-done.11.refs_0_, bf16[64,3712]{1,0:T(8,128)(2,1)S(1)} %collective-permute-done.12.refs_1_, bf16[3584,512]{1,0:T(8,128)(2,1)S(1)} %get-tuple-element.112.refs_3_.refs_2_, ...), custom_call_target="tpu_custom_call" | custom-call | flops 1024 | bytes 1024 | tf_op jit(solution)/shard_map/pallas_call | solution.py:74
  72.6 1.5 collective-permute-done.9.refs_0_
  74.0 1.6 %collective-permute-done.10.refs_1_ = bf16[64,3712]{1,0:T(8,128)(2,1)S(1)} collective-permute-done((bf16[64,3712]{1,0:T(8,128)(2,1)S(1)}, bf16[64,3712]{1,0:T(8,128)(2,1)S(1)}, u32[]{:S(2)}, u32[]{:S(2)}) %collective-permute-start.10) | collective-permute-done | bytes 475168 | tf_op jit(solution)/shard_map/ppermute | solution.py:251
  75.6 5.1 %shard_map.71 = (bf16[64,3584]{1,0:T(8,128)(2,1)S(1)}, bf16[64,3584]{1,0:T(8,128)(2,1)S(1)}) custom-call(s32[1]{0:T(128)} %bitcast.expert_ref, bf16[64,3712]{1,0:T(8,128)(2,1)S(1)} %collective-permute-done.9.refs_0_, bf16[64,3712]{1,0:T(8,128)(2,1)S(1)} %collective-permute-done.10.refs_1_, bf16[3584,512]{1,0:T(8,128)(2,1)S(1)} %get-tuple-element.112.refs_3_.refs_2_, ...), custom_call_target="tpu_custom_call" | custom-call | flops 1024 | bytes 1024 | tf_op jit(solution)/shard_map/pallas_call | solution.py:74
  80.7 1.8 %collective-permute-done.13.refs_0_ = bf16[64,3712]{1,0:T(8,128)(2,1)S(1)} collective-permute-done((bf16[64,3712]{1,0:T(8,128)(2,1)S(1)}, bf16[64,3712]{1,0:T(8,128)(2,1)S(1)}, u32[]{:S(2)}, u32[]{:S(2)}) %collective-permute-start.13) | collective-permute-done | bytes 475168 | tf_op jit(solution)/shard_map/ppermute | solution.py:250
  82.5 1.3 collective-permute-done.14.refs_1_
  84.3 1.6 %collective-permute-start.16 = (bf16[64,3584]{1,0:T(8,128)(2,1)S(1)}, bf16[64,3584]{1,0:T(8,128)(2,1)S(1)}, u32[]{:S(2)}, u32[]{:S(2)}) collective-permute-start(bf16[64,3584]{1,0:T(8,128)(2,1)S(1)} %get-tuple-element.158), channel_id=1, source_target_pairs={{0,4},{1,5},{4,8},{5,9},{8,12},{9,13},{12,14},{13,15},{14,10},{15,... | collective-permute-start | bytes 1376264 | tf_op jit(solution)/shard_map/ppermute | solution.py:279
  85.8 5.1 %shard_map.75 = (bf16[64,3584]{1,0:T(8,128)(2,1)S(1)}, bf16[64,3584]{1,0:T(8,128)(2,1)S(1)}) custom-call(s32[1]{0:T(128)} %bitcast.expert_ref, bf16[64,3712]{1,0:T(8,128)(2,1)S(1)} %collective-permute-done.13.refs_0_, bf16[64,3712]{1,0:T(8,128)(2,1)S(1)} %collective-permute-done.14.refs_1_, bf16[3584,512]{1,0:T(8,128)(2,1)S(1)} %get-tuple-element.112.refs_3_.refs_2_, ...), custom_call_target="tpu_custom_call" | custom-call | flops 1024 | bytes 1024 | tf_op jit(solution)/shard_map/pallas_call | solution.py:74
  90.9 1.6 %collective-permute-start.21 = (bf16[64,3584]{1,0:T(8,128)(2,1)S(1)}, bf16[64,3584]{1,0:T(8,128)(2,1)S(1)}, u32[]{:S(2)}, u32[]{:S(2)}) collective-permute-start(bf16[64,3584]{1,0:T(8,128)(2,1)S(1)} %get-tuple-element.173), channel_id=1, source_target_pairs={{0,4},{1,5},{4,8},{5,9},{8,12},{9,13},{12,14},{13,15},{14,10},{15,... | collective-permute-start | bytes 1376264 | tf_op jit(solution)/shard_map/ppermute | solution.py:279
  93.0 3.2 %collective-permute-done.15.refs_2_ = bf16[64,3584]{1,0:T(8,128)(2,1)S(1)} collective-permute-done((bf16[64,3584]{1,0:T(8,128)(2,1)S(1)}, bf16[64,3584]{1,0:T(8,128)(2,1)S(1)}, u32[]{:S(2)}, u32[]{:S(2)}) %collective-permute-start.15) | collective-permute-done | bytes 458784 | tf_op jit(solution)/shard_map/ppermute | solution.py:279
  96.2 1.5 collective-permute-done.16.refs_3_
  98.5 1.4 collective-permute-start.18
  99.9 7.7 %collective-permute-done.21.refs_2_ = bf16[64,3584]{1,0:T(8,128)(2,1)S(1)} collective-permute-done((bf16[64,3584]{1,0:T(8,128)(2,1)S(1)}, bf16[64,3584]{1,0:T(8,128)(2,1)S(1)}, u32[]{:S(2)}, u32[]{:S(2)}) %collective-permute-start.21) | collective-permute-done | bytes 458784 | tf_op jit(solution)/shard_map/ppermute | solution.py:279
  107.6 1.6 %collective-permute-start.23 = (bf16[64,3584]{1,0:T(8,128)(2,1)S(1)}, bf16[64,3584]{1,0:T(8,128)(2,1)S(1)}, u32[]{:S(2)}, u32[]{:S(2)}) collective-permute-start(bf16[64,3584]{1,0:T(8,128)(2,1)S(1)} %get-tuple-element.175), channel_id=1, source_target_pairs={{0,4},{1,5},{4,8},{5,9},{8,12},{9,13},{12,14},{13,15},{14,10},{15,... | collective-permute-start | bytes 1376264 | tf_op jit(solution)/shard_map/ppermute | solution.py:279
  109.7 6.1 %collective-permute-done.17.refs_2_ = bf16[64,3584]{1,0:T(8,128)(2,1)S(1)} collective-permute-done((bf16[64,3584]{1,0:T(8,128)(2,1)S(1)}, bf16[64,3584]{1,0:T(8,128)(2,1)S(1)}, u32[]{:S(2)}, u32[]{:S(2)}) %collective-permute-start.17) | collective-permute-done | bytes 458784 | tf_op jit(solution)/shard_map/ppermute | solution.py:279
  115.9 1.5 collective-permute-done.18.refs_3_
  118.1 1.4 collective-permute-start.20
  119.6 7.7 %collective-permute-done.23.refs_2_ = bf16[64,3584]{1,0:T(8,128)(2,1)S(1)} collective-permute-done((bf16[64,3584]{1,0:T(8,128)(2,1)S(1)}, bf16[64,3584]{1,0:T(8,128)(2,1)S(1)}, u32[]{:S(2)}, u32[]{:S(2)}) %collective-permute-start.23) | collective-permute-done | bytes 458784 | tf_op jit(solution)/shard_map/ppermute | solution.py:279
  127.3 1.6 %collective-permute-start.25 = (bf16[32,3584]{1,0:T(8,128)(2,1)S(1)}, bf16[32,3584]{1,0:T(8,128)(2,1)S(1)}, u32[]{:S(2)}, u32[]{:S(2)}) collective-permute-start(bf16[32,3584]{1,0:T(8,128)(2,1)S(1)} %get-tuple-element.177), channel_id=1, source_target_pairs={{0,4},{1,5},{4,8},{5,9},{8,12},{9,13},{12,14},{13,15},{14,10},{15,... | collective-permute-start | bytes 688136 | tf_op jit(solution)/shard_map/ppermute | solution.py:279
  129.4 1.6 %collective-permute-start.29 = (bf16[32,3584]{1,0:T(8,128)(2,1)S(1)}, bf16[32,3584]{1,0:T(8,128)(2,1)S(1)}, u32[]{:S(2)}, u32[]{:S(2)}) collective-permute-start(bf16[32,3584]{1,0:T(8,128)(2,1)S(1)} %get-tuple-element.181), channel_id=1, source_target_pairs={{0,4},{1,5},{4,8},{5,9},{8,12},{9,13},{12,14},{13,15},{14,10},{15,... | collective-permute-start | bytes 688136 | tf_op jit(solution)/shard_map/ppermute | solution.py:279
  131.0 4.6 %collective-permute-done.19.refs_2_ = bf16[64,3584]{1,0:T(8,128)(2,1)S(1)} collective-permute-done((bf16[64,3584]{1,0:T(8,128)(2,1)S(1)}, bf16[64,3584]{1,0:T(8,128)(2,1)S(1)}, u32[]{:S(2)}, u32[]{:S(2)}) %collective-permute-start.19) | collective-permute-done | bytes 458784 | tf_op jit(solution)/shard_map/ppermute | solution.py:279
  136.0 1.1 collective-permute-done.20.refs_3_
  137.2 4.7 %collective-permute-done.25.refs_2_ = bf16[32,3584]{1,0:T(8,128)(2,1)S(1)} collective-permute-done((bf16[32,3584]{1,0:T(8,128)(2,1)S(1)}, bf16[32,3584]{1,0:T(8,128)(2,1)S(1)}, u32[]{:S(2)}, u32[]{:S(2)}) %collective-permute-start.25) | collective-permute-done | bytes 229408 | tf_op jit(solution)/shard_map/ppermute | solution.py:279
  142.0 1.6 %collective-permute-start.27 = (bf16[32,3584]{1,0:T(8,128)(2,1)S(1)}, bf16[32,3584]{1,0:T(8,128)(2,1)S(1)}, u32[]{:S(2)}, u32[]{:S(2)}) collective-permute-start(bf16[32,3584]{1,0:T(8,128)(2,1)S(1)} %get-tuple-element.179), channel_id=1, source_target_pairs={{0,4},{1,5},{4,8},{5,9},{8,12},{9,13},{12,14},{13,15},{14,10},{15,... | collective-permute-start | bytes 688136 | tf_op jit(solution)/shard_map/ppermute | solution.py:279
  144.1 2.8 %collective-permute-done.29.refs_2_ = bf16[32,3584]{1,0:T(8,128)(2,1)S(1)} collective-permute-done((bf16[32,3584]{1,0:T(8,128)(2,1)S(1)}, bf16[32,3584]{1,0:T(8,128)(2,1)S(1)}, u32[]{:S(2)}, u32[]{:S(2)}) %collective-permute-start.29) | collective-permute-done | bytes 229408 | tf_op jit(solution)/shard_map/ppermute | solution.py:279
  146.9 1.6 %collective-permute-start.31 = (bf16[32,3584]{1,0:T(8,128)(2,1)S(1)}, bf16[32,3584]{1,0:T(8,128)(2,1)S(1)}, u32[]{:S(2)}, u32[]{:S(2)}) collective-permute-start(bf16[32,3584]{1,0:T(8,128)(2,1)S(1)} %get-tuple-element.183), channel_id=1, source_target_pairs={{0,4},{1,5},{4,8},{5,9},{8,12},{9,13},{12,14},{13,15},{14,10},{15,... | collective-permute-start | bytes 688136 | tf_op jit(solution)/shard_map/ppermute | solution.py:279
  149.0 2.1 %collective-permute-done.27.refs_2_ = bf16[32,3584]{1,0:T(8,128)(2,1)S(1)} collective-permute-done((bf16[32,3584]{1,0:T(8,128)(2,1)S(1)}, bf16[32,3584]{1,0:T(8,128)(2,1)S(1)}, u32[]{:S(2)}, u32[]{:S(2)}) %collective-permute-start.27) | collective-permute-done | bytes 229408 | tf_op jit(solution)/shard_map/ppermute | solution.py:279
  151.1 2.5 %collective-permute-done.31.refs_4_ = bf16[32,3584]{1,0:T(8,128)(2,1)S(1)} collective-permute-done((bf16[32,3584]{1,0:T(8,128)(2,1)S(1)}, bf16[32,3584]{1,0:T(8,128)(2,1)S(1)}, u32[]{:S(2)}, u32[]{:S(2)}) %collective-permute-start.31) | collective-permute-done | bytes 229408 | tf_op jit(solution)/shard_map/ppermute | solution.py:279
  154.6 1.1 shard_map.80
  (47 shorter events, 12.4 us)
Async XLA Ops:
  0.0 1.2 copy-start.3
  1.2 0.7 copy-start.4
  1.9 0.7 copy-start.5
  2.7 29.0 %collective-permute-start.4 = (bf16[3584,512]{1,0:T(8,128)(2,1)}, bf16[3584,512]{1,0:T(8,128)(2,1)S(1)}, u32[]{:S(2)}, u32[]{:S(2)}) collective-permute-start(bf16[3584,512]{1,0:T(8,128)(2,1)} %refs_0_), channel_id=1, source_target_pairs={{0,1},{1,0},{2,3},{3,2},{4,5},{5,4},{6,7},{7,6},{8,9},{9,8},{10,11... | collective-permute-start | bytes 11010056 | tf_op jit(solution)/shard_map/ppermute | solution.py:229
  3.2 30.1 %collective-permute-start.5 = (bf16[3584,512]{1,0:T(8,128)(2,1)}, bf16[3584,512]{1,0:T(8,128)(2,1)S(1)}, u32[]{:S(2)}, u32[]{:S(2)}) collective-permute-start(bf16[3584,512]{1,0:T(8,128)(2,1)} %refs_1_), channel_id=1, source_target_pairs={{0,1},{1,0},{2,3},{3,2},{4,5},{5,4},{6,7},{7,6},{8,9},{9,8},{10,11... | collective-permute-start | bytes 11010056 | tf_op jit(solution)/shard_map/ppermute | solution.py:229
  3.3 30.5 %collective-permute-start.6 = (bf16[512,3584]{1,0:T(8,128)(2,1)}, bf16[512,3584]{1,0:T(8,128)(2,1)S(1)}, u32[]{:S(2)}, u32[]{:S(2)}) collective-permute-start(bf16[512,3584]{1,0:T(8,128)(2,1)} %refs_2_), channel_id=1, source_target_pairs={{0,1},{1,0},{2,3},{3,2},{4,5},{5,4},{6,7},{7,6},{8,9},{9,8},{10,11... | collective-permute-start | bytes 11010056 | tf_op jit(solution)/shard_map/ppermute | solution.py:229
  3.7 24.2 %collective-permute-start = (bf16[128,3712]{1,0:T(8,128)(2,1)S(1)}, bf16[128,3712]{1,0:T(8,128)(2,1)S(1)}, u32[]{:S(2)}, u32[]{:S(2)}) collective-permute-start(bf16[128,3712]{1,0:T(8,128)(2,1)S(1)} %shard_map.64.refs_0_), channel_id=1, source_target_pairs={{0,4},{1,5},{4,8},{5,9},{8,12},{9,13},{12,14},{13,15},{14,10},{15,... | collective-permute-start | bytes 2850824 | tf_op jit(solution)/shard_map/ppermute | solution.py:227
  6.4 23.1 %collective-permute-start.1 = (bf16[128,3712]{1,0:T(8,128)(2,1)S(1)}, bf16[128,3712]{1,0:T(8,128)(2,1)S(1)}, u32[]{:S(2)}, u32[]{:S(2)}) collective-permute-start(bf16[128,3712]{1,0:T(8,128)(2,1)S(1)} %shard_map.64.refs_0_), channel_id=1, source_target_pairs={{0,2},{1,3},{4,0},{5,1},{8,4},{9,5},{12,8},{13,9},{14,12},{15,13},... | collective-permute-start | bytes 2850824 | tf_op jit(solution)/shard_map/ppermute | solution.py:227
  6.4 2.0 %copy-start = (bf16[3584,512]{1,0:T(8,128)(2,1)S(1)}, bf16[3584,512]{1,0:T(8,128)(2,1)}, u32[]{:S(2)}) copy-start(bf16[3584,512]{1,0:T(8,128)(2,1)} %refs_0_) | copy-start | bytes 11010052
  8.4 2.0 %copy-start.1 = (bf16[3584,512]{1,0:T(8,128)(2,1)S(1)}, bf16[3584,512]{1,0:T(8,128)(2,1)}, u32[]{:S(2)}) copy-start(bf16[3584,512]{1,0:T(8,128)(2,1)} %refs_1_) | copy-start | bytes 11010052
  10.4 2.0 %copy-start.2 = (bf16[512,3584]{1,0:T(8,128)(2,1)S(1)}, bf16[512,3584]{1,0:T(8,128)(2,1)}, u32[]{:S(2)}) copy-start(bf16[512,3584]{1,0:T(8,128)(2,1)} %refs_2_) | copy-start | bytes 11010052
  29.6 14.9 %collective-permute-start.2 = (bf16[64,3712]{1,0:T(8,128)(2,1)S(1)}, bf16[64,3712]{1,0:T(8,128)(2,1)S(1)}, u32[]{:S(2)}, u32[]{:S(2)}) collective-permute-start(bf16[64,3712]{1,0:T(8,128)(2,1)S(1)} %get-tuple-element.106), channel_id=1, source_target_pairs={{0,4},{1,5},{4,8},{5,9},{8,12},{9,13},{12,14},{13,15},{14,10},{15,... | collective-permute-start | bytes 1425416 | tf_op jit(solution)/shard_map/ppermute | solution.py:250
  31.2 13.8 %collective-permute-start.3 = (bf16[64,3712]{1,0:T(8,128)(2,1)S(1)}, bf16[64,3712]{1,0:T(8,128)(2,1)S(1)}, u32[]{:S(2)}, u32[]{:S(2)}) collective-permute-start(bf16[64,3712]{1,0:T(8,128)(2,1)S(1)} %get-tuple-element.107), channel_id=1, source_target_pairs={{0,2},{1,3},{4,0},{5,1},{8,4},{9,5},{12,8},{13,9},{14,12},{15,13},... | collective-permute-start | bytes 1425416 | tf_op jit(solution)/shard_map/ppermute | solution.py:251
  31.7 22.0 %collective-permute-start.7 = (bf16[64,3712]{1,0:T(8,128)(2,1)S(1)}, bf16[64,3712]{1,0:T(8,128)(2,1)S(1)}, u32[]{:S(2)}, u32[]{:S(2)}) collective-permute-start(bf16[64,3712]{1,0:T(8,128)(2,1)S(1)} %get-tuple-element.127), channel_id=1, source_target_pairs={{0,4},{1,5},{4,8},{5,9},{8,12},{9,13},{12,14},{13,15},{14,10},{15,... | collective-permute-start | bytes 1425416 | tf_op jit(solution)/shard_map/ppermute | solution.py:250
  33.3 22.0 %collective-permute-start.8 = (bf16[64,3712]{1,0:T(8,128)(2,1)S(1)}, bf16[64,3712]{1,0:T(8,128)(2,1)S(1)}, u32[]{:S(2)}, u32[]{:S(2)}) collective-permute-start(bf16[64,3712]{1,0:T(8,128)(2,1)S(1)} %get-tuple-element.128), channel_id=1, source_target_pairs={{0,2},{1,3},{4,0},{5,1},{8,4},{9,5},{12,8},{13,9},{14,12},{15,13},... | collective-permute-start | bytes 1425416 | tf_op jit(solution)/shard_map/ppermute | solution.py:251
  45.1 18.8 %collective-permute-start.11 = (bf16[64,3712]{1,0:T(8,128)(2,1)S(1)}, bf16[64,3712]{1,0:T(8,128)(2,1)S(1)}, u32[]{:S(2)}, u32[]{:S(2)}) collective-permute-start(bf16[64,3712]{1,0:T(8,128)(2,1)S(1)} %collective-permute-done.2.refs_0_), channel_id=1, source_target_pairs={{0,4},{1,5},{4,8},{5,9},{8,12},{9,13},{12,14},{13,15},{14,10},{15,... | collective-permute-start | bytes 1425416 | tf_op jit(solution)/shard_map/ppermute | solution.py:250
  46.6 18.8 %collective-permute-start.12 = (bf16[64,3712]{1,0:T(8,128)(2,1)S(1)}, bf16[64,3712]{1,0:T(8,128)(2,1)S(1)}, u32[]{:S(2)}, u32[]{:S(2)}) collective-permute-start(bf16[64,3712]{1,0:T(8,128)(2,1)S(1)} %collective-permute-done.3.refs_1_), channel_id=1, source_target_pairs={{0,2},{1,3},{4,0},{5,1},{8,4},{9,5},{12,8},{13,9},{14,12},{15,13},... | collective-permute-start | bytes 1425416 | tf_op jit(solution)/shard_map/ppermute | solution.py:251
  55.2 18.8 %collective-permute-start.9 = (bf16[64,3712]{1,0:T(8,128)(2,1)S(1)}, bf16[64,3712]{1,0:T(8,128)(2,1)S(1)}, u32[]{:S(2)}, u32[]{:S(2)}) collective-permute-start(bf16[64,3712]{1,0:T(8,128)(2,1)S(1)} %collective-permute-done.7.refs_0_), channel_id=1, source_target_pairs={{0,4},{1,5},{4,8},{5,9},{8,12},{9,13},{12,14},{13,15},{14,10},{15,... | collective-permute-start | bytes 1425416 | tf_op jit(solution)/shard_map/ppermute | solution.py:250
  56.8 18.8 %collective-permute-start.10 = (bf16[64,3712]{1,0:T(8,128)(2,1)S(1)}, bf16[64,3712]{1,0:T(8,128)(2,1)S(1)}, u32[]{:S(2)}, u32[]{:S(2)}) collective-permute-start(bf16[64,3712]{1,0:T(8,128)(2,1)S(1)} %collective-permute-done.8.refs_1_), channel_id=1, source_target_pairs={{0,2},{1,3},{4,0},{5,1},{8,4},{9,5},{12,8},{13,9},{14,12},{15,13},... | collective-permute-start | bytes 1425416 | tf_op jit(solution)/shard_map/ppermute | solution.py:251
  65.4 17.1 %collective-permute-start.13 = (bf16[64,3712]{1,0:T(8,128)(2,1)S(1)}, bf16[64,3712]{1,0:T(8,128)(2,1)S(1)}, u32[]{:S(2)}, u32[]{:S(2)}) collective-permute-start(bf16[64,3712]{1,0:T(8,128)(2,1)S(1)} %collective-permute-done.11.refs_0_), channel_id=1, source_target_pairs={{0,4},{1,5},{4,8},{5,9},{8,12},{9,13},{12,14},{13,15},{14,10},{15,... | collective-permute-start | bytes 1425416 | tf_op jit(solution)/shard_map/ppermute | solution.py:250
  67.0 16.8 %collective-permute-start.14 = (bf16[64,3712]{1,0:T(8,128)(2,1)S(1)}, bf16[64,3712]{1,0:T(8,128)(2,1)S(1)}, u32[]{:S(2)}, u32[]{:S(2)}) collective-permute-start(bf16[64,3712]{1,0:T(8,128)(2,1)S(1)} %collective-permute-done.12.refs_1_), channel_id=1, source_target_pairs={{0,2},{1,3},{4,0},{5,1},{8,4},{9,5},{12,8},{13,9},{14,12},{15,13},... | collective-permute-start | bytes 1425416 | tf_op jit(solution)/shard_map/ppermute | solution.py:251
  83.8 12.4 %collective-permute-start.15 = (bf16[64,3584]{1,0:T(8,128)(2,1)S(1)}, bf16[64,3584]{1,0:T(8,128)(2,1)S(1)}, u32[]{:S(2)}, u32[]{:S(2)}) collective-permute-start(bf16[64,3584]{1,0:T(8,128)(2,1)S(1)} %get-tuple-element.157), channel_id=1, source_target_pairs={{0,2},{1,3},{4,0},{5,1},{8,4},{9,5},{12,8},{13,9},{14,12},{15,13},... | collective-permute-start | bytes 1376264 | tf_op jit(solution)/shard_map/ppermute | solution.py:279
  84.3 13.5 %collective-permute-start.16 = (bf16[64,3584]{1,0:T(8,128)(2,1)S(1)}, bf16[64,3584]{1,0:T(8,128)(2,1)S(1)}, u32[]{:S(2)}, u32[]{:S(2)}) collective-permute-start(bf16[64,3584]{1,0:T(8,128)(2,1)S(1)} %get-tuple-element.158), channel_id=1, source_target_pairs={{0,4},{1,5},{4,8},{5,9},{8,12},{9,13},{12,14},{13,15},{14,10},{15,... | collective-permute-start | bytes 1376264 | tf_op jit(solution)/shard_map/ppermute | solution.py:279
  90.9 16.6 %collective-permute-start.21 = (bf16[64,3584]{1,0:T(8,128)(2,1)S(1)}, bf16[64,3584]{1,0:T(8,128)(2,1)S(1)}, u32[]{:S(2)}, u32[]{:S(2)}) collective-permute-start(bf16[64,3584]{1,0:T(8,128)(2,1)S(1)} %get-tuple-element.173), channel_id=1, source_target_pairs={{0,4},{1,5},{4,8},{5,9},{8,12},{9,13},{12,14},{13,15},{14,10},{15,... | collective-permute-start | bytes 1376264 | tf_op jit(solution)/shard_map/ppermute | solution.py:279
  92.6 15.0 %collective-permute-start.22 = (bf16[64,3584]{1,0:T(8,128)(2,1)S(1)}, bf16[64,3584]{1,0:T(8,128)(2,1)S(1)}, u32[]{:S(2)}, u32[]{:S(2)}) collective-permute-start(bf16[64,3584]{1,0:T(8,128)(2,1)S(1)} %get-tuple-element.174), channel_id=1, source_target_pairs={{0,2},{1,3},{4,0},{5,1},{8,4},{9,5},{12,8},{13,9},{14,12},{15,13},... | collective-permute-start | bytes 1376264 | tf_op jit(solution)/shard_map/ppermute | solution.py:279
  97.8 18.1 %collective-permute-start.17 = (bf16[64,3584]{1,0:T(8,128)(2,1)S(1)}, bf16[64,3584]{1,0:T(8,128)(2,1)S(1)}, u32[]{:S(2)}, u32[]{:S(2)}) collective-permute-start(bf16[64,3584]{1,0:T(8,128)(2,1)S(1)} %get-tuple-element.159), channel_id=1, source_target_pairs={{0,2},{1,3},{4,0},{5,1},{8,4},{9,5},{12,8},{13,9},{14,12},{15,13},... | collective-permute-start | bytes 1376264 | tf_op jit(solution)/shard_map/ppermute | solution.py:279
  98.5 18.9 %collective-permute-start.18 = (bf16[64,3584]{1,0:T(8,128)(2,1)S(1)}, bf16[64,3584]{1,0:T(8,128)(2,1)S(1)}, u32[]{:S(2)}, u32[]{:S(2)}) collective-permute-start(bf16[64,3584]{1,0:T(8,128)(2,1)S(1)} %get-tuple-element.160), channel_id=1, source_target_pairs={{0,4},{1,5},{4,8},{5,9},{8,12},{9,13},{12,14},{13,15},{14,10},{15,... | collective-permute-start | bytes 1376264 | tf_op jit(solution)/shard_map/ppermute | solution.py:279
  107.6 19.6 %collective-permute-start.23 = (bf16[64,3584]{1,0:T(8,128)(2,1)S(1)}, bf16[64,3584]{1,0:T(8,128)(2,1)S(1)}, u32[]{:S(2)}, u32[]{:S(2)}) collective-permute-start(bf16[64,3584]{1,0:T(8,128)(2,1)S(1)} %get-tuple-element.175), channel_id=1, source_target_pairs={{0,4},{1,5},{4,8},{5,9},{8,12},{9,13},{12,14},{13,15},{14,10},{15,... | collective-permute-start | bytes 1376264 | tf_op jit(solution)/shard_map/ppermute | solution.py:279
  109.3 17.9 %collective-permute-start.24 = (bf16[64,3584]{1,0:T(8,128)(2,1)S(1)}, bf16[64,3584]{1,0:T(8,128)(2,1)S(1)}, u32[]{:S(2)}, u32[]{:S(2)}) collective-permute-start(bf16[64,3584]{1,0:T(8,128)(2,1)S(1)} %get-tuple-element.176), channel_id=1, source_target_pairs={{0,2},{1,3},{4,0},{5,1},{8,4},{9,5},{12,8},{13,9},{14,12},{15,13},... | collective-permute-start | bytes 1376264 | tf_op jit(solution)/shard_map/ppermute | solution.py:279
  117.5 18.1 %collective-permute-start.19 = (bf16[64,3584]{1,0:T(8,128)(2,1)S(1)}, bf16[64,3584]{1,0:T(8,128)(2,1)S(1)}, u32[]{:S(2)}, u32[]{:S(2)}) collective-permute-start(bf16[64,3584]{1,0:T(8,128)(2,1)S(1)} %get-tuple-element.161), channel_id=1, source_target_pairs={{0,2},{1,3},{4,0},{5,1},{8,4},{9,5},{12,8},{13,9},{14,12},{15,13},... | collective-permute-start | bytes 1376264 | tf_op jit(solution)/shard_map/ppermute | solution.py:279
  118.1 18.9 %collective-permute-start.20 = (bf16[64,3584]{1,0:T(8,128)(2,1)S(1)}, bf16[64,3584]{1,0:T(8,128)(2,1)S(1)}, u32[]{:S(2)}, u32[]{:S(2)}) collective-permute-start(bf16[64,3584]{1,0:T(8,128)(2,1)S(1)} %get-tuple-element.162), channel_id=1, source_target_pairs={{0,4},{1,5},{4,8},{5,9},{8,12},{9,13},{12,14},{13,15},{14,10},{15,... | collective-permute-start | bytes 1376264 | tf_op jit(solution)/shard_map/ppermute | solution.py:279
  127.3 14.6 %collective-permute-start.25 = (bf16[32,3584]{1,0:T(8,128)(2,1)S(1)}, bf16[32,3584]{1,0:T(8,128)(2,1)S(1)}, u32[]{:S(2)}, u32[]{:S(2)}) collective-permute-start(bf16[32,3584]{1,0:T(8,128)(2,1)S(1)} %get-tuple-element.177), channel_id=1, source_target_pairs={{0,4},{1,5},{4,8},{5,9},{8,12},{9,13},{12,14},{13,15},{14,10},{15,... | collective-permute-start | bytes 688136 | tf_op jit(solution)/shard_map/ppermute | solution.py:279
  128.9 13.0 %collective-permute-start.26 = (bf16[32,3584]{1,0:T(8,128)(2,1)S(1)}, bf16[32,3584]{1,0:T(8,128)(2,1)S(1)}, u32[]{:S(2)}, u32[]{:S(2)}) collective-permute-start(bf16[32,3584]{1,0:T(8,128)(2,1)S(1)} %get-tuple-element.178), channel_id=1, source_target_pairs={{0,2},{1,3},{4,0},{5,1},{8,4},{9,5},{12,8},{13,9},{14,12},{15,13},... | collective-permute-start | bytes 688136 | tf_op jit(solution)/shard_map/ppermute | solution.py:279
  129.4 17.5 %collective-permute-start.29 = (bf16[32,3584]{1,0:T(8,128)(2,1)S(1)}, bf16[32,3584]{1,0:T(8,128)(2,1)S(1)}, u32[]{:S(2)}, u32[]{:S(2)}) collective-permute-start(bf16[32,3584]{1,0:T(8,128)(2,1)S(1)} %get-tuple-element.181), channel_id=1, source_target_pairs={{0,4},{1,5},{4,8},{5,9},{8,12},{9,13},{12,14},{13,15},{14,10},{15,... | collective-permute-start | bytes 688136 | tf_op jit(solution)/shard_map/ppermute | solution.py:279
  135.5 11.3 %collective-permute-start.30 = (bf16[32,3584]{1,0:T(8,128)(2,1)S(1)}, bf16[32,3584]{1,0:T(8,128)(2,1)S(1)}, u32[]{:S(2)}, u32[]{:S(2)}) collective-permute-start(bf16[32,3584]{1,0:T(8,128)(2,1)S(1)} %get-tuple-element.182), channel_id=1, source_target_pairs={{0,2},{1,3},{4,0},{5,1},{8,4},{9,5},{12,8},{13,9},{14,12},{15,13},... | collective-permute-start | bytes 688136 | tf_op jit(solution)/shard_map/ppermute | solution.py:279
  142.0 9.1 %collective-permute-start.27 = (bf16[32,3584]{1,0:T(8,128)(2,1)S(1)}, bf16[32,3584]{1,0:T(8,128)(2,1)S(1)}, u32[]{:S(2)}, u32[]{:S(2)}) collective-permute-start(bf16[32,3584]{1,0:T(8,128)(2,1)S(1)} %get-tuple-element.179), channel_id=1, source_target_pairs={{0,4},{1,5},{4,8},{5,9},{8,12},{9,13},{12,14},{13,15},{14,10},{15,... | collective-permute-start | bytes 688136 | tf_op jit(solution)/shard_map/ppermute | solution.py:279
  143.6 7.4 %collective-permute-start.28 = (bf16[32,3584]{1,0:T(8,128)(2,1)S(1)}, bf16[32,3584]{1,0:T(8,128)(2,1)S(1)}, u32[]{:S(2)}, u32[]{:S(2)}) collective-permute-start(bf16[32,3584]{1,0:T(8,128)(2,1)S(1)} %get-tuple-element.180), channel_id=1, source_target_pairs={{0,2},{1,3},{4,0},{5,1},{8,4},{9,5},{12,8},{13,9},{14,12},{15,13},... | collective-permute-start | bytes 688136 | tf_op jit(solution)/shard_map/ppermute | solution.py:279
  146.9 6.6 %collective-permute-start.31 = (bf16[32,3584]{1,0:T(8,128)(2,1)S(1)}, bf16[32,3584]{1,0:T(8,128)(2,1)S(1)}, u32[]{:S(2)}, u32[]{:S(2)}) collective-permute-start(bf16[32,3584]{1,0:T(8,128)(2,1)S(1)} %get-tuple-element.183), channel_id=1, source_target_pairs={{0,4},{1,5},{4,8},{5,9},{8,12},{9,13},{12,14},{13,15},{14,10},{15,... | collective-permute-start | bytes 688136 | tf_op jit(solution)/shard_map/ppermute | solution.py:279
  148.6 6.0 %collective-permute-start.32 = (bf16[32,3584]{1,0:T(8,128)(2,1)S(1)}, bf16[32,3584]{1,0:T(8,128)(2,1)S(1)}, u32[]{:S(2)}, u32[]{:S(2)}) collective-permute-start(bf16[32,3584]{1,0:T(8,128)(2,1)S(1)} %get-tuple-element.184), channel_id=1, source_target_pairs={{0,2},{1,3},{4,0},{5,1},{8,4},{9,5},{12,8},{13,9},{14,12},{15,13},... | collective-permute-start | bytes 688136 | tf_op jit(solution)/shard_map/ppermute | solution.py:279

commit v11 on v10

--- a/solution.py
+++ b/solution.py
@@ -9,30 +9,33 @@
 
 SPAN = 2
 LANES = 128
-DIGIT = 64
 TILE = 256
 WIDE = 512
 MIB = 1 << 20
-AHEAD = 6 * MIB
-
-
-def expert_kernel(n, experts, dim, half, expert_ref, *refs):
+FORWARD = 40 * 10**9
+
+
+def expert_kernel(marks, ring, dim, half, chip_ref, table_ref, *refs):
+    n = len(marks)
     blocks, weights, outs = refs[:n], refs[n : n + 6], refs[n + 6 : -3]
     rows_ref, scale_ref, hidden_ref = refs[-3:]
     hid = weights[0].shape[1]
-    expert = expert_ref[0]
+    table = table_ref[...]
+    filler = jnp.zeros((LANES - table.shape[0], table.shape[1]), table.dtype)
+    table = jnp.transpose(jnp.concatenate([table, filler], 0))
+    lane = lax.broadcasted_iota(jnp.int32, table.shape, 1)
+    chip = chip_ref[0]
+    pos = jnp.where(lax.rem(chip, 2) == 0, lax.div(chip, 2), ring - 1 - lax.div(chip, 2))
     first = 0
-    for block in blocks:
+    for (offset, start), block in zip(marks, blocks):
         count = block.shape[0]
-        lane = lax.broadcasted_iota(jnp.int32, (count, LANES), 1)
+        origin = lax.rem(pos + (offset + ring), ring)
+        origin = jnp.where(origin < ring // 2, 2 * origin, 2 * (ring - 1 - origin) + 1)
+        scale = jnp.sum(jnp.where(lane == origin, table, 0.0), 1, keepdims=True)
         at = pl.ds(first, count)
         first += count
-        rows_ref[at, :] = block[:, :dim]
-        digits = block[:, dim:].astype(jnp.float32)
-        codes = jnp.where(lane == expert, digits * float(DIGIT), 0.0)
-        codes = codes + jnp.where(lane == expert + experts, digits, 0.0)
-        code = jnp.sum(codes, 1, keepdims=True) * (1.0 / 4096.0)
-        scale_ref[at, :] = jnp.broadcast_to(code, (count, LANES))
+        rows_ref[at, :] = block[...]
+        scale_ref[at, :] = jnp.broadcast_to(scale[start : start + count], (count, LANES))
 
     for side in range(SPAN):
         gate_ref, up_ref, _ = weights[3 * side : 3 * side + 3]
@@ -66,13 +69,13 @@
     return pl.CostEstimate(flops=1024, bytes_accessed=1024, transcendentals=0)
 
 
-def expert_parts(experts, half, expert, blocks, own, other, cost=1024):
+def expert_parts(marks, ring, half, chip, table, blocks, own, other):
     dim, hid = own[0].shape
     n, rows = len(blocks), sum(block.shape[0] for block in blocks)
     specs = [pl.BlockSpec(memory_space=pltpu.SMEM)]
-    specs += [pl.BlockSpec(memory_space=pltpu.VMEM)] * (n + 6)
-    return pl.pallas_call(
-        functools.partial(expert_kernel, n, experts, dim, half),
+    specs += [pl.BlockSpec(memory_space=pltpu.VMEM)] * (n + 7)
+    return pl.pallas_call(
+        functools.partial(expert_kernel, marks, ring, dim, half),
         in_specs=specs,
         out_specs=[pl.BlockSpec(memory_space=pltpu.VMEM)] * (rows // half),
         out_shape=[jax.ShapeDtypeStruct((half, dim), jnp.bfloat16)] * (rows // half),
@@ -82,8 +85,8 @@
             pltpu.VMEM((rows, SPAN * hid), jnp.bfloat16),
         ],
         compiler_params=pltpu.CompilerParams(vmem_limit_bytes=8 * MIB),
-        cost_estimate=pl.CostEstimate(flops=1024, bytes_accessed=cost, transcendentals=0),
-    )(expert, *blocks, *own, *other)
+        cost_estimate=small_cost(),
+    )(chip, table, *blocks, *own, *other)
 
 
 def add_kernel(n, pieces, first, *refs):
@@ -97,7 +100,7 @@
             out[...] = left.astype(out.dtype) + right.astype(out.dtype)
 
 
-def add(lefts, rights, after=(), pieces=1, first=0, dtype=None, cost=1024):
+def add(lefts, rights, after=(), pieces=1, first=0, dtype=None):
     n = len(lefts)
     rows, dim = rights[0].shape
     shape = jax.ShapeDtypeStruct((rows // pieces, dim), dtype or rights[0].dtype)
@@ -108,7 +111,7 @@
         out_specs=[pl.BlockSpec(memory_space=pltpu.VMEM)] * (n * pieces),
         out_shape=[shape] * (n * pieces),
         compiler_params=pltpu.CompilerParams(vmem_limit_bytes=6 * MIB),
-        cost_estimate=pl.CostEstimate(flops=1024, bytes_accessed=cost, transcendentals=0),
+        cost_estimate=small_cost(),
     )(*lefts, *rights, *after)
 
 
@@ -128,7 +131,7 @@
         out_specs=[pl.BlockSpec(memory_space=pltpu.VMEM)] * (2 * n),
         out_shape=[jax.ShapeDtypeStruct((rows // 2, dim), arrays[0].dtype)] * (2 * n),
         compiler_params=pltpu.CompilerParams(vmem_limit_bytes=6 * MIB),
-        cost_estimate=small_cost(),
+        cost_estimate=pl.CostEstimate(flops=FORWARD, bytes_accessed=1024, transcendentals=0),
     )(*arrays)
 
 
@@ -155,26 +158,22 @@
     )(*bases, *terms)
 
 
-def rows_kernel(experts, top, tokens_ref, ids_ref, codes_ref, out_ref):
-    tok, dim = tokens_ref.shape
-    row = lax.broadcasted_iota(jnp.int32, (LANES, tok), 0)
-    expert = jnp.where(row < experts, row, row - experts)
-    code = jnp.zeros((LANES, tok), jnp.int32)
-    for k in range(top):
+def table_kernel(ids_ref, codes_ref, out_ref):
+    expert = lax.broadcasted_iota(jnp.int32, out_ref.shape, 0)
+    code = jnp.zeros(out_ref.shape, jnp.int32)
+    for k in range(ids_ref.shape[0]):
         code = code + jnp.where(ids_ref[k : k + 1, :] == expert, codes_ref[k : k + 1, :], 0)
-    digits = jnp.where(row < experts, code // DIGIT, code % DIGIT)
-    out_ref[:, :dim] = tokens_ref[...]
-    out_ref[:, dim:] = jnp.transpose(digits.astype(jnp.float32)).astype(out_ref.dtype)
-
-
-def with_codes(experts, tokens, ids, codes):
-    tok, dim = tokens.shape
-    return pl.pallas_call(
-        functools.partial(rows_kernel, experts, ids.shape[1]),
-        out_shape=jax.ShapeDtypeStruct((tok, dim + LANES), tokens.dtype),
-        compiler_params=pltpu.CompilerParams(vmem_limit_bytes=6 * MIB),
-        cost_estimate=small_cost(),
-    )(tokens, ids.T, codes.T)
+    out_ref[...] = code.astype(jnp.float32) * (1.0 / 4096.0)
+
+
+def gate_table(experts, ids, codes):
+    return pl.pallas_call(
+        table_kernel,
+        in_specs=[pl.BlockSpec(memory_space=pltpu.VMEM)] * 2,
+        out_shape=jax.ShapeDtypeStruct((experts, ids.shape[0]), jnp.float32),
+        compiler_params=pltpu.CompilerParams(vmem_limit_bytes=2 * MIB),
+        cost_estimate=small_cost(),
+    )(ids.T, codes.T)
 
 
 def bring_in_kernel(n, *refs):
@@ -219,13 +218,21 @@
 
     forward, backward = perm(1), perm(-1)
     swap = [(node, node ^ 1) for node in range(nodes)]
-    expert = lax.div(lax.axis_index("node"), jnp.int32(SPAN)).reshape(1)
-    tokens, expert = lax.optimization_barrier((tokens, expert))
-
-    rows = with_codes(ring, tokens, expert_ids, gate_codes)
-
-    near = [lax.ppermute(rows, "node", forward), lax.ppermute(rows, "node", backward)]
-    weights, _ = lax.optimization_barrier(((w_gate, w_up, w_down), rows))
+    chip = lax.div(lax.axis_index("node"), jnp.int32(SPAN)).reshape(1)
+    weights = (w_gate, w_up, w_down)
+    tokens, weights, chip = lax.optimization_barrier((tokens, weights, chip))
+
+    near = [lax.ppermute(tokens, "node", forward), lax.ppermute(tokens, "node", backward)]
+    rails = [[SPAN * c + core for c in range(ring)] for core in range(SPAN)]
+    table = lax.all_to_all(
+        gate_table(ring, expert_ids, gate_codes),
+        "node",
+        split_axis=0,
+        concat_axis=0,
+        axis_index_groups=rails,
+        tiled=True,
+    )
+    weights, table = lax.optimization_barrier((weights, table))
     other = [lax.ppermute(weight, "node", swap) for weight in weights]
     own = bring_in(weights)
 
@@ -235,11 +242,14 @@
     behind = [[None, halves[3]], [None, halves[2]]]
     parts = {}
 
-    def work(names, blocks, after=(), **how):
+    def work(names, blocks, after=()):
         held = [parts[name] for name in after]
         blocks, held = lax.optimization_barrier((blocks, held))
         parts.update(zip(after, held))
-        parts.update(zip(names, expert_parts(ring, half, expert, blocks, own, other, **how)))
+        marks = names[::2] if len(blocks) < len(names) else names
+        marks = [(offset, h * half) for offset, h in marks]
+        shares = expert_parts(marks, ring, half, chip, table, blocks, own, other)
+        parts.update(zip(names, shares))
         return names
 
     def send(s, wave, after):
@@ -253,7 +263,7 @@
     for wave in range(2):
         send(2, wave, [])
     names = [(offset, h) for offset in (0, -1, 1) for h in range(2)]
-    done = [work(names, [rows, *near])]
+    done = [work(names, [tokens, *near])]
     for s in range(3, far + 1):
         for wave in range(2):
             if s < far or wave == 0:
@@ -285,10 +295,10 @@
     last = [pass_on(late, shares(late, far))]
     for k in range(2, far + 1):
         if k < far:
-            first = pass_on(early, add(shares(early, far - k), first, cost=AHEAD))
+            first = pass_on(early, add(shares(early, far - k), first))
             after = []
         else:
-            first = add(shares(early, 0), first, dtype=jnp.float32, cost=AHEAD)
+            first = add(shares(early, 0), first, dtype=jnp.float32)
             after = first
         terms = shares(late, far - k + 1)
         if k == far - 1:

time: 156 us -> 161 us (1.032)
  blocking collectives: 0 us -> 23.7 us
  waiting for transfers between devices: 75.4 us -> 59.2 us
    all_to_all x0 -> x1, blocking collectives: none -> 23.7 us  [body(): lax.all_to_all(gate_table(ring, expert_ids, gate_codes), 'node', split_ax...]
    ppermute x2, waiting for transfers between devices: 16.2 us -> 0.01 us  [the longest x1 0.01 us: body(): lax.ppermute(tokens, 'node', forward)]
    ppermute x3, waiting for transfers between devices: 0.01 us -> 6.38 us  [body(): other = [lax.ppermute(weight, 'node', swap) for weight in weights]]
    ppermute x5, waiting for transfers between devices: 6.57 us -> 0.85 us  [send(): behind[wave].append(lax.ppermute(pair[1], 'node', backward))]
    ppermute x5, starting transfers between devices: 7.94 us -> 2.94 us  [send(): ahead[wave].append(lax.ppermute(pair[0], 'node', forward))]
    ppermute x5, starting transfers between devices: 2.25 us -> 6.47 us  [send(): behind[wave].append(lax.ppermute(pair[1], 'node', backward))]
  transfers between devices with their start and end apart: 33 -> 33, of which waited for: 24 -> 17; matrix products, arithmetic and copies ran while one was open for 0% -> 0% of each run, Pallas kernels for 24% -> 24%
where the time goes in v11:
time: 161 us
  waiting for transfers between devices  59.2 us (37%)
  Pallas kernels  39.1 us (24%)
  starting transfers between devices  31.6 us (20%)
  blocking collectives  23.7 us (15%)
  local copies, waits for them, and re-layouts  7.48 us (5%)
    ppermute x18, waiting for transfers between devices, pass_on(): lax.ppermute(t, 'node', ways[sign])  47.1 us
    pallas_call x6, Pallas kernels, expert_parts(): pl.pallas_call(functools.partial(expert_kernel, marks, ring, dim, half),...  36.4 us
    all_to_all x1, blocking collectives, body(): lax.all_to_all(gate_table(ring, expert_ids, gate_codes), 'node', split_ax...  23.7 us
    ppermute x18, starting transfers between devices, pass_on(): lax.ppermute(t, 'node', ways[sign])  18.6 us
    unnamed x12, local copies, waits for them, and re-layouts  7.48 us
    ppermute x5, starting transfers between devices, send(): behind[wave].append(lax.ppermute(pair[1], 'node', backward))  6.47 us
    ppermute x3, waiting for transfers between devices, body(): other = [lax.ppermute(weight, 'node', swap) for weight in weights]  6.38 us
    ppermute x5, waiting for transfers between devices, send(): ahead[wave].append(lax.ppermute(pair[0], 'node', forward))  4.86 us
  transfers between devices with their start and end apart: 33, of which 17 were waited for; matrix products, arithmetic and copies ran while one was open for 0% of the time, Pallas kernels for 24%

profile of v11, /device:TPU:0, one launch (start us, length us, event | category | flops | bytes accessed | tf_op | source)
XLA Modules:
  0.0 161.2 jit_solution(1148893231477387000)
XLA Ops:
  0.0 3.0 %collective-permute-start.1 = (bf16[128,3584]{1,0:T(8,128)(2,1)}, bf16[128,3584]{1,0:T(8,128)(2,1)S(1)}, u32[]{:S(2)}, u32[]{:S(2)}) collective-permute-start(bf16[128,3584]{1,0:T(8,128)(2,1)} %refs_0_.1), channel_id=1, source_target_pairs={{0,2},{1,3},{4,0},{5,1},{8,4},{9,5},{12,8},{13,9},{14,12},{15,13},... | collective-permute-start | bytes 2752520 | tf_op jit(solution)/shard_map/ppermute | solution.py:225
  3.0 0.7 copy-done.4
  3.7 0.7 copy-done.5
  4.4 23.7 %all_to_all.12 = f32[8,1,128]{2,1,0:T(1,128)S(1)} all-to-all(f32[8,1,128]{2,1,0:T(1,128)S(1)} %bitcast.13), channel_id=1, replica_groups={{0,2,4,6,8,10,12,14},{1,3,5,7,9,11,13,15},{16,18,20,22,24,26,28,30},{17..., dimensions={0} | all-to-all | bytes 8192 | tf_op jit(solution)/shard_map/all_to_all | solution.py:227
  28.6 2.0 %copy-done = bf16[3584,512]{1,0:T(8,128)(2,1)S(1)} copy-done((bf16[3584,512]{1,0:T(8,128)(2,1)S(1)}, bf16[3584,512]{1,0:T(8,128)(2,1)}, u32[]{:S(2)}) %copy-start) | copy-done | bytes 3670040
  30.6 2.0 %copy-done.1 = bf16[3584,512]{1,0:T(8,128)(2,1)S(1)} copy-done((bf16[3584,512]{1,0:T(8,128)(2,1)S(1)}, bf16[3584,512]{1,0:T(8,128)(2,1)}, u32[]{:S(2)}) %copy-start.1) | copy-done | bytes 3670040
  32.7 2.0 %copy-done.2 = bf16[512,3584]{1,0:T(8,128)(2,1)S(1)} copy-done((bf16[512,3584]{1,0:T(8,128)(2,1)S(1)}, bf16[512,3584]{1,0:T(8,128)(2,1)}, u32[]{:S(2)}) %copy-start.2) | copy-done | bytes 3670040
  34.7 0.8 shard_map.65
  36.2 1.5 collective-permute-start.3
  38.2 1.7 %collective-permute-done.5.refs_7_.refs_6_ = bf16[3584,512]{1,0:T(8,128)(2,1)S(1)} collective-permute-done((bf16[3584,512]{1,0:T(8,128)(2,1)}, bf16[3584,512]{1,0:T(8,128)(2,1)S(1)}, u32[]{:S(2)}, u32[]{:S(2)}) %collective-permute-start.5) | collective-permute-done | bytes 3670048 | tf_op jit(solution)/shard_map/ppermute | solution.py:236
  40.5 4.7 %collective-permute-done.6.refs_8_.refs_7_ = bf16[512,3584]{1,0:T(8,128)(2,1)S(1)} collective-permute-done((bf16[512,3584]{1,0:T(8,128)(2,1)}, bf16[512,3584]{1,0:T(8,128)(2,1)S(1)}, u32[]{:S(2)}, u32[]{:S(2)}) %collective-permute-start.6) | collective-permute-done | bytes 3670048 | tf_op jit(solution)/shard_map/ppermute | solution.py:236
  45.2 10.8 %shard_map.67 = (bf16[64,3584]{1,0:T(8,128)(2,1)S(1)}, bf16[64,3584]{1,0:T(8,128)(2,1)S(1)}, bf16[64,3584]{1,0:T(8,128)(2,1)S(1)}, bf16[64,3584]{1,0:T(8,128)(2,...) custom-call(s32[1]{0:T(128)} %bitcast.chip_ref, f32[8,128]{1,0:T(8,128)S(1)} %bitcast.7, ...), custom_call_target="tpu_custom_call" | custom-call | flops 1024 | bytes 1024 | tf_op jit(solution)/shard_map/pallas_call | solution.py:77
  56.6 1.5 collective-permute-start.12
  58.1 5.1 %shard_map.68 = (bf16[64,3584]{1,0:T(8,128)(2,1)S(1)}, bf16[64,3584]{1,0:T(8,128)(2,1)S(1)}) custom-call(s32[1]{0:T(128)} %bitcast.chip_ref, f32[8,128]{1,0:T(8,128)S(1)} %bitcast.8, bf16[64,3584]{1,0:T(8,128)(2,1)S(1)} %collective-permute-done.2.refs_0_, bf16[64,3584]{1,0:T(8,128)(2,1)S(1)} %collective-permute-done.3.refs_1_, ...), custom_call_target="tpu_custom_call" | custom-call | flops 1024 | bytes 1024 | tf_op jit(solution)/shard_map/pallas_call | solution.py:77
  63.2 0.6 collective-permute-start.9
  63.8 1.5 collective-permute-start.10
  65.3 5.1 %shard_map.69 = (bf16[64,3584]{1,0:T(8,128)(2,1)S(1)}, bf16[64,3584]{1,0:T(8,128)(2,1)S(1)}) custom-call(s32[1]{0:T(128)} %bitcast.chip_ref, f32[8,128]{1,0:T(8,128)S(1)} %bitcast.9, bf16[64,3584]{1,0:T(8,128)(2,1)S(1)} %collective-permute-done.7.refs_0_, bf16[64,3584]{1,0:T(8,128)(2,1)S(1)} %collective-permute-done.8.refs_1_, ...), custom_call_target="tpu_custom_call" | custom-call | flops 1024 | bytes 1024 | tf_op jit(solution)/shard_map/pallas_call | solution.py:77
  70.5 0.6 collective-permute-start.13
  71.1 1.5 collective-permute-start.14
  72.5 5.1 %shard_map.70 = (bf16[64,3584]{1,0:T(8,128)(2,1)S(1)}, bf16[64,3584]{1,0:T(8,128)(2,1)S(1)}) custom-call(s32[1]{0:T(128)} %bitcast.chip_ref, f32[8,128]{1,0:T(8,128)S(1)} %bitcast.10, bf16[64,3584]{1,0:T(8,128)(2,1)S(1)} %collective-permute-done.11.refs_0_, bf16[64,3584]{1,0:T(8,128)(2,1)S(1)} %collective-permute-done.12.refs_1_, ...), custom_call_target="tpu_custom_call" | custom-call | flops 1024 | bytes 1024 | tf_op jit(solution)/shard_map/pallas_call | solution.py:77
  77.7 1.6 collective-permute-done.9.refs_0_
  79.8 5.1 %shard_map.71 = (bf16[64,3584]{1,0:T(8,128)(2,1)S(1)}, bf16[64,3584]{1,0:T(8,128)(2,1)S(1)}) custom-call(s32[1]{0:T(128)} %bitcast.chip_ref, f32[8,128]{1,0:T(8,128)S(1)} %bitcast.11, bf16[64,3584]{1,0:T(8,128)(2,1)S(1)} %collective-permute-done.9.refs_0_, bf16[64,3584]{1,0:T(8,128)(2,1)S(1)} %collective-permute-done.10.refs_1_, ...), custom_call_target="tpu_custom_call" | custom-call | flops 1024 | bytes 1024 | tf_op jit(solution)/shard_map/pallas_call | solution.py:77
  84.9 3.3 %collective-permute-done.13.refs_0_ = bf16[64,3584]{1,0:T(8,128)(2,1)S(1)} collective-permute-done((bf16[64,3584]{1,0:T(8,128)(2,1)S(1)}, bf16[64,3584]{1,0:T(8,128)(2,1)S(1)}, u32[]{:S(2)}, u32[]{:S(2)}) %collective-permute-start.13) | collective-permute-done | bytes 458784 | tf_op jit(solution)/shard_map/ppermute | solution.py:260
  88.5 1.5 collective-permute-start.15
  90.5 5.2 %shard_map.75 = (bf16[64,3584]{1,0:T(8,128)(2,1)S(1)}, bf16[64,3584]{1,0:T(8,128)(2,1)S(1)}) custom-call(s32[1]{0:T(128)} %bitcast.chip_ref, f32[8,128]{1,0:T(8,128)S(1)} %bitcast.12, bf16[64,3584]{1,0:T(8,128)(2,1)S(1)} %collective-permute-done.13.refs_0_, bf16[64,3584]{1,0:T(8,128)(2,1)S(1)} %collective-permute-done.14.refs_1_, ...), custom_call_target="tpu_custom_call" | custom-call | flops 1024 | bytes 1024 | tf_op jit(solution)/shard_map/pallas_call | solution.py:77
  95.7 0.6 collective-permute-start.21
  96.3 1.5 collective-permute-start.22
  97.8 4.2 %collective-permute-done.15.refs_2_ = bf16[64,3584]{1,0:T(8,128)(2,1)S(1)} collective-permute-done((bf16[64,3584]{1,0:T(8,128)(2,1)S(1)}, bf16[64,3584]{1,0:T(8,128)(2,1)S(1)}, u32[]{:S(2)}, u32[]{:S(2)}) %collective-permute-start.15) | collective-permute-done | bytes 458784 | tf_op jit(solution)/shard_map/ppermute | solution.py:289
  102.0 1.5 collective-permute-done.16.refs_3_
  103.5 0.6 collective-permute-start.17
  104.2 1.5 collective-permute-start.18
  105.6 7.7 %collective-permute-done.21.refs_2_ = bf16[64,3584]{1,0:T(8,128)(2,1)S(1)} collective-permute-done((bf16[64,3584]{1,0:T(8,128)(2,1)S(1)}, bf16[64,3584]{1,0:T(8,128)(2,1)S(1)}, u32[]{:S(2)}, u32[]{:S(2)}) %collective-permute-start.21) | collective-permute-done | bytes 458784 | tf_op jit(solution)/shard_map/ppermute | solution.py:289
  114.0 1.5 collective-permute-start.24
  115.5 6.1 %collective-permute-done.17.refs_2_ = bf16[64,3584]{1,0:T(8,128)(2,1)S(1)} collective-permute-done((bf16[64,3584]{1,0:T(8,128)(2,1)S(1)}, bf16[64,3584]{1,0:T(8,128)(2,1)S(1)}, u32[]{:S(2)}, u32[]{:S(2)}) %collective-permute-start.17) | collective-permute-done | bytes 458784 | tf_op jit(solution)/shard_map/ppermute | solution.py:289
  121.6 1.5 collective-permute-done.18.refs_3_
  123.2 0.6 collective-permute-start.19
  123.8 1.5 collective-permute-start.20
  125.3 7.6 %collective-permute-done.23.refs_2_ = bf16[64,3584]{1,0:T(8,128)(2,1)S(1)} collective-permute-done((bf16[64,3584]{1,0:T(8,128)(2,1)S(1)}, bf16[64,3584]{1,0:T(8,128)(2,1)S(1)}, u32[]{:S(2)}, u32[]{:S(2)}) %collective-permute-start.23) | collective-permute-done | bytes 458784 | tf_op jit(solution)/shard_map/ppermute | solution.py:289
  133.6 1.5 collective-permute-start.26
  135.7 5.6 %collective-permute-done.19.refs_2_ = bf16[64,3584]{1,0:T(8,128)(2,1)S(1)} collective-permute-done((bf16[64,3584]{1,0:T(8,128)(2,1)S(1)}, bf16[64,3584]{1,0:T(8,128)(2,1)S(1)}, u32[]{:S(2)}, u32[]{:S(2)}) %collective-permute-start.19) | collective-permute-done | bytes 458784 | tf_op jit(solution)/shard_map/ppermute | solution.py:289
  141.3 1.5 collective-permute-start.30
  143.0 4.7 %collective-permute-done.25.refs_2_ = bf16[32,3584]{1,0:T(8,128)(2,1)S(1)} collective-permute-done((bf16[32,3584]{1,0:T(8,128)(2,1)S(1)}, bf16[32,3584]{1,0:T(8,128)(2,1)S(1)}, u32[]{:S(2)}, u32[]{:S(2)}) %collective-permute-start.25) | collective-permute-done | bytes 229408 | tf_op jit(solution)/shard_map/ppermute | solution.py:289
  148.3 1.5 collective-permute-start.28
  149.8 2.8 %collective-permute-done.29.refs_2_ = bf16[32,3584]{1,0:T(8,128)(2,1)S(1)} collective-permute-done((bf16[32,3584]{1,0:T(8,128)(2,1)S(1)}, bf16[32,3584]{1,0:T(8,128)(2,1)S(1)}, u32[]{:S(2)}, u32[]{:S(2)}) %collective-permute-start.29) | collective-permute-done | bytes 229408 | tf_op jit(solution)/shard_map/ppermute | solution.py:289
  153.3 1.5 collective-permute-start.32
  154.7 2.8 %collective-permute-done.27.refs_2_ = bf16[32,3584]{1,0:T(8,128)(2,1)S(1)} collective-permute-done((bf16[32,3584]{1,0:T(8,128)(2,1)S(1)}, bf16[32,3584]{1,0:T(8,128)(2,1)S(1)}, u32[]{:S(2)}, u32[]{:S(2)}) %collective-permute-start.27) | collective-permute-done | bytes 229408 | tf_op jit(solution)/shard_map/ppermute | solution.py:289
  157.5 2.6 %collective-permute-done.31.refs_4_ = bf16[32,3584]{1,0:T(8,128)(2,1)S(1)} collective-permute-done((bf16[32,3584]{1,0:T(8,128)(2,1)S(1)}, bf16[32,3584]{1,0:T(8,128)(2,1)S(1)}, u32[]{:S(2)}, u32[]{:S(2)}) %collective-permute-start.31) | collective-permute-done | bytes 229408 | tf_op jit(solution)/shard_map/ppermute | solution.py:289
  160.1 1.1 shard_map.80
  (48 shorter events, 8.0 us)
Async XLA Ops:
  0.0 35.5 %collective-permute-start.1 = (bf16[128,3584]{1,0:T(8,128)(2,1)}, bf16[128,3584]{1,0:T(8,128)(2,1)S(1)}, u32[]{:S(2)}, u32[]{:S(2)}) collective-permute-start(bf16[128,3584]{1,0:T(8,128)(2,1)} %refs_0_.1), channel_id=1, source_target_pairs={{0,2},{1,3},{4,0},{5,1},{8,4},{9,5},{12,8},{13,9},{14,12},{15,13},... | collective-permute-start | bytes 2752520 | tf_op jit(solution)/shard_map/ppermute | solution.py:225
  3.0 32.5 %collective-permute-start = (bf16[128,3584]{1,0:T(8,128)(2,1)}, bf16[128,3584]{1,0:T(8,128)(2,1)S(1)}, u32[]{:S(2)}, u32[]{:S(2)}) collective-permute-start(bf16[128,3584]{1,0:T(8,128)(2,1)} %refs_0_.1), channel_id=1, source_target_pairs={{0,4},{1,5},{4,8},{5,9},{8,12},{9,13},{12,14},{13,15},{14,10},{15,... | collective-permute-start | bytes 2752520 | tf_op jit(solution)/shard_map/ppermute | solution.py:225
  3.0 0.7 copy-start.4
  3.7 0.7 copy-start.5
  28.1 9.6 %collective-permute-start.4 = (bf16[3584,512]{1,0:T(8,128)(2,1)}, bf16[3584,512]{1,0:T(8,128)(2,1)S(1)}, u32[]{:S(2)}, u32[]{:S(2)}) collective-permute-start(bf16[3584,512]{1,0:T(8,128)(2,1)} %refs_0_), channel_id=1, source_target_pairs={{0,1},{1,0},{2,3},{3,2},{4,5},{5,4},{6,7},{7,6},{8,9},{9,8},{10,11... | collective-permute-start | bytes 11010056 | tf_op jit(solution)/shard_map/ppermute | solution.py:236
  28.1 11.9 %collective-permute-start.5 = (bf16[3584,512]{1,0:T(8,128)(2,1)}, bf16[3584,512]{1,0:T(8,128)(2,1)S(1)}, u32[]{:S(2)}, u32[]{:S(2)}) collective-permute-start(bf16[3584,512]{1,0:T(8,128)(2,1)} %refs_1_), channel_id=1, source_target_pairs={{0,1},{1,0},{2,3},{3,2},{4,5},{5,4},{6,7},{7,6},{8,9},{9,8},{10,11... | collective-permute-start | bytes 11010056 | tf_op jit(solution)/shard_map/ppermute | solution.py:236
  28.6 16.6 %collective-permute-start.6 = (bf16[512,3584]{1,0:T(8,128)(2,1)}, bf16[512,3584]{1,0:T(8,128)(2,1)S(1)}, u32[]{:S(2)}, u32[]{:S(2)}) collective-permute-start(bf16[512,3584]{1,0:T(8,128)(2,1)} %refs_2_), channel_id=1, source_target_pairs={{0,1},{1,0},{2,3},{3,2},{4,5},{5,4},{6,7},{7,6},{8,9},{9,8},{10,11... | collective-permute-start | bytes 11010056 | tf_op jit(solution)/shard_map/ppermute | solution.py:236
  28.6 2.0 %copy-start = (bf16[3584,512]{1,0:T(8,128)(2,1)S(1)}, bf16[3584,512]{1,0:T(8,128)(2,1)}, u32[]{:S(2)}) copy-start(bf16[3584,512]{1,0:T(8,128)(2,1)} %refs_0_) | copy-start | bytes 11010052
  30.6 2.0 %copy-start.1 = (bf16[3584,512]{1,0:T(8,128)(2,1)S(1)}, bf16[3584,512]{1,0:T(8,128)(2,1)}, u32[]{:S(2)}) copy-start(bf16[3584,512]{1,0:T(8,128)(2,1)} %refs_1_) | copy-start | bytes 11010052
  32.7 2.0 %copy-start.2 = (bf16[512,3584]{1,0:T(8,128)(2,1)S(1)}, bf16[512,3584]{1,0:T(8,128)(2,1)}, u32[]{:S(2)}) copy-start(bf16[512,3584]{1,0:T(8,128)(2,1)} %refs_2_) | copy-start | bytes 11010052
  35.5 9.7 %copy-start.3 = (bf16[128,3584]{1,0:T(8,128)(2,1)S(1)}, bf16[128,3584]{1,0:T(8,128)(2,1)}, u32[]{:S(2)}) copy-start(bf16[128,3584]{1,0:T(8,128)(2,1)} %refs_0_.1) | copy-start | bytes 2752516
  35.6 20.3 %collective-permute-start.2 = (bf16[64,3584]{1,0:T(8,128)(2,1)S(1)}, bf16[64,3584]{1,0:T(8,128)(2,1)S(1)}, u32[]{:S(2)}, u32[]{:S(2)}) collective-permute-start(bf16[64,3584]{1,0:T(8,128)(2,1)S(1)} %get-tuple-element.113), channel_id=1, source_target_pairs={{0,4},{1,5},{4,8},{5,9},{8,12},{9,13},{12,14},{13,15},{14,10},{15,... | collective-permute-start | bytes 1376264 | tf_op jit(solution)/shard_map/ppermute | solution.py:260
  36.2 19.8 %collective-permute-start.3 = (bf16[64,3584]{1,0:T(8,128)(2,1)S(1)}, bf16[64,3584]{1,0:T(8,128)(2,1)S(1)}, u32[]{:S(2)}, u32[]{:S(2)}) collective-permute-start(bf16[64,3584]{1,0:T(8,128)(2,1)S(1)} %get-tuple-element.114), channel_id=1, source_target_pairs={{0,2},{1,3},{4,0},{5,1},{8,4},{9,5},{12,8},{13,9},{14,12},{15,13},... | collective-permute-start | bytes 1376264 | tf_op jit(solution)/shard_map/ppermute | solution.py:261
  37.7 25.5 %collective-permute-start.7 = (bf16[64,3584]{1,0:T(8,128)(2,1)S(1)}, bf16[64,3584]{1,0:T(8,128)(2,1)S(1)}, u32[]{:S(2)}, u32[]{:S(2)}) collective-permute-start(bf16[64,3584]{1,0:T(8,128)(2,1)S(1)} %get-tuple-element.135), channel_id=1, source_target_pairs={{0,4},{1,5},{4,8},{5,9},{8,12},{9,13},{12,14},{13,15},{14,10},{15,... | collective-permute-start | bytes 1376264 | tf_op jit(solution)/shard_map/ppermute | solution.py:260
  39.9 23.3 %collective-permute-start.8 = (bf16[64,3584]{1,0:T(8,128)(2,1)S(1)}, bf16[64,3584]{1,0:T(8,128)(2,1)S(1)}, u32[]{:S(2)}, u32[]{:S(2)}) collective-permute-start(bf16[64,3584]{1,0:T(8,128)(2,1)S(1)} %get-tuple-element.136), channel_id=1, source_target_pairs={{0,2},{1,3},{4,0},{5,1},{8,4},{9,5},{12,8},{13,9},{14,12},{15,13},... | collective-permute-start | bytes 1376264 | tf_op jit(solution)/shard_map/ppermute | solution.py:261
  56.0 14.5 %collective-permute-start.11 = (bf16[64,3584]{1,0:T(8,128)(2,1)S(1)}, bf16[64,3584]{1,0:T(8,128)(2,1)S(1)}, u32[]{:S(2)}, u32[]{:S(2)}) collective-permute-start(bf16[64,3584]{1,0:T(8,128)(2,1)S(1)} %collective-permute-done.2.refs_0_), channel_id=1, source_target_pairs={{0,4},{1,5},{4,8},{5,9},{8,12},{9,13},{12,14},{13,15},{14,10},{15,... | collective-permute-start | bytes 1376264 | tf_op jit(solution)/shard_map/ppermute | solution.py:260
  56.6 13.9 %collective-permute-start.12 = (bf16[64,3584]{1,0:T(8,128)(2,1)S(1)}, bf16[64,3584]{1,0:T(8,128)(2,1)S(1)}, u32[]{:S(2)}, u32[]{:S(2)}) collective-permute-start(bf16[64,3584]{1,0:T(8,128)(2,1)S(1)} %collective-permute-done.3.refs_1_), channel_id=1, source_target_pairs={{0,2},{1,3},{4,0},{5,1},{8,4},{9,5},{12,8},{13,9},{14,12},{15,13},... | collective-permute-start | bytes 1376264 | tf_op jit(solution)/shard_map/ppermute | solution.py:261
  63.2 16.0 %collective-permute-start.9 = (bf16[64,3584]{1,0:T(8,128)(2,1)S(1)}, bf16[64,3584]{1,0:T(8,128)(2,1)S(1)}, u32[]{:S(2)}, u32[]{:S(2)}) collective-permute-start(bf16[64,3584]{1,0:T(8,128)(2,1)S(1)} %collective-permute-done.7.refs_0_), channel_id=1, source_target_pairs={{0,4},{1,5},{4,8},{5,9},{8,12},{9,13},{12,14},{13,15},{14,10},{15,... | collective-permute-start | bytes 1376264 | tf_op jit(solution)/shard_map/ppermute | solution.py:260
  63.8 16.0 %collective-permute-start.10 = (bf16[64,3584]{1,0:T(8,128)(2,1)S(1)}, bf16[64,3584]{1,0:T(8,128)(2,1)S(1)}, u32[]{:S(2)}, u32[]{:S(2)}) collective-permute-start(bf16[64,3584]{1,0:T(8,128)(2,1)S(1)} %collective-permute-done.8.refs_1_), channel_id=1, source_target_pairs={{0,2},{1,3},{4,0},{5,1},{8,4},{9,5},{12,8},{13,9},{14,12},{15,13},... | collective-permute-start | bytes 1376264 | tf_op jit(solution)/shard_map/ppermute | solution.py:261
  70.5 17.8 %collective-permute-start.13 = (bf16[64,3584]{1,0:T(8,128)(2,1)S(1)}, bf16[64,3584]{1,0:T(8,128)(2,1)S(1)}, u32[]{:S(2)}, u32[]{:S(2)}) collective-permute-start(bf16[64,3584]{1,0:T(8,128)(2,1)S(1)} %collective-permute-done.11.refs_0_), channel_id=1, source_target_pairs={{0,4},{1,5},{4,8},{5,9},{8,12},{9,13},{12,14},{13,15},{14,10},{15,... | collective-permute-start | bytes 1376264 | tf_op jit(solution)/shard_map/ppermute | solution.py:260
  71.1 17.5 %collective-permute-start.14 = (bf16[64,3584]{1,0:T(8,128)(2,1)S(1)}, bf16[64,3584]{1,0:T(8,128)(2,1)S(1)}, u32[]{:S(2)}, u32[]{:S(2)}) collective-permute-start(bf16[64,3584]{1,0:T(8,128)(2,1)S(1)} %collective-permute-done.12.refs_1_), channel_id=1, source_target_pairs={{0,2},{1,3},{4,0},{5,1},{8,4},{9,5},{12,8},{13,9},{14,12},{15,13},... | collective-permute-start | bytes 1376264 | tf_op jit(solution)/shard_map/ppermute | solution.py:261
  88.5 13.5 %collective-permute-start.15 = (bf16[64,3584]{1,0:T(8,128)(2,1)S(1)}, bf16[64,3584]{1,0:T(8,128)(2,1)S(1)}, u32[]{:S(2)}, u32[]{:S(2)}) collective-permute-start(bf16[64,3584]{1,0:T(8,128)(2,1)S(1)} %get-tuple-element.165), channel_id=1, source_target_pairs={{0,2},{1,3},{4,0},{5,1},{8,4},{9,5},{12,8},{13,9},{14,12},{15,13},... | collective-permute-start | bytes 1376264 | tf_op jit(solution)/shard_map/ppermute | solution.py:289
  90.0 13.5 %collective-permute-start.16 = (bf16[64,3584]{1,0:T(8,128)(2,1)S(1)}, bf16[64,3584]{1,0:T(8,128)(2,1)S(1)}, u32[]{:S(2)}, u32[]{:S(2)}) collective-permute-start(bf16[64,3584]{1,0:T(8,128)(2,1)S(1)} %get-tuple-element.166), channel_id=1, source_target_pairs={{0,4},{1,5},{4,8},{5,9},{8,12},{9,13},{12,14},{13,15},{14,10},{15,... | collective-permute-start | bytes 1376264 | tf_op jit(solution)/shard_map/ppermute | solution.py:289
  95.7 17.6 %collective-permute-start.21 = (bf16[64,3584]{1,0:T(8,128)(2,1)S(1)}, bf16[64,3584]{1,0:T(8,128)(2,1)S(1)}, u32[]{:S(2)}, u32[]{:S(2)}) collective-permute-start(bf16[64,3584]{1,0:T(8,128)(2,1)S(1)} %get-tuple-element.181), channel_id=1, source_target_pairs={{0,4},{1,5},{4,8},{5,9},{8,12},{9,13},{12,14},{13,15},{14,10},{15,... | collective-permute-start | bytes 1376264 | tf_op jit(solution)/shard_map/ppermute | solution.py:289
  96.3 17.0 %collective-permute-start.22 = (bf16[64,3584]{1,0:T(8,128)(2,1)S(1)}, bf16[64,3584]{1,0:T(8,128)(2,1)S(1)}, u32[]{:S(2)}, u32[]{:S(2)}) collective-permute-start(bf16[64,3584]{1,0:T(8,128)(2,1)S(1)} %get-tuple-element.182), channel_id=1, source_target_pairs={{0,2},{1,3},{4,0},{5,1},{8,4},{9,5},{12,8},{13,9},{14,12},{15,13},... | collective-permute-start | bytes 1376264 | tf_op jit(solution)/shard_map/ppermute | solution.py:289
  103.5 18.1 %collective-permute-start.17 = (bf16[64,3584]{1,0:T(8,128)(2,1)S(1)}, bf16[64,3584]{1,0:T(8,128)(2,1)S(1)}, u32[]{:S(2)}, u32[]{:S(2)}) collective-permute-start(bf16[64,3584]{1,0:T(8,128)(2,1)S(1)} %get-tuple-element.167), channel_id=1, source_target_pairs={{0,2},{1,3},{4,0},{5,1},{8,4},{9,5},{12,8},{13,9},{14,12},{15,13},... | collective-permute-start | bytes 1376264 | tf_op jit(solution)/shard_map/ppermute | solution.py:289
  104.2 19.0 %collective-permute-start.18 = (bf16[64,3584]{1,0:T(8,128)(2,1)S(1)}, bf16[64,3584]{1,0:T(8,128)(2,1)S(1)}, u32[]{:S(2)}, u32[]{:S(2)}) collective-permute-start(bf16[64,3584]{1,0:T(8,128)(2,1)S(1)} %get-tuple-element.168), channel_id=1, source_target_pairs={{0,4},{1,5},{4,8},{5,9},{8,12},{9,13},{12,14},{13,15},{14,10},{15,... | collective-permute-start | bytes 1376264 | tf_op jit(solution)/shard_map/ppermute | solution.py:289
  113.4 19.5 %collective-permute-start.23 = (bf16[64,3584]{1,0:T(8,128)(2,1)S(1)}, bf16[64,3584]{1,0:T(8,128)(2,1)S(1)}, u32[]{:S(2)}, u32[]{:S(2)}) collective-permute-start(bf16[64,3584]{1,0:T(8,128)(2,1)S(1)} %get-tuple-element.183), channel_id=1, source_target_pairs={{0,4},{1,5},{4,8},{5,9},{8,12},{9,13},{12,14},{13,15},{14,10},{15,... | collective-permute-start | bytes 1376264 | tf_op jit(solution)/shard_map/ppermute | solution.py:289
  114.0 18.9 %collective-permute-start.24 = (bf16[64,3584]{1,0:T(8,128)(2,1)S(1)}, bf16[64,3584]{1,0:T(8,128)(2,1)S(1)}, u32[]{:S(2)}, u32[]{:S(2)}) collective-permute-start(bf16[64,3584]{1,0:T(8,128)(2,1)S(1)} %get-tuple-element.184), channel_id=1, source_target_pairs={{0,2},{1,3},{4,0},{5,1},{8,4},{9,5},{12,8},{13,9},{14,12},{15,13},... | collective-permute-start | bytes 1376264 | tf_op jit(solution)/shard_map/ppermute | solution.py:289
  123.2 18.1 %collective-permute-start.19 = (bf16[64,3584]{1,0:T(8,128)(2,1)S(1)}, bf16[64,3584]{1,0:T(8,128)(2,1)S(1)}, u32[]{:S(2)}, u32[]{:S(2)}) collective-permute-start(bf16[64,3584]{1,0:T(8,128)(2,1)S(1)} %get-tuple-element.169), channel_id=1, source_target_pairs={{0,2},{1,3},{4,0},{5,1},{8,4},{9,5},{12,8},{13,9},{14,12},{15,13},... | collective-permute-start | bytes 1376264 | tf_op jit(solution)/shard_map/ppermute | solution.py:289
  123.8 18.9 %collective-permute-start.20 = (bf16[64,3584]{1,0:T(8,128)(2,1)S(1)}, bf16[64,3584]{1,0:T(8,128)(2,1)S(1)}, u32[]{:S(2)}, u32[]{:S(2)}) collective-permute-start(bf16[64,3584]{1,0:T(8,128)(2,1)S(1)} %get-tuple-element.170), channel_id=1, source_target_pairs={{0,4},{1,5},{4,8},{5,9},{8,12},{9,13},{12,14},{13,15},{14,10},{15,... | collective-permute-start | bytes 1376264 | tf_op jit(solution)/shard_map/ppermute | solution.py:289
  133.0 14.6 %collective-permute-start.25 = (bf16[32,3584]{1,0:T(8,128)(2,1)S(1)}, bf16[32,3584]{1,0:T(8,128)(2,1)S(1)}, u32[]{:S(2)}, u32[]{:S(2)}) collective-permute-start(bf16[32,3584]{1,0:T(8,128)(2,1)S(1)} %get-tuple-element.185), channel_id=1, source_target_pairs={{0,4},{1,5},{4,8},{5,9},{8,12},{9,13},{12,14},{13,15},{14,10},{15,... | collective-permute-start | bytes 688136 | tf_op jit(solution)/shard_map/ppermute | solution.py:289
  133.6 14.1 %collective-permute-start.26 = (bf16[32,3584]{1,0:T(8,128)(2,1)S(1)}, bf16[32,3584]{1,0:T(8,128)(2,1)S(1)}, u32[]{:S(2)}, u32[]{:S(2)}) collective-permute-start(bf16[32,3584]{1,0:T(8,128)(2,1)S(1)} %get-tuple-element.186), channel_id=1, source_target_pairs={{0,2},{1,3},{4,0},{5,1},{8,4},{9,5},{12,8},{13,9},{14,12},{15,13},... | collective-permute-start | bytes 688136 | tf_op jit(solution)/shard_map/ppermute | solution.py:289
  135.1 17.5 %collective-permute-start.29 = (bf16[32,3584]{1,0:T(8,128)(2,1)S(1)}, bf16[32,3584]{1,0:T(8,128)(2,1)S(1)}, u32[]{:S(2)}, u32[]{:S(2)}) collective-permute-start(bf16[32,3584]{1,0:T(8,128)(2,1)S(1)} %get-tuple-element.189), channel_id=1, source_target_pairs={{0,4},{1,5},{4,8},{5,9},{8,12},{9,13},{12,14},{13,15},{14,10},{15,... | collective-permute-start | bytes 688136 | tf_op jit(solution)/shard_map/ppermute | solution.py:289
  141.3 11.3 %collective-permute-start.30 = (bf16[32,3584]{1,0:T(8,128)(2,1)S(1)}, bf16[32,3584]{1,0:T(8,128)(2,1)S(1)}, u32[]{:S(2)}, u32[]{:S(2)}) collective-permute-start(bf16[32,3584]{1,0:T(8,128)(2,1)S(1)} %get-tuple-element.190), channel_id=1, source_target_pairs={{0,2},{1,3},{4,0},{5,1},{8,4},{9,5},{12,8},{13,9},{14,12},{15,13},... | collective-permute-start | bytes 688136 | tf_op jit(solution)/shard_map/ppermute | solution.py:289
  147.7 9.8 %collective-permute-start.27 = (bf16[32,3584]{1,0:T(8,128)(2,1)S(1)}, bf16[32,3584]{1,0:T(8,128)(2,1)S(1)}, u32[]{:S(2)}, u32[]{:S(2)}) collective-permute-start(bf16[32,3584]{1,0:T(8,128)(2,1)S(1)} %get-tuple-element.187), channel_id=1, source_target_pairs={{0,4},{1,5},{4,8},{5,9},{8,12},{9,13},{12,14},{13,15},{14,10},{15,... | collective-permute-start | bytes 688136 | tf_op jit(solution)/shard_map/ppermute | solution.py:289
  148.3 9.2 %collective-permute-start.28 = (bf16[32,3584]{1,0:T(8,128)(2,1)S(1)}, bf16[32,3584]{1,0:T(8,128)(2,1)S(1)}, u32[]{:S(2)}, u32[]{:S(2)}) collective-permute-start(bf16[32,3584]{1,0:T(8,128)(2,1)S(1)} %get-tuple-element.188), channel_id=1, source_target_pairs={{0,2},{1,3},{4,0},{5,1},{8,4},{9,5},{12,8},{13,9},{14,12},{15,13},... | collective-permute-start | bytes 688136 | tf_op jit(solution)/shard_map/ppermute | solution.py:289
  152.7 7.4 %collective-permute-start.31 = (bf16[32,3584]{1,0:T(8,128)(2,1)S(1)}, bf16[32,3584]{1,0:T(8,128)(2,1)S(1)}, u32[]{:S(2)}, u32[]{:S(2)}) collective-permute-start(bf16[32,3584]{1,0:T(8,128)(2,1)S(1)} %get-tuple-element.191), channel_id=1, source_target_pairs={{0,4},{1,5},{4,8},{5,9},{8,12},{9,13},{12,14},{13,15},{14,10},{15,... | collective-permute-start | bytes 688136 | tf_op jit(solution)/shard_map/ppermute | solution.py:289
  153.3 6.9 %collective-permute-start.32 = (bf16[32,3584]{1,0:T(8,128)(2,1)S(1)}, bf16[32,3584]{1,0:T(8,128)(2,1)S(1)}, u32[]{:S(2)}, u32[]{:S(2)}) collective-permute-start(bf16[32,3584]{1,0:T(8,128)(2,1)S(1)} %get-tuple-element.192), channel_id=1, source_target_pairs={{0,2},{1,3},{4,0},{5,1},{8,4},{9,5},{12,8},{13,9},{14,12},{15,13},... | collective-permute-start | bytes 688136 | tf_op jit(solution)/shard_map/ppermute | solution.py:289

commit v12 on v11

--- a/solution.py
+++ b/solution.py
@@ -223,6 +223,7 @@
     tokens, weights, chip = lax.optimization_barrier((tokens, weights, chip))
 
     near = [lax.ppermute(tokens, "node", forward), lax.ppermute(tokens, "node", backward)]
+    other = [lax.ppermute(weight, "node", swap) for weight in weights]
     rails = [[SPAN * c + core for c in range(ring)] for core in range(SPAN)]
     table = lax.all_to_all(
         gate_table(ring, expert_ids, gate_codes),
@@ -232,11 +233,9 @@
         axis_index_groups=rails,
         tiled=True,
     )
-    weights, table = lax.optimization_barrier((weights, table))
-    other = [lax.ppermute(weight, "node", swap) for weight in weights]
+    near, weights, other, table = lax.optimization_barrier((near, weights, other, table))
     own = bring_in(weights)
 
-    near, own = lax.optimization_barrier((near, own))
     halves = split(near)
     ahead = [[None, halves[0]], [None, halves[1]]]
     behind = [[None, halves[3]], [None, halves[2]]]
@@ -263,14 +262,14 @@
     for wave in range(2):
         send(2, wave, [])
     names = [(offset, h) for offset in (0, -1, 1) for h in range(2)]
-    done = [work(names, [tokens, *near])]
+    done = [[], work(names, [tokens, *near])]
     for s in range(3, far + 1):
         for wave in range(2):
             if s < far or wave == 0:
                 send(s, wave, done.pop(0))
             names = [(1 - s, wave), (s - 1, 1 - wave)]
-            after = done[-1] if s == far and wave == 1 else []
-            done.append(work(names, [ahead[wave][s - 1], behind[wave][s - 1]], after))
+            blocks = [ahead[wave][s - 1], behind[wave][s - 1]]
+            done.append(work(names, blocks, done[-1]))
     work([(far, 0), (far, 1)], [ahead[0][far], behind[0][far]], done[-1])
     parts[-far, 1] = parts[far, 1]
 

time: 161 us -> 154 us (0.957)
  local copies, waits for them, and re-layouts: 7.48 us -> 1.38 us
  waiting for transfers between devices: 59.2 us -> 56 us
    ppermute x3, waiting for transfers between devices: 6.38 us -> 0.01 us  [body(): other = [lax.ppermute(weight, 'node', swap) for weight in weights]]
    unnamed x12, local copies, waits for them, and re-layouts: 7.48 us -> 1.38 us
    ppermute x5, waiting for transfers between devices: 4.86 us -> 9.41 us  [send(): ahead[wave].append(lax.ppermute(pair[0], 'node', forward))]
  transfers between devices with their start and end apart: 33 -> 33, of which waited for: 17 -> 15; matrix products, arithmetic and copies ran while one was open for 0% -> 0% of each run, Pallas kernels for 24% -> 25%
where the time goes in v12:
time: 154 us; the launch traced here: 153 us
  waiting for transfers between devices  56 us (36%)
  Pallas kernels  39.1 us (25%)
  starting transfers between devices  32.5 us (21%)
  blocking collectives  24.3 us (16%)
    ppermute x18, waiting for transfers between devices, pass_on(): lax.ppermute(t, 'node', ways[sign])  46 us
    pallas_call x6, Pallas kernels, expert_parts(): pl.pallas_call(functools.partial(expert_kernel, marks, ring, dim, half),...  36.4 us
    all_to_all x1, blocking collectives, body(): lax.all_to_all(gate_table(ring, expert_ids, gate_codes), 'node', split_ax...  24.3 us
    ppermute x18, starting transfers between devices, pass_on(): lax.ppermute(t, 'node', ways[sign])  18.6 us
    ppermute x5, waiting for transfers between devices, send(): ahead[wave].append(lax.ppermute(pair[0], 'node', forward))  9.41 us
    ppermute x5, starting transfers between devices, send(): behind[wave].append(lax.ppermute(pair[1], 'node', backward))  7.3 us
  transfers between devices with their start and end apart: 33, of which 15 were waited for; matrix products, arithmetic and copies ran while one was open for 0% of the time, Pallas kernels for 25%

profile of v12, /device:TPU:0, one launch (start us, length us, event | category | flops | bytes accessed | tf_op | source)
XLA Modules:
  0.0 153.5 jit_solution(16212473942498855881)
XLA Ops:
  1.0 2.5 %collective-permute-start.1 = (bf16[128,3584]{1,0:T(8,128)(2,1)}, bf16[128,3584]{1,0:T(8,128)(2,1)S(1)}, u32[]{:S(2)}, u32[]{:S(2)}) collective-permute-start(bf16[128,3584]{1,0:T(8,128)(2,1)} %refs_0_.1), channel_id=1, source_target_pairs={{0,2},{1,3},{4,0},{5,1},{8,4},{9,5},{12,8},{13,9},{14,12},{15,13},... | collective-permute-start | bytes 2752520 | tf_op jit(solution)/shard_map/ppermute | solution.py:225
  3.5 0.7 copy-done.4
  4.2 0.7 copy-done.5
  4.9 24.3 %all_to_all.12 = f32[8,1,128]{2,1,0:T(1,128)S(1)} all-to-all(f32[8,1,128]{2,1,0:T(1,128)S(1)} %bitcast.13), channel_id=1, replica_groups={{0,2,4,6,8,10,12,14},{1,3,5,7,9,11,13,15},{16,18,20,22,24,26,28,30},{17..., dimensions={0} | all-to-all | bytes 8192 | tf_op jit(solution)/shard_map/all_to_all | solution.py:228
  30.0 1.5 collective-permute-start.8
  32.1 1.5 collective-permute-start.6
  33.6 9.4 %collective-permute-done.7.refs_0_ = bf16[64,3584]{1,0:T(8,128)(2,1)S(1)} collective-permute-done((bf16[64,3584]{1,0:T(8,128)(2,1)S(1)}, bf16[64,3584]{1,0:T(8,128)(2,1)S(1)}, u32[]{:S(2)}, u32[]{:S(2)}) %collective-permute-start.7) | collective-permute-done | bytes 458784 | tf_op jit(solution)/shard_map/ppermute | solution.py:259
  44.1 1.4 collective-permute-start.10
  45.5 0.8 shard_map.66
  46.3 10.8 %shard_map.67 = (bf16[64,3584]{1,0:T(8,128)(2,1)S(1)}, bf16[64,3584]{1,0:T(8,128)(2,1)S(1)}, bf16[64,3584]{1,0:T(8,128)(2,1)S(1)}, bf16[64,3584]{1,0:T(8,128)(2,...) custom-call(s32[1]{0:T(128)} %bitcast.chip_ref, f32[8,128]{1,0:T(8,128)S(1)} %bitcast.7, ...), custom_call_target="tpu_custom_call" | custom-call | flops 1024 | bytes 1024 | tf_op jit(solution)/shard_map/pallas_call | solution.py:77
  57.1 0.6 collective-permute-start.11
  57.7 1.4 collective-permute-start.12
  59.2 5.1 %shard_map.68 = (bf16[64,3584]{1,0:T(8,128)(2,1)S(1)}, bf16[64,3584]{1,0:T(8,128)(2,1)S(1)}) custom-call(s32[1]{0:T(128)} %bitcast.chip_ref, f32[8,128]{1,0:T(8,128)S(1)} %bitcast.8, bf16[64,3584]{1,0:T(8,128)(2,1)S(1)} %collective-permute-done.7.refs_0_, bf16[64,3584]{1,0:T(8,128)(2,1)S(1)} %collective-permute-done.8.refs_1_, ...), custom_call_target="tpu_custom_call" | custom-call | flops 1024 | bytes 1024 | tf_op jit(solution)/shard_map/pallas_call | solution.py:77
  64.3 0.6 collective-permute-start.13
  65.0 1.4 collective-permute-start.14
  66.4 5.1 %shard_map.69 = (bf16[64,3584]{1,0:T(8,128)(2,1)S(1)}, bf16[64,3584]{1,0:T(8,128)(2,1)S(1)}) custom-call(s32[1]{0:T(128)} %bitcast.chip_ref, f32[8,128]{1,0:T(8,128)S(1)} %bitcast.9, bf16[64,3584]{1,0:T(8,128)(2,1)S(1)} %collective-permute-done.5.refs_0_, bf16[64,3584]{1,0:T(8,128)(2,1)S(1)} %collective-permute-done.6.refs_1_, ...), custom_call_target="tpu_custom_call" | custom-call | flops 1024 | bytes 1024 | tf_op jit(solution)/shard_map/pallas_call | solution.py:77
  71.6 5.1 %shard_map.70 = (bf16[64,3584]{1,0:T(8,128)(2,1)S(1)}, bf16[64,3584]{1,0:T(8,128)(2,1)S(1)}) custom-call(s32[1]{0:T(128)} %bitcast.chip_ref, f32[8,128]{1,0:T(8,128)S(1)} %bitcast.10, bf16[64,3584]{1,0:T(8,128)(2,1)S(1)} %collective-permute-done.9.refs_0_, bf16[64,3584]{1,0:T(8,128)(2,1)S(1)} %collective-permute-done.10.refs_1_, ...), custom_call_target="tpu_custom_call" | custom-call | flops 1024 | bytes 1024 | tf_op jit(solution)/shard_map/pallas_call | solution.py:77
  76.7 5.1 %shard_map.71 = (bf16[64,3584]{1,0:T(8,128)(2,1)S(1)}, bf16[64,3584]{1,0:T(8,128)(2,1)S(1)}) custom-call(s32[1]{0:T(128)} %bitcast.chip_ref, f32[8,128]{1,0:T(8,128)S(1)} %bitcast.11, bf16[64,3584]{1,0:T(8,128)(2,1)S(1)} %collective-permute-done.11.refs_0_, bf16[64,3584]{1,0:T(8,128)(2,1)S(1)} %collective-permute-done.12.refs_1_, ...), custom_call_target="tpu_custom_call" | custom-call | flops 1024 | bytes 1024 | tf_op jit(solution)/shard_map/pallas_call | solution.py:77
  81.9 1.5 %collective-permute-start.15 = (bf16[64,3584]{1,0:T(8,128)(2,1)S(1)}, bf16[64,3584]{1,0:T(8,128)(2,1)S(1)}, u32[]{:S(2)}, u32[]{:S(2)}) collective-permute-start(bf16[64,3584]{1,0:T(8,128)(2,1)S(1)} %get-tuple-element.181), channel_id=1, source_target_pairs={{0,2},{1,3},{4,0},{5,1},{8,4},{9,5},{12,8},{13,9},{14,12},{15,13},... | collective-permute-start | bytes 1376264 | tf_op jit(solution)/shard_map/ppermute | solution.py:288
  84.0 5.1 %shard_map.75 = (bf16[64,3584]{1,0:T(8,128)(2,1)S(1)}, bf16[64,3584]{1,0:T(8,128)(2,1)S(1)}) custom-call(s32[1]{0:T(128)} %bitcast.chip_ref, f32[8,128]{1,0:T(8,128)S(1)} %bitcast.12, bf16[64,3584]{1,0:T(8,128)(2,1)S(1)} %collective-permute-done.13.refs_0_, bf16[64,3584]{1,0:T(8,128)(2,1)S(1)} %collective-permute-done.14.refs_1_, ...), custom_call_target="tpu_custom_call" | custom-call | flops 1024 | bytes 1024 | tf_op jit(solution)/shard_map/pallas_call | solution.py:77
  89.1 0.6 collective-permute-start.21
  89.7 1.4 collective-permute-start.22
  91.2 2.6 %collective-permute-done.15.refs_2_ = bf16[64,3584]{1,0:T(8,128)(2,1)S(1)} collective-permute-done((bf16[64,3584]{1,0:T(8,128)(2,1)S(1)}, bf16[64,3584]{1,0:T(8,128)(2,1)S(1)}, u32[]{:S(2)}, u32[]{:S(2)}) %collective-permute-start.15) | collective-permute-done | bytes 458784 | tf_op jit(solution)/shard_map/ppermute | solution.py:288
  93.8 2.7 %collective-permute-done.16.refs_3_ = bf16[64,3584]{1,0:T(8,128)(2,1)S(1)} collective-permute-done((bf16[64,3584]{1,0:T(8,128)(2,1)S(1)}, bf16[64,3584]{1,0:T(8,128)(2,1)S(1)}, u32[]{:S(2)}, u32[]{:S(2)}) %collective-permute-start.16) | collective-permute-done | bytes 458784 | tf_op jit(solution)/shard_map/ppermute | solution.py:288
  96.7 2.0 %collective-permute-start.18 = (bf16[64,3584]{1,0:T(8,128)(2,1)S(1)}, bf16[64,3584]{1,0:T(8,128)(2,1)S(1)}, u32[]{:S(2)}, u32[]{:S(2)}) collective-permute-start(bf16[64,3584]{1,0:T(8,128)(2,1)S(1)} %get-tuple-element.184), channel_id=1, source_target_pairs={{0,4},{1,5},{4,8},{5,9},{8,12},{9,13},{12,14},{13,15},{14,10},{15,... | collective-permute-start | bytes 1376264 | tf_op jit(solution)/shard_map/ppermute | solution.py:288
  98.7 7.7 %collective-permute-done.21.refs_2_ = bf16[64,3584]{1,0:T(8,128)(2,1)S(1)} collective-permute-done((bf16[64,3584]{1,0:T(8,128)(2,1)S(1)}, bf16[64,3584]{1,0:T(8,128)(2,1)S(1)}, u32[]{:S(2)}, u32[]{:S(2)}) %collective-permute-start.21) | collective-permute-done | bytes 458784 | tf_op jit(solution)/shard_map/ppermute | solution.py:288
  106.4 0.6 collective-permute-start.23
  107.1 1.4 collective-permute-start.24
  108.5 4.9 %collective-permute-done.17.refs_2_ = bf16[64,3584]{1,0:T(8,128)(2,1)S(1)} collective-permute-done((bf16[64,3584]{1,0:T(8,128)(2,1)S(1)}, bf16[64,3584]{1,0:T(8,128)(2,1)S(1)}, u32[]{:S(2)}, u32[]{:S(2)}) %collective-permute-start.17) | collective-permute-done | bytes 458784 | tf_op jit(solution)/shard_map/ppermute | solution.py:288
  113.5 2.7 %collective-permute-done.18.refs_3_ = bf16[64,3584]{1,0:T(8,128)(2,1)S(1)} collective-permute-done((bf16[64,3584]{1,0:T(8,128)(2,1)S(1)}, bf16[64,3584]{1,0:T(8,128)(2,1)S(1)}, u32[]{:S(2)}, u32[]{:S(2)}) %collective-permute-start.18) | collective-permute-done | bytes 458784 | tf_op jit(solution)/shard_map/ppermute | solution.py:288
  116.3 2.0 %collective-permute-start.20 = (bf16[64,3584]{1,0:T(8,128)(2,1)S(1)}, bf16[64,3584]{1,0:T(8,128)(2,1)S(1)}, u32[]{:S(2)}, u32[]{:S(2)}) collective-permute-start(bf16[64,3584]{1,0:T(8,128)(2,1)S(1)} %get-tuple-element.186), channel_id=1, source_target_pairs={{0,4},{1,5},{4,8},{5,9},{8,12},{9,13},{12,14},{13,15},{14,10},{15,... | collective-permute-start | bytes 1376264 | tf_op jit(solution)/shard_map/ppermute | solution.py:288
  118.4 7.6 %collective-permute-done.23.refs_2_ = bf16[64,3584]{1,0:T(8,128)(2,1)S(1)} collective-permute-done((bf16[64,3584]{1,0:T(8,128)(2,1)S(1)}, bf16[64,3584]{1,0:T(8,128)(2,1)S(1)}, u32[]{:S(2)}, u32[]{:S(2)}) %collective-permute-start.23) | collective-permute-done | bytes 458784 | tf_op jit(solution)/shard_map/ppermute | solution.py:288
  126.1 0.6 collective-permute-start.25
  126.8 1.4 collective-permute-start.26
  128.2 0.6 collective-permute-start.29
  128.8 4.3 %collective-permute-done.19.refs_2_ = bf16[64,3584]{1,0:T(8,128)(2,1)S(1)} collective-permute-done((bf16[64,3584]{1,0:T(8,128)(2,1)S(1)}, bf16[64,3584]{1,0:T(8,128)(2,1)S(1)}, u32[]{:S(2)}, u32[]{:S(2)}) %collective-permute-start.19) | collective-permute-done | bytes 458784 | tf_op jit(solution)/shard_map/ppermute | solution.py:288
  133.1 1.4 collective-permute-start.30
  134.5 1.3 collective-permute-done.20.refs_3_
  136.0 4.7 %collective-permute-done.25.refs_2_ = bf16[32,3584]{1,0:T(8,128)(2,1)S(1)} collective-permute-done((bf16[32,3584]{1,0:T(8,128)(2,1)S(1)}, bf16[32,3584]{1,0:T(8,128)(2,1)S(1)}, u32[]{:S(2)}, u32[]{:S(2)}) %collective-permute-start.25) | collective-permute-done | bytes 229408 | tf_op jit(solution)/shard_map/ppermute | solution.py:288
  140.8 0.6 collective-permute-start.27
  141.4 1.4 collective-permute-start.28
  142.9 2.8 %collective-permute-done.29.refs_2_ = bf16[32,3584]{1,0:T(8,128)(2,1)S(1)} collective-permute-done((bf16[32,3584]{1,0:T(8,128)(2,1)S(1)}, bf16[32,3584]{1,0:T(8,128)(2,1)S(1)}, u32[]{:S(2)}, u32[]{:S(2)}) %collective-permute-start.29) | collective-permute-done | bytes 229408 | tf_op jit(solution)/shard_map/ppermute | solution.py:288
  145.7 0.6 collective-permute-start.31
  146.4 1.4 collective-permute-start.32
  147.8 0.9 collective-permute-done.27.refs_2_
  148.7 3.1 %collective-permute-done.31.refs_4_ = bf16[32,3584]{1,0:T(8,128)(2,1)S(1)} collective-permute-done((bf16[32,3584]{1,0:T(8,128)(2,1)S(1)}, bf16[32,3584]{1,0:T(8,128)(2,1)S(1)}, u32[]{:S(2)}, u32[]{:S(2)}) %collective-permute-start.31) | collective-permute-done | bytes 229408 | tf_op jit(solution)/shard_map/ppermute | solution.py:288
  151.8 0.6 collective-permute-done.32.refs_5_
  152.4 1.1 shard_map.80
  (48 shorter events, 4.8 us)
Async XLA Ops:
  0.0 29.3 %collective-permute-start.2 = (bf16[3584,512]{1,0:T(8,128)(2,1)}, bf16[3584,512]{1,0:T(8,128)(2,1)S(1)}, u32[]{:S(2)}, u32[]{:S(2)}) collective-permute-start(bf16[3584,512]{1,0:T(8,128)(2,1)} %refs_0_), channel_id=1, source_target_pairs={{0,1},{1,0},{2,3},{3,2},{4,5},{5,4},{6,7},{7,6},{8,9},{9,8},{10,11... | collective-permute-start | bytes 11010056 | tf_op jit(solution)/shard_map/ppermute | solution.py:226
  0.5 28.8 %collective-permute-start.3 = (bf16[3584,512]{1,0:T(8,128)(2,1)}, bf16[3584,512]{1,0:T(8,128)(2,1)S(1)}, u32[]{:S(2)}, u32[]{:S(2)}) collective-permute-start(bf16[3584,512]{1,0:T(8,128)(2,1)} %refs_1_), channel_id=1, source_target_pairs={{0,1},{1,0},{2,3},{3,2},{4,5},{5,4},{6,7},{7,6},{8,9},{9,8},{10,11... | collective-permute-start | bytes 11010056 | tf_op jit(solution)/shard_map/ppermute | solution.py:226
  0.5 28.8 %collective-permute-start.4 = (bf16[512,3584]{1,0:T(8,128)(2,1)}, bf16[512,3584]{1,0:T(8,128)(2,1)S(1)}, u32[]{:S(2)}, u32[]{:S(2)}) collective-permute-start(bf16[512,3584]{1,0:T(8,128)(2,1)} %refs_2_), channel_id=1, source_target_pairs={{0,1},{1,0},{2,3},{3,2},{4,5},{5,4},{6,7},{7,6},{8,9},{9,8},{10,11... | collective-permute-start | bytes 11010056 | tf_op jit(solution)/shard_map/ppermute | solution.py:226
  1.0 28.3 %collective-permute-start.1 = (bf16[128,3584]{1,0:T(8,128)(2,1)}, bf16[128,3584]{1,0:T(8,128)(2,1)S(1)}, u32[]{:S(2)}, u32[]{:S(2)}) collective-permute-start(bf16[128,3584]{1,0:T(8,128)(2,1)} %refs_0_.1), channel_id=1, source_target_pairs={{0,2},{1,3},{4,0},{5,1},{8,4},{9,5},{12,8},{13,9},{14,12},{15,13},... | collective-permute-start | bytes 2752520 | tf_op jit(solution)/shard_map/ppermute | solution.py:225
  3.5 25.8 %collective-permute-start = (bf16[128,3584]{1,0:T(8,128)(2,1)}, bf16[128,3584]{1,0:T(8,128)(2,1)S(1)}, u32[]{:S(2)}, u32[]{:S(2)}) collective-permute-start(bf16[128,3584]{1,0:T(8,128)(2,1)} %refs_0_.1), channel_id=1, source_target_pairs={{0,4},{1,5},{4,8},{5,9},{8,12},{9,13},{12,14},{13,15},{14,10},{15,... | collective-permute-start | bytes 2752520 | tf_op jit(solution)/shard_map/ppermute | solution.py:225
  3.5 0.7 copy-start.4
  4.2 0.7 copy-start.5
  29.3 16.2 %copy-start = (bf16[3584,512]{1,0:T(8,128)(2,1)S(1)}, bf16[3584,512]{1,0:T(8,128)(2,1)}, u32[]{:S(2)}) copy-start(bf16[3584,512]{1,0:T(8,128)(2,1)} %refs_0_) | copy-start | bytes 11010052
  29.3 16.2 %copy-start.1 = (bf16[3584,512]{1,0:T(8,128)(2,1)S(1)}, bf16[3584,512]{1,0:T(8,128)(2,1)}, u32[]{:S(2)}) copy-start(bf16[3584,512]{1,0:T(8,128)(2,1)} %refs_1_) | copy-start | bytes 11010052
  29.3 16.2 %copy-start.2 = (bf16[512,3584]{1,0:T(8,128)(2,1)S(1)}, bf16[512,3584]{1,0:T(8,128)(2,1)}, u32[]{:S(2)}) copy-start(bf16[512,3584]{1,0:T(8,128)(2,1)} %refs_2_) | copy-start | bytes 11010052
  29.4 13.5 %collective-permute-start.7 = (bf16[64,3584]{1,0:T(8,128)(2,1)S(1)}, bf16[64,3584]{1,0:T(8,128)(2,1)S(1)}, u32[]{:S(2)}, u32[]{:S(2)}) collective-permute-start(bf16[64,3584]{1,0:T(8,128)(2,1)S(1)} %get-tuple-element.119), channel_id=1, source_target_pairs={{0,4},{1,5},{4,8},{5,9},{8,12},{9,13},{12,14},{13,15},{14,10},{15,... | collective-permute-start | bytes 1376264 | tf_op jit(solution)/shard_map/ppermute | solution.py:259
  30.0 13.5 %collective-permute-start.8 = (bf16[64,3584]{1,0:T(8,128)(2,1)S(1)}, bf16[64,3584]{1,0:T(8,128)(2,1)S(1)}, u32[]{:S(2)}, u32[]{:S(2)}) collective-permute-start(bf16[64,3584]{1,0:T(8,128)(2,1)S(1)} %get-tuple-element.120), channel_id=1, source_target_pairs={{0,2},{1,3},{4,0},{5,1},{8,4},{9,5},{12,8},{13,9},{14,12},{15,13},... | collective-permute-start | bytes 1376264 | tf_op jit(solution)/shard_map/ppermute | solution.py:260
  31.5 14.8 %copy-start.3 = (bf16[128,3584]{1,0:T(8,128)(2,1)S(1)}, bf16[128,3584]{1,0:T(8,128)(2,1)}, u32[]{:S(2)}) copy-start(bf16[128,3584]{1,0:T(8,128)(2,1)} %refs_0_.1) | copy-start | bytes 2752516
  31.5 25.6 %collective-permute-start.5 = (bf16[64,3584]{1,0:T(8,128)(2,1)S(1)}, bf16[64,3584]{1,0:T(8,128)(2,1)S(1)}, u32[]{:S(2)}, u32[]{:S(2)}) collective-permute-start(bf16[64,3584]{1,0:T(8,128)(2,1)S(1)} %get-tuple-element.115), channel_id=1, source_target_pairs={{0,4},{1,5},{4,8},{5,9},{8,12},{9,13},{12,14},{13,15},{14,10},{15,... | collective-permute-start | bytes 1376264 | tf_op jit(solution)/shard_map/ppermute | solution.py:259
  32.1 25.0 %collective-permute-start.6 = (bf16[64,3584]{1,0:T(8,128)(2,1)S(1)}, bf16[64,3584]{1,0:T(8,128)(2,1)S(1)}, u32[]{:S(2)}, u32[]{:S(2)}) collective-permute-start(bf16[64,3584]{1,0:T(8,128)(2,1)S(1)} %get-tuple-element.116), channel_id=1, source_target_pairs={{0,2},{1,3},{4,0},{5,1},{8,4},{9,5},{12,8},{13,9},{14,12},{15,13},... | collective-permute-start | bytes 1376264 | tf_op jit(solution)/shard_map/ppermute | solution.py:260
  43.5 20.8 %collective-permute-start.9 = (bf16[64,3584]{1,0:T(8,128)(2,1)S(1)}, bf16[64,3584]{1,0:T(8,128)(2,1)S(1)}, u32[]{:S(2)}, u32[]{:S(2)}) collective-permute-start(bf16[64,3584]{1,0:T(8,128)(2,1)S(1)} %collective-permute-done.7.refs_0_), channel_id=1, source_target_pairs={{0,4},{1,5},{4,8},{5,9},{8,12},{9,13},{12,14},{13,15},{14,10},{15,... | collective-permute-start | bytes 1376264 | tf_op jit(solution)/shard_map/ppermute | solution.py:259
  44.1 20.3 %collective-permute-start.10 = (bf16[64,3584]{1,0:T(8,128)(2,1)S(1)}, bf16[64,3584]{1,0:T(8,128)(2,1)S(1)}, u32[]{:S(2)}, u32[]{:S(2)}) collective-permute-start(bf16[64,3584]{1,0:T(8,128)(2,1)S(1)} %collective-permute-done.8.refs_1_), channel_id=1, source_target_pairs={{0,2},{1,3},{4,0},{5,1},{8,4},{9,5},{12,8},{13,9},{14,12},{15,13},... | collective-permute-start | bytes 1376264 | tf_op jit(solution)/shard_map/ppermute | solution.py:260
  57.1 19.6 %collective-permute-start.11 = (bf16[64,3584]{1,0:T(8,128)(2,1)S(1)}, bf16[64,3584]{1,0:T(8,128)(2,1)S(1)}, u32[]{:S(2)}, u32[]{:S(2)}) collective-permute-start(bf16[64,3584]{1,0:T(8,128)(2,1)S(1)} %collective-permute-done.5.refs_0_), channel_id=1, source_target_pairs={{0,4},{1,5},{4,8},{5,9},{8,12},{9,13},{12,14},{13,15},{14,10},{15,... | collective-permute-start | bytes 1376264 | tf_op jit(solution)/shard_map/ppermute | solution.py:259
  57.7 19.0 %collective-permute-start.12 = (bf16[64,3584]{1,0:T(8,128)(2,1)S(1)}, bf16[64,3584]{1,0:T(8,128)(2,1)S(1)}, u32[]{:S(2)}, u32[]{:S(2)}) collective-permute-start(bf16[64,3584]{1,0:T(8,128)(2,1)S(1)} %collective-permute-done.6.refs_1_), channel_id=1, source_target_pairs={{0,2},{1,3},{4,0},{5,1},{8,4},{9,5},{12,8},{13,9},{14,12},{15,13},... | collective-permute-start | bytes 1376264 | tf_op jit(solution)/shard_map/ppermute | solution.py:260
  64.3 17.5 %collective-permute-start.13 = (bf16[64,3584]{1,0:T(8,128)(2,1)S(1)}, bf16[64,3584]{1,0:T(8,128)(2,1)S(1)}, u32[]{:S(2)}, u32[]{:S(2)}) collective-permute-start(bf16[64,3584]{1,0:T(8,128)(2,1)S(1)} %collective-permute-done.9.refs_0_), channel_id=1, source_target_pairs={{0,4},{1,5},{4,8},{5,9},{8,12},{9,13},{12,14},{13,15},{14,10},{15,... | collective-permute-start | bytes 1376264 | tf_op jit(solution)/shard_map/ppermute | solution.py:259
  65.0 16.9 %collective-permute-start.14 = (bf16[64,3584]{1,0:T(8,128)(2,1)S(1)}, bf16[64,3584]{1,0:T(8,128)(2,1)S(1)}, u32[]{:S(2)}, u32[]{:S(2)}) collective-permute-start(bf16[64,3584]{1,0:T(8,128)(2,1)S(1)} %collective-permute-done.10.refs_1_), channel_id=1, source_target_pairs={{0,2},{1,3},{4,0},{5,1},{8,4},{9,5},{12,8},{13,9},{14,12},{15,13},... | collective-permute-start | bytes 1376264 | tf_op jit(solution)/shard_map/ppermute | solution.py:260
  81.9 11.9 %collective-permute-start.15 = (bf16[64,3584]{1,0:T(8,128)(2,1)S(1)}, bf16[64,3584]{1,0:T(8,128)(2,1)S(1)}, u32[]{:S(2)}, u32[]{:S(2)}) collective-permute-start(bf16[64,3584]{1,0:T(8,128)(2,1)S(1)} %get-tuple-element.181), channel_id=1, source_target_pairs={{0,2},{1,3},{4,0},{5,1},{8,4},{9,5},{12,8},{13,9},{14,12},{15,13},... | collective-permute-start | bytes 1376264 | tf_op jit(solution)/shard_map/ppermute | solution.py:288
  83.4 13.1 %collective-permute-start.16 = (bf16[64,3584]{1,0:T(8,128)(2,1)S(1)}, bf16[64,3584]{1,0:T(8,128)(2,1)S(1)}, u32[]{:S(2)}, u32[]{:S(2)}) collective-permute-start(bf16[64,3584]{1,0:T(8,128)(2,1)S(1)} %get-tuple-element.182), channel_id=1, source_target_pairs={{0,4},{1,5},{4,8},{5,9},{8,12},{9,13},{12,14},{13,15},{14,10},{15,... | collective-permute-start | bytes 1376264 | tf_op jit(solution)/shard_map/ppermute | solution.py:288
  89.1 17.2 %collective-permute-start.21 = (bf16[64,3584]{1,0:T(8,128)(2,1)S(1)}, bf16[64,3584]{1,0:T(8,128)(2,1)S(1)}, u32[]{:S(2)}, u32[]{:S(2)}) collective-permute-start(bf16[64,3584]{1,0:T(8,128)(2,1)S(1)} %get-tuple-element.197), channel_id=1, source_target_pairs={{0,4},{1,5},{4,8},{5,9},{8,12},{9,13},{12,14},{13,15},{14,10},{15,... | collective-permute-start | bytes 1376264 | tf_op jit(solution)/shard_map/ppermute | solution.py:288
  89.7 16.6 %collective-permute-start.22 = (bf16[64,3584]{1,0:T(8,128)(2,1)S(1)}, bf16[64,3584]{1,0:T(8,128)(2,1)S(1)}, u32[]{:S(2)}, u32[]{:S(2)}) collective-permute-start(bf16[64,3584]{1,0:T(8,128)(2,1)S(1)} %get-tuple-element.198), channel_id=1, source_target_pairs={{0,2},{1,3},{4,0},{5,1},{8,4},{9,5},{12,8},{13,9},{14,12},{15,13},... | collective-permute-start | bytes 1376264 | tf_op jit(solution)/shard_map/ppermute | solution.py:288
  96.6 16.9 %collective-permute-start.17 = (bf16[64,3584]{1,0:T(8,128)(2,1)S(1)}, bf16[64,3584]{1,0:T(8,128)(2,1)S(1)}, u32[]{:S(2)}, u32[]{:S(2)}) collective-permute-start(bf16[64,3584]{1,0:T(8,128)(2,1)S(1)} %get-tuple-element.183), channel_id=1, source_target_pairs={{0,2},{1,3},{4,0},{5,1},{8,4},{9,5},{12,8},{13,9},{14,12},{15,13},... | collective-permute-start | bytes 1376264 | tf_op jit(solution)/shard_map/ppermute | solution.py:288
  96.7 19.5 %collective-permute-start.18 = (bf16[64,3584]{1,0:T(8,128)(2,1)S(1)}, bf16[64,3584]{1,0:T(8,128)(2,1)S(1)}, u32[]{:S(2)}, u32[]{:S(2)}) collective-permute-start(bf16[64,3584]{1,0:T(8,128)(2,1)S(1)} %get-tuple-element.184), channel_id=1, source_target_pairs={{0,4},{1,5},{4,8},{5,9},{8,12},{9,13},{12,14},{13,15},{14,10},{15,... | collective-permute-start | bytes 1376264 | tf_op jit(solution)/shard_map/ppermute | solution.py:288
  106.4 19.6 %collective-permute-start.23 = (bf16[64,3584]{1,0:T(8,128)(2,1)S(1)}, bf16[64,3584]{1,0:T(8,128)(2,1)S(1)}, u32[]{:S(2)}, u32[]{:S(2)}) collective-permute-start(bf16[64,3584]{1,0:T(8,128)(2,1)S(1)} %get-tuple-element.199), channel_id=1, source_target_pairs={{0,4},{1,5},{4,8},{5,9},{8,12},{9,13},{12,14},{13,15},{14,10},{15,... | collective-permute-start | bytes 1376264 | tf_op jit(solution)/shard_map/ppermute | solution.py:288
  107.1 18.9 %collective-permute-start.24 = (bf16[64,3584]{1,0:T(8,128)(2,1)S(1)}, bf16[64,3584]{1,0:T(8,128)(2,1)S(1)}, u32[]{:S(2)}, u32[]{:S(2)}) collective-permute-start(bf16[64,3584]{1,0:T(8,128)(2,1)S(1)} %get-tuple-element.200), channel_id=1, source_target_pairs={{0,2},{1,3},{4,0},{5,1},{8,4},{9,5},{12,8},{13,9},{14,12},{15,13},... | collective-permute-start | bytes 1376264 | tf_op jit(solution)/shard_map/ppermute | solution.py:288
  116.3 16.8 %collective-permute-start.19 = (bf16[64,3584]{1,0:T(8,128)(2,1)S(1)}, bf16[64,3584]{1,0:T(8,128)(2,1)S(1)}, u32[]{:S(2)}, u32[]{:S(2)}) collective-permute-start(bf16[64,3584]{1,0:T(8,128)(2,1)S(1)} %get-tuple-element.185), channel_id=1, source_target_pairs={{0,2},{1,3},{4,0},{5,1},{8,4},{9,5},{12,8},{13,9},{14,12},{15,13},... | collective-permute-start | bytes 1376264 | tf_op jit(solution)/shard_map/ppermute | solution.py:288
  116.3 19.5 %collective-permute-start.20 = (bf16[64,3584]{1,0:T(8,128)(2,1)S(1)}, bf16[64,3584]{1,0:T(8,128)(2,1)S(1)}, u32[]{:S(2)}, u32[]{:S(2)}) collective-permute-start(bf16[64,3584]{1,0:T(8,128)(2,1)S(1)} %get-tuple-element.186), channel_id=1, source_target_pairs={{0,4},{1,5},{4,8},{5,9},{8,12},{9,13},{12,14},{13,15},{14,10},{15,... | collective-permute-start | bytes 1376264 | tf_op jit(solution)/shard_map/ppermute | solution.py:288
  126.1 14.6 %collective-permute-start.25 = (bf16[32,3584]{1,0:T(8,128)(2,1)S(1)}, bf16[32,3584]{1,0:T(8,128)(2,1)S(1)}, u32[]{:S(2)}, u32[]{:S(2)}) collective-permute-start(bf16[32,3584]{1,0:T(8,128)(2,1)S(1)} %get-tuple-element.201), channel_id=1, source_target_pairs={{0,4},{1,5},{4,8},{5,9},{8,12},{9,13},{12,14},{13,15},{14,10},{15,... | collective-permute-start | bytes 688136 | tf_op jit(solution)/shard_map/ppermute | solution.py:288
  126.8 14.0 %collective-permute-start.26 = (bf16[32,3584]{1,0:T(8,128)(2,1)S(1)}, bf16[32,3584]{1,0:T(8,128)(2,1)S(1)}, u32[]{:S(2)}, u32[]{:S(2)}) collective-permute-start(bf16[32,3584]{1,0:T(8,128)(2,1)S(1)} %get-tuple-element.202), channel_id=1, source_target_pairs={{0,2},{1,3},{4,0},{5,1},{8,4},{9,5},{12,8},{13,9},{14,12},{15,13},... | collective-permute-start | bytes 688136 | tf_op jit(solution)/shard_map/ppermute | solution.py:288
  128.2 17.5 %collective-permute-start.29 = (bf16[32,3584]{1,0:T(8,128)(2,1)S(1)}, bf16[32,3584]{1,0:T(8,128)(2,1)S(1)}, u32[]{:S(2)}, u32[]{:S(2)}) collective-permute-start(bf16[32,3584]{1,0:T(8,128)(2,1)S(1)} %get-tuple-element.205), channel_id=1, source_target_pairs={{0,4},{1,5},{4,8},{5,9},{8,12},{9,13},{12,14},{13,15},{14,10},{15,... | collective-permute-start | bytes 688136 | tf_op jit(solution)/shard_map/ppermute | solution.py:288
  133.1 12.5 %collective-permute-start.30 = (bf16[32,3584]{1,0:T(8,128)(2,1)S(1)}, bf16[32,3584]{1,0:T(8,128)(2,1)S(1)}, u32[]{:S(2)}, u32[]{:S(2)}) collective-permute-start(bf16[32,3584]{1,0:T(8,128)(2,1)S(1)} %get-tuple-element.206), channel_id=1, source_target_pairs={{0,2},{1,3},{4,0},{5,1},{8,4},{9,5},{12,8},{13,9},{14,12},{15,13},... | collective-permute-start | bytes 688136 | tf_op jit(solution)/shard_map/ppermute | solution.py:288
  140.8 7.9 %collective-permute-start.27 = (bf16[32,3584]{1,0:T(8,128)(2,1)S(1)}, bf16[32,3584]{1,0:T(8,128)(2,1)S(1)}, u32[]{:S(2)}, u32[]{:S(2)}) collective-permute-start(bf16[32,3584]{1,0:T(8,128)(2,1)S(1)} %get-tuple-element.203), channel_id=1, source_target_pairs={{0,4},{1,5},{4,8},{5,9},{8,12},{9,13},{12,14},{13,15},{14,10},{15,... | collective-permute-start | bytes 688136 | tf_op jit(solution)/shard_map/ppermute | solution.py:288
  141.4 7.2 %collective-permute-start.28 = (bf16[32,3584]{1,0:T(8,128)(2,1)S(1)}, bf16[32,3584]{1,0:T(8,128)(2,1)S(1)}, u32[]{:S(2)}, u32[]{:S(2)}) collective-permute-start(bf16[32,3584]{1,0:T(8,128)(2,1)S(1)} %get-tuple-element.204), channel_id=1, source_target_pairs={{0,2},{1,3},{4,0},{5,1},{8,4},{9,5},{12,8},{13,9},{14,12},{15,13},... | collective-permute-start | bytes 688136 | tf_op jit(solution)/shard_map/ppermute | solution.py:288
  145.7 6.1 %collective-permute-start.31 = (bf16[32,3584]{1,0:T(8,128)(2,1)S(1)}, bf16[32,3584]{1,0:T(8,128)(2,1)S(1)}, u32[]{:S(2)}, u32[]{:S(2)}) collective-permute-start(bf16[32,3584]{1,0:T(8,128)(2,1)S(1)} %get-tuple-element.207), channel_id=1, source_target_pairs={{0,4},{1,5},{4,8},{5,9},{8,12},{9,13},{12,14},{13,15},{14,10},{15,... | collective-permute-start | bytes 688136 | tf_op jit(solution)/shard_map/ppermute | solution.py:288
  146.4 6.0 %collective-permute-start.32 = (bf16[32,3584]{1,0:T(8,128)(2,1)S(1)}, bf16[32,3584]{1,0:T(8,128)(2,1)S(1)}, u32[]{:S(2)}, u32[]{:S(2)}) collective-permute-start(bf16[32,3584]{1,0:T(8,128)(2,1)S(1)} %get-tuple-element.208), channel_id=1, source_target_pairs={{0,2},{1,3},{4,0},{5,1},{8,4},{9,5},{12,8},{13,9},{14,12},{15,13},... | collective-permute-start | bytes 688136 | tf_op jit(solution)/shard_map/ppermute | solution.py:288

commit v13 on v12

--- a/solution.py
+++ b/solution.py
@@ -262,14 +262,14 @@
     for wave in range(2):
         send(2, wave, [])
     names = [(offset, h) for offset in (0, -1, 1) for h in range(2)]
-    done = [[], work(names, [tokens, *near])]
+    done = [work(names, [tokens, *near])]
     for s in range(3, far + 1):
         for wave in range(2):
             if s < far or wave == 0:
                 send(s, wave, done.pop(0))
             names = [(1 - s, wave), (s - 1, 1 - wave)]
             blocks = [ahead[wave][s - 1], behind[wave][s - 1]]
-            done.append(work(names, blocks, done[-1]))
+            done.append(work(names, blocks, done[-1] if done else []))
     work([(far, 0), (far, 1)], [ahead[0][far], behind[0][far]], done[-1])
     parts[-far, 1] = parts[far, 1]
 

time: 154 us -> 153 us (level)
    ppermute x5, waiting for transfers between devices: 9.41 us -> 6.91 us  [send(): ahead[wave].append(lax.ppermute(pair[0], 'node', forward))]
  transfers between devices with their start and end apart: 33 -> 33, of which waited for: 15 -> 21; matrix products, arithmetic and copies ran while one was open for 0% -> 0% of each run, Pallas kernels for 25% -> 25%
where the time goes in v13:
time: 153 us; the launch traced here: 152 us
  waiting for transfers between devices  55.2 us (36%)
  Pallas kernels  39.1 us (26%)
  starting transfers between devices  32.3 us (21%)
  blocking collectives  24.3 us (16%)
    ppermute x18, waiting for transfers between devices, pass_on(): lax.ppermute(t, 'node', ways[sign])  46.4 us
    pallas_call x6, Pallas kernels, expert_parts(): pl.pallas_call(functools.partial(expert_kernel, marks, ring, dim, half),...  36.4 us
    all_to_all x1, blocking collectives, body(): lax.all_to_all(gate_table(ring, expert_ids, gate_codes), 'node', split_ax...  24.3 us
    ppermute x18, starting transfers between devices, pass_on(): lax.ppermute(t, 'node', ways[sign])  18.5 us
    ppermute x5, starting transfers between devices, send(): behind[wave].append(lax.ppermute(pair[1], 'node', backward))  7.35 us
    ppermute x5, waiting for transfers between devices, send(): ahead[wave].append(lax.ppermute(pair[0], 'node', forward))  6.91 us
  transfers between devices with their start and end apart: 33, of which 21 were waited for; matrix products, arithmetic and copies ran while one was open for 0% of the time, Pallas kernels for 25%

profile of v13, /device:TPU:0, one launch (start us, length us, event | category | flops | bytes accessed | tf_op | source)
XLA Modules:
  0.0 152.4 jit_solution(7681816791022570316)
XLA Ops:
  1.0 2.5 %collective-permute-start.1 = (bf16[128,3584]{1,0:T(8,128)(2,1)}, bf16[128,3584]{1,0:T(8,128)(2,1)S(1)}, u32[]{:S(2)}, u32[]{:S(2)}) collective-permute-start(bf16[128,3584]{1,0:T(8,128)(2,1)} %refs_0_.1), channel_id=1, source_target_pairs={{0,2},{1,3},{4,0},{5,1},{8,4},{9,5},{12,8},{13,9},{14,12},{15,13},... | collective-permute-start | bytes 2752520 | tf_op jit(solution)/shard_map/ppermute | solution.py:225
  3.5 0.7 copy-done.4
  4.2 0.7 copy-done.5
  4.9 24.3 %all_to_all.12 = f32[8,1,128]{2,1,0:T(1,128)S(1)} all-to-all(f32[8,1,128]{2,1,0:T(1,128)S(1)} %bitcast.13), channel_id=1, replica_groups={{0,2,4,6,8,10,12,14},{1,3,5,7,9,11,13,15},{16,18,20,22,24,26,28,30},{17..., dimensions={0} | all-to-all | bytes 8192 | tf_op jit(solution)/shard_map/all_to_all | solution.py:228
  29.4 0.6 collective-permute-start.5
  30.0 1.5 collective-permute-start.6
  32.1 1.5 collective-permute-start.8
  33.6 0.8 shard_map.66
  34.3 10.8 %shard_map.67 = (bf16[64,3584]{1,0:T(8,128)(2,1)S(1)}, bf16[64,3584]{1,0:T(8,128)(2,1)S(1)}, bf16[64,3584]{1,0:T(8,128)(2,1)S(1)}, bf16[64,3584]{1,0:T(8,128)(2,...) custom-call(s32[1]{0:T(128)} %bitcast.chip_ref, f32[8,128]{1,0:T(8,128)S(1)} %bitcast.7, ...), custom_call_target="tpu_custom_call" | custom-call | flops 1024 | bytes 1024 | tf_op jit(solution)/shard_map/pallas_call | solution.py:77
  45.1 0.6 collective-permute-start.11
  45.7 1.5 collective-permute-start.12
  47.2 5.1 %shard_map.68 = (bf16[64,3584]{1,0:T(8,128)(2,1)S(1)}, bf16[64,3584]{1,0:T(8,128)(2,1)S(1)}) custom-call(s32[1]{0:T(128)} %bitcast.chip_ref, f32[8,128]{1,0:T(8,128)S(1)} %bitcast.8, bf16[64,3584]{1,0:T(8,128)(2,1)S(1)} %collective-permute-done.5.refs_0_, bf16[64,3584]{1,0:T(8,128)(2,1)S(1)} %collective-permute-done.6.refs_1_, ...), custom_call_target="tpu_custom_call" | custom-call | flops 1024 | bytes 1024 | tf_op jit(solution)/shard_map/pallas_call | solution.py:77
  53.3 0.6 collective-permute-start.9
  53.9 1.4 collective-permute-start.10
  55.4 5.1 %shard_map.69 = (bf16[64,3584]{1,0:T(8,128)(2,1)S(1)}, bf16[64,3584]{1,0:T(8,128)(2,1)S(1)}) custom-call(s32[1]{0:T(128)} %bitcast.chip_ref, f32[8,128]{1,0:T(8,128)S(1)} %bitcast.9, bf16[64,3584]{1,0:T(8,128)(2,1)S(1)} %collective-permute-done.7.refs_0_, bf16[64,3584]{1,0:T(8,128)(2,1)S(1)} %collective-permute-done.8.refs_1_, ...), custom_call_target="tpu_custom_call" | custom-call | flops 1024 | bytes 1024 | tf_op jit(solution)/shard_map/pallas_call | solution.py:77
  60.5 2.1 %collective-permute-done.11.refs_0_ = bf16[64,3584]{1,0:T(8,128)(2,1)S(1)} collective-permute-done((bf16[64,3584]{1,0:T(8,128)(2,1)S(1)}, bf16[64,3584]{1,0:T(8,128)(2,1)S(1)}, u32[]{:S(2)}, u32[]{:S(2)}) %collective-permute-start.11) | collective-permute-done | bytes 458784 | tf_op jit(solution)/shard_map/ppermute | solution.py:259
  63.2 0.6 collective-permute-start.13
  63.7 1.4 collective-permute-start.14
  65.2 5.1 %shard_map.70 = (bf16[64,3584]{1,0:T(8,128)(2,1)S(1)}, bf16[64,3584]{1,0:T(8,128)(2,1)S(1)}) custom-call(s32[1]{0:T(128)} %bitcast.chip_ref, f32[8,128]{1,0:T(8,128)S(1)} %bitcast.10, bf16[64,3584]{1,0:T(8,128)(2,1)S(1)} %collective-permute-done.11.refs_0_, bf16[64,3584]{1,0:T(8,128)(2,1)S(1)} %collective-permute-done.12.refs_1_, ...), custom_call_target="tpu_custom_call" | custom-call | flops 1024 | bytes 1024 | tf_op jit(solution)/shard_map/pallas_call | solution.py:77
  70.3 2.1 %collective-permute-done.9.refs_0_ = bf16[64,3584]{1,0:T(8,128)(2,1)S(1)} collective-permute-done((bf16[64,3584]{1,0:T(8,128)(2,1)S(1)}, bf16[64,3584]{1,0:T(8,128)(2,1)S(1)}, u32[]{:S(2)}, u32[]{:S(2)}) %collective-permute-start.9) | collective-permute-done | bytes 458784 | tf_op jit(solution)/shard_map/ppermute | solution.py:259
  73.0 5.1 %shard_map.71 = (bf16[64,3584]{1,0:T(8,128)(2,1)S(1)}, bf16[64,3584]{1,0:T(8,128)(2,1)S(1)}) custom-call(s32[1]{0:T(128)} %bitcast.chip_ref, f32[8,128]{1,0:T(8,128)S(1)} %bitcast.11, bf16[64,3584]{1,0:T(8,128)(2,1)S(1)} %collective-permute-done.9.refs_0_, bf16[64,3584]{1,0:T(8,128)(2,1)S(1)} %collective-permute-done.10.refs_1_, ...), custom_call_target="tpu_custom_call" | custom-call | flops 1024 | bytes 1024 | tf_op jit(solution)/shard_map/pallas_call | solution.py:77
  78.1 2.2 %collective-permute-done.13.refs_0_ = bf16[64,3584]{1,0:T(8,128)(2,1)S(1)} collective-permute-done((bf16[64,3584]{1,0:T(8,128)(2,1)S(1)}, bf16[64,3584]{1,0:T(8,128)(2,1)S(1)}, u32[]{:S(2)}, u32[]{:S(2)}) %collective-permute-start.13) | collective-permute-done | bytes 458784 | tf_op jit(solution)/shard_map/ppermute | solution.py:259
  80.6 1.5 collective-permute-start.15
  82.6 5.1 %shard_map.75 = (bf16[64,3584]{1,0:T(8,128)(2,1)S(1)}, bf16[64,3584]{1,0:T(8,128)(2,1)S(1)}) custom-call(s32[1]{0:T(128)} %bitcast.chip_ref, f32[8,128]{1,0:T(8,128)S(1)} %bitcast.12, bf16[64,3584]{1,0:T(8,128)(2,1)S(1)} %collective-permute-done.13.refs_0_, bf16[64,3584]{1,0:T(8,128)(2,1)S(1)} %collective-permute-done.14.refs_1_, ...), custom_call_target="tpu_custom_call" | custom-call | flops 1024 | bytes 1024 | tf_op jit(solution)/shard_map/pallas_call | solution.py:77
  87.8 0.7 collective-permute-start.21
  88.4 1.4 collective-permute-start.22
  89.8 4.0 %collective-permute-done.15.refs_2_ = bf16[64,3584]{1,0:T(8,128)(2,1)S(1)} collective-permute-done((bf16[64,3584]{1,0:T(8,128)(2,1)S(1)}, bf16[64,3584]{1,0:T(8,128)(2,1)S(1)}, u32[]{:S(2)}, u32[]{:S(2)}) %collective-permute-start.15) | collective-permute-done | bytes 458784 | tf_op jit(solution)/shard_map/ppermute | solution.py:288
  93.8 1.8 %collective-permute-done.16.refs_3_ = bf16[64,3584]{1,0:T(8,128)(2,1)S(1)} collective-permute-done((bf16[64,3584]{1,0:T(8,128)(2,1)S(1)}, bf16[64,3584]{1,0:T(8,128)(2,1)S(1)}, u32[]{:S(2)}, u32[]{:S(2)}) %collective-permute-start.16) | collective-permute-done | bytes 458784 | tf_op jit(solution)/shard_map/ppermute | solution.py:288
  95.7 0.6 collective-permute-start.17
  96.2 1.5 collective-permute-start.18
  97.7 7.7 %collective-permute-done.21.refs_2_ = bf16[64,3584]{1,0:T(8,128)(2,1)S(1)} collective-permute-done((bf16[64,3584]{1,0:T(8,128)(2,1)S(1)}, bf16[64,3584]{1,0:T(8,128)(2,1)S(1)}, u32[]{:S(2)}, u32[]{:S(2)}) %collective-permute-start.21) | collective-permute-done | bytes 458784 | tf_op jit(solution)/shard_map/ppermute | solution.py:288
  106.1 1.5 collective-permute-start.24
  107.6 5.9 %collective-permute-done.17.refs_2_ = bf16[64,3584]{1,0:T(8,128)(2,1)S(1)} collective-permute-done((bf16[64,3584]{1,0:T(8,128)(2,1)S(1)}, bf16[64,3584]{1,0:T(8,128)(2,1)S(1)}, u32[]{:S(2)}, u32[]{:S(2)}) %collective-permute-start.17) | collective-permute-done | bytes 458784 | tf_op jit(solution)/shard_map/ppermute | solution.py:288
  113.5 1.8 %collective-permute-done.18.refs_3_ = bf16[64,3584]{1,0:T(8,128)(2,1)S(1)} collective-permute-done((bf16[64,3584]{1,0:T(8,128)(2,1)S(1)}, bf16[64,3584]{1,0:T(8,128)(2,1)S(1)}, u32[]{:S(2)}, u32[]{:S(2)}) %collective-permute-start.18) | collective-permute-done | bytes 458784 | tf_op jit(solution)/shard_map/ppermute | solution.py:288
  115.3 0.6 collective-permute-start.19
  115.9 1.5 collective-permute-start.20
  117.4 7.6 %collective-permute-done.23.refs_2_ = bf16[64,3584]{1,0:T(8,128)(2,1)S(1)} collective-permute-done((bf16[64,3584]{1,0:T(8,128)(2,1)S(1)}, bf16[64,3584]{1,0:T(8,128)(2,1)S(1)}, u32[]{:S(2)}, u32[]{:S(2)}) %collective-permute-start.23) | collective-permute-done | bytes 458784 | tf_op jit(solution)/shard_map/ppermute | solution.py:288
  125.7 1.5 collective-permute-start.26
  127.8 5.4 %collective-permute-done.19.refs_2_ = bf16[64,3584]{1,0:T(8,128)(2,1)S(1)} collective-permute-done((bf16[64,3584]{1,0:T(8,128)(2,1)S(1)}, bf16[64,3584]{1,0:T(8,128)(2,1)S(1)}, u32[]{:S(2)}, u32[]{:S(2)}) %collective-permute-start.19) | collective-permute-done | bytes 458784 | tf_op jit(solution)/shard_map/ppermute | solution.py:288
  133.1 1.4 collective-permute-start.30
  135.1 4.7 %collective-permute-done.25.refs_2_ = bf16[32,3584]{1,0:T(8,128)(2,1)S(1)} collective-permute-done((bf16[32,3584]{1,0:T(8,128)(2,1)S(1)}, bf16[32,3584]{1,0:T(8,128)(2,1)S(1)}, u32[]{:S(2)}, u32[]{:S(2)}) %collective-permute-start.25) | collective-permute-done | bytes 229408 | tf_op jit(solution)/shard_map/ppermute | solution.py:288
  140.4 1.5 collective-permute-start.28
  141.9 2.8 %collective-permute-done.29.refs_2_ = bf16[32,3584]{1,0:T(8,128)(2,1)S(1)} collective-permute-done((bf16[32,3584]{1,0:T(8,128)(2,1)S(1)}, bf16[32,3584]{1,0:T(8,128)(2,1)S(1)}, u32[]{:S(2)}, u32[]{:S(2)}) %collective-permute-start.29) | collective-permute-done | bytes 229408 | tf_op jit(solution)/shard_map/ppermute | solution.py:288
  144.8 0.6 collective-permute-start.31
  145.3 1.5 collective-permute-start.32
  146.8 1.8 %collective-permute-done.27.refs_2_ = bf16[32,3584]{1,0:T(8,128)(2,1)S(1)} collective-permute-done((bf16[32,3584]{1,0:T(8,128)(2,1)S(1)}, bf16[32,3584]{1,0:T(8,128)(2,1)S(1)}, u32[]{:S(2)}, u32[]{:S(2)}) %collective-permute-start.27) | collective-permute-done | bytes 229408 | tf_op jit(solution)/shard_map/ppermute | solution.py:288
  148.7 2.5 %collective-permute-done.31.refs_4_ = bf16[32,3584]{1,0:T(8,128)(2,1)S(1)} collective-permute-done((bf16[32,3584]{1,0:T(8,128)(2,1)S(1)}, bf16[32,3584]{1,0:T(8,128)(2,1)S(1)}, u32[]{:S(2)}, u32[]{:S(2)}) %collective-permute-start.31) | collective-permute-done | bytes 229408 | tf_op jit(solution)/shard_map/ppermute | solution.py:288
  151.4 1.1 shard_map.80
  (48 shorter events, 8.0 us)
Async XLA Ops:
  0.0 29.3 %collective-permute-start.2 = (bf16[3584,512]{1,0:T(8,128)(2,1)}, bf16[3584,512]{1,0:T(8,128)(2,1)S(1)}, u32[]{:S(2)}, u32[]{:S(2)}) collective-permute-start(bf16[3584,512]{1,0:T(8,128)(2,1)} %refs_0_), channel_id=1, source_target_pairs={{0,1},{1,0},{2,3},{3,2},{4,5},{5,4},{6,7},{7,6},{8,9},{9,8},{10,11... | collective-permute-start | bytes 11010056 | tf_op jit(solution)/shard_map/ppermute | solution.py:226
  0.5 28.8 %collective-permute-start.3 = (bf16[3584,512]{1,0:T(8,128)(2,1)}, bf16[3584,512]{1,0:T(8,128)(2,1)S(1)}, u32[]{:S(2)}, u32[]{:S(2)}) collective-permute-start(bf16[3584,512]{1,0:T(8,128)(2,1)} %refs_1_), channel_id=1, source_target_pairs={{0,1},{1,0},{2,3},{3,2},{4,5},{5,4},{6,7},{7,6},{8,9},{9,8},{10,11... | collective-permute-start | bytes 11010056 | tf_op jit(solution)/shard_map/ppermute | solution.py:226
  0.5 28.8 %collective-permute-start.4 = (bf16[512,3584]{1,0:T(8,128)(2,1)}, bf16[512,3584]{1,0:T(8,128)(2,1)S(1)}, u32[]{:S(2)}, u32[]{:S(2)}) collective-permute-start(bf16[512,3584]{1,0:T(8,128)(2,1)} %refs_2_), channel_id=1, source_target_pairs={{0,1},{1,0},{2,3},{3,2},{4,5},{5,4},{6,7},{7,6},{8,9},{9,8},{10,11... | collective-permute-start | bytes 11010056 | tf_op jit(solution)/shard_map/ppermute | solution.py:226
  1.0 28.3 %collective-permute-start.1 = (bf16[128,3584]{1,0:T(8,128)(2,1)}, bf16[128,3584]{1,0:T(8,128)(2,1)S(1)}, u32[]{:S(2)}, u32[]{:S(2)}) collective-permute-start(bf16[128,3584]{1,0:T(8,128)(2,1)} %refs_0_.1), channel_id=1, source_target_pairs={{0,2},{1,3},{4,0},{5,1},{8,4},{9,5},{12,8},{13,9},{14,12},{15,13},... | collective-permute-start | bytes 2752520 | tf_op jit(solution)/shard_map/ppermute | solution.py:225
  3.5 25.8 %collective-permute-start = (bf16[128,3584]{1,0:T(8,128)(2,1)}, bf16[128,3584]{1,0:T(8,128)(2,1)S(1)}, u32[]{:S(2)}, u32[]{:S(2)}) collective-permute-start(bf16[128,3584]{1,0:T(8,128)(2,1)} %refs_0_.1), channel_id=1, source_target_pairs={{0,4},{1,5},{4,8},{5,9},{8,12},{9,13},{12,14},{13,15},{14,10},{15,... | collective-permute-start | bytes 2752520 | tf_op jit(solution)/shard_map/ppermute | solution.py:225
  3.5 0.7 copy-start.4
  4.2 0.7 copy-start.5
  29.3 4.3 %copy-start = (bf16[3584,512]{1,0:T(8,128)(2,1)S(1)}, bf16[3584,512]{1,0:T(8,128)(2,1)}, u32[]{:S(2)}) copy-start(bf16[3584,512]{1,0:T(8,128)(2,1)} %refs_0_) | copy-start | bytes 11010052
  29.3 4.3 %copy-start.1 = (bf16[3584,512]{1,0:T(8,128)(2,1)S(1)}, bf16[3584,512]{1,0:T(8,128)(2,1)}, u32[]{:S(2)}) copy-start(bf16[3584,512]{1,0:T(8,128)(2,1)} %refs_1_) | copy-start | bytes 11010052
  29.3 4.3 %copy-start.2 = (bf16[512,3584]{1,0:T(8,128)(2,1)S(1)}, bf16[512,3584]{1,0:T(8,128)(2,1)}, u32[]{:S(2)}) copy-start(bf16[512,3584]{1,0:T(8,128)(2,1)} %refs_2_) | copy-start | bytes 11010052
  29.4 15.7 %collective-permute-start.5 = (bf16[64,3584]{1,0:T(8,128)(2,1)S(1)}, bf16[64,3584]{1,0:T(8,128)(2,1)S(1)}, u32[]{:S(2)}, u32[]{:S(2)}) collective-permute-start(bf16[64,3584]{1,0:T(8,128)(2,1)S(1)} %get-tuple-element.107), channel_id=1, source_target_pairs={{0,4},{1,5},{4,8},{5,9},{8,12},{9,13},{12,14},{13,15},{14,10},{15,... | collective-permute-start | bytes 1376264 | tf_op jit(solution)/shard_map/ppermute | solution.py:259
  30.0 15.1 %collective-permute-start.6 = (bf16[64,3584]{1,0:T(8,128)(2,1)S(1)}, bf16[64,3584]{1,0:T(8,128)(2,1)S(1)}, u32[]{:S(2)}, u32[]{:S(2)}) collective-permute-start(bf16[64,3584]{1,0:T(8,128)(2,1)S(1)} %get-tuple-element.108), channel_id=1, source_target_pairs={{0,2},{1,3},{4,0},{5,1},{8,4},{9,5},{12,8},{13,9},{14,12},{15,13},... | collective-permute-start | bytes 1376264 | tf_op jit(solution)/shard_map/ppermute | solution.py:260
  31.5 2.8 %copy-start.3 = (bf16[128,3584]{1,0:T(8,128)(2,1)S(1)}, bf16[128,3584]{1,0:T(8,128)(2,1)}, u32[]{:S(2)}) copy-start(bf16[128,3584]{1,0:T(8,128)(2,1)} %refs_0_.1) | copy-start | bytes 2752516
  31.5 21.3 %collective-permute-start.7 = (bf16[64,3584]{1,0:T(8,128)(2,1)S(1)}, bf16[64,3584]{1,0:T(8,128)(2,1)S(1)}, u32[]{:S(2)}, u32[]{:S(2)}) collective-permute-start(bf16[64,3584]{1,0:T(8,128)(2,1)S(1)} %get-tuple-element.135), channel_id=1, source_target_pairs={{0,4},{1,5},{4,8},{5,9},{8,12},{9,13},{12,14},{13,15},{14,10},{15,... | collective-permute-start | bytes 1376264 | tf_op jit(solution)/shard_map/ppermute | solution.py:259
  32.1 21.3 %collective-permute-start.8 = (bf16[64,3584]{1,0:T(8,128)(2,1)S(1)}, bf16[64,3584]{1,0:T(8,128)(2,1)S(1)}, u32[]{:S(2)}, u32[]{:S(2)}) collective-permute-start(bf16[64,3584]{1,0:T(8,128)(2,1)S(1)} %get-tuple-element.136), channel_id=1, source_target_pairs={{0,2},{1,3},{4,0},{5,1},{8,4},{9,5},{12,8},{13,9},{14,12},{15,13},... | collective-permute-start | bytes 1376264 | tf_op jit(solution)/shard_map/ppermute | solution.py:260
  45.1 17.5 %collective-permute-start.11 = (bf16[64,3584]{1,0:T(8,128)(2,1)S(1)}, bf16[64,3584]{1,0:T(8,128)(2,1)S(1)}, u32[]{:S(2)}, u32[]{:S(2)}) collective-permute-start(bf16[64,3584]{1,0:T(8,128)(2,1)S(1)} %collective-permute-done.5.refs_0_), channel_id=1, source_target_pairs={{0,4},{1,5},{4,8},{5,9},{8,12},{9,13},{12,14},{13,15},{14,10},{15,... | collective-permute-start | bytes 1376264 | tf_op jit(solution)/shard_map/ppermute | solution.py:259
  45.7 17.4 %collective-permute-start.12 = (bf16[64,3584]{1,0:T(8,128)(2,1)S(1)}, bf16[64,3584]{1,0:T(8,128)(2,1)S(1)}, u32[]{:S(2)}, u32[]{:S(2)}) collective-permute-start(bf16[64,3584]{1,0:T(8,128)(2,1)S(1)} %collective-permute-done.6.refs_1_), channel_id=1, source_target_pairs={{0,2},{1,3},{4,0},{5,1},{8,4},{9,5},{12,8},{13,9},{14,12},{15,13},... | collective-permute-start | bytes 1376264 | tf_op jit(solution)/shard_map/ppermute | solution.py:260
  53.3 19.1 %collective-permute-start.9 = (bf16[64,3584]{1,0:T(8,128)(2,1)S(1)}, bf16[64,3584]{1,0:T(8,128)(2,1)S(1)}, u32[]{:S(2)}, u32[]{:S(2)}) collective-permute-start(bf16[64,3584]{1,0:T(8,128)(2,1)S(1)} %collective-permute-done.7.refs_0_), channel_id=1, source_target_pairs={{0,4},{1,5},{4,8},{5,9},{8,12},{9,13},{12,14},{13,15},{14,10},{15,... | collective-permute-start | bytes 1376264 | tf_op jit(solution)/shard_map/ppermute | solution.py:259
  53.9 19.1 %collective-permute-start.10 = (bf16[64,3584]{1,0:T(8,128)(2,1)S(1)}, bf16[64,3584]{1,0:T(8,128)(2,1)S(1)}, u32[]{:S(2)}, u32[]{:S(2)}) collective-permute-start(bf16[64,3584]{1,0:T(8,128)(2,1)S(1)} %collective-permute-done.8.refs_1_), channel_id=1, source_target_pairs={{0,2},{1,3},{4,0},{5,1},{8,4},{9,5},{12,8},{13,9},{14,12},{15,13},... | collective-permute-start | bytes 1376264 | tf_op jit(solution)/shard_map/ppermute | solution.py:260
  63.2 17.2 %collective-permute-start.13 = (bf16[64,3584]{1,0:T(8,128)(2,1)S(1)}, bf16[64,3584]{1,0:T(8,128)(2,1)S(1)}, u32[]{:S(2)}, u32[]{:S(2)}) collective-permute-start(bf16[64,3584]{1,0:T(8,128)(2,1)S(1)} %collective-permute-done.11.refs_0_), channel_id=1, source_target_pairs={{0,4},{1,5},{4,8},{5,9},{8,12},{9,13},{12,14},{13,15},{14,10},{15,... | collective-permute-start | bytes 1376264 | tf_op jit(solution)/shard_map/ppermute | solution.py:259
  63.7 16.9 %collective-permute-start.14 = (bf16[64,3584]{1,0:T(8,128)(2,1)S(1)}, bf16[64,3584]{1,0:T(8,128)(2,1)S(1)}, u32[]{:S(2)}, u32[]{:S(2)}) collective-permute-start(bf16[64,3584]{1,0:T(8,128)(2,1)S(1)} %collective-permute-done.12.refs_1_), channel_id=1, source_target_pairs={{0,2},{1,3},{4,0},{5,1},{8,4},{9,5},{12,8},{13,9},{14,12},{15,13},... | collective-permute-start | bytes 1376264 | tf_op jit(solution)/shard_map/ppermute | solution.py:260
  80.6 13.2 %collective-permute-start.15 = (bf16[64,3584]{1,0:T(8,128)(2,1)S(1)}, bf16[64,3584]{1,0:T(8,128)(2,1)S(1)}, u32[]{:S(2)}, u32[]{:S(2)}) collective-permute-start(bf16[64,3584]{1,0:T(8,128)(2,1)S(1)} %get-tuple-element.165), channel_id=1, source_target_pairs={{0,2},{1,3},{4,0},{5,1},{8,4},{9,5},{12,8},{13,9},{14,12},{15,13},... | collective-permute-start | bytes 1376264 | tf_op jit(solution)/shard_map/ppermute | solution.py:288
  82.1 13.5 %collective-permute-start.16 = (bf16[64,3584]{1,0:T(8,128)(2,1)S(1)}, bf16[64,3584]{1,0:T(8,128)(2,1)S(1)}, u32[]{:S(2)}, u32[]{:S(2)}) collective-permute-start(bf16[64,3584]{1,0:T(8,128)(2,1)S(1)} %get-tuple-element.166), channel_id=1, source_target_pairs={{0,4},{1,5},{4,8},{5,9},{8,12},{9,13},{12,14},{13,15},{14,10},{15,... | collective-permute-start | bytes 1376264 | tf_op jit(solution)/shard_map/ppermute | solution.py:288
  87.8 17.6 %collective-permute-start.21 = (bf16[64,3584]{1,0:T(8,128)(2,1)S(1)}, bf16[64,3584]{1,0:T(8,128)(2,1)S(1)}, u32[]{:S(2)}, u32[]{:S(2)}) collective-permute-start(bf16[64,3584]{1,0:T(8,128)(2,1)S(1)} %get-tuple-element.181), channel_id=1, source_target_pairs={{0,4},{1,5},{4,8},{5,9},{8,12},{9,13},{12,14},{13,15},{14,10},{15,... | collective-permute-start | bytes 1376264 | tf_op jit(solution)/shard_map/ppermute | solution.py:288
  88.4 17.0 %collective-permute-start.22 = (bf16[64,3584]{1,0:T(8,128)(2,1)S(1)}, bf16[64,3584]{1,0:T(8,128)(2,1)S(1)}, u32[]{:S(2)}, u32[]{:S(2)}) collective-permute-start(bf16[64,3584]{1,0:T(8,128)(2,1)S(1)} %get-tuple-element.182), channel_id=1, source_target_pairs={{0,2},{1,3},{4,0},{5,1},{8,4},{9,5},{12,8},{13,9},{14,12},{15,13},... | collective-permute-start | bytes 1376264 | tf_op jit(solution)/shard_map/ppermute | solution.py:288
  95.7 17.8 %collective-permute-start.17 = (bf16[64,3584]{1,0:T(8,128)(2,1)S(1)}, bf16[64,3584]{1,0:T(8,128)(2,1)S(1)}, u32[]{:S(2)}, u32[]{:S(2)}) collective-permute-start(bf16[64,3584]{1,0:T(8,128)(2,1)S(1)} %get-tuple-element.167), channel_id=1, source_target_pairs={{0,2},{1,3},{4,0},{5,1},{8,4},{9,5},{12,8},{13,9},{14,12},{15,13},... | collective-permute-start | bytes 1376264 | tf_op jit(solution)/shard_map/ppermute | solution.py:288
  96.2 19.0 %collective-permute-start.18 = (bf16[64,3584]{1,0:T(8,128)(2,1)S(1)}, bf16[64,3584]{1,0:T(8,128)(2,1)S(1)}, u32[]{:S(2)}, u32[]{:S(2)}) collective-permute-start(bf16[64,3584]{1,0:T(8,128)(2,1)S(1)} %get-tuple-element.168), channel_id=1, source_target_pairs={{0,4},{1,5},{4,8},{5,9},{8,12},{9,13},{12,14},{13,15},{14,10},{15,... | collective-permute-start | bytes 1376264 | tf_op jit(solution)/shard_map/ppermute | solution.py:288
  105.5 19.6 %collective-permute-start.23 = (bf16[64,3584]{1,0:T(8,128)(2,1)S(1)}, bf16[64,3584]{1,0:T(8,128)(2,1)S(1)}, u32[]{:S(2)}, u32[]{:S(2)}) collective-permute-start(bf16[64,3584]{1,0:T(8,128)(2,1)S(1)} %get-tuple-element.183), channel_id=1, source_target_pairs={{0,4},{1,5},{4,8},{5,9},{8,12},{9,13},{12,14},{13,15},{14,10},{15,... | collective-permute-start | bytes 1376264 | tf_op jit(solution)/shard_map/ppermute | solution.py:288
  106.1 19.0 %collective-permute-start.24 = (bf16[64,3584]{1,0:T(8,128)(2,1)S(1)}, bf16[64,3584]{1,0:T(8,128)(2,1)S(1)}, u32[]{:S(2)}, u32[]{:S(2)}) collective-permute-start(bf16[64,3584]{1,0:T(8,128)(2,1)S(1)} %get-tuple-element.184), channel_id=1, source_target_pairs={{0,2},{1,3},{4,0},{5,1},{8,4},{9,5},{12,8},{13,9},{14,12},{15,13},... | collective-permute-start | bytes 1376264 | tf_op jit(solution)/shard_map/ppermute | solution.py:288
  115.3 17.8 %collective-permute-start.19 = (bf16[64,3584]{1,0:T(8,128)(2,1)S(1)}, bf16[64,3584]{1,0:T(8,128)(2,1)S(1)}, u32[]{:S(2)}, u32[]{:S(2)}) collective-permute-start(bf16[64,3584]{1,0:T(8,128)(2,1)S(1)} %get-tuple-element.169), channel_id=1, source_target_pairs={{0,2},{1,3},{4,0},{5,1},{8,4},{9,5},{12,8},{13,9},{14,12},{15,13},... | collective-permute-start | bytes 1376264 | tf_op jit(solution)/shard_map/ppermute | solution.py:288
  115.9 19.0 %collective-permute-start.20 = (bf16[64,3584]{1,0:T(8,128)(2,1)S(1)}, bf16[64,3584]{1,0:T(8,128)(2,1)S(1)}, u32[]{:S(2)}, u32[]{:S(2)}) collective-permute-start(bf16[64,3584]{1,0:T(8,128)(2,1)S(1)} %get-tuple-element.170), channel_id=1, source_target_pairs={{0,4},{1,5},{4,8},{5,9},{8,12},{9,13},{12,14},{13,15},{14,10},{15,... | collective-permute-start | bytes 1376264 | tf_op jit(solution)/shard_map/ppermute | solution.py:288
  125.2 14.6 %collective-permute-start.25 = (bf16[32,3584]{1,0:T(8,128)(2,1)S(1)}, bf16[32,3584]{1,0:T(8,128)(2,1)S(1)}, u32[]{:S(2)}, u32[]{:S(2)}) collective-permute-start(bf16[32,3584]{1,0:T(8,128)(2,1)S(1)} %get-tuple-element.185), channel_id=1, source_target_pairs={{0,4},{1,5},{4,8},{5,9},{8,12},{9,13},{12,14},{13,15},{14,10},{15,... | collective-permute-start | bytes 688136 | tf_op jit(solution)/shard_map/ppermute | solution.py:288
  125.7 14.1 %collective-permute-start.26 = (bf16[32,3584]{1,0:T(8,128)(2,1)S(1)}, bf16[32,3584]{1,0:T(8,128)(2,1)S(1)}, u32[]{:S(2)}, u32[]{:S(2)}) collective-permute-start(bf16[32,3584]{1,0:T(8,128)(2,1)S(1)} %get-tuple-element.186), channel_id=1, source_target_pairs={{0,2},{1,3},{4,0},{5,1},{8,4},{9,5},{12,8},{13,9},{14,12},{15,13},... | collective-permute-start | bytes 688136 | tf_op jit(solution)/shard_map/ppermute | solution.py:288
  127.2 17.5 %collective-permute-start.29 = (bf16[32,3584]{1,0:T(8,128)(2,1)S(1)}, bf16[32,3584]{1,0:T(8,128)(2,1)S(1)}, u32[]{:S(2)}, u32[]{:S(2)}) collective-permute-start(bf16[32,3584]{1,0:T(8,128)(2,1)S(1)} %get-tuple-element.189), channel_id=1, source_target_pairs={{0,4},{1,5},{4,8},{5,9},{8,12},{9,13},{12,14},{13,15},{14,10},{15,... | collective-permute-start | bytes 688136 | tf_op jit(solution)/shard_map/ppermute | solution.py:288
  133.1 11.6 %collective-permute-start.30 = (bf16[32,3584]{1,0:T(8,128)(2,1)S(1)}, bf16[32,3584]{1,0:T(8,128)(2,1)S(1)}, u32[]{:S(2)}, u32[]{:S(2)}) collective-permute-start(bf16[32,3584]{1,0:T(8,128)(2,1)S(1)} %get-tuple-element.190), channel_id=1, source_target_pairs={{0,2},{1,3},{4,0},{5,1},{8,4},{9,5},{12,8},{13,9},{14,12},{15,13},... | collective-permute-start | bytes 688136 | tf_op jit(solution)/shard_map/ppermute | solution.py:288
  139.9 8.8 %collective-permute-start.27 = (bf16[32,3584]{1,0:T(8,128)(2,1)S(1)}, bf16[32,3584]{1,0:T(8,128)(2,1)S(1)}, u32[]{:S(2)}, u32[]{:S(2)}) collective-permute-start(bf16[32,3584]{1,0:T(8,128)(2,1)S(1)} %get-tuple-element.187), channel_id=1, source_target_pairs={{0,4},{1,5},{4,8},{5,9},{8,12},{9,13},{12,14},{13,15},{14,10},{15,... | collective-permute-start | bytes 688136 | tf_op jit(solution)/shard_map/ppermute | solution.py:288
  140.4 8.3 %collective-permute-start.28 = (bf16[32,3584]{1,0:T(8,128)(2,1)S(1)}, bf16[32,3584]{1,0:T(8,128)(2,1)S(1)}, u32[]{:S(2)}, u32[]{:S(2)}) collective-permute-start(bf16[32,3584]{1,0:T(8,128)(2,1)S(1)} %get-tuple-element.188), channel_id=1, source_target_pairs={{0,2},{1,3},{4,0},{5,1},{8,4},{9,5},{12,8},{13,9},{14,12},{15,13},... | collective-permute-start | bytes 688136 | tf_op jit(solution)/shard_map/ppermute | solution.py:288
  144.8 6.4 %collective-permute-start.31 = (bf16[32,3584]{1,0:T(8,128)(2,1)S(1)}, bf16[32,3584]{1,0:T(8,128)(2,1)S(1)}, u32[]{:S(2)}, u32[]{:S(2)}) collective-permute-start(bf16[32,3584]{1,0:T(8,128)(2,1)S(1)} %get-tuple-element.191), channel_id=1, source_target_pairs={{0,4},{1,5},{4,8},{5,9},{8,12},{9,13},{12,14},{13,15},{14,10},{15,... | collective-permute-start | bytes 688136 | tf_op jit(solution)/shard_map/ppermute | solution.py:288
  145.3 6.0 %collective-permute-start.32 = (bf16[32,3584]{1,0:T(8,128)(2,1)S(1)}, bf16[32,3584]{1,0:T(8,128)(2,1)S(1)}, u32[]{:S(2)}, u32[]{:S(2)}) collective-permute-start(bf16[32,3584]{1,0:T(8,128)(2,1)S(1)} %get-tuple-element.192), channel_id=1, source_target_pairs={{0,2},{1,3},{4,0},{5,1},{8,4},{9,5},{12,8},{13,9},{14,12},{15,13},... | collective-permute-start | bytes 688136 | tf_op jit(solution)/shard_map/ppermute | solution.py:288

commit v14 on v10

--- a/solution.py
+++ b/solution.py
@@ -14,6 +14,7 @@
 WIDE = 512
 MIB = 1 << 20
 AHEAD = 6 * MIB
+FORWARD = 40 * 10**9
 
 
 def expert_kernel(n, experts, dim, half, expert_ref, *refs):
@@ -128,8 +129,30 @@
         out_specs=[pl.BlockSpec(memory_space=pltpu.VMEM)] * (2 * n),
         out_shape=[jax.ShapeDtypeStruct((rows // 2, dim), arrays[0].dtype)] * (2 * n),
         compiler_params=pltpu.CompilerParams(vmem_limit_bytes=6 * MIB),
+        cost_estimate=pl.CostEstimate(flops=FORWARD, bytes_accessed=1024, transcendentals=0),
+    )(*arrays)
+
+
+def merge_kernel(n, *refs):
+    for i, out in enumerate(refs[n + n // 2 :]):
+        rows_ref, digits_ref = refs[i], refs[n + i // 2]
+        half, dim = rows_ref.shape
+        start = i % 2 * half
+        out[:, :dim] = rows_ref[...]
+        out[:, dim:] = digits_ref[start : start + half, :]
+
+
+def merged(halves, digits):
+    n = len(halves)
+    rows, dim = halves[0].shape
+    return pl.pallas_call(
+        functools.partial(merge_kernel, n),
+        in_specs=[pl.BlockSpec(memory_space=pltpu.VMEM)] * (n + n // 2),
+        out_specs=[pl.BlockSpec(memory_space=pltpu.VMEM)] * n,
+        out_shape=[jax.ShapeDtypeStruct((rows, dim + LANES), halves[0].dtype)] * n,
+        compiler_params=pltpu.CompilerParams(vmem_limit_bytes=6 * MIB),
         cost_estimate=small_cost(),
-    )(*arrays)
+    )(*halves, *digits)
 
 
 def close_kernel(*refs):
@@ -155,26 +178,25 @@
     )(*bases, *terms)
 
 
-def rows_kernel(experts, top, tokens_ref, ids_ref, codes_ref, out_ref):
-    tok, dim = tokens_ref.shape
+def digits_kernel(experts, ids_ref, codes_ref, out_ref):
+    tok = out_ref.shape[0]
     row = lax.broadcasted_iota(jnp.int32, (LANES, tok), 0)
     expert = jnp.where(row < experts, row, row - experts)
     code = jnp.zeros((LANES, tok), jnp.int32)
-    for k in range(top):
+    for k in range(ids_ref.shape[0]):
         code = code + jnp.where(ids_ref[k : k + 1, :] == expert, codes_ref[k : k + 1, :], 0)
     digits = jnp.where(row < experts, code // DIGIT, code % DIGIT)
-    out_ref[:, :dim] = tokens_ref[...]
-    out_ref[:, dim:] = jnp.transpose(digits.astype(jnp.float32)).astype(out_ref.dtype)
-
-
-def with_codes(experts, tokens, ids, codes):
-    tok, dim = tokens.shape
-    return pl.pallas_call(
-        functools.partial(rows_kernel, experts, ids.shape[1]),
-        out_shape=jax.ShapeDtypeStruct((tok, dim + LANES), tokens.dtype),
-        compiler_params=pltpu.CompilerParams(vmem_limit_bytes=6 * MIB),
+    out_ref[...] = jnp.transpose(digits.astype(jnp.float32)).astype(out_ref.dtype)
+
+
+def code_digits(experts, ids, codes):
+    return pl.pallas_call(
+        functools.partial(digits_kernel, experts),
+        in_specs=[pl.BlockSpec(memory_space=pltpu.VMEM)] * 2,
+        out_shape=jax.ShapeDtypeStruct((ids.shape[0], LANES), jnp.bfloat16),
+        compiler_params=pltpu.CompilerParams(vmem_limit_bytes=2 * MIB),
         cost_estimate=small_cost(),
-    )(tokens, ids.T, codes.T)
+    )(ids.T, codes.T)
 
 
 def bring_in_kernel(n, *refs):
@@ -220,17 +242,21 @@
     forward, backward = perm(1), perm(-1)
     swap = [(node, node ^ 1) for node in range(nodes)]
     expert = lax.div(lax.axis_index("node"), jnp.int32(SPAN)).reshape(1)
-    tokens, expert = lax.optimization_barrier((tokens, expert))
-
-    rows = with_codes(ring, tokens, expert_ids, gate_codes)
-
-    near = [lax.ppermute(rows, "node", forward), lax.ppermute(rows, "node", backward)]
-    weights, _ = lax.optimization_barrier(((w_gate, w_up, w_down), rows))
+    weights = (w_gate, w_up, w_down)
+    tokens, weights, expert = lax.optimization_barrier((tokens, weights, expert))
+
+    near = [lax.ppermute(tokens, "node", way) for way in (forward, backward)]
     other = [lax.ppermute(weight, "node", swap) for weight in weights]
+    digits = code_digits(ring, expert_ids, gate_codes)
+    digits, *other[:2] = lax.optimization_barrier((digits, *other[:2]))
+    marks = [lax.ppermute(digits, "node", way) for way in (forward, backward)]
+    halves, marks, other, weights = lax.optimization_barrier(
+        (split(near), marks, other, weights)
+    )
     own = bring_in(weights)
 
-    near, own = lax.optimization_barrier((near, own))
-    halves = split(near)
+    halves = merged(halves, marks)
+    mine = merged([tokens[:half], tokens[half:]], [digits])
     ahead = [[None, halves[0]], [None, halves[1]]]
     behind = [[None, halves[3]], [None, halves[2]]]
     parts = {}
@@ -253,7 +279,7 @@
     for wave in range(2):
         send(2, wave, [])
     names = [(offset, h) for offset in (0, -1, 1) for h in range(2)]
-    done = [work(names, [rows, *near])]
+    done = [work(names, [*mine, *halves])]
     for s in range(3, far + 1):
         for wave in range(2):
             if s < far or wave == 0:

time: 156 us -> 152 us (0.974)
  local copies, waits for them, and re-layouts: 8.65 us -> 1.44 us
  starting transfers between devices: 32.4 us -> 35.4 us
    unnamed x12, local copies, waits for them, and re-layouts: 8.65 us -> 1.38 us
    ppermute x3, waiting for transfers between devices: 0.01 us -> 6.91 us  [body(): other = [lax.ppermute(weight, 'node', swap) for weight in weights]]
    ppermute x2 -> x4, waiting for transfers between devices: 16.2 us -> 11.4 us  [the longest x2 11.2 us: body(): near = [lax.ppermute(tokens, 'node', way) for way in (forward, backward)]]
    ppermute x2 -> x4, starting transfers between devices: 2.65 us -> 5.97 us  [the longest x2 3.03 us: body(): near = [lax.ppermute(tokens, 'node', way) for way in (forward, backward)]]
  transfers between devices with their start and end apart: 33 -> 35, of which waited for: 24 -> 26; matrix products, arithmetic and copies ran while one was open for 0% -> 0% of each run, Pallas kernels for 24% -> 25%
where the time goes in v14:
time: 152 us
  waiting for transfers between devices  75.3 us (50%)
  Pallas kernels  39.4 us (26%)
  starting transfers between devices  35.4 us (23%)
    ppermute x18, waiting for transfers between devices, pass_on(): lax.ppermute(t, 'node', ways[sign])  45.9 us
    pallas_call x6, Pallas kernels, expert_parts(): pl.pallas_call(functools.partial(expert_kernel, n, experts, dim, half), i...  36.4 us
    ppermute x18, starting transfers between devices, pass_on(): lax.ppermute(t, 'node', ways[sign])  18.6 us
    ppermute x2, waiting for transfers between devices, body(): near = [lax.ppermute(tokens, 'node', way) for way in (forward, backward)]  11.2 us
    ppermute x5, starting transfers between devices, send(): ahead[wave].append(lax.ppermute(pair[0], 'node', forward))  8.04 us
    ppermute x3, waiting for transfers between devices, body(): other = [lax.ppermute(weight, 'node', swap) for weight in weights]  6.91 us
    ppermute x5, waiting for transfers between devices, send(): behind[wave].append(lax.ppermute(pair[1], 'node', backward))  6.03 us
    ppermute x5, waiting for transfers between devices, send(): ahead[wave].append(lax.ppermute(pair[0], 'node', forward))  5.08 us
  transfers between devices with their start and end apart: 35, of which 26 were waited for; matrix products, arithmetic and copies ran while one was open for 0% of the time, Pallas kernels for 25%

profile of v14, /device:TPU:0, one launch (start us, length us, event | category | flops | bytes accessed | tf_op | source)
XLA Modules:
  0.0 151.7 jit_solution(6710106331576929023)
XLA Ops:
  0.5 3.0 %collective-permute-start = (bf16[128,3584]{1,0:T(8,128)(2,1)}, bf16[128,3584]{1,0:T(8,128)(2,1)S(1)}, u32[]{:S(2)}, u32[]{:S(2)}) collective-permute-start(bf16[128,3584]{1,0:T(8,128)(2,1)} %param.6), channel_id=1, source_target_pairs={{0,4},{1,5},{4,8},{5,9},{8,12},{9,13},{12,14},{13,15},{14,10},{15,... | collective-permute-start | bytes 2752520 | tf_op jit(solution)/shard_map/ppermute | solution.py:248
  5.0 1.7 %collective-permute-done.2.refs_9_.refs_5_ = bf16[3584,512]{1,0:T(8,128)(2,1)S(1)} collective-permute-done((bf16[3584,512]{1,0:T(8,128)(2,1)}, bf16[3584,512]{1,0:T(8,128)(2,1)S(1)}, u32[]{:S(2)}, u32[]{:S(2)}) %collective-permute-start.2) | collective-permute-done | bytes 3670048 | tf_op jit(solution)/shard_map/ppermute | solution.py:249
  6.7 5.2 %collective-permute-done.3.refs_10_.refs_6_ = bf16[3584,512]{1,0:T(8,128)(2,1)S(1)} collective-permute-done((bf16[3584,512]{1,0:T(8,128)(2,1)}, bf16[3584,512]{1,0:T(8,128)(2,1)S(1)}, u32[]{:S(2)}, u32[]{:S(2)}) %collective-permute-start.3) | collective-permute-done | bytes 3670048 | tf_op jit(solution)/shard_map/ppermute | solution.py:249
  11.9 2.9 %collective-permute-start.4 = (bf16[128,128]{1,0:T(8,128)(2,1)S(1)}, bf16[128,128]{1,0:T(8,128)(2,1)S(1)}, u32[]{:S(2)}, u32[]{:S(2)}) collective-permute-start(bf16[128,128]{1,0:T(8,128)(2,1)S(1)} %shard_map.65.refs_2_), channel_id=1, source_target_pairs={{0,4},{1,5},{4,8},{5,9},{8,12},{9,13},{12,14},{13,15},{14,10},{15,... | collective-permute-start | bytes 98312 | tf_op jit(solution)/shard_map/ppermute | solution.py:252
  14.9 9.7 %collective-permute-done.refs_0_ = bf16[128,3584]{1,0:T(8,128)(2,1)S(1)} collective-permute-done((bf16[128,3584]{1,0:T(8,128)(2,1)}, bf16[128,3584]{1,0:T(8,128)(2,1)S(1)}, u32[]{:S(2)}, u32[]{:S(2)}) %collective-permute-start) | collective-permute-done | bytes 917536 | tf_op jit(solution)/shard_map/ppermute | solution.py:248
  24.6 1.5 %collective-permute-done.1.refs_1_ = bf16[128,3584]{1,0:T(8,128)(2,1)S(1)} collective-permute-done((bf16[128,3584]{1,0:T(8,128)(2,1)}, bf16[128,3584]{1,0:T(8,128)(2,1)S(1)}, u32[]{:S(2)}, u32[]{:S(2)}) %collective-permute-start.1) | collective-permute-done | bytes 917536 | tf_op jit(solution)/shard_map/ppermute | solution.py:248
  26.6 1.6 %collective-permute-start.7 = (bf16[64,3712]{1,0:T(8,128)(2,1)S(1)}, bf16[64,3712]{1,0:T(8,128)(2,1)S(1)}, u32[]{:S(2)}, u32[]{:S(2)}) collective-permute-start(bf16[64,3712]{1,0:T(8,128)(2,1)S(1)} %get-tuple-element.142.refs_2_), channel_id=1, source_target_pairs={{0,4},{1,5},{4,8},{5,9},{8,12},{9,13},{12,14},{13,15},{14,10},{15,... | collective-permute-start | bytes 1425416 | tf_op jit(solution)/shard_map/ppermute | solution.py:276
  28.8 1.6 %collective-permute-start.9 = (bf16[64,3712]{1,0:T(8,128)(2,1)S(1)}, bf16[64,3712]{1,0:T(8,128)(2,1)S(1)}, u32[]{:S(2)}, u32[]{:S(2)}) collective-permute-start(bf16[64,3712]{1,0:T(8,128)(2,1)S(1)} %get-tuple-element.165.refs_3_), channel_id=1, source_target_pairs={{0,4},{1,5},{4,8},{5,9},{8,12},{9,13},{12,14},{13,15},{14,10},{15,... | collective-permute-start | bytes 1425416 | tf_op jit(solution)/shard_map/ppermute | solution.py:276
  31.6 10.8 %shard_map.69 = (bf16[64,3584]{1,0:T(8,128)(2,1)S(1)}, bf16[64,3584]{1,0:T(8,128)(2,1)S(1)}, bf16[64,3584]{1,0:T(8,128)(2,1)S(1)}, bf16[64,3584]{1,0:T(8,128)(2,...) custom-call(s32[1]{0:T(128)} %bitcast.expert_ref, bf16[64,3712]{1,0:T(8,128)(2,1)S(1)} %get-tuple-element.140.refs_0_, ...), custom_call_target="tpu_custom_call" | custom-call | flops 1024 | bytes 1024 | tf_op jit(solution)/shard_map/pallas_call | solution.py:75
  42.5 1.6 %collective-permute-start.13 = (bf16[64,3712]{1,0:T(8,128)(2,1)S(1)}, bf16[64,3712]{1,0:T(8,128)(2,1)S(1)}, u32[]{:S(2)}, u32[]{:S(2)}) collective-permute-start(bf16[64,3712]{1,0:T(8,128)(2,1)S(1)} %collective-permute-done.7.refs_0_), channel_id=1, source_target_pairs={{0,4},{1,5},{4,8},{5,9},{8,12},{9,13},{12,14},{13,15},{14,10},{15,... | collective-permute-start | bytes 1425416 | tf_op jit(solution)/shard_map/ppermute | solution.py:276
  44.6 5.1 %shard_map.70 = (bf16[64,3584]{1,0:T(8,128)(2,1)S(1)}, bf16[64,3584]{1,0:T(8,128)(2,1)S(1)}) custom-call(s32[1]{0:T(128)} %bitcast.expert_ref, bf16[64,3712]{1,0:T(8,128)(2,1)S(1)} %collective-permute-done.7.refs_0_, bf16[64,3712]{1,0:T(8,128)(2,1)S(1)} %collective-permute-done.8.refs_1_, bf16[3584,512]{1,0:T(8,128)(2,1)S(1)} %get-tuple-element.149.refs_6_.refs_2_, ...), custom_call_target="tpu_custom_call" | custom-call | flops 1024 | bytes 1024 | tf_op jit(solution)/shard_map/pallas_call | solution.py:75
  50.6 1.6 %collective-permute-done.10.refs_1_ = bf16[64,3712]{1,0:T(8,128)(2,1)S(1)} collective-permute-done((bf16[64,3712]{1,0:T(8,128)(2,1)S(1)}, bf16[64,3712]{1,0:T(8,128)(2,1)S(1)}, u32[]{:S(2)}, u32[]{:S(2)}) %collective-permute-start.10) | collective-permute-done | bytes 475168 | tf_op jit(solution)/shard_map/ppermute | solution.py:277
  52.2 1.6 %collective-permute-start.11 = (bf16[64,3712]{1,0:T(8,128)(2,1)S(1)}, bf16[64,3712]{1,0:T(8,128)(2,1)S(1)}, u32[]{:S(2)}, u32[]{:S(2)}) collective-permute-start(bf16[64,3712]{1,0:T(8,128)(2,1)S(1)} %collective-permute-done.9.refs_0_), channel_id=1, source_target_pairs={{0,4},{1,5},{4,8},{5,9},{8,12},{9,13},{12,14},{13,15},{14,10},{15,... | collective-permute-start | bytes 1425416 | tf_op jit(solution)/shard_map/ppermute | solution.py:276
  54.2 5.1 %shard_map.71 = (bf16[64,3584]{1,0:T(8,128)(2,1)S(1)}, bf16[64,3584]{1,0:T(8,128)(2,1)S(1)}) custom-call(s32[1]{0:T(128)} %bitcast.expert_ref, bf16[64,3712]{1,0:T(8,128)(2,1)S(1)} %collective-permute-done.9.refs_0_, bf16[64,3712]{1,0:T(8,128)(2,1)S(1)} %collective-permute-done.10.refs_1_, bf16[3584,512]{1,0:T(8,128)(2,1)S(1)} %get-tuple-element.149.refs_6_.refs_2_, ...), custom_call_target="tpu_custom_call" | custom-call | flops 1024 | bytes 1024 | tf_op jit(solution)/shard_map/pallas_call | solution.py:75
  59.3 1.5 collective-permute-done.13.refs_0_
  60.8 1.6 %collective-permute-done.14.refs_1_ = bf16[64,3712]{1,0:T(8,128)(2,1)S(1)} collective-permute-done((bf16[64,3712]{1,0:T(8,128)(2,1)S(1)}, bf16[64,3712]{1,0:T(8,128)(2,1)S(1)}, u32[]{:S(2)}, u32[]{:S(2)}) %collective-permute-start.14) | collective-permute-done | bytes 475168 | tf_op jit(solution)/shard_map/ppermute | solution.py:277
  62.4 1.6 %collective-permute-start.15 = (bf16[64,3712]{1,0:T(8,128)(2,1)S(1)}, bf16[64,3712]{1,0:T(8,128)(2,1)S(1)}, u32[]{:S(2)}, u32[]{:S(2)}) collective-permute-start(bf16[64,3712]{1,0:T(8,128)(2,1)S(1)} %collective-permute-done.13.refs_0_), channel_id=1, source_target_pairs={{0,4},{1,5},{4,8},{5,9},{8,12},{9,13},{12,14},{13,15},{14,10},{15,... | collective-permute-start | bytes 1425416 | tf_op jit(solution)/shard_map/ppermute | solution.py:276
  64.4 5.1 %shard_map.72 = (bf16[64,3584]{1,0:T(8,128)(2,1)S(1)}, bf16[64,3584]{1,0:T(8,128)(2,1)S(1)}) custom-call(s32[1]{0:T(128)} %bitcast.expert_ref, bf16[64,3712]{1,0:T(8,128)(2,1)S(1)} %collective-permute-done.13.refs_0_, bf16[64,3712]{1,0:T(8,128)(2,1)S(1)} %collective-permute-done.14.refs_1_, bf16[3584,512]{1,0:T(8,128)(2,1)S(1)} %get-tuple-element.149.refs_6_.refs_2_, ...), custom_call_target="tpu_custom_call" | custom-call | flops 1024 | bytes 1024 | tf_op jit(solution)/shard_map/pallas_call | solution.py:75
  69.5 1.5 collective-permute-done.11.refs_0_
  71.0 1.6 %collective-permute-done.12.refs_1_ = bf16[64,3712]{1,0:T(8,128)(2,1)S(1)} collective-permute-done((bf16[64,3712]{1,0:T(8,128)(2,1)S(1)}, bf16[64,3712]{1,0:T(8,128)(2,1)S(1)}, u32[]{:S(2)}, u32[]{:S(2)}) %collective-permute-start.12) | collective-permute-done | bytes 475168 | tf_op jit(solution)/shard_map/ppermute | solution.py:277
  72.5 5.1 %shard_map.73 = (bf16[64,3584]{1,0:T(8,128)(2,1)S(1)}, bf16[64,3584]{1,0:T(8,128)(2,1)S(1)}) custom-call(s32[1]{0:T(128)} %bitcast.expert_ref, bf16[64,3712]{1,0:T(8,128)(2,1)S(1)} %collective-permute-done.11.refs_0_, bf16[64,3712]{1,0:T(8,128)(2,1)S(1)} %collective-permute-done.12.refs_1_, bf16[3584,512]{1,0:T(8,128)(2,1)S(1)} %get-tuple-element.149.refs_6_.refs_2_, ...), custom_call_target="tpu_custom_call" | custom-call | flops 1024 | bytes 1024 | tf_op jit(solution)/shard_map/pallas_call | solution.py:75
  77.7 1.3 collective-permute-done.15.refs_0_
  78.9 1.3 collective-permute-done.16.refs_1_
  80.7 1.6 %collective-permute-start.18 = (bf16[64,3584]{1,0:T(8,128)(2,1)S(1)}, bf16[64,3584]{1,0:T(8,128)(2,1)S(1)}, u32[]{:S(2)}, u32[]{:S(2)}) collective-permute-start(bf16[64,3584]{1,0:T(8,128)(2,1)S(1)} %get-tuple-element.196), channel_id=1, source_target_pairs={{0,4},{1,5},{4,8},{5,9},{8,12},{9,13},{12,14},{13,15},{14,10},{15,... | collective-permute-start | bytes 1376264 | tf_op jit(solution)/shard_map/ppermute | solution.py:305
  82.3 5.1 %shard_map.77 = (bf16[64,3584]{1,0:T(8,128)(2,1)S(1)}, bf16[64,3584]{1,0:T(8,128)(2,1)S(1)}) custom-call(s32[1]{0:T(128)} %bitcast.expert_ref, bf16[64,3712]{1,0:T(8,128)(2,1)S(1)} %collective-permute-done.15.refs_0_, bf16[64,3712]{1,0:T(8,128)(2,1)S(1)} %collective-permute-done.16.refs_1_, bf16[3584,512]{1,0:T(8,128)(2,1)S(1)} %get-tuple-element.149.refs_6_.refs_2_, ...), custom_call_target="tpu_custom_call" | custom-call | flops 1024 | bytes 1024 | tf_op jit(solution)/shard_map/pallas_call | solution.py:75
  87.4 1.6 %collective-permute-start.23 = (bf16[64,3584]{1,0:T(8,128)(2,1)S(1)}, bf16[64,3584]{1,0:T(8,128)(2,1)S(1)}, u32[]{:S(2)}, u32[]{:S(2)}) collective-permute-start(bf16[64,3584]{1,0:T(8,128)(2,1)S(1)} %get-tuple-element.211), channel_id=1, source_target_pairs={{0,4},{1,5},{4,8},{5,9},{8,12},{9,13},{12,14},{13,15},{14,10},{15,... | collective-permute-start | bytes 1376264 | tf_op jit(solution)/shard_map/ppermute | solution.py:305
  89.5 2.7 %collective-permute-done.17.refs_2_ = bf16[64,3584]{1,0:T(8,128)(2,1)S(1)} collective-permute-done((bf16[64,3584]{1,0:T(8,128)(2,1)S(1)}, bf16[64,3584]{1,0:T(8,128)(2,1)S(1)}, u32[]{:S(2)}, u32[]{:S(2)}) %collective-permute-start.17) | collective-permute-done | bytes 458784 | tf_op jit(solution)/shard_map/ppermute | solution.py:305
  92.1 1.6 %collective-permute-done.18.refs_3_ = bf16[64,3584]{1,0:T(8,128)(2,1)S(1)} collective-permute-done((bf16[64,3584]{1,0:T(8,128)(2,1)S(1)}, bf16[64,3584]{1,0:T(8,128)(2,1)S(1)}, u32[]{:S(2)}, u32[]{:S(2)}) %collective-permute-start.18) | collective-permute-done | bytes 458784 | tf_op jit(solution)/shard_map/ppermute | solution.py:305
  93.9 1.1 collective-permute-start.19
  95.0 1.0 collective-permute-start.20
  95.9 7.6 %collective-permute-done.23.refs_2_ = bf16[64,3584]{1,0:T(8,128)(2,1)S(1)} collective-permute-done((bf16[64,3584]{1,0:T(8,128)(2,1)S(1)}, bf16[64,3584]{1,0:T(8,128)(2,1)S(1)}, u32[]{:S(2)}, u32[]{:S(2)}) %collective-permute-start.23) | collective-permute-done | bytes 458784 | tf_op jit(solution)/shard_map/ppermute | solution.py:305
  103.7 1.7 %collective-permute-start.25 = (bf16[64,3584]{1,0:T(8,128)(2,1)S(1)}, bf16[64,3584]{1,0:T(8,128)(2,1)S(1)}, u32[]{:S(2)}, u32[]{:S(2)}) collective-permute-start(bf16[64,3584]{1,0:T(8,128)(2,1)S(1)} %get-tuple-element.213), channel_id=1, source_target_pairs={{0,4},{1,5},{4,8},{5,9},{8,12},{9,13},{12,14},{13,15},{14,10},{15,... | collective-permute-start | bytes 1376264 | tf_op jit(solution)/shard_map/ppermute | solution.py:305
  105.8 6.6 %collective-permute-done.19.refs_2_ = bf16[64,3584]{1,0:T(8,128)(2,1)S(1)} collective-permute-done((bf16[64,3584]{1,0:T(8,128)(2,1)S(1)}, bf16[64,3584]{1,0:T(8,128)(2,1)S(1)}, u32[]{:S(2)}, u32[]{:S(2)}) %collective-permute-start.19) | collective-permute-done | bytes 458784 | tf_op jit(solution)/shard_map/ppermute | solution.py:305
  112.3 1.1 collective-permute-done.20.refs_3_
  113.5 1.1 collective-permute-start.21
  114.6 1.0 collective-permute-start.22
  115.6 7.7 %collective-permute-done.25.refs_2_ = bf16[64,3584]{1,0:T(8,128)(2,1)S(1)} collective-permute-done((bf16[64,3584]{1,0:T(8,128)(2,1)S(1)}, bf16[64,3584]{1,0:T(8,128)(2,1)S(1)}, u32[]{:S(2)}, u32[]{:S(2)}) %collective-permute-start.25) | collective-permute-done | bytes 458784 | tf_op jit(solution)/shard_map/ppermute | solution.py:305
  123.3 1.6 %collective-permute-start.27 = (bf16[32,3584]{1,0:T(8,128)(2,1)S(1)}, bf16[32,3584]{1,0:T(8,128)(2,1)S(1)}, u32[]{:S(2)}, u32[]{:S(2)}) collective-permute-start(bf16[32,3584]{1,0:T(8,128)(2,1)S(1)} %get-tuple-element.215), channel_id=1, source_target_pairs={{0,4},{1,5},{4,8},{5,9},{8,12},{9,13},{12,14},{13,15},{14,10},{15,... | collective-permute-start | bytes 688136 | tf_op jit(solution)/shard_map/ppermute | solution.py:305
  125.4 1.6 %collective-permute-start.31 = (bf16[32,3584]{1,0:T(8,128)(2,1)S(1)}, bf16[32,3584]{1,0:T(8,128)(2,1)S(1)}, u32[]{:S(2)}, u32[]{:S(2)}) collective-permute-start(bf16[32,3584]{1,0:T(8,128)(2,1)S(1)} %get-tuple-element.219), channel_id=1, source_target_pairs={{0,4},{1,5},{4,8},{5,9},{8,12},{9,13},{12,14},{13,15},{14,10},{15,... | collective-permute-start | bytes 688136 | tf_op jit(solution)/shard_map/ppermute | solution.py:305
  127.0 5.0 %collective-permute-done.21.refs_2_ = bf16[64,3584]{1,0:T(8,128)(2,1)S(1)} collective-permute-done((bf16[64,3584]{1,0:T(8,128)(2,1)S(1)}, bf16[64,3584]{1,0:T(8,128)(2,1)S(1)}, u32[]{:S(2)}, u32[]{:S(2)}) %collective-permute-start.21) | collective-permute-done | bytes 458784 | tf_op jit(solution)/shard_map/ppermute | solution.py:305
  133.3 4.7 %collective-permute-done.27.refs_2_ = bf16[32,3584]{1,0:T(8,128)(2,1)S(1)} collective-permute-done((bf16[32,3584]{1,0:T(8,128)(2,1)S(1)}, bf16[32,3584]{1,0:T(8,128)(2,1)S(1)}, u32[]{:S(2)}, u32[]{:S(2)}) %collective-permute-start.27) | collective-permute-done | bytes 229408 | tf_op jit(solution)/shard_map/ppermute | solution.py:305
  138.0 1.7 %collective-permute-start.29 = (bf16[32,3584]{1,0:T(8,128)(2,1)S(1)}, bf16[32,3584]{1,0:T(8,128)(2,1)S(1)}, u32[]{:S(2)}, u32[]{:S(2)}) collective-permute-start(bf16[32,3584]{1,0:T(8,128)(2,1)S(1)} %get-tuple-element.217), channel_id=1, source_target_pairs={{0,4},{1,5},{4,8},{5,9},{8,12},{9,13},{12,14},{13,15},{14,10},{15,... | collective-permute-start | bytes 688136 | tf_op jit(solution)/shard_map/ppermute | solution.py:305
  140.1 2.8 %collective-permute-done.31.refs_2_ = bf16[32,3584]{1,0:T(8,128)(2,1)S(1)} collective-permute-done((bf16[32,3584]{1,0:T(8,128)(2,1)S(1)}, bf16[32,3584]{1,0:T(8,128)(2,1)S(1)}, u32[]{:S(2)}, u32[]{:S(2)}) %collective-permute-start.31) | collective-permute-done | bytes 229408 | tf_op jit(solution)/shard_map/ppermute | solution.py:305
  143.0 1.7 %collective-permute-start.33 = (bf16[32,3584]{1,0:T(8,128)(2,1)S(1)}, bf16[32,3584]{1,0:T(8,128)(2,1)S(1)}, u32[]{:S(2)}, u32[]{:S(2)}) collective-permute-start(bf16[32,3584]{1,0:T(8,128)(2,1)S(1)} %get-tuple-element.221), channel_id=1, source_target_pairs={{0,4},{1,5},{4,8},{5,9},{8,12},{9,13},{12,14},{13,15},{14,10},{15,... | collective-permute-start | bytes 688136 | tf_op jit(solution)/shard_map/ppermute | solution.py:305
  145.0 2.0 %collective-permute-done.29.refs_2_ = bf16[32,3584]{1,0:T(8,128)(2,1)S(1)} collective-permute-done((bf16[32,3584]{1,0:T(8,128)(2,1)S(1)}, bf16[32,3584]{1,0:T(8,128)(2,1)S(1)}, u32[]{:S(2)}, u32[]{:S(2)}) %collective-permute-start.29) | collective-permute-done | bytes 229408 | tf_op jit(solution)/shard_map/ppermute | solution.py:305
  147.0 2.5 %collective-permute-done.33.refs_4_ = bf16[32,3584]{1,0:T(8,128)(2,1)S(1)} collective-permute-done((bf16[32,3584]{1,0:T(8,128)(2,1)S(1)}, bf16[32,3584]{1,0:T(8,128)(2,1)S(1)}, u32[]{:S(2)}, u32[]{:S(2)}) %collective-permute-start.33) | collective-permute-done | bytes 229408 | tf_op jit(solution)/shard_map/ppermute | solution.py:305
  149.5 1.2 collective-permute-done.34.refs_5_
  150.6 1.1 shard_map.82
  (54 shorter events, 10.8 us)
Async XLA Ops:
  0.0 6.7 %collective-permute-start.2 = (bf16[3584,512]{1,0:T(8,128)(2,1)}, bf16[3584,512]{1,0:T(8,128)(2,1)S(1)}, u32[]{:S(2)}, u32[]{:S(2)}) collective-permute-start(bf16[3584,512]{1,0:T(8,128)(2,1)} %refs_0_), channel_id=1, source_target_pairs={{0,1},{1,0},{2,3},{3,2},{4,5},{5,4},{6,7},{7,6},{8,9},{9,8},{10,11... | collective-permute-start | bytes 11010056 | tf_op jit(solution)/shard_map/ppermute | solution.py:249
  0.5 11.5 %collective-permute-start.3 = (bf16[3584,512]{1,0:T(8,128)(2,1)}, bf16[3584,512]{1,0:T(8,128)(2,1)S(1)}, u32[]{:S(2)}, u32[]{:S(2)}) collective-permute-start(bf16[3584,512]{1,0:T(8,128)(2,1)} %refs_1_), channel_id=1, source_target_pairs={{0,1},{1,0},{2,3},{3,2},{4,5},{5,4},{6,7},{7,6},{8,9},{9,8},{10,11... | collective-permute-start | bytes 11010056 | tf_op jit(solution)/shard_map/ppermute | solution.py:249
  0.5 24.0 %collective-permute-start = (bf16[128,3584]{1,0:T(8,128)(2,1)}, bf16[128,3584]{1,0:T(8,128)(2,1)S(1)}, u32[]{:S(2)}, u32[]{:S(2)}) collective-permute-start(bf16[128,3584]{1,0:T(8,128)(2,1)} %param.6), channel_id=1, source_target_pairs={{0,4},{1,5},{4,8},{5,9},{8,12},{9,13},{12,14},{13,15},{14,10},{15,... | collective-permute-start | bytes 2752520 | tf_op jit(solution)/shard_map/ppermute | solution.py:248
  3.5 22.5 %collective-permute-start.1 = (bf16[128,3584]{1,0:T(8,128)(2,1)}, bf16[128,3584]{1,0:T(8,128)(2,1)S(1)}, u32[]{:S(2)}, u32[]{:S(2)}) collective-permute-start(bf16[128,3584]{1,0:T(8,128)(2,1)} %param.6), channel_id=1, source_target_pairs={{0,2},{1,3},{4,0},{5,1},{8,4},{9,5},{12,8},{13,9},{14,12},{15,13},... | collective-permute-start | bytes 2752520 | tf_op jit(solution)/shard_map/ppermute | solution.py:248
  3.5 22.7 %collective-permute-start.6 = (bf16[512,3584]{1,0:T(8,128)(2,1)}, bf16[512,3584]{1,0:T(8,128)(2,1)S(1)}, u32[]{:S(2)}, u32[]{:S(2)}) collective-permute-start(bf16[512,3584]{1,0:T(8,128)(2,1)} %refs_2_), channel_id=1, source_target_pairs={{0,1},{1,0},{2,3},{3,2},{4,5},{5,4},{6,7},{7,6},{8,9},{9,8},{10,11... | collective-permute-start | bytes 11010056 | tf_op jit(solution)/shard_map/ppermute | solution.py:249
  3.5 0.7 copy-start.3
  4.2 0.7 copy-start.4
  5.0 23.6 %copy-start.5 = (bf16[128,3584]{1,0:T(8,128)(2,1)S(1)}, bf16[128,3584]{1,0:T(8,128)(2,1)}, u32[]{:S(2)}) copy-start(bf16[128,3584]{1,0:T(8,128)(2,1)} %param.6) | copy-start | bytes 2752516
  11.9 14.3 %collective-permute-start.4 = (bf16[128,128]{1,0:T(8,128)(2,1)S(1)}, bf16[128,128]{1,0:T(8,128)(2,1)S(1)}, u32[]{:S(2)}, u32[]{:S(2)}) collective-permute-start(bf16[128,128]{1,0:T(8,128)(2,1)S(1)} %shard_map.65.refs_2_), channel_id=1, source_target_pairs={{0,4},{1,5},{4,8},{5,9},{8,12},{9,13},{12,14},{13,15},{14,10},{15,... | collective-permute-start | bytes 98312 | tf_op jit(solution)/shard_map/ppermute | solution.py:252
  14.9 11.5 %collective-permute-start.5 = (bf16[128,128]{1,0:T(8,128)(2,1)S(1)}, bf16[128,128]{1,0:T(8,128)(2,1)S(1)}, u32[]{:S(2)}, u32[]{:S(2)}) collective-permute-start(bf16[128,128]{1,0:T(8,128)(2,1)S(1)} %shard_map.65.refs_2_), channel_id=1, source_target_pairs={{0,2},{1,3},{4,0},{5,1},{8,4},{9,5},{12,8},{13,9},{14,12},{15,13},... | collective-permute-start | bytes 98312 | tf_op jit(solution)/shard_map/ppermute | solution.py:252
  26.1 4.8 %copy-start.1 = (bf16[3584,512]{1,0:T(8,128)(2,1)S(1)}, bf16[3584,512]{1,0:T(8,128)(2,1)}, u32[]{:S(2)}) copy-start(bf16[3584,512]{1,0:T(8,128)(2,1)} %refs_1_) | copy-start | bytes 11010052
  26.1 4.8 %copy-start.2 = (bf16[512,3584]{1,0:T(8,128)(2,1)S(1)}, bf16[512,3584]{1,0:T(8,128)(2,1)}, u32[]{:S(2)}) copy-start(bf16[512,3584]{1,0:T(8,128)(2,1)} %refs_2_) | copy-start | bytes 11010052
  26.2 4.7 %copy-start = (bf16[3584,512]{1,0:T(8,128)(2,1)S(1)}, bf16[3584,512]{1,0:T(8,128)(2,1)}, u32[]{:S(2)}) copy-start(bf16[3584,512]{1,0:T(8,128)(2,1)} %refs_0_) | copy-start | bytes 11010052
  26.6 15.9 %collective-permute-start.7 = (bf16[64,3712]{1,0:T(8,128)(2,1)S(1)}, bf16[64,3712]{1,0:T(8,128)(2,1)S(1)}, u32[]{:S(2)}, u32[]{:S(2)}) collective-permute-start(bf16[64,3712]{1,0:T(8,128)(2,1)S(1)} %get-tuple-element.142.refs_2_), channel_id=1, source_target_pairs={{0,4},{1,5},{4,8},{5,9},{8,12},{9,13},{12,14},{13,15},{14,10},{15,... | collective-permute-start | bytes 1425416 | tf_op jit(solution)/shard_map/ppermute | solution.py:276
  28.2 14.3 %collective-permute-start.8 = (bf16[64,3712]{1,0:T(8,128)(2,1)S(1)}, bf16[64,3712]{1,0:T(8,128)(2,1)S(1)}, u32[]{:S(2)}, u32[]{:S(2)}) collective-permute-start(bf16[64,3712]{1,0:T(8,128)(2,1)S(1)} %get-tuple-element.145.refs_5_), channel_id=1, source_target_pairs={{0,2},{1,3},{4,0},{5,1},{8,4},{9,5},{12,8},{13,9},{14,12},{15,13},... | collective-permute-start | bytes 1425416 | tf_op jit(solution)/shard_map/ppermute | solution.py:277
  28.8 21.8 %collective-permute-start.9 = (bf16[64,3712]{1,0:T(8,128)(2,1)S(1)}, bf16[64,3712]{1,0:T(8,128)(2,1)S(1)}, u32[]{:S(2)}, u32[]{:S(2)}) collective-permute-start(bf16[64,3712]{1,0:T(8,128)(2,1)S(1)} %get-tuple-element.165.refs_3_), channel_id=1, source_target_pairs={{0,4},{1,5},{4,8},{5,9},{8,12},{9,13},{12,14},{13,15},{14,10},{15,... | collective-permute-start | bytes 1425416 | tf_op jit(solution)/shard_map/ppermute | solution.py:276
  30.4 21.8 %collective-permute-start.10 = (bf16[64,3712]{1,0:T(8,128)(2,1)S(1)}, bf16[64,3712]{1,0:T(8,128)(2,1)S(1)}, u32[]{:S(2)}, u32[]{:S(2)}) collective-permute-start(bf16[64,3712]{1,0:T(8,128)(2,1)S(1)} %get-tuple-element.166.refs_4_), channel_id=1, source_target_pairs={{0,2},{1,3},{4,0},{5,1},{8,4},{9,5},{12,8},{13,9},{14,12},{15,13},... | collective-permute-start | bytes 1425416 | tf_op jit(solution)/shard_map/ppermute | solution.py:277
  42.5 18.3 %collective-permute-start.13 = (bf16[64,3712]{1,0:T(8,128)(2,1)S(1)}, bf16[64,3712]{1,0:T(8,128)(2,1)S(1)}, u32[]{:S(2)}, u32[]{:S(2)}) collective-permute-start(bf16[64,3712]{1,0:T(8,128)(2,1)S(1)} %collective-permute-done.7.refs_0_), channel_id=1, source_target_pairs={{0,4},{1,5},{4,8},{5,9},{8,12},{9,13},{12,14},{13,15},{14,10},{15,... | collective-permute-start | bytes 1425416 | tf_op jit(solution)/shard_map/ppermute | solution.py:276
  44.1 18.2 %collective-permute-start.14 = (bf16[64,3712]{1,0:T(8,128)(2,1)S(1)}, bf16[64,3712]{1,0:T(8,128)(2,1)S(1)}, u32[]{:S(2)}, u32[]{:S(2)}) collective-permute-start(bf16[64,3712]{1,0:T(8,128)(2,1)S(1)} %collective-permute-done.8.refs_1_), channel_id=1, source_target_pairs={{0,2},{1,3},{4,0},{5,1},{8,4},{9,5},{12,8},{13,9},{14,12},{15,13},... | collective-permute-start | bytes 1425416 | tf_op jit(solution)/shard_map/ppermute | solution.py:277
  52.2 18.8 %collective-permute-start.11 = (bf16[64,3712]{1,0:T(8,128)(2,1)S(1)}, bf16[64,3712]{1,0:T(8,128)(2,1)S(1)}, u32[]{:S(2)}, u32[]{:S(2)}) collective-permute-start(bf16[64,3712]{1,0:T(8,128)(2,1)S(1)} %collective-permute-done.9.refs_0_), channel_id=1, source_target_pairs={{0,4},{1,5},{4,8},{5,9},{8,12},{9,13},{12,14},{13,15},{14,10},{15,... | collective-permute-start | bytes 1425416 | tf_op jit(solution)/shard_map/ppermute | solution.py:276
  53.8 18.8 %collective-permute-start.12 = (bf16[64,3712]{1,0:T(8,128)(2,1)S(1)}, bf16[64,3712]{1,0:T(8,128)(2,1)S(1)}, u32[]{:S(2)}, u32[]{:S(2)}) collective-permute-start(bf16[64,3712]{1,0:T(8,128)(2,1)S(1)} %collective-permute-done.10.refs_1_), channel_id=1, source_target_pairs={{0,2},{1,3},{4,0},{5,1},{8,4},{9,5},{12,8},{13,9},{14,12},{15,13},... | collective-permute-start | bytes 1425416 | tf_op jit(solution)/shard_map/ppermute | solution.py:277
  62.4 16.6 %collective-permute-start.15 = (bf16[64,3712]{1,0:T(8,128)(2,1)S(1)}, bf16[64,3712]{1,0:T(8,128)(2,1)S(1)}, u32[]{:S(2)}, u32[]{:S(2)}) collective-permute-start(bf16[64,3712]{1,0:T(8,128)(2,1)S(1)} %collective-permute-done.13.refs_0_), channel_id=1, source_target_pairs={{0,4},{1,5},{4,8},{5,9},{8,12},{9,13},{12,14},{13,15},{14,10},{15,... | collective-permute-start | bytes 1425416 | tf_op jit(solution)/shard_map/ppermute | solution.py:276
  63.9 16.3 %collective-permute-start.16 = (bf16[64,3712]{1,0:T(8,128)(2,1)S(1)}, bf16[64,3712]{1,0:T(8,128)(2,1)S(1)}, u32[]{:S(2)}, u32[]{:S(2)}) collective-permute-start(bf16[64,3712]{1,0:T(8,128)(2,1)S(1)} %collective-permute-done.14.refs_1_), channel_id=1, source_target_pairs={{0,2},{1,3},{4,0},{5,1},{8,4},{9,5},{12,8},{13,9},{14,12},{15,13},... | collective-permute-start | bytes 1425416 | tf_op jit(solution)/shard_map/ppermute | solution.py:277
  80.2 11.9 %collective-permute-start.17 = (bf16[64,3584]{1,0:T(8,128)(2,1)S(1)}, bf16[64,3584]{1,0:T(8,128)(2,1)S(1)}, u32[]{:S(2)}, u32[]{:S(2)}) collective-permute-start(bf16[64,3584]{1,0:T(8,128)(2,1)S(1)} %get-tuple-element.195), channel_id=1, source_target_pairs={{0,2},{1,3},{4,0},{5,1},{8,4},{9,5},{12,8},{13,9},{14,12},{15,13},... | collective-permute-start | bytes 1376264 | tf_op jit(solution)/shard_map/ppermute | solution.py:305
  80.7 13.1 %collective-permute-start.18 = (bf16[64,3584]{1,0:T(8,128)(2,1)S(1)}, bf16[64,3584]{1,0:T(8,128)(2,1)S(1)}, u32[]{:S(2)}, u32[]{:S(2)}) collective-permute-start(bf16[64,3584]{1,0:T(8,128)(2,1)S(1)} %get-tuple-element.196), channel_id=1, source_target_pairs={{0,4},{1,5},{4,8},{5,9},{8,12},{9,13},{12,14},{13,15},{14,10},{15,... | collective-permute-start | bytes 1376264 | tf_op jit(solution)/shard_map/ppermute | solution.py:305
  87.4 16.2 %collective-permute-start.23 = (bf16[64,3584]{1,0:T(8,128)(2,1)S(1)}, bf16[64,3584]{1,0:T(8,128)(2,1)S(1)}, u32[]{:S(2)}, u32[]{:S(2)}) collective-permute-start(bf16[64,3584]{1,0:T(8,128)(2,1)S(1)} %get-tuple-element.211), channel_id=1, source_target_pairs={{0,4},{1,5},{4,8},{5,9},{8,12},{9,13},{12,14},{13,15},{14,10},{15,... | collective-permute-start | bytes 1376264 | tf_op jit(solution)/shard_map/ppermute | solution.py:305
  89.0 14.6 %collective-permute-start.24 = (bf16[64,3584]{1,0:T(8,128)(2,1)S(1)}, bf16[64,3584]{1,0:T(8,128)(2,1)S(1)}, u32[]{:S(2)}, u32[]{:S(2)}) collective-permute-start(bf16[64,3584]{1,0:T(8,128)(2,1)S(1)} %get-tuple-element.212), channel_id=1, source_target_pairs={{0,2},{1,3},{4,0},{5,1},{8,4},{9,5},{12,8},{13,9},{14,12},{15,13},... | collective-permute-start | bytes 1376264 | tf_op jit(solution)/shard_map/ppermute | solution.py:305
  93.9 18.5 %collective-permute-start.19 = (bf16[64,3584]{1,0:T(8,128)(2,1)S(1)}, bf16[64,3584]{1,0:T(8,128)(2,1)S(1)}, u32[]{:S(2)}, u32[]{:S(2)}) collective-permute-start(bf16[64,3584]{1,0:T(8,128)(2,1)S(1)} %get-tuple-element.197), channel_id=1, source_target_pairs={{0,2},{1,3},{4,0},{5,1},{8,4},{9,5},{12,8},{13,9},{14,12},{15,13},... | collective-permute-start | bytes 1376264 | tf_op jit(solution)/shard_map/ppermute | solution.py:305
  95.0 18.5 %collective-permute-start.20 = (bf16[64,3584]{1,0:T(8,128)(2,1)S(1)}, bf16[64,3584]{1,0:T(8,128)(2,1)S(1)}, u32[]{:S(2)}, u32[]{:S(2)}) collective-permute-start(bf16[64,3584]{1,0:T(8,128)(2,1)S(1)} %get-tuple-element.198), channel_id=1, source_target_pairs={{0,4},{1,5},{4,8},{5,9},{8,12},{9,13},{12,14},{13,15},{14,10},{15,... | collective-permute-start | bytes 1376264 | tf_op jit(solution)/shard_map/ppermute | solution.py:305
  103.7 19.6 %collective-permute-start.25 = (bf16[64,3584]{1,0:T(8,128)(2,1)S(1)}, bf16[64,3584]{1,0:T(8,128)(2,1)S(1)}, u32[]{:S(2)}, u32[]{:S(2)}) collective-permute-start(bf16[64,3584]{1,0:T(8,128)(2,1)S(1)} %get-tuple-element.213), channel_id=1, source_target_pairs={{0,4},{1,5},{4,8},{5,9},{8,12},{9,13},{12,14},{13,15},{14,10},{15,... | collective-permute-start | bytes 1376264 | tf_op jit(solution)/shard_map/ppermute | solution.py:305
  105.3 17.9 %collective-permute-start.26 = (bf16[64,3584]{1,0:T(8,128)(2,1)S(1)}, bf16[64,3584]{1,0:T(8,128)(2,1)S(1)}, u32[]{:S(2)}, u32[]{:S(2)}) collective-permute-start(bf16[64,3584]{1,0:T(8,128)(2,1)S(1)} %get-tuple-element.214), channel_id=1, source_target_pairs={{0,2},{1,3},{4,0},{5,1},{8,4},{9,5},{12,8},{13,9},{14,12},{15,13},... | collective-permute-start | bytes 1376264 | tf_op jit(solution)/shard_map/ppermute | solution.py:305
  113.5 18.5 %collective-permute-start.21 = (bf16[64,3584]{1,0:T(8,128)(2,1)S(1)}, bf16[64,3584]{1,0:T(8,128)(2,1)S(1)}, u32[]{:S(2)}, u32[]{:S(2)}) collective-permute-start(bf16[64,3584]{1,0:T(8,128)(2,1)S(1)} %get-tuple-element.199), channel_id=1, source_target_pairs={{0,2},{1,3},{4,0},{5,1},{8,4},{9,5},{12,8},{13,9},{14,12},{15,13},... | collective-permute-start | bytes 1376264 | tf_op jit(solution)/shard_map/ppermute | solution.py:305
  114.6 18.5 %collective-permute-start.22 = (bf16[64,3584]{1,0:T(8,128)(2,1)S(1)}, bf16[64,3584]{1,0:T(8,128)(2,1)S(1)}, u32[]{:S(2)}, u32[]{:S(2)}) collective-permute-start(bf16[64,3584]{1,0:T(8,128)(2,1)S(1)} %get-tuple-element.200), channel_id=1, source_target_pairs={{0,4},{1,5},{4,8},{5,9},{8,12},{9,13},{12,14},{13,15},{14,10},{15,... | collective-permute-start | bytes 1376264 | tf_op jit(solution)/shard_map/ppermute | solution.py:305
  123.3 14.6 %collective-permute-start.27 = (bf16[32,3584]{1,0:T(8,128)(2,1)S(1)}, bf16[32,3584]{1,0:T(8,128)(2,1)S(1)}, u32[]{:S(2)}, u32[]{:S(2)}) collective-permute-start(bf16[32,3584]{1,0:T(8,128)(2,1)S(1)} %get-tuple-element.215), channel_id=1, source_target_pairs={{0,4},{1,5},{4,8},{5,9},{8,12},{9,13},{12,14},{13,15},{14,10},{15,... | collective-permute-start | bytes 688136 | tf_op jit(solution)/shard_map/ppermute | solution.py:305
  125.0 13.0 %collective-permute-start.28 = (bf16[32,3584]{1,0:T(8,128)(2,1)S(1)}, bf16[32,3584]{1,0:T(8,128)(2,1)S(1)}, u32[]{:S(2)}, u32[]{:S(2)}) collective-permute-start(bf16[32,3584]{1,0:T(8,128)(2,1)S(1)} %get-tuple-element.216), channel_id=1, source_target_pairs={{0,2},{1,3},{4,0},{5,1},{8,4},{9,5},{12,8},{13,9},{14,12},{15,13},... | collective-permute-start | bytes 688136 | tf_op jit(solution)/shard_map/ppermute | solution.py:305
  125.4 17.5 %collective-permute-start.31 = (bf16[32,3584]{1,0:T(8,128)(2,1)S(1)}, bf16[32,3584]{1,0:T(8,128)(2,1)S(1)}, u32[]{:S(2)}, u32[]{:S(2)}) collective-permute-start(bf16[32,3584]{1,0:T(8,128)(2,1)S(1)} %get-tuple-element.219), channel_id=1, source_target_pairs={{0,4},{1,5},{4,8},{5,9},{8,12},{9,13},{12,14},{13,15},{14,10},{15,... | collective-permute-start | bytes 688136 | tf_op jit(solution)/shard_map/ppermute | solution.py:305
  132.0 10.9 %collective-permute-start.32 = (bf16[32,3584]{1,0:T(8,128)(2,1)S(1)}, bf16[32,3584]{1,0:T(8,128)(2,1)S(1)}, u32[]{:S(2)}, u32[]{:S(2)}) collective-permute-start(bf16[32,3584]{1,0:T(8,128)(2,1)S(1)} %get-tuple-element.220), channel_id=1, source_target_pairs={{0,2},{1,3},{4,0},{5,1},{8,4},{9,5},{12,8},{13,9},{14,12},{15,13},... | collective-permute-start | bytes 688136 | tf_op jit(solution)/shard_map/ppermute | solution.py:305
  138.0 9.0 %collective-permute-start.29 = (bf16[32,3584]{1,0:T(8,128)(2,1)S(1)}, bf16[32,3584]{1,0:T(8,128)(2,1)S(1)}, u32[]{:S(2)}, u32[]{:S(2)}) collective-permute-start(bf16[32,3584]{1,0:T(8,128)(2,1)S(1)} %get-tuple-element.217), channel_id=1, source_target_pairs={{0,4},{1,5},{4,8},{5,9},{8,12},{9,13},{12,14},{13,15},{14,10},{15,... | collective-permute-start | bytes 688136 | tf_op jit(solution)/shard_map/ppermute | solution.py:305
  139.7 7.3 %collective-permute-start.30 = (bf16[32,3584]{1,0:T(8,128)(2,1)S(1)}, bf16[32,3584]{1,0:T(8,128)(2,1)S(1)}, u32[]{:S(2)}, u32[]{:S(2)}) collective-permute-start(bf16[32,3584]{1,0:T(8,128)(2,1)S(1)} %get-tuple-element.218), channel_id=1, source_target_pairs={{0,2},{1,3},{4,0},{5,1},{8,4},{9,5},{12,8},{13,9},{14,12},{15,13},... | collective-permute-start | bytes 688136 | tf_op jit(solution)/shard_map/ppermute | solution.py:305
  143.0 6.5 %collective-permute-start.33 = (bf16[32,3584]{1,0:T(8,128)(2,1)S(1)}, bf16[32,3584]{1,0:T(8,128)(2,1)S(1)}, u32[]{:S(2)}, u32[]{:S(2)}) collective-permute-start(bf16[32,3584]{1,0:T(8,128)(2,1)S(1)} %get-tuple-element.221), channel_id=1, source_target_pairs={{0,4},{1,5},{4,8},{5,9},{8,12},{9,13},{12,14},{13,15},{14,10},{15,... | collective-permute-start | bytes 688136 | tf_op jit(solution)/shard_map/ppermute | solution.py:305
  144.6 6.0 %collective-permute-start.34 = (bf16[32,3584]{1,0:T(8,128)(2,1)S(1)}, bf16[32,3584]{1,0:T(8,128)(2,1)S(1)}, u32[]{:S(2)}, u32[]{:S(2)}) collective-permute-start(bf16[32,3584]{1,0:T(8,128)(2,1)S(1)} %get-tuple-element.222), channel_id=1, source_target_pairs={{0,2},{1,3},{4,0},{5,1},{8,4},{9,5},{12,8},{13,9},{14,12},{15,13},... | collective-permute-start | bytes 688136 | tf_op jit(solution)/shard_map/ppermute | solution.py:305

commit v15 on v14

--- a/solution.py
+++ b/solution.py
@@ -17,21 +17,23 @@
 FORWARD = 40 * 10**9
 
 
-def expert_kernel(n, experts, dim, half, expert_ref, *refs):
-    blocks, weights, outs = refs[:n], refs[n : n + 6], refs[n + 6 : -3]
+def expert_kernel(n, shifts, experts, dim, half, expert_ref, *refs):
+    blocks, sources = refs[:n], refs[n : 2 * n]
+    weights, outs = refs[2 * n : 2 * n + 6], refs[2 * n + 6 : -3]
     rows_ref, scale_ref, hidden_ref = refs[-3:]
     hid = weights[0].shape[1]
     expert = expert_ref[0]
     first = 0
-    for block in blocks:
+    for block, source, shift in zip(blocks, sources, shifts):
         count = block.shape[0]
+        mine = expert + shift
         lane = lax.broadcasted_iota(jnp.int32, (count, LANES), 1)
         at = pl.ds(first, count)
         first += count
         rows_ref[at, :] = block[:, :dim]
-        digits = block[:, dim:].astype(jnp.float32)
-        codes = jnp.where(lane == expert, digits * float(DIGIT), 0.0)
-        codes = codes + jnp.where(lane == expert + experts, digits, 0.0)
+        digits = source[:, dim:].astype(jnp.float32)
+        codes = jnp.where(lane == mine, digits * float(DIGIT), 0.0)
+        codes = codes + jnp.where(lane == mine + experts, digits, 0.0)
         code = jnp.sum(codes, 1, keepdims=True) * (1.0 / 4096.0)
         scale_ref[at, :] = jnp.broadcast_to(code, (count, LANES))
 
@@ -67,13 +69,13 @@
     return pl.CostEstimate(flops=1024, bytes_accessed=1024, transcendentals=0)
 
 
-def expert_parts(experts, half, expert, blocks, own, other, cost=1024):
+def expert_parts(experts, half, expert, blocks, sources, shifts, own, other, cost=1024):
     dim, hid = own[0].shape
     n, rows = len(blocks), sum(block.shape[0] for block in blocks)
     specs = [pl.BlockSpec(memory_space=pltpu.SMEM)]
-    specs += [pl.BlockSpec(memory_space=pltpu.VMEM)] * (n + 6)
-    return pl.pallas_call(
-        functools.partial(expert_kernel, n, experts, dim, half),
+    specs += [pl.BlockSpec(memory_space=pltpu.VMEM)] * (2 * n + 6)
+    return pl.pallas_call(
+        functools.partial(expert_kernel, n, shifts, experts, dim, half),
         in_specs=specs,
         out_specs=[pl.BlockSpec(memory_space=pltpu.VMEM)] * (rows // half),
         out_shape=[jax.ShapeDtypeStruct((half, dim), jnp.bfloat16)] * (rows // half),
@@ -83,8 +85,8 @@
             pltpu.VMEM((rows, SPAN * hid), jnp.bfloat16),
         ],
         compiler_params=pltpu.CompilerParams(vmem_limit_bytes=8 * MIB),
-        cost_estimate=pl.CostEstimate(flops=1024, bytes_accessed=cost, transcendentals=0),
-    )(expert, *blocks, *own, *other)
+        cost_estimate=pl.CostEstimate(flops=cost, bytes_accessed=1024, transcendentals=0),
+    )(expert, *blocks, *sources, *own, *other)
 
 
 def add_kernel(n, pieces, first, *refs):
@@ -133,21 +135,19 @@
     )(*arrays)
 
 
-def merge_kernel(n, *refs):
-    for i, out in enumerate(refs[n + n // 2 :]):
-        rows_ref, digits_ref = refs[i], refs[n + i // 2]
-        half, dim = rows_ref.shape
-        start = i % 2 * half
-        out[:, :dim] = rows_ref[...]
-        out[:, dim:] = digits_ref[start : start + half, :]
-
-
-def merged(halves, digits):
+def merge_kernel(n, starts, *refs):
+    for i, out in enumerate(refs[2 * n :]):
+        half, dim = refs[i].shape
+        out[:, :dim] = refs[i][...]
+        out[:, dim:] = refs[n + i][starts[i] : starts[i] + half, :]
+
+
+def merged(halves, digits, starts):
     n = len(halves)
     rows, dim = halves[0].shape
     return pl.pallas_call(
-        functools.partial(merge_kernel, n),
-        in_specs=[pl.BlockSpec(memory_space=pltpu.VMEM)] * (n + n // 2),
+        functools.partial(merge_kernel, n, starts),
+        in_specs=[pl.BlockSpec(memory_space=pltpu.VMEM)] * (2 * n),
         out_specs=[pl.BlockSpec(memory_space=pltpu.VMEM)] * n,
         out_shape=[jax.ShapeDtypeStruct((rows, dim + LANES), halves[0].dtype)] * n,
         compiler_params=pltpu.CompilerParams(vmem_limit_bytes=6 * MIB),
@@ -181,11 +181,17 @@
 def digits_kernel(experts, ids_ref, codes_ref, out_ref):
     tok = out_ref.shape[0]
     row = lax.broadcasted_iota(jnp.int32, (LANES, tok), 0)
-    expert = jnp.where(row < experts, row, row - experts)
+    part, expert = row // experts, lax.rem(row, experts)
+
+    def swapped(ref, k):
+        return jnp.concatenate([ref[k : k + 1, tok // 2 :], ref[k : k + 1, : tok // 2]], 1)
+
     code = jnp.zeros((LANES, tok), jnp.int32)
     for k in range(ids_ref.shape[0]):
-        code = code + jnp.where(ids_ref[k : k + 1, :] == expert, codes_ref[k : k + 1, :], 0)
-    digits = jnp.where(row < experts, code // DIGIT, code % DIGIT)
+        ids = jnp.where(part < 2, ids_ref[k : k + 1, :], swapped(ids_ref, k))
+        codes = jnp.where(part < 2, codes_ref[k : k + 1, :], swapped(codes_ref, k))
+        code = code + jnp.where(ids == expert, codes, 0)
+    digits = jnp.where(lax.rem(part, 2) == 0, code // DIGIT, code % DIGIT)
     out_ref[...] = jnp.transpose(digits.astype(jnp.float32)).astype(out_ref.dtype)
 
 
@@ -255,17 +261,19 @@
     )
     own = bring_in(weights)
 
-    halves = merged(halves, marks)
-    mine = merged([tokens[:half], tokens[half:]], [digits])
-    ahead = [[None, halves[0]], [None, halves[1]]]
-    behind = [[None, halves[3]], [None, halves[2]]]
+    lead = merged([halves[0], halves[3]], marks, (0, half))
+    mine = merged([tokens[:half], tokens[half:]], [digits, digits], (0, half))
+    ahead = [[None, lead[0]], [None, halves[1]]]
+    behind = [[None, lead[1]], [None, halves[2]]]
     parts = {}
 
-    def work(names, blocks, after=(), **how):
+    def work(names, blocks, sources, after=(), **how):
         held = [parts[name] for name in after]
         blocks, held = lax.optimization_barrier((blocks, held))
         parts.update(zip(after, held))
-        parts.update(zip(names, expert_parts(ring, half, expert, blocks, own, other, **how)))
+        shifts = [0 if block.shape == source.shape else 2 * ring for block, source in zip(blocks, sources)]
+        shares = expert_parts(ring, half, expert, blocks, sources, shifts, own, other, **how)
+        parts.update(zip(names, shares))
         return names
 
     def send(s, wave, after):
@@ -279,15 +287,20 @@
     for wave in range(2):
         send(2, wave, [])
     names = [(offset, h) for offset in (0, -1, 1) for h in range(2)]
-    done = [work(names, [*mine, *halves])]
+    blocks = [*mine, lead[0], halves[1], halves[2], lead[1]]
+    done = [work(names, blocks, [*mine, lead[0], lead[0], lead[1], lead[1]])]
     for s in range(3, far + 1):
         for wave in range(2):
             if s < far or wave == 0:
                 send(s, wave, done.pop(0))
             names = [(1 - s, wave), (s - 1, 1 - wave)]
             after = done[-1] if s == far and wave == 1 else []
-            done.append(work(names, [ahead[wave][s - 1], behind[wave][s - 1]], after))
-    work([(far, 0), (far, 1)], [ahead[0][far], behind[0][far]], done[-1])
+            blocks = [ahead[wave][s - 1], behind[wave][s - 1]]
+            sources = [ahead[0][s - 1], behind[0][s - 1]]
+            cost = FORWARD // 4 if wave else 1024
+            done.append(work(names, blocks, sources, after, cost=cost))
+    last = [ahead[0][far], behind[0][far]]
+    work([(far, 0), (far, 1)], last, last, done[-1])
     parts[-far, 1] = parts[far, 1]
 
     firsts = [(1 - far, 0), (far - 1, 1)]

time: 152 us -> 151 us (level)
  transfers between devices with their start and end apart: 35 -> 35, of which waited for: 26 -> 25; matrix products, arithmetic and copies ran while one was open for 0% -> 0% of each run, Pallas kernels for 25% -> 25%
where the time goes in v15:
time: 151 us
  waiting for transfers between devices  74.9 us (50%)
  Pallas kernels  39.1 us (26%)
  starting transfers between devices  35.3 us (23%)
    ppermute x18, waiting for transfers between devices, pass_on(): lax.ppermute(t, 'node', ways[sign])  46 us
    pallas_call x6, Pallas kernels, expert_parts(): pl.pallas_call(functools.partial(expert_kernel, n, shifts, experts, dim,...  36.1 us
    ppermute x18, starting transfers between devices, pass_on(): lax.ppermute(t, 'node', ways[sign])  18.6 us
    ppermute x2, waiting for transfers between devices, body(): near = [lax.ppermute(tokens, 'node', way) for way in (forward, backward)]  11.2 us
    ppermute x5, starting transfers between devices, send(): ahead[wave].append(lax.ppermute(pair[0], 'node', forward))  8.12 us
    ppermute x3, waiting for transfers between devices, body(): other = [lax.ppermute(weight, 'node', swap) for weight in weights]  6.84 us
    ppermute x5, waiting for transfers between devices, send(): behind[wave].append(lax.ppermute(pair[1], 'node', backward))  6.68 us
    ppermute x5, waiting for transfers between devices, send(): ahead[wave].append(lax.ppermute(pair[0], 'node', forward))  4 us
  transfers between devices with their start and end apart: 35, of which 25 were waited for; matrix products, arithmetic and copies ran while one was open for 0% of the time, Pallas kernels for 25%

profile of v15, /device:TPU:0, one launch (start us, length us, event | category | flops | bytes accessed | tf_op | source)
XLA Modules:
  0.0 151.0 jit_solution(17063295752657302133)
XLA Ops:
  0.5 3.0 %collective-permute-start = (bf16[128,3584]{1,0:T(8,128)(2,1)}, bf16[128,3584]{1,0:T(8,128)(2,1)S(1)}, u32[]{:S(2)}, u32[]{:S(2)}) collective-permute-start(bf16[128,3584]{1,0:T(8,128)(2,1)} %param.6), channel_id=1, source_target_pairs={{0,4},{1,5},{4,8},{5,9},{8,12},{9,13},{12,14},{13,15},{14,10},{15,... | collective-permute-start | bytes 2752520 | tf_op jit(solution)/shard_map/ppermute | solution.py:254
  5.1 1.6 %collective-permute-done.2.refs_15_.refs_7_ = bf16[3584,512]{1,0:T(8,128)(2,1)S(1)} collective-permute-done((bf16[3584,512]{1,0:T(8,128)(2,1)}, bf16[3584,512]{1,0:T(8,128)(2,1)S(1)}, u32[]{:S(2)}, u32[]{:S(2)}) %collective-permute-start.2) | collective-permute-done | bytes 3670048 | tf_op jit(solution)/shard_map/ppermute | solution.py:255
  6.7 5.2 %collective-permute-done.3.refs_16_.refs_8_ = bf16[3584,512]{1,0:T(8,128)(2,1)S(1)} collective-permute-done((bf16[3584,512]{1,0:T(8,128)(2,1)}, bf16[3584,512]{1,0:T(8,128)(2,1)S(1)}, u32[]{:S(2)}, u32[]{:S(2)}) %collective-permute-start.3) | collective-permute-done | bytes 3670048 | tf_op jit(solution)/shard_map/ppermute | solution.py:255
  11.9 2.9 %collective-permute-start.4 = (bf16[128,128]{1,0:T(8,128)(2,1)S(1)}, bf16[128,128]{1,0:T(8,128)(2,1)S(1)}, u32[]{:S(2)}, u32[]{:S(2)}) collective-permute-start(bf16[128,128]{1,0:T(8,128)(2,1)S(1)} %shard_map.65.refs_2_.refs_3_), channel_id=1, source_target_pairs={{0,4},{1,5},{4,8},{5,9},{8,12},{9,13},{12,14},{13,15},{14,10},{15,... | collective-permute-start | bytes 98312 | tf_op jit(solution)/shard_map/ppermute | solution.py:258
  14.9 9.7 %collective-permute-done.refs_0_ = bf16[128,3584]{1,0:T(8,128)(2,1)S(1)} collective-permute-done((bf16[128,3584]{1,0:T(8,128)(2,1)}, bf16[128,3584]{1,0:T(8,128)(2,1)S(1)}, u32[]{:S(2)}, u32[]{:S(2)}) %collective-permute-start) | collective-permute-done | bytes 917536 | tf_op jit(solution)/shard_map/ppermute | solution.py:254
  24.6 1.5 %collective-permute-done.1.refs_1_ = bf16[128,3584]{1,0:T(8,128)(2,1)S(1)} collective-permute-done((bf16[128,3584]{1,0:T(8,128)(2,1)}, bf16[128,3584]{1,0:T(8,128)(2,1)S(1)}, u32[]{:S(2)}, u32[]{:S(2)}) %collective-permute-start.1) | collective-permute-done | bytes 917536 | tf_op jit(solution)/shard_map/ppermute | solution.py:254
  26.5 1.6 %collective-permute-start.7 = (bf16[64,3712]{1,0:T(8,128)(2,1)S(1)}, bf16[64,3712]{1,0:T(8,128)(2,1)S(1)}, u32[]{:S(2)}, u32[]{:S(2)}) collective-permute-start(bf16[64,3712]{1,0:T(8,128)(2,1)S(1)} %get-tuple-element.138.refs_2_.refs_8_.refs_9_), channel_id=1, source_target_pairs={{0,4},{1,5},{4,8},{5,9},{8,12},{9,13},{12,14},{13,15},{14,10},{15,... | collective-permute-start | bytes 1425416 | tf_op jit(solution)/shard_map/ppermute | solution.py:284
  28.9 1.7 %collective-permute-start.9 = (bf16[64,3584]{1,0:T(8,128)(2,1)S(1)}, bf16[64,3584]{1,0:T(8,128)(2,1)S(1)}, u32[]{:S(2)}, u32[]{:S(2)}) collective-permute-start(bf16[64,3584]{1,0:T(8,128)(2,1)S(1)} %get-tuple-element.161.refs_3_), channel_id=1, source_target_pairs={{0,4},{1,5},{4,8},{5,9},{8,12},{9,13},{12,14},{13,15},{14,10},{15,... | collective-permute-start | bytes 1376264 | tf_op jit(solution)/shard_map/ppermute | solution.py:284
  31.5 10.8 %shard_map.69 = (bf16[64,3584]{1,0:T(8,128)(2,1)S(1)}, bf16[64,3584]{1,0:T(8,128)(2,1)S(1)}, bf16[64,3584]{1,0:T(8,128)(2,1)S(1)}, bf16[64,3584]{1,0:T(8,128)(2,...) custom-call(s32[1]{0:T(128)} %bitcast.expert_ref, ...), custom_call_target="tpu_custom_call" | custom-call | flops 1024 | bytes 1024 | tf_op jit(solution)/shard_map/pallas_call | solution.py:77
  42.4 1.6 %collective-permute-start.13 = (bf16[64,3712]{1,0:T(8,128)(2,1)S(1)}, bf16[64,3712]{1,0:T(8,128)(2,1)S(1)}, u32[]{:S(2)}, u32[]{:S(2)}) collective-permute-start(bf16[64,3712]{1,0:T(8,128)(2,1)S(1)} %collective-permute-done.7.refs_0_.refs_2_), channel_id=1, source_target_pairs={{0,4},{1,5},{4,8},{5,9},{8,12},{9,13},{12,14},{13,15},{14,10},{15,... | collective-permute-start | bytes 1425416 | tf_op jit(solution)/shard_map/ppermute | solution.py:284
  44.5 5.1 %shard_map.70 = (bf16[64,3584]{1,0:T(8,128)(2,1)S(1)}, bf16[64,3584]{1,0:T(8,128)(2,1)S(1)}) custom-call(s32[1]{0:T(128)} %bitcast.expert_ref, bf16[64,3712]{1,0:T(8,128)(2,1)S(1)} %collective-permute-done.7.refs_0_.refs_2_, bf16[64,3712]{1,0:T(8,128)(2,1)S(1)} %collective-permute-done.8.refs_1_.refs_3_, ...), custom_call_target="tpu_custom_call" | custom-call | flops 1024 | bytes 1024 | tf_op jit(solution)/shard_map/pallas_call | solution.py:77
  49.5 2.2 %collective-permute-done.10.refs_1_ = bf16[64,3584]{1,0:T(8,128)(2,1)S(1)} collective-permute-done((bf16[64,3584]{1,0:T(8,128)(2,1)S(1)}, bf16[64,3584]{1,0:T(8,128)(2,1)S(1)}, u32[]{:S(2)}, u32[]{:S(2)}) %collective-permute-start.10) | collective-permute-done | bytes 458784 | tf_op jit(solution)/shard_map/ppermute | solution.py:285
  51.8 1.6 %collective-permute-start.11 = (bf16[64,3584]{1,0:T(8,128)(2,1)S(1)}, bf16[64,3584]{1,0:T(8,128)(2,1)S(1)}, u32[]{:S(2)}, u32[]{:S(2)}) collective-permute-start(bf16[64,3584]{1,0:T(8,128)(2,1)S(1)} %collective-permute-done.9.refs_0_), channel_id=1, source_target_pairs={{0,4},{1,5},{4,8},{5,9},{8,12},{9,13},{12,14},{13,15},{14,10},{15,... | collective-permute-start | bytes 1376264 | tf_op jit(solution)/shard_map/ppermute | solution.py:284
  53.8 5.1 %shard_map.71 = (bf16[64,3584]{1,0:T(8,128)(2,1)S(1)}, bf16[64,3584]{1,0:T(8,128)(2,1)S(1)}) custom-call(s32[1]{0:T(128)} %bitcast.expert_ref, bf16[64,3584]{1,0:T(8,128)(2,1)S(1)} %collective-permute-done.9.refs_0_, bf16[64,3584]{1,0:T(8,128)(2,1)S(1)} %collective-permute-done.10.refs_1_, bf16[64,3712]{1,0:T(8,128)(2,1)S(1)} %collective-permute-done.7.refs_0_.refs_2_, ...), custom_call_target="tpu_custom_call" | custom-call | flops 10000000000 | bytes 1024 | tf_op jit(solution)/shard_map/pallas_call | solution.py:77
  58.9 1.5 collective-permute-done.13.refs_0_.refs_2_
  60.4 1.6 %collective-permute-done.14.refs_1_.refs_3_ = bf16[64,3712]{1,0:T(8,128)(2,1)S(1)} collective-permute-done((bf16[64,3712]{1,0:T(8,128)(2,1)S(1)}, bf16[64,3712]{1,0:T(8,128)(2,1)S(1)}, u32[]{:S(2)}, u32[]{:S(2)}) %collective-permute-start.14) | collective-permute-done | bytes 475168 | tf_op jit(solution)/shard_map/ppermute | solution.py:285
  61.9 1.6 %collective-permute-start.15 = (bf16[64,3712]{1,0:T(8,128)(2,1)S(1)}, bf16[64,3712]{1,0:T(8,128)(2,1)S(1)}, u32[]{:S(2)}, u32[]{:S(2)}) collective-permute-start(bf16[64,3712]{1,0:T(8,128)(2,1)S(1)} %collective-permute-done.13.refs_0_.refs_2_), channel_id=1, source_target_pairs={{0,4},{1,5},{4,8},{5,9},{8,12},{9,13},{12,14},{13,15},{14,10},{15,... | collective-permute-start | bytes 1425416 | tf_op jit(solution)/shard_map/ppermute | solution.py:284
  64.0 5.1 %shard_map.72 = (bf16[64,3584]{1,0:T(8,128)(2,1)S(1)}, bf16[64,3584]{1,0:T(8,128)(2,1)S(1)}) custom-call(s32[1]{0:T(128)} %bitcast.expert_ref, bf16[64,3712]{1,0:T(8,128)(2,1)S(1)} %collective-permute-done.13.refs_0_.refs_2_, bf16[64,3712]{1,0:T(8,128)(2,1)S(1)} %collective-permute-done.14.refs_1_.refs_3_, ...), custom_call_target="tpu_custom_call" | custom-call | flops 1024 | bytes 1024 | tf_op jit(solution)/shard_map/pallas_call | solution.py:77
  69.0 1.2 collective-permute-done.11.refs_0_
  70.2 1.6 %collective-permute-done.12.refs_1_ = bf16[64,3584]{1,0:T(8,128)(2,1)S(1)} collective-permute-done((bf16[64,3584]{1,0:T(8,128)(2,1)S(1)}, bf16[64,3584]{1,0:T(8,128)(2,1)S(1)}, u32[]{:S(2)}, u32[]{:S(2)}) %collective-permute-start.12) | collective-permute-done | bytes 458784 | tf_op jit(solution)/shard_map/ppermute | solution.py:285
  71.8 5.1 %shard_map.73 = (bf16[64,3584]{1,0:T(8,128)(2,1)S(1)}, bf16[64,3584]{1,0:T(8,128)(2,1)S(1)}) custom-call(s32[1]{0:T(128)} %bitcast.expert_ref, bf16[64,3584]{1,0:T(8,128)(2,1)S(1)} %collective-permute-done.11.refs_0_, bf16[64,3584]{1,0:T(8,128)(2,1)S(1)} %collective-permute-done.12.refs_1_, bf16[64,3712]{1,0:T(8,128)(2,1)S(1)} %collective-permute-done.13.refs_0_.refs_2_, ...), custom_call_target="tpu_custom_call" | custom-call | flops 10000000000 | bytes 1024 | tf_op jit(solution)/shard_map/pallas_call | solution.py:77
  76.8 1.3 collective-permute-done.15.refs_0_.refs_2_
  78.2 1.3 collective-permute-done.16.refs_1_.refs_3_
  79.9 1.6 %collective-permute-start.18 = (bf16[64,3584]{1,0:T(8,128)(2,1)S(1)}, bf16[64,3584]{1,0:T(8,128)(2,1)S(1)}, u32[]{:S(2)}, u32[]{:S(2)}) collective-permute-start(bf16[64,3584]{1,0:T(8,128)(2,1)S(1)} %get-tuple-element.192), channel_id=1, source_target_pairs={{0,4},{1,5},{4,8},{5,9},{8,12},{9,13},{12,14},{13,15},{14,10},{15,... | collective-permute-start | bytes 1376264 | tf_op jit(solution)/shard_map/ppermute | solution.py:318
  81.5 5.1 %shard_map.77 = (bf16[64,3584]{1,0:T(8,128)(2,1)S(1)}, bf16[64,3584]{1,0:T(8,128)(2,1)S(1)}) custom-call(s32[1]{0:T(128)} %bitcast.expert_ref, bf16[64,3712]{1,0:T(8,128)(2,1)S(1)} %collective-permute-done.15.refs_0_.refs_2_, bf16[64,3712]{1,0:T(8,128)(2,1)S(1)} %collective-permute-done.16.refs_1_.refs_3_, ...), custom_call_target="tpu_custom_call" | custom-call | flops 1024 | bytes 1024 | tf_op jit(solution)/shard_map/pallas_call | solution.py:77
  86.6 1.6 %collective-permute-start.23 = (bf16[64,3584]{1,0:T(8,128)(2,1)S(1)}, bf16[64,3584]{1,0:T(8,128)(2,1)S(1)}, u32[]{:S(2)}, u32[]{:S(2)}) collective-permute-start(bf16[64,3584]{1,0:T(8,128)(2,1)S(1)} %get-tuple-element.207), channel_id=1, source_target_pairs={{0,4},{1,5},{4,8},{5,9},{8,12},{9,13},{12,14},{13,15},{14,10},{15,... | collective-permute-start | bytes 1376264 | tf_op jit(solution)/shard_map/ppermute | solution.py:318
  88.7 2.8 %collective-permute-done.17.refs_2_ = bf16[64,3584]{1,0:T(8,128)(2,1)S(1)} collective-permute-done((bf16[64,3584]{1,0:T(8,128)(2,1)S(1)}, bf16[64,3584]{1,0:T(8,128)(2,1)S(1)}, u32[]{:S(2)}, u32[]{:S(2)}) %collective-permute-start.17) | collective-permute-done | bytes 458784 | tf_op jit(solution)/shard_map/ppermute | solution.py:318
  91.4 1.6 %collective-permute-done.18.refs_3_ = bf16[64,3584]{1,0:T(8,128)(2,1)S(1)} collective-permute-done((bf16[64,3584]{1,0:T(8,128)(2,1)S(1)}, bf16[64,3584]{1,0:T(8,128)(2,1)S(1)}, u32[]{:S(2)}, u32[]{:S(2)}) %collective-permute-start.18) | collective-permute-done | bytes 458784 | tf_op jit(solution)/shard_map/ppermute | solution.py:318
  93.1 1.0 collective-permute-start.19
  94.2 1.0 collective-permute-start.20
  95.2 7.7 %collective-permute-done.23.refs_2_ = bf16[64,3584]{1,0:T(8,128)(2,1)S(1)} collective-permute-done((bf16[64,3584]{1,0:T(8,128)(2,1)S(1)}, bf16[64,3584]{1,0:T(8,128)(2,1)S(1)}, u32[]{:S(2)}, u32[]{:S(2)}) %collective-permute-start.23) | collective-permute-done | bytes 458784 | tf_op jit(solution)/shard_map/ppermute | solution.py:318
  103.0 1.6 %collective-permute-start.25 = (bf16[64,3584]{1,0:T(8,128)(2,1)S(1)}, bf16[64,3584]{1,0:T(8,128)(2,1)S(1)}, u32[]{:S(2)}, u32[]{:S(2)}) collective-permute-start(bf16[64,3584]{1,0:T(8,128)(2,1)S(1)} %get-tuple-element.209), channel_id=1, source_target_pairs={{0,4},{1,5},{4,8},{5,9},{8,12},{9,13},{12,14},{13,15},{14,10},{15,... | collective-permute-start | bytes 1376264 | tf_op jit(solution)/shard_map/ppermute | solution.py:318
  105.0 6.5 %collective-permute-done.19.refs_2_ = bf16[64,3584]{1,0:T(8,128)(2,1)S(1)} collective-permute-done((bf16[64,3584]{1,0:T(8,128)(2,1)S(1)}, bf16[64,3584]{1,0:T(8,128)(2,1)S(1)}, u32[]{:S(2)}, u32[]{:S(2)}) %collective-permute-start.19) | collective-permute-done | bytes 458784 | tf_op jit(solution)/shard_map/ppermute | solution.py:318
  111.5 1.2 collective-permute-done.20.refs_3_
  112.8 1.0 collective-permute-start.21
  113.8 1.0 collective-permute-start.22
  114.9 7.7 %collective-permute-done.25.refs_2_ = bf16[64,3584]{1,0:T(8,128)(2,1)S(1)} collective-permute-done((bf16[64,3584]{1,0:T(8,128)(2,1)S(1)}, bf16[64,3584]{1,0:T(8,128)(2,1)S(1)}, u32[]{:S(2)}, u32[]{:S(2)}) %collective-permute-start.25) | collective-permute-done | bytes 458784 | tf_op jit(solution)/shard_map/ppermute | solution.py:318
  122.6 1.7 %collective-permute-start.31 = (bf16[32,3584]{1,0:T(8,128)(2,1)S(1)}, bf16[32,3584]{1,0:T(8,128)(2,1)S(1)}, u32[]{:S(2)}, u32[]{:S(2)}) collective-permute-start(bf16[32,3584]{1,0:T(8,128)(2,1)S(1)} %get-tuple-element.215), channel_id=1, source_target_pairs={{0,4},{1,5},{4,8},{5,9},{8,12},{9,13},{12,14},{13,15},{14,10},{15,... | collective-permute-start | bytes 688136 | tf_op jit(solution)/shard_map/ppermute | solution.py:318
  124.7 1.6 %collective-permute-start.27 = (bf16[32,3584]{1,0:T(8,128)(2,1)S(1)}, bf16[32,3584]{1,0:T(8,128)(2,1)S(1)}, u32[]{:S(2)}, u32[]{:S(2)}) collective-permute-start(bf16[32,3584]{1,0:T(8,128)(2,1)S(1)} %get-tuple-element.211), channel_id=1, source_target_pairs={{0,4},{1,5},{4,8},{5,9},{8,12},{9,13},{12,14},{13,15},{14,10},{15,... | collective-permute-start | bytes 688136 | tf_op jit(solution)/shard_map/ppermute | solution.py:318
  126.3 4.9 %collective-permute-done.21.refs_2_ = bf16[64,3584]{1,0:T(8,128)(2,1)S(1)} collective-permute-done((bf16[64,3584]{1,0:T(8,128)(2,1)S(1)}, bf16[64,3584]{1,0:T(8,128)(2,1)S(1)}, u32[]{:S(2)}, u32[]{:S(2)}) %collective-permute-start.21) | collective-permute-done | bytes 458784 | tf_op jit(solution)/shard_map/ppermute | solution.py:318
  132.5 4.7 %collective-permute-done.31.refs_2_ = bf16[32,3584]{1,0:T(8,128)(2,1)S(1)} collective-permute-done((bf16[32,3584]{1,0:T(8,128)(2,1)S(1)}, bf16[32,3584]{1,0:T(8,128)(2,1)S(1)}, u32[]{:S(2)}, u32[]{:S(2)}) %collective-permute-start.31) | collective-permute-done | bytes 229408 | tf_op jit(solution)/shard_map/ppermute | solution.py:318
  137.3 1.6 %collective-permute-start.33 = (bf16[32,3584]{1,0:T(8,128)(2,1)S(1)}, bf16[32,3584]{1,0:T(8,128)(2,1)S(1)}, u32[]{:S(2)}, u32[]{:S(2)}) collective-permute-start(bf16[32,3584]{1,0:T(8,128)(2,1)S(1)} %get-tuple-element.217), channel_id=1, source_target_pairs={{0,4},{1,5},{4,8},{5,9},{8,12},{9,13},{12,14},{13,15},{14,10},{15,... | collective-permute-start | bytes 688136 | tf_op jit(solution)/shard_map/ppermute | solution.py:318
  139.4 2.8 %collective-permute-done.27.refs_2_ = bf16[32,3584]{1,0:T(8,128)(2,1)S(1)} collective-permute-done((bf16[32,3584]{1,0:T(8,128)(2,1)S(1)}, bf16[32,3584]{1,0:T(8,128)(2,1)S(1)}, u32[]{:S(2)}, u32[]{:S(2)}) %collective-permute-start.27) | collective-permute-done | bytes 229408 | tf_op jit(solution)/shard_map/ppermute | solution.py:318
  142.2 1.7 %collective-permute-start.29 = (bf16[32,3584]{1,0:T(8,128)(2,1)S(1)}, bf16[32,3584]{1,0:T(8,128)(2,1)S(1)}, u32[]{:S(2)}, u32[]{:S(2)}) collective-permute-start(bf16[32,3584]{1,0:T(8,128)(2,1)S(1)} %get-tuple-element.213), channel_id=1, source_target_pairs={{0,4},{1,5},{4,8},{5,9},{8,12},{9,13},{12,14},{13,15},{14,10},{15,... | collective-permute-start | bytes 688136 | tf_op jit(solution)/shard_map/ppermute | solution.py:318
  144.3 1.9 %collective-permute-done.33.refs_4_ = bf16[32,3584]{1,0:T(8,128)(2,1)S(1)} collective-permute-done((bf16[32,3584]{1,0:T(8,128)(2,1)S(1)}, bf16[32,3584]{1,0:T(8,128)(2,1)S(1)}, u32[]{:S(2)}, u32[]{:S(2)}) %collective-permute-start.33) | collective-permute-done | bytes 229408 | tf_op jit(solution)/shard_map/ppermute | solution.py:318
  146.2 2.5 %collective-permute-done.29.refs_2_ = bf16[32,3584]{1,0:T(8,128)(2,1)S(1)} collective-permute-done((bf16[32,3584]{1,0:T(8,128)(2,1)S(1)}, bf16[32,3584]{1,0:T(8,128)(2,1)S(1)}, u32[]{:S(2)}, u32[]{:S(2)}) %collective-permute-start.29) | collective-permute-done | bytes 229408 | tf_op jit(solution)/shard_map/ppermute | solution.py:318
  148.7 1.2 collective-permute-done.30.refs_3_
  149.9 1.1 shard_map.82
  (54 shorter events, 9.9 us)
Async XLA Ops:
  0.0 6.7 %collective-permute-start.2 = (bf16[3584,512]{1,0:T(8,128)(2,1)}, bf16[3584,512]{1,0:T(8,128)(2,1)S(1)}, u32[]{:S(2)}, u32[]{:S(2)}) collective-permute-start(bf16[3584,512]{1,0:T(8,128)(2,1)} %refs_0_), channel_id=1, source_target_pairs={{0,1},{1,0},{2,3},{3,2},{4,5},{5,4},{6,7},{7,6},{8,9},{9,8},{10,11... | collective-permute-start | bytes 11010056 | tf_op jit(solution)/shard_map/ppermute | solution.py:255
  0.5 11.5 %collective-permute-start.3 = (bf16[3584,512]{1,0:T(8,128)(2,1)}, bf16[3584,512]{1,0:T(8,128)(2,1)S(1)}, u32[]{:S(2)}, u32[]{:S(2)}) collective-permute-start(bf16[3584,512]{1,0:T(8,128)(2,1)} %refs_1_), channel_id=1, source_target_pairs={{0,1},{1,0},{2,3},{3,2},{4,5},{5,4},{6,7},{7,6},{8,9},{9,8},{10,11... | collective-permute-start | bytes 11010056 | tf_op jit(solution)/shard_map/ppermute | solution.py:255
  0.5 24.0 %collective-permute-start = (bf16[128,3584]{1,0:T(8,128)(2,1)}, bf16[128,3584]{1,0:T(8,128)(2,1)S(1)}, u32[]{:S(2)}, u32[]{:S(2)}) collective-permute-start(bf16[128,3584]{1,0:T(8,128)(2,1)} %param.6), channel_id=1, source_target_pairs={{0,4},{1,5},{4,8},{5,9},{8,12},{9,13},{12,14},{13,15},{14,10},{15,... | collective-permute-start | bytes 2752520 | tf_op jit(solution)/shard_map/ppermute | solution.py:254
  3.5 22.5 %collective-permute-start.1 = (bf16[128,3584]{1,0:T(8,128)(2,1)}, bf16[128,3584]{1,0:T(8,128)(2,1)S(1)}, u32[]{:S(2)}, u32[]{:S(2)}) collective-permute-start(bf16[128,3584]{1,0:T(8,128)(2,1)} %param.6), channel_id=1, source_target_pairs={{0,2},{1,3},{4,0},{5,1},{8,4},{9,5},{12,8},{13,9},{14,12},{15,13},... | collective-permute-start | bytes 2752520 | tf_op jit(solution)/shard_map/ppermute | solution.py:254
  3.5 22.7 %collective-permute-start.6 = (bf16[512,3584]{1,0:T(8,128)(2,1)}, bf16[512,3584]{1,0:T(8,128)(2,1)S(1)}, u32[]{:S(2)}, u32[]{:S(2)}) collective-permute-start(bf16[512,3584]{1,0:T(8,128)(2,1)} %refs_2_), channel_id=1, source_target_pairs={{0,1},{1,0},{2,3},{3,2},{4,5},{5,4},{6,7},{7,6},{8,9},{9,8},{10,11... | collective-permute-start | bytes 11010056 | tf_op jit(solution)/shard_map/ppermute | solution.py:255
  3.5 0.7 copy-start.3
  4.2 0.7 copy-start.4
  5.1 25.5 %copy-start.5 = (bf16[128,3584]{1,0:T(8,128)(2,1)S(1)}, bf16[128,3584]{1,0:T(8,128)(2,1)}, u32[]{:S(2)}) copy-start(bf16[128,3584]{1,0:T(8,128)(2,1)} %param.6) | copy-start | bytes 2752516
  11.9 14.3 %collective-permute-start.4 = (bf16[128,128]{1,0:T(8,128)(2,1)S(1)}, bf16[128,128]{1,0:T(8,128)(2,1)S(1)}, u32[]{:S(2)}, u32[]{:S(2)}) collective-permute-start(bf16[128,128]{1,0:T(8,128)(2,1)S(1)} %shard_map.65.refs_2_.refs_3_), channel_id=1, source_target_pairs={{0,4},{1,5},{4,8},{5,9},{8,12},{9,13},{12,14},{13,15},{14,10},{15,... | collective-permute-start | bytes 98312 | tf_op jit(solution)/shard_map/ppermute | solution.py:258
  14.9 11.5 %collective-permute-start.5 = (bf16[128,128]{1,0:T(8,128)(2,1)S(1)}, bf16[128,128]{1,0:T(8,128)(2,1)S(1)}, u32[]{:S(2)}, u32[]{:S(2)}) collective-permute-start(bf16[128,128]{1,0:T(8,128)(2,1)S(1)} %shard_map.65.refs_2_.refs_3_), channel_id=1, source_target_pairs={{0,2},{1,3},{4,0},{5,1},{8,4},{9,5},{12,8},{13,9},{14,12},{15,13},... | collective-permute-start | bytes 98312 | tf_op jit(solution)/shard_map/ppermute | solution.py:258
  26.1 4.7 %copy-start.1 = (bf16[3584,512]{1,0:T(8,128)(2,1)S(1)}, bf16[3584,512]{1,0:T(8,128)(2,1)}, u32[]{:S(2)}) copy-start(bf16[3584,512]{1,0:T(8,128)(2,1)} %refs_1_) | copy-start | bytes 11010052
  26.1 4.7 %copy-start.2 = (bf16[512,3584]{1,0:T(8,128)(2,1)S(1)}, bf16[512,3584]{1,0:T(8,128)(2,1)}, u32[]{:S(2)}) copy-start(bf16[512,3584]{1,0:T(8,128)(2,1)} %refs_2_) | copy-start | bytes 11010052
  26.2 4.6 %copy-start = (bf16[3584,512]{1,0:T(8,128)(2,1)S(1)}, bf16[3584,512]{1,0:T(8,128)(2,1)}, u32[]{:S(2)}) copy-start(bf16[3584,512]{1,0:T(8,128)(2,1)} %refs_0_) | copy-start | bytes 11010052
  26.5 15.9 %collective-permute-start.7 = (bf16[64,3712]{1,0:T(8,128)(2,1)S(1)}, bf16[64,3712]{1,0:T(8,128)(2,1)S(1)}, u32[]{:S(2)}, u32[]{:S(2)}) collective-permute-start(bf16[64,3712]{1,0:T(8,128)(2,1)S(1)} %get-tuple-element.138.refs_2_.refs_8_.refs_9_), channel_id=1, source_target_pairs={{0,4},{1,5},{4,8},{5,9},{8,12},{9,13},{12,14},{13,15},{14,10},{15,... | collective-permute-start | bytes 1425416 | tf_op jit(solution)/shard_map/ppermute | solution.py:284
  28.1 14.2 %collective-permute-start.8 = (bf16[64,3712]{1,0:T(8,128)(2,1)S(1)}, bf16[64,3712]{1,0:T(8,128)(2,1)S(1)}, u32[]{:S(2)}, u32[]{:S(2)}) collective-permute-start(bf16[64,3712]{1,0:T(8,128)(2,1)S(1)} %get-tuple-element.128), channel_id=1, source_target_pairs={{0,2},{1,3},{4,0},{5,1},{8,4},{9,5},{12,8},{13,9},{14,12},{15,13},... | collective-permute-start | bytes 1425416 | tf_op jit(solution)/shard_map/ppermute | solution.py:285
  28.6 23.2 %collective-permute-start.10 = (bf16[64,3584]{1,0:T(8,128)(2,1)S(1)}, bf16[64,3584]{1,0:T(8,128)(2,1)S(1)}, u32[]{:S(2)}, u32[]{:S(2)}) collective-permute-start(bf16[64,3584]{1,0:T(8,128)(2,1)S(1)} %get-tuple-element.162.refs_4_), channel_id=1, source_target_pairs={{0,2},{1,3},{4,0},{5,1},{8,4},{9,5},{12,8},{13,9},{14,12},{15,13},... | collective-permute-start | bytes 1376264 | tf_op jit(solution)/shard_map/ppermute | solution.py:285
  28.9 22.9 %collective-permute-start.9 = (bf16[64,3584]{1,0:T(8,128)(2,1)S(1)}, bf16[64,3584]{1,0:T(8,128)(2,1)S(1)}, u32[]{:S(2)}, u32[]{:S(2)}) collective-permute-start(bf16[64,3584]{1,0:T(8,128)(2,1)S(1)} %get-tuple-element.161.refs_3_), channel_id=1, source_target_pairs={{0,4},{1,5},{4,8},{5,9},{8,12},{9,13},{12,14},{13,15},{14,10},{15,... | collective-permute-start | bytes 1376264 | tf_op jit(solution)/shard_map/ppermute | solution.py:284
  42.4 18.0 %collective-permute-start.13 = (bf16[64,3712]{1,0:T(8,128)(2,1)S(1)}, bf16[64,3712]{1,0:T(8,128)(2,1)S(1)}, u32[]{:S(2)}, u32[]{:S(2)}) collective-permute-start(bf16[64,3712]{1,0:T(8,128)(2,1)S(1)} %collective-permute-done.7.refs_0_.refs_2_), channel_id=1, source_target_pairs={{0,4},{1,5},{4,8},{5,9},{8,12},{9,13},{12,14},{13,15},{14,10},{15,... | collective-permute-start | bytes 1425416 | tf_op jit(solution)/shard_map/ppermute | solution.py:284
  44.0 17.9 %collective-permute-start.14 = (bf16[64,3712]{1,0:T(8,128)(2,1)S(1)}, bf16[64,3712]{1,0:T(8,128)(2,1)S(1)}, u32[]{:S(2)}, u32[]{:S(2)}) collective-permute-start(bf16[64,3712]{1,0:T(8,128)(2,1)S(1)} %collective-permute-done.8.refs_1_.refs_3_), channel_id=1, source_target_pairs={{0,2},{1,3},{4,0},{5,1},{8,4},{9,5},{12,8},{13,9},{14,12},{15,13},... | collective-permute-start | bytes 1425416 | tf_op jit(solution)/shard_map/ppermute | solution.py:285
  51.8 18.4 %collective-permute-start.11 = (bf16[64,3584]{1,0:T(8,128)(2,1)S(1)}, bf16[64,3584]{1,0:T(8,128)(2,1)S(1)}, u32[]{:S(2)}, u32[]{:S(2)}) collective-permute-start(bf16[64,3584]{1,0:T(8,128)(2,1)S(1)} %collective-permute-done.9.refs_0_), channel_id=1, source_target_pairs={{0,4},{1,5},{4,8},{5,9},{8,12},{9,13},{12,14},{13,15},{14,10},{15,... | collective-permute-start | bytes 1376264 | tf_op jit(solution)/shard_map/ppermute | solution.py:284
  53.3 18.4 %collective-permute-start.12 = (bf16[64,3584]{1,0:T(8,128)(2,1)S(1)}, bf16[64,3584]{1,0:T(8,128)(2,1)S(1)}, u32[]{:S(2)}, u32[]{:S(2)}) collective-permute-start(bf16[64,3584]{1,0:T(8,128)(2,1)S(1)} %collective-permute-done.10.refs_1_), channel_id=1, source_target_pairs={{0,2},{1,3},{4,0},{5,1},{8,4},{9,5},{12,8},{13,9},{14,12},{15,13},... | collective-permute-start | bytes 1376264 | tf_op jit(solution)/shard_map/ppermute | solution.py:285
  61.9 16.2 %collective-permute-start.15 = (bf16[64,3712]{1,0:T(8,128)(2,1)S(1)}, bf16[64,3712]{1,0:T(8,128)(2,1)S(1)}, u32[]{:S(2)}, u32[]{:S(2)}) collective-permute-start(bf16[64,3712]{1,0:T(8,128)(2,1)S(1)} %collective-permute-done.13.refs_0_.refs_2_), channel_id=1, source_target_pairs={{0,4},{1,5},{4,8},{5,9},{8,12},{9,13},{12,14},{13,15},{14,10},{15,... | collective-permute-start | bytes 1425416 | tf_op jit(solution)/shard_map/ppermute | solution.py:284
  63.5 16.0 %collective-permute-start.16 = (bf16[64,3712]{1,0:T(8,128)(2,1)S(1)}, bf16[64,3712]{1,0:T(8,128)(2,1)S(1)}, u32[]{:S(2)}, u32[]{:S(2)}) collective-permute-start(bf16[64,3712]{1,0:T(8,128)(2,1)S(1)} %collective-permute-done.14.refs_1_.refs_3_), channel_id=1, source_target_pairs={{0,2},{1,3},{4,0},{5,1},{8,4},{9,5},{12,8},{13,9},{14,12},{15,13},... | collective-permute-start | bytes 1425416 | tf_op jit(solution)/shard_map/ppermute | solution.py:285
  79.5 11.9 %collective-permute-start.17 = (bf16[64,3584]{1,0:T(8,128)(2,1)S(1)}, bf16[64,3584]{1,0:T(8,128)(2,1)S(1)}, u32[]{:S(2)}, u32[]{:S(2)}) collective-permute-start(bf16[64,3584]{1,0:T(8,128)(2,1)S(1)} %get-tuple-element.191), channel_id=1, source_target_pairs={{0,2},{1,3},{4,0},{5,1},{8,4},{9,5},{12,8},{13,9},{14,12},{15,13},... | collective-permute-start | bytes 1376264 | tf_op jit(solution)/shard_map/ppermute | solution.py:318
  79.9 13.1 %collective-permute-start.18 = (bf16[64,3584]{1,0:T(8,128)(2,1)S(1)}, bf16[64,3584]{1,0:T(8,128)(2,1)S(1)}, u32[]{:S(2)}, u32[]{:S(2)}) collective-permute-start(bf16[64,3584]{1,0:T(8,128)(2,1)S(1)} %get-tuple-element.192), channel_id=1, source_target_pairs={{0,4},{1,5},{4,8},{5,9},{8,12},{9,13},{12,14},{13,15},{14,10},{15,... | collective-permute-start | bytes 1376264 | tf_op jit(solution)/shard_map/ppermute | solution.py:318
  86.6 16.3 %collective-permute-start.23 = (bf16[64,3584]{1,0:T(8,128)(2,1)S(1)}, bf16[64,3584]{1,0:T(8,128)(2,1)S(1)}, u32[]{:S(2)}, u32[]{:S(2)}) collective-permute-start(bf16[64,3584]{1,0:T(8,128)(2,1)S(1)} %get-tuple-element.207), channel_id=1, source_target_pairs={{0,4},{1,5},{4,8},{5,9},{8,12},{9,13},{12,14},{13,15},{14,10},{15,... | collective-permute-start | bytes 1376264 | tf_op jit(solution)/shard_map/ppermute | solution.py:318
  88.2 14.6 %collective-permute-start.24 = (bf16[64,3584]{1,0:T(8,128)(2,1)S(1)}, bf16[64,3584]{1,0:T(8,128)(2,1)S(1)}, u32[]{:S(2)}, u32[]{:S(2)}) collective-permute-start(bf16[64,3584]{1,0:T(8,128)(2,1)S(1)} %get-tuple-element.208), channel_id=1, source_target_pairs={{0,2},{1,3},{4,0},{5,1},{8,4},{9,5},{12,8},{13,9},{14,12},{15,13},... | collective-permute-start | bytes 1376264 | tf_op jit(solution)/shard_map/ppermute | solution.py:318
  93.1 18.4 %collective-permute-start.19 = (bf16[64,3584]{1,0:T(8,128)(2,1)S(1)}, bf16[64,3584]{1,0:T(8,128)(2,1)S(1)}, u32[]{:S(2)}, u32[]{:S(2)}) collective-permute-start(bf16[64,3584]{1,0:T(8,128)(2,1)S(1)} %get-tuple-element.193), channel_id=1, source_target_pairs={{0,2},{1,3},{4,0},{5,1},{8,4},{9,5},{12,8},{13,9},{14,12},{15,13},... | collective-permute-start | bytes 1376264 | tf_op jit(solution)/shard_map/ppermute | solution.py:318
  94.2 18.5 %collective-permute-start.20 = (bf16[64,3584]{1,0:T(8,128)(2,1)S(1)}, bf16[64,3584]{1,0:T(8,128)(2,1)S(1)}, u32[]{:S(2)}, u32[]{:S(2)}) collective-permute-start(bf16[64,3584]{1,0:T(8,128)(2,1)S(1)} %get-tuple-element.194), channel_id=1, source_target_pairs={{0,4},{1,5},{4,8},{5,9},{8,12},{9,13},{12,14},{13,15},{14,10},{15,... | collective-permute-start | bytes 1376264 | tf_op jit(solution)/shard_map/ppermute | solution.py:318
  103.0 19.6 %collective-permute-start.25 = (bf16[64,3584]{1,0:T(8,128)(2,1)S(1)}, bf16[64,3584]{1,0:T(8,128)(2,1)S(1)}, u32[]{:S(2)}, u32[]{:S(2)}) collective-permute-start(bf16[64,3584]{1,0:T(8,128)(2,1)S(1)} %get-tuple-element.209), channel_id=1, source_target_pairs={{0,4},{1,5},{4,8},{5,9},{8,12},{9,13},{12,14},{13,15},{14,10},{15,... | collective-permute-start | bytes 1376264 | tf_op jit(solution)/shard_map/ppermute | solution.py:318
  104.6 17.9 %collective-permute-start.26 = (bf16[64,3584]{1,0:T(8,128)(2,1)S(1)}, bf16[64,3584]{1,0:T(8,128)(2,1)S(1)}, u32[]{:S(2)}, u32[]{:S(2)}) collective-permute-start(bf16[64,3584]{1,0:T(8,128)(2,1)S(1)} %get-tuple-element.210), channel_id=1, source_target_pairs={{0,2},{1,3},{4,0},{5,1},{8,4},{9,5},{12,8},{13,9},{14,12},{15,13},... | collective-permute-start | bytes 1376264 | tf_op jit(solution)/shard_map/ppermute | solution.py:318
  112.8 18.4 %collective-permute-start.21 = (bf16[64,3584]{1,0:T(8,128)(2,1)S(1)}, bf16[64,3584]{1,0:T(8,128)(2,1)S(1)}, u32[]{:S(2)}, u32[]{:S(2)}) collective-permute-start(bf16[64,3584]{1,0:T(8,128)(2,1)S(1)} %get-tuple-element.195), channel_id=1, source_target_pairs={{0,2},{1,3},{4,0},{5,1},{8,4},{9,5},{12,8},{13,9},{14,12},{15,13},... | collective-permute-start | bytes 1376264 | tf_op jit(solution)/shard_map/ppermute | solution.py:318
  113.8 18.5 %collective-permute-start.22 = (bf16[64,3584]{1,0:T(8,128)(2,1)S(1)}, bf16[64,3584]{1,0:T(8,128)(2,1)S(1)}, u32[]{:S(2)}, u32[]{:S(2)}) collective-permute-start(bf16[64,3584]{1,0:T(8,128)(2,1)S(1)} %get-tuple-element.196), channel_id=1, source_target_pairs={{0,4},{1,5},{4,8},{5,9},{8,12},{9,13},{12,14},{13,15},{14,10},{15,... | collective-permute-start | bytes 1376264 | tf_op jit(solution)/shard_map/ppermute | solution.py:318
  122.6 14.6 %collective-permute-start.31 = (bf16[32,3584]{1,0:T(8,128)(2,1)S(1)}, bf16[32,3584]{1,0:T(8,128)(2,1)S(1)}, u32[]{:S(2)}, u32[]{:S(2)}) collective-permute-start(bf16[32,3584]{1,0:T(8,128)(2,1)S(1)} %get-tuple-element.215), channel_id=1, source_target_pairs={{0,4},{1,5},{4,8},{5,9},{8,12},{9,13},{12,14},{13,15},{14,10},{15,... | collective-permute-start | bytes 688136 | tf_op jit(solution)/shard_map/ppermute | solution.py:318
  124.3 13.0 %collective-permute-start.32 = (bf16[32,3584]{1,0:T(8,128)(2,1)S(1)}, bf16[32,3584]{1,0:T(8,128)(2,1)S(1)}, u32[]{:S(2)}, u32[]{:S(2)}) collective-permute-start(bf16[32,3584]{1,0:T(8,128)(2,1)S(1)} %get-tuple-element.216), channel_id=1, source_target_pairs={{0,2},{1,3},{4,0},{5,1},{8,4},{9,5},{12,8},{13,9},{14,12},{15,13},... | collective-permute-start | bytes 688136 | tf_op jit(solution)/shard_map/ppermute | solution.py:318
  124.7 17.5 %collective-permute-start.27 = (bf16[32,3584]{1,0:T(8,128)(2,1)S(1)}, bf16[32,3584]{1,0:T(8,128)(2,1)S(1)}, u32[]{:S(2)}, u32[]{:S(2)}) collective-permute-start(bf16[32,3584]{1,0:T(8,128)(2,1)S(1)} %get-tuple-element.211), channel_id=1, source_target_pairs={{0,4},{1,5},{4,8},{5,9},{8,12},{9,13},{12,14},{13,15},{14,10},{15,... | collective-permute-start | bytes 688136 | tf_op jit(solution)/shard_map/ppermute | solution.py:318
  131.2 11.0 %collective-permute-start.28 = (bf16[32,3584]{1,0:T(8,128)(2,1)S(1)}, bf16[32,3584]{1,0:T(8,128)(2,1)S(1)}, u32[]{:S(2)}, u32[]{:S(2)}) collective-permute-start(bf16[32,3584]{1,0:T(8,128)(2,1)S(1)} %get-tuple-element.212), channel_id=1, source_target_pairs={{0,2},{1,3},{4,0},{5,1},{8,4},{9,5},{12,8},{13,9},{14,12},{15,13},... | collective-permute-start | bytes 688136 | tf_op jit(solution)/shard_map/ppermute | solution.py:318
  137.3 8.9 %collective-permute-start.33 = (bf16[32,3584]{1,0:T(8,128)(2,1)S(1)}, bf16[32,3584]{1,0:T(8,128)(2,1)S(1)}, u32[]{:S(2)}, u32[]{:S(2)}) collective-permute-start(bf16[32,3584]{1,0:T(8,128)(2,1)S(1)} %get-tuple-element.217), channel_id=1, source_target_pairs={{0,4},{1,5},{4,8},{5,9},{8,12},{9,13},{12,14},{13,15},{14,10},{15,... | collective-permute-start | bytes 688136 | tf_op jit(solution)/shard_map/ppermute | solution.py:318
  139.0 7.3 %collective-permute-start.34 = (bf16[32,3584]{1,0:T(8,128)(2,1)S(1)}, bf16[32,3584]{1,0:T(8,128)(2,1)S(1)}, u32[]{:S(2)}, u32[]{:S(2)}) collective-permute-start(bf16[32,3584]{1,0:T(8,128)(2,1)S(1)} %get-tuple-element.218), channel_id=1, source_target_pairs={{0,2},{1,3},{4,0},{5,1},{8,4},{9,5},{12,8},{13,9},{14,12},{15,13},... | collective-permute-start | bytes 688136 | tf_op jit(solution)/shard_map/ppermute | solution.py:318
  142.2 6.5 %collective-permute-start.29 = (bf16[32,3584]{1,0:T(8,128)(2,1)S(1)}, bf16[32,3584]{1,0:T(8,128)(2,1)S(1)}, u32[]{:S(2)}, u32[]{:S(2)}) collective-permute-start(bf16[32,3584]{1,0:T(8,128)(2,1)S(1)} %get-tuple-element.213), channel_id=1, source_target_pairs={{0,4},{1,5},{4,8},{5,9},{8,12},{9,13},{12,14},{13,15},{14,10},{15,... | collective-permute-start | bytes 688136 | tf_op jit(solution)/shard_map/ppermute | solution.py:318
  143.9 6.0 %collective-permute-start.30 = (bf16[32,3584]{1,0:T(8,128)(2,1)S(1)}, bf16[32,3584]{1,0:T(8,128)(2,1)S(1)}, u32[]{:S(2)}, u32[]{:S(2)}) collective-permute-start(bf16[32,3584]{1,0:T(8,128)(2,1)S(1)} %get-tuple-element.214), channel_id=1, source_target_pairs={{0,2},{1,3},{4,0},{5,1},{8,4},{9,5},{12,8},{13,9},{14,12},{15,13},... | collective-permute-start | bytes 688136 | tf_op jit(solution)/shard_map/ppermute | solution.py:318

commit v16 on v15

--- a/solution.py
+++ b/solution.py
@@ -302,13 +302,6 @@
     last = [ahead[0][far], behind[0][far]]
     work([(far, 0), (far, 1)], last, last, done[-1])
     parts[-far, 1] = parts[far, 1]
-
-    firsts = [(1 - far, 0), (far - 1, 1)]
-    held, after = lax.optimization_barrier(
-        ([parts[name] for name in firsts], [parts[name] for name in done[-1]])
-    )
-    parts.update(zip(firsts, held))
-    parts.update(zip(done[-1], after))
 
     early = [(h, sign) for h in range(2) for sign in (1, -1) if (h == 0) != (sign == 1)]
     late = [(h, -sign) for h, sign in early]

time: 151 us -> 150 us (level)
  transfers between devices with their start and end apart: 35 -> 35, of which waited for: 25 -> 27; matrix products, arithmetic and copies ran while one was open for 0% -> 0% of each run, Pallas kernels for 25% -> 25%
where the time goes in v16:
time: 150 us
  waiting for transfers between devices  74.1 us (49%)
  Pallas kernels  39.1 us (26%)
  starting transfers between devices  35.3 us (24%)
    ppermute x18, waiting for transfers between devices, pass_on(): lax.ppermute(t, 'node', ways[sign])  44.8 us
    pallas_call x6, Pallas kernels, expert_parts(): pl.pallas_call(functools.partial(expert_kernel, n, shifts, experts, dim,...  36.1 us
    ppermute x18, starting transfers between devices, pass_on(): lax.ppermute(t, 'node', ways[sign])  18.6 us
    ppermute x2, waiting for transfers between devices, body(): near = [lax.ppermute(tokens, 'node', way) for way in (forward, backward)]  11.2 us
    ppermute x5, starting transfers between devices, send(): ahead[wave].append(lax.ppermute(pair[0], 'node', forward))  8.12 us
    ppermute x5, waiting for transfers between devices, send(): behind[wave].append(lax.ppermute(pair[1], 'node', backward))  6.96 us
    ppermute x3, waiting for transfers between devices, body(): other = [lax.ppermute(weight, 'node', swap) for weight in weights]  6.84 us
    ppermute x5, waiting for transfers between devices, send(): ahead[wave].append(lax.ppermute(pair[0], 'node', forward))  4.17 us
  transfers between devices with their start and end apart: 35, of which 27 were waited for; matrix products, arithmetic and copies ran while one was open for 0% of the time, Pallas kernels for 25%

profile of v16, /device:TPU:0, one launch (start us, length us, event | category | flops | bytes accessed | tf_op | source)
XLA Modules:
  0.0 150.2 jit_solution(17458808996808406765)
XLA Ops:
  0.5 3.0 %collective-permute-start = (bf16[128,3584]{1,0:T(8,128)(2,1)}, bf16[128,3584]{1,0:T(8,128)(2,1)S(1)}, u32[]{:S(2)}, u32[]{:S(2)}) collective-permute-start(bf16[128,3584]{1,0:T(8,128)(2,1)} %param.6), channel_id=1, source_target_pairs={{0,4},{1,5},{4,8},{5,9},{8,12},{9,13},{12,14},{13,15},{14,10},{15,... | collective-permute-start | bytes 2752520 | tf_op jit(solution)/shard_map/ppermute | solution.py:254
  5.1 1.6 %collective-permute-done.2.refs_15_.refs_7_ = bf16[3584,512]{1,0:T(8,128)(2,1)S(1)} collective-permute-done((bf16[3584,512]{1,0:T(8,128)(2,1)}, bf16[3584,512]{1,0:T(8,128)(2,1)S(1)}, u32[]{:S(2)}, u32[]{:S(2)}) %collective-permute-start.2) | collective-permute-done | bytes 3670048 | tf_op jit(solution)/shard_map/ppermute | solution.py:255
  6.7 5.2 %collective-permute-done.3.refs_16_.refs_8_ = bf16[3584,512]{1,0:T(8,128)(2,1)S(1)} collective-permute-done((bf16[3584,512]{1,0:T(8,128)(2,1)}, bf16[3584,512]{1,0:T(8,128)(2,1)S(1)}, u32[]{:S(2)}, u32[]{:S(2)}) %collective-permute-start.3) | collective-permute-done | bytes 3670048 | tf_op jit(solution)/shard_map/ppermute | solution.py:255
  11.9 2.9 %collective-permute-start.4 = (bf16[128,128]{1,0:T(8,128)(2,1)S(1)}, bf16[128,128]{1,0:T(8,128)(2,1)S(1)}, u32[]{:S(2)}, u32[]{:S(2)}) collective-permute-start(bf16[128,128]{1,0:T(8,128)(2,1)S(1)} %shard_map.65.refs_2_.refs_3_), channel_id=1, source_target_pairs={{0,4},{1,5},{4,8},{5,9},{8,12},{9,13},{12,14},{13,15},{14,10},{15,... | collective-permute-start | bytes 98312 | tf_op jit(solution)/shard_map/ppermute | solution.py:258
  14.9 9.7 %collective-permute-done.refs_0_ = bf16[128,3584]{1,0:T(8,128)(2,1)S(1)} collective-permute-done((bf16[128,3584]{1,0:T(8,128)(2,1)}, bf16[128,3584]{1,0:T(8,128)(2,1)S(1)}, u32[]{:S(2)}, u32[]{:S(2)}) %collective-permute-start) | collective-permute-done | bytes 917536 | tf_op jit(solution)/shard_map/ppermute | solution.py:254
  24.6 1.5 %collective-permute-done.1.refs_1_ = bf16[128,3584]{1,0:T(8,128)(2,1)S(1)} collective-permute-done((bf16[128,3584]{1,0:T(8,128)(2,1)}, bf16[128,3584]{1,0:T(8,128)(2,1)S(1)}, u32[]{:S(2)}, u32[]{:S(2)}) %collective-permute-start.1) | collective-permute-done | bytes 917536 | tf_op jit(solution)/shard_map/ppermute | solution.py:254
  26.5 1.6 %collective-permute-start.7 = (bf16[64,3712]{1,0:T(8,128)(2,1)S(1)}, bf16[64,3712]{1,0:T(8,128)(2,1)S(1)}, u32[]{:S(2)}, u32[]{:S(2)}) collective-permute-start(bf16[64,3712]{1,0:T(8,128)(2,1)S(1)} %get-tuple-element.134.refs_2_.refs_8_.refs_9_), channel_id=1, source_target_pairs={{0,4},{1,5},{4,8},{5,9},{8,12},{9,13},{12,14},{13,15},{14,10},{15,... | collective-permute-start | bytes 1425416 | tf_op jit(solution)/shard_map/ppermute | solution.py:284
  28.9 1.7 %collective-permute-start.9 = (bf16[64,3584]{1,0:T(8,128)(2,1)S(1)}, bf16[64,3584]{1,0:T(8,128)(2,1)S(1)}, u32[]{:S(2)}, u32[]{:S(2)}) collective-permute-start(bf16[64,3584]{1,0:T(8,128)(2,1)S(1)} %get-tuple-element.157.refs_3_), channel_id=1, source_target_pairs={{0,4},{1,5},{4,8},{5,9},{8,12},{9,13},{12,14},{13,15},{14,10},{15,... | collective-permute-start | bytes 1376264 | tf_op jit(solution)/shard_map/ppermute | solution.py:284
  31.5 10.8 %shard_map.69 = (bf16[64,3584]{1,0:T(8,128)(2,1)S(1)}, bf16[64,3584]{1,0:T(8,128)(2,1)S(1)}, bf16[64,3584]{1,0:T(8,128)(2,1)S(1)}, bf16[64,3584]{1,0:T(8,128)(2,...) custom-call(s32[1]{0:T(128)} %bitcast.expert_ref, ...), custom_call_target="tpu_custom_call" | custom-call | flops 1024 | bytes 1024 | tf_op jit(solution)/shard_map/pallas_call | solution.py:77
  42.4 1.6 %collective-permute-start.13 = (bf16[64,3712]{1,0:T(8,128)(2,1)S(1)}, bf16[64,3712]{1,0:T(8,128)(2,1)S(1)}, u32[]{:S(2)}, u32[]{:S(2)}) collective-permute-start(bf16[64,3712]{1,0:T(8,128)(2,1)S(1)} %collective-permute-done.7.refs_0_.refs_2_), channel_id=1, source_target_pairs={{0,4},{1,5},{4,8},{5,9},{8,12},{9,13},{12,14},{13,15},{14,10},{15,... | collective-permute-start | bytes 1425416 | tf_op jit(solution)/shard_map/ppermute | solution.py:284
  44.5 5.1 %shard_map.70 = (bf16[64,3584]{1,0:T(8,128)(2,1)S(1)}, bf16[64,3584]{1,0:T(8,128)(2,1)S(1)}) custom-call(s32[1]{0:T(128)} %bitcast.expert_ref, bf16[64,3712]{1,0:T(8,128)(2,1)S(1)} %collective-permute-done.7.refs_0_.refs_2_, bf16[64,3712]{1,0:T(8,128)(2,1)S(1)} %collective-permute-done.8.refs_1_.refs_3_, ...), custom_call_target="tpu_custom_call" | custom-call | flops 1024 | bytes 1024 | tf_op jit(solution)/shard_map/pallas_call | solution.py:77
  49.5 2.2 %collective-permute-done.10.refs_1_ = bf16[64,3584]{1,0:T(8,128)(2,1)S(1)} collective-permute-done((bf16[64,3584]{1,0:T(8,128)(2,1)S(1)}, bf16[64,3584]{1,0:T(8,128)(2,1)S(1)}, u32[]{:S(2)}, u32[]{:S(2)}) %collective-permute-start.10) | collective-permute-done | bytes 458784 | tf_op jit(solution)/shard_map/ppermute | solution.py:285
  51.8 1.6 %collective-permute-start.11 = (bf16[64,3584]{1,0:T(8,128)(2,1)S(1)}, bf16[64,3584]{1,0:T(8,128)(2,1)S(1)}, u32[]{:S(2)}, u32[]{:S(2)}) collective-permute-start(bf16[64,3584]{1,0:T(8,128)(2,1)S(1)} %collective-permute-done.9.refs_0_), channel_id=1, source_target_pairs={{0,4},{1,5},{4,8},{5,9},{8,12},{9,13},{12,14},{13,15},{14,10},{15,... | collective-permute-start | bytes 1376264 | tf_op jit(solution)/shard_map/ppermute | solution.py:284
  53.8 5.1 %shard_map.71 = (bf16[64,3584]{1,0:T(8,128)(2,1)S(1)}, bf16[64,3584]{1,0:T(8,128)(2,1)S(1)}) custom-call(s32[1]{0:T(128)} %bitcast.expert_ref, bf16[64,3584]{1,0:T(8,128)(2,1)S(1)} %collective-permute-done.9.refs_0_, bf16[64,3584]{1,0:T(8,128)(2,1)S(1)} %collective-permute-done.10.refs_1_, bf16[64,3712]{1,0:T(8,128)(2,1)S(1)} %collective-permute-done.7.refs_0_.refs_2_, ...), custom_call_target="tpu_custom_call" | custom-call | flops 10000000000 | bytes 1024 | tf_op jit(solution)/shard_map/pallas_call | solution.py:77
  58.9 1.5 collective-permute-done.13.refs_0_.refs_2_
  60.4 1.6 %collective-permute-done.14.refs_1_.refs_3_ = bf16[64,3712]{1,0:T(8,128)(2,1)S(1)} collective-permute-done((bf16[64,3712]{1,0:T(8,128)(2,1)S(1)}, bf16[64,3712]{1,0:T(8,128)(2,1)S(1)}, u32[]{:S(2)}, u32[]{:S(2)}) %collective-permute-start.14) | collective-permute-done | bytes 475168 | tf_op jit(solution)/shard_map/ppermute | solution.py:285
  61.9 1.6 %collective-permute-start.21 = (bf16[64,3712]{1,0:T(8,128)(2,1)S(1)}, bf16[64,3712]{1,0:T(8,128)(2,1)S(1)}, u32[]{:S(2)}, u32[]{:S(2)}) collective-permute-start(bf16[64,3712]{1,0:T(8,128)(2,1)S(1)} %collective-permute-done.13.refs_0_.refs_2_), channel_id=1, source_target_pairs={{0,4},{1,5},{4,8},{5,9},{8,12},{9,13},{12,14},{13,15},{14,10},{15,... | collective-permute-start | bytes 1425416 | tf_op jit(solution)/shard_map/ppermute | solution.py:284
  64.0 5.1 %shard_map.72 = (bf16[64,3584]{1,0:T(8,128)(2,1)S(1)}, bf16[64,3584]{1,0:T(8,128)(2,1)S(1)}) custom-call(s32[1]{0:T(128)} %bitcast.expert_ref, bf16[64,3712]{1,0:T(8,128)(2,1)S(1)} %collective-permute-done.13.refs_0_.refs_2_, bf16[64,3712]{1,0:T(8,128)(2,1)S(1)} %collective-permute-done.14.refs_1_.refs_3_, ...), custom_call_target="tpu_custom_call" | custom-call | flops 1024 | bytes 1024 | tf_op jit(solution)/shard_map/pallas_call | solution.py:77
  69.0 1.2 collective-permute-done.11.refs_0_
  70.2 1.6 %collective-permute-done.12.refs_1_ = bf16[64,3584]{1,0:T(8,128)(2,1)S(1)} collective-permute-done((bf16[64,3584]{1,0:T(8,128)(2,1)S(1)}, bf16[64,3584]{1,0:T(8,128)(2,1)S(1)}, u32[]{:S(2)}, u32[]{:S(2)}) %collective-permute-start.12) | collective-permute-done | bytes 458784 | tf_op jit(solution)/shard_map/ppermute | solution.py:285
  72.2 1.6 %collective-permute-start.16 = (bf16[64,3584]{1,0:T(8,128)(2,1)S(1)}, bf16[64,3584]{1,0:T(8,128)(2,1)S(1)}, u32[]{:S(2)}, u32[]{:S(2)}) collective-permute-start(bf16[64,3584]{1,0:T(8,128)(2,1)S(1)} %get-tuple-element.180), channel_id=1, source_target_pairs={{0,4},{1,5},{4,8},{5,9},{8,12},{9,13},{12,14},{13,15},{14,10},{15,... | collective-permute-start | bytes 1376264 | tf_op jit(solution)/shard_map/ppermute | solution.py:311
  73.8 5.1 %shard_map.76 = (bf16[64,3584]{1,0:T(8,128)(2,1)S(1)}, bf16[64,3584]{1,0:T(8,128)(2,1)S(1)}) custom-call(s32[1]{0:T(128)} %bitcast.expert_ref, bf16[64,3584]{1,0:T(8,128)(2,1)S(1)} %collective-permute-done.11.refs_0_, bf16[64,3584]{1,0:T(8,128)(2,1)S(1)} %collective-permute-done.12.refs_1_, bf16[64,3712]{1,0:T(8,128)(2,1)S(1)} %collective-permute-done.13.refs_0_.refs_2_, ...), custom_call_target="tpu_custom_call" | custom-call | flops 10000000000 | bytes 1024 | tf_op jit(solution)/shard_map/pallas_call | solution.py:77
  78.9 1.5 %collective-permute-done.21.refs_0_.refs_2_ = bf16[64,3712]{1,0:T(8,128)(2,1)S(1)} collective-permute-done((bf16[64,3712]{1,0:T(8,128)(2,1)S(1)}, bf16[64,3712]{1,0:T(8,128)(2,1)S(1)}, u32[]{:S(2)}, u32[]{:S(2)}) %collective-permute-start.21) | collective-permute-done | bytes 475168 | tf_op jit(solution)/shard_map/ppermute | solution.py:284
  80.4 1.6 %collective-permute-done.22.refs_1_.refs_3_ = bf16[64,3712]{1,0:T(8,128)(2,1)S(1)} collective-permute-done((bf16[64,3712]{1,0:T(8,128)(2,1)S(1)}, bf16[64,3712]{1,0:T(8,128)(2,1)S(1)}, u32[]{:S(2)}, u32[]{:S(2)}) %collective-permute-start.22) | collective-permute-done | bytes 475168 | tf_op jit(solution)/shard_map/ppermute | solution.py:285
  82.0 5.1 %shard_map.77 = (bf16[64,3584]{1,0:T(8,128)(2,1)S(1)}, bf16[64,3584]{1,0:T(8,128)(2,1)S(1)}) custom-call(s32[1]{0:T(128)} %bitcast.expert_ref, bf16[64,3712]{1,0:T(8,128)(2,1)S(1)} %collective-permute-done.21.refs_0_.refs_2_, bf16[64,3712]{1,0:T(8,128)(2,1)S(1)} %collective-permute-done.22.refs_1_.refs_3_, ...), custom_call_target="tpu_custom_call" | custom-call | flops 1024 | bytes 1024 | tf_op jit(solution)/shard_map/pallas_call | solution.py:77
  87.0 1.6 %collective-permute-start.23 = (bf16[64,3584]{1,0:T(8,128)(2,1)S(1)}, bf16[64,3584]{1,0:T(8,128)(2,1)S(1)}, u32[]{:S(2)}, u32[]{:S(2)}) collective-permute-start(bf16[64,3584]{1,0:T(8,128)(2,1)S(1)} %get-tuple-element.199), channel_id=1, source_target_pairs={{0,4},{1,5},{4,8},{5,9},{8,12},{9,13},{12,14},{13,15},{14,10},{15,... | collective-permute-start | bytes 1376264 | tf_op jit(solution)/shard_map/ppermute | solution.py:311
  89.1 2.7 %collective-permute-done.15.refs_2_ = bf16[64,3584]{1,0:T(8,128)(2,1)S(1)} collective-permute-done((bf16[64,3584]{1,0:T(8,128)(2,1)S(1)}, bf16[64,3584]{1,0:T(8,128)(2,1)S(1)}, u32[]{:S(2)}, u32[]{:S(2)}) %collective-permute-start.15) | collective-permute-done | bytes 458784 | tf_op jit(solution)/shard_map/ppermute | solution.py:311
  92.4 1.6 %collective-permute-start.18 = (bf16[64,3584]{1,0:T(8,128)(2,1)S(1)}, bf16[64,3584]{1,0:T(8,128)(2,1)S(1)}, u32[]{:S(2)}, u32[]{:S(2)}) collective-permute-start(bf16[64,3584]{1,0:T(8,128)(2,1)S(1)} %get-tuple-element.182), channel_id=1, source_target_pairs={{0,4},{1,5},{4,8},{5,9},{8,12},{9,13},{12,14},{13,15},{14,10},{15,... | collective-permute-start | bytes 1376264 | tf_op jit(solution)/shard_map/ppermute | solution.py:311
  94.0 6.6 %collective-permute-done.23.refs_2_ = bf16[64,3584]{1,0:T(8,128)(2,1)S(1)} collective-permute-done((bf16[64,3584]{1,0:T(8,128)(2,1)S(1)}, bf16[64,3584]{1,0:T(8,128)(2,1)S(1)}, u32[]{:S(2)}, u32[]{:S(2)}) %collective-permute-start.23) | collective-permute-done | bytes 458784 | tf_op jit(solution)/shard_map/ppermute | solution.py:311
  100.6 1.6 %collective-permute-done.24.refs_3_ = bf16[64,3584]{1,0:T(8,128)(2,1)S(1)} collective-permute-done((bf16[64,3584]{1,0:T(8,128)(2,1)S(1)}, bf16[64,3584]{1,0:T(8,128)(2,1)S(1)}, u32[]{:S(2)}, u32[]{:S(2)}) %collective-permute-start.24) | collective-permute-done | bytes 458784 | tf_op jit(solution)/shard_map/ppermute | solution.py:311
  102.2 1.6 %collective-permute-start.25 = (bf16[64,3584]{1,0:T(8,128)(2,1)S(1)}, bf16[64,3584]{1,0:T(8,128)(2,1)S(1)}, u32[]{:S(2)}, u32[]{:S(2)}) collective-permute-start(bf16[64,3584]{1,0:T(8,128)(2,1)S(1)} %get-tuple-element.201), channel_id=1, source_target_pairs={{0,4},{1,5},{4,8},{5,9},{8,12},{9,13},{12,14},{13,15},{14,10},{15,... | collective-permute-start | bytes 1376264 | tf_op jit(solution)/shard_map/ppermute | solution.py:311
  104.3 7.7 %collective-permute-done.17.refs_2_ = bf16[64,3584]{1,0:T(8,128)(2,1)S(1)} collective-permute-done((bf16[64,3584]{1,0:T(8,128)(2,1)S(1)}, bf16[64,3584]{1,0:T(8,128)(2,1)S(1)}, u32[]{:S(2)}, u32[]{:S(2)}) %collective-permute-start.17) | collective-permute-done | bytes 458784 | tf_op jit(solution)/shard_map/ppermute | solution.py:311
  112.6 1.6 %collective-permute-start.20 = (bf16[64,3584]{1,0:T(8,128)(2,1)S(1)}, bf16[64,3584]{1,0:T(8,128)(2,1)S(1)}, u32[]{:S(2)}, u32[]{:S(2)}) collective-permute-start(bf16[64,3584]{1,0:T(8,128)(2,1)S(1)} %get-tuple-element.184), channel_id=1, source_target_pairs={{0,4},{1,5},{4,8},{5,9},{8,12},{9,13},{12,14},{13,15},{14,10},{15,... | collective-permute-start | bytes 1376264 | tf_op jit(solution)/shard_map/ppermute | solution.py:311
  114.1 6.1 %collective-permute-done.25.refs_2_ = bf16[64,3584]{1,0:T(8,128)(2,1)S(1)} collective-permute-done((bf16[64,3584]{1,0:T(8,128)(2,1)S(1)}, bf16[64,3584]{1,0:T(8,128)(2,1)S(1)}, u32[]{:S(2)}, u32[]{:S(2)}) %collective-permute-start.25) | collective-permute-done | bytes 458784 | tf_op jit(solution)/shard_map/ppermute | solution.py:311
  120.2 1.6 %collective-permute-done.26.refs_3_ = bf16[64,3584]{1,0:T(8,128)(2,1)S(1)} collective-permute-done((bf16[64,3584]{1,0:T(8,128)(2,1)S(1)}, bf16[64,3584]{1,0:T(8,128)(2,1)S(1)}, u32[]{:S(2)}, u32[]{:S(2)}) %collective-permute-start.26) | collective-permute-done | bytes 458784 | tf_op jit(solution)/shard_map/ppermute | solution.py:311
  121.9 1.6 %collective-permute-start.31 = (bf16[32,3584]{1,0:T(8,128)(2,1)S(1)}, bf16[32,3584]{1,0:T(8,128)(2,1)S(1)}, u32[]{:S(2)}, u32[]{:S(2)}) collective-permute-start(bf16[32,3584]{1,0:T(8,128)(2,1)S(1)} %get-tuple-element.207), channel_id=1, source_target_pairs={{0,4},{1,5},{4,8},{5,9},{8,12},{9,13},{12,14},{13,15},{14,10},{15,... | collective-permute-start | bytes 688136 | tf_op jit(solution)/shard_map/ppermute | solution.py:311
  123.9 1.5 %collective-permute-start.27 = (bf16[32,3584]{1,0:T(8,128)(2,1)S(1)}, bf16[32,3584]{1,0:T(8,128)(2,1)S(1)}, u32[]{:S(2)}, u32[]{:S(2)}) collective-permute-start(bf16[32,3584]{1,0:T(8,128)(2,1)S(1)} %get-tuple-element.203), channel_id=1, source_target_pairs={{0,4},{1,5},{4,8},{5,9},{8,12},{9,13},{12,14},{13,15},{14,10},{15,... | collective-permute-start | bytes 688136 | tf_op jit(solution)/shard_map/ppermute | solution.py:311
  125.5 6.1 %collective-permute-done.19.refs_2_ = bf16[64,3584]{1,0:T(8,128)(2,1)S(1)} collective-permute-done((bf16[64,3584]{1,0:T(8,128)(2,1)S(1)}, bf16[64,3584]{1,0:T(8,128)(2,1)S(1)}, u32[]{:S(2)}, u32[]{:S(2)}) %collective-permute-start.19) | collective-permute-done | bytes 458784 | tf_op jit(solution)/shard_map/ppermute | solution.py:311
  132.3 2.7 %collective-permute-done.31.refs_2_ = bf16[32,3584]{1,0:T(8,128)(2,1)S(1)} collective-permute-done((bf16[32,3584]{1,0:T(8,128)(2,1)S(1)}, bf16[32,3584]{1,0:T(8,128)(2,1)S(1)}, u32[]{:S(2)}, u32[]{:S(2)}) %collective-permute-start.31) | collective-permute-done | bytes 229408 | tf_op jit(solution)/shard_map/ppermute | solution.py:311
  135.0 1.6 %collective-permute-done.32.refs_3_ = bf16[32,3584]{1,0:T(8,128)(2,1)S(1)} collective-permute-done((bf16[32,3584]{1,0:T(8,128)(2,1)S(1)}, bf16[32,3584]{1,0:T(8,128)(2,1)S(1)}, u32[]{:S(2)}, u32[]{:S(2)}) %collective-permute-start.32) | collective-permute-done | bytes 229408 | tf_op jit(solution)/shard_map/ppermute | solution.py:311
  136.6 1.6 %collective-permute-start.33 = (bf16[32,3584]{1,0:T(8,128)(2,1)S(1)}, bf16[32,3584]{1,0:T(8,128)(2,1)S(1)}, u32[]{:S(2)}, u32[]{:S(2)}) collective-permute-start(bf16[32,3584]{1,0:T(8,128)(2,1)S(1)} %get-tuple-element.209), channel_id=1, source_target_pairs={{0,4},{1,5},{4,8},{5,9},{8,12},{9,13},{12,14},{13,15},{14,10},{15,... | collective-permute-start | bytes 688136 | tf_op jit(solution)/shard_map/ppermute | solution.py:311
  138.6 1.2 collective-permute-done.27.refs_2_
  139.9 1.6 %collective-permute-done.28.refs_3_ = bf16[32,3584]{1,0:T(8,128)(2,1)S(1)} collective-permute-done((bf16[32,3584]{1,0:T(8,128)(2,1)S(1)}, bf16[32,3584]{1,0:T(8,128)(2,1)S(1)}, u32[]{:S(2)}, u32[]{:S(2)}) %collective-permute-start.28) | collective-permute-done | bytes 229408 | tf_op jit(solution)/shard_map/ppermute | solution.py:311
  141.5 1.6 %collective-permute-start.29 = (bf16[32,3584]{1,0:T(8,128)(2,1)S(1)}, bf16[32,3584]{1,0:T(8,128)(2,1)S(1)}, u32[]{:S(2)}, u32[]{:S(2)}) collective-permute-start(bf16[32,3584]{1,0:T(8,128)(2,1)S(1)} %get-tuple-element.205), channel_id=1, source_target_pairs={{0,4},{1,5},{4,8},{5,9},{8,12},{9,13},{12,14},{13,15},{14,10},{15,... | collective-permute-start | bytes 688136 | tf_op jit(solution)/shard_map/ppermute | solution.py:311
  144.5 1.3 collective-permute-done.34.refs_5_
  145.8 1.7 %collective-permute-done.29.refs_2_ = bf16[32,3584]{1,0:T(8,128)(2,1)S(1)} collective-permute-done((bf16[32,3584]{1,0:T(8,128)(2,1)S(1)}, bf16[32,3584]{1,0:T(8,128)(2,1)S(1)}, u32[]{:S(2)}, u32[]{:S(2)}) %collective-permute-start.29) | collective-permute-done | bytes 229408 | tf_op jit(solution)/shard_map/ppermute | solution.py:311
  147.6 1.5 %collective-permute-done.30.refs_3_ = bf16[32,3584]{1,0:T(8,128)(2,1)S(1)} collective-permute-done((bf16[32,3584]{1,0:T(8,128)(2,1)S(1)}, bf16[32,3584]{1,0:T(8,128)(2,1)S(1)}, u32[]{:S(2)}, u32[]{:S(2)}) %collective-permute-start.30) | collective-permute-done | bytes 229408 | tf_op jit(solution)/shard_map/ppermute | solution.py:311
  149.1 1.1 shard_map.82
  (54 shorter events, 11.5 us)
Async XLA Ops:
  0.0 6.7 %collective-permute-start.2 = (bf16[3584,512]{1,0:T(8,128)(2,1)}, bf16[3584,512]{1,0:T(8,128)(2,1)S(1)}, u32[]{:S(2)}, u32[]{:S(2)}) collective-permute-start(bf16[3584,512]{1,0:T(8,128)(2,1)} %refs_0_), channel_id=1, source_target_pairs={{0,1},{1,0},{2,3},{3,2},{4,5},{5,4},{6,7},{7,6},{8,9},{9,8},{10,11... | collective-permute-start | bytes 11010056 | tf_op jit(solution)/shard_map/ppermute | solution.py:255
  0.5 11.5 %collective-permute-start.3 = (bf16[3584,512]{1,0:T(8,128)(2,1)}, bf16[3584,512]{1,0:T(8,128)(2,1)S(1)}, u32[]{:S(2)}, u32[]{:S(2)}) collective-permute-start(bf16[3584,512]{1,0:T(8,128)(2,1)} %refs_1_), channel_id=1, source_target_pairs={{0,1},{1,0},{2,3},{3,2},{4,5},{5,4},{6,7},{7,6},{8,9},{9,8},{10,11... | collective-permute-start | bytes 11010056 | tf_op jit(solution)/shard_map/ppermute | solution.py:255
  0.5 24.0 %collective-permute-start = (bf16[128,3584]{1,0:T(8,128)(2,1)}, bf16[128,3584]{1,0:T(8,128)(2,1)S(1)}, u32[]{:S(2)}, u32[]{:S(2)}) collective-permute-start(bf16[128,3584]{1,0:T(8,128)(2,1)} %param.6), channel_id=1, source_target_pairs={{0,4},{1,5},{4,8},{5,9},{8,12},{9,13},{12,14},{13,15},{14,10},{15,... | collective-permute-start | bytes 2752520 | tf_op jit(solution)/shard_map/ppermute | solution.py:254
  3.5 22.5 %collective-permute-start.1 = (bf16[128,3584]{1,0:T(8,128)(2,1)}, bf16[128,3584]{1,0:T(8,128)(2,1)S(1)}, u32[]{:S(2)}, u32[]{:S(2)}) collective-permute-start(bf16[128,3584]{1,0:T(8,128)(2,1)} %param.6), channel_id=1, source_target_pairs={{0,2},{1,3},{4,0},{5,1},{8,4},{9,5},{12,8},{13,9},{14,12},{15,13},... | collective-permute-start | bytes 2752520 | tf_op jit(solution)/shard_map/ppermute | solution.py:254
  3.5 22.7 %collective-permute-start.6 = (bf16[512,3584]{1,0:T(8,128)(2,1)}, bf16[512,3584]{1,0:T(8,128)(2,1)S(1)}, u32[]{:S(2)}, u32[]{:S(2)}) collective-permute-start(bf16[512,3584]{1,0:T(8,128)(2,1)} %refs_2_), channel_id=1, source_target_pairs={{0,1},{1,0},{2,3},{3,2},{4,5},{5,4},{6,7},{7,6},{8,9},{9,8},{10,11... | collective-permute-start | bytes 11010056 | tf_op jit(solution)/shard_map/ppermute | solution.py:255
  3.5 0.7 copy-start.3
  4.2 0.7 copy-start.4
  5.1 25.5 %copy-start.5 = (bf16[128,3584]{1,0:T(8,128)(2,1)S(1)}, bf16[128,3584]{1,0:T(8,128)(2,1)}, u32[]{:S(2)}) copy-start(bf16[128,3584]{1,0:T(8,128)(2,1)} %param.6) | copy-start | bytes 2752516
  11.9 14.3 %collective-permute-start.4 = (bf16[128,128]{1,0:T(8,128)(2,1)S(1)}, bf16[128,128]{1,0:T(8,128)(2,1)S(1)}, u32[]{:S(2)}, u32[]{:S(2)}) collective-permute-start(bf16[128,128]{1,0:T(8,128)(2,1)S(1)} %shard_map.65.refs_2_.refs_3_), channel_id=1, source_target_pairs={{0,4},{1,5},{4,8},{5,9},{8,12},{9,13},{12,14},{13,15},{14,10},{15,... | collective-permute-start | bytes 98312 | tf_op jit(solution)/shard_map/ppermute | solution.py:258
  14.9 11.5 %collective-permute-start.5 = (bf16[128,128]{1,0:T(8,128)(2,1)S(1)}, bf16[128,128]{1,0:T(8,128)(2,1)S(1)}, u32[]{:S(2)}, u32[]{:S(2)}) collective-permute-start(bf16[128,128]{1,0:T(8,128)(2,1)S(1)} %shard_map.65.refs_2_.refs_3_), channel_id=1, source_target_pairs={{0,2},{1,3},{4,0},{5,1},{8,4},{9,5},{12,8},{13,9},{14,12},{15,13},... | collective-permute-start | bytes 98312 | tf_op jit(solution)/shard_map/ppermute | solution.py:258
  26.1 4.7 %copy-start.1 = (bf16[3584,512]{1,0:T(8,128)(2,1)S(1)}, bf16[3584,512]{1,0:T(8,128)(2,1)}, u32[]{:S(2)}) copy-start(bf16[3584,512]{1,0:T(8,128)(2,1)} %refs_1_) | copy-start | bytes 11010052
  26.1 4.7 %copy-start.2 = (bf16[512,3584]{1,0:T(8,128)(2,1)S(1)}, bf16[512,3584]{1,0:T(8,128)(2,1)}, u32[]{:S(2)}) copy-start(bf16[512,3584]{1,0:T(8,128)(2,1)} %refs_2_) | copy-start | bytes 11010052
  26.2 4.6 %copy-start = (bf16[3584,512]{1,0:T(8,128)(2,1)S(1)}, bf16[3584,512]{1,0:T(8,128)(2,1)}, u32[]{:S(2)}) copy-start(bf16[3584,512]{1,0:T(8,128)(2,1)} %refs_0_) | copy-start | bytes 11010052
  26.5 15.9 %collective-permute-start.7 = (bf16[64,3712]{1,0:T(8,128)(2,1)S(1)}, bf16[64,3712]{1,0:T(8,128)(2,1)S(1)}, u32[]{:S(2)}, u32[]{:S(2)}) collective-permute-start(bf16[64,3712]{1,0:T(8,128)(2,1)S(1)} %get-tuple-element.134.refs_2_.refs_8_.refs_9_), channel_id=1, source_target_pairs={{0,4},{1,5},{4,8},{5,9},{8,12},{9,13},{12,14},{13,15},{14,10},{15,... | collective-permute-start | bytes 1425416 | tf_op jit(solution)/shard_map/ppermute | solution.py:284
  28.1 14.2 %collective-permute-start.8 = (bf16[64,3712]{1,0:T(8,128)(2,1)S(1)}, bf16[64,3712]{1,0:T(8,128)(2,1)S(1)}, u32[]{:S(2)}, u32[]{:S(2)}) collective-permute-start(bf16[64,3712]{1,0:T(8,128)(2,1)S(1)} %get-tuple-element.124), channel_id=1, source_target_pairs={{0,2},{1,3},{4,0},{5,1},{8,4},{9,5},{12,8},{13,9},{14,12},{15,13},... | collective-permute-start | bytes 1425416 | tf_op jit(solution)/shard_map/ppermute | solution.py:285
  28.6 23.2 %collective-permute-start.10 = (bf16[64,3584]{1,0:T(8,128)(2,1)S(1)}, bf16[64,3584]{1,0:T(8,128)(2,1)S(1)}, u32[]{:S(2)}, u32[]{:S(2)}) collective-permute-start(bf16[64,3584]{1,0:T(8,128)(2,1)S(1)} %get-tuple-element.158.refs_4_), channel_id=1, source_target_pairs={{0,2},{1,3},{4,0},{5,1},{8,4},{9,5},{12,8},{13,9},{14,12},{15,13},... | collective-permute-start | bytes 1376264 | tf_op jit(solution)/shard_map/ppermute | solution.py:285
  28.9 22.9 %collective-permute-start.9 = (bf16[64,3584]{1,0:T(8,128)(2,1)S(1)}, bf16[64,3584]{1,0:T(8,128)(2,1)S(1)}, u32[]{:S(2)}, u32[]{:S(2)}) collective-permute-start(bf16[64,3584]{1,0:T(8,128)(2,1)S(1)} %get-tuple-element.157.refs_3_), channel_id=1, source_target_pairs={{0,4},{1,5},{4,8},{5,9},{8,12},{9,13},{12,14},{13,15},{14,10},{15,... | collective-permute-start | bytes 1376264 | tf_op jit(solution)/shard_map/ppermute | solution.py:284
  42.4 18.0 %collective-permute-start.13 = (bf16[64,3712]{1,0:T(8,128)(2,1)S(1)}, bf16[64,3712]{1,0:T(8,128)(2,1)S(1)}, u32[]{:S(2)}, u32[]{:S(2)}) collective-permute-start(bf16[64,3712]{1,0:T(8,128)(2,1)S(1)} %collective-permute-done.7.refs_0_.refs_2_), channel_id=1, source_target_pairs={{0,4},{1,5},{4,8},{5,9},{8,12},{9,13},{12,14},{13,15},{14,10},{15,... | collective-permute-start | bytes 1425416 | tf_op jit(solution)/shard_map/ppermute | solution.py:284
  44.0 17.9 %collective-permute-start.14 = (bf16[64,3712]{1,0:T(8,128)(2,1)S(1)}, bf16[64,3712]{1,0:T(8,128)(2,1)S(1)}, u32[]{:S(2)}, u32[]{:S(2)}) collective-permute-start(bf16[64,3712]{1,0:T(8,128)(2,1)S(1)} %collective-permute-done.8.refs_1_.refs_3_), channel_id=1, source_target_pairs={{0,2},{1,3},{4,0},{5,1},{8,4},{9,5},{12,8},{13,9},{14,12},{15,13},... | collective-permute-start | bytes 1425416 | tf_op jit(solution)/shard_map/ppermute | solution.py:285
  51.8 18.4 %collective-permute-start.11 = (bf16[64,3584]{1,0:T(8,128)(2,1)S(1)}, bf16[64,3584]{1,0:T(8,128)(2,1)S(1)}, u32[]{:S(2)}, u32[]{:S(2)}) collective-permute-start(bf16[64,3584]{1,0:T(8,128)(2,1)S(1)} %collective-permute-done.9.refs_0_), channel_id=1, source_target_pairs={{0,4},{1,5},{4,8},{5,9},{8,12},{9,13},{12,14},{13,15},{14,10},{15,... | collective-permute-start | bytes 1376264 | tf_op jit(solution)/shard_map/ppermute | solution.py:284
  53.3 18.4 %collective-permute-start.12 = (bf16[64,3584]{1,0:T(8,128)(2,1)S(1)}, bf16[64,3584]{1,0:T(8,128)(2,1)S(1)}, u32[]{:S(2)}, u32[]{:S(2)}) collective-permute-start(bf16[64,3584]{1,0:T(8,128)(2,1)S(1)} %collective-permute-done.10.refs_1_), channel_id=1, source_target_pairs={{0,2},{1,3},{4,0},{5,1},{8,4},{9,5},{12,8},{13,9},{14,12},{15,13},... | collective-permute-start | bytes 1376264 | tf_op jit(solution)/shard_map/ppermute | solution.py:285
  61.9 18.4 %collective-permute-start.21 = (bf16[64,3712]{1,0:T(8,128)(2,1)S(1)}, bf16[64,3712]{1,0:T(8,128)(2,1)S(1)}, u32[]{:S(2)}, u32[]{:S(2)}) collective-permute-start(bf16[64,3712]{1,0:T(8,128)(2,1)S(1)} %collective-permute-done.13.refs_0_.refs_2_), channel_id=1, source_target_pairs={{0,4},{1,5},{4,8},{5,9},{8,12},{9,13},{12,14},{13,15},{14,10},{15,... | collective-permute-start | bytes 1425416 | tf_op jit(solution)/shard_map/ppermute | solution.py:284
  63.5 18.4 %collective-permute-start.22 = (bf16[64,3712]{1,0:T(8,128)(2,1)S(1)}, bf16[64,3712]{1,0:T(8,128)(2,1)S(1)}, u32[]{:S(2)}, u32[]{:S(2)}) collective-permute-start(bf16[64,3712]{1,0:T(8,128)(2,1)S(1)} %collective-permute-done.14.refs_1_.refs_3_), channel_id=1, source_target_pairs={{0,2},{1,3},{4,0},{5,1},{8,4},{9,5},{12,8},{13,9},{14,12},{15,13},... | collective-permute-start | bytes 1425416 | tf_op jit(solution)/shard_map/ppermute | solution.py:285
  71.8 20.0 %collective-permute-start.15 = (bf16[64,3584]{1,0:T(8,128)(2,1)S(1)}, bf16[64,3584]{1,0:T(8,128)(2,1)S(1)}, u32[]{:S(2)}, u32[]{:S(2)}) collective-permute-start(bf16[64,3584]{1,0:T(8,128)(2,1)S(1)} %get-tuple-element.179), channel_id=1, source_target_pairs={{0,2},{1,3},{4,0},{5,1},{8,4},{9,5},{12,8},{13,9},{14,12},{15,13},... | collective-permute-start | bytes 1376264 | tf_op jit(solution)/shard_map/ppermute | solution.py:311
  72.2 19.6 %collective-permute-start.16 = (bf16[64,3584]{1,0:T(8,128)(2,1)S(1)}, bf16[64,3584]{1,0:T(8,128)(2,1)S(1)}, u32[]{:S(2)}, u32[]{:S(2)}) collective-permute-start(bf16[64,3584]{1,0:T(8,128)(2,1)S(1)} %get-tuple-element.180), channel_id=1, source_target_pairs={{0,4},{1,5},{4,8},{5,9},{8,12},{9,13},{12,14},{13,15},{14,10},{15,... | collective-permute-start | bytes 1376264 | tf_op jit(solution)/shard_map/ppermute | solution.py:311
  87.0 13.5 %collective-permute-start.23 = (bf16[64,3584]{1,0:T(8,128)(2,1)S(1)}, bf16[64,3584]{1,0:T(8,128)(2,1)S(1)}, u32[]{:S(2)}, u32[]{:S(2)}) collective-permute-start(bf16[64,3584]{1,0:T(8,128)(2,1)S(1)} %get-tuple-element.199), channel_id=1, source_target_pairs={{0,4},{1,5},{4,8},{5,9},{8,12},{9,13},{12,14},{13,15},{14,10},{15,... | collective-permute-start | bytes 1376264 | tf_op jit(solution)/shard_map/ppermute | solution.py:311
  88.7 13.5 %collective-permute-start.24 = (bf16[64,3584]{1,0:T(8,128)(2,1)S(1)}, bf16[64,3584]{1,0:T(8,128)(2,1)S(1)}, u32[]{:S(2)}, u32[]{:S(2)}) collective-permute-start(bf16[64,3584]{1,0:T(8,128)(2,1)S(1)} %get-tuple-element.200), channel_id=1, source_target_pairs={{0,2},{1,3},{4,0},{5,1},{8,4},{9,5},{12,8},{13,9},{14,12},{15,13},... | collective-permute-start | bytes 1376264 | tf_op jit(solution)/shard_map/ppermute | solution.py:311
  91.9 20.0 %collective-permute-start.17 = (bf16[64,3584]{1,0:T(8,128)(2,1)S(1)}, bf16[64,3584]{1,0:T(8,128)(2,1)S(1)}, u32[]{:S(2)}, u32[]{:S(2)}) collective-permute-start(bf16[64,3584]{1,0:T(8,128)(2,1)S(1)} %get-tuple-element.181), channel_id=1, source_target_pairs={{0,2},{1,3},{4,0},{5,1},{8,4},{9,5},{12,8},{13,9},{14,12},{15,13},... | collective-permute-start | bytes 1376264 | tf_op jit(solution)/shard_map/ppermute | solution.py:311
  92.4 19.5 %collective-permute-start.18 = (bf16[64,3584]{1,0:T(8,128)(2,1)S(1)}, bf16[64,3584]{1,0:T(8,128)(2,1)S(1)}, u32[]{:S(2)}, u32[]{:S(2)}) collective-permute-start(bf16[64,3584]{1,0:T(8,128)(2,1)S(1)} %get-tuple-element.182), channel_id=1, source_target_pairs={{0,4},{1,5},{4,8},{5,9},{8,12},{9,13},{12,14},{13,15},{14,10},{15,... | collective-permute-start | bytes 1376264 | tf_op jit(solution)/shard_map/ppermute | solution.py:311
  102.2 18.0 %collective-permute-start.25 = (bf16[64,3584]{1,0:T(8,128)(2,1)S(1)}, bf16[64,3584]{1,0:T(8,128)(2,1)S(1)}, u32[]{:S(2)}, u32[]{:S(2)}) collective-permute-start(bf16[64,3584]{1,0:T(8,128)(2,1)S(1)} %get-tuple-element.201), channel_id=1, source_target_pairs={{0,4},{1,5},{4,8},{5,9},{8,12},{9,13},{12,14},{13,15},{14,10},{15,... | collective-permute-start | bytes 1376264 | tf_op jit(solution)/shard_map/ppermute | solution.py:311
  103.8 18.0 %collective-permute-start.26 = (bf16[64,3584]{1,0:T(8,128)(2,1)S(1)}, bf16[64,3584]{1,0:T(8,128)(2,1)S(1)}, u32[]{:S(2)}, u32[]{:S(2)}) collective-permute-start(bf16[64,3584]{1,0:T(8,128)(2,1)S(1)} %get-tuple-element.202), channel_id=1, source_target_pairs={{0,2},{1,3},{4,0},{5,1},{8,4},{9,5},{12,8},{13,9},{14,12},{15,13},... | collective-permute-start | bytes 1376264 | tf_op jit(solution)/shard_map/ppermute | solution.py:311
  112.0 19.6 %collective-permute-start.19 = (bf16[64,3584]{1,0:T(8,128)(2,1)S(1)}, bf16[64,3584]{1,0:T(8,128)(2,1)S(1)}, u32[]{:S(2)}, u32[]{:S(2)}) collective-permute-start(bf16[64,3584]{1,0:T(8,128)(2,1)S(1)} %get-tuple-element.183), channel_id=1, source_target_pairs={{0,2},{1,3},{4,0},{5,1},{8,4},{9,5},{12,8},{13,9},{14,12},{15,13},... | collective-permute-start | bytes 1376264 | tf_op jit(solution)/shard_map/ppermute | solution.py:311
  112.6 19.5 %collective-permute-start.20 = (bf16[64,3584]{1,0:T(8,128)(2,1)S(1)}, bf16[64,3584]{1,0:T(8,128)(2,1)S(1)}, u32[]{:S(2)}, u32[]{:S(2)}) collective-permute-start(bf16[64,3584]{1,0:T(8,128)(2,1)S(1)} %get-tuple-element.184), channel_id=1, source_target_pairs={{0,4},{1,5},{4,8},{5,9},{8,12},{9,13},{12,14},{13,15},{14,10},{15,... | collective-permute-start | bytes 1376264 | tf_op jit(solution)/shard_map/ppermute | solution.py:311
  121.9 13.1 %collective-permute-start.31 = (bf16[32,3584]{1,0:T(8,128)(2,1)S(1)}, bf16[32,3584]{1,0:T(8,128)(2,1)S(1)}, u32[]{:S(2)}, u32[]{:S(2)}) collective-permute-start(bf16[32,3584]{1,0:T(8,128)(2,1)S(1)} %get-tuple-element.207), channel_id=1, source_target_pairs={{0,4},{1,5},{4,8},{5,9},{8,12},{9,13},{12,14},{13,15},{14,10},{15,... | collective-permute-start | bytes 688136 | tf_op jit(solution)/shard_map/ppermute | solution.py:311
  123.5 13.1 %collective-permute-start.32 = (bf16[32,3584]{1,0:T(8,128)(2,1)S(1)}, bf16[32,3584]{1,0:T(8,128)(2,1)S(1)}, u32[]{:S(2)}, u32[]{:S(2)}) collective-permute-start(bf16[32,3584]{1,0:T(8,128)(2,1)S(1)} %get-tuple-element.208), channel_id=1, source_target_pairs={{0,2},{1,3},{4,0},{5,1},{8,4},{9,5},{12,8},{13,9},{14,12},{15,13},... | collective-permute-start | bytes 688136 | tf_op jit(solution)/shard_map/ppermute | solution.py:311
  123.9 15.9 %collective-permute-start.27 = (bf16[32,3584]{1,0:T(8,128)(2,1)S(1)}, bf16[32,3584]{1,0:T(8,128)(2,1)S(1)}, u32[]{:S(2)}, u32[]{:S(2)}) collective-permute-start(bf16[32,3584]{1,0:T(8,128)(2,1)S(1)} %get-tuple-element.203), channel_id=1, source_target_pairs={{0,4},{1,5},{4,8},{5,9},{8,12},{9,13},{12,14},{13,15},{14,10},{15,... | collective-permute-start | bytes 688136 | tf_op jit(solution)/shard_map/ppermute | solution.py:311
  131.6 9.8 %collective-permute-start.28 = (bf16[32,3584]{1,0:T(8,128)(2,1)S(1)}, bf16[32,3584]{1,0:T(8,128)(2,1)S(1)}, u32[]{:S(2)}, u32[]{:S(2)}) collective-permute-start(bf16[32,3584]{1,0:T(8,128)(2,1)S(1)} %get-tuple-element.204), channel_id=1, source_target_pairs={{0,2},{1,3},{4,0},{5,1},{8,4},{9,5},{12,8},{13,9},{14,12},{15,13},... | collective-permute-start | bytes 688136 | tf_op jit(solution)/shard_map/ppermute | solution.py:311
  136.6 8.0 %collective-permute-start.33 = (bf16[32,3584]{1,0:T(8,128)(2,1)S(1)}, bf16[32,3584]{1,0:T(8,128)(2,1)S(1)}, u32[]{:S(2)}, u32[]{:S(2)}) collective-permute-start(bf16[32,3584]{1,0:T(8,128)(2,1)S(1)} %get-tuple-element.209), channel_id=1, source_target_pairs={{0,4},{1,5},{4,8},{5,9},{8,12},{9,13},{12,14},{13,15},{14,10},{15,... | collective-permute-start | bytes 688136 | tf_op jit(solution)/shard_map/ppermute | solution.py:311
  138.2 7.7 %collective-permute-start.34 = (bf16[32,3584]{1,0:T(8,128)(2,1)S(1)}, bf16[32,3584]{1,0:T(8,128)(2,1)S(1)}, u32[]{:S(2)}, u32[]{:S(2)}) collective-permute-start(bf16[32,3584]{1,0:T(8,128)(2,1)S(1)} %get-tuple-element.210), channel_id=1, source_target_pairs={{0,2},{1,3},{4,0},{5,1},{8,4},{9,5},{12,8},{13,9},{14,12},{15,13},... | collective-permute-start | bytes 688136 | tf_op jit(solution)/shard_map/ppermute | solution.py:311
  141.5 6.1 %collective-permute-start.29 = (bf16[32,3584]{1,0:T(8,128)(2,1)S(1)}, bf16[32,3584]{1,0:T(8,128)(2,1)S(1)}, u32[]{:S(2)}, u32[]{:S(2)}) collective-permute-start(bf16[32,3584]{1,0:T(8,128)(2,1)S(1)} %get-tuple-element.205), channel_id=1, source_target_pairs={{0,4},{1,5},{4,8},{5,9},{8,12},{9,13},{12,14},{13,15},{14,10},{15,... | collective-permute-start | bytes 688136 | tf_op jit(solution)/shard_map/ppermute | solution.py:311
  143.1 6.0 %collective-permute-start.30 = (bf16[32,3584]{1,0:T(8,128)(2,1)S(1)}, bf16[32,3584]{1,0:T(8,128)(2,1)S(1)}, u32[]{:S(2)}, u32[]{:S(2)}) collective-permute-start(bf16[32,3584]{1,0:T(8,128)(2,1)S(1)} %get-tuple-element.206), channel_id=1, source_target_pairs={{0,2},{1,3},{4,0},{5,1},{8,4},{9,5},{12,8},{13,9},{14,12},{15,13},... | collective-permute-start | bytes 688136 | tf_op jit(solution)/shard_map/ppermute | solution.py:311

commit v17 on v16

--- a/solution.py
+++ b/solution.py
@@ -300,7 +300,7 @@
             cost = FORWARD // 4 if wave else 1024
             done.append(work(names, blocks, sources, after, cost=cost))
     last = [ahead[0][far], behind[0][far]]
-    work([(far, 0), (far, 1)], last, last, done[-1])
+    work([(far, 0), (far, 1)], last, last)
     parts[-far, 1] = parts[far, 1]
 
     early = [(h, sign) for h in range(2) for sign in (1, -1) if (h == 0) != (sign == 1)]

time: 150 us -> 154 us (1.027)
  waiting for transfers between devices: 74.1 us -> 77.1 us
    ppermute x18, waiting for transfers between devices: 44.8 us -> 50.9 us  [pass_on(): lax.ppermute(t, 'node', ways[sign])]
    ppermute x5, waiting for transfers between devices: 6.96 us -> 4.73 us  [send(): behind[wave].append(lax.ppermute(pair[1], 'node', backward))]
  transfers between devices with their start and end apart: 35 -> 35, of which waited for: 27 -> 24; matrix products, arithmetic and copies ran while one was open for 0% -> 0% of each run, Pallas kernels for 25% -> 25%
where the time goes in v17:
time: 154 us; the launch traced here: 153 us
  waiting for transfers between devices  77.1 us (50%)
  Pallas kernels  39 us (25%)
  starting transfers between devices  35.6 us (23%)
    ppermute x18, waiting for transfers between devices, pass_on(): lax.ppermute(t, 'node', ways[sign])  50.9 us
    pallas_call x6, Pallas kernels, expert_parts(): pl.pallas_call(functools.partial(expert_kernel, n, shifts, experts, dim,...  36.1 us
    ppermute x18, starting transfers between devices, pass_on(): lax.ppermute(t, 'node', ways[sign])  18.9 us
    ppermute x2, waiting for transfers between devices, body(): near = [lax.ppermute(tokens, 'node', way) for way in (forward, backward)]  11.2 us
    ppermute x5, starting transfers between devices, send(): ahead[wave].append(lax.ppermute(pair[0], 'node', forward))  7.98 us
    ppermute x3, waiting for transfers between devices, body(): other = [lax.ppermute(weight, 'node', swap) for weight in weights]  6.84 us
    ppermute x5, waiting for transfers between devices, send(): behind[wave].append(lax.ppermute(pair[1], 'node', backward))  4.73 us
    ppermute x5, waiting for transfers between devices, send(): ahead[wave].append(lax.ppermute(pair[0], 'node', forward))  3.32 us
  transfers between devices with their start and end apart: 35, of which 24 were waited for; matrix products, arithmetic and copies ran while one was open for 0% of the time, Pallas kernels for 25%

profile of v17, /device:TPU:0, one launch (start us, length us, event | category | flops | bytes accessed | tf_op | source)
XLA Modules:
  0.0 153.4 jit_solution(13753022623809226053)
XLA Ops:
  0.5 3.0 %collective-permute-start = (bf16[128,3584]{1,0:T(8,128)(2,1)}, bf16[128,3584]{1,0:T(8,128)(2,1)S(1)}, u32[]{:S(2)}, u32[]{:S(2)}) collective-permute-start(bf16[128,3584]{1,0:T(8,128)(2,1)} %param.6), channel_id=1, source_target_pairs={{0,4},{1,5},{4,8},{5,9},{8,12},{9,13},{12,14},{13,15},{14,10},{15,... | collective-permute-start | bytes 2752520 | tf_op jit(solution)/shard_map/ppermute | solution.py:254
  3.5 0.7 copy-done.3
  4.2 0.7 copy-done.4
  5.1 1.6 %collective-permute-done.2.refs_15_.refs_7_ = bf16[3584,512]{1,0:T(8,128)(2,1)S(1)} collective-permute-done((bf16[3584,512]{1,0:T(8,128)(2,1)}, bf16[3584,512]{1,0:T(8,128)(2,1)S(1)}, u32[]{:S(2)}, u32[]{:S(2)}) %collective-permute-start.2) | collective-permute-done | bytes 3670048 | tf_op jit(solution)/shard_map/ppermute | solution.py:255
  6.7 5.2 %collective-permute-done.3.refs_16_.refs_8_ = bf16[3584,512]{1,0:T(8,128)(2,1)S(1)} collective-permute-done((bf16[3584,512]{1,0:T(8,128)(2,1)}, bf16[3584,512]{1,0:T(8,128)(2,1)S(1)}, u32[]{:S(2)}, u32[]{:S(2)}) %collective-permute-start.3) | collective-permute-done | bytes 3670048 | tf_op jit(solution)/shard_map/ppermute | solution.py:255
  11.9 2.9 %collective-permute-start.4 = (bf16[128,128]{1,0:T(8,128)(2,1)S(1)}, bf16[128,128]{1,0:T(8,128)(2,1)S(1)}, u32[]{:S(2)}, u32[]{:S(2)}) collective-permute-start(bf16[128,128]{1,0:T(8,128)(2,1)S(1)} %shard_map.65.refs_2_.refs_3_), channel_id=1, source_target_pairs={{0,4},{1,5},{4,8},{5,9},{8,12},{9,13},{12,14},{13,15},{14,10},{15,... | collective-permute-start | bytes 98312 | tf_op jit(solution)/shard_map/ppermute | solution.py:258
  14.9 9.7 %collective-permute-done.refs_0_ = bf16[128,3584]{1,0:T(8,128)(2,1)S(1)} collective-permute-done((bf16[128,3584]{1,0:T(8,128)(2,1)}, bf16[128,3584]{1,0:T(8,128)(2,1)S(1)}, u32[]{:S(2)}, u32[]{:S(2)}) %collective-permute-start) | collective-permute-done | bytes 917536 | tf_op jit(solution)/shard_map/ppermute | solution.py:254
  24.6 1.5 collective-permute-done.1.refs_1_
  26.5 1.6 %collective-permute-start.7 = (bf16[64,3712]{1,0:T(8,128)(2,1)S(1)}, bf16[64,3712]{1,0:T(8,128)(2,1)S(1)}, u32[]{:S(2)}, u32[]{:S(2)}) collective-permute-start(bf16[64,3712]{1,0:T(8,128)(2,1)S(1)} %get-tuple-element.132.refs_2_.refs_8_.refs_9_), channel_id=1, source_target_pairs={{0,4},{1,5},{4,8},{5,9},{8,12},{9,13},{12,14},{13,15},{14,10},{15,... | collective-permute-start | bytes 1425416 | tf_op jit(solution)/shard_map/ppermute | solution.py:284
  28.6 1.6 %collective-permute-start.9 = (bf16[64,3584]{1,0:T(8,128)(2,1)S(1)}, bf16[64,3584]{1,0:T(8,128)(2,1)S(1)}, u32[]{:S(2)}, u32[]{:S(2)}) collective-permute-start(bf16[64,3584]{1,0:T(8,128)(2,1)S(1)} %get-tuple-element.155.refs_3_), channel_id=1, source_target_pairs={{0,4},{1,5},{4,8},{5,9},{8,12},{9,13},{12,14},{13,15},{14,10},{15,... | collective-permute-start | bytes 1376264 | tf_op jit(solution)/shard_map/ppermute | solution.py:284
  30.8 0.8 shard_map.68
  31.5 10.8 %shard_map.69 = (bf16[64,3584]{1,0:T(8,128)(2,1)S(1)}, bf16[64,3584]{1,0:T(8,128)(2,1)S(1)}, bf16[64,3584]{1,0:T(8,128)(2,1)S(1)}, bf16[64,3584]{1,0:T(8,128)(2,...) custom-call(s32[1]{0:T(128)} %bitcast.expert_ref, ...), custom_call_target="tpu_custom_call" | custom-call | flops 1024 | bytes 1024 | tf_op jit(solution)/shard_map/pallas_call | solution.py:77
  42.4 1.6 %collective-permute-start.13 = (bf16[64,3712]{1,0:T(8,128)(2,1)S(1)}, bf16[64,3712]{1,0:T(8,128)(2,1)S(1)}, u32[]{:S(2)}, u32[]{:S(2)}) collective-permute-start(bf16[64,3712]{1,0:T(8,128)(2,1)S(1)} %collective-permute-done.7.refs_0_.refs_2_), channel_id=1, source_target_pairs={{0,4},{1,5},{4,8},{5,9},{8,12},{9,13},{12,14},{13,15},{14,10},{15,... | collective-permute-start | bytes 1425416 | tf_op jit(solution)/shard_map/ppermute | solution.py:284
  44.5 5.1 %shard_map.70 = (bf16[64,3584]{1,0:T(8,128)(2,1)S(1)}, bf16[64,3584]{1,0:T(8,128)(2,1)S(1)}) custom-call(s32[1]{0:T(128)} %bitcast.expert_ref, bf16[64,3712]{1,0:T(8,128)(2,1)S(1)} %collective-permute-done.7.refs_0_.refs_2_, bf16[64,3712]{1,0:T(8,128)(2,1)S(1)} %collective-permute-done.8.refs_1_.refs_3_, ...), custom_call_target="tpu_custom_call" | custom-call | flops 1024 | bytes 1024 | tf_op jit(solution)/shard_map/pallas_call | solution.py:77
  50.2 1.6 %collective-permute-done.10.refs_1_ = bf16[64,3584]{1,0:T(8,128)(2,1)S(1)} collective-permute-done((bf16[64,3584]{1,0:T(8,128)(2,1)S(1)}, bf16[64,3584]{1,0:T(8,128)(2,1)S(1)}, u32[]{:S(2)}, u32[]{:S(2)}) %collective-permute-start.10) | collective-permute-done | bytes 458784 | tf_op jit(solution)/shard_map/ppermute | solution.py:285
  51.8 1.6 %collective-permute-start.11 = (bf16[64,3584]{1,0:T(8,128)(2,1)S(1)}, bf16[64,3584]{1,0:T(8,128)(2,1)S(1)}, u32[]{:S(2)}, u32[]{:S(2)}) collective-permute-start(bf16[64,3584]{1,0:T(8,128)(2,1)S(1)} %collective-permute-done.9.refs_0_), channel_id=1, source_target_pairs={{0,4},{1,5},{4,8},{5,9},{8,12},{9,13},{12,14},{13,15},{14,10},{15,... | collective-permute-start | bytes 1376264 | tf_op jit(solution)/shard_map/ppermute | solution.py:284
  53.8 5.1 %shard_map.71 = (bf16[64,3584]{1,0:T(8,128)(2,1)S(1)}, bf16[64,3584]{1,0:T(8,128)(2,1)S(1)}) custom-call(s32[1]{0:T(128)} %bitcast.expert_ref, bf16[64,3584]{1,0:T(8,128)(2,1)S(1)} %collective-permute-done.9.refs_0_, bf16[64,3584]{1,0:T(8,128)(2,1)S(1)} %collective-permute-done.10.refs_1_, bf16[64,3712]{1,0:T(8,128)(2,1)S(1)} %collective-permute-done.7.refs_0_.refs_2_, ...), custom_call_target="tpu_custom_call" | custom-call | flops 10000000000 | bytes 1024 | tf_op jit(solution)/shard_map/pallas_call | solution.py:77
  58.9 1.5 collective-permute-done.13.refs_0_.refs_2_
  60.4 1.6 %collective-permute-done.14.refs_1_.refs_3_ = bf16[64,3712]{1,0:T(8,128)(2,1)S(1)} collective-permute-done((bf16[64,3712]{1,0:T(8,128)(2,1)S(1)}, bf16[64,3712]{1,0:T(8,128)(2,1)S(1)}, u32[]{:S(2)}, u32[]{:S(2)}) %collective-permute-start.14) | collective-permute-done | bytes 475168 | tf_op jit(solution)/shard_map/ppermute | solution.py:285
  61.9 1.6 %collective-permute-start.21 = (bf16[64,3712]{1,0:T(8,128)(2,1)S(1)}, bf16[64,3712]{1,0:T(8,128)(2,1)S(1)}, u32[]{:S(2)}, u32[]{:S(2)}) collective-permute-start(bf16[64,3712]{1,0:T(8,128)(2,1)S(1)} %collective-permute-done.13.refs_0_.refs_2_), channel_id=1, source_target_pairs={{0,4},{1,5},{4,8},{5,9},{8,12},{9,13},{12,14},{13,15},{14,10},{15,... | collective-permute-start | bytes 1425416 | tf_op jit(solution)/shard_map/ppermute | solution.py:284
  64.0 5.1 %shard_map.72 = (bf16[64,3584]{1,0:T(8,128)(2,1)S(1)}, bf16[64,3584]{1,0:T(8,128)(2,1)S(1)}) custom-call(s32[1]{0:T(128)} %bitcast.expert_ref, bf16[64,3712]{1,0:T(8,128)(2,1)S(1)} %collective-permute-done.13.refs_0_.refs_2_, bf16[64,3712]{1,0:T(8,128)(2,1)S(1)} %collective-permute-done.14.refs_1_.refs_3_, ...), custom_call_target="tpu_custom_call" | custom-call | flops 1024 | bytes 1024 | tf_op jit(solution)/shard_map/pallas_call | solution.py:77
  69.0 1.2 collective-permute-done.11.refs_0_
  70.2 1.6 %collective-permute-done.12.refs_1_ = bf16[64,3584]{1,0:T(8,128)(2,1)S(1)} collective-permute-done((bf16[64,3584]{1,0:T(8,128)(2,1)S(1)}, bf16[64,3584]{1,0:T(8,128)(2,1)S(1)}, u32[]{:S(2)}, u32[]{:S(2)}) %collective-permute-start.12) | collective-permute-done | bytes 458784 | tf_op jit(solution)/shard_map/ppermute | solution.py:285
  72.2 1.6 %collective-permute-start.16 = (bf16[64,3584]{1,0:T(8,128)(2,1)S(1)}, bf16[64,3584]{1,0:T(8,128)(2,1)S(1)}, u32[]{:S(2)}, u32[]{:S(2)}) collective-permute-start(bf16[64,3584]{1,0:T(8,128)(2,1)S(1)} %get-tuple-element.178), channel_id=1, source_target_pairs={{0,4},{1,5},{4,8},{5,9},{8,12},{9,13},{12,14},{13,15},{14,10},{15,... | collective-permute-start | bytes 1376264 | tf_op jit(solution)/shard_map/ppermute | solution.py:311
  73.8 15.5 %collective-permute-done.15.refs_2_ = bf16[64,3584]{1,0:T(8,128)(2,1)S(1)} collective-permute-done((bf16[64,3584]{1,0:T(8,128)(2,1)S(1)}, bf16[64,3584]{1,0:T(8,128)(2,1)S(1)}, u32[]{:S(2)}, u32[]{:S(2)}) %collective-permute-start.15) | collective-permute-done | bytes 458784 | tf_op jit(solution)/shard_map/ppermute | solution.py:311
  89.9 1.6 %collective-permute-start.18 = (bf16[64,3584]{1,0:T(8,128)(2,1)S(1)}, bf16[64,3584]{1,0:T(8,128)(2,1)S(1)}, u32[]{:S(2)}, u32[]{:S(2)}) collective-permute-start(bf16[64,3584]{1,0:T(8,128)(2,1)S(1)} %get-tuple-element.180), channel_id=1, source_target_pairs={{0,4},{1,5},{4,8},{5,9},{8,12},{9,13},{12,14},{13,15},{14,10},{15,... | collective-permute-start | bytes 1376264 | tf_op jit(solution)/shard_map/ppermute | solution.py:311
  91.5 5.1 %shard_map.77 = (bf16[64,3584]{1,0:T(8,128)(2,1)S(1)}, bf16[64,3584]{1,0:T(8,128)(2,1)S(1)}) custom-call(s32[1]{0:T(128)} %bitcast.expert_ref, bf16[64,3712]{1,0:T(8,128)(2,1)S(1)} %collective-permute-done.21.refs_0_.refs_2_, bf16[64,3712]{1,0:T(8,128)(2,1)S(1)} %collective-permute-done.22.refs_1_.refs_3_, ...), custom_call_target="tpu_custom_call" | custom-call | flops 1024 | bytes 1024 | tf_op jit(solution)/shard_map/pallas_call | solution.py:77
  96.6 1.6 %collective-permute-start.23 = (bf16[64,3584]{1,0:T(8,128)(2,1)S(1)}, bf16[64,3584]{1,0:T(8,128)(2,1)S(1)}, u32[]{:S(2)}, u32[]{:S(2)}) collective-permute-start(bf16[64,3584]{1,0:T(8,128)(2,1)S(1)} %get-tuple-element.195), channel_id=1, source_target_pairs={{0,4},{1,5},{4,8},{5,9},{8,12},{9,13},{12,14},{13,15},{14,10},{15,... | collective-permute-start | bytes 1376264 | tf_op jit(solution)/shard_map/ppermute | solution.py:311
  98.6 5.1 %shard_map.76 = (bf16[64,3584]{1,0:T(8,128)(2,1)S(1)}, bf16[64,3584]{1,0:T(8,128)(2,1)S(1)}) custom-call(s32[1]{0:T(128)} %bitcast.expert_ref, bf16[64,3584]{1,0:T(8,128)(2,1)S(1)} %collective-permute-done.11.refs_0_, bf16[64,3584]{1,0:T(8,128)(2,1)S(1)} %collective-permute-done.12.refs_1_, bf16[64,3712]{1,0:T(8,128)(2,1)S(1)} %collective-permute-done.13.refs_0_.refs_2_, ...), custom_call_target="tpu_custom_call" | custom-call | flops 10000000000 | bytes 1024 | tf_op jit(solution)/shard_map/pallas_call | solution.py:77
  103.7 5.8 %collective-permute-done.23.refs_2_ = bf16[64,3584]{1,0:T(8,128)(2,1)S(1)} collective-permute-done((bf16[64,3584]{1,0:T(8,128)(2,1)S(1)}, bf16[64,3584]{1,0:T(8,128)(2,1)S(1)}, u32[]{:S(2)}, u32[]{:S(2)}) %collective-permute-start.23) | collective-permute-done | bytes 458784 | tf_op jit(solution)/shard_map/ppermute | solution.py:311
  109.6 1.6 %collective-permute-start.25 = (bf16[64,3584]{1,0:T(8,128)(2,1)S(1)}, bf16[64,3584]{1,0:T(8,128)(2,1)S(1)}, u32[]{:S(2)}, u32[]{:S(2)}) collective-permute-start(bf16[64,3584]{1,0:T(8,128)(2,1)S(1)} %get-tuple-element.197), channel_id=1, source_target_pairs={{0,4},{1,5},{4,8},{5,9},{8,12},{9,13},{12,14},{13,15},{14,10},{15,... | collective-permute-start | bytes 1376264 | tf_op jit(solution)/shard_map/ppermute | solution.py:311
  111.8 1.1 collective-permute-start.19
  112.9 1.0 collective-permute-start.20
  113.9 9.2 %collective-permute-done.25.refs_2_ = bf16[64,3584]{1,0:T(8,128)(2,1)S(1)} collective-permute-done((bf16[64,3584]{1,0:T(8,128)(2,1)S(1)}, bf16[64,3584]{1,0:T(8,128)(2,1)S(1)}, u32[]{:S(2)}, u32[]{:S(2)}) %collective-permute-start.25) | collective-permute-done | bytes 458784 | tf_op jit(solution)/shard_map/ppermute | solution.py:311
  123.1 1.6 %collective-permute-done.26.refs_3_ = bf16[64,3584]{1,0:T(8,128)(2,1)S(1)} collective-permute-done((bf16[64,3584]{1,0:T(8,128)(2,1)S(1)}, bf16[64,3584]{1,0:T(8,128)(2,1)S(1)}, u32[]{:S(2)}, u32[]{:S(2)}) %collective-permute-start.26) | collective-permute-done | bytes 458784 | tf_op jit(solution)/shard_map/ppermute | solution.py:311
  124.8 1.9 %collective-permute-start.27 = (bf16[32,3584]{1,0:T(8,128)(2,1)S(1)}, bf16[32,3584]{1,0:T(8,128)(2,1)S(1)}, u32[]{:S(2)}, u32[]{:S(2)}) collective-permute-start(bf16[32,3584]{1,0:T(8,128)(2,1)S(1)} %get-tuple-element.199), channel_id=1, source_target_pairs={{0,4},{1,5},{4,8},{5,9},{8,12},{9,13},{12,14},{13,15},{14,10},{15,... | collective-permute-start | bytes 688136 | tf_op jit(solution)/shard_map/ppermute | solution.py:311
  126.9 1.8 %collective-permute-start.31 = (bf16[32,3584]{1,0:T(8,128)(2,1)S(1)}, bf16[32,3584]{1,0:T(8,128)(2,1)S(1)}, u32[]{:S(2)}, u32[]{:S(2)}) collective-permute-start(bf16[32,3584]{1,0:T(8,128)(2,1)S(1)} %get-tuple-element.203), channel_id=1, source_target_pairs={{0,4},{1,5},{4,8},{5,9},{8,12},{9,13},{12,14},{13,15},{14,10},{15,... | collective-permute-start | bytes 688136 | tf_op jit(solution)/shard_map/ppermute | solution.py:311
  128.7 5.8 %collective-permute-done.19.refs_2_ = bf16[64,3584]{1,0:T(8,128)(2,1)S(1)} collective-permute-done((bf16[64,3584]{1,0:T(8,128)(2,1)S(1)}, bf16[64,3584]{1,0:T(8,128)(2,1)S(1)}, u32[]{:S(2)}, u32[]{:S(2)}) %collective-permute-start.19) | collective-permute-done | bytes 458784 | tf_op jit(solution)/shard_map/ppermute | solution.py:311
  135.2 2.7 %collective-permute-done.27.refs_2_ = bf16[32,3584]{1,0:T(8,128)(2,1)S(1)} collective-permute-done((bf16[32,3584]{1,0:T(8,128)(2,1)S(1)}, bf16[32,3584]{1,0:T(8,128)(2,1)S(1)}, u32[]{:S(2)}, u32[]{:S(2)}) %collective-permute-start.27) | collective-permute-done | bytes 229408 | tf_op jit(solution)/shard_map/ppermute | solution.py:311
  137.9 1.6 %collective-permute-done.28.refs_3_ = bf16[32,3584]{1,0:T(8,128)(2,1)S(1)} collective-permute-done((bf16[32,3584]{1,0:T(8,128)(2,1)S(1)}, bf16[32,3584]{1,0:T(8,128)(2,1)S(1)}, u32[]{:S(2)}, u32[]{:S(2)}) %collective-permute-start.28) | collective-permute-done | bytes 229408 | tf_op jit(solution)/shard_map/ppermute | solution.py:311
  139.5 1.9 %collective-permute-start.29 = (bf16[32,3584]{1,0:T(8,128)(2,1)S(1)}, bf16[32,3584]{1,0:T(8,128)(2,1)S(1)}, u32[]{:S(2)}, u32[]{:S(2)}) collective-permute-start(bf16[32,3584]{1,0:T(8,128)(2,1)S(1)} %get-tuple-element.201), channel_id=1, source_target_pairs={{0,4},{1,5},{4,8},{5,9},{8,12},{9,13},{12,14},{13,15},{14,10},{15,... | collective-permute-start | bytes 688136 | tf_op jit(solution)/shard_map/ppermute | solution.py:311
  141.6 1.2 collective-permute-done.31.refs_2_
  142.8 1.6 %collective-permute-done.32.refs_3_ = bf16[32,3584]{1,0:T(8,128)(2,1)S(1)} collective-permute-done((bf16[32,3584]{1,0:T(8,128)(2,1)S(1)}, bf16[32,3584]{1,0:T(8,128)(2,1)S(1)}, u32[]{:S(2)}, u32[]{:S(2)}) %collective-permute-start.32) | collective-permute-done | bytes 229408 | tf_op jit(solution)/shard_map/ppermute | solution.py:311
  144.4 1.9 %collective-permute-start.33 = (bf16[32,3584]{1,0:T(8,128)(2,1)S(1)}, bf16[32,3584]{1,0:T(8,128)(2,1)S(1)}, u32[]{:S(2)}, u32[]{:S(2)}) collective-permute-start(bf16[32,3584]{1,0:T(8,128)(2,1)S(1)} %get-tuple-element.205), channel_id=1, source_target_pairs={{0,4},{1,5},{4,8},{5,9},{8,12},{9,13},{12,14},{13,15},{14,10},{15,... | collective-permute-start | bytes 688136 | tf_op jit(solution)/shard_map/ppermute | solution.py:311
  146.8 1.3 collective-permute-done.30.refs_3_
  148.1 2.4 %collective-permute-done.33.refs_4_ = bf16[32,3584]{1,0:T(8,128)(2,1)S(1)} collective-permute-done((bf16[32,3584]{1,0:T(8,128)(2,1)S(1)}, bf16[32,3584]{1,0:T(8,128)(2,1)S(1)}, u32[]{:S(2)}, u32[]{:S(2)}) %collective-permute-start.33) | collective-permute-done | bytes 229408 | tf_op jit(solution)/shard_map/ppermute | solution.py:311
  150.5 1.8 %collective-permute-done.34.refs_5_ = bf16[32,3584]{1,0:T(8,128)(2,1)S(1)} collective-permute-done((bf16[32,3584]{1,0:T(8,128)(2,1)S(1)}, bf16[32,3584]{1,0:T(8,128)(2,1)S(1)}, u32[]{:S(2)}, u32[]{:S(2)}) %collective-permute-start.34) | collective-permute-done | bytes 229408 | tf_op jit(solution)/shard_map/ppermute | solution.py:311
  152.3 1.1 shard_map.82
  (54 shorter events, 7.9 us)
Async XLA Ops:
  0.0 6.7 %collective-permute-start.2 = (bf16[3584,512]{1,0:T(8,128)(2,1)}, bf16[3584,512]{1,0:T(8,128)(2,1)S(1)}, u32[]{:S(2)}, u32[]{:S(2)}) collective-permute-start(bf16[3584,512]{1,0:T(8,128)(2,1)} %refs_0_), channel_id=1, source_target_pairs={{0,1},{1,0},{2,3},{3,2},{4,5},{5,4},{6,7},{7,6},{8,9},{9,8},{10,11... | collective-permute-start | bytes 11010056 | tf_op jit(solution)/shard_map/ppermute | solution.py:255
  0.5 11.5 %collective-permute-start.3 = (bf16[3584,512]{1,0:T(8,128)(2,1)}, bf16[3584,512]{1,0:T(8,128)(2,1)S(1)}, u32[]{:S(2)}, u32[]{:S(2)}) collective-permute-start(bf16[3584,512]{1,0:T(8,128)(2,1)} %refs_1_), channel_id=1, source_target_pairs={{0,1},{1,0},{2,3},{3,2},{4,5},{5,4},{6,7},{7,6},{8,9},{9,8},{10,11... | collective-permute-start | bytes 11010056 | tf_op jit(solution)/shard_map/ppermute | solution.py:255
  0.5 24.0 %collective-permute-start = (bf16[128,3584]{1,0:T(8,128)(2,1)}, bf16[128,3584]{1,0:T(8,128)(2,1)S(1)}, u32[]{:S(2)}, u32[]{:S(2)}) collective-permute-start(bf16[128,3584]{1,0:T(8,128)(2,1)} %param.6), channel_id=1, source_target_pairs={{0,4},{1,5},{4,8},{5,9},{8,12},{9,13},{12,14},{13,15},{14,10},{15,... | collective-permute-start | bytes 2752520 | tf_op jit(solution)/shard_map/ppermute | solution.py:254
  3.5 22.5 %collective-permute-start.1 = (bf16[128,3584]{1,0:T(8,128)(2,1)}, bf16[128,3584]{1,0:T(8,128)(2,1)S(1)}, u32[]{:S(2)}, u32[]{:S(2)}) collective-permute-start(bf16[128,3584]{1,0:T(8,128)(2,1)} %param.6), channel_id=1, source_target_pairs={{0,2},{1,3},{4,0},{5,1},{8,4},{9,5},{12,8},{13,9},{14,12},{15,13},... | collective-permute-start | bytes 2752520 | tf_op jit(solution)/shard_map/ppermute | solution.py:254
  3.5 22.7 %collective-permute-start.6 = (bf16[512,3584]{1,0:T(8,128)(2,1)}, bf16[512,3584]{1,0:T(8,128)(2,1)S(1)}, u32[]{:S(2)}, u32[]{:S(2)}) collective-permute-start(bf16[512,3584]{1,0:T(8,128)(2,1)} %refs_2_), channel_id=1, source_target_pairs={{0,1},{1,0},{2,3},{3,2},{4,5},{5,4},{6,7},{7,6},{8,9},{9,8},{10,11... | collective-permute-start | bytes 11010056 | tf_op jit(solution)/shard_map/ppermute | solution.py:255
  3.5 0.7 copy-start.3
  4.2 0.7 copy-start.4
  5.1 25.5 %copy-start.5 = (bf16[128,3584]{1,0:T(8,128)(2,1)S(1)}, bf16[128,3584]{1,0:T(8,128)(2,1)}, u32[]{:S(2)}) copy-start(bf16[128,3584]{1,0:T(8,128)(2,1)} %param.6) | copy-start | bytes 2752516
  11.9 14.3 %collective-permute-start.4 = (bf16[128,128]{1,0:T(8,128)(2,1)S(1)}, bf16[128,128]{1,0:T(8,128)(2,1)S(1)}, u32[]{:S(2)}, u32[]{:S(2)}) collective-permute-start(bf16[128,128]{1,0:T(8,128)(2,1)S(1)} %shard_map.65.refs_2_.refs_3_), channel_id=1, source_target_pairs={{0,4},{1,5},{4,8},{5,9},{8,12},{9,13},{12,14},{13,15},{14,10},{15,... | collective-permute-start | bytes 98312 | tf_op jit(solution)/shard_map/ppermute | solution.py:258
  14.9 11.5 %collective-permute-start.5 = (bf16[128,128]{1,0:T(8,128)(2,1)S(1)}, bf16[128,128]{1,0:T(8,128)(2,1)S(1)}, u32[]{:S(2)}, u32[]{:S(2)}) collective-permute-start(bf16[128,128]{1,0:T(8,128)(2,1)S(1)} %shard_map.65.refs_2_.refs_3_), channel_id=1, source_target_pairs={{0,2},{1,3},{4,0},{5,1},{8,4},{9,5},{12,8},{13,9},{14,12},{15,13},... | collective-permute-start | bytes 98312 | tf_op jit(solution)/shard_map/ppermute | solution.py:258
  26.1 4.7 %copy-start.1 = (bf16[3584,512]{1,0:T(8,128)(2,1)S(1)}, bf16[3584,512]{1,0:T(8,128)(2,1)}, u32[]{:S(2)}) copy-start(bf16[3584,512]{1,0:T(8,128)(2,1)} %refs_1_) | copy-start | bytes 11010052
  26.1 4.7 %copy-start.2 = (bf16[512,3584]{1,0:T(8,128)(2,1)S(1)}, bf16[512,3584]{1,0:T(8,128)(2,1)}, u32[]{:S(2)}) copy-start(bf16[512,3584]{1,0:T(8,128)(2,1)} %refs_2_) | copy-start | bytes 11010052
  26.2 4.6 %copy-start = (bf16[3584,512]{1,0:T(8,128)(2,1)S(1)}, bf16[3584,512]{1,0:T(8,128)(2,1)}, u32[]{:S(2)}) copy-start(bf16[3584,512]{1,0:T(8,128)(2,1)} %refs_0_) | copy-start | bytes 11010052
  26.5 15.9 %collective-permute-start.7 = (bf16[64,3712]{1,0:T(8,128)(2,1)S(1)}, bf16[64,3712]{1,0:T(8,128)(2,1)S(1)}, u32[]{:S(2)}, u32[]{:S(2)}) collective-permute-start(bf16[64,3712]{1,0:T(8,128)(2,1)S(1)} %get-tuple-element.132.refs_2_.refs_8_.refs_9_), channel_id=1, source_target_pairs={{0,4},{1,5},{4,8},{5,9},{8,12},{9,13},{12,14},{13,15},{14,10},{15,... | collective-permute-start | bytes 1425416 | tf_op jit(solution)/shard_map/ppermute | solution.py:284
  28.1 14.2 %collective-permute-start.8 = (bf16[64,3712]{1,0:T(8,128)(2,1)S(1)}, bf16[64,3712]{1,0:T(8,128)(2,1)S(1)}, u32[]{:S(2)}, u32[]{:S(2)}) collective-permute-start(bf16[64,3712]{1,0:T(8,128)(2,1)S(1)} %get-tuple-element.122), channel_id=1, source_target_pairs={{0,2},{1,3},{4,0},{5,1},{8,4},{9,5},{12,8},{13,9},{14,12},{15,13},... | collective-permute-start | bytes 1425416 | tf_op jit(solution)/shard_map/ppermute | solution.py:285
  28.6 21.6 %collective-permute-start.9 = (bf16[64,3584]{1,0:T(8,128)(2,1)S(1)}, bf16[64,3584]{1,0:T(8,128)(2,1)S(1)}, u32[]{:S(2)}, u32[]{:S(2)}) collective-permute-start(bf16[64,3584]{1,0:T(8,128)(2,1)S(1)} %get-tuple-element.155.refs_3_), channel_id=1, source_target_pairs={{0,4},{1,5},{4,8},{5,9},{8,12},{9,13},{12,14},{13,15},{14,10},{15,... | collective-permute-start | bytes 1376264 | tf_op jit(solution)/shard_map/ppermute | solution.py:284
  30.2 21.6 %collective-permute-start.10 = (bf16[64,3584]{1,0:T(8,128)(2,1)S(1)}, bf16[64,3584]{1,0:T(8,128)(2,1)S(1)}, u32[]{:S(2)}, u32[]{:S(2)}) collective-permute-start(bf16[64,3584]{1,0:T(8,128)(2,1)S(1)} %get-tuple-element.156.refs_4_), channel_id=1, source_target_pairs={{0,2},{1,3},{4,0},{5,1},{8,4},{9,5},{12,8},{13,9},{14,12},{15,13},... | collective-permute-start | bytes 1376264 | tf_op jit(solution)/shard_map/ppermute | solution.py:285
  42.4 18.0 %collective-permute-start.13 = (bf16[64,3712]{1,0:T(8,128)(2,1)S(1)}, bf16[64,3712]{1,0:T(8,128)(2,1)S(1)}, u32[]{:S(2)}, u32[]{:S(2)}) collective-permute-start(bf16[64,3712]{1,0:T(8,128)(2,1)S(1)} %collective-permute-done.7.refs_0_.refs_2_), channel_id=1, source_target_pairs={{0,4},{1,5},{4,8},{5,9},{8,12},{9,13},{12,14},{13,15},{14,10},{15,... | collective-permute-start | bytes 1425416 | tf_op jit(solution)/shard_map/ppermute | solution.py:284
  44.0 17.9 %collective-permute-start.14 = (bf16[64,3712]{1,0:T(8,128)(2,1)S(1)}, bf16[64,3712]{1,0:T(8,128)(2,1)S(1)}, u32[]{:S(2)}, u32[]{:S(2)}) collective-permute-start(bf16[64,3712]{1,0:T(8,128)(2,1)S(1)} %collective-permute-done.8.refs_1_.refs_3_), channel_id=1, source_target_pairs={{0,2},{1,3},{4,0},{5,1},{8,4},{9,5},{12,8},{13,9},{14,12},{15,13},... | collective-permute-start | bytes 1425416 | tf_op jit(solution)/shard_map/ppermute | solution.py:285
  51.8 18.4 %collective-permute-start.11 = (bf16[64,3584]{1,0:T(8,128)(2,1)S(1)}, bf16[64,3584]{1,0:T(8,128)(2,1)S(1)}, u32[]{:S(2)}, u32[]{:S(2)}) collective-permute-start(bf16[64,3584]{1,0:T(8,128)(2,1)S(1)} %collective-permute-done.9.refs_0_), channel_id=1, source_target_pairs={{0,4},{1,5},{4,8},{5,9},{8,12},{9,13},{12,14},{13,15},{14,10},{15,... | collective-permute-start | bytes 1376264 | tf_op jit(solution)/shard_map/ppermute | solution.py:284
  53.3 18.4 %collective-permute-start.12 = (bf16[64,3584]{1,0:T(8,128)(2,1)S(1)}, bf16[64,3584]{1,0:T(8,128)(2,1)S(1)}, u32[]{:S(2)}, u32[]{:S(2)}) collective-permute-start(bf16[64,3584]{1,0:T(8,128)(2,1)S(1)} %collective-permute-done.10.refs_1_), channel_id=1, source_target_pairs={{0,2},{1,3},{4,0},{5,1},{8,4},{9,5},{12,8},{13,9},{14,12},{15,13},... | collective-permute-start | bytes 1376264 | tf_op jit(solution)/shard_map/ppermute | solution.py:285
  61.9 29.5 %collective-permute-start.21 = (bf16[64,3712]{1,0:T(8,128)(2,1)S(1)}, bf16[64,3712]{1,0:T(8,128)(2,1)S(1)}, u32[]{:S(2)}, u32[]{:S(2)}) collective-permute-start(bf16[64,3712]{1,0:T(8,128)(2,1)S(1)} %collective-permute-done.13.refs_0_.refs_2_), channel_id=1, source_target_pairs={{0,4},{1,5},{4,8},{5,9},{8,12},{9,13},{12,14},{13,15},{14,10},{15,... | collective-permute-start | bytes 1425416 | tf_op jit(solution)/shard_map/ppermute | solution.py:284
  63.5 28.0 %collective-permute-start.22 = (bf16[64,3712]{1,0:T(8,128)(2,1)S(1)}, bf16[64,3712]{1,0:T(8,128)(2,1)S(1)}, u32[]{:S(2)}, u32[]{:S(2)}) collective-permute-start(bf16[64,3712]{1,0:T(8,128)(2,1)S(1)} %collective-permute-done.14.refs_1_.refs_3_), channel_id=1, source_target_pairs={{0,2},{1,3},{4,0},{5,1},{8,4},{9,5},{12,8},{13,9},{14,12},{15,13},... | collective-permute-start | bytes 1425416 | tf_op jit(solution)/shard_map/ppermute | solution.py:285
  71.8 17.5 %collective-permute-start.15 = (bf16[64,3584]{1,0:T(8,128)(2,1)S(1)}, bf16[64,3584]{1,0:T(8,128)(2,1)S(1)}, u32[]{:S(2)}, u32[]{:S(2)}) collective-permute-start(bf16[64,3584]{1,0:T(8,128)(2,1)S(1)} %get-tuple-element.177), channel_id=1, source_target_pairs={{0,2},{1,3},{4,0},{5,1},{8,4},{9,5},{12,8},{13,9},{14,12},{15,13},... | collective-permute-start | bytes 1376264 | tf_op jit(solution)/shard_map/ppermute | solution.py:311
  72.2 17.1 %collective-permute-start.16 = (bf16[64,3584]{1,0:T(8,128)(2,1)S(1)}, bf16[64,3584]{1,0:T(8,128)(2,1)S(1)}, u32[]{:S(2)}, u32[]{:S(2)}) collective-permute-start(bf16[64,3584]{1,0:T(8,128)(2,1)S(1)} %get-tuple-element.178), channel_id=1, source_target_pairs={{0,4},{1,5},{4,8},{5,9},{8,12},{9,13},{12,14},{13,15},{14,10},{15,... | collective-permute-start | bytes 1376264 | tf_op jit(solution)/shard_map/ppermute | solution.py:311
  89.4 22.3 %collective-permute-start.17 = (bf16[64,3584]{1,0:T(8,128)(2,1)S(1)}, bf16[64,3584]{1,0:T(8,128)(2,1)S(1)}, u32[]{:S(2)}, u32[]{:S(2)}) collective-permute-start(bf16[64,3584]{1,0:T(8,128)(2,1)S(1)} %get-tuple-element.179), channel_id=1, source_target_pairs={{0,2},{1,3},{4,0},{5,1},{8,4},{9,5},{12,8},{13,9},{14,12},{15,13},... | collective-permute-start | bytes 1376264 | tf_op jit(solution)/shard_map/ppermute | solution.py:311
  89.9 21.8 %collective-permute-start.18 = (bf16[64,3584]{1,0:T(8,128)(2,1)S(1)}, bf16[64,3584]{1,0:T(8,128)(2,1)S(1)}, u32[]{:S(2)}, u32[]{:S(2)}) collective-permute-start(bf16[64,3584]{1,0:T(8,128)(2,1)S(1)} %get-tuple-element.180), channel_id=1, source_target_pairs={{0,4},{1,5},{4,8},{5,9},{8,12},{9,13},{12,14},{13,15},{14,10},{15,... | collective-permute-start | bytes 1376264 | tf_op jit(solution)/shard_map/ppermute | solution.py:311
  96.6 13.0 %collective-permute-start.23 = (bf16[64,3584]{1,0:T(8,128)(2,1)S(1)}, bf16[64,3584]{1,0:T(8,128)(2,1)S(1)}, u32[]{:S(2)}, u32[]{:S(2)}) collective-permute-start(bf16[64,3584]{1,0:T(8,128)(2,1)S(1)} %get-tuple-element.195), channel_id=1, source_target_pairs={{0,4},{1,5},{4,8},{5,9},{8,12},{9,13},{12,14},{13,15},{14,10},{15,... | collective-permute-start | bytes 1376264 | tf_op jit(solution)/shard_map/ppermute | solution.py:311
  98.2 11.3 %collective-permute-start.24 = (bf16[64,3584]{1,0:T(8,128)(2,1)S(1)}, bf16[64,3584]{1,0:T(8,128)(2,1)S(1)}, u32[]{:S(2)}, u32[]{:S(2)}) collective-permute-start(bf16[64,3584]{1,0:T(8,128)(2,1)S(1)} %get-tuple-element.196), channel_id=1, source_target_pairs={{0,2},{1,3},{4,0},{5,1},{8,4},{9,5},{12,8},{13,9},{14,12},{15,13},... | collective-permute-start | bytes 1376264 | tf_op jit(solution)/shard_map/ppermute | solution.py:311
  109.6 13.5 %collective-permute-start.25 = (bf16[64,3584]{1,0:T(8,128)(2,1)S(1)}, bf16[64,3584]{1,0:T(8,128)(2,1)S(1)}, u32[]{:S(2)}, u32[]{:S(2)}) collective-permute-start(bf16[64,3584]{1,0:T(8,128)(2,1)S(1)} %get-tuple-element.197), channel_id=1, source_target_pairs={{0,4},{1,5},{4,8},{5,9},{8,12},{9,13},{12,14},{13,15},{14,10},{15,... | collective-permute-start | bytes 1376264 | tf_op jit(solution)/shard_map/ppermute | solution.py:311
  111.2 13.5 %collective-permute-start.26 = (bf16[64,3584]{1,0:T(8,128)(2,1)S(1)}, bf16[64,3584]{1,0:T(8,128)(2,1)S(1)}, u32[]{:S(2)}, u32[]{:S(2)}) collective-permute-start(bf16[64,3584]{1,0:T(8,128)(2,1)S(1)} %get-tuple-element.198), channel_id=1, source_target_pairs={{0,2},{1,3},{4,0},{5,1},{8,4},{9,5},{12,8},{13,9},{14,12},{15,13},... | collective-permute-start | bytes 1376264 | tf_op jit(solution)/shard_map/ppermute | solution.py:311
  111.8 22.7 %collective-permute-start.19 = (bf16[64,3584]{1,0:T(8,128)(2,1)S(1)}, bf16[64,3584]{1,0:T(8,128)(2,1)S(1)}, u32[]{:S(2)}, u32[]{:S(2)}) collective-permute-start(bf16[64,3584]{1,0:T(8,128)(2,1)S(1)} %get-tuple-element.181), channel_id=1, source_target_pairs={{0,2},{1,3},{4,0},{5,1},{8,4},{9,5},{12,8},{13,9},{14,12},{15,13},... | collective-permute-start | bytes 1376264 | tf_op jit(solution)/shard_map/ppermute | solution.py:311
  112.9 22.1 %collective-permute-start.20 = (bf16[64,3584]{1,0:T(8,128)(2,1)S(1)}, bf16[64,3584]{1,0:T(8,128)(2,1)S(1)}, u32[]{:S(2)}, u32[]{:S(2)}) collective-permute-start(bf16[64,3584]{1,0:T(8,128)(2,1)S(1)} %get-tuple-element.182), channel_id=1, source_target_pairs={{0,4},{1,5},{4,8},{5,9},{8,12},{9,13},{12,14},{13,15},{14,10},{15,... | collective-permute-start | bytes 1376264 | tf_op jit(solution)/shard_map/ppermute | solution.py:311
  124.8 13.1 %collective-permute-start.27 = (bf16[32,3584]{1,0:T(8,128)(2,1)S(1)}, bf16[32,3584]{1,0:T(8,128)(2,1)S(1)}, u32[]{:S(2)}, u32[]{:S(2)}) collective-permute-start(bf16[32,3584]{1,0:T(8,128)(2,1)S(1)} %get-tuple-element.199), channel_id=1, source_target_pairs={{0,4},{1,5},{4,8},{5,9},{8,12},{9,13},{12,14},{13,15},{14,10},{15,... | collective-permute-start | bytes 688136 | tf_op jit(solution)/shard_map/ppermute | solution.py:311
  126.7 12.8 %collective-permute-start.28 = (bf16[32,3584]{1,0:T(8,128)(2,1)S(1)}, bf16[32,3584]{1,0:T(8,128)(2,1)S(1)}, u32[]{:S(2)}, u32[]{:S(2)}) collective-permute-start(bf16[32,3584]{1,0:T(8,128)(2,1)S(1)} %get-tuple-element.200), channel_id=1, source_target_pairs={{0,2},{1,3},{4,0},{5,1},{8,4},{9,5},{12,8},{13,9},{14,12},{15,13},... | collective-permute-start | bytes 688136 | tf_op jit(solution)/shard_map/ppermute | solution.py:311
  126.9 15.9 %collective-permute-start.31 = (bf16[32,3584]{1,0:T(8,128)(2,1)S(1)}, bf16[32,3584]{1,0:T(8,128)(2,1)S(1)}, u32[]{:S(2)}, u32[]{:S(2)}) collective-permute-start(bf16[32,3584]{1,0:T(8,128)(2,1)S(1)} %get-tuple-element.203), channel_id=1, source_target_pairs={{0,4},{1,5},{4,8},{5,9},{8,12},{9,13},{12,14},{13,15},{14,10},{15,... | collective-permute-start | bytes 688136 | tf_op jit(solution)/shard_map/ppermute | solution.py:311
  134.5 9.8 %collective-permute-start.32 = (bf16[32,3584]{1,0:T(8,128)(2,1)S(1)}, bf16[32,3584]{1,0:T(8,128)(2,1)S(1)}, u32[]{:S(2)}, u32[]{:S(2)}) collective-permute-start(bf16[32,3584]{1,0:T(8,128)(2,1)S(1)} %get-tuple-element.204), channel_id=1, source_target_pairs={{0,2},{1,3},{4,0},{5,1},{8,4},{9,5},{12,8},{13,9},{14,12},{15,13},... | collective-permute-start | bytes 688136 | tf_op jit(solution)/shard_map/ppermute | solution.py:311
  139.5 7.2 %collective-permute-start.29 = (bf16[32,3584]{1,0:T(8,128)(2,1)S(1)}, bf16[32,3584]{1,0:T(8,128)(2,1)S(1)}, u32[]{:S(2)}, u32[]{:S(2)}) collective-permute-start(bf16[32,3584]{1,0:T(8,128)(2,1)S(1)} %get-tuple-element.201), channel_id=1, source_target_pairs={{0,4},{1,5},{4,8},{5,9},{8,12},{9,13},{12,14},{13,15},{14,10},{15,... | collective-permute-start | bytes 688136 | tf_op jit(solution)/shard_map/ppermute | solution.py:311
  141.4 6.7 %collective-permute-start.30 = (bf16[32,3584]{1,0:T(8,128)(2,1)S(1)}, bf16[32,3584]{1,0:T(8,128)(2,1)S(1)}, u32[]{:S(2)}, u32[]{:S(2)}) collective-permute-start(bf16[32,3584]{1,0:T(8,128)(2,1)S(1)} %get-tuple-element.202), channel_id=1, source_target_pairs={{0,2},{1,3},{4,0},{5,1},{8,4},{9,5},{12,8},{13,9},{14,12},{15,13},... | collective-permute-start | bytes 688136 | tf_op jit(solution)/shard_map/ppermute | solution.py:311
  144.4 6.1 %collective-permute-start.33 = (bf16[32,3584]{1,0:T(8,128)(2,1)S(1)}, bf16[32,3584]{1,0:T(8,128)(2,1)S(1)}, u32[]{:S(2)}, u32[]{:S(2)}) collective-permute-start(bf16[32,3584]{1,0:T(8,128)(2,1)S(1)} %get-tuple-element.205), channel_id=1, source_target_pairs={{0,4},{1,5},{4,8},{5,9},{8,12},{9,13},{12,14},{13,15},{14,10},{15,... | collective-permute-start | bytes 688136 | tf_op jit(solution)/shard_map/ppermute | solution.py:311
  146.3 6.0 %collective-permute-start.34 = (bf16[32,3584]{1,0:T(8,128)(2,1)S(1)}, bf16[32,3584]{1,0:T(8,128)(2,1)S(1)}, u32[]{:S(2)}, u32[]{:S(2)}) collective-permute-start(bf16[32,3584]{1,0:T(8,128)(2,1)S(1)} %get-tuple-element.206), channel_id=1, source_target_pairs={{0,2},{1,3},{4,0},{5,1},{8,4},{9,5},{12,8},{13,9},{14,12},{15,13},... | collective-permute-start | bytes 688136 | tf_op jit(solution)/shard_map/ppermute | solution.py:311
